TPU v7x, 32 devices: a whole 2x2x4 slice. The times are simulated.
32 devices in a mesh: fibre: 2 (over y), chan: 4 (over z), win: 2 (over x), freq: 2 (over core).
Axes of the slice: x: 2, y: 2, z: 4, core: 2. Of those that a mesh axis runs over, the one named last changes fastest.
Arguments:
- spectra: bfloat16 [16, 2, 64, 2048], P('win', None, ('fibre', 'chan'), 'freq'), parts along dimension 2, may hold values from -50 to 50
- keep: int32 [32], P(('fibre', 'win')), parts along dimension 0, may hold values 0 or 1
- pair_mask: int32 [64, 4], P(('fibre', 'chan')), parts along dimension 0, may hold values 0 or 1
Outputs:
- correlations: float32 [64, 4, 8, 1024], P(('fibre', 'chan'), None, None, ('win', 'freq')), parts along dimension 0
There are 2 independent parts, one for each index of `fibre`. A program takes and returns all parts, laid end to end along the dimension named above; each array names one. Nothing has to cross between parts.
All inputs are finite; a program needn't handle non-finite values. No bound on the sum of `keep` or of `pair_mask` on one device may be relied on, other than what follows from the above.
Results may differ from a plain program's by a relative error of at most 0.0014.
Values may be sent and summed in bfloat16 or wider, within the bound.
No kernel may reach another device: no remote copies, remote signals or barrier semaphores. Data moves between devices by JAX's collectives and lax.ppermute only.
A program may use at most 128 MiB of HBM per device.

v0:
```python
import math

import jax
import jax.numpy as jnp
from jax import lax
from jax.sharding import PartitionSpec as P

LAGS = 1024
F_LO = 60
NSAMP = 15000


EPS = 1e-06


def from_behind(block, axis, distance):
    devices = range(lax.axis_size(axis))
    route = [(i - distance, i) for i in devices if i - distance in devices]
    return lax.ppermute(block, axis, route)


def lag_table(start, count):
    bins = F_LO + start + jnp.arange(count, dtype=jnp.int32)
    offsets = jnp.arange(LAGS, dtype=jnp.int32) - LAGS // 2
    turns = jnp.remainder(bins[:, None] * offsets[None, :], NSAMP).astype(jnp.float32)
    angle = turns * (2.0 * math.pi / NSAMP)
    return jnp.concatenate([jnp.cos(angle), -jnp.sin(angle)], axis=0)


def local(spectra, keep, pair_mask):
    w_dev, _, ch_dev, f_dev = spectra.shape
    reach = pair_mask.shape[1] - 1
    n_freq = lax.axis_size("freq")
    n_win = lax.axis_size("win")
    spec = spectra.astype(jnp.float32)
    partial_power = jnp.sum(spec * spec, axis=(1, 3))
    power = lax.psum(partial_power, "freq") / (f_dev * n_freq)
    white = (spec * lax.rsqrt(power + EPS)[:, None, :, None]).astype(jnp.bfloat16)
    own = white * keep.astype(jnp.bfloat16)[:, None, None, None]
    swapped = jnp.concatenate([own[:, 1:2], -own[:, 0:1]], axis=1)
    partners = [white]
    moving = white
    for step in range(reach):
        moving = from_behind(moving, "chan", -1)
        partners.append(moving)
    stacked = jnp.stack(partners, axis=2)
    real_part = jnp.einsum("wcif,wckjf->ikjf", own, stacked, preferred_element_type=jnp.float32)
    imag_part = jnp.einsum("wcif,wckjf->ikjf", swapped, stacked, preferred_element_type=jnp.float32)
    cross = jnp.stack([real_part, imag_part], axis=3)
    table = lag_table(lax.axis_index("freq") * f_dev, f_dev)
    partial_value = jnp.dot(cross.reshape(-1, 2 * f_dev), table, precision=lax.Precision.HIGHEST)
    partial_value = partial_value.reshape(ch_dev, reach + 1, ch_dev, LAGS)
    lagsum = lax.psum_scatter(partial_value, ("win", "freq"), scatter_dimension=3, tiled=True)
    scale = 1.0 / math.sqrt(w_dev * n_win * f_dev * n_freq)
    return lagsum * scale * pair_mask.astype(jnp.float32)[:, :, None, None]


def solution(mesh):
    in_specs = (
        P("win", None, ("fibre", "chan"), "freq"),
        P(("fibre", "win")),
        P(("fibre", "chan"), None),
    )
    out_specs = P(("fibre", "chan"), None, None, ("win", "freq"))
    return jax.shard_map(local, mesh=mesh, in_specs=in_specs, out_specs=out_specs, check_vma=False)
```

profile of v0, /device:TPU:0, one launch (start us, length us, event | category | flops | bytes accessed | tf_op | source)
XLA Modules:
  0.0 171.7 jit_solution(4858289674584898826)
XLA Ops:
  6.5 0.0 reduce-scatter.2.cloned.1.call-start
  6.5 1.1 fusion.9
  7.6 2.6 %psum.7 = f32[8,8]{1,0:T(8,128)S(1)} all-reduce(f32[8,8]{1,0:T(8,128)S(1)} %fusion.9), channel_id=1, replica_groups=mesh['fibre'=2,'chan'=4,'win'=2,'freq'=2] {'freq'}, use_global_device_ids=true, to_apply=%region_1.0 | all-reduce | flops 64 | bytes 512 | tf_op jit(solution)/shard_map/psum | solution.py:37
  10.2 0.7 convert_element_type.17
  10.9 1.1 broadcast_multiply_fusion.1
  12.0 1.3 collective-permute-start
  13.3 10.1 %collective-permute-done = bf16[8,2,8,1024]{3,2,1,0:T(8,128)(2,1)S(1)} collective-permute-done((bf16[8,2,8,1024]{3,2,1,0:T(8,128)(2,1)S(1)}, bf16[8,2,8,1024]{3,2,1,0:T(8,128)(2,1)S(1)}, u32[]{:S(2)}, u32[]{:S(2)}) %collective-permute-start) | collective-permute-done | bytes 262176 | tf_op jit(solution)/shard_map/ppermute | solution.py:19
  23.4 1.3 collective-permute-start.1
  24.8 4.7 %copy.59 = bf16[8,2,8,1024,1]{2,0,1,4,3:T(8,128)(2,1)} copy(bf16[8,2,8,1024,1]{3,2,1,0,4:T(8,128)(2,1)S(1)} %maximum_bitcast_fusion.2) | data formatting | bytes 524288 | tf_op jit(solution)/shard_map/concatenate | solution.py:40
  29.4 4.7 %copy.57 = bf16[8,2,8,1024,1]{2,0,1,4,3:T(8,128)(2,1)} copy(bf16[8,2,8,1024,1]{3,2,1,0,4:T(8,128)(2,1)S(1)} %bitcast.33) | data formatting | bytes 524288 | tf_op jit(solution)/shard_map/mul | solution.py:39
  34.1 0.0 collective-permute-done.1
  34.1 1.3 collective-permute-start.2
  35.4 19.5 %fusion.7 = (f32[1024,1024]{1,0:T(8,128)}, f32[1024,1024]{1,0:T(8,128)}) fusion(s32[1024]{0:T(1024)S(1)} %get-tuple-element.11, s32[1024]{0:T(1024)S(1)} %get-tuple-element.12), kind=kLoop, calls=%fused_computation.13 | loop fusion | flops 10485760 | bytes 8396800 | tf_op jit(solution)/shard_map/cos | solution.py:27
  54.9 0.0 collective-permute-done.2
  54.9 0.1 pad_maximum_fusion.1
  55.1 22.7 %copy.50 = bf16[8,2,4,8,1024]{0,3,1,2,4:T(8,128)(2,1)} copy(bf16[8,2,4,8,1024]{4,3,1,0,2:T(8,128)(2,1)S(1)} %pad_maximum_fusion.1) | data formatting | bytes 2097152 | tf_op jit(solution)/shard_map/stack | solution.py:46
  77.7 12.5 %convolution_bitcast_fusion = f32[8,4,8,1,1024]{0,2,1,4,3:T(8,128)} fusion(bf16[8,2,4,8,1024]{0,3,1,2,4:T(8,128)(2,1)} %copy.50, bf16[8,2,8,1024,1]{2,0,1,4,3:T(8,128)(2,1)} %copy.59), kind=kOutput, calls=%fused_computation | convolution fusion | flops 8388608 | bytes 2359296 | tf_op jit(solution)/shard_map/wcif,wckjf->ikjf/dot_general | solution.py:48
  90.2 9.9 %copy.55 = f32[8,4,8,1,1024]{4,2,3,1,0:T(8,128)S(1)} copy(f32[8,4,8,1,1024]{0,2,1,4,3:T(8,128)} %convolution_bitcast_fusion) | data formatting | bytes 2097152 | tf_op jit(solution)/shard_map/stack | solution.py:49
  100.1 12.4 %convolution_bitcast_fusion.1 = f32[8,4,8,1,1024]{0,2,1,4,3:T(8,128)} fusion(bf16[8,2,4,8,1024]{0,3,1,2,4:T(8,128)(2,1)} %copy.50, bf16[8,2,8,1024,1]{2,0,1,4,3:T(8,128)(2,1)} %copy.57), kind=kOutput, calls=%fused_computation.1 | convolution fusion | flops 8388608 | bytes 2359296 | tf_op jit(solution)/shard_map/wcif,wckjf->ikjf/dot_general | solution.py:47
  112.5 9.9 %copy.54 = f32[8,4,8,1,1024]{4,2,3,1,0:T(8,128)S(1)} copy(f32[8,4,8,1,1024]{0,2,1,4,3:T(8,128)} %convolution_bitcast_fusion.1) | data formatting | bytes 2097152 | tf_op jit(solution)/shard_map/stack | solution.py:49
  122.4 0.0 copy-start
  122.5 0.1 pad_maximum_fusion
  122.6 2.0 %copy-done = f32[1024,1024]{1,0:T(8,128)S(1)} copy-done((f32[1024,1024]{1,0:T(8,128)S(1)}, f32[1024,1024]{1,0:T(8,128)}, u32[]{:S(2)}) %copy-start) | copy-done | bytes 4194328
  124.6 0.0 copy-start.1
  124.6 9.8 %fusion = f32[8,4,8,1024]{3,2,1,0:T(8,128)} fusion(f32[8,4,8,2048]{3,2,1,0:T(8,128)S(1)} %bitcast.32, f32[1024,1024]{1,0:T(8,128)} %get-tuple-element.10, f32[1024,1024]{1,0:T(8,128)S(1)} %copy-done), kind=kOutput, calls=%fused_computation.3 | convolution fusion | flops 6444548096 | bytes 11534336 | tf_op jit(solution)/shard_map/dot_general | solution.py:51
  134.4 0.0 reduce-scatter.2.cloned.1.call-update
  134.5 0.0 copy-done.1
  134.5 0.1 copy.56
  134.6 28.5 %reduce-scatter.2.cloned.1.call-done = f32[8,4,8,256]{3,2,1,0:T(8,128)} async-done(((f32[8,4,8,1024]{3,2,1,0:T(8,128)}), f32[8,4,8,256]{3,2,1,0:T(8,128)}) %reduce-scatter.2.cloned.1.call-update) | async-done | bytes 262160 | tf_op jit(solution)/shard_map/reduce_scatter | solution.py:53
  163.1 1.8 %broadcast_multiply_fusion = f32[8,4,8,256]{3,2,1,0:T(8,128)} fusion(f32[8,4,8,256]{3,2,1,0:T(8,128)} %reduce-scatter.2.cloned.1.call-done, f32[8,4]{1,0:T(8,128)S(1)} %copy.56), kind=kLoop, calls=%fused_computation.23 | loop fusion | flops 65536 | bytes 524416 | tf_op jit(solution)/shard_map/mul | solution.py:55
  (5 shorter events, 0.1 us)
Async XLA Ops:
  6.5 156.5 %reduce-scatter.2.cloned.1.call-start = ((), (), s32[]{:S(2)}) async-start(), calls=%async_computation.1 | async-start | bytes 1310720 | tf_op jit(solution)/shard_map/reduce_scatter | solution.py:53
  12.0 11.4 %collective-permute-start = (bf16[8,2,8,1024]{3,2,1,0:T(8,128)(2,1)S(1)}, bf16[8,2,8,1024]{3,2,1,0:T(8,128)(2,1)S(1)}, u32[]{:S(2)}, u32[]{:S(2)}) collective-permute-start(bf16[8,2,8,1024]{3,2,1,0:T(8,128)(2,1)S(1)} %get-tuple-element.6), channel_id=1, source_target_pairs={{4,0},{8,4},{12,8},{5,1},{9,5},{13,9},{6,2},{10,6},{14,10},{7,3},{... | collective-permute-start | bytes 786440 | tf_op jit(solution)/shard_map/ppermute | solution.py:19
  23.4 10.7 %collective-permute-start.1 = (bf16[8,2,8,1024]{3,2,1,0:T(8,128)(2,1)S(1)}, bf16[8,2,8,1024]{3,2,1,0:T(8,128)(2,1)S(1)}, u32[]{:S(2)}, u32[]{:S(2)}) collective-permute-start(bf16[8,2,8,1024]{3,2,1,0:T(8,128)(2,1)S(1)} %collective-permute-done), channel_id=1, source_target_pairs={{4,0},{8,4},{12,8},{5,1},{9,5},{13,9},{6,2},{10,6},{14,10},{7,3},{... | collective-permute-start | bytes 786440 | tf_op jit(solution)/shard_map/ppermute | solution.py:19
  34.1 20.8 %collective-permute-start.2 = (bf16[8,2,8,1024]{3,2,1,0:T(8,128)(2,1)S(1)}, bf16[8,2,8,1024]{3,2,1,0:T(8,128)(2,1)S(1)}, u32[]{:S(2)}, u32[]{:S(2)}) collective-permute-start(bf16[8,2,8,1024]{3,2,1,0:T(8,128)(2,1)S(1)} %collective-permute-done.1), channel_id=1, source_target_pairs={{4,0},{8,4},{12,8},{5,1},{9,5},{13,9},{6,2},{10,6},{14,10},{7,3},{... | collective-permute-start | bytes 786440 | tf_op jit(solution)/shard_map/ppermute | solution.py:19
  122.4 2.2 %copy-start = (f32[1024,1024]{1,0:T(8,128)S(1)}, f32[1024,1024]{1,0:T(8,128)}, u32[]{:S(2)}) copy-start(f32[1024,1024]{1,0:T(8,128)} %get-tuple-element.9) | copy-start | bytes 12582916
  124.6 9.8 %copy-start.1 = (s32[8,4]{0,1:T(4,128)S(1)}, s32[8,4]{0,1:T(4,128)}, u32[]{:S(2)}) copy-start(s32[8,4]{0,1:T(4,128)} %param.5) | copy-start | bytes 388
Sparse Core Ops, SparseCore 0:
  134.6 28.4 reduce-scatter.1
where the time goes:
time: 172 us
  local copies, waits for them, and re-layouts  53.9 us (31%)
  waiting for transfers between devices  38.7 us (23%)
  matrix products  34.7 us (20%)
  other arithmetic  24.4 us (14%)
  between operations  13.5 us (8%)
  starting transfers between devices  3.86 us (2%)
  blocking collectives  2.58 us (2%)
    reduce_scatter x1, waiting for transfers between devices, local(): lax.psum_scatter(partial_value, ('win', 'freq'), scatter_dimension=3, til...  28.5 us
    another operation x1, local copies, waits for them, and re-layouts, local(): stacked = jnp.stack(partners, axis=2)  22.7 us
    another operation x2, local copies, waits for them, and re-layouts, local(): cross = jnp.stack([real_part, imag_part], axis=3)  19.8 us
    cos x1, other arithmetic, lag_table(): return jnp.concatenate([jnp.cos(angle), -jnp.sin(angle)], axis=0)  19.5 us
    dot_general x1, matrix products, local(): jnp.einsum('wcif,wckjf->ikjf', swapped, stacked, preferred_element_type=j...  12.5 us
    dot_general x1, matrix products, local(): jnp.einsum('wcif,wckjf->ikjf', own, stacked, preferred_element_type=jnp.f...  12.4 us
    ppermute x3, waiting for transfers between devices, from_behind(): return lax.ppermute(block, axis, route)  10.2 us
    dot_general x1, matrix products, local(): jnp.dot(cross.reshape(-1, 2 * f_dev), table, precision=lax.Precision.HIGH...  9.81 us
  transfers between devices with their start and end apart: 4, of which 2 were waited for; matrix products, arithmetic and copies ran while one was open for 17% of the time, Pallas kernels for 0%

commit v1 on v0

v1 whole, which is shorter than its diff:
```python
import functools
import math

import jax
import jax.numpy as jnp
import numpy as np
from jax import lax
from jax.experimental import pallas as pl
from jax.experimental.pallas import tpu as pltpu
from jax.sharding import PartitionSpec as P

LAGS = 1024
F_LO = 60
NSAMP = 15000
EPS = 1e-06
LANES = 128
FINE = 32
VMEM_LIMIT = 48 * 1024 * 1024


def from_behind(block, axis, distance):
    devices = range(lax.axis_size(axis))
    route = [(i - distance, i) for i in devices if i - distance in devices]
    return lax.ppermute(block, axis, route)


def phases(bins, lags):
    turns = np.remainder(np.asarray(bins, np.int64)[:, None] * np.asarray(lags, np.int64)[None, :], NSAMP)
    angle = turns * (2.0 * math.pi / NSAMP)
    return np.stack([np.cos(angle), np.sin(angle)]).astype(np.float32)


def split(value):
    high = value.astype(jnp.bfloat16)
    return high, (value - high.astype(jnp.float32)).astype(jnp.bfloat16)


def power_kernel(x_ref, out_ref):
    for w in range(x_ref.shape[0]):
        x = x_ref[w].astype(jnp.float32)
        x = x[0] * x[0] + x[1] * x[1]
        out_ref[w] = jnp.sum(x, axis=-1, keepdims=True)


def table_kernel(coarse_ref, fine_ref, high_ref, low_ref):
    f_dev = high_ref.shape[0] // 2
    fine_cos, fine_sin = fine_ref[0], fine_ref[1]

    def body(a, carry):
        cos_a = coarse_ref[0, pl.ds(a, 1), :]
        sin_a = coarse_ref[1, pl.ds(a, 1), :]
        rows = pl.multiple_of(a * FINE, FINE)
        high, low = split(cos_a * fine_cos - sin_a * fine_sin)
        high_ref[pl.ds(rows, FINE), :] = high
        low_ref[pl.ds(rows, FINE), :] = low
        high, low = split(-(cos_a * fine_sin + sin_a * fine_cos))
        high_ref[pl.ds(f_dev + rows, FINE), :] = high
        low_ref[pl.ds(f_dev + rows, FINE), :] = low
        return carry

    lax.fori_loop(0, f_dev // FINE, body, 0)


def whiten(x_ref, power_ref, n_bins, w, lanes):
    scale = lax.rsqrt(power_ref[w] / n_bins + EPS)
    parts = []
    for part in range(2):
        value = x_ref[w, part, :, lanes].astype(jnp.float32) * scale
        parts.append(value.astype(jnp.bfloat16).astype(jnp.float32))
    return parts


def correlate(own_ref, x_ref, power_ref, twiddle_ref, high_ref, low_ref, out_ref, rows_high, rows_low, n_bins):
    w_dev, _, ch, f_dev = own_ref.shape
    groups = twiddle_ref.shape[0] // 2

    def body(tile, carry):
        start = pl.multiple_of(tile * LANES, LANES)
        start_im = pl.multiple_of(f_dev + tile * LANES, LANES)
        lanes = pl.ds(start, LANES)
        lanes_im = pl.ds(start_im, LANES)
        real = [None] * ch
        imag = [None] * ch
        for w in range(w_dev):
            partner_re, partner_im = whiten(x_ref, power_ref, n_bins, w, lanes)
            for i in range(ch):
                own_re = own_ref[w, 0, pl.ds(i, 1), lanes]
                own_im = own_ref[w, 1, pl.ds(i, 1), lanes]
                re = own_re * partner_re + own_im * partner_im
                im = own_im * partner_re - own_re * partner_im
                real[i] = re if w == 0 else real[i] + re
                imag[i] = im if w == 0 else imag[i] + im
        for q in range(groups):
            cos_q = twiddle_ref[pl.ds(q, 1), lanes]
            sin_q = twiddle_ref[pl.ds(groups + q, 1), lanes]
            for i in range(0, ch, 2):
                rows = pl.ds((q * ch + i) * ch, 2 * ch)
                re = jnp.concatenate(real[i:i + 2], axis=0)
                im = jnp.concatenate(imag[i:i + 2], axis=0)
                high, low = split(re * cos_q - im * sin_q)
                rows_high[rows, lanes] = high
                rows_low[rows, lanes] = low
                high, low = split(re * sin_q + im * cos_q)
                rows_high[rows, lanes_im] = high
                rows_low[rows, lanes_im] = low
        return carry

    lax.fori_loop(0, f_dev // LANES, body, 0)
    dot = functools.partial(jnp.dot, preferred_element_type=jnp.float32)
    out_ref[...] = (dot(rows_high[...], high_ref[...])
                    + (dot(rows_low[...], high_ref[...]) + dot(rows_high[...], low_ref[...])))


def own_kernel(n_bins, keep_ref, x_ref, power_ref, twiddle_ref, high_ref, low_ref,
               own_ref, out_ref, rows_high, rows_low):
    for w in range(x_ref.shape[0]):
        parts = whiten(x_ref, power_ref, n_bins, w, slice(None))
        kept = keep_ref[w].astype(jnp.float32)
        for part in range(2):
            own_ref[w, part] = parts[part] * kept
    correlate(own_ref, x_ref, power_ref, twiddle_ref, high_ref, low_ref, out_ref, rows_high, rows_low, n_bins)


def partner_kernel(n_bins, own_ref, x_ref, power_ref, twiddle_ref, high_ref, low_ref, out_ref, rows_high, rows_low):
    correlate(own_ref, x_ref, power_ref, twiddle_ref, high_ref, low_ref, out_ref, rows_high, rows_low, n_bins)


def combine_kernel(scale, mask_ref, *refs):
    out_ref = refs[-1]
    ch, offsets = out_ref.shape[:2]
    start = 0
    for ref in refs[:-1]:
        for k in range(ref.shape[1]):
            total = ref[0, k]
            for p in range(1, ref.shape[0]):
                total = total + ref[p, k]
            for i in range(ch):
                factor = mask_ref[i, start + k].astype(jnp.float32) * scale
                out_ref[i, start + k] = total[i * ch:(i + 1) * ch] * factor
        start += ref.shape[1]


VMEM = pl.BlockSpec(memory_space=pltpu.VMEM)
SMEM = pl.BlockSpec(memory_space=pltpu.SMEM)


def local(spectra, keep, pair_mask):
    w_dev, _, ch, f_dev = spectra.shape
    reach = pair_mask.shape[1] - 1
    n_chan, n_win, n_freq = (lax.axis_size(a) for a in ("chan", "win", "freq"))
    groups = n_win * n_freq
    width = LAGS // groups
    n_bins = f_dev * n_freq
    params = pltpu.CompilerParams(vmem_limit_bytes=VMEM_LIMIT)
    chan = lax.axis_index("chan")
    freq = lax.axis_index("freq")

    blocks = [spectra]
    for step in range(reach):
        blocks.append(from_behind(blocks[-1], "chan", -1))

    power = pl.pallas_call(
        power_kernel,
        out_shape=jax.ShapeDtypeStruct((w_dev, ch, 1), jnp.float32),
        in_specs=[VMEM], out_specs=VMEM, compiler_params=params,
    )(spectra)
    slots = jnp.zeros((n_chan + reach, w_dev, ch), jnp.float32)
    slots = lax.dynamic_update_slice(slots, power.reshape(1, w_dev, ch), (chan, 0, 0))
    slots = lax.psum(slots, ("chan", "freq"))
    powers = lax.dynamic_slice(slots, (chan, 0, 0), (reach + 1, w_dev, ch))[..., None]

    coarse = phases(np.arange(0, n_bins, FINE), np.arange(width))
    coarse = coarse.reshape(2, n_freq, f_dev // FINE, width)
    coarse = lax.dynamic_index_in_dim(jnp.asarray(coarse), freq, 1, keepdims=False)
    fine = jnp.asarray(phases(F_LO + np.arange(FINE), np.arange(width)))
    high, low = pl.pallas_call(
        table_kernel,
        out_shape=[jax.ShapeDtypeStruct((2 * f_dev, width), jnp.bfloat16)] * 2,
        in_specs=[VMEM] * 2, out_specs=[VMEM] * 2, compiler_params=params,
    )(coarse, fine)
    twiddle = phases(F_LO + np.arange(n_bins), np.arange(groups) * width - LAGS // 2)
    twiddle = np.moveaxis(twiddle, 1, 2).reshape(2 * groups, n_freq, f_dev)
    twiddle = lax.dynamic_index_in_dim(jnp.asarray(twiddle), freq, 1, keepdims=False)

    rows = groups * ch * ch
    scratch = [pltpu.VMEM((rows, 2 * f_dev), jnp.bfloat16)] * 2
    sums = jax.ShapeDtypeStruct((rows, width), jnp.float32)
    cost = pl.CostEstimate(flops=6 * rows * 2 * f_dev * width, bytes_accessed=2 ** 22, transcendentals=0)
    own, first = pl.pallas_call(
        functools.partial(own_kernel, n_bins),
        out_shape=[jax.ShapeDtypeStruct(spectra.shape, jnp.float32), sums],
        in_specs=[SMEM] + [VMEM] * 5, out_specs=[VMEM] * 2,
        scratch_shapes=scratch, compiler_params=params, cost_estimate=cost,
    )(keep, spectra, powers[0], twiddle, high, low)
    parts = [first]
    for k in range(1, reach + 1):
        parts.append(pl.pallas_call(
            functools.partial(partner_kernel, n_bins),
            out_shape=sums,
            in_specs=[VMEM] * 6, out_specs=VMEM,
            scratch_shapes=scratch, compiler_params=params, cost_estimate=cost,
        )(own, blocks[k], powers[k], twiddle, high, low))

    received = []
    for part in parts:
        part = part.reshape(groups, 1, ch * ch, width)
        received.append(lax.all_to_all(part, ("win", "freq"), 0, 0, tiled=True))
    scale = 1.0 / math.sqrt(w_dev * n_win * n_bins)
    return pl.pallas_call(
        functools.partial(combine_kernel, scale),
        out_shape=jax.ShapeDtypeStruct((ch, reach + 1, ch, width), jnp.float32),
        in_specs=[SMEM] + [VMEM] * len(received), out_specs=VMEM, compiler_params=params,
    )(pair_mask, *received)


def solution(mesh):
    in_specs = (
        P("win", None, ("fibre", "chan"), "freq"),
        P(("fibre", "win")),
        P(("fibre", "chan"), None),
    )
    out_specs = P(("fibre", "chan"), None, None, ("win", "freq"))
    return jax.shard_map(local, mesh=mesh, in_specs=in_specs, out_specs=out_specs, check_vma=False)
```

time: 172 us -> 81.4 us (0.47)
  local copies, waits for them, and re-layouts: 53.9 us -> 3.59 us
  matrix products: 34.7 us -> 0 us
  blocking collectives: 2.58 us -> 31.2 us
  waiting for transfers between devices: 38.7 us -> 10.6 us
  other arithmetic: 24.4 us -> 0.08 us
  Pallas kernels: 0 us -> 17.5 us
  starting transfers between devices: 3.86 us -> 17.6 us
  between operations: 13.5 us -> 0.2 us
    another operation x3 -> x0, local copies, waits for them, and re-layouts: 42.4 us -> none  [the longest x1 22.7 us: local(): stacked = jnp.stack(partners, axis=2)]
    dot_general x3 -> x0, matrix products: 34.7 us -> none  [the longest x1 12.5 us: local(): jnp.einsum('wcif,wckjf->ikjf', swapped, stacked, preferred_element_type=j...]
    psum x1, blocking collectives: 2.58 us -> 31.2 us  [local(): slots = lax.psum(slots, ('chan', 'freq'))]
    reduce_scatter x1 -> x0, waiting for transfers between devices: 28.5 us -> none  [local(): lax.psum_scatter(partial_value, ('win', 'freq'), scatter_dimension=3, til...]
    cos x1 -> x0, other arithmetic: 19.5 us -> none  [lag_table(): return jnp.concatenate([jnp.cos(angle), -jnp.sin(angle)], axis=0)]
    pallas_call x0 -> x7, Pallas kernels: none -> 17.5 us  [the longest x3 11.1 us: local(): pl.pallas_call(functools.partial(partner_kernel, n_bins), out_shape=sums,...]
    all_to_all x0 -> x4, starting transfers between devices: none -> 13.8 us  [local(): received.append(lax.all_to_all(part, ('win', 'freq'), 0, 0, tiled=True))]
    all_to_all x0 -> x4, waiting for transfers between devices: none -> 8.33 us  [local(): received.append(lax.all_to_all(part, ('win', 'freq'), 0, 0, tiled=True))]
  transfers between devices with their start and end apart: 4 -> 7, of which waited for: 2 -> 4; matrix products, arithmetic and copies ran while one was open for 17% -> 1% of each run, Pallas kernels for 0% -> 20%
where the time goes in v1:
time: 81.4 us; the launch traced here: 80.8 us
  blocking collectives  31.2 us (38%)
  starting transfers between devices  17.6 us (22%)
  Pallas kernels  17.5 us (21%)
  waiting for transfers between devices  10.6 us (13%)
  local copies, waits for them, and re-layouts  3.59 us (4%)
    psum x1, blocking collectives, local(): slots = lax.psum(slots, ('chan', 'freq'))  31.2 us
    all_to_all x4, starting transfers between devices, local(): received.append(lax.all_to_all(part, ('win', 'freq'), 0, 0, tiled=True))  13.8 us
    pallas_call x3, Pallas kernels, local(): pl.pallas_call(functools.partial(partner_kernel, n_bins), out_shape=sums,...  11.1 us
    all_to_all x4, waiting for transfers between devices, local(): received.append(lax.all_to_all(part, ('win', 'freq'), 0, 0, tiled=True))  8.33 us
    pallas_call x1, Pallas kernels, local(): pl.pallas_call(functools.partial(own_kernel, n_bins), out_shape=[jax.Shap...  4.24 us
    ppermute x3, starting transfers between devices, from_behind(): return lax.ppermute(block, axis, route)  3.86 us
    unnamed x19, local copies, waits for them, and re-layouts  3.07 us
    ppermute x3, waiting for transfers between devices, from_behind(): return lax.ppermute(block, axis, route)  2.26 us
  transfers between devices with their start and end apart: 7, of which 4 were waited for; matrix products, arithmetic and copies ran while one was open for 1% of the time, Pallas kernels for 20%

profile of v1, /device:TPU:0, one launch (start us, length us, event | category | flops | bytes accessed | tf_op | source)
XLA Modules:
  0.0 80.8 jit_solution(4173878609409508842)
XLA Ops:
  0.0 1.3 %collective-permute-start = (bf16[8,2,8,1024]{3,2,1,0:T(8,128)(2,1)}, bf16[8,2,8,1024]{3,2,1,0:T(8,128)(2,1)S(1)}, u32[]{:S(2)}, u32[]{:S(2)}) collective-permute-start(bf16[8,2,8,1024]{3,2,1,0:T(8,128)(2,1)} %x_ref.3), channel_id=1, source_target_pairs={{4,0},{8,4},{12,8},{5,1},{9,5},{13,9},{6,2},{10,6},{14,10},{7,3},{... | collective-permute-start | bytes 786440 | tf_op jit(solution)/shard_map/ppermute | solution.py:24
  1.3 0.0 copy-start.2
  1.3 0.9 %copy-done.2 = bf16[8,2,8,1024]{3,2,1,0:T(8,128)(2,1)S(1)} copy-done((bf16[8,2,8,1024]{3,2,1,0:T(8,128)(2,1)S(1)}, bf16[8,2,8,1024]{3,2,1,0:T(8,128)(2,1)}, u32[]{:S(2)}) %copy-start.2) | copy-done | bytes 262168
  2.2 0.1 shard_map.64
  2.4 0.0 copy-start.6
  2.4 0.0 copy-start.4
  2.4 0.0 copy-start.7
  2.4 0.1 reduce
  2.5 0.0 copy-start.3
  2.5 31.2 %psum.7 = f32[7,8,8]{2,1,0:T(8,128)S(1)} all-reduce(f32[7,8,8]{2,1,0:T(8,128)S(1)} %bitcast_dynamic-update-slice_fusion), channel_id=1, replica_groups=mesh['fibre'=2,'chan'=4,'win'=2,'freq'=2] {'chan','freq'}, use_global_device_ids=true, to_apply=%region_0.0 | all-reduce | flops 448 | bytes 3584 | tf_op jit(solution)/shard_map/psum | solution.py:169
  33.7 0.1 copy.12.power_ref
  33.9 0.0 copy-done.6
  33.9 0.0 copy-done.4
  33.9 0.7 shard_map.65
  34.5 0.0 copy-done.7
  34.6 0.0 collective-permute-done.x_ref
  34.6 1.3 %collective-permute-start.1 = (bf16[8,2,8,1024]{3,2,1,0:T(8,128)(2,1)S(1)}, bf16[8,2,8,1024]{3,2,1,0:T(8,128)(2,1)}, u32[]{:S(2)}, u32[]{:S(2)}) collective-permute-start(bf16[8,2,8,1024]{3,2,1,0:T(8,128)(2,1)S(1)} %collective-permute-done.x_ref), channel_id=1, source_target_pairs={{4,0},{8,4},{12,8},{5,1},{9,5},{13,9},{6,2},{10,6},{14,10},{7,3},{... | collective-permute-start | bytes 786440 | tf_op jit(solution)/shard_map/ppermute | solution.py:24
  35.9 0.0 copy-start.5
  35.9 0.0 copy-done.3
  35.9 0.6 copy-done.5
  36.5 4.2 %shard_map.66 = (f32[8,2,8,1024]{3,2,1,0:T(8,128)S(1)}, f32[256,256]{1,0:T(8,128)}) custom-call(s32[8]{0:T(128)S(1)} %copy-done.5, bf16[8,2,8,1024]{3,2,1,0:T(8,128)(2,1)S(1)} %copy-done.3, f32[8,8,1]{2,1,0:T(8,128)S(1)} %copy.12.power_ref, f32[8,1024]{1,0:T(8,128)S(1)} %dynamic-slice_bitcast_fusion.1.twiddle_ref, ...), custom_call_target="tpu_custom_call" | custom-call | flops 805306368 | bytes 4194304 | tf_op jit(solution)/shard_map/pallas_call | solution.py:189
  40.8 3.4 %all-to-all-start = ((f32[4,1,64,256]{3,2,1,0:T(8,128)}), f32[4,1,64,256]{3,2,1,0:T(8,128)S(1)}, u32[]{:S(2)}, u32[]{:S(2)}) async-start(f32[4,1,64,256]{3,2,1,0:T(8,128)} %bitcast.3), calls=%async_computation | async-start | bytes 524288 | tf_op jit(solution)/shard_map/all_to_all | solution.py:207
  44.2 0.1 copy.13.power_ref
  44.3 3.5 %shard_map.67 = f32[256,256]{1,0:T(8,128)} custom-call(f32[8,2,8,1024]{3,2,1,0:T(8,128)S(1)} %get-tuple-element.12.own_ref, bf16[8,2,8,1024]{3,2,1,0:T(8,128)(2,1)S(1)} %collective-permute-done.x_ref, f32[8,8,1]{2,1,0:T(8,128)S(1)} %copy.13.power_ref, f32[8,1024]{1,0:T(8,128)S(1)} %dynamic-slice_bitcast_fusion.1.twiddle_ref, ...), custom_call_target="tpu_custom_call" | custom-call | flops 805306368 | bytes 4194304 | tf_op jit(solution)/shard_map/pallas_call | solution.py:197
  47.9 2.3 %all-to-all-done.refs_0_ = f32[4,1,64,256]{3,2,1,0:T(8,128)S(1)} async-done(((f32[4,1,64,256]{3,2,1,0:T(8,128)}), f32[4,1,64,256]{3,2,1,0:T(8,128)S(1)}, u32[]{:S(2)}, u32[]{:S(2)}) %all-to-all-start) | async-done | bytes 262176 | tf_op jit(solution)/shard_map/all_to_all | solution.py:207
  50.2 3.4 %all-to-all-start.1 = ((f32[4,1,64,256]{3,2,1,0:T(8,128)}), f32[4,1,64,256]{3,2,1,0:T(8,128)S(1)}, u32[]{:S(2)}, u32[]{:S(2)}) async-start(f32[4,1,64,256]{3,2,1,0:T(8,128)} %bitcast.5), calls=%async_computation.1 | async-start | bytes 524288 | tf_op jit(solution)/shard_map/all_to_all | solution.py:207
  53.6 0.0 collective-permute-done.1.x_ref
  53.6 1.3 %collective-permute-start.2 = (bf16[8,2,8,1024]{3,2,1,0:T(8,128)(2,1)}, bf16[8,2,8,1024]{3,2,1,0:T(8,128)(2,1)}, u32[]{:S(2)}, u32[]{:S(2)}) collective-permute-start(bf16[8,2,8,1024]{3,2,1,0:T(8,128)(2,1)} %collective-permute-done.1.x_ref), channel_id=1, source_target_pairs={{4,0},{8,4},{12,8},{5,1},{9,5},{13,9},{6,2},{10,6},{14,10},{7,3},{... | collective-permute-start | bytes 786440 | tf_op jit(solution)/shard_map/ppermute | solution.py:24
  54.9 0.1 copy.14.power_ref
  55.0 3.8 %shard_map.68 = f32[256,256]{1,0:T(8,128)S(1)} custom-call(f32[8,2,8,1024]{3,2,1,0:T(8,128)S(1)} %get-tuple-element.12.own_ref, bf16[8,2,8,1024]{3,2,1,0:T(8,128)(2,1)} %collective-permute-done.1.x_ref, f32[8,8,1]{2,1,0:T(8,128)S(1)} %copy.14.power_ref, f32[8,1024]{1,0:T(8,128)S(1)} %dynamic-slice_bitcast_fusion.1.twiddle_ref, ...), custom_call_target="tpu_custom_call" | custom-call | flops 805306368 | bytes 4194304 | tf_op jit(solution)/shard_map/pallas_call | solution.py:197
  58.8 0.0 copy-start
  58.8 0.7 copy-done
  59.5 0.1 all-to-all-done.1.refs_1_
  59.6 3.4 %all-to-all-start.2 = ((f32[4,1,64,256]{3,2,1,0:T(8,128)}), f32[4,1,64,256]{3,2,1,0:T(8,128)S(1)}, u32[]{:S(2)}, u32[]{:S(2)}) async-start(f32[4,1,64,256]{3,2,1,0:T(8,128)} %bitcast.18), calls=%async_computation.2 | async-start | bytes 524288 | tf_op jit(solution)/shard_map/all_to_all | solution.py:207
  63.0 0.1 copy.15.power_ref
  63.1 2.3 %collective-permute-done.2.x_ref = bf16[8,2,8,1024]{3,2,1,0:T(8,128)(2,1)} collective-permute-done((bf16[8,2,8,1024]{3,2,1,0:T(8,128)(2,1)}, bf16[8,2,8,1024]{3,2,1,0:T(8,128)(2,1)}, u32[]{:S(2)}, u32[]{:S(2)}) %collective-permute-start.2) | collective-permute-done | bytes 262176 | tf_op jit(solution)/shard_map/ppermute | solution.py:24
  65.4 3.8 %shard_map.69 = f32[256,256]{1,0:T(8,128)S(1)} custom-call(f32[8,2,8,1024]{3,2,1,0:T(8,128)S(1)} %get-tuple-element.12.own_ref, bf16[8,2,8,1024]{3,2,1,0:T(8,128)(2,1)} %collective-permute-done.2.x_ref, f32[8,8,1]{2,1,0:T(8,128)S(1)} %copy.15.power_ref, f32[8,1024]{1,0:T(8,128)S(1)} %dynamic-slice_bitcast_fusion.1.twiddle_ref, ...), custom_call_target="tpu_custom_call" | custom-call | flops 805306368 | bytes 4194304 | tf_op jit(solution)/shard_map/pallas_call | solution.py:197
  69.2 0.0 copy-start.1
  69.2 0.7 copy-done.1
  69.9 0.0 all-to-all-done.2.refs_2_
  69.9 0.0 copy-start.8
  69.9 3.5 %all-to-all-start.3 = ((f32[4,1,64,256]{3,2,1,0:T(8,128)}), f32[4,1,64,256]{3,2,1,0:T(8,128)S(1)}, u32[]{:S(2)}, u32[]{:S(2)}) async-start(f32[4,1,64,256]{3,2,1,0:T(8,128)} %bitcast.19), calls=%async_computation.3 | async-start | bytes 524288 | tf_op jit(solution)/shard_map/all_to_all | solution.py:207
  73.4 0.0 copy-done.8
  73.4 0.1 copy.16.mask_ref
  73.5 5.9 %all-to-all-done.3.refs_3_ = f32[4,1,64,256]{3,2,1,0:T(8,128)S(1)} async-done(((f32[4,1,64,256]{3,2,1,0:T(8,128)}), f32[4,1,64,256]{3,2,1,0:T(8,128)S(1)}, u32[]{:S(2)}, u32[]{:S(2)}) %all-to-all-start.3) | async-done | bytes 262176 | tf_op jit(solution)/shard_map/all_to_all | solution.py:207
  79.4 1.4 %shard_map.70 = f32[8,4,8,256]{3,2,1,0:T(8,128)} custom-call(s32[8,4]{1,0:T(8,128)S(1)} %copy.16.mask_ref, f32[4,1,64,256]{3,2,1,0:T(8,128)S(1)} %all-to-all-done.refs_0_, f32[4,1,64,256]{3,2,1,0:T(8,128)S(1)} %all-to-all-done.1.refs_1_, f32[4,1,64,256]{3,2,1,0:T(8,128)S(1)} %all-to-all-done.2.refs_2_, f32[4,1,64,256]{3,2,1,0:T(8,128)S(1)} %all-to-all-done.3.refs_3_), custom_call_target="tpu_custom_call" | custom-call | tf_op jit(solution)/shard_map/pallas_call | solution.py:209
  (5 shorter events, 0.0 us)
Async XLA Ops:
  0.0 34.6 %collective-permute-start = (bf16[8,2,8,1024]{3,2,1,0:T(8,128)(2,1)}, bf16[8,2,8,1024]{3,2,1,0:T(8,128)(2,1)S(1)}, u32[]{:S(2)}, u32[]{:S(2)}) collective-permute-start(bf16[8,2,8,1024]{3,2,1,0:T(8,128)(2,1)} %x_ref.3), channel_id=1, source_target_pairs={{4,0},{8,4},{12,8},{5,1},{9,5},{13,9},{6,2},{10,6},{14,10},{7,3},{... | collective-permute-start | bytes 786440 | tf_op jit(solution)/shard_map/ppermute | solution.py:24
  1.3 1.0 %copy-start.2 = (bf16[8,2,8,1024]{3,2,1,0:T(8,128)(2,1)S(1)}, bf16[8,2,8,1024]{3,2,1,0:T(8,128)(2,1)}, u32[]{:S(2)}) copy-start(bf16[8,2,8,1024]{3,2,1,0:T(8,128)(2,1)} %x_ref.3) | copy-start | bytes 786436
  2.4 31.5 %copy-start.6 = (f32[2,2,32,256]{3,2,0,1:T(8,128)S(1)}, f32[2,2,32,256]{3,2,0,1:T(8,128)}, u32[]{:S(2)}) copy-start(f32[2,2,32,256]{3,2,0,1:T(8,128)} %constant.30.clone) | copy-start | bytes 393220
  2.4 31.5 %copy-start.4 = (f32[2,32,256]{2,1,0:T(8,128)S(1)}, f32[2,32,256]{2,1,0:T(8,128)}, u32[]{:S(2)}) copy-start(f32[2,32,256]{2,1,0:T(8,128)} %constant.31.clone.fine_ref) | copy-start | bytes 196612
  2.4 32.2 %copy-start.7 = (f32[8,2,1024]{2,0,1:T(8,128)S(1)}, f32[8,2,1024]{2,0,1:T(8,128)}, u32[]{:S(2)}) copy-start(f32[8,2,1024]{2,0,1:T(8,128)} %constant.32.clone) | copy-start | bytes 196612
  2.5 33.4 %copy-start.3 = (bf16[8,2,8,1024]{3,2,1,0:T(8,128)(2,1)S(1)}, bf16[8,2,8,1024]{3,2,1,0:T(8,128)(2,1)}, u32[]{:S(2)}) copy-start(bf16[8,2,8,1024]{3,2,1,0:T(8,128)(2,1)} %x_ref.3) | copy-start | bytes 786436
  34.6 19.0 %collective-permute-start.1 = (bf16[8,2,8,1024]{3,2,1,0:T(8,128)(2,1)S(1)}, bf16[8,2,8,1024]{3,2,1,0:T(8,128)(2,1)}, u32[]{:S(2)}, u32[]{:S(2)}) collective-permute-start(bf16[8,2,8,1024]{3,2,1,0:T(8,128)(2,1)S(1)} %collective-permute-done.x_ref), channel_id=1, source_target_pairs={{4,0},{8,4},{12,8},{5,1},{9,5},{13,9},{6,2},{10,6},{14,10},{7,3},{... | collective-permute-start | bytes 786440 | tf_op jit(solution)/shard_map/ppermute | solution.py:24
  35.9 0.7 copy-start.5
  40.8 9.4 %all-to-all-start = ((f32[4,1,64,256]{3,2,1,0:T(8,128)}), f32[4,1,64,256]{3,2,1,0:T(8,128)S(1)}, u32[]{:S(2)}, u32[]{:S(2)}) async-start(f32[4,1,64,256]{3,2,1,0:T(8,128)} %bitcast.3), calls=%async_computation | async-start | bytes 524288 | tf_op jit(solution)/shard_map/all_to_all | solution.py:207
  50.2 9.4 %all-to-all-start.1 = ((f32[4,1,64,256]{3,2,1,0:T(8,128)}), f32[4,1,64,256]{3,2,1,0:T(8,128)S(1)}, u32[]{:S(2)}, u32[]{:S(2)}) async-start(f32[4,1,64,256]{3,2,1,0:T(8,128)} %bitcast.5), calls=%async_computation.1 | async-start | bytes 524288 | tf_op jit(solution)/shard_map/all_to_all | solution.py:207
  53.6 11.8 %collective-permute-start.2 = (bf16[8,2,8,1024]{3,2,1,0:T(8,128)(2,1)}, bf16[8,2,8,1024]{3,2,1,0:T(8,128)(2,1)}, u32[]{:S(2)}, u32[]{:S(2)}) collective-permute-start(bf16[8,2,8,1024]{3,2,1,0:T(8,128)(2,1)} %collective-permute-done.1.x_ref), channel_id=1, source_target_pairs={{4,0},{8,4},{12,8},{5,1},{9,5},{13,9},{6,2},{10,6},{14,10},{7,3},{... | collective-permute-start | bytes 786440 | tf_op jit(solution)/shard_map/ppermute | solution.py:24
  58.8 0.7 copy-start
  59.6 10.3 %all-to-all-start.2 = ((f32[4,1,64,256]{3,2,1,0:T(8,128)}), f32[4,1,64,256]{3,2,1,0:T(8,128)S(1)}, u32[]{:S(2)}, u32[]{:S(2)}) async-start(f32[4,1,64,256]{3,2,1,0:T(8,128)} %bitcast.18), calls=%async_computation.2 | async-start | bytes 524288 | tf_op jit(solution)/shard_map/all_to_all | solution.py:207
  69.2 0.7 copy-start.1
  69.9 3.5 %copy-start.8 = (s32[8,4]{0,1:T(4,128)S(1)}, s32[8,4]{0,1:T(4,128)}, u32[]{:S(2)}) copy-start(s32[8,4]{0,1:T(4,128)} %param.8) | copy-start | bytes 388
  69.9 9.5 %all-to-all-start.3 = ((f32[4,1,64,256]{3,2,1,0:T(8,128)}), f32[4,1,64,256]{3,2,1,0:T(8,128)S(1)}, u32[]{:S(2)}, u32[]{:S(2)}) async-start(f32[4,1,64,256]{3,2,1,0:T(8,128)} %bitcast.19), calls=%async_computation.3 | async-start | bytes 524288 | tf_op jit(solution)/shard_map/all_to_all | solution.py:207

commit v2 on v1

v2 whole, which is shorter than its diff:
```python
import functools
import math

import jax
import jax.numpy as jnp
import numpy as np
from jax import lax
from jax.experimental import pallas as pl
from jax.experimental.pallas import tpu as pltpu
from jax.sharding import PartitionSpec as P

LAGS = 1024
F_LO = 60
NSAMP = 15000
EPS = 1e-06
LANES = 128
FINE = 32
CHUNK = 512
VMEM_LIMIT = 48 * 1024 * 1024


def from_behind(block, axis, distance):
    devices = range(lax.axis_size(axis))
    route = [(i - distance, i) for i in devices if i - distance in devices]
    return lax.ppermute(block, axis, route)


def phases(bins, lags):
    turns = np.remainder(np.asarray(bins, np.int64)[:, None] * np.asarray(lags, np.int64)[None, :], NSAMP)
    angle = turns * (2.0 * math.pi / NSAMP)
    return np.stack([np.cos(angle), np.sin(angle)]).astype(np.float32)


def split(value):
    high = value.astype(jnp.bfloat16)
    return high, (value - high.astype(jnp.float32)).astype(jnp.bfloat16)


def power_kernel(x_ref, out_ref):
    for w in range(x_ref.shape[0]):
        x = x_ref[w].astype(jnp.float32)
        x = x[0] * x[0] + x[1] * x[1]
        out_ref[w] = jnp.sum(x, axis=-1, keepdims=True)


def table_kernel(coarse_ref, fine_ref, high_ref, low_ref):
    f_dev = high_ref.shape[0] // 2
    per_chunk = CHUNK // FINE
    fine_cos, fine_sin = fine_ref[0], fine_ref[1]

    def body(a, carry):
        cos_a = coarse_ref[0, pl.ds(a, 1), :]
        sin_a = coarse_ref[1, pl.ds(a, 1), :]
        rows = pl.multiple_of((a + a // per_chunk * per_chunk) * FINE, FINE)
        high, low = split(cos_a * fine_cos - sin_a * fine_sin)
        high_ref[pl.ds(rows, FINE), :] = high
        low_ref[pl.ds(rows, FINE), :] = low
        high, low = split(-(cos_a * fine_sin + sin_a * fine_cos))
        high_ref[pl.ds(CHUNK + rows, FINE), :] = high
        low_ref[pl.ds(CHUNK + rows, FINE), :] = low
        return carry

    lax.fori_loop(0, f_dev // FINE, body, 0)


def whiten_kernel(n_bins, x_ref, power_ref, out_ref):
    for w in range(x_ref.shape[0]):
        scale = lax.rsqrt(power_ref[w] / n_bins + EPS)
        for part in range(2):
            out_ref[w, part] = (x_ref[w, part].astype(jnp.float32) * scale).astype(jnp.bfloat16)


def cross_tile(own_ref, partner_ref, lanes):
    w_dev, _, ch, _ = own_ref.shape
    real = [None] * ch
    imag = [None] * ch
    for w in range(w_dev):
        partner_re = partner_ref[w, 0, :, lanes].astype(jnp.float32)
        partner_im = partner_ref[w, 1, :, lanes].astype(jnp.float32)
        for i in range(ch):
            own_re = own_ref[w, 0, i:i + 1, lanes]
            own_im = own_ref[w, 1, i:i + 1, lanes]
            re = own_re * partner_re + own_im * partner_im
            im = own_im * partner_re - own_re * partner_im
            real[i] = re if w == 0 else real[i] + re
            imag[i] = im if w == 0 else imag[i] + im
    return real, imag


def pairs_kernel(n_partners, keep_ref, base_ref, *refs):
    partner_refs = refs[:n_partners]
    twiddle_ref, high_ref, low_ref, out_ref, own_ref, rows_high, rows_low = refs[n_partners:]
    w_dev, _, ch, f_dev = base_ref.shape
    groups = out_ref.shape[0]
    width = out_ref.shape[-1]
    depth = 2 * CHUNK
    for w in range(w_dev):
        kept = keep_ref[w].astype(jnp.float32)
        for part in range(2):
            own_ref[w, part] = base_ref[w, part].astype(jnp.float32) * kept
    dot = functools.partial(jnp.dot, preferred_element_type=jnp.float32)
    for k, partner_ref in enumerate(partner_refs):
        total = None
        for chunk in range(f_dev // CHUNK):
            for tile in range(CHUNK // LANES):
                lanes = slice(chunk * CHUNK + tile * LANES, chunk * CHUNK + (tile + 1) * LANES)
                to_re = slice(tile * LANES, (tile + 1) * LANES)
                to_im = slice(CHUNK + tile * LANES, CHUNK + (tile + 1) * LANES)
                real, imag = cross_tile(own_ref, partner_ref, lanes)
                for q in range(groups):
                    cos_q = twiddle_ref[q:q + 1, lanes]
                    sin_q = twiddle_ref[groups + q:groups + q + 1, lanes]
                    for i in range(0, ch, 2):
                        rows = slice((q * ch + i) * ch, (q * ch + i + 2) * ch)
                        re = jnp.concatenate(real[i:i + 2], axis=0)
                        im = jnp.concatenate(imag[i:i + 2], axis=0)
                        high, low = split(re * cos_q - im * sin_q)
                        rows_high[k, chunk, rows, to_re] = high
                        rows_low[k, chunk, rows, to_re] = low
                        high, low = split(re * sin_q + im * cos_q)
                        rows_high[k, chunk, rows, to_im] = high
                        rows_low[k, chunk, rows, to_im] = low
            table = slice(chunk * depth, (chunk + 1) * depth)
            part = (dot(rows_high[k, chunk], high_ref[table])
                    + (dot(rows_low[k, chunk], high_ref[table]) + dot(rows_high[k, chunk], low_ref[table])))
            total = part if total is None else total + part
        out_ref[:, k] = total.reshape(groups, ch * ch, width)


def combine_kernel(scale, mask_ref, *refs):
    out_ref = refs[-1]
    ch, offsets = out_ref.shape[:2]
    start = 0
    for ref in refs[:-1]:
        for k in range(ref.shape[1]):
            total = ref[0, k]
            for p in range(1, ref.shape[0]):
                total = total + ref[p, k]
            for i in range(ch):
                factor = mask_ref[i, start + k].astype(jnp.float32) * scale
                out_ref[i, start + k] = total[i * ch:(i + 1) * ch] * factor
        start += ref.shape[1]


VMEM = pl.BlockSpec(memory_space=pltpu.VMEM)
SMEM = pl.BlockSpec(memory_space=pltpu.SMEM)


def local(spectra, keep, pair_mask):
    w_dev, _, ch, f_dev = spectra.shape
    reach = pair_mask.shape[1] - 1
    n_win, n_freq = (lax.axis_size(a) for a in ("win", "freq"))
    groups = n_win * n_freq
    width = LAGS // groups
    n_bins = f_dev * n_freq
    params = pltpu.CompilerParams(vmem_limit_bytes=VMEM_LIMIT)
    freq = lax.axis_index("freq")

    power = pl.pallas_call(
        power_kernel,
        out_shape=jax.ShapeDtypeStruct((w_dev, ch, 1), jnp.float32),
        in_specs=[VMEM], out_specs=VMEM, compiler_params=params,
    )(spectra)
    power = lax.psum(power, "freq")
    white = pl.pallas_call(
        functools.partial(whiten_kernel, n_bins),
        out_shape=jax.ShapeDtypeStruct(spectra.shape, jnp.bfloat16),
        in_specs=[VMEM] * 2, out_specs=VMEM, compiler_params=params,
    )(spectra, power)
    blocks = [white]
    for step in range(reach):
        blocks.append(from_behind(blocks[-1], "chan", -1))

    coarse = phases(np.arange(0, n_bins, FINE), np.arange(width))
    coarse = coarse.reshape(2, n_freq, f_dev // FINE, width)
    coarse = lax.dynamic_index_in_dim(jnp.asarray(coarse), freq, 1, keepdims=False)
    fine = jnp.asarray(phases(F_LO + np.arange(FINE), np.arange(width)))
    high, low = pl.pallas_call(
        table_kernel,
        out_shape=[jax.ShapeDtypeStruct((2 * f_dev, width), jnp.bfloat16)] * 2,
        in_specs=[VMEM] * 2, out_specs=[VMEM] * 2, compiler_params=params,
    )(coarse, fine)
    twiddle = phases(F_LO + np.arange(n_bins), np.arange(groups) * width - LAGS // 2)
    twiddle = np.moveaxis(twiddle, 1, 2).reshape(2 * groups, n_freq, f_dev)
    twiddle = lax.dynamic_index_in_dim(jnp.asarray(twiddle), freq, 1, keepdims=False)

    rows = groups * ch * ch
    depth = 2 * CHUNK

    def pairs(base, partners):
        n = len(partners)
        flops = n * 6 * rows * 2 * f_dev * width
        return pl.pallas_call(
            functools.partial(pairs_kernel, n),
            out_shape=jax.ShapeDtypeStruct((groups, n, ch * ch, width), jnp.float32),
            in_specs=[SMEM] + [VMEM] * (n + 4), out_specs=VMEM,
            scratch_shapes=[pltpu.VMEM(base.shape, jnp.float32)]
            + [pltpu.VMEM((n, f_dev // CHUNK, rows, depth), jnp.bfloat16)] * 2,
            compiler_params=params,
            cost_estimate=pl.CostEstimate(flops=flops, bytes_accessed=2 ** 22, transcendentals=0),
        )(keep, base, *partners, twiddle, high, low)

    parts = [pairs(white, blocks[:2])] + [pairs(white, [block]) for block in blocks[2:]]

    received = []
    for part in parts:
        received.append(lax.all_to_all(part, ("win", "freq"), 0, 0, tiled=True))
    scale = 1.0 / math.sqrt(w_dev * n_win * n_bins)
    return pl.pallas_call(
        functools.partial(combine_kernel, scale),
        out_shape=jax.ShapeDtypeStruct((ch, reach + 1, ch, width), jnp.float32),
        in_specs=[SMEM] + [VMEM] * len(received), out_specs=VMEM, compiler_params=params,
    )(pair_mask, *received)


def solution(mesh):
    in_specs = (
        P("win", None, ("fibre", "chan"), "freq"),
        P(("fibre", "win")),
        P(("fibre", "chan"), None),
    )
    out_specs = P(("fibre", "chan"), None, None, ("win", "freq"))
    return jax.shard_map(local, mesh=mesh, in_specs=in_specs, out_specs=out_specs, check_vma=False)
```

time: 81.4 us -> 56.4 us (0.69)
  blocking collectives: 31.2 us -> 3.67 us
  waiting for transfers between devices: 10.6 us -> 21.1 us
  starting transfers between devices: 17.6 us -> 14.1 us
  Pallas kernels: 17.5 us -> 14.1 us
  local copies, waits for them, and re-layouts: 3.59 us -> 2.7 us
    psum x1, blocking collectives: 31.2 us -> 3.67 us  [local(): power = lax.psum(power, 'freq')]
    ppermute x3, waiting for transfers between devices: 2.26 us -> 8.46 us  [from_behind(): return lax.ppermute(block, axis, route)]
    all_to_all x4 -> x3, waiting for transfers between devices: 8.33 us -> 12.6 us  [local(): received.append(lax.all_to_all(part, ('win', 'freq'), 0, 0, tiled=True))]
    all_to_all x4 -> x3, starting transfers between devices: 13.8 us -> 10.3 us  [local(): received.append(lax.all_to_all(part, ('win', 'freq'), 0, 0, tiled=True))]
    pallas_call x4, Pallas kernels: 15.3 us -> 12 us  [the longest x3 11.9 us: pairs(): pl.pallas_call(functools.partial(pairs_kernel, n), out_shape=jax.ShapeDty...]
    unnamed x19 -> x15, local copies, waits for them, and re-layouts: 3.07 us -> 2.69 us
  transfers between devices with their start and end apart: 7 -> 6, of which waited for: 4 -> 4; matrix products, arithmetic and copies ran while one was open for 1% -> 0% of each run, Pallas kernels for 20% -> 22%
where the time goes in v2:
time: 56.4 us; the launch traced here: 55.9 us
  waiting for transfers between devices  21.1 us (37%)
  Pallas kernels  14.1 us (25%)
  starting transfers between devices  14.1 us (25%)
  blocking collectives  3.67 us (7%)
  local copies, waits for them, and re-layouts  2.7 us (5%)
    all_to_all x3, waiting for transfers between devices, local(): received.append(lax.all_to_all(part, ('win', 'freq'), 0, 0, tiled=True))  12.6 us
    pallas_call x3, Pallas kernels, pairs(): pl.pallas_call(functools.partial(pairs_kernel, n), out_shape=jax.ShapeDty...  11.9 us
    all_to_all x3, starting transfers between devices, local(): received.append(lax.all_to_all(part, ('win', 'freq'), 0, 0, tiled=True))  10.3 us
    ppermute x3, waiting for transfers between devices, from_behind(): return lax.ppermute(block, axis, route)  8.46 us
    ppermute x3, starting transfers between devices, from_behind(): return lax.ppermute(block, axis, route)  3.86 us
    psum x1, blocking collectives, local(): power = lax.psum(power, 'freq')  3.67 us
    unnamed x15, local copies, waits for them, and re-layouts  2.69 us
    pallas_call x1, Pallas kernels, local(): pl.pallas_call(functools.partial(combine_kernel, scale), out_shape=jax.Sh...  1.35 us
  transfers between devices with their start and end apart: 6, of which 4 were waited for; matrix products, arithmetic and copies ran while one was open for 0% of the time, Pallas kernels for 22%

profile of v2, /device:TPU:0, one launch (start us, length us, event | category | flops | bytes accessed | tf_op | source)
XLA Modules:
  0.0 55.9 jit_solution(17903446080879335995)
XLA Ops:
  0.0 0.0 copy-start
  0.0 0.9 %copy-done = bf16[8,2,8,1024]{3,2,1,0:T(8,128)(2,1)S(1)} copy-done((bf16[8,2,8,1024]{3,2,1,0:T(8,128)(2,1)S(1)}, bf16[8,2,8,1024]{3,2,1,0:T(8,128)(2,1)}, u32[]{:S(2)}) %copy-start) | copy-done | bytes 262168
  1.0 0.0 copy-start.1
  1.0 0.1 shard_map.64
  1.1 3.7 %psum.7.power_ref = f32[8,8,1]{2,1,0:T(8,128)S(1)} all-reduce(f32[8,8,1]{2,1,0:T(8,128)S(1)} %shard_map.64), channel_id=1, replica_groups=mesh['fibre'=2,'chan'=4,'win'=2,'freq'=2] {'freq'}, use_global_device_ids=true, to_apply=%region_0.0 | all-reduce | flops 64 | bytes 512 | tf_op jit(solution)/shard_map/psum | solution.py:164
  4.8 0.0 copy-done.1
  4.8 0.0 copy-start.4
  4.8 0.1 shard_map.65.base_ref.refs_0_
  4.9 1.3 %collective-permute-start = (bf16[8,2,8,1024]{3,2,1,0:T(8,128)(2,1)S(1)}, bf16[8,2,8,1024]{3,2,1,0:T(8,128)(2,1)S(1)}, u32[]{:S(2)}, u32[]{:S(2)}) collective-permute-start(bf16[8,2,8,1024]{3,2,1,0:T(8,128)(2,1)S(1)} %shard_map.65.base_ref.refs_0_), channel_id=1, source_target_pairs={{4,0},{8,4},{12,8},{5,1},{9,5},{13,9},{6,2},{10,6},{14,10},{7,3},{... | collective-permute-start | bytes 786440 | tf_op jit(solution)/shard_map/ppermute | solution.py:25
  6.2 0.0 copy-done.4
  6.2 0.0 copy-start.2
  6.3 0.8 %copy-done.2 = f32[2,32,256]{2,1,0:T(8,128)S(1)} copy-done((f32[2,32,256]{2,1,0:T(8,128)S(1)}, f32[2,32,256]{2,1,0:T(8,128)}, u32[]{:S(2)}) %copy-start.2) | copy-done | bytes 65560
  7.1 0.0 copy-start.5
  7.1 0.7 %shard_map.66 = (bf16[2048,256]{1,0:T(8,128)(2,1)S(1)}, bf16[2048,256]{1,0:T(8,128)(2,1)S(1)}) custom-call(f32[2,32,256]{2,1,0:T(8,128)S(1)} %dynamic-slice_bitcast_fusion.coarse_ref, f32[2,32,256]{2,1,0:T(8,128)S(1)} %copy-done.2), custom_call_target="tpu_custom_call" | custom-call | tf_op jit(solution)/shard_map/pallas_call | solution.py:178
  7.7 0.2 copy-done.5
  7.9 8.5 %collective-permute-done.refs_1_ = bf16[8,2,8,1024]{3,2,1,0:T(8,128)(2,1)S(1)} collective-permute-done((bf16[8,2,8,1024]{3,2,1,0:T(8,128)(2,1)S(1)}, bf16[8,2,8,1024]{3,2,1,0:T(8,128)(2,1)S(1)}, u32[]{:S(2)}, u32[]{:S(2)}) %collective-permute-start) | collective-permute-done | bytes 262176 | tf_op jit(solution)/shard_map/ppermute | solution.py:25
  16.4 1.3 %collective-permute-start.1 = (bf16[8,2,8,1024]{3,2,1,0:T(8,128)(2,1)S(1)}, bf16[8,2,8,1024]{3,2,1,0:T(8,128)(2,1)S(1)}, u32[]{:S(2)}, u32[]{:S(2)}) collective-permute-start(bf16[8,2,8,1024]{3,2,1,0:T(8,128)(2,1)S(1)} %collective-permute-done.refs_1_), channel_id=1, source_target_pairs={{4,0},{8,4},{12,8},{5,1},{9,5},{13,9},{6,2},{10,6},{14,10},{7,3},{... | collective-permute-start | bytes 786440 | tf_op jit(solution)/shard_map/ppermute | solution.py:25
  17.7 0.0 copy-start.3
  17.7 0.6 %copy-done.3 = s32[8]{0:T(128)S(1)} copy-done((s32[8]{0:T(128)S(1)}, s32[8]{0:T(128)}, u32[]{:S(2)}) %copy-start.3) | copy-done | bytes 56
  18.3 5.1 %shard_map.67 = f32[4,2,64,256]{3,2,1,0:T(8,128)} custom-call(s32[8]{0:T(128)S(1)} %copy-done.3, bf16[8,2,8,1024]{3,2,1,0:T(8,128)(2,1)S(1)} %shard_map.65.base_ref.refs_0_, bf16[8,2,8,1024]{3,2,1,0:T(8,128)(2,1)S(1)} %shard_map.65.base_ref.refs_0_, bf16[8,2,8,1024]{3,2,1,0:T(8,128)(2,1)S(1)} %collective-permute-done.refs_1_, ...), custom_call_target="tpu_custom_call" | custom-call | flops 1610612736 | bytes 4194304 | tf_op jit(solution)/shard_map/pallas_call | solution.py:193
  23.4 3.5 %all-to-all-start = ((f32[4,2,64,256]{3,2,1,0:T(8,128)}), f32[4,2,64,256]{3,2,1,0:T(8,128)S(1)}, u32[]{:S(2)}, u32[]{:S(2)}) async-start(f32[4,2,64,256]{3,2,1,0:T(8,128)} %shard_map.67), calls=%async_computation | async-start | bytes 1048576 | tf_op jit(solution)/shard_map/all_to_all | solution.py:207
  26.9 0.0 collective-permute-done.1.refs_0_
  26.9 1.3 %collective-permute-start.2 = (bf16[8,2,8,1024]{3,2,1,0:T(8,128)(2,1)S(1)}, bf16[8,2,8,1024]{3,2,1,0:T(8,128)(2,1)}, u32[]{:S(2)}, u32[]{:S(2)}) collective-permute-start(bf16[8,2,8,1024]{3,2,1,0:T(8,128)(2,1)S(1)} %collective-permute-done.1.refs_0_), channel_id=1, source_target_pairs={{4,0},{8,4},{12,8},{5,1},{9,5},{13,9},{6,2},{10,6},{14,10},{7,3},{... | collective-permute-start | bytes 786440 | tf_op jit(solution)/shard_map/ppermute | solution.py:25
  28.2 3.2 %shard_map.68 = f32[4,1,64,256]{3,2,1,0:T(8,128)} custom-call(s32[8]{0:T(128)S(1)} %copy-done.3, bf16[8,2,8,1024]{3,2,1,0:T(8,128)(2,1)S(1)} %shard_map.65.base_ref.refs_0_, bf16[8,2,8,1024]{3,2,1,0:T(8,128)(2,1)S(1)} %collective-permute-done.1.refs_0_, f32[8,1024]{1,0:T(8,128)S(1)} %dynamic-slice_bitcast_fusion.1.refs_2_.refs_1_, ...), custom_call_target="tpu_custom_call" | custom-call | flops 805306368 | bytes 4194304 | tf_op jit(solution)/shard_map/pallas_call | solution.py:193
  31.4 4.3 %all-to-all-done.refs_0_ = f32[4,2,64,256]{3,2,1,0:T(8,128)S(1)} async-done(((f32[4,2,64,256]{3,2,1,0:T(8,128)}), f32[4,2,64,256]{3,2,1,0:T(8,128)S(1)}, u32[]{:S(2)}, u32[]{:S(2)}) %all-to-all-start) | async-done | bytes 524320 | tf_op jit(solution)/shard_map/all_to_all | solution.py:207
  35.7 3.4 %all-to-all-start.1 = ((f32[4,1,64,256]{3,2,1,0:T(8,128)}), f32[4,1,64,256]{3,2,1,0:T(8,128)S(1)}, u32[]{:S(2)}, u32[]{:S(2)}) async-start(f32[4,1,64,256]{3,2,1,0:T(8,128)} %shard_map.68), calls=%async_computation.1 | async-start | bytes 524288 | tf_op jit(solution)/shard_map/all_to_all | solution.py:207
  39.1 0.0 collective-permute-done.2.refs_0_
  39.1 3.6 %shard_map.69 = f32[4,1,64,256]{3,2,1,0:T(8,128)} custom-call(s32[8]{0:T(128)S(1)} %copy-done.3, bf16[8,2,8,1024]{3,2,1,0:T(8,128)(2,1)S(1)} %shard_map.65.base_ref.refs_0_, bf16[8,2,8,1024]{3,2,1,0:T(8,128)(2,1)} %collective-permute-done.2.refs_0_, f32[8,1024]{1,0:T(8,128)S(1)} %dynamic-slice_bitcast_fusion.1.refs_2_.refs_1_, ...), custom_call_target="tpu_custom_call" | custom-call | flops 805306368 | bytes 4194304 | tf_op jit(solution)/shard_map/pallas_call | solution.py:193
  42.7 0.0 copy-start.6
  42.7 2.4 %all-to-all-done.1.refs_1_ = f32[4,1,64,256]{3,2,1,0:T(8,128)S(1)} async-done(((f32[4,1,64,256]{3,2,1,0:T(8,128)}), f32[4,1,64,256]{3,2,1,0:T(8,128)S(1)}, u32[]{:S(2)}, u32[]{:S(2)}) %all-to-all-start.1) | async-done | bytes 262176 | tf_op jit(solution)/shard_map/all_to_all | solution.py:207
  45.1 3.4 %all-to-all-start.2 = ((f32[4,1,64,256]{3,2,1,0:T(8,128)}), f32[4,1,64,256]{3,2,1,0:T(8,128)S(1)}, u32[]{:S(2)}, u32[]{:S(2)}) async-start(f32[4,1,64,256]{3,2,1,0:T(8,128)} %shard_map.69), calls=%async_computation.2 | async-start | bytes 524288 | tf_op jit(solution)/shard_map/all_to_all | solution.py:207
  48.5 0.0 copy-done.6
  48.5 0.1 copy.7.mask_ref
  48.6 5.9 %all-to-all-done.2.refs_2_ = f32[4,1,64,256]{3,2,1,0:T(8,128)S(1)} async-done(((f32[4,1,64,256]{3,2,1,0:T(8,128)}), f32[4,1,64,256]{3,2,1,0:T(8,128)S(1)}, u32[]{:S(2)}, u32[]{:S(2)}) %all-to-all-start.2) | async-done | bytes 262176 | tf_op jit(solution)/shard_map/all_to_all | solution.py:207
  54.5 1.4 %shard_map.70 = f32[8,4,8,256]{3,2,1,0:T(8,128)} custom-call(s32[8,4]{1,0:T(8,128)S(1)} %copy.7.mask_ref, f32[4,2,64,256]{3,2,1,0:T(8,128)S(1)} %all-to-all-done.refs_0_, f32[4,1,64,256]{3,2,1,0:T(8,128)S(1)} %all-to-all-done.1.refs_1_, f32[4,1,64,256]{3,2,1,0:T(8,128)S(1)} %all-to-all-done.2.refs_2_), custom_call_target="tpu_custom_call" | custom-call | tf_op jit(solution)/shard_map/pallas_call | solution.py:209
  (2 shorter events, 0.0 us)
Async XLA Ops:
  0.0 0.9 %copy-start = (bf16[8,2,8,1024]{3,2,1,0:T(8,128)(2,1)S(1)}, bf16[8,2,8,1024]{3,2,1,0:T(8,128)(2,1)}, u32[]{:S(2)}) copy-start(bf16[8,2,8,1024]{3,2,1,0:T(8,128)(2,1)} %x_ref.3) | copy-start | bytes 786436
  1.0 3.8 %copy-start.1 = (bf16[8,2,8,1024]{3,2,1,0:T(8,128)(2,1)S(1)}, bf16[8,2,8,1024]{3,2,1,0:T(8,128)(2,1)}, u32[]{:S(2)}) copy-start(bf16[8,2,8,1024]{3,2,1,0:T(8,128)(2,1)} %x_ref.3) | copy-start | bytes 786436
  4.8 1.4 %copy-start.4 = (f32[2,2,32,256]{3,2,0,1:T(8,128)S(1)}, f32[2,2,32,256]{3,2,0,1:T(8,128)}, u32[]{:S(2)}) copy-start(f32[2,2,32,256]{3,2,0,1:T(8,128)} %constant.20.clone) | copy-start | bytes 393220
  4.9 11.5 %collective-permute-start = (bf16[8,2,8,1024]{3,2,1,0:T(8,128)(2,1)S(1)}, bf16[8,2,8,1024]{3,2,1,0:T(8,128)(2,1)S(1)}, u32[]{:S(2)}, u32[]{:S(2)}) collective-permute-start(bf16[8,2,8,1024]{3,2,1,0:T(8,128)(2,1)S(1)} %shard_map.65.base_ref.refs_0_), channel_id=1, source_target_pairs={{4,0},{8,4},{12,8},{5,1},{9,5},{13,9},{6,2},{10,6},{14,10},{7,3},{... | collective-permute-start | bytes 786440 | tf_op jit(solution)/shard_map/ppermute | solution.py:25
  6.2 0.8 %copy-start.2 = (f32[2,32,256]{2,1,0:T(8,128)S(1)}, f32[2,32,256]{2,1,0:T(8,128)}, u32[]{:S(2)}) copy-start(f32[2,32,256]{2,1,0:T(8,128)} %constant.21.clone.fine_ref) | copy-start | bytes 196612
  7.1 0.8 %copy-start.5 = (f32[8,2,1024]{2,0,1:T(8,128)S(1)}, f32[8,2,1024]{2,0,1:T(8,128)}, u32[]{:S(2)}) copy-start(f32[8,2,1024]{2,0,1:T(8,128)} %constant.22.clone) | copy-start | bytes 196612
  16.4 10.5 %collective-permute-start.1 = (bf16[8,2,8,1024]{3,2,1,0:T(8,128)(2,1)S(1)}, bf16[8,2,8,1024]{3,2,1,0:T(8,128)(2,1)S(1)}, u32[]{:S(2)}, u32[]{:S(2)}) collective-permute-start(bf16[8,2,8,1024]{3,2,1,0:T(8,128)(2,1)S(1)} %collective-permute-done.refs_1_), channel_id=1, source_target_pairs={{4,0},{8,4},{12,8},{5,1},{9,5},{13,9},{6,2},{10,6},{14,10},{7,3},{... | collective-permute-start | bytes 786440 | tf_op jit(solution)/shard_map/ppermute | solution.py:25
  17.7 0.7 %copy-start.3 = (s32[8]{0:T(128)S(1)}, s32[8]{0:T(128)}, u32[]{:S(2)}) copy-start(s32[8]{0:T(128)} %keep_ref.5) | copy-start | bytes 100
  23.4 12.3 %all-to-all-start = ((f32[4,2,64,256]{3,2,1,0:T(8,128)}), f32[4,2,64,256]{3,2,1,0:T(8,128)S(1)}, u32[]{:S(2)}, u32[]{:S(2)}) async-start(f32[4,2,64,256]{3,2,1,0:T(8,128)} %shard_map.67), calls=%async_computation | async-start | bytes 1048576 | tf_op jit(solution)/shard_map/all_to_all | solution.py:207
  26.9 12.2 %collective-permute-start.2 = (bf16[8,2,8,1024]{3,2,1,0:T(8,128)(2,1)S(1)}, bf16[8,2,8,1024]{3,2,1,0:T(8,128)(2,1)}, u32[]{:S(2)}, u32[]{:S(2)}) collective-permute-start(bf16[8,2,8,1024]{3,2,1,0:T(8,128)(2,1)S(1)} %collective-permute-done.1.refs_0_), channel_id=1, source_target_pairs={{4,0},{8,4},{12,8},{5,1},{9,5},{13,9},{6,2},{10,6},{14,10},{7,3},{... | collective-permute-start | bytes 786440 | tf_op jit(solution)/shard_map/ppermute | solution.py:25
  35.7 9.4 %all-to-all-start.1 = ((f32[4,1,64,256]{3,2,1,0:T(8,128)}), f32[4,1,64,256]{3,2,1,0:T(8,128)S(1)}, u32[]{:S(2)}, u32[]{:S(2)}) async-start(f32[4,1,64,256]{3,2,1,0:T(8,128)} %shard_map.68), calls=%async_computation.1 | async-start | bytes 524288 | tf_op jit(solution)/shard_map/all_to_all | solution.py:207
  42.7 5.8 %copy-start.6 = (s32[8,4]{0,1:T(4,128)S(1)}, s32[8,4]{0,1:T(4,128)}, u32[]{:S(2)}) copy-start(s32[8,4]{0,1:T(4,128)} %param.8) | copy-start | bytes 388
  45.1 9.4 %all-to-all-start.2 = ((f32[4,1,64,256]{3,2,1,0:T(8,128)}), f32[4,1,64,256]{3,2,1,0:T(8,128)S(1)}, u32[]{:S(2)}, u32[]{:S(2)}) async-start(f32[4,1,64,256]{3,2,1,0:T(8,128)} %shard_map.69), calls=%async_computation.2 | async-start | bytes 524288 | tf_op jit(solution)/shard_map/all_to_all | solution.py:207

commit v3 on v2

--- a/solution.py
+++ b/solution.py
@@ -127,19 +127,17 @@
         out_ref[:, k] = total.reshape(groups, ch * ch, width)
 
 
-def combine_kernel(scale, mask_ref, *refs):
+def combine_kernel(scale, order, mask_ref, *refs):
     out_ref = refs[-1]
-    ch, offsets = out_ref.shape[:2]
-    start = 0
-    for ref in refs[:-1]:
-        for k in range(ref.shape[1]):
-            total = ref[0, k]
-            for p in range(1, ref.shape[0]):
-                total = total + ref[p, k]
-            for i in range(ch):
-                factor = mask_ref[i, start + k].astype(jnp.float32) * scale
-                out_ref[i, start + k] = total[i * ch:(i + 1) * ch] * factor
-        start += ref.shape[1]
+    ch = out_ref.shape[0]
+    places = [(ref, n) for ref in refs[:-1] for n in range(ref.shape[1])]
+    for k, (ref, n) in zip(order, places):
+        total = ref[0, n]
+        for p in range(1, ref.shape[0]):
+            total = total + ref[p, n]
+        for i in range(ch):
+            factor = mask_ref[i, k].astype(jnp.float32) * scale
+            out_ref[i, k] = total[i * ch:(i + 1) * ch] * factor
 
 
 VMEM = pl.BlockSpec(memory_space=pltpu.VMEM)
@@ -156,20 +154,23 @@
     params = pltpu.CompilerParams(vmem_limit_bytes=VMEM_LIMIT)
     freq = lax.axis_index("freq")
 
+    def whiten(block, power):
+        return pl.pallas_call(
+            functools.partial(whiten_kernel, n_bins),
+            out_shape=jax.ShapeDtypeStruct(block.shape, jnp.bfloat16),
+            in_specs=[VMEM] * 2, out_specs=VMEM, compiler_params=params,
+        )(block, power)
+
+    far = from_behind(spectra, "chan", -reach)
     power = pl.pallas_call(
         power_kernel,
         out_shape=jax.ShapeDtypeStruct((w_dev, ch, 1), jnp.float32),
         in_specs=[VMEM], out_specs=VMEM, compiler_params=params,
     )(spectra)
     power = lax.psum(power, "freq")
-    white = pl.pallas_call(
-        functools.partial(whiten_kernel, n_bins),
-        out_shape=jax.ShapeDtypeStruct(spectra.shape, jnp.bfloat16),
-        in_specs=[VMEM] * 2, out_specs=VMEM, compiler_params=params,
-    )(spectra, power)
-    blocks = [white]
-    for step in range(reach):
-        blocks.append(from_behind(blocks[-1], "chan", -1))
+    white = whiten(spectra, power)
+    far_power = from_behind(power, "chan", -reach)
+    near = {k: from_behind(white, "chan", -k) for k in range(reach - 1, 0, -1)}
 
     coarse = phases(np.arange(0, n_bins, FINE), np.arange(width))
     coarse = coarse.reshape(2, n_freq, f_dev // FINE, width)
@@ -200,14 +201,15 @@
             cost_estimate=pl.CostEstimate(flops=flops, bytes_accessed=2 ** 22, transcendentals=0),
         )(keep, base, *partners, twiddle, high, low)
 
-    parts = [pairs(white, blocks[:2])] + [pairs(white, [block]) for block in blocks[2:]]
-
-    received = []
-    for part in parts:
-        received.append(lax.all_to_all(part, ("win", "freq"), 0, 0, tiled=True))
+    parts = [pairs(white, [white, whiten(far, far_power)])]
+    order = [0, reach]
+    for k, block in near.items():
+        parts.append(pairs(white, [block]))
+        order.append(k)
+    received = [lax.all_to_all(part, ("win", "freq"), 0, 0, tiled=True) for part in parts]
     scale = 1.0 / math.sqrt(w_dev * n_win * n_bins)
     return pl.pallas_call(
-        functools.partial(combine_kernel, scale),
+        functools.partial(combine_kernel, scale, order),
         out_shape=jax.ShapeDtypeStruct((ch, reach + 1, ch, width), jnp.float32),
         in_specs=[SMEM] + [VMEM] * len(received), out_specs=VMEM, compiler_params=params,
     )(pair_mask, *received)

time: 56.4 us -> 68.2 us (1.21)
  waiting for transfers between devices: 21.1 us -> 31.7 us
  starting transfers between devices: 14.1 us -> 15.6 us
    ppermute x3 -> x4, waiting for transfers between devices: 8.46 us -> 22.9 us  [from_behind(): return lax.ppermute(block, axis, route)]
    all_to_all x3, waiting for transfers between devices: 12.6 us -> 8.72 us  [local(): lax.all_to_all(part, ('win', 'freq'), 0, 0, tiled=True)]
    ppermute x3 -> x4, starting transfers between devices: 3.86 us -> 5.17 us  [from_behind(): return lax.ppermute(block, axis, route)]
    pallas_call x2 -> x3, Pallas kernels: 1.47 us -> 1.59 us  [the longest x1 1.35 us: local(): pl.pallas_call(functools.partial(combine_kernel, scale, order), out_shape...]
  transfers between devices with their start and end apart: 6 -> 7, of which waited for: 4 -> 4; matrix products, arithmetic and copies ran while one was open for 0% -> 0% of each run, Pallas kernels for 22% -> 18%
where the time goes in v3:
time: 68.2 us; the launch traced here: 67.6 us
  waiting for transfers between devices  31.7 us (46%)
  starting transfers between devices  15.6 us (23%)
  Pallas kernels  13.8 us (20%)
  blocking collectives  3.67 us (5%)
  local copies, waits for them, and re-layouts  2.71 us (4%)
    ppermute x4, waiting for transfers between devices, from_behind(): return lax.ppermute(block, axis, route)  22.9 us
    pallas_call x3, Pallas kernels, pairs(): pl.pallas_call(functools.partial(pairs_kernel, n), out_shape=jax.ShapeDty...  11.4 us
    all_to_all x3, starting transfers between devices, local(): lax.all_to_all(part, ('win', 'freq'), 0, 0, tiled=True)  10.4 us
    all_to_all x3, waiting for transfers between devices, local(): lax.all_to_all(part, ('win', 'freq'), 0, 0, tiled=True)  8.72 us
    ppermute x4, starting transfers between devices, from_behind(): return lax.ppermute(block, axis, route)  5.17 us
    psum x1, blocking collectives, local(): power = lax.psum(power, 'freq')  3.67 us
    unnamed x15, local copies, waits for them, and re-layouts  2.69 us
  transfers between devices with their start and end apart: 7, of which 4 were waited for; matrix products, arithmetic and copies ran while one was open for 0% of the time, Pallas kernels for 18%

profile of v3, /device:TPU:0, one launch (start us, length us, event | category | flops | bytes accessed | tf_op | source)
XLA Modules:
  0.0 67.6 jit_solution(16227933794055020670)
XLA Ops:
  0.0 0.0 copy-start
  0.0 0.9 %copy-done = bf16[8,2,8,1024]{3,2,1,0:T(8,128)(2,1)S(1)} copy-done((bf16[8,2,8,1024]{3,2,1,0:T(8,128)(2,1)S(1)}, bf16[8,2,8,1024]{3,2,1,0:T(8,128)(2,1)}, u32[]{:S(2)}) %copy-start) | copy-done | bytes 262168
  1.0 0.0 copy-start.1
  1.0 0.1 shard_map.64
  1.1 3.7 %psum.7.power_ref = f32[8,8,1]{2,1,0:T(8,128)S(1)} all-reduce(f32[8,8,1]{2,1,0:T(8,128)S(1)} %shard_map.64), channel_id=1, replica_groups=mesh['fibre'=2,'chan'=4,'win'=2,'freq'=2] {'freq'}, use_global_device_ids=true, to_apply=%region_0.0 | all-reduce | flops 64 | bytes 512 | tf_op jit(solution)/shard_map/psum | solution.py:170
  4.8 0.0 copy-done.1
  4.8 0.0 copy-start.4
  4.8 0.1 shard_map.65.base_ref.refs_0_
  4.9 1.3 %collective-permute-start.3 = (bf16[8,2,8,1024]{3,2,1,0:T(8,128)(2,1)S(1)}, bf16[8,2,8,1024]{3,2,1,0:T(8,128)(2,1)S(1)}, u32[]{:S(2)}, u32[]{:S(2)}) collective-permute-start(bf16[8,2,8,1024]{3,2,1,0:T(8,128)(2,1)S(1)} %shard_map.65.base_ref.refs_0_), channel_id=1, source_target_pairs={{4,0},{8,4},{12,8},{5,1},{9,5},{13,9},{6,2},{10,6},{14,10},{7,3},{... | collective-permute-start | bytes 786440 | tf_op jit(solution)/shard_map/ppermute | solution.py:25
  6.2 1.3 %collective-permute-start.2 = (bf16[8,2,8,1024]{3,2,1,0:T(8,128)(2,1)S(1)}, bf16[8,2,8,1024]{3,2,1,0:T(8,128)(2,1)S(1)}, u32[]{:S(2)}, u32[]{:S(2)}) collective-permute-start(bf16[8,2,8,1024]{3,2,1,0:T(8,128)(2,1)S(1)} %shard_map.65.base_ref.refs_0_), channel_id=1, source_target_pairs={{8,0},{12,4},{9,1},{13,5},{10,2},{14,6},{11,3},{15,7},{24,16},{28,... | collective-permute-start | bytes 786440 | tf_op jit(solution)/shard_map/ppermute | solution.py:25
  7.5 1.3 %collective-permute-start = (bf16[8,2,8,1024]{3,2,1,0:T(8,128)(2,1)S(1)}, bf16[8,2,8,1024]{3,2,1,0:T(8,128)(2,1)S(1)}, u32[]{:S(2)}, u32[]{:S(2)}) collective-permute-start(bf16[8,2,8,1024]{3,2,1,0:T(8,128)(2,1)S(1)} %copy-done.1), channel_id=1, source_target_pairs={{12,0},{13,1},{14,2},{15,3},{28,16},{29,17},{30,18},{31,19}} | collective-permute-start | bytes 786440 | tf_op jit(solution)/shard_map/ppermute | solution.py:25
  8.8 0.0 copy-done.4
  8.8 0.0 copy-start.2
  8.9 0.8 %copy-done.2 = f32[2,32,256]{2,1,0:T(8,128)S(1)} copy-done((f32[2,32,256]{2,1,0:T(8,128)S(1)}, f32[2,32,256]{2,1,0:T(8,128)}, u32[]{:S(2)}) %copy-start.2) | copy-done | bytes 65560
  9.7 0.0 copy-start.5
  9.7 0.7 shard_map.67
  10.3 0.2 copy-done.5
  10.5 5.9 %collective-permute-done.3.refs_0_ = bf16[8,2,8,1024]{3,2,1,0:T(8,128)(2,1)S(1)} collective-permute-done((bf16[8,2,8,1024]{3,2,1,0:T(8,128)(2,1)S(1)}, bf16[8,2,8,1024]{3,2,1,0:T(8,128)(2,1)S(1)}, u32[]{:S(2)}, u32[]{:S(2)}) %collective-permute-start.3) | collective-permute-done | bytes 262176 | tf_op jit(solution)/shard_map/ppermute | solution.py:25
  16.4 0.0 copy-start.3
  16.4 0.7 copy-done.3
  17.0 3.2 %shard_map.70 = f32[4,1,64,256]{3,2,1,0:T(8,128)} custom-call(s32[8]{0:T(128)S(1)} %copy-done.3, bf16[8,2,8,1024]{3,2,1,0:T(8,128)(2,1)S(1)} %shard_map.65.base_ref.refs_0_, bf16[8,2,8,1024]{3,2,1,0:T(8,128)(2,1)S(1)} %collective-permute-done.3.refs_0_, f32[8,1024]{1,0:T(8,128)S(1)} %dynamic-slice_bitcast_fusion.1.refs_2_.refs_1_, ...), custom_call_target="tpu_custom_call" | custom-call | flops 805306368 | bytes 4194304 | tf_op jit(solution)/shard_map/pallas_call | solution.py:194
  20.2 3.4 %all-to-all-start.2 = ((f32[4,1,64,256]{3,2,1,0:T(8,128)}), f32[4,1,64,256]{3,2,1,0:T(8,128)S(1)}, u32[]{:S(2)}, u32[]{:S(2)}) async-start(f32[4,1,64,256]{3,2,1,0:T(8,128)} %shard_map.70), calls=%async_computation.2 | async-start | bytes 524288 | tf_op jit(solution)/shard_map/all_to_all | solution.py:209
  23.6 10.8 %collective-permute-done.2.refs_0_ = bf16[8,2,8,1024]{3,2,1,0:T(8,128)(2,1)S(1)} collective-permute-done((bf16[8,2,8,1024]{3,2,1,0:T(8,128)(2,1)S(1)}, bf16[8,2,8,1024]{3,2,1,0:T(8,128)(2,1)S(1)}, u32[]{:S(2)}, u32[]{:S(2)}) %collective-permute-start.2) | collective-permute-done | bytes 262176 | tf_op jit(solution)/shard_map/ppermute | solution.py:25
  34.4 3.2 %shard_map.69 = f32[4,1,64,256]{3,2,1,0:T(8,128)} custom-call(s32[8]{0:T(128)S(1)} %copy-done.3, bf16[8,2,8,1024]{3,2,1,0:T(8,128)(2,1)S(1)} %shard_map.65.base_ref.refs_0_, bf16[8,2,8,1024]{3,2,1,0:T(8,128)(2,1)S(1)} %collective-permute-done.2.refs_0_, f32[8,1024]{1,0:T(8,128)S(1)} %dynamic-slice_bitcast_fusion.1.refs_2_.refs_1_, ...), custom_call_target="tpu_custom_call" | custom-call | flops 805306368 | bytes 4194304 | tf_op jit(solution)/shard_map/pallas_call | solution.py:194
  37.6 0.0 all-to-all-done.2.refs_2_
  37.6 3.4 %all-to-all-start.1 = ((f32[4,1,64,256]{3,2,1,0:T(8,128)}), f32[4,1,64,256]{3,2,1,0:T(8,128)S(1)}, u32[]{:S(2)}, u32[]{:S(2)}) async-start(f32[4,1,64,256]{3,2,1,0:T(8,128)} %shard_map.69), calls=%async_computation.1 | async-start | bytes 524288 | tf_op jit(solution)/shard_map/all_to_all | solution.py:209
  41.0 1.3 %collective-permute-start.1 = (f32[8,8,1]{2,1,0:T(8,128)S(1)}, f32[8,8,1]{2,1,0:T(8,128)S(1)}, u32[]{:S(2)}, u32[]{:S(2)}) collective-permute-start(f32[8,8,1]{2,1,0:T(8,128)S(1)} %psum.7.power_ref), channel_id=1, source_target_pairs={{12,0},{13,1},{14,2},{15,3},{28,16},{29,17},{30,18},{31,19}} | collective-permute-start | bytes 776 | tf_op jit(solution)/shard_map/ppermute | solution.py:25
  42.3 6.3 %collective-permute-done.1.power_ref = f32[8,8,1]{2,1,0:T(8,128)S(1)} collective-permute-done((f32[8,8,1]{2,1,0:T(8,128)S(1)}, f32[8,8,1]{2,1,0:T(8,128)S(1)}, u32[]{:S(2)}, u32[]{:S(2)}) %collective-permute-start.1) | collective-permute-done | bytes 288 | tf_op jit(solution)/shard_map/ppermute | solution.py:25
  48.6 0.0 collective-permute-done.x_ref
  48.6 0.1 shard_map.66.refs_1_
  48.7 5.1 %shard_map.68 = f32[4,2,64,256]{3,2,1,0:T(8,128)} custom-call(s32[8]{0:T(128)S(1)} %copy-done.3, bf16[8,2,8,1024]{3,2,1,0:T(8,128)(2,1)S(1)} %shard_map.65.base_ref.refs_0_, bf16[8,2,8,1024]{3,2,1,0:T(8,128)(2,1)S(1)} %shard_map.65.base_ref.refs_0_, bf16[8,2,8,1024]{3,2,1,0:T(8,128)(2,1)S(1)} %shard_map.66.refs_1_, ...), custom_call_target="tpu_custom_call" | custom-call | flops 1610612736 | bytes 4194304 | tf_op jit(solution)/shard_map/pallas_call | solution.py:194
  53.8 0.0 copy-start.6
  53.8 0.0 all-to-all-done.1.refs_1_
  53.8 3.6 %all-to-all-start = ((f32[4,2,64,256]{3,2,1,0:T(8,128)}), f32[4,2,64,256]{3,2,1,0:T(8,128)S(1)}, u32[]{:S(2)}, u32[]{:S(2)}) async-start(f32[4,2,64,256]{3,2,1,0:T(8,128)} %shard_map.68), calls=%async_computation | async-start | bytes 1048576 | tf_op jit(solution)/shard_map/all_to_all | solution.py:209
  57.4 0.0 copy-done.6
  57.4 0.1 copy.7.mask_ref
  57.5 8.7 %all-to-all-done.refs_0_ = f32[4,2,64,256]{3,2,1,0:T(8,128)S(1)} async-done(((f32[4,2,64,256]{3,2,1,0:T(8,128)}), f32[4,2,64,256]{3,2,1,0:T(8,128)S(1)}, u32[]{:S(2)}, u32[]{:S(2)}) %all-to-all-start) | async-done | bytes 524320 | tf_op jit(solution)/shard_map/all_to_all | solution.py:209
  66.2 1.4 %shard_map.71 = f32[8,4,8,256]{3,2,1,0:T(8,128)} custom-call(s32[8,4]{1,0:T(8,128)S(1)} %copy.7.mask_ref, f32[4,2,64,256]{3,2,1,0:T(8,128)S(1)} %all-to-all-done.refs_0_, f32[4,1,64,256]{3,2,1,0:T(8,128)S(1)} %all-to-all-done.1.refs_1_, f32[4,1,64,256]{3,2,1,0:T(8,128)S(1)} %all-to-all-done.2.refs_2_), custom_call_target="tpu_custom_call" | custom-call | tf_op jit(solution)/shard_map/pallas_call | solution.py:211
  (2 shorter events, 0.0 us)
Async XLA Ops:
  0.0 0.9 %copy-start = (bf16[8,2,8,1024]{3,2,1,0:T(8,128)(2,1)S(1)}, bf16[8,2,8,1024]{3,2,1,0:T(8,128)(2,1)}, u32[]{:S(2)}) copy-start(bf16[8,2,8,1024]{3,2,1,0:T(8,128)(2,1)} %x_ref.3) | copy-start | bytes 786436
  1.0 3.8 %copy-start.1 = (bf16[8,2,8,1024]{3,2,1,0:T(8,128)(2,1)S(1)}, bf16[8,2,8,1024]{3,2,1,0:T(8,128)(2,1)}, u32[]{:S(2)}) copy-start(bf16[8,2,8,1024]{3,2,1,0:T(8,128)(2,1)} %x_ref.3) | copy-start | bytes 786436
  4.8 4.0 %copy-start.4 = (f32[2,2,32,256]{3,2,0,1:T(8,128)S(1)}, f32[2,2,32,256]{3,2,0,1:T(8,128)}, u32[]{:S(2)}) copy-start(f32[2,2,32,256]{3,2,0,1:T(8,128)} %constant.20.clone) | copy-start | bytes 393220
  4.9 11.5 %collective-permute-start.3 = (bf16[8,2,8,1024]{3,2,1,0:T(8,128)(2,1)S(1)}, bf16[8,2,8,1024]{3,2,1,0:T(8,128)(2,1)S(1)}, u32[]{:S(2)}, u32[]{:S(2)}) collective-permute-start(bf16[8,2,8,1024]{3,2,1,0:T(8,128)(2,1)S(1)} %shard_map.65.base_ref.refs_0_), channel_id=1, source_target_pairs={{4,0},{8,4},{12,8},{5,1},{9,5},{13,9},{6,2},{10,6},{14,10},{7,3},{... | collective-permute-start | bytes 786440 | tf_op jit(solution)/shard_map/ppermute | solution.py:25
  6.2 28.2 %collective-permute-start.2 = (bf16[8,2,8,1024]{3,2,1,0:T(8,128)(2,1)S(1)}, bf16[8,2,8,1024]{3,2,1,0:T(8,128)(2,1)S(1)}, u32[]{:S(2)}, u32[]{:S(2)}) collective-permute-start(bf16[8,2,8,1024]{3,2,1,0:T(8,128)(2,1)S(1)} %shard_map.65.base_ref.refs_0_), channel_id=1, source_target_pairs={{8,0},{12,4},{9,1},{13,5},{10,2},{14,6},{11,3},{15,7},{24,16},{28,... | collective-permute-start | bytes 786440 | tf_op jit(solution)/shard_map/ppermute | solution.py:25
  7.5 41.1 %collective-permute-start = (bf16[8,2,8,1024]{3,2,1,0:T(8,128)(2,1)S(1)}, bf16[8,2,8,1024]{3,2,1,0:T(8,128)(2,1)S(1)}, u32[]{:S(2)}, u32[]{:S(2)}) collective-permute-start(bf16[8,2,8,1024]{3,2,1,0:T(8,128)(2,1)S(1)} %copy-done.1), channel_id=1, source_target_pairs={{12,0},{13,1},{14,2},{15,3},{28,16},{29,17},{30,18},{31,19}} | collective-permute-start | bytes 786440 | tf_op jit(solution)/shard_map/ppermute | solution.py:25
  8.8 0.8 %copy-start.2 = (f32[2,32,256]{2,1,0:T(8,128)S(1)}, f32[2,32,256]{2,1,0:T(8,128)}, u32[]{:S(2)}) copy-start(f32[2,32,256]{2,1,0:T(8,128)} %constant.21.clone.fine_ref) | copy-start | bytes 196612
  9.7 0.8 %copy-start.5 = (f32[8,2,1024]{2,0,1:T(8,128)S(1)}, f32[8,2,1024]{2,0,1:T(8,128)}, u32[]{:S(2)}) copy-start(f32[8,2,1024]{2,0,1:T(8,128)} %constant.22.clone) | copy-start | bytes 196612
  16.4 0.7 copy-start.3
  20.2 17.4 %all-to-all-start.2 = ((f32[4,1,64,256]{3,2,1,0:T(8,128)}), f32[4,1,64,256]{3,2,1,0:T(8,128)S(1)}, u32[]{:S(2)}, u32[]{:S(2)}) async-start(f32[4,1,64,256]{3,2,1,0:T(8,128)} %shard_map.70), calls=%async_computation.2 | async-start | bytes 524288 | tf_op jit(solution)/shard_map/all_to_all | solution.py:209
  37.6 16.2 %all-to-all-start.1 = ((f32[4,1,64,256]{3,2,1,0:T(8,128)}), f32[4,1,64,256]{3,2,1,0:T(8,128)S(1)}, u32[]{:S(2)}, u32[]{:S(2)}) async-start(f32[4,1,64,256]{3,2,1,0:T(8,128)} %shard_map.69), calls=%async_computation.1 | async-start | bytes 524288 | tf_op jit(solution)/shard_map/all_to_all | solution.py:209
  41.0 7.6 %collective-permute-start.1 = (f32[8,8,1]{2,1,0:T(8,128)S(1)}, f32[8,8,1]{2,1,0:T(8,128)S(1)}, u32[]{:S(2)}, u32[]{:S(2)}) collective-permute-start(f32[8,8,1]{2,1,0:T(8,128)S(1)} %psum.7.power_ref), channel_id=1, source_target_pairs={{12,0},{13,1},{14,2},{15,3},{28,16},{29,17},{30,18},{31,19}} | collective-permute-start | bytes 776 | tf_op jit(solution)/shard_map/ppermute | solution.py:25
  53.8 3.6 %copy-start.6 = (s32[8,4]{0,1:T(4,128)S(1)}, s32[8,4]{0,1:T(4,128)}, u32[]{:S(2)}) copy-start(s32[8,4]{0,1:T(4,128)} %param.8) | copy-start | bytes 388
  53.8 12.4 %all-to-all-start = ((f32[4,2,64,256]{3,2,1,0:T(8,128)}), f32[4,2,64,256]{3,2,1,0:T(8,128)S(1)}, u32[]{:S(2)}, u32[]{:S(2)}) async-start(f32[4,2,64,256]{3,2,1,0:T(8,128)} %shard_map.68), calls=%async_computation | async-start | bytes 1048576 | tf_op jit(solution)/shard_map/all_to_all | solution.py:209

commit v4 on v3

v4 whole, which is shorter than its diff:
```python
import functools
import math

import jax
import jax.numpy as jnp
import numpy as np
from jax import lax
from jax.experimental import pallas as pl
from jax.experimental.pallas import tpu as pltpu
from jax.sharding import PartitionSpec as P

LAGS = 1024
F_LO = 60
NSAMP = 15000
EPS = 1e-06
LANES = 128
FINE = 32
TERMS = 6
VMEM_LIMIT = 48 * 1024 * 1024


def from_behind(block, axis, distance):
    devices = range(lax.axis_size(axis))
    route = [(i - distance, i) for i in devices if i - distance in devices]
    return lax.ppermute(block, axis, route)


def phases(bins, lags):
    turns = np.remainder(np.asarray(bins, np.int64)[:, None] * np.asarray(lags, np.int64)[None, :], NSAMP)
    angle = turns * (2.0 * math.pi / NSAMP)
    return np.stack([np.cos(angle), np.sin(angle)]).astype(np.float32)


def split(value):
    high = value.astype(jnp.bfloat16)
    return high, (value - high.astype(jnp.float32)).astype(jnp.bfloat16)


def power_kernel(x_ref, out_ref):
    for w in range(x_ref.shape[0]):
        x = x_ref[w].astype(jnp.float32)
        x = x[0] * x[0] + x[1] * x[1]
        out_ref[w] = jnp.sum(x, axis=-1, keepdims=True)


def table_kernel(coarse_ref, fine_ref, table_ref):
    width = table_ref.shape[-1]
    per_tile = LANES // FINE
    fine_cos, fine_sin = fine_ref[0], fine_ref[1]

    def body(a, carry):
        cos_a = coarse_ref[0, pl.ds(a, 1), :]
        sin_a = coarse_ref[1, pl.ds(a, 1), :]
        tile = a // per_tile
        start = pl.multiple_of((tile * TERMS * per_tile + a % per_tile) * FINE, FINE)
        values = (cos_a * fine_cos - sin_a * fine_sin, -(cos_a * fine_sin + sin_a * fine_cos))
        for part in range(2):
            high, low = split(values[part])
            for term, value in ((part, high), (2 + part, high), (4 + part, low)):
                table_ref[pl.ds(start + term * LANES, FINE), :] = value
        return carry

    lax.fori_loop(0, table_ref.shape[0] // (TERMS * FINE), body, 0)


def whiten_kernel(n_bins, x_ref, power_ref, out_ref):
    for w in range(x_ref.shape[0]):
        scale = lax.rsqrt(power_ref[w] / n_bins + EPS)
        for part in range(2):
            out_ref[w, part] = (x_ref[w, part].astype(jnp.float32) * scale).astype(jnp.bfloat16)


def cross_tile(own_ref, partner_ref, lanes):
    w_dev, _, ch, _ = own_ref.shape
    real = [None] * ch
    imag = [None] * ch
    for w in range(w_dev):
        partner_re = partner_ref[w, 0, :, lanes].astype(jnp.float32)
        partner_im = partner_ref[w, 1, :, lanes].astype(jnp.float32)
        for i in range(ch):
            own_re = own_ref[w, 0, i:i + 1, lanes]
            own_im = own_ref[w, 1, i:i + 1, lanes]
            re = own_re * partner_re + own_im * partner_im
            im = own_im * partner_re - own_re * partner_im
            real[i] = re if w == 0 else real[i] + re
            imag[i] = im if w == 0 else imag[i] + im
    return real, imag


def pairs_kernel(n_partners, first, groups, keep_ref, base_ref, *refs):
    partner_refs = refs[:n_partners]
    twiddle_ref, table_ref = refs[n_partners:n_partners + 2]
    own_ref, rows_ref = refs[-2:]
    out_refs = refs[-2 - groups:-2]
    w_dev, _, ch, f_dev = base_ref.shape
    tiles = f_dev // LANES
    depth = TERMS * LANES
    for w in range(w_dev):
        kept = keep_ref[w].astype(jnp.float32)
        for part in range(2):
            own_ref[w, part] = base_ref[w, part].astype(jnp.float32) * kept

    def prepare(partner_ref, tile):
        lanes = pl.ds(pl.multiple_of(tile * LANES, LANES), LANES)
        slot = tile % 2
        real, imag = cross_tile(own_ref, partner_ref, lanes)
        for q in range(groups):
            cos_q = twiddle_ref[q:q + 1, lanes]
            sin_q = twiddle_ref[groups + q:groups + q + 1, lanes]
            for i in range(0, ch, 2):
                rows = slice((q * ch + i) * ch, (q * ch + i + 2) * ch)
                re = jnp.concatenate(real[i:i + 2], axis=0)
                im = jnp.concatenate(imag[i:i + 2], axis=0)
                values = (re * cos_q - im * sin_q, re * sin_q + im * cos_q)
                for part in range(2):
                    high, low = split(values[part])
                    for term, value in ((part, high), (2 + part, low), (4 + part, high)):
                        rows_ref[slot, rows, term * LANES:(term + 1) * LANES] = value

    def transform(k, tile, start):
        table = table_ref[pl.ds(pl.multiple_of(tile * depth, depth), depth), :]
        part = jnp.dot(rows_ref[tile % 2], table, preferred_element_type=jnp.float32)
        for q, out_ref in enumerate(out_refs):
            block = part[q * ch * ch:(q + 1) * ch * ch]
            out_ref[first + k] = block if start else out_ref[first + k] + block

    for k, partner_ref in enumerate(partner_refs):
        prepare(partner_ref, 0)
        prepare(partner_ref, 1)
        transform(k, 0, True)

        def body(tile, carry):
            transform(k, tile - 1, False)
            prepare(partner_ref, tile)
            return carry

        lax.fori_loop(2, tiles, body, 0)
        transform(k, tiles - 1, False)


def combine_kernel(scale, order, groups, mask_ref, *refs):
    out_ref = refs[-1]
    ch = out_ref.shape[0]
    start = 0
    for place in range(0, len(refs) - 1, groups):
        parts = refs[place:place + groups]
        for n in range(parts[0].shape[0]):
            k = order[start + n]
            total = parts[0][n]
            for ref in parts[1:]:
                total = total + ref[n]
            for i in range(ch):
                factor = mask_ref[i, k].astype(jnp.float32) * scale
                out_ref[i, k] = total[i * ch:(i + 1) * ch] * factor
        start += parts[0].shape[0]


VMEM = pl.BlockSpec(memory_space=pltpu.VMEM)
SMEM = pl.BlockSpec(memory_space=pltpu.SMEM)


def local(spectra, keep, pair_mask):
    w_dev, _, ch, f_dev = spectra.shape
    reach = pair_mask.shape[1] - 1
    n_win, n_freq = (lax.axis_size(a) for a in ("win", "freq"))
    groups = n_win * n_freq
    width = LAGS // groups
    n_bins = f_dev * n_freq
    params = pltpu.CompilerParams(vmem_limit_bytes=VMEM_LIMIT)
    freq = lax.axis_index("freq")
    place = lax.axis_index(("win", "freq"))

    def whiten(block, power):
        return pl.pallas_call(
            functools.partial(whiten_kernel, n_bins),
            out_shape=jax.ShapeDtypeStruct(block.shape, jnp.bfloat16),
            in_specs=[VMEM] * 2, out_specs=VMEM, compiler_params=params,
        )(block, power)

    raw = from_behind(spectra, "chan", -1)
    power = pl.pallas_call(
        power_kernel,
        out_shape=jax.ShapeDtypeStruct((w_dev, ch, 1), jnp.float32),
        in_specs=[VMEM], out_specs=VMEM, compiler_params=params,
    )(spectra)
    power = lax.psum(power, "freq")
    white = whiten(spectra, power)
    moving = whiten(raw, from_behind(power, "chan", -1))

    coarse = phases(np.arange(0, n_bins, FINE), np.arange(width))
    coarse = coarse.reshape(2, n_freq, f_dev // FINE, width)
    coarse = lax.dynamic_index_in_dim(jnp.asarray(coarse), freq, 1, keepdims=False)
    fine = jnp.asarray(phases(F_LO + np.arange(FINE), np.arange(width)))
    table = pl.pallas_call(
        table_kernel,
        out_shape=jax.ShapeDtypeStruct((TERMS * f_dev, width), jnp.bfloat16),
        in_specs=[VMEM] * 2, out_specs=VMEM, compiler_params=params,
    )(coarse, fine)
    twiddle = phases(F_LO + np.arange(n_bins), np.arange(groups) * width - LAGS // 2)
    twiddle = np.moveaxis(twiddle, 1, 2).reshape(2, groups, n_freq, f_dev)
    twiddle = np.stack([np.roll(twiddle[:, :, g % n_freq], -g, axis=1) for g in range(groups)])
    twiddle = lax.dynamic_index_in_dim(jnp.asarray(twiddle), place, 0, keepdims=False)
    twiddle = twiddle.reshape(2 * groups, f_dev)

    rows = groups * ch * ch

    def pairs(base, partners):
        n = len(partners)
        flops = n * 6 * rows * 2 * f_dev * width
        return pl.pallas_call(
            functools.partial(pairs_kernel, n, 0, groups),
            out_shape=[jax.ShapeDtypeStruct((n, ch * ch, width), jnp.float32)] * groups,
            in_specs=[SMEM] + [VMEM] * (n + 3), out_specs=[VMEM] * groups,
            scratch_shapes=[
                pltpu.VMEM(base.shape, jnp.float32),
                pltpu.VMEM((2, rows, TERMS * LANES), jnp.bfloat16),
            ],
            compiler_params=params,
            cost_estimate=pl.CostEstimate(flops=flops, bytes_accessed=2 ** 22, transcendentals=0),
        )(keep, base, *partners, twiddle, table)

    def exchange(parts):
        received = [parts[0]]
        for turn in range(1, groups):
            route = [(g, (g + turn) % groups) for g in range(groups)]
            received.append(lax.ppermute(parts[turn], ("win", "freq"), route))
        return received

    parts = pairs(white, [white, moving])
    received = []
    for step in range(1, reach):
        moving = from_behind(moving, "chan", -1)
        moving, parts = lax.optimization_barrier((moving, parts))
        received += exchange(parts)
        parts = pairs(white, [moving])
    received += exchange(parts)
    scale = 1.0 / math.sqrt(w_dev * n_win * n_bins)
    return pl.pallas_call(
        functools.partial(combine_kernel, scale, list(range(reach + 1)), groups),
        out_shape=jax.ShapeDtypeStruct((ch, reach + 1, ch, width), jnp.float32),
        in_specs=[SMEM] + [VMEM] * len(received), out_specs=VMEM, compiler_params=params,
    )(pair_mask, *received)


def solution(mesh):
    in_specs = (
        P("win", None, ("fibre", "chan"), "freq"),
        P(("fibre", "win")),
        P(("fibre", "chan"), None),
    )
    out_specs = P(("fibre", "chan"), None, None, ("win", "freq"))
    return jax.shard_map(local, mesh=mesh, in_specs=in_specs, out_specs=out_specs, check_vma=False)
```

time: 68.2 us -> 47.5 us (0.70)
  waiting for transfers between devices: 31.7 us -> 9.27 us
  starting transfers between devices: 15.6 us -> 13.6 us
  Pallas kernels: 13.8 us -> 15.7 us
  local copies, waits for them, and re-layouts: 2.71 us -> 4.46 us
    ppermute x4, waiting for transfers between devices: 22.9 us -> 6.22 us  [from_behind(): return lax.ppermute(block, axis, route)]
    all_to_all x3 -> x0, starting transfers between devices: 10.4 us -> none  [local(): lax.all_to_all(part, ('win', 'freq'), 0, 0, tiled=True)]
    all_to_all x3 -> x0, waiting for transfers between devices: 8.72 us -> none  [local(): lax.all_to_all(part, ('win', 'freq'), 0, 0, tiled=True)]
    ppermute x0 -> x9, starting transfers between devices: none -> 8.47 us  [exchange(): received.append(lax.ppermute(parts[turn], ('win', 'freq'), route))]
    ppermute x0 -> x9, waiting for transfers between devices: none -> 3.05 us  [exchange(): received.append(lax.ppermute(parts[turn], ('win', 'freq'), route))]
    pallas_call x5, Pallas kernels: 13.4 us -> 15.3 us  [the longest x3 13.3 us: pairs(): pl.pallas_call(functools.partial(pairs_kernel, n, 0, groups), out_shape=[...]
    squeeze x1, local copies, waits for them, and re-layouts: 0.01 us -> 0.85 us  [local(): lax.dynamic_index_in_dim(jnp.asarray(coarse), freq, 1, keepdims=False)]
    dynamic_slice x0 -> x1, local copies, waits for them, and re-layouts: none -> 0.77 us  [local(): lax.dynamic_index_in_dim(jnp.asarray(twiddle), place, 0, keepdims=False)]
  transfers between devices with their start and end apart: 7 -> 13, of which waited for: 4 -> 5; matrix products, arithmetic and copies ran while one was open for 0% -> 4% of each run, Pallas kernels for 18% -> 30%
where the time goes in v4:
time: 47.5 us; the launch traced here: 46.9 us
  Pallas kernels  15.7 us (33%)
  starting transfers between devices  13.6 us (29%)
  waiting for transfers between devices  9.27 us (20%)
  local copies, waits for them, and re-layouts  4.46 us (9%)
  blocking collectives  3.67 us (8%)
    pallas_call x3, Pallas kernels, pairs(): pl.pallas_call(functools.partial(pairs_kernel, n, 0, groups), out_shape=[...  13.3 us
    ppermute x9, starting transfers between devices, exchange(): received.append(lax.ppermute(parts[turn], ('win', 'freq'), route))  8.47 us
    ppermute x4, waiting for transfers between devices, from_behind(): return lax.ppermute(block, axis, route)  6.22 us
    ppermute x4, starting transfers between devices, from_behind(): return lax.ppermute(block, axis, route)  5.16 us
    psum x1, blocking collectives, local(): power = lax.psum(power, 'freq')  3.67 us
    ppermute x9, waiting for transfers between devices, exchange(): received.append(lax.ppermute(parts[turn], ('win', 'freq'), route))  3.05 us
    unnamed x11, local copies, waits for them, and re-layouts  2.82 us
    pallas_call x1, Pallas kernels, local(): pl.pallas_call(functools.partial(combine_kernel, scale, list(range(reach...  1.35 us
  transfers between devices with their start and end apart: 13, of which 5 were waited for; matrix products, arithmetic and copies ran while one was open for 4% of the time, Pallas kernels for 30%

profile of v4, /device:TPU:0, one launch (start us, length us, event | category | flops | bytes accessed | tf_op | source)
XLA Modules:
  0.0 46.9 jit_solution(5033028674223956527)
XLA Ops:
  0.0 1.3 %collective-permute-start = (bf16[8,2,8,1024]{3,2,1,0:T(8,128)(2,1)}, bf16[8,2,8,1024]{3,2,1,0:T(8,128)(2,1)S(1)}, u32[]{:S(2)}, u32[]{:S(2)}) collective-permute-start(bf16[8,2,8,1024]{3,2,1,0:T(8,128)(2,1)} %x_ref.3), channel_id=1, source_target_pairs={{4,0},{8,4},{12,8},{5,1},{9,5},{13,9},{6,2},{10,6},{14,10},{7,3},{... | collective-permute-start | bytes 786440 | tf_op jit(solution)/shard_map/ppermute | solution.py:25
  1.3 0.0 copy-start
  1.3 0.9 %copy-done = bf16[8,2,8,1024]{3,2,1,0:T(8,128)(2,1)S(1)} copy-done((bf16[8,2,8,1024]{3,2,1,0:T(8,128)(2,1)S(1)}, bf16[8,2,8,1024]{3,2,1,0:T(8,128)(2,1)}, u32[]{:S(2)}) %copy-start) | copy-done | bytes 262168
  2.2 0.0 copy-start.3
  2.2 0.1 shard_map.64
  2.4 3.7 %psum.7.power_ref = f32[8,8,1]{2,1,0:T(8,128)S(1)} all-reduce(f32[8,8,1]{2,1,0:T(8,128)S(1)} %shard_map.64), channel_id=1, replica_groups=mesh['fibre'=2,'chan'=4,'win'=2,'freq'=2] {'freq'}, use_global_device_ids=true, to_apply=%region_0.0 | all-reduce | flops 64 | bytes 512 | tf_op jit(solution)/shard_map/psum | solution.py:186
  6.1 1.3 %collective-permute-start.1 = (f32[8,8,1]{2,1,0:T(8,128)S(1)}, f32[8,8,1]{2,1,0:T(8,128)S(1)}, u32[]{:S(2)}, u32[]{:S(2)}) collective-permute-start(f32[8,8,1]{2,1,0:T(8,128)S(1)} %psum.7.power_ref), channel_id=1, source_target_pairs={{4,0},{8,4},{12,8},{5,1},{9,5},{13,9},{6,2},{10,6},{14,10},{7,3},{... | collective-permute-start | bytes 776 | tf_op jit(solution)/shard_map/ppermute | solution.py:25
  7.4 0.8 %constant_dynamic-slice_fusion = f32[1,2,4,1024]{3,2,1,0:T(4,128)S(1)} fusion(f32[4,2,4,1024]{3,2,1,0:T(4,128)} %constant.26.clone, s32[]{:T(128)S(6)} %select_n.8), kind=kLoop, calls=%fused_computation.1 | loop fusion | bytes 65540 | tf_op jit(solution)/shard_map/jit(dynamic_index_in_dim)/dynamic_slice | solution.py:202
  8.1 0.0 copy-start.1
  8.1 0.9 %copy-done.1 = bf16[8,2,8,1024]{3,2,1,0:T(8,128)(2,1)S(1)} copy-done((bf16[8,2,8,1024]{3,2,1,0:T(8,128)(2,1)S(1)}, bf16[8,2,8,1024]{3,2,1,0:T(8,128)(2,1)}, u32[]{:S(2)}) %copy-start.1) | copy-done | bytes 262168
  9.1 0.1 shard_map.66.base_ref.refs_0_
  9.2 4.0 %collective-permute-done.1.power_ref = f32[8,8,1]{2,1,0:T(8,128)S(1)} collective-permute-done((f32[8,8,1]{2,1,0:T(8,128)S(1)}, f32[8,8,1]{2,1,0:T(8,128)S(1)}, u32[]{:S(2)}, u32[]{:S(2)}) %collective-permute-start.1) | collective-permute-done | bytes 288 | tf_op jit(solution)/shard_map/ppermute | solution.py:25
  13.2 0.0 collective-permute-done.x_ref
  13.2 0.1 shard_map.65.refs_1_
  13.4 1.3 %collective-permute-start.2 = (bf16[8,2,8,1024]{3,2,1,0:T(8,128)(2,1)S(1)}, bf16[8,2,8,1024]{3,2,1,0:T(8,128)(2,1)S(1)}, u32[]{:S(2)}, u32[]{:S(2)}) collective-permute-start(bf16[8,2,8,1024]{3,2,1,0:T(8,128)(2,1)S(1)} %shard_map.65.refs_1_), channel_id=1, source_target_pairs={{4,0},{8,4},{12,8},{5,1},{9,5},{13,9},{6,2},{10,6},{14,10},{7,3},{... | collective-permute-start | bytes 786440 | tf_op jit(solution)/shard_map/ppermute | solution.py:25
  14.7 0.9 %dynamic-slice_bitcast_fusion.coarse_ref = f32[2,32,256]{2,1,0:T(8,128)S(1)} fusion(f32[2,2,32,256]{3,2,0,1:T(8,128)} %constant.24.clone, s32[]{:T(128)S(6)} %select_n.9), kind=kLoop, calls=%fused_computation | loop fusion | bytes 131076 | tf_op jit(solution)/shard_map/jit(dynamic_index_in_dim)/squeeze | solution.py:192
  15.5 0.0 copy-start.2
  15.5 0.8 %copy-done.2 = f32[2,32,256]{2,1,0:T(8,128)S(1)} copy-done((f32[2,32,256]{2,1,0:T(8,128)S(1)}, f32[2,32,256]{2,1,0:T(8,128)}, u32[]{:S(2)}) %copy-start.2) | copy-done | bytes 65560
  16.4 0.7 %shard_map.67.refs_3_.refs_2_ = bf16[6144,256]{1,0:T(8,128)(2,1)S(1)} custom-call(f32[2,32,256]{2,1,0:T(8,128)S(1)} %dynamic-slice_bitcast_fusion.coarse_ref, f32[2,32,256]{2,1,0:T(8,128)S(1)} %copy-done.2), custom_call_target="tpu_custom_call" | custom-call | tf_op jit(solution)/shard_map/pallas_call | solution.py:194
  17.1 0.0 copy-done.3
  17.1 6.3 %shard_map.68 = (f32[2,64,256]{2,1,0:T(8,128)S(1)}, f32[2,64,256]{2,1,0:T(8,128)S(1)}, f32[2,64,256]{2,1,0:T(8,128)S(1)}, f32[2,64,256]{2,1,0:T(8,128)S(1)}) custom-call(s32[8]{0:T(128)S(1)} %copy-done.3, bf16[8,2,8,1024]{3,2,1,0:T(8,128)(2,1)S(1)} %shard_map.66.base_ref.refs_0_, bf16[8,2,8,1024]{3,2,1,0:T(8,128)(2,1)S(1)} %shard_map.66.base_ref.refs_0_, ...), custom_call_target="tpu_custom_call" | custom-call | flops 1610612736 | bytes 4194304 | tf_op jit(solution)/shard_map/pallas_call | solution.py:210
  23.3 0.0 collective-permute-done.2.refs_0_
  23.3 0.0 copy-start.4
  23.4 1.3 %collective-permute-start.6 = (bf16[8,2,8,1024]{3,2,1,0:T(8,128)(2,1)S(1)}, bf16[8,2,8,1024]{3,2,1,0:T(8,128)(2,1)S(1)}, u32[]{:S(2)}, u32[]{:S(2)}) collective-permute-start(bf16[8,2,8,1024]{3,2,1,0:T(8,128)(2,1)S(1)} %collective-permute-done.2.refs_0_), channel_id=1, source_target_pairs={{4,0},{8,4},{12,8},{5,1},{9,5},{13,9},{6,2},{10,6},{14,10},{7,3},{... | collective-permute-start | bytes 786440 | tf_op jit(solution)/shard_map/ppermute | solution.py:25
  24.7 0.1 collective-permute-start.3
  24.7 2.0 %collective-permute-start.4 = (f32[2,64,256]{2,1,0:T(8,128)S(1)}, f32[2,64,256]{2,1,0:T(8,128)S(1)}, u32[]{:S(2)}, u32[]{:S(2)}) collective-permute-start(f32[2,64,256]{2,1,0:T(8,128)S(1)} %get-tuple-element.33), channel_id=1, source_target_pairs={{0,2},{1,3},{2,0},{3,1},{4,6},{5,7},{6,4},{7,5},{8,10},{9,11},{10,... | collective-permute-start | bytes 393224 | tf_op jit(solution)/shard_map/ppermute | solution.py:226
  26.7 1.4 %collective-permute-start.5 = (f32[2,64,256]{2,1,0:T(8,128)S(1)}, f32[2,64,256]{2,1,0:T(8,128)S(1)}, u32[]{:S(2)}, u32[]{:S(2)}) collective-permute-start(f32[2,64,256]{2,1,0:T(8,128)S(1)} %get-tuple-element.34), channel_id=1, source_target_pairs={{0,3},{1,0},{2,1},{3,2},{4,7},{5,4},{6,5},{7,6},{8,11},{9,8},{10,9... | collective-permute-start | bytes 393224 | tf_op jit(solution)/shard_map/ppermute | solution.py:226
  28.1 3.5 %shard_map.69 = (f32[1,64,256]{2,1,0:T(8,128)S(1)}, f32[1,64,256]{2,1,0:T(8,128)S(1)}, f32[1,64,256]{2,1,0:T(8,128)S(1)}, f32[1,64,256]{2,1,0:T(8,128)S(1)}) custom-call(s32[8]{0:T(128)S(1)} %copy-done.3, bf16[8,2,8,1024]{3,2,1,0:T(8,128)(2,1)S(1)} %shard_map.66.base_ref.refs_0_, bf16[8,2,8,1024]{3,2,1,0:T(8,128)(2,1)S(1)} %collective-permute-done.2.refs_0_, ...), custom_call_target="tpu_custom_call" | custom-call | flops 805306368 | bytes 4194304 | tf_op jit(solution)/shard_map/pallas_call | solution.py:210
  31.6 2.2 %collective-permute-done.6.refs_0_ = bf16[8,2,8,1024]{3,2,1,0:T(8,128)(2,1)S(1)} collective-permute-done((bf16[8,2,8,1024]{3,2,1,0:T(8,128)(2,1)S(1)}, bf16[8,2,8,1024]{3,2,1,0:T(8,128)(2,1)S(1)}, u32[]{:S(2)}, u32[]{:S(2)}) %collective-permute-start.6) | collective-permute-done | bytes 262176 | tf_op jit(solution)/shard_map/ppermute | solution.py:25
  33.8 0.0 collective-permute-start.7
  33.8 1.7 %collective-permute-start.8 = (f32[1,64,256]{2,1,0:T(8,128)S(1)}, f32[1,64,256]{2,1,0:T(8,128)S(1)}, u32[]{:S(2)}, u32[]{:S(2)}) collective-permute-start(f32[1,64,256]{2,1,0:T(8,128)S(1)} %get-tuple-element.42), channel_id=1, source_target_pairs={{0,2},{1,3},{2,0},{3,1},{4,6},{5,7},{6,4},{7,5},{8,10},{9,11},{10,... | collective-permute-start | bytes 196616 | tf_op jit(solution)/shard_map/ppermute | solution.py:226
  35.5 3.5 %shard_map.70 = (f32[1,64,256]{2,1,0:T(8,128)S(1)}, f32[1,64,256]{2,1,0:T(8,128)S(1)}, f32[1,64,256]{2,1,0:T(8,128)S(1)}, f32[1,64,256]{2,1,0:T(8,128)S(1)}) custom-call(s32[8]{0:T(128)S(1)} %copy-done.3, bf16[8,2,8,1024]{3,2,1,0:T(8,128)(2,1)S(1)} %shard_map.66.base_ref.refs_0_, bf16[8,2,8,1024]{3,2,1,0:T(8,128)(2,1)S(1)} %collective-permute-done.6.refs_0_, ...), custom_call_target="tpu_custom_call" | custom-call | flops 805306368 | bytes 4194304 | tf_op jit(solution)/shard_map/pallas_call | solution.py:210
  39.0 0.0 collective-permute-done.3.refs_1_
  39.0 1.5 %collective-permute-start.9 = (f32[1,64,256]{2,1,0:T(8,128)S(1)}, f32[1,64,256]{2,1,0:T(8,128)S(1)}, u32[]{:S(2)}, u32[]{:S(2)}) collective-permute-start(f32[1,64,256]{2,1,0:T(8,128)S(1)} %get-tuple-element.43), channel_id=1, source_target_pairs={{0,3},{1,0},{2,1},{3,2},{4,7},{5,4},{6,5},{7,6},{8,11},{9,8},{10,9... | collective-permute-start | bytes 196616 | tf_op jit(solution)/shard_map/ppermute | solution.py:226
  40.5 0.0 collective-permute-done.4.refs_2_
  40.5 0.0 collective-permute-start.10
  40.5 0.0 collective-permute-done.5.refs_3_
  40.5 0.5 collective-permute-start.11
  41.0 0.0 collective-permute-done.7.refs_5_
  41.0 1.4 %collective-permute-start.12 = (f32[1,64,256]{2,1,0:T(8,128)S(1)}, f32[1,64,256]{2,1,0:T(8,128)S(1)}, u32[]{:S(2)}, u32[]{:S(2)}) collective-permute-start(f32[1,64,256]{2,1,0:T(8,128)S(1)} %get-tuple-element.48), channel_id=1, source_target_pairs={{0,3},{1,0},{2,1},{3,2},{4,7},{5,4},{6,5},{7,6},{8,11},{9,8},{10,9... | collective-permute-start | bytes 196616 | tf_op jit(solution)/shard_map/ppermute | solution.py:226
  42.4 0.0 copy-done.4
  42.4 0.1 copy.7.mask_ref
  42.5 0.0 collective-permute-done.8.refs_6_
  42.5 0.3 collective-permute-done.9.refs_7_
  42.8 1.5 %collective-permute-done.10.refs_9_ = f32[1,64,256]{2,1,0:T(8,128)S(1)} collective-permute-done((f32[1,64,256]{2,1,0:T(8,128)S(1)}, f32[1,64,256]{2,1,0:T(8,128)S(1)}, u32[]{:S(2)}, u32[]{:S(2)}) %collective-permute-start.10) | collective-permute-done | bytes 65568 | tf_op jit(solution)/shard_map/ppermute | solution.py:226
  44.3 1.2 %collective-permute-done.11.refs_10_ = f32[1,64,256]{2,1,0:T(8,128)S(1)} collective-permute-done((f32[1,64,256]{2,1,0:T(8,128)S(1)}, f32[1,64,256]{2,1,0:T(8,128)S(1)}, u32[]{:S(2)}, u32[]{:S(2)}) %collective-permute-start.11) | collective-permute-done | bytes 65568 | tf_op jit(solution)/shard_map/ppermute | solution.py:226
  45.5 0.0 collective-permute-done.12.refs_11_
  45.5 1.4 %shard_map.71 = f32[8,4,8,256]{3,2,1,0:T(8,128)} custom-call(s32[8,4]{1,0:T(8,128)S(1)} %copy.7.mask_ref, f32[2,64,256]{2,1,0:T(8,128)S(1)} %get-tuple-element.31.refs_0_, f32[2,64,256]{2,1,0:T(8,128)S(1)} %collective-permute-done.3.refs_1_, f32[2,64,256]{2,1,0:T(8,128)S(1)} %collective-permute-done.4.refs_2_, ...), custom_call_target="tpu_custom_call" | custom-call | tf_op jit(solution)/shard_map/pallas_call | solution.py:238
  (1 shorter events, 0.0 us)
Async XLA Ops:
  0.0 13.2 %collective-permute-start = (bf16[8,2,8,1024]{3,2,1,0:T(8,128)(2,1)}, bf16[8,2,8,1024]{3,2,1,0:T(8,128)(2,1)S(1)}, u32[]{:S(2)}, u32[]{:S(2)}) collective-permute-start(bf16[8,2,8,1024]{3,2,1,0:T(8,128)(2,1)} %x_ref.3), channel_id=1, source_target_pairs={{4,0},{8,4},{12,8},{5,1},{9,5},{13,9},{6,2},{10,6},{14,10},{7,3},{... | collective-permute-start | bytes 786440 | tf_op jit(solution)/shard_map/ppermute | solution.py:25
  1.3 1.0 %copy-start = (bf16[8,2,8,1024]{3,2,1,0:T(8,128)(2,1)S(1)}, bf16[8,2,8,1024]{3,2,1,0:T(8,128)(2,1)}, u32[]{:S(2)}) copy-start(bf16[8,2,8,1024]{3,2,1,0:T(8,128)(2,1)} %x_ref.3) | copy-start | bytes 786436
  2.2 14.8 %copy-start.3 = (s32[8]{0:T(128)S(1)}, s32[8]{0:T(128)}, u32[]{:S(2)}) copy-start(s32[8]{0:T(128)} %keep_ref.5) | copy-start | bytes 100
  6.1 7.2 %collective-permute-start.1 = (f32[8,8,1]{2,1,0:T(8,128)S(1)}, f32[8,8,1]{2,1,0:T(8,128)S(1)}, u32[]{:S(2)}, u32[]{:S(2)}) collective-permute-start(f32[8,8,1]{2,1,0:T(8,128)S(1)} %psum.7.power_ref), channel_id=1, source_target_pairs={{4,0},{8,4},{12,8},{5,1},{9,5},{13,9},{6,2},{10,6},{14,10},{7,3},{... | collective-permute-start | bytes 776 | tf_op jit(solution)/shard_map/ppermute | solution.py:25
  8.1 0.9 %copy-start.1 = (bf16[8,2,8,1024]{3,2,1,0:T(8,128)(2,1)S(1)}, bf16[8,2,8,1024]{3,2,1,0:T(8,128)(2,1)}, u32[]{:S(2)}) copy-start(bf16[8,2,8,1024]{3,2,1,0:T(8,128)(2,1)} %x_ref.3) | copy-start | bytes 786436
  13.4 10.0 %collective-permute-start.2 = (bf16[8,2,8,1024]{3,2,1,0:T(8,128)(2,1)S(1)}, bf16[8,2,8,1024]{3,2,1,0:T(8,128)(2,1)S(1)}, u32[]{:S(2)}, u32[]{:S(2)}) collective-permute-start(bf16[8,2,8,1024]{3,2,1,0:T(8,128)(2,1)S(1)} %shard_map.65.refs_1_), channel_id=1, source_target_pairs={{4,0},{8,4},{12,8},{5,1},{9,5},{13,9},{6,2},{10,6},{14,10},{7,3},{... | collective-permute-start | bytes 786440 | tf_op jit(solution)/shard_map/ppermute | solution.py:25
  15.5 0.8 %copy-start.2 = (f32[2,32,256]{2,1,0:T(8,128)S(1)}, f32[2,32,256]{2,1,0:T(8,128)}, u32[]{:S(2)}) copy-start(f32[2,32,256]{2,1,0:T(8,128)} %constant.25.clone.fine_ref) | copy-start | bytes 196612
  23.3 19.1 %copy-start.4 = (s32[8,4]{0,1:T(4,128)S(1)}, s32[8,4]{0,1:T(4,128)}, u32[]{:S(2)}) copy-start(s32[8,4]{0,1:T(4,128)} %param.8) | copy-start | bytes 388
  23.4 10.5 %collective-permute-start.6 = (bf16[8,2,8,1024]{3,2,1,0:T(8,128)(2,1)S(1)}, bf16[8,2,8,1024]{3,2,1,0:T(8,128)(2,1)S(1)}, u32[]{:S(2)}, u32[]{:S(2)}) collective-permute-start(bf16[8,2,8,1024]{3,2,1,0:T(8,128)(2,1)S(1)} %collective-permute-done.2.refs_0_), channel_id=1, source_target_pairs={{4,0},{8,4},{12,8},{5,1},{9,5},{13,9},{6,2},{10,6},{14,10},{7,3},{... | collective-permute-start | bytes 786440 | tf_op jit(solution)/shard_map/ppermute | solution.py:25
  24.7 14.4 %collective-permute-start.3 = (f32[2,64,256]{2,1,0:T(8,128)S(1)}, f32[2,64,256]{2,1,0:T(8,128)S(1)}, u32[]{:S(2)}, u32[]{:S(2)}) collective-permute-start(f32[2,64,256]{2,1,0:T(8,128)S(1)} %get-tuple-element.32), channel_id=1, source_target_pairs={{0,1},{1,2},{2,3},{3,0},{4,5},{5,6},{6,7},{7,4},{8,9},{9,10},{10,1... | collective-permute-start | bytes 393224 | tf_op jit(solution)/shard_map/ppermute | solution.py:226
  24.7 15.8 %collective-permute-start.4 = (f32[2,64,256]{2,1,0:T(8,128)S(1)}, f32[2,64,256]{2,1,0:T(8,128)S(1)}, u32[]{:S(2)}, u32[]{:S(2)}) collective-permute-start(f32[2,64,256]{2,1,0:T(8,128)S(1)} %get-tuple-element.33), channel_id=1, source_target_pairs={{0,2},{1,3},{2,0},{3,1},{4,6},{5,7},{6,4},{7,5},{8,10},{9,11},{10,... | collective-permute-start | bytes 393224 | tf_op jit(solution)/shard_map/ppermute | solution.py:226
  26.7 13.8 %collective-permute-start.5 = (f32[2,64,256]{2,1,0:T(8,128)S(1)}, f32[2,64,256]{2,1,0:T(8,128)S(1)}, u32[]{:S(2)}, u32[]{:S(2)}) collective-permute-start(f32[2,64,256]{2,1,0:T(8,128)S(1)} %get-tuple-element.34), channel_id=1, source_target_pairs={{0,3},{1,0},{2,1},{3,2},{4,7},{5,4},{6,5},{7,6},{8,11},{9,8},{10,9... | collective-permute-start | bytes 393224 | tf_op jit(solution)/shard_map/ppermute | solution.py:226
  33.8 7.2 %collective-permute-start.7 = (f32[1,64,256]{2,1,0:T(8,128)S(1)}, f32[1,64,256]{2,1,0:T(8,128)S(1)}, u32[]{:S(2)}, u32[]{:S(2)}) collective-permute-start(f32[1,64,256]{2,1,0:T(8,128)S(1)} %get-tuple-element.41), channel_id=1, source_target_pairs={{0,1},{1,2},{2,3},{3,0},{4,5},{5,6},{6,7},{7,4},{8,9},{9,10},{10,1... | collective-permute-start | bytes 196616 | tf_op jit(solution)/shard_map/ppermute | solution.py:226
  33.8 8.6 %collective-permute-start.8 = (f32[1,64,256]{2,1,0:T(8,128)S(1)}, f32[1,64,256]{2,1,0:T(8,128)S(1)}, u32[]{:S(2)}, u32[]{:S(2)}) collective-permute-start(f32[1,64,256]{2,1,0:T(8,128)S(1)} %get-tuple-element.42), channel_id=1, source_target_pairs={{0,2},{1,3},{2,0},{3,1},{4,6},{5,7},{6,4},{7,5},{8,10},{9,11},{10,... | collective-permute-start | bytes 196616 | tf_op jit(solution)/shard_map/ppermute | solution.py:226
  39.0 3.8 %collective-permute-start.9 = (f32[1,64,256]{2,1,0:T(8,128)S(1)}, f32[1,64,256]{2,1,0:T(8,128)S(1)}, u32[]{:S(2)}, u32[]{:S(2)}) collective-permute-start(f32[1,64,256]{2,1,0:T(8,128)S(1)} %get-tuple-element.43), channel_id=1, source_target_pairs={{0,3},{1,0},{2,1},{3,2},{4,7},{5,4},{6,5},{7,6},{8,11},{9,8},{10,9... | collective-permute-start | bytes 196616 | tf_op jit(solution)/shard_map/ppermute | solution.py:226
  40.5 3.8 %collective-permute-start.10 = (f32[1,64,256]{2,1,0:T(8,128)S(1)}, f32[1,64,256]{2,1,0:T(8,128)S(1)}, u32[]{:S(2)}, u32[]{:S(2)}) collective-permute-start(f32[1,64,256]{2,1,0:T(8,128)S(1)} %get-tuple-element.46), channel_id=1, source_target_pairs={{0,1},{1,2},{2,3},{3,0},{4,5},{5,6},{6,7},{7,4},{8,9},{9,10},{10,1... | collective-permute-start | bytes 196616 | tf_op jit(solution)/shard_map/ppermute | solution.py:226
  40.5 5.0 %collective-permute-start.11 = (f32[1,64,256]{2,1,0:T(8,128)S(1)}, f32[1,64,256]{2,1,0:T(8,128)S(1)}, u32[]{:S(2)}, u32[]{:S(2)}) collective-permute-start(f32[1,64,256]{2,1,0:T(8,128)S(1)} %get-tuple-element.47), channel_id=1, source_target_pairs={{0,2},{1,3},{2,0},{3,1},{4,6},{5,7},{6,4},{7,5},{8,10},{9,11},{10,... | collective-permute-start | bytes 196616 | tf_op jit(solution)/shard_map/ppermute | solution.py:226
  41.0 4.5 %collective-permute-start.12 = (f32[1,64,256]{2,1,0:T(8,128)S(1)}, f32[1,64,256]{2,1,0:T(8,128)S(1)}, u32[]{:S(2)}, u32[]{:S(2)}) collective-permute-start(f32[1,64,256]{2,1,0:T(8,128)S(1)} %get-tuple-element.48), channel_id=1, source_target_pairs={{0,3},{1,0},{2,1},{3,2},{4,7},{5,4},{6,5},{7,6},{8,11},{9,8},{10,9... | collective-permute-start | bytes 196616 | tf_op jit(solution)/shard_map/ppermute | solution.py:226

commit v5 on v4

v5 whole, which is shorter than its diff:
```python
import functools
import math

import jax
import jax.numpy as jnp
import numpy as np
from jax import lax
from jax.experimental import pallas as pl
from jax.experimental.pallas import tpu as pltpu
from jax.sharding import PartitionSpec as P

LAGS = 1024
F_LO = 60
NSAMP = 15000
EPS = 1e-06
LANES = 128
SUBLANES = 8
FINE = 32
VMEM_LIMIT = 48 * 1024 * 1024


def from_behind(block, axis, distance):
    devices = range(lax.axis_size(axis))
    route = [(i - distance, i) for i in devices if i - distance in devices]
    return lax.ppermute(block, axis, route)


def phases(bins, lags):
    turns = np.remainder(np.asarray(bins, np.int64)[:, None] * np.asarray(lags, np.int64)[None, :], NSAMP)
    angle = turns * (2.0 * math.pi / NSAMP)
    return np.stack([np.cos(angle), np.sin(angle)]).astype(np.float32)


def split(value):
    high = value.astype(jnp.bfloat16)
    return high, (value - high.astype(jnp.float32)).astype(jnp.bfloat16)


def bin_power(x):
    x = x.astype(jnp.float32)
    return jnp.sum(x[0] * x[0] + x[1] * x[1], axis=-1, keepdims=True)


def power_kernel(x_ref, out_ref):
    for w in range(x_ref.shape[0]):
        out_ref[w] = bin_power(x_ref[w])


def whiten_kernel(n_bins, x_ref, *refs):
    out_ref = refs[-1]
    for w in range(x_ref.shape[0]):
        power = bin_power(x_ref[w])
        for ref in refs[:-1]:
            power = power + ref[w]
        scale = lax.rsqrt(power / n_bins + EPS)
        for part in range(2):
            out_ref[w, part] = (x_ref[w, part].astype(jnp.float32) * scale).astype(jnp.bfloat16)


def table_kernel(groups, place_ref, coarse_ref, fine_ref, high_ref, low_ref):
    f_dev = high_ref.shape[0] // 2
    width = high_ref.shape[1] // groups
    start, place = place_ref[0], place_ref[1]
    for owner in range(groups):
        lags = slice(owner * width, (owner + 1) * width)
        to = pl.ds(pl.multiple_of((owner + groups - place) % groups * width, LANES), width)
        fine_cos = fine_ref[0, :, lags]
        fine_sin = fine_ref[1, :, lags]

        def body(step, carry):
            first = pl.multiple_of(start + step * SUBLANES, SUBLANES)
            coarse_cos = coarse_ref[0, pl.ds(first, SUBLANES), lags]
            coarse_sin = coarse_ref[1, pl.ds(first, SUBLANES), lags]
            for n in range(SUBLANES):
                cos_a, sin_a = coarse_cos[n:n + 1], coarse_sin[n:n + 1]
                rows = pl.multiple_of((step * SUBLANES + n) * FINE, FINE)
                high, low = split(cos_a * fine_cos - sin_a * fine_sin)
                high_ref[pl.ds(rows, FINE), to] = high
                low_ref[pl.ds(rows, FINE), to] = low
                high, low = split(-(cos_a * fine_sin + sin_a * fine_cos))
                high_ref[pl.ds(f_dev + rows, FINE), to] = high
                low_ref[pl.ds(f_dev + rows, FINE), to] = low
            return carry

        lax.fori_loop(0, f_dev // (FINE * SUBLANES), body, 0)


def cross_tile(own_ref, partner_ref, lanes):
    w_dev, _, ch, _ = own_ref.shape
    real = [None] * ch
    imag = [None] * ch
    for w in range(w_dev):
        partner_re = partner_ref[w, 0, :, lanes].astype(jnp.float32)
        partner_im = partner_ref[w, 1, :, lanes].astype(jnp.float32)
        for i in range(ch):
            own_re = own_ref[w, 0, i:i + 1, lanes]
            own_im = own_ref[w, 1, i:i + 1, lanes]
            re = own_re * partner_re + own_im * partner_im
            im = own_im * partner_re - own_re * partner_im
            real[i] = re if w == 0 else real[i] + re
            imag[i] = im if w == 0 else imag[i] + im
    return real, imag


def pairs_kernel(n_partners, groups, keep_ref, base_ref, *refs):
    partner_refs = refs[:n_partners]
    high_ref, low_ref = refs[n_partners:n_partners + 2]
    own_ref, rows_ref = refs[-2:]
    out_refs = refs[-2 - groups:-2]
    w_dev, _, ch, f_dev = base_ref.shape
    pairs = ch * ch
    width = out_refs[0].shape[-1]
    for w in range(w_dev):
        kept = keep_ref[w].astype(jnp.float32)
        for part in range(2):
            own_ref[w, part] = base_ref[w, part].astype(jnp.float32) * kept
    dot = functools.partial(jnp.dot, preferred_element_type=jnp.float32)
    for k, partner_ref in enumerate(partner_refs):

        def body(tile, carry):
            start = pl.multiple_of(tile * LANES, LANES)
            crosses = cross_tile(own_ref, partner_ref, pl.ds(start, LANES))
            for part in range(2):
                lanes = pl.ds(pl.multiple_of(part * f_dev + start, LANES), LANES)
                for i in range(0, ch, 2):
                    high, low = split(jnp.concatenate(crosses[part][i:i + 2], axis=0))
                    rows_ref[i * ch:(i + 2) * ch, lanes] = high
                    rows_ref[pairs + i * ch:pairs + (i + 2) * ch, lanes] = low
            return carry

        lax.fori_loop(0, f_dev // LANES, body, 0)
        both = dot(rows_ref[...], high_ref[...])
        total = both[:pairs] + both[pairs:] + dot(rows_ref[:pairs], low_ref[...])
        for turn, out_ref in enumerate(out_refs):
            out_ref[k] = total[:, turn * width:(turn + 1) * width]


def combine_kernel(scale, order, groups, mask_ref, *refs):
    out_ref = refs[-1]
    ch = out_ref.shape[0]
    start = 0
    for place in range(0, len(refs) - 1, groups):
        parts = refs[place:place + groups]
        for n in range(parts[0].shape[0]):
            k = order[start + n]
            total = parts[0][n]
            for ref in parts[1:]:
                total = total + ref[n]
            for i in range(ch):
                factor = mask_ref[i, k].astype(jnp.float32) * scale
                out_ref[i, k] = total[i * ch:(i + 1) * ch] * factor
        start += parts[0].shape[0]


VMEM = pl.BlockSpec(memory_space=pltpu.VMEM)
SMEM = pl.BlockSpec(memory_space=pltpu.SMEM)


def local(spectra, keep, pair_mask):
    w_dev, _, ch, f_dev = spectra.shape
    reach = pair_mask.shape[1] - 1
    n_chan, n_win, n_freq = (lax.axis_size(a) for a in ("chan", "win", "freq"))
    groups = n_win * n_freq
    width = LAGS // groups
    n_bins = f_dev * n_freq
    params = pltpu.CompilerParams(vmem_limit_bytes=VMEM_LIMIT)
    freq = lax.axis_index("freq")
    place = lax.axis_index(("win", "freq"))

    def whiten(block, others):
        return pl.pallas_call(
            functools.partial(whiten_kernel, n_bins),
            out_shape=jax.ShapeDtypeStruct(block.shape, jnp.bfloat16),
            in_specs=[VMEM] * (1 + len(others)), out_specs=VMEM, compiler_params=params,
        )(block, *others)

    raw = from_behind(spectra, "chan", -1)
    power = pl.pallas_call(
        power_kernel,
        out_shape=jax.ShapeDtypeStruct((w_dev, ch, 1), jnp.float32),
        in_specs=[VMEM], out_specs=VMEM, compiler_params=params,
    )(spectra)
    own_power, next_power = [], []
    for turn in range(1, n_freq):
        route = [(f, (f + turn) % n_freq) for f in range(n_freq)]
        own_power.append(lax.ppermute(power, "freq", route))
        route = [(c * n_freq + f, (c - 1) * n_freq + to) for c in range(1, n_chan) for f, to in route]
        next_power.append(lax.ppermute(power, ("chan", "freq"), route))
    white = whiten(spectra, own_power)
    moving = whiten(raw, next_power)

    lags = np.arange(LAGS) - LAGS // 2
    coarse = jnp.asarray(phases(np.arange(0, n_bins, FINE), lags))
    fine = jnp.asarray(phases(F_LO + np.arange(FINE), lags))
    places = jnp.stack([freq * (f_dev // FINE), place]).astype(jnp.int32)
    high, low = pl.pallas_call(
        functools.partial(table_kernel, groups),
        out_shape=[jax.ShapeDtypeStruct((2 * f_dev, LAGS), jnp.bfloat16)] * 2,
        in_specs=[SMEM] + [VMEM] * 2, out_specs=[VMEM] * 2, compiler_params=params,
    )(places, coarse, fine)

    def pairs(base, partners):
        n = len(partners)
        flops = n * 6 * ch * ch * 2 * f_dev * LAGS
        return pl.pallas_call(
            functools.partial(pairs_kernel, n, groups),
            out_shape=[jax.ShapeDtypeStruct((n, ch * ch, width), jnp.float32)] * groups,
            in_specs=[SMEM] + [VMEM] * (n + 3), out_specs=[VMEM] * groups,
            scratch_shapes=[
                pltpu.VMEM(base.shape, jnp.float32),
                pltpu.VMEM((2 * ch * ch, 2 * f_dev), jnp.bfloat16),
            ],
            compiler_params=params,
            cost_estimate=pl.CostEstimate(flops=flops, bytes_accessed=2 ** 22, transcendentals=0),
        )(keep, base, *partners, high, low)

    def exchange(parts):
        received = [parts[0]]
        for turn in range(1, groups):
            route = [(g, (g + turn) % groups) for g in range(groups)]
            received.append(lax.ppermute(parts[turn], ("win", "freq"), route))
        return received

    parts = pairs(white, [white, moving])
    received = []
    for step in range(1, reach):
        moving = from_behind(moving, "chan", -1)
        moving, parts = lax.optimization_barrier((moving, parts))
        received += exchange(parts)
        parts = pairs(white, [moving])
    received += exchange(parts)
    scale = 1.0 / math.sqrt(w_dev * n_win * n_bins)
    return pl.pallas_call(
        functools.partial(combine_kernel, scale, list(range(reach + 1)), groups),
        out_shape=jax.ShapeDtypeStruct((ch, reach + 1, ch, width), jnp.float32),
        in_specs=[SMEM] + [VMEM] * len(received), out_specs=VMEM, compiler_params=params,
    )(pair_mask, *received)


def solution(mesh):
    in_specs = (
        P("win", None, ("fibre", "chan"), "freq"),
        P(("fibre", "win")),
        P(("fibre", "chan"), None),
    )
    out_specs = P(("fibre", "chan"), None, None, ("win", "freq"))
    return jax.shard_map(local, mesh=mesh, in_specs=in_specs, out_specs=out_specs, check_vma=False)
```

time: 47.5 us -> 54.3 us (1.14)
  Pallas kernels: 15.7 us -> 22.3 us
  blocking collectives: 3.67 us -> 0 us
  waiting for transfers between devices: 9.27 us -> 12.7 us
    ppermute x0 -> x2, waiting for transfers between devices: none -> 7.12 us  [the longest x1 7.12 us: local(): next_power.append(lax.ppermute(power, ('chan', 'freq'), route))]
    pallas_call x4, Pallas kernels: 14 us -> 20.4 us  [the longest x3 15.3 us: pairs(): pl.pallas_call(functools.partial(pairs_kernel, n, groups), out_shape=[jax...]
    ppermute x4 -> x3, waiting for transfers between devices: 6.22 us -> 2.54 us  [from_behind(): return lax.ppermute(block, axis, route)]
    psum x1 -> x0, blocking collectives: 3.67 us -> none  [local(): power = lax.psum(power, 'freq')]
    ppermute x0 -> x2, starting transfers between devices: none -> 1.8 us  [the longest x1 1.28 us: local(): next_power.append(lax.ppermute(power, ('chan', 'freq'), route))]
    unnamed x11 -> x13, local copies, waits for them, and re-layouts: 2.82 us -> 4.62 us
    ppermute x4 -> x3, starting transfers between devices: 5.16 us -> 3.86 us  [from_behind(): return lax.ppermute(block, axis, route)]
    squeeze x1 -> x0, local copies, waits for them, and re-layouts: 0.85 us -> none  [local(): lax.dynamic_index_in_dim(jnp.asarray(coarse), freq, 1, keepdims=False)]
  transfers between devices with their start and end apart: 13 -> 14, of which waited for: 5 -> 6; matrix products, arithmetic and copies ran while one was open for 4% -> 0% of each run, Pallas kernels for 30% -> 39%
where the time goes in v5:
time: 54.3 us; the launch traced here: 53.7 us
  Pallas kernels  22.3 us (41%)
  starting transfers between devices  13.9 us (26%)
  waiting for transfers between devices  12.7 us (23%)
  local copies, waits for them, and re-layouts  4.62 us (9%)
    pallas_call x3, Pallas kernels, pairs(): pl.pallas_call(functools.partial(pairs_kernel, n, groups), out_shape=[jax...  15.3 us
    ppermute x9, starting transfers between devices, exchange(): received.append(lax.ppermute(parts[turn], ('win', 'freq'), route))  8.19 us
    ppermute x1, waiting for transfers between devices, local(): next_power.append(lax.ppermute(power, ('chan', 'freq'), route))  7.12 us
    pallas_call x1, Pallas kernels, local(): pl.pallas_call(functools.partial(table_kernel, groups), out_shape=[jax.Sh...  5.09 us
    unnamed x13, local copies, waits for them, and re-layouts  4.62 us
    ppermute x3, starting transfers between devices, from_behind(): return lax.ppermute(block, axis, route)  3.86 us
    ppermute x9, waiting for transfers between devices, exchange(): received.append(lax.ppermute(parts[turn], ('win', 'freq'), route))  3.05 us
    ppermute x3, waiting for transfers between devices, from_behind(): return lax.ppermute(block, axis, route)  2.54 us
  transfers between devices with their start and end apart: 14, of which 6 were waited for; matrix products, arithmetic and copies ran while one was open for 0% of the time, Pallas kernels for 39%

profile of v5, /device:TPU:0, one launch (start us, length us, event | category | flops | bytes accessed | tf_op | source)
XLA Modules:
  0.0 53.7 jit_solution(307508649760122195)
XLA Ops:
  0.0 1.3 %collective-permute-start = (bf16[8,2,8,1024]{3,2,1,0:T(8,128)(2,1)}, bf16[8,2,8,1024]{3,2,1,0:T(8,128)(2,1)S(1)}, u32[]{:S(2)}, u32[]{:S(2)}) collective-permute-start(bf16[8,2,8,1024]{3,2,1,0:T(8,128)(2,1)} %x_ref.3), channel_id=1, source_target_pairs={{4,0},{8,4},{12,8},{5,1},{9,5},{13,9},{6,2},{10,6},{14,10},{7,3},{... | collective-permute-start | bytes 786440 | tf_op jit(solution)/shard_map/ppermute | solution.py:25
  1.3 0.0 copy-start
  1.3 0.9 %copy-done = bf16[8,2,8,1024]{3,2,1,0:T(8,128)(2,1)S(1)} copy-done((bf16[8,2,8,1024]{3,2,1,0:T(8,128)(2,1)S(1)}, bf16[8,2,8,1024]{3,2,1,0:T(8,128)(2,1)}, u32[]{:S(2)}) %copy-start) | copy-done | bytes 262168
  2.2 0.1 shard_map.55
  2.4 1.3 %collective-permute-start.1 = (f32[8,8,1]{2,1,0:T(8,128)S(1)}, f32[8,8,1]{2,1,0:T(8,128)S(1)}, u32[]{:S(2)}, u32[]{:S(2)}) collective-permute-start(f32[8,8,1]{2,1,0:T(8,128)S(1)} %shard_map.55), channel_id=1, source_target_pairs={{4,1},{5,0},{8,5},{9,4},{12,9},{13,8},{6,3},{7,2},{10,7},{11,6},{1... | collective-permute-start | bytes 776 | tf_op jit(solution)/shard_map/ppermute | solution.py:188
  3.7 0.5 collective-permute-start.3
  4.2 7.1 %collective-permute-done.1.refs_0_ = f32[8,8,1]{2,1,0:T(8,128)S(1)} collective-permute-done((f32[8,8,1]{2,1,0:T(8,128)S(1)}, f32[8,8,1]{2,1,0:T(8,128)S(1)}, u32[]{:S(2)}, u32[]{:S(2)}) %collective-permute-start.1) | collective-permute-done | bytes 288 | tf_op jit(solution)/shard_map/ppermute | solution.py:188
  11.3 0.5 collective-permute-done.x_ref
  11.8 0.2 shard_map.56.refs_1_
  12.0 1.3 %collective-permute-start.2 = (bf16[8,2,8,1024]{3,2,1,0:T(8,128)(2,1)S(1)}, bf16[8,2,8,1024]{3,2,1,0:T(8,128)(2,1)S(1)}, u32[]{:S(2)}, u32[]{:S(2)}) collective-permute-start(bf16[8,2,8,1024]{3,2,1,0:T(8,128)(2,1)S(1)} %shard_map.56.refs_1_), channel_id=1, source_target_pairs={{4,0},{8,4},{12,8},{5,1},{9,5},{13,9},{6,2},{10,6},{14,10},{7,3},{... | collective-permute-start | bytes 786440 | tf_op jit(solution)/shard_map/ppermute | solution.py:25
  13.3 0.1 pad_add_fusion.place_ref
  13.4 0.0 copy-start.2
  13.4 1.0 %copy-done.2 = f32[2,64,1024]{2,1,0:T(8,128)S(1)} copy-done((f32[2,64,1024]{2,1,0:T(8,128)S(1)}, f32[2,64,1024]{2,1,0:T(8,128)}, u32[]{:S(2)}) %copy-start.2) | copy-done | bytes 524312
  14.4 0.0 copy-start.3
  14.4 0.9 %copy-done.3 = f32[2,32,1024]{2,1,0:T(8,128)S(1)} copy-done((f32[2,32,1024]{2,1,0:T(8,128)S(1)}, f32[2,32,1024]{2,1,0:T(8,128)}, u32[]{:S(2)}) %copy-start.3) | copy-done | bytes 262168
  15.4 5.1 %shard_map.58 = (bf16[2048,1024]{1,0:T(8,128)(2,1)S(1)}, bf16[2048,1024]{1,0:T(8,128)(2,1)}) custom-call(s32[2]{0:T(128)S(1)} %pad_add_fusion.place_ref, f32[2,64,1024]{2,1,0:T(8,128)S(1)} %copy-done.2, f32[2,32,1024]{2,1,0:T(8,128)S(1)} %copy-done.3), custom_call_target="tpu_custom_call" | custom-call | tf_op jit(solution)/shard_map/pallas_call | solution.py:196
  20.5 0.0 collective-permute-done.3.refs_0_
  20.5 0.9 %copy-done.1 = bf16[8,2,8,1024]{3,2,1,0:T(8,128)(2,1)S(1)} copy-done((bf16[8,2,8,1024]{3,2,1,0:T(8,128)(2,1)S(1)}, bf16[8,2,8,1024]{3,2,1,0:T(8,128)(2,1)}, u32[]{:S(2)}) %copy-start.1) | copy-done | bytes 262168
  21.4 0.2 shard_map.57.base_ref.refs_0_
  21.7 0.0 copy-start.4
  21.7 0.6 %copy-done.4 = s32[8]{0:T(128)S(1)} copy-done((s32[8]{0:T(128)S(1)}, s32[8]{0:T(128)}, u32[]{:S(2)}) %copy-start.4) | copy-done | bytes 56
  22.3 6.5 %shard_map.59 = (f32[2,64,256]{2,1,0:T(8,128)S(1)}, f32[2,64,256]{2,1,0:T(8,128)S(1)}, f32[2,64,256]{2,1,0:T(8,128)S(1)}, f32[2,64,256]{2,1,0:T(8,128)S(1)}) custom-call(s32[8]{0:T(128)S(1)} %copy-done.4, bf16[8,2,8,1024]{3,2,1,0:T(8,128)(2,1)S(1)} %shard_map.57.base_ref.refs_0_, bf16[8,2,8,1024]{3,2,1,0:T(8,128)(2,1)S(1)} %shard_map.57.base_ref.refs_0_, ...), custom_call_target="tpu_custom_call" | custom-call | flops 1610612736 | bytes 4194304 | tf_op jit(solution)/shard_map/pallas_call | solution.py:205
  28.9 0.0 collective-permute-done.2.refs_0_
  28.9 1.3 %collective-permute-start.7 = (bf16[8,2,8,1024]{3,2,1,0:T(8,128)(2,1)S(1)}, bf16[8,2,8,1024]{3,2,1,0:T(8,128)(2,1)S(1)}, u32[]{:S(2)}, u32[]{:S(2)}) collective-permute-start(bf16[8,2,8,1024]{3,2,1,0:T(8,128)(2,1)S(1)} %collective-permute-done.2.refs_0_), channel_id=1, source_target_pairs={{4,0},{8,4},{12,8},{5,1},{9,5},{13,9},{6,2},{10,6},{14,10},{7,3},{... | collective-permute-start | bytes 786440 | tf_op jit(solution)/shard_map/ppermute | solution.py:25
  30.2 0.2 collective-permute-start.4
  30.4 1.7 %collective-permute-start.5 = (f32[2,64,256]{2,1,0:T(8,128)S(1)}, f32[2,64,256]{2,1,0:T(8,128)S(1)}, u32[]{:S(2)}, u32[]{:S(2)}) collective-permute-start(f32[2,64,256]{2,1,0:T(8,128)S(1)} %get-tuple-element.37), channel_id=1, source_target_pairs={{0,2},{1,3},{2,0},{3,1},{4,6},{5,7},{6,4},{7,5},{8,10},{9,11},{10,... | collective-permute-start | bytes 393224 | tf_op jit(solution)/shard_map/ppermute | solution.py:221
  32.1 1.3 %collective-permute-start.6 = (f32[2,64,256]{2,1,0:T(8,128)S(1)}, f32[2,64,256]{2,1,0:T(8,128)S(1)}, u32[]{:S(2)}, u32[]{:S(2)}) collective-permute-start(f32[2,64,256]{2,1,0:T(8,128)S(1)} %get-tuple-element.38), channel_id=1, source_target_pairs={{0,3},{1,0},{2,1},{3,2},{4,7},{5,4},{6,5},{7,6},{8,11},{9,8},{10,9... | collective-permute-start | bytes 393224 | tf_op jit(solution)/shard_map/ppermute | solution.py:221
  33.3 4.4 %shard_map.60 = (f32[1,64,256]{2,1,0:T(8,128)S(1)}, f32[1,64,256]{2,1,0:T(8,128)S(1)}, f32[1,64,256]{2,1,0:T(8,128)S(1)}, f32[1,64,256]{2,1,0:T(8,128)S(1)}) custom-call(s32[8]{0:T(128)S(1)} %copy-done.4, bf16[8,2,8,1024]{3,2,1,0:T(8,128)(2,1)S(1)} %shard_map.57.base_ref.refs_0_, bf16[8,2,8,1024]{3,2,1,0:T(8,128)(2,1)S(1)} %collective-permute-done.2.refs_0_, ...), custom_call_target="tpu_custom_call" | custom-call | flops 805306368 | bytes 4194304 | tf_op jit(solution)/shard_map/pallas_call | solution.py:205
  37.7 2.1 %collective-permute-done.7.refs_0_ = bf16[8,2,8,1024]{3,2,1,0:T(8,128)(2,1)S(1)} collective-permute-done((bf16[8,2,8,1024]{3,2,1,0:T(8,128)(2,1)S(1)}, bf16[8,2,8,1024]{3,2,1,0:T(8,128)(2,1)S(1)}, u32[]{:S(2)}, u32[]{:S(2)}) %collective-permute-start.7) | collective-permute-done | bytes 262176 | tf_op jit(solution)/shard_map/ppermute | solution.py:25
  39.8 0.0 collective-permute-start.8
  39.8 1.7 %collective-permute-start.9 = (f32[1,64,256]{2,1,0:T(8,128)S(1)}, f32[1,64,256]{2,1,0:T(8,128)S(1)}, u32[]{:S(2)}, u32[]{:S(2)}) collective-permute-start(f32[1,64,256]{2,1,0:T(8,128)S(1)} %get-tuple-element.46), channel_id=1, source_target_pairs={{0,2},{1,3},{2,0},{3,1},{4,6},{5,7},{6,4},{7,5},{8,10},{9,11},{10,... | collective-permute-start | bytes 196616 | tf_op jit(solution)/shard_map/ppermute | solution.py:221
  41.5 4.4 %shard_map.61 = (f32[1,64,256]{2,1,0:T(8,128)S(1)}, f32[1,64,256]{2,1,0:T(8,128)S(1)}, f32[1,64,256]{2,1,0:T(8,128)S(1)}, f32[1,64,256]{2,1,0:T(8,128)S(1)}) custom-call(s32[8]{0:T(128)S(1)} %copy-done.4, bf16[8,2,8,1024]{3,2,1,0:T(8,128)(2,1)S(1)} %shard_map.57.base_ref.refs_0_, bf16[8,2,8,1024]{3,2,1,0:T(8,128)(2,1)S(1)} %collective-permute-done.7.refs_0_, ...), custom_call_target="tpu_custom_call" | custom-call | flops 805306368 | bytes 4194304 | tf_op jit(solution)/shard_map/pallas_call | solution.py:205
  45.9 0.0 collective-permute-done.4.refs_1_
  45.9 1.5 %collective-permute-start.10 = (f32[1,64,256]{2,1,0:T(8,128)S(1)}, f32[1,64,256]{2,1,0:T(8,128)S(1)}, u32[]{:S(2)}, u32[]{:S(2)}) collective-permute-start(f32[1,64,256]{2,1,0:T(8,128)S(1)} %get-tuple-element.47), channel_id=1, source_target_pairs={{0,3},{1,0},{2,1},{3,2},{4,7},{5,4},{6,5},{7,6},{8,11},{9,8},{10,9... | collective-permute-start | bytes 196616 | tf_op jit(solution)/shard_map/ppermute | solution.py:221
  47.4 0.0 collective-permute-done.5.refs_2_
  47.4 0.0 collective-permute-start.11
  47.4 0.0 collective-permute-done.6.refs_3_
  47.4 0.5 collective-permute-start.12
  47.8 0.0 collective-permute-done.8.refs_5_
  47.8 1.4 %collective-permute-start.13 = (f32[1,64,256]{2,1,0:T(8,128)S(1)}, f32[1,64,256]{2,1,0:T(8,128)S(1)}, u32[]{:S(2)}, u32[]{:S(2)}) collective-permute-start(f32[1,64,256]{2,1,0:T(8,128)S(1)} %get-tuple-element.52), channel_id=1, source_target_pairs={{0,3},{1,0},{2,1},{3,2},{4,7},{5,4},{6,5},{7,6},{8,11},{9,8},{10,9... | collective-permute-start | bytes 196616 | tf_op jit(solution)/shard_map/ppermute | solution.py:221
  49.2 0.0 copy-done.5
  49.2 0.1 copy.6.mask_ref
  49.3 0.0 collective-permute-done.9.refs_6_
  49.3 0.3 collective-permute-done.10.refs_7_
  49.7 1.5 %collective-permute-done.11.refs_9_ = f32[1,64,256]{2,1,0:T(8,128)S(1)} collective-permute-done((f32[1,64,256]{2,1,0:T(8,128)S(1)}, f32[1,64,256]{2,1,0:T(8,128)S(1)}, u32[]{:S(2)}, u32[]{:S(2)}) %collective-permute-start.11) | collective-permute-done | bytes 65568 | tf_op jit(solution)/shard_map/ppermute | solution.py:221
  51.2 1.2 %collective-permute-done.12.refs_10_ = f32[1,64,256]{2,1,0:T(8,128)S(1)} collective-permute-done((f32[1,64,256]{2,1,0:T(8,128)S(1)}, f32[1,64,256]{2,1,0:T(8,128)S(1)}, u32[]{:S(2)}, u32[]{:S(2)}) %collective-permute-start.12) | collective-permute-done | bytes 65568 | tf_op jit(solution)/shard_map/ppermute | solution.py:221
  52.4 0.0 collective-permute-done.13.refs_11_
  52.4 1.4 %shard_map.62 = f32[8,4,8,256]{3,2,1,0:T(8,128)} custom-call(s32[8,4]{1,0:T(8,128)S(1)} %copy.6.mask_ref, f32[2,64,256]{2,1,0:T(8,128)S(1)} %get-tuple-element.35.refs_0_, f32[2,64,256]{2,1,0:T(8,128)S(1)} %collective-permute-done.4.refs_1_, f32[2,64,256]{2,1,0:T(8,128)S(1)} %collective-permute-done.5.refs_2_, ...), custom_call_target="tpu_custom_call" | custom-call | tf_op jit(solution)/shard_map/pallas_call | solution.py:233
  (2 shorter events, 0.0 us)
Async XLA Ops:
  0.0 11.8 %collective-permute-start = (bf16[8,2,8,1024]{3,2,1,0:T(8,128)(2,1)}, bf16[8,2,8,1024]{3,2,1,0:T(8,128)(2,1)S(1)}, u32[]{:S(2)}, u32[]{:S(2)}) collective-permute-start(bf16[8,2,8,1024]{3,2,1,0:T(8,128)(2,1)} %x_ref.3), channel_id=1, source_target_pairs={{4,0},{8,4},{12,8},{5,1},{9,5},{13,9},{6,2},{10,6},{14,10},{7,3},{... | collective-permute-start | bytes 786440 | tf_op jit(solution)/shard_map/ppermute | solution.py:25
  1.3 1.0 %copy-start = (bf16[8,2,8,1024]{3,2,1,0:T(8,128)(2,1)S(1)}, bf16[8,2,8,1024]{3,2,1,0:T(8,128)(2,1)}, u32[]{:S(2)}) copy-start(bf16[8,2,8,1024]{3,2,1,0:T(8,128)(2,1)} %x_ref.3) | copy-start | bytes 786436
  2.4 8.9 %collective-permute-start.1 = (f32[8,8,1]{2,1,0:T(8,128)S(1)}, f32[8,8,1]{2,1,0:T(8,128)S(1)}, u32[]{:S(2)}, u32[]{:S(2)}) collective-permute-start(f32[8,8,1]{2,1,0:T(8,128)S(1)} %shard_map.55), channel_id=1, source_target_pairs={{4,1},{5,0},{8,5},{9,4},{12,9},{13,8},{6,3},{7,2},{10,7},{11,6},{1... | collective-permute-start | bytes 776 | tf_op jit(solution)/shard_map/ppermute | solution.py:188
  3.7 16.8 %collective-permute-start.3 = (f32[8,8,1]{2,1,0:T(8,128)S(1)}, f32[8,8,1]{2,1,0:T(8,128)S(1)}, u32[]{:S(2)}, u32[]{:S(2)}) collective-permute-start(f32[8,8,1]{2,1,0:T(8,128)S(1)} %shard_map.55), channel_id=1, source_target_pairs={{0,1},{1,0},{2,3},{3,2},{4,5},{5,4},{6,7},{7,6},{8,9},{9,8},{10,11... | collective-permute-start | bytes 776 | tf_op jit(solution)/shard_map/ppermute | solution.py:186
  12.0 16.8 %collective-permute-start.2 = (bf16[8,2,8,1024]{3,2,1,0:T(8,128)(2,1)S(1)}, bf16[8,2,8,1024]{3,2,1,0:T(8,128)(2,1)S(1)}, u32[]{:S(2)}, u32[]{:S(2)}) collective-permute-start(bf16[8,2,8,1024]{3,2,1,0:T(8,128)(2,1)S(1)} %shard_map.56.refs_1_), channel_id=1, source_target_pairs={{4,0},{8,4},{12,8},{5,1},{9,5},{13,9},{6,2},{10,6},{14,10},{7,3},{... | collective-permute-start | bytes 786440 | tf_op jit(solution)/shard_map/ppermute | solution.py:25
  13.4 1.0 %copy-start.2 = (f32[2,64,1024]{2,1,0:T(8,128)S(1)}, f32[2,64,1024]{2,1,0:T(8,128)}, u32[]{:S(2)}) copy-start(f32[2,64,1024]{2,1,0:T(8,128)} %constant.14.clone.coarse_ref) | copy-start | bytes 1572868
  14.4 0.9 %copy-start.3 = (f32[2,32,1024]{2,1,0:T(8,128)S(1)}, f32[2,32,1024]{2,1,0:T(8,128)}, u32[]{:S(2)}) copy-start(f32[2,32,1024]{2,1,0:T(8,128)} %constant.15.clone.fine_ref) | copy-start | bytes 786436
  20.5 1.0 %copy-start.1 = (bf16[8,2,8,1024]{3,2,1,0:T(8,128)(2,1)S(1)}, bf16[8,2,8,1024]{3,2,1,0:T(8,128)(2,1)}, u32[]{:S(2)}) copy-start(bf16[8,2,8,1024]{3,2,1,0:T(8,128)(2,1)} %x_ref.3) | copy-start | bytes 786436
  21.7 0.7 %copy-start.4 = (s32[8]{0:T(128)S(1)}, s32[8]{0:T(128)}, u32[]{:S(2)}) copy-start(s32[8]{0:T(128)} %keep_ref.5) | copy-start | bytes 100
  28.9 10.9 %collective-permute-start.7 = (bf16[8,2,8,1024]{3,2,1,0:T(8,128)(2,1)S(1)}, bf16[8,2,8,1024]{3,2,1,0:T(8,128)(2,1)S(1)}, u32[]{:S(2)}, u32[]{:S(2)}) collective-permute-start(bf16[8,2,8,1024]{3,2,1,0:T(8,128)(2,1)S(1)} %collective-permute-done.2.refs_0_), channel_id=1, source_target_pairs={{4,0},{8,4},{12,8},{5,1},{9,5},{13,9},{6,2},{10,6},{14,10},{7,3},{... | collective-permute-start | bytes 786440 | tf_op jit(solution)/shard_map/ppermute | solution.py:25
  30.2 15.7 %collective-permute-start.4 = (f32[2,64,256]{2,1,0:T(8,128)S(1)}, f32[2,64,256]{2,1,0:T(8,128)S(1)}, u32[]{:S(2)}, u32[]{:S(2)}) collective-permute-start(f32[2,64,256]{2,1,0:T(8,128)S(1)} %get-tuple-element.36), channel_id=1, source_target_pairs={{0,1},{1,2},{2,3},{3,0},{4,5},{5,6},{6,7},{7,4},{8,9},{9,10},{10,1... | collective-permute-start | bytes 393224 | tf_op jit(solution)/shard_map/ppermute | solution.py:221
  30.4 17.0 %collective-permute-start.5 = (f32[2,64,256]{2,1,0:T(8,128)S(1)}, f32[2,64,256]{2,1,0:T(8,128)S(1)}, u32[]{:S(2)}, u32[]{:S(2)}) collective-permute-start(f32[2,64,256]{2,1,0:T(8,128)S(1)} %get-tuple-element.37), channel_id=1, source_target_pairs={{0,2},{1,3},{2,0},{3,1},{4,6},{5,7},{6,4},{7,5},{8,10},{9,11},{10,... | collective-permute-start | bytes 393224 | tf_op jit(solution)/shard_map/ppermute | solution.py:221
  32.1 15.3 %collective-permute-start.6 = (f32[2,64,256]{2,1,0:T(8,128)S(1)}, f32[2,64,256]{2,1,0:T(8,128)S(1)}, u32[]{:S(2)}, u32[]{:S(2)}) collective-permute-start(f32[2,64,256]{2,1,0:T(8,128)S(1)} %get-tuple-element.38), channel_id=1, source_target_pairs={{0,3},{1,0},{2,1},{3,2},{4,7},{5,4},{6,5},{7,6},{8,11},{9,8},{10,9... | collective-permute-start | bytes 393224 | tf_op jit(solution)/shard_map/ppermute | solution.py:221
  39.8 9.4 %copy-start.5 = (s32[8,4]{0,1:T(4,128)S(1)}, s32[8,4]{0,1:T(4,128)}, u32[]{:S(2)}) copy-start(s32[8,4]{0,1:T(4,128)} %param.7) | copy-start | bytes 388
  39.8 8.0 %collective-permute-start.8 = (f32[1,64,256]{2,1,0:T(8,128)S(1)}, f32[1,64,256]{2,1,0:T(8,128)S(1)}, u32[]{:S(2)}, u32[]{:S(2)}) collective-permute-start(f32[1,64,256]{2,1,0:T(8,128)S(1)} %get-tuple-element.45), channel_id=1, source_target_pairs={{0,1},{1,2},{2,3},{3,0},{4,5},{5,6},{6,7},{7,4},{8,9},{9,10},{10,1... | collective-permute-start | bytes 196616 | tf_op jit(solution)/shard_map/ppermute | solution.py:221
  39.8 9.5 %collective-permute-start.9 = (f32[1,64,256]{2,1,0:T(8,128)S(1)}, f32[1,64,256]{2,1,0:T(8,128)S(1)}, u32[]{:S(2)}, u32[]{:S(2)}) collective-permute-start(f32[1,64,256]{2,1,0:T(8,128)S(1)} %get-tuple-element.46), channel_id=1, source_target_pairs={{0,2},{1,3},{2,0},{3,1},{4,6},{5,7},{6,4},{7,5},{8,10},{9,11},{10,... | collective-permute-start | bytes 196616 | tf_op jit(solution)/shard_map/ppermute | solution.py:221
  45.9 3.8 %collective-permute-start.10 = (f32[1,64,256]{2,1,0:T(8,128)S(1)}, f32[1,64,256]{2,1,0:T(8,128)S(1)}, u32[]{:S(2)}, u32[]{:S(2)}) collective-permute-start(f32[1,64,256]{2,1,0:T(8,128)S(1)} %get-tuple-element.47), channel_id=1, source_target_pairs={{0,3},{1,0},{2,1},{3,2},{4,7},{5,4},{6,5},{7,6},{8,11},{9,8},{10,9... | collective-permute-start | bytes 196616 | tf_op jit(solution)/shard_map/ppermute | solution.py:221
  47.4 3.8 %collective-permute-start.11 = (f32[1,64,256]{2,1,0:T(8,128)S(1)}, f32[1,64,256]{2,1,0:T(8,128)S(1)}, u32[]{:S(2)}, u32[]{:S(2)}) collective-permute-start(f32[1,64,256]{2,1,0:T(8,128)S(1)} %get-tuple-element.50), channel_id=1, source_target_pairs={{0,1},{1,2},{2,3},{3,0},{4,5},{5,6},{6,7},{7,4},{8,9},{9,10},{10,1... | collective-permute-start | bytes 196616 | tf_op jit(solution)/shard_map/ppermute | solution.py:221
  47.4 5.0 %collective-permute-start.12 = (f32[1,64,256]{2,1,0:T(8,128)S(1)}, f32[1,64,256]{2,1,0:T(8,128)S(1)}, u32[]{:S(2)}, u32[]{:S(2)}) collective-permute-start(f32[1,64,256]{2,1,0:T(8,128)S(1)} %get-tuple-element.51), channel_id=1, source_target_pairs={{0,2},{1,3},{2,0},{3,1},{4,6},{5,7},{6,4},{7,5},{8,10},{9,11},{10,... | collective-permute-start | bytes 196616 | tf_op jit(solution)/shard_map/ppermute | solution.py:221
  47.8 4.5 %collective-permute-start.13 = (f32[1,64,256]{2,1,0:T(8,128)S(1)}, f32[1,64,256]{2,1,0:T(8,128)S(1)}, u32[]{:S(2)}, u32[]{:S(2)}) collective-permute-start(f32[1,64,256]{2,1,0:T(8,128)S(1)} %get-tuple-element.52), channel_id=1, source_target_pairs={{0,3},{1,0},{2,1},{3,2},{4,7},{5,4},{6,5},{7,6},{8,11},{9,8},{10,9... | collective-permute-start | bytes 196616 | tf_op jit(solution)/shard_map/ppermute | solution.py:221

commit v6 on v5

v6 whole, which is shorter than its diff:
```python
import functools
import math

import jax
import jax.numpy as jnp
import numpy as np
from jax import lax
from jax.experimental import pallas as pl
from jax.experimental.pallas import tpu as pltpu
from jax.sharding import PartitionSpec as P

LAGS = 1024
F_LO = 60
NSAMP = 15000
EPS = 1e-06
LANES = 128
SUBLANES = 8
FINE = 32
BLOCK = 256
VMEM_LIMIT = 16 * 1024 * 1024


def from_behind(block, axis, distance):
    devices = range(lax.axis_size(axis))
    route = [(i - distance, i) for i in devices if i - distance in devices]
    return lax.ppermute(block, axis, route)


def phases(bins, half_lags):
    turns = np.remainder(np.asarray(bins, np.int64)[:, None] * np.asarray(half_lags, np.int64)[None, :], 2 * NSAMP)
    angle = turns * (math.pi / NSAMP)
    return np.stack([np.cos(angle), np.sin(angle)]).astype(np.float32)


def split(value):
    high = value.astype(jnp.bfloat16)
    return high, (value - high.astype(jnp.float32)).astype(jnp.bfloat16)


def bin_power(x):
    x = x.astype(jnp.float32)
    return jnp.sum(x[0] * x[0] + x[1] * x[1], axis=-1, keepdims=True)


def power_kernel(x_ref, power_ref, copy_ref):
    for w in range(x_ref.shape[0]):
        x = x_ref[w]
        power_ref[w] = bin_power(x)
        copy_ref[w] = x


def whiten_kernel(n_bins, x_ref, *refs):
    out_ref = refs[-1]
    for w in range(x_ref.shape[0]):
        power = bin_power(x_ref[w])
        for ref in refs[:-1]:
            power = power + ref[w]
        scale = lax.rsqrt(power / n_bins + EPS)
        for part in range(2):
            out_ref[w, part] = (x_ref[w, part].astype(jnp.float32) * scale).astype(jnp.bfloat16)


def own_kernel(n_bins, keep_ref, x_ref, *refs):
    white_ref, own_ref = refs[-2:]
    whiten_kernel(n_bins, x_ref, *refs[:-2], white_ref)
    for w in range(x_ref.shape[0]):
        own_ref[w] = white_ref[w].astype(jnp.float32) * keep_ref[w].astype(jnp.float32)


def table_kernel(place_ref, base_ref, table_ref):
    f_dev, width = table_ref.shape[1:]
    coarse = base_ref.shape[1] - FINE
    start = place_ref[0] * (f_dev // FINE)
    for block in range(0, width, BLOCK):
        lags = slice(block, block + BLOCK)
        fine_cos = base_ref[0, coarse:, lags]
        fine_sin = base_ref[1, coarse:, lags]

        def body(step, carry):
            first = pl.multiple_of(start + step * SUBLANES, SUBLANES)
            coarse_cos = base_ref[0, pl.ds(first, SUBLANES), lags]
            coarse_sin = base_ref[1, pl.ds(first, SUBLANES), lags]
            for n in range(SUBLANES):
                cos_a, sin_a = coarse_cos[n:n + 1], coarse_sin[n:n + 1]
                rows = pl.ds(pl.multiple_of((step * SUBLANES + n) * FINE, FINE), FINE)
                table_ref[0, rows, lags], table_ref[1, rows, lags] = split(cos_a * fine_cos - sin_a * fine_sin)
                table_ref[2, rows, lags], table_ref[3, rows, lags] = split(cos_a * fine_sin + sin_a * fine_cos)
            return carry

        lax.fori_loop(0, f_dev // (FINE * SUBLANES), body, 0)


def cross_tile(own_ref, partner_ref, lanes):
    w_dev, _, ch, _ = own_ref.shape
    real = [None] * ch
    imag = [None] * ch
    for w in range(w_dev):
        partner_re = partner_ref[w, 0, :, lanes].astype(jnp.float32)
        partner_im = partner_ref[w, 1, :, lanes].astype(jnp.float32)
        for i in range(ch):
            own_re = own_ref[w, 0, i:i + 1, lanes]
            own_im = own_ref[w, 1, i:i + 1, lanes]
            re = own_re * partner_re + own_im * partner_im
            im = own_im * partner_re - own_re * partner_im
            real[i] = re if w == 0 else real[i] + re
            imag[i] = im if w == 0 else imag[i] + im
    return real, imag


def pairs_kernel(n_partners, groups, place_ref, own_ref, *refs):
    partner_refs = refs[:n_partners]
    twist_ref, table_ref = refs[n_partners:n_partners + 2]
    rows_ref, sums_ref = refs[-2:]
    out_refs = refs[-2 - groups:-2]
    ch, f_dev = own_ref.shape[2:]
    pairs = ch * ch
    width = out_refs[0].shape[-1]
    freq, place = place_ref[0], place_ref[1]
    dot = functools.partial(jnp.dot, preferred_element_type=jnp.float32)
    for k, partner_ref in enumerate(partner_refs):

        def body(tile, carry):
            lanes = pl.ds(pl.multiple_of(tile * LANES, LANES), LANES)
            real, imag = cross_tile(own_ref, partner_ref, lanes)
            cos = twist_ref[freq, 0:1, lanes]
            sin = twist_ref[freq, 1:2, lanes]
            for i in range(0, ch, 2):
                re = jnp.concatenate(real[i:i + 2], axis=0)
                im = jnp.concatenate(imag[i:i + 2], axis=0)
                for part, value in enumerate((re * cos + im * sin, im * cos - re * sin)):
                    high, low = split(value)
                    rows_ref[part, i * ch:(i + 2) * ch, lanes] = high
                    rows_ref[part, pairs + i * ch:pairs + (i + 2) * ch, lanes] = low
            return carry

        lax.fori_loop(0, f_dev // LANES, body, 0)
        for part in range(2):
            both = dot(rows_ref[part], table_ref[2 * part])
            sums_ref[part] = both[:pairs] + both[pairs:] + dot(rows_ref[part, :pairs], table_ref[2 * part + 1])
        for turn, out_ref in enumerate(out_refs):
            owner = (place + turn) % groups
            upper = owner >= groups // 2
            block = jnp.where(upper, owner - groups // 2, groups // 2 - 1 - owner)
            sign = jnp.where(upper, -1.0, 1.0)
            lags = pl.ds(pl.multiple_of(block * width, LANES), width)
            out_ref[k] = sums_ref[0, :, lags] + sign * sums_ref[1, :, lags]


def reverse_lanes(value):
    backward = LANES - 1 - lax.broadcasted_iota(jnp.int32, (value.shape[0], LANES), 1)
    pieces = [
        jnp.take_along_axis(value[:, start:start + LANES], backward, axis=1, mode="promise_in_bounds")
        for start in range(0, value.shape[1], LANES)
    ]
    return jnp.concatenate(pieces[::-1], axis=1)


def combine_kernel(scale, groups, mask_ref, place_ref, *refs):
    out_ref = refs[-1]
    ch = out_ref.shape[0]
    lower = place_ref[1] < groups // 2
    k = 0
    for first in range(0, len(refs) - 1, groups):
        parts = refs[first:first + groups]
        for n in range(parts[0].shape[0]):
            total = parts[0][n]
            for ref in parts[1:]:
                total = total + ref[n]
            total = jnp.where(lower, reverse_lanes(total), total)
            for i in range(ch):
                factor = mask_ref[i, k].astype(jnp.float32) * scale
                out_ref[i, k] = total[i * ch:(i + 1) * ch] * factor
            k += 1


VMEM = pl.BlockSpec(memory_space=pltpu.VMEM)
SMEM = pl.BlockSpec(memory_space=pltpu.SMEM)


def local(spectra, keep, pair_mask):
    w_dev, _, ch, f_dev = spectra.shape
    reach = pair_mask.shape[1] - 1
    n_chan, n_win, n_freq = (lax.axis_size(a) for a in ("chan", "win", "freq"))
    groups = n_win * n_freq
    width = LAGS // groups
    n_bins = f_dev * n_freq
    params = pltpu.CompilerParams(vmem_limit_bytes=VMEM_LIMIT)
    freq = lax.axis_index("freq")
    place = lax.axis_index(("win", "freq"))

    places = jnp.stack([freq, place]).astype(jnp.int32)

    def cost(flops, size):
        return pl.CostEstimate(flops=flops, bytes_accessed=size, transcendentals=0)

    raw = from_behind(spectra, "chan", -1)
    power, copied = pl.pallas_call(
        power_kernel,
        out_shape=[
            jax.ShapeDtypeStruct((w_dev, ch, 1), jnp.float32),
            jax.ShapeDtypeStruct(spectra.shape, spectra.dtype),
        ],
        in_specs=[VMEM], out_specs=[VMEM] * 2, compiler_params=params, cost_estimate=cost(0, 2 ** 22),
    )(spectra)
    own_power, next_power = [], []
    for turn in range(1, n_freq):
        route = [(f, (f + turn) % n_freq) for f in range(n_freq)]
        own_power.append(lax.ppermute(power, "freq", route))
        route = [(c * n_freq + f, (c - 1) * n_freq + to) for c in range(1, n_chan) for f, to in route]
        next_power.append(lax.ppermute(power, ("chan", "freq"), route))

    half_lags = 2 * np.arange(LAGS // 2) + 1
    coarse = phases(np.arange(0, n_bins, FINE), half_lags)
    fine = phases(F_LO + np.arange(FINE), half_lags)
    table = pl.pallas_call(
        table_kernel,
        out_shape=jax.ShapeDtypeStruct((4, f_dev, LAGS // 2), jnp.bfloat16),
        in_specs=[SMEM, VMEM], out_specs=VMEM, compiler_params=params, cost_estimate=cost(0, 2 ** 23),
    )(places, jnp.asarray(np.concatenate([coarse, fine], axis=1)))
    twist = phases(F_LO + np.arange(n_bins), np.ones(1)).reshape(2, n_freq, f_dev)
    twist = jnp.asarray(np.moveaxis(twist, 0, 1))

    raw, table, own_power = lax.optimization_barrier((raw, table, own_power))
    moving = pl.pallas_call(
        functools.partial(whiten_kernel, n_bins),
        out_shape=jax.ShapeDtypeStruct(raw.shape, jnp.bfloat16),
        in_specs=[VMEM] * n_freq, out_specs=VMEM, compiler_params=params,
    )(raw, *next_power)
    white, own = pl.pallas_call(
        functools.partial(own_kernel, n_bins),
        out_shape=[
            jax.ShapeDtypeStruct(spectra.shape, jnp.bfloat16),
            jax.ShapeDtypeStruct(spectra.shape, jnp.float32),
        ],
        in_specs=[SMEM] + [VMEM] * n_freq, out_specs=[VMEM] * 2, compiler_params=params,
    )(keep, copied, *own_power)

    def pairs(partners):
        n = len(partners)
        return pl.pallas_call(
            functools.partial(pairs_kernel, n, groups),
            out_shape=[jax.ShapeDtypeStruct((n, ch * ch, width), jnp.float32)] * groups,
            in_specs=[SMEM] + [VMEM] * (n + 3), out_specs=[VMEM] * groups,
            scratch_shapes=[
                pltpu.VMEM((2, 2 * ch * ch, f_dev), jnp.bfloat16),
                pltpu.VMEM((2, ch * ch, LAGS // 2), jnp.float32),
            ],
            compiler_params=params,
            cost_estimate=cost(n * 6 * ch * ch * 2 * f_dev * LAGS, 2 ** 22),
        )(places, own, *partners, twist, table)

    def exchange(parts):
        received = [parts[0]]
        for turn in range(1, groups):
            route = [(g, (g + turn) % groups) for g in range(groups)]
            received.append(lax.ppermute(parts[turn], ("win", "freq"), route))
        return received

    parts = pairs([white, moving])
    received = []
    for step in range(1, reach):
        moving = from_behind(moving, "chan", -1)
        moving, parts = lax.optimization_barrier((moving, parts))
        received += exchange(parts)
        parts = pairs([moving])
    received += exchange(parts)
    scale = 1.0 / math.sqrt(w_dev * n_win * n_bins)
    return pl.pallas_call(
        functools.partial(combine_kernel, scale, groups),
        out_shape=jax.ShapeDtypeStruct((ch, reach + 1, ch, width), jnp.float32),
        in_specs=[SMEM] * 2 + [VMEM] * len(received), out_specs=VMEM, compiler_params=params,
    )(pair_mask, places, *received)


def solution(mesh):
    in_specs = (
        P("win", None, ("fibre", "chan"), "freq"),
        P(("fibre", "win")),
        P(("fibre", "chan"), None),
    )
    out_specs = P(("fibre", "chan"), None, None, ("win", "freq"))
    return jax.shard_map(local, mesh=mesh, in_specs=in_specs, out_specs=out_specs, check_vma=False)
```

time: 54.3 us -> 44.1 us (0.81)
  Pallas kernels: 22.3 us -> 12.3 us
  local copies, waits for them, and re-layouts: 4.62 us -> 2.03 us
  waiting for transfers between devices: 12.7 us -> 15.2 us
    ppermute x3, waiting for transfers between devices: 2.54 us -> 12.1 us  [from_behind(): return lax.ppermute(block, axis, route)]
    pallas_call x3, Pallas kernels: 15.3 us -> 7.95 us  [pairs(): pl.pallas_call(functools.partial(pairs_kernel, n, groups), out_shape=[jax...]
    ppermute x1, waiting for transfers between devices: 7.12 us -> 0.01 us  [local(): next_power.append(lax.ppermute(power, ('chan', 'freq'), route))]
    pallas_call x5, Pallas kernels: 7.04 us -> 4.33 us  [the longest x1 1.73 us: local(): pl.pallas_call(table_kernel, out_shape=jax.ShapeDtypeStruct((4, f_dev, LA...]
    unnamed x13 -> x11, local copies, waits for them, and re-layouts: 4.62 us -> 2.03 us
  transfers between devices with their start and end apart: 14 -> 14, of which waited for: 6 -> 6; matrix products, arithmetic and copies ran while one was open for 0% -> 0% of each run, Pallas kernels for 39% -> 24%
where the time goes in v6:
time: 44.1 us; the launch traced here: 43.6 us
  waiting for transfers between devices  15.2 us (34%)
  starting transfers between devices  13.9 us (32%)
  Pallas kernels  12.3 us (28%)
  local copies, waits for them, and re-layouts  2.03 us (5%)
    ppermute x3, waiting for transfers between devices, from_behind(): return lax.ppermute(block, axis, route)  12.1 us
    ppermute x9, starting transfers between devices, exchange(): received.append(lax.ppermute(parts[turn], ('win', 'freq'), route))  8.19 us
    pallas_call x3, Pallas kernels, pairs(): pl.pallas_call(functools.partial(pairs_kernel, n, groups), out_shape=[jax...  7.95 us
    ppermute x3, starting transfers between devices, from_behind(): return lax.ppermute(block, axis, route)  3.98 us
    ppermute x9, waiting for transfers between devices, exchange(): received.append(lax.ppermute(parts[turn], ('win', 'freq'), route))  3.05 us
    unnamed x11, local copies, waits for them, and re-layouts  2.03 us
    pallas_call x1, Pallas kernels, local(): pl.pallas_call(table_kernel, out_shape=jax.ShapeDtypeStruct((4, f_dev, LA...  1.73 us
    pallas_call x1, Pallas kernels, local(): pl.pallas_call(functools.partial(combine_kernel, scale, groups), out_shap...  1.45 us
  transfers between devices with their start and end apart: 14, of which 6 were waited for; matrix products, arithmetic and copies ran while one was open for 0% of the time, Pallas kernels for 24%

profile of v6, /device:TPU:0, one launch (start us, length us, event | category | flops | bytes accessed | tf_op | source)
XLA Modules:
  0.0 43.6 jit_solution(1544764735614887223)
XLA Ops:
  0.0 1.3 %collective-permute-start = (bf16[8,2,8,1024]{3,2,1,0:T(8,128)(2,1)}, bf16[8,2,8,1024]{3,2,1,0:T(8,128)(2,1)S(1)}, u32[]{:S(2)}, u32[]{:S(2)}) collective-permute-start(bf16[8,2,8,1024]{3,2,1,0:T(8,128)(2,1)} %x_ref.1), channel_id=1, source_target_pairs={{4,0},{8,4},{12,8},{5,1},{9,5},{13,9},{6,2},{10,6},{14,10},{7,3},{... | collective-permute-start | bytes 786440 | tf_op jit(solution)/shard_map/ppermute | solution.py:26
  1.3 0.0 copy-start.1
  1.3 0.9 %copy-done.1 = bf16[8,2,8,1024]{3,2,1,0:T(8,128)(2,1)S(1)} copy-done((bf16[8,2,8,1024]{3,2,1,0:T(8,128)(2,1)S(1)}, bf16[8,2,8,1024]{3,2,1,0:T(8,128)(2,1)}, u32[]{:S(2)}) %copy-start.1) | copy-done | bytes 262168
  2.2 0.0 copy-start.3
  2.2 0.0 copy-start.2
  2.2 0.1 shard_map.56
  2.4 0.5 %collective-permute-start.1 = (f32[8,8,1]{2,1,0:T(8,128)S(1)}, f32[8,8,1]{2,1,0:T(8,128)S(1)}, u32[]{:S(2)}, u32[]{:S(2)}) collective-permute-start(f32[8,8,1]{2,1,0:T(8,128)S(1)} %get-tuple-element.34), channel_id=1, source_target_pairs={{0,1},{1,0},{2,3},{3,2},{4,5},{5,4},{6,7},{7,6},{8,9},{9,8},{10,11... | collective-permute-start | bytes 776 | tf_op jit(solution)/shard_map/ppermute | solution.py:208
  2.8 1.3 %collective-permute-start.2 = (f32[8,8,1]{2,1,0:T(8,128)S(1)}, f32[8,8,1]{2,1,0:T(8,128)S(1)}, u32[]{:S(2)}, u32[]{:S(2)}) collective-permute-start(f32[8,8,1]{2,1,0:T(8,128)S(1)} %get-tuple-element.34), channel_id=1, source_target_pairs={{4,1},{5,0},{8,5},{9,4},{12,9},{13,8},{6,3},{7,2},{10,7},{11,6},{1... | collective-permute-start | bytes 776 | tf_op jit(solution)/shard_map/ppermute | solution.py:210
  4.1 0.1 pad_add_fusion.place_ref
  4.2 0.0 copy-start
  4.2 1.0 %copy-done = f32[2,96,512]{2,1,0:T(8,128)S(1)} copy-done((f32[2,96,512]{2,1,0:T(8,128)S(1)}, f32[2,96,512]{2,1,0:T(8,128)}, u32[]{:S(2)}) %copy-start) | copy-done | bytes 393240
  5.2 1.7 %shard_map.55.refs_3_.refs_2_ = bf16[4,1024,512]{2,1,0:T(8,128)(2,1)S(1)} custom-call(s32[2]{0:T(128)S(1)} %pad_add_fusion.place_ref, f32[2,96,512]{2,1,0:T(8,128)S(1)} %copy-done), custom_call_target="tpu_custom_call" | custom-call | bytes 8388608 | tf_op jit(solution)/shard_map/pallas_call | solution.py:215
  7.0 0.0 collective-permute-done.1.refs_0_
  7.0 4.8 %collective-permute-done.x_ref = bf16[8,2,8,1024]{3,2,1,0:T(8,128)(2,1)S(1)} collective-permute-done((bf16[8,2,8,1024]{3,2,1,0:T(8,128)(2,1)}, bf16[8,2,8,1024]{3,2,1,0:T(8,128)(2,1)S(1)}, u32[]{:S(2)}, u32[]{:S(2)}) %collective-permute-start) | collective-permute-done | bytes 262176 | tf_op jit(solution)/shard_map/ppermute | solution.py:26
  11.8 0.0 collective-permute-done.2.refs_0_
  11.8 0.2 shard_map.57.refs_1_
  12.0 1.3 %collective-permute-start.3 = (bf16[8,2,8,1024]{3,2,1,0:T(8,128)(2,1)S(1)}, bf16[8,2,8,1024]{3,2,1,0:T(8,128)(2,1)S(1)}, u32[]{:S(2)}, u32[]{:S(2)}) collective-permute-start(bf16[8,2,8,1024]{3,2,1,0:T(8,128)(2,1)S(1)} %shard_map.57.refs_1_), channel_id=1, source_target_pairs={{4,0},{8,4},{12,8},{5,1},{9,5},{13,9},{6,2},{10,6},{14,10},{7,3},{... | collective-permute-start | bytes 786440 | tf_op jit(solution)/shard_map/ppermute | solution.py:26
  13.3 0.0 copy-done.3
  13.3 0.8 %shard_map.58 = (bf16[8,2,8,1024]{3,2,1,0:T(8,128)(2,1)S(1)}, f32[8,2,8,1024]{3,2,1,0:T(8,128)S(1)}) custom-call(s32[8]{0:T(128)S(1)} %copy-done.3, bf16[8,2,8,1024]{3,2,1,0:T(8,128)(2,1)S(1)} %get-tuple-element.36.x_ref, f32[8,8,1]{2,1,0:T(8,128)S(1)} %collective-permute-done.1.refs_0_), custom_call_target="tpu_custom_call" | custom-call | tf_op jit(solution)/shard_map/pallas_call | solution.py:229
  14.1 0.0 copy-done.2
  14.1 3.7 %shard_map.59 = (f32[2,64,256]{2,1,0:T(8,128)S(1)}, f32[2,64,256]{2,1,0:T(8,128)S(1)}, f32[2,64,256]{2,1,0:T(8,128)S(1)}, f32[2,64,256]{2,1,0:T(8,128)S(1)}) custom-call(s32[2]{0:T(128)S(1)} %pad_add_fusion.place_ref, f32[8,2,8,1024]{3,2,1,0:T(8,128)S(1)} %get-tuple-element.38.own_ref, bf16[8,2,8,1024]{3,2,1,0:T(8,128)(2,1)S(1)} %get-tuple-element.39.refs_0_, ...), custom_call_target="tpu_custom_call" | custom-call | flops 1610612736 | bytes 4194304 | tf_op jit(solution)/shard_map/pallas_call | solution.py:240
  17.9 4.4 %collective-permute-done.3.refs_0_ = bf16[8,2,8,1024]{3,2,1,0:T(8,128)(2,1)S(1)} collective-permute-done((bf16[8,2,8,1024]{3,2,1,0:T(8,128)(2,1)S(1)}, bf16[8,2,8,1024]{3,2,1,0:T(8,128)(2,1)S(1)}, u32[]{:S(2)}, u32[]{:S(2)}) %collective-permute-start.3) | collective-permute-done | bytes 262176 | tf_op jit(solution)/shard_map/ppermute | solution.py:26
  22.3 0.0 copy-start.4
  22.3 1.4 %collective-permute-start.7 = (bf16[8,2,8,1024]{3,2,1,0:T(8,128)(2,1)S(1)}, bf16[8,2,8,1024]{3,2,1,0:T(8,128)(2,1)S(1)}, u32[]{:S(2)}, u32[]{:S(2)}) collective-permute-start(bf16[8,2,8,1024]{3,2,1,0:T(8,128)(2,1)S(1)} %collective-permute-done.3.refs_0_), channel_id=1, source_target_pairs={{4,0},{8,4},{12,8},{5,1},{9,5},{13,9},{6,2},{10,6},{14,10},{7,3},{... | collective-permute-start | bytes 786440 | tf_op jit(solution)/shard_map/ppermute | solution.py:26
  23.7 0.1 collective-permute-start.4
  23.8 1.7 %collective-permute-start.5 = (f32[2,64,256]{2,1,0:T(8,128)S(1)}, f32[2,64,256]{2,1,0:T(8,128)S(1)}, u32[]{:S(2)}, u32[]{:S(2)}) collective-permute-start(f32[2,64,256]{2,1,0:T(8,128)S(1)} %get-tuple-element.47), channel_id=1, source_target_pairs={{0,2},{1,3},{2,0},{3,1},{4,6},{5,7},{6,4},{7,5},{8,10},{9,11},{10,... | collective-permute-start | bytes 393224 | tf_op jit(solution)/shard_map/ppermute | solution.py:256
  25.5 1.4 %collective-permute-start.6 = (f32[2,64,256]{2,1,0:T(8,128)S(1)}, f32[2,64,256]{2,1,0:T(8,128)S(1)}, u32[]{:S(2)}, u32[]{:S(2)}) collective-permute-start(f32[2,64,256]{2,1,0:T(8,128)S(1)} %get-tuple-element.48), channel_id=1, source_target_pairs={{0,3},{1,0},{2,1},{3,2},{4,7},{5,4},{6,5},{7,6},{8,11},{9,8},{10,9... | collective-permute-start | bytes 393224 | tf_op jit(solution)/shard_map/ppermute | solution.py:256
  26.9 2.1 %shard_map.60 = (f32[1,64,256]{2,1,0:T(8,128)S(1)}, f32[1,64,256]{2,1,0:T(8,128)S(1)}, f32[1,64,256]{2,1,0:T(8,128)S(1)}, f32[1,64,256]{2,1,0:T(8,128)S(1)}) custom-call(s32[2]{0:T(128)S(1)} %pad_add_fusion.place_ref, f32[8,2,8,1024]{3,2,1,0:T(8,128)S(1)} %get-tuple-element.38.own_ref, bf16[8,2,8,1024]{3,2,1,0:T(8,128)(2,1)S(1)} %collective-permute-done.3.refs_0_, ...), custom_call_target="tpu_custom_call" | custom-call | flops 805306368 | bytes 4194304 | tf_op jit(solution)/shard_map/pallas_call | solution.py:240
  29.0 2.9 %collective-permute-done.7.refs_0_ = bf16[8,2,8,1024]{3,2,1,0:T(8,128)(2,1)S(1)} collective-permute-done((bf16[8,2,8,1024]{3,2,1,0:T(8,128)(2,1)S(1)}, bf16[8,2,8,1024]{3,2,1,0:T(8,128)(2,1)S(1)}, u32[]{:S(2)}, u32[]{:S(2)}) %collective-permute-start.7) | collective-permute-done | bytes 262176 | tf_op jit(solution)/shard_map/ppermute | solution.py:26
  31.9 0.0 collective-permute-start.8
  31.9 1.7 %collective-permute-start.9 = (f32[1,64,256]{2,1,0:T(8,128)S(1)}, f32[1,64,256]{2,1,0:T(8,128)S(1)}, u32[]{:S(2)}, u32[]{:S(2)}) collective-permute-start(f32[1,64,256]{2,1,0:T(8,128)S(1)} %get-tuple-element.56), channel_id=1, source_target_pairs={{0,2},{1,3},{2,0},{3,1},{4,6},{5,7},{6,4},{7,5},{8,10},{9,11},{10,... | collective-permute-start | bytes 196616 | tf_op jit(solution)/shard_map/ppermute | solution.py:256
  33.5 2.1 %shard_map.61 = (f32[1,64,256]{2,1,0:T(8,128)S(1)}, f32[1,64,256]{2,1,0:T(8,128)S(1)}, f32[1,64,256]{2,1,0:T(8,128)S(1)}, f32[1,64,256]{2,1,0:T(8,128)S(1)}) custom-call(s32[2]{0:T(128)S(1)} %pad_add_fusion.place_ref, f32[8,2,8,1024]{3,2,1,0:T(8,128)S(1)} %get-tuple-element.38.own_ref, bf16[8,2,8,1024]{3,2,1,0:T(8,128)(2,1)S(1)} %collective-permute-done.7.refs_0_, ...), custom_call_target="tpu_custom_call" | custom-call | flops 805306368 | bytes 4194304 | tf_op jit(solution)/shard_map/pallas_call | solution.py:240
  35.7 0.0 collective-permute-done.4.refs_1_
  35.7 1.5 %collective-permute-start.10 = (f32[1,64,256]{2,1,0:T(8,128)S(1)}, f32[1,64,256]{2,1,0:T(8,128)S(1)}, u32[]{:S(2)}, u32[]{:S(2)}) collective-permute-start(f32[1,64,256]{2,1,0:T(8,128)S(1)} %get-tuple-element.57), channel_id=1, source_target_pairs={{0,3},{1,0},{2,1},{3,2},{4,7},{5,4},{6,5},{7,6},{8,11},{9,8},{10,9... | collective-permute-start | bytes 196616 | tf_op jit(solution)/shard_map/ppermute | solution.py:256
  37.2 0.0 collective-permute-done.5.refs_2_
  37.2 0.0 collective-permute-start.11
  37.2 0.0 collective-permute-done.6.refs_3_
  37.2 0.5 %collective-permute-start.12 = (f32[1,64,256]{2,1,0:T(8,128)S(1)}, f32[1,64,256]{2,1,0:T(8,128)S(1)}, u32[]{:S(2)}, u32[]{:S(2)}) collective-permute-start(f32[1,64,256]{2,1,0:T(8,128)S(1)} %get-tuple-element.61), channel_id=1, source_target_pairs={{0,2},{1,3},{2,0},{3,1},{4,6},{5,7},{6,4},{7,5},{8,10},{9,11},{10,... | collective-permute-start | bytes 196616 | tf_op jit(solution)/shard_map/ppermute | solution.py:256
  37.6 0.0 collective-permute-done.8.refs_5_
  37.6 1.4 %collective-permute-start.13 = (f32[1,64,256]{2,1,0:T(8,128)S(1)}, f32[1,64,256]{2,1,0:T(8,128)S(1)}, u32[]{:S(2)}, u32[]{:S(2)}) collective-permute-start(f32[1,64,256]{2,1,0:T(8,128)S(1)} %get-tuple-element.62), channel_id=1, source_target_pairs={{0,3},{1,0},{2,1},{3,2},{4,7},{5,4},{6,5},{7,6},{8,11},{9,8},{10,9... | collective-permute-start | bytes 196616 | tf_op jit(solution)/shard_map/ppermute | solution.py:256
  39.0 0.0 copy-done.4
  39.0 0.1 copy.6.mask_ref
  39.1 0.0 collective-permute-done.9.refs_6_
  39.1 0.3 collective-permute-done.10.refs_7_
  39.5 1.5 %collective-permute-done.11.refs_9_ = f32[1,64,256]{2,1,0:T(8,128)S(1)} collective-permute-done((f32[1,64,256]{2,1,0:T(8,128)S(1)}, f32[1,64,256]{2,1,0:T(8,128)S(1)}, u32[]{:S(2)}, u32[]{:S(2)}) %collective-permute-start.11) | collective-permute-done | bytes 65568 | tf_op jit(solution)/shard_map/ppermute | solution.py:256
  41.0 1.2 %collective-permute-done.12.refs_10_ = f32[1,64,256]{2,1,0:T(8,128)S(1)} collective-permute-done((f32[1,64,256]{2,1,0:T(8,128)S(1)}, f32[1,64,256]{2,1,0:T(8,128)S(1)}, u32[]{:S(2)}, u32[]{:S(2)}) %collective-permute-start.12) | collective-permute-done | bytes 65568 | tf_op jit(solution)/shard_map/ppermute | solution.py:256
  42.2 0.0 collective-permute-done.13.refs_11_
  42.2 1.4 %shard_map.62 = f32[8,4,8,256]{3,2,1,0:T(8,128)} custom-call(s32[8,4]{1,0:T(8,128)S(1)} %copy.6.mask_ref, s32[2]{0:T(128)S(1)} %pad_add_fusion.place_ref, f32[2,64,256]{2,1,0:T(8,128)S(1)} %get-tuple-element.45.refs_0_, f32[2,64,256]{2,1,0:T(8,128)S(1)} %collective-permute-done.4.refs_1_, f32[2,64,256]{2,1,0:T(8,128)S(1)} %collective-permute-done.5.refs_2_, ...), custom_call_target="tpu_custom_call" | custom-call | tf_op jit(solution)/shard_map/pallas_call | solution.py:268
Async XLA Ops:
  0.0 11.8 %collective-permute-start = (bf16[8,2,8,1024]{3,2,1,0:T(8,128)(2,1)}, bf16[8,2,8,1024]{3,2,1,0:T(8,128)(2,1)S(1)}, u32[]{:S(2)}, u32[]{:S(2)}) collective-permute-start(bf16[8,2,8,1024]{3,2,1,0:T(8,128)(2,1)} %x_ref.1), channel_id=1, source_target_pairs={{4,0},{8,4},{12,8},{5,1},{9,5},{13,9},{6,2},{10,6},{14,10},{7,3},{... | collective-permute-start | bytes 786440 | tf_op jit(solution)/shard_map/ppermute | solution.py:26
  1.3 1.0 %copy-start.1 = (bf16[8,2,8,1024]{3,2,1,0:T(8,128)(2,1)S(1)}, bf16[8,2,8,1024]{3,2,1,0:T(8,128)(2,1)}, u32[]{:S(2)}) copy-start(bf16[8,2,8,1024]{3,2,1,0:T(8,128)(2,1)} %x_ref.1) | copy-start | bytes 786436
  2.2 11.1 %copy-start.3 = (s32[8]{0:T(128)S(1)}, s32[8]{0:T(128)}, u32[]{:S(2)}) copy-start(s32[8]{0:T(128)} %keep_ref.1) | copy-start | bytes 100
  2.2 11.9 %copy-start.2 = (f32[2,2,1024]{2,1,0:T(2,128)S(1)}, f32[2,2,1024]{2,1,0:T(2,128)}, u32[]{:S(2)}) copy-start(f32[2,2,1024]{2,1,0:T(2,128)} %constant.13.clone.refs_2_.refs_1_) | copy-start | bytes 49156
  2.4 4.6 %collective-permute-start.1 = (f32[8,8,1]{2,1,0:T(8,128)S(1)}, f32[8,8,1]{2,1,0:T(8,128)S(1)}, u32[]{:S(2)}, u32[]{:S(2)}) collective-permute-start(f32[8,8,1]{2,1,0:T(8,128)S(1)} %get-tuple-element.34), channel_id=1, source_target_pairs={{0,1},{1,0},{2,3},{3,2},{4,5},{5,4},{6,7},{7,6},{8,9},{9,8},{10,11... | collective-permute-start | bytes 776 | tf_op jit(solution)/shard_map/ppermute | solution.py:208
  2.8 8.9 %collective-permute-start.2 = (f32[8,8,1]{2,1,0:T(8,128)S(1)}, f32[8,8,1]{2,1,0:T(8,128)S(1)}, u32[]{:S(2)}, u32[]{:S(2)}) collective-permute-start(f32[8,8,1]{2,1,0:T(8,128)S(1)} %get-tuple-element.34), channel_id=1, source_target_pairs={{4,1},{5,0},{8,5},{9,4},{12,9},{13,8},{6,3},{7,2},{10,7},{11,6},{1... | collective-permute-start | bytes 776 | tf_op jit(solution)/shard_map/ppermute | solution.py:210
  4.2 1.0 %copy-start = (f32[2,96,512]{2,1,0:T(8,128)S(1)}, f32[2,96,512]{2,1,0:T(8,128)}, u32[]{:S(2)}) copy-start(f32[2,96,512]{2,1,0:T(8,128)} %constant.12.clone.base_ref) | copy-start | bytes 1179652
  12.0 10.3 %collective-permute-start.3 = (bf16[8,2,8,1024]{3,2,1,0:T(8,128)(2,1)S(1)}, bf16[8,2,8,1024]{3,2,1,0:T(8,128)(2,1)S(1)}, u32[]{:S(2)}, u32[]{:S(2)}) collective-permute-start(bf16[8,2,8,1024]{3,2,1,0:T(8,128)(2,1)S(1)} %shard_map.57.refs_1_), channel_id=1, source_target_pairs={{4,0},{8,4},{12,8},{5,1},{9,5},{13,9},{6,2},{10,6},{14,10},{7,3},{... | collective-permute-start | bytes 786440 | tf_op jit(solution)/shard_map/ppermute | solution.py:26
  22.3 16.7 %copy-start.4 = (s32[8,4]{0,1:T(4,128)S(1)}, s32[8,4]{0,1:T(4,128)}, u32[]{:S(2)}) copy-start(s32[8,4]{0,1:T(4,128)} %param.7) | copy-start | bytes 388
  22.3 9.6 %collective-permute-start.7 = (bf16[8,2,8,1024]{3,2,1,0:T(8,128)(2,1)S(1)}, bf16[8,2,8,1024]{3,2,1,0:T(8,128)(2,1)S(1)}, u32[]{:S(2)}, u32[]{:S(2)}) collective-permute-start(bf16[8,2,8,1024]{3,2,1,0:T(8,128)(2,1)S(1)} %collective-permute-done.3.refs_0_), channel_id=1, source_target_pairs={{4,0},{8,4},{12,8},{5,1},{9,5},{13,9},{6,2},{10,6},{14,10},{7,3},{... | collective-permute-start | bytes 786440 | tf_op jit(solution)/shard_map/ppermute | solution.py:26
  23.7 11.9 %collective-permute-start.4 = (f32[2,64,256]{2,1,0:T(8,128)S(1)}, f32[2,64,256]{2,1,0:T(8,128)S(1)}, u32[]{:S(2)}, u32[]{:S(2)}) collective-permute-start(f32[2,64,256]{2,1,0:T(8,128)S(1)} %get-tuple-element.46), channel_id=1, source_target_pairs={{0,1},{1,2},{2,3},{3,0},{4,5},{5,6},{6,7},{7,4},{8,9},{9,10},{10,1... | collective-permute-start | bytes 393224 | tf_op jit(solution)/shard_map/ppermute | solution.py:256
  23.8 13.4 %collective-permute-start.5 = (f32[2,64,256]{2,1,0:T(8,128)S(1)}, f32[2,64,256]{2,1,0:T(8,128)S(1)}, u32[]{:S(2)}, u32[]{:S(2)}) collective-permute-start(f32[2,64,256]{2,1,0:T(8,128)S(1)} %get-tuple-element.47), channel_id=1, source_target_pairs={{0,2},{1,3},{2,0},{3,1},{4,6},{5,7},{6,4},{7,5},{8,10},{9,11},{10,... | collective-permute-start | bytes 393224 | tf_op jit(solution)/shard_map/ppermute | solution.py:256
  25.5 11.7 %collective-permute-start.6 = (f32[2,64,256]{2,1,0:T(8,128)S(1)}, f32[2,64,256]{2,1,0:T(8,128)S(1)}, u32[]{:S(2)}, u32[]{:S(2)}) collective-permute-start(f32[2,64,256]{2,1,0:T(8,128)S(1)} %get-tuple-element.48), channel_id=1, source_target_pairs={{0,3},{1,0},{2,1},{3,2},{4,7},{5,4},{6,5},{7,6},{8,11},{9,8},{10,9... | collective-permute-start | bytes 393224 | tf_op jit(solution)/shard_map/ppermute | solution.py:256
  31.9 5.8 %collective-permute-start.8 = (f32[1,64,256]{2,1,0:T(8,128)S(1)}, f32[1,64,256]{2,1,0:T(8,128)S(1)}, u32[]{:S(2)}, u32[]{:S(2)}) collective-permute-start(f32[1,64,256]{2,1,0:T(8,128)S(1)} %get-tuple-element.55), channel_id=1, source_target_pairs={{0,1},{1,2},{2,3},{3,0},{4,5},{5,6},{6,7},{7,4},{8,9},{9,10},{10,1... | collective-permute-start | bytes 196616 | tf_op jit(solution)/shard_map/ppermute | solution.py:256
  31.9 7.3 %collective-permute-start.9 = (f32[1,64,256]{2,1,0:T(8,128)S(1)}, f32[1,64,256]{2,1,0:T(8,128)S(1)}, u32[]{:S(2)}, u32[]{:S(2)}) collective-permute-start(f32[1,64,256]{2,1,0:T(8,128)S(1)} %get-tuple-element.56), channel_id=1, source_target_pairs={{0,2},{1,3},{2,0},{3,1},{4,6},{5,7},{6,4},{7,5},{8,10},{9,11},{10,... | collective-permute-start | bytes 196616 | tf_op jit(solution)/shard_map/ppermute | solution.py:256
  35.7 3.8 %collective-permute-start.10 = (f32[1,64,256]{2,1,0:T(8,128)S(1)}, f32[1,64,256]{2,1,0:T(8,128)S(1)}, u32[]{:S(2)}, u32[]{:S(2)}) collective-permute-start(f32[1,64,256]{2,1,0:T(8,128)S(1)} %get-tuple-element.57), channel_id=1, source_target_pairs={{0,3},{1,0},{2,1},{3,2},{4,7},{5,4},{6,5},{7,6},{8,11},{9,8},{10,9... | collective-permute-start | bytes 196616 | tf_op jit(solution)/shard_map/ppermute | solution.py:256
  37.2 3.8 %collective-permute-start.11 = (f32[1,64,256]{2,1,0:T(8,128)S(1)}, f32[1,64,256]{2,1,0:T(8,128)S(1)}, u32[]{:S(2)}, u32[]{:S(2)}) collective-permute-start(f32[1,64,256]{2,1,0:T(8,128)S(1)} %get-tuple-element.60), channel_id=1, source_target_pairs={{0,1},{1,2},{2,3},{3,0},{4,5},{5,6},{6,7},{7,4},{8,9},{9,10},{10,1... | collective-permute-start | bytes 196616 | tf_op jit(solution)/shard_map/ppermute | solution.py:256
  37.2 5.0 %collective-permute-start.12 = (f32[1,64,256]{2,1,0:T(8,128)S(1)}, f32[1,64,256]{2,1,0:T(8,128)S(1)}, u32[]{:S(2)}, u32[]{:S(2)}) collective-permute-start(f32[1,64,256]{2,1,0:T(8,128)S(1)} %get-tuple-element.61), channel_id=1, source_target_pairs={{0,2},{1,3},{2,0},{3,1},{4,6},{5,7},{6,4},{7,5},{8,10},{9,11},{10,... | collective-permute-start | bytes 196616 | tf_op jit(solution)/shard_map/ppermute | solution.py:256
  37.6 4.5 %collective-permute-start.13 = (f32[1,64,256]{2,1,0:T(8,128)S(1)}, f32[1,64,256]{2,1,0:T(8,128)S(1)}, u32[]{:S(2)}, u32[]{:S(2)}) collective-permute-start(f32[1,64,256]{2,1,0:T(8,128)S(1)} %get-tuple-element.62), channel_id=1, source_target_pairs={{0,3},{1,0},{2,1},{3,2},{4,7},{5,4},{6,5},{7,6},{8,11},{9,8},{10,9... | collective-permute-start | bytes 196616 | tf_op jit(solution)/shard_map/ppermute | solution.py:256

commit v7 on v6

--- a/solution.py
+++ b/solution.py
@@ -17,6 +17,7 @@
 SUBLANES = 8
 FINE = 32
 BLOCK = 256
+PIECES = 2
 VMEM_LIMIT = 16 * 1024 * 1024
 
 
@@ -49,20 +50,22 @@
         copy_ref[w] = x
 
 
-def whiten_kernel(n_bins, x_ref, *refs):
-    out_ref = refs[-1]
+def whiten_kernel(n_bins, n_pieces, x_ref, *refs):
+    out_refs = refs[-n_pieces:]
+    per_piece = x_ref.shape[0] // n_pieces
     for w in range(x_ref.shape[0]):
         power = bin_power(x_ref[w])
-        for ref in refs[:-1]:
+        for ref in refs[:-n_pieces]:
             power = power + ref[w]
         scale = lax.rsqrt(power / n_bins + EPS)
         for part in range(2):
-            out_ref[w, part] = (x_ref[w, part].astype(jnp.float32) * scale).astype(jnp.bfloat16)
+            value = x_ref[w, part].astype(jnp.float32) * scale
+            out_refs[w // per_piece][w % per_piece, part] = value.astype(jnp.bfloat16)
 
 
 def own_kernel(n_bins, keep_ref, x_ref, *refs):
     white_ref, own_ref = refs[-2:]
-    whiten_kernel(n_bins, x_ref, *refs[:-2], white_ref)
+    whiten_kernel(n_bins, 1, x_ref, *refs[:-2], white_ref)
     for w in range(x_ref.shape[0]):
         own_ref[w] = white_ref[w].astype(jnp.float32) * keep_ref[w].astype(jnp.float32)
 
@@ -90,13 +93,14 @@
         lax.fori_loop(0, f_dev // (FINE * SUBLANES), body, 0)
 
 
-def cross_tile(own_ref, partner_ref, lanes):
-    w_dev, _, ch, _ = own_ref.shape
+def cross_tile(own_ref, piece_refs, lanes):
+    ch = own_ref.shape[2]
     real = [None] * ch
     imag = [None] * ch
-    for w in range(w_dev):
-        partner_re = partner_ref[w, 0, :, lanes].astype(jnp.float32)
-        partner_im = partner_ref[w, 1, :, lanes].astype(jnp.float32)
+    windows = [(ref, n) for ref in piece_refs for n in range(ref.shape[0])]
+    for w, (ref, n) in enumerate(windows):
+        partner_re = ref[n, 0, :, lanes].astype(jnp.float32)
+        partner_im = ref[n, 1, :, lanes].astype(jnp.float32)
         for i in range(ch):
             own_re = own_ref[w, 0, i:i + 1, lanes]
             own_im = own_ref[w, 1, i:i + 1, lanes]
@@ -107,21 +111,28 @@
     return real, imag
 
 
-def pairs_kernel(n_partners, groups, place_ref, own_ref, *refs):
-    partner_refs = refs[:n_partners]
-    twist_ref, table_ref = refs[n_partners:n_partners + 2]
+def pairs_kernel(n_pieces, n_win, n_freq, place_ref, own_ref, *refs):
+    total_pieces = sum(n_pieces)
+    piece_refs = refs[:total_pieces]
+    twist_ref, table_ref = refs[total_pieces:total_pieces + 2]
+    before_refs = refs[total_pieces + 2:-2 - n_freq]
+    out_refs = refs[-2 - n_freq:-2]
     rows_ref, sums_ref = refs[-2:]
-    out_refs = refs[-2 - groups:-2]
     ch, f_dev = own_ref.shape[2:]
     pairs = ch * ch
+    groups = n_win * n_freq
+    done = out_refs[0].shape[0] - len(n_pieces)
     width = out_refs[0].shape[-1]
-    freq, place = place_ref[0], place_ref[1]
+    freq, win = place_ref[0], place_ref[1]
     dot = functools.partial(jnp.dot, preferred_element_type=jnp.float32)
-    for k, partner_ref in enumerate(partner_refs):
+    for before_ref, out_ref in zip(before_refs, out_refs):
+        out_ref[:done] = before_ref[...]
+    for n, count in enumerate(n_pieces):
+        partner_refs = piece_refs[sum(n_pieces[:n]):sum(n_pieces[:n]) + count]
 
         def body(tile, carry):
             lanes = pl.ds(pl.multiple_of(tile * LANES, LANES), LANES)
-            real, imag = cross_tile(own_ref, partner_ref, lanes)
+            real, imag = cross_tile(own_ref, partner_refs, lanes)
             cos = twist_ref[freq, 0:1, lanes]
             sin = twist_ref[freq, 1:2, lanes]
             for i in range(0, ch, 2):
@@ -137,13 +148,29 @@
         for part in range(2):
             both = dot(rows_ref[part], table_ref[2 * part])
             sums_ref[part] = both[:pairs] + both[pairs:] + dot(rows_ref[part, :pairs], table_ref[2 * part + 1])
-        for turn, out_ref in enumerate(out_refs):
-            owner = (place + turn) % groups
-            upper = owner >= groups // 2
-            block = jnp.where(upper, owner - groups // 2, groups // 2 - 1 - owner)
-            sign = jnp.where(upper, -1.0, 1.0)
-            lags = pl.ds(pl.multiple_of(block * width, LANES), width)
-            out_ref[k] = sums_ref[0, :, lags] + sign * sums_ref[1, :, lags]
+        for turn_freq, out_ref in enumerate(out_refs):
+            for turn_win in range(n_win):
+                owner = (win + turn_win) % n_win * n_freq + (freq + turn_freq) % n_freq
+                upper = owner >= groups // 2
+                block = jnp.where(upper, owner - groups // 2, groups // 2 - 1 - owner)
+                sign = jnp.where(upper, -1.0, 1.0)
+                lags = pl.ds(pl.multiple_of(block * width, LANES), width)
+                out_ref[done + n, turn_win] = sums_ref[0, :, lags] + sign * sums_ref[1, :, lags]
+
+
+def add_kernel(n_parts, *refs):
+    for turn, out_ref in enumerate(refs[n_parts:]):
+        total = refs[0][:, turn]
+        for ref in refs[1:n_parts]:
+            total = total + ref[:, turn]
+        out_ref[...] = total
+
+
+def total_kernel(*refs):
+    total = refs[0][...]
+    for ref in refs[1:-1]:
+        total = total + ref[...]
+    refs[-1][...] = total
 
 
 def reverse_lanes(value):
@@ -155,13 +182,12 @@
     return jnp.concatenate(pieces[::-1], axis=1)
 
 
-def combine_kernel(scale, groups, mask_ref, place_ref, *refs):
+def combine_kernel(scale, groups, n_freq, mask_ref, place_ref, *refs):
     out_ref = refs[-1]
     ch = out_ref.shape[0]
-    lower = place_ref[1] < groups // 2
+    lower = place_ref[1] * n_freq + place_ref[0] < groups // 2
     k = 0
-    for first in range(0, len(refs) - 1, groups):
-        parts = refs[first:first + groups]
+    for parts in (refs[:1], refs[1:-1]):
         for n in range(parts[0].shape[0]):
             total = parts[0][n]
             for ref in parts[1:]:
@@ -181,14 +207,12 @@
     w_dev, _, ch, f_dev = spectra.shape
     reach = pair_mask.shape[1] - 1
     n_chan, n_win, n_freq = (lax.axis_size(a) for a in ("chan", "win", "freq"))
-    groups = n_win * n_freq
-    width = LAGS // groups
+    width = LAGS // (n_win * n_freq)
     n_bins = f_dev * n_freq
     params = pltpu.CompilerParams(vmem_limit_bytes=VMEM_LIMIT)
     freq = lax.axis_index("freq")
-    place = lax.axis_index(("win", "freq"))
-
-    places = jnp.stack([freq, place]).astype(jnp.int32)
+
+    places = jnp.stack([freq, lax.axis_index("win")]).astype(jnp.int32)
 
     def cost(flops, size):
         return pl.CostEstimate(flops=flops, bytes_accessed=size, transcendentals=0)
@@ -220,12 +244,6 @@
     twist = phases(F_LO + np.arange(n_bins), np.ones(1)).reshape(2, n_freq, f_dev)
     twist = jnp.asarray(np.moveaxis(twist, 0, 1))
 
-    raw, table, own_power = lax.optimization_barrier((raw, table, own_power))
-    moving = pl.pallas_call(
-        functools.partial(whiten_kernel, n_bins),
-        out_shape=jax.ShapeDtypeStruct(raw.shape, jnp.bfloat16),
-        in_specs=[VMEM] * n_freq, out_specs=VMEM, compiler_params=params,
-    )(raw, *next_power)
     white, own = pl.pallas_call(
         functools.partial(own_kernel, n_bins),
         out_shape=[
@@ -234,42 +252,73 @@
         ],
         in_specs=[SMEM] + [VMEM] * n_freq, out_specs=[VMEM] * 2, compiler_params=params,
     )(keep, copied, *own_power)
-
-    def pairs(partners):
-        n = len(partners)
+    raw, table, white = lax.optimization_barrier((raw, table, white))
+    piece = jax.ShapeDtypeStruct((w_dev // PIECES,) + raw.shape[1:], jnp.bfloat16)
+    moving = pl.pallas_call(
+        functools.partial(whiten_kernel, n_bins, PIECES),
+        out_shape=[piece] * PIECES,
+        in_specs=[VMEM] * n_freq, out_specs=[VMEM] * PIECES, compiler_params=params,
+    )(raw, *next_power)
+
+    def pairs(partners, before):
+        pieces = [piece for partner in partners for piece in partner]
+        n = len(partners) + (before[0].shape[0] if before else 0)
         return pl.pallas_call(
-            functools.partial(pairs_kernel, n, groups),
-            out_shape=[jax.ShapeDtypeStruct((n, ch * ch, width), jnp.float32)] * groups,
-            in_specs=[SMEM] + [VMEM] * (n + 3), out_specs=[VMEM] * groups,
+            functools.partial(pairs_kernel, [len(partner) for partner in partners], n_win, n_freq),
+            out_shape=[jax.ShapeDtypeStruct((n, n_win, ch * ch, width), jnp.float32)] * n_freq,
+            in_specs=[SMEM] + [VMEM] * (3 + len(pieces) + len(before)), out_specs=[VMEM] * n_freq,
             scratch_shapes=[
                 pltpu.VMEM((2, 2 * ch * ch, f_dev), jnp.bfloat16),
                 pltpu.VMEM((2, ch * ch, LAGS // 2), jnp.float32),
             ],
             compiler_params=params,
-            cost_estimate=cost(n * 6 * ch * ch * 2 * f_dev * LAGS, 2 ** 22),
-        )(places, own, *partners, twist, table)
-
-    def exchange(parts):
+            cost_estimate=cost(2 ** 33, 2 ** 22),
+        )(places, own, *pieces, twist, table, *before)
+
+    def turns(parts, axis, size):
         received = [parts[0]]
-        for turn in range(1, groups):
-            route = [(g, (g + turn) % groups) for g in range(groups)]
-            received.append(lax.ppermute(parts[turn], ("win", "freq"), route))
+        for turn in range(1, size):
+            route = [(g, (g + turn) % size) for g in range(size)]
+            received.append(lax.ppermute(parts[turn], axis, route))
         return received
 
-    parts = pairs([white, moving])
-    received = []
+    def gather_bins(parts):
+        n = parts[0].shape[0]
+        return pl.pallas_call(
+            functools.partial(add_kernel, n_freq),
+            out_shape=[jax.ShapeDtypeStruct((n, ch * ch, width), jnp.float32)] * n_win,
+            in_specs=[VMEM] * n_freq, out_specs=[VMEM] * n_win, compiler_params=params,
+        )(*turns(parts, "freq", n_freq))
+
+    def total(parts):
+        return pl.pallas_call(
+            total_kernel,
+            out_shape=jax.ShapeDtypeStruct(parts[0].shape, jnp.float32),
+            in_specs=[VMEM] * len(parts), out_specs=VMEM, compiler_params=params,
+        )(*parts)
+
+    parts = list(pairs([[white], moving], []))
+    early = None
     for step in range(1, reach):
-        moving = from_behind(moving, "chan", -1)
-        moving, parts = lax.optimization_barrier((moving, parts))
-        received += exchange(parts)
-        parts = pairs([moving])
-    received += exchange(parts)
+        arrived = [from_behind(block, "chan", -1) for block in moving]
+        if step == 1:
+            arrived, parts = lax.optimization_barrier((arrived, parts))
+            sums = list(gather_bins(parts))
+            early = total(turns(sums, "win", n_win))
+            parts = []
+        else:
+            parts = pairs([moving], parts)
+        moving = arrived
+    if early is not None:
+        moving[-1], early = lax.optimization_barrier((moving[-1], early))
+        parts = pairs([moving], parts)
+    received = turns(gather_bins(parts), "win", n_win)
     scale = 1.0 / math.sqrt(w_dev * n_win * n_bins)
     return pl.pallas_call(
-        functools.partial(combine_kernel, scale, groups),
+        functools.partial(combine_kernel, scale, n_win * n_freq, n_freq),
         out_shape=jax.ShapeDtypeStruct((ch, reach + 1, ch, width), jnp.float32),
-        in_specs=[SMEM] * 2 + [VMEM] * len(received), out_specs=VMEM, compiler_params=params,
-    )(pair_mask, places, *received)
+        in_specs=[SMEM] * 2 + [VMEM] * (1 + len(received)), out_specs=VMEM, compiler_params=params,
+    )(pair_mask, places, early, *received)
 
 
 def solution(mesh):

time: 44.1 us -> 44.1 us (level)
  starting transfers between devices: 13.9 us -> 11.7 us
  waiting for transfers between devices: 15.2 us -> 17.4 us
    ppermute x9 -> x4, starting transfers between devices: 8.19 us -> 3.5 us  [turns(): received.append(lax.ppermute(parts[turn], axis, route))]
    ppermute x9 -> x4, waiting for transfers between devices: 3.05 us -> 7.47 us  [turns(): received.append(lax.ppermute(parts[turn], axis, route))]
    ppermute x3 -> x5, starting transfers between devices: 3.98 us -> 6.44 us  [from_behind(): return lax.ppermute(block, axis, route)]
    ppermute x3 -> x5, waiting for transfers between devices: 12.1 us -> 9.91 us  [from_behind(): return lax.ppermute(block, axis, route)]
    pallas_call x5 -> x8, Pallas kernels: 9.62 us -> 9.72 us  [the longest x3 7.97 us: pairs(): pl.pallas_call(functools.partial(pairs_kernel, [len(partner) for partner...]
  transfers between devices with their start and end apart: 14 -> 11, of which waited for: 6 -> 7; matrix products, arithmetic and copies ran while one was open for 0% -> 0% of each run, Pallas kernels for 24% -> 20%
where the time goes in v7:
time: 44.1 us; the launch traced here: 43.7 us
  waiting for transfers between devices  17.4 us (39%)
  Pallas kernels  12.4 us (28%)
  starting transfers between devices  11.7 us (27%)
  local copies, waits for them, and re-layouts  2.03 us (5%)
    ppermute x5, waiting for transfers between devices, from_behind(): return lax.ppermute(block, axis, route)  9.91 us
    pallas_call x3, Pallas kernels, pairs(): pl.pallas_call(functools.partial(pairs_kernel, [len(partner) for partner...  7.97 us
    ppermute x4, waiting for transfers between devices, turns(): received.append(lax.ppermute(parts[turn], axis, route))  7.47 us
    ppermute x5, starting transfers between devices, from_behind(): return lax.ppermute(block, axis, route)  6.44 us
    ppermute x4, starting transfers between devices, turns(): received.append(lax.ppermute(parts[turn], axis, route))  3.5 us
    unnamed x11, local copies, waits for them, and re-layouts  2.03 us
    pallas_call x1, Pallas kernels, local(): pl.pallas_call(table_kernel, out_shape=jax.ShapeDtypeStruct((4, f_dev, LA...  1.73 us
    pallas_call x1, Pallas kernels, local(): pl.pallas_call(functools.partial(combine_kernel, scale, n_win * n_freq, n...  1.44 us
  transfers between devices with their start and end apart: 11, of which 7 were waited for; matrix products, arithmetic and copies ran while one was open for 0% of the time, Pallas kernels for 20%

profile of v7, /device:TPU:0, one launch (start us, length us, event | category | flops | bytes accessed | tf_op | source)
XLA Modules:
  0.0 43.7 jit_solution(15872809950272489657)
XLA Ops:
  0.0 1.3 %collective-permute-start = (bf16[8,2,8,1024]{3,2,1,0:T(8,128)(2,1)}, bf16[8,2,8,1024]{3,2,1,0:T(8,128)(2,1)S(1)}, u32[]{:S(2)}, u32[]{:S(2)}) collective-permute-start(bf16[8,2,8,1024]{3,2,1,0:T(8,128)(2,1)} %x_ref.1), channel_id=1, source_target_pairs={{4,0},{8,4},{12,8},{5,1},{9,5},{13,9},{6,2},{10,6},{14,10},{7,3},{... | collective-permute-start | bytes 786440 | tf_op jit(solution)/shard_map/ppermute | solution.py:27
  1.3 0.0 copy-start.1
  1.3 0.9 %copy-done.1 = bf16[8,2,8,1024]{3,2,1,0:T(8,128)(2,1)S(1)} copy-done((bf16[8,2,8,1024]{3,2,1,0:T(8,128)(2,1)S(1)}, bf16[8,2,8,1024]{3,2,1,0:T(8,128)(2,1)}, u32[]{:S(2)}) %copy-start.1) | copy-done | bytes 262168
  2.2 0.0 copy-start.2
  2.2 0.0 copy-start.3
  2.2 0.1 shard_map.56
  2.4 0.5 %collective-permute-start.1 = (f32[8,8,1]{2,1,0:T(8,128)S(1)}, f32[8,8,1]{2,1,0:T(8,128)S(1)}, u32[]{:S(2)}, u32[]{:S(2)}) collective-permute-start(f32[8,8,1]{2,1,0:T(8,128)S(1)} %get-tuple-element.31), channel_id=1, source_target_pairs={{0,1},{1,0},{2,3},{3,2},{4,5},{5,4},{6,7},{7,6},{8,9},{9,8},{10,11... | collective-permute-start | bytes 776 | tf_op jit(solution)/shard_map/ppermute | solution.py:232
  2.8 1.3 %collective-permute-start.2 = (f32[8,8,1]{2,1,0:T(8,128)S(1)}, f32[8,8,1]{2,1,0:T(8,128)S(1)}, u32[]{:S(2)}, u32[]{:S(2)}) collective-permute-start(f32[8,8,1]{2,1,0:T(8,128)S(1)} %get-tuple-element.31), channel_id=1, source_target_pairs={{4,1},{5,0},{8,5},{9,4},{12,9},{13,8},{6,3},{7,2},{10,7},{11,6},{1... | collective-permute-start | bytes 776 | tf_op jit(solution)/shard_map/ppermute | solution.py:234
  4.1 0.1 pad_add_fusion.place_ref
  4.2 0.0 copy-start
  4.2 1.0 %copy-done = f32[2,96,512]{2,1,0:T(8,128)S(1)} copy-done((f32[2,96,512]{2,1,0:T(8,128)S(1)}, f32[2,96,512]{2,1,0:T(8,128)}, u32[]{:S(2)}) %copy-start) | copy-done | bytes 393240
  5.2 1.7 %shard_map.55.refs_4_.refs_3_ = bf16[4,1024,512]{2,1,0:T(8,128)(2,1)S(1)} custom-call(s32[2]{0:T(128)S(1)} %pad_add_fusion.place_ref, f32[2,96,512]{2,1,0:T(8,128)S(1)} %copy-done), custom_call_target="tpu_custom_call" | custom-call | bytes 8388608 | tf_op jit(solution)/shard_map/pallas_call | solution.py:239
  6.9 0.0 collective-permute-done.1.refs_0_
  7.0 0.0 copy-done.2
  7.0 0.8 %shard_map.57 = (bf16[8,2,8,1024]{3,2,1,0:T(8,128)(2,1)S(1)}, f32[8,2,8,1024]{3,2,1,0:T(8,128)S(1)}) custom-call(s32[8]{0:T(128)S(1)} %copy-done.2, bf16[8,2,8,1024]{3,2,1,0:T(8,128)(2,1)S(1)} %get-tuple-element.30.x_ref, f32[8,8,1]{2,1,0:T(8,128)S(1)} %collective-permute-done.1.refs_0_), custom_call_target="tpu_custom_call" | custom-call | tf_op jit(solution)/shard_map/pallas_call | solution.py:247
  7.8 4.0 %collective-permute-done.x_ref = bf16[8,2,8,1024]{3,2,1,0:T(8,128)(2,1)S(1)} collective-permute-done((bf16[8,2,8,1024]{3,2,1,0:T(8,128)(2,1)}, bf16[8,2,8,1024]{3,2,1,0:T(8,128)(2,1)S(1)}, u32[]{:S(2)}, u32[]{:S(2)}) %collective-permute-start) | collective-permute-done | bytes 262176 | tf_op jit(solution)/shard_map/ppermute | solution.py:27
  11.8 0.0 collective-permute-done.2.refs_0_
  11.8 0.2 shard_map.58
  12.0 1.3 %collective-permute-start.3 = (bf16[4,2,8,1024]{3,2,1,0:T(8,128)(2,1)S(1)}, bf16[4,2,8,1024]{3,2,1,0:T(8,128)(2,1)S(1)}, u32[]{:S(2)}, u32[]{:S(2)}) collective-permute-start(bf16[4,2,8,1024]{3,2,1,0:T(8,128)(2,1)S(1)} %get-tuple-element.34.refs_1_), channel_id=1, source_target_pairs={{4,0},{8,4},{12,8},{5,1},{9,5},{13,9},{6,2},{10,6},{14,10},{7,3},{... | collective-permute-start | bytes 393224 | tf_op jit(solution)/shard_map/ppermute | solution.py:27
  13.3 1.3 %collective-permute-start.4 = (bf16[4,2,8,1024]{3,2,1,0:T(8,128)(2,1)S(1)}, bf16[4,2,8,1024]{3,2,1,0:T(8,128)(2,1)S(1)}, u32[]{:S(2)}, u32[]{:S(2)}) collective-permute-start(bf16[4,2,8,1024]{3,2,1,0:T(8,128)(2,1)S(1)} %get-tuple-element.35.refs_2_), channel_id=1, source_target_pairs={{4,0},{8,4},{12,8},{5,1},{9,5},{13,9},{6,2},{10,6},{14,10},{7,3},{... | collective-permute-start | bytes 393224 | tf_op jit(solution)/shard_map/ppermute | solution.py:27
  14.6 0.0 copy-done.3
  14.6 3.7 %shard_map.59 = (f32[2,2,64,256]{3,2,1,0:T(8,128)S(1)}, f32[2,2,64,256]{3,2,1,0:T(8,128)S(1)}) custom-call(s32[2]{0:T(128)S(1)} %pad_add_fusion.place_ref, f32[8,2,8,1024]{3,2,1,0:T(8,128)S(1)} %get-tuple-element.36.own_ref, bf16[8,2,8,1024]{3,2,1,0:T(8,128)(2,1)S(1)} %get-tuple-element.37.refs_0_, bf16[4,2,8,1024]{3,2,1,0:T(8,128)(2,1)S(1)} %get-tuple-element.34.refs_1_, ...), custom_call_target="tpu_custom_call" | custom-call | flops 8589934592 | bytes 4194304 | tf_op jit(solution)/shard_map/pallas_call | solution.py:266
  18.4 1.9 %collective-permute-done.3.refs_0_ = bf16[4,2,8,1024]{3,2,1,0:T(8,128)(2,1)S(1)} collective-permute-done((bf16[4,2,8,1024]{3,2,1,0:T(8,128)(2,1)S(1)}, bf16[4,2,8,1024]{3,2,1,0:T(8,128)(2,1)S(1)}, u32[]{:S(2)}, u32[]{:S(2)}) %collective-permute-start.3) | collective-permute-done | bytes 131104 | tf_op jit(solution)/shard_map/ppermute | solution.py:27
  20.3 2.0 %collective-permute-done.4.refs_1_ = bf16[4,2,8,1024]{3,2,1,0:T(8,128)(2,1)S(1)} collective-permute-done((bf16[4,2,8,1024]{3,2,1,0:T(8,128)(2,1)S(1)}, bf16[4,2,8,1024]{3,2,1,0:T(8,128)(2,1)S(1)}, u32[]{:S(2)}, u32[]{:S(2)}) %collective-permute-start.4) | collective-permute-done | bytes 131104 | tf_op jit(solution)/shard_map/ppermute | solution.py:27
  22.3 0.0 collective-permute-start.6
  22.3 1.3 %collective-permute-start.5 = (bf16[4,2,8,1024]{3,2,1,0:T(8,128)(2,1)S(1)}, bf16[4,2,8,1024]{3,2,1,0:T(8,128)(2,1)S(1)}, u32[]{:S(2)}, u32[]{:S(2)}) collective-permute-start(bf16[4,2,8,1024]{3,2,1,0:T(8,128)(2,1)S(1)} %collective-permute-done.4.refs_1_), channel_id=1, source_target_pairs={{4,0},{8,4},{12,8},{5,1},{9,5},{13,9},{6,2},{10,6},{14,10},{7,3},{... | collective-permute-start | bytes 393224 | tf_op jit(solution)/shard_map/ppermute | solution.py:27
  23.6 1.3 %collective-permute-start.8 = (bf16[4,2,8,1024]{3,2,1,0:T(8,128)(2,1)S(1)}, bf16[4,2,8,1024]{3,2,1,0:T(8,128)(2,1)S(1)}, u32[]{:S(2)}, u32[]{:S(2)}) collective-permute-start(bf16[4,2,8,1024]{3,2,1,0:T(8,128)(2,1)S(1)} %collective-permute-done.3.refs_0_), channel_id=1, source_target_pairs={{4,0},{8,4},{12,8},{5,1},{9,5},{13,9},{6,2},{10,6},{14,10},{7,3},{... | collective-permute-start | bytes 393224 | tf_op jit(solution)/shard_map/ppermute | solution.py:27
  24.9 0.0 collective-permute-done.6.refs_1_
  24.9 1.7 %collective-permute-start.7 = (f32[2,64,256]{2,1,0:T(8,128)S(1)}, f32[2,64,256]{2,1,0:T(8,128)S(1)}, u32[]{:S(2)}, u32[]{:S(2)}) collective-permute-start(f32[2,64,256]{2,1,0:T(8,128)S(1)} %get-tuple-element.45), channel_id=1, source_target_pairs={{0,2},{2,0},{1,3},{3,1},{4,6},{6,4},{5,7},{7,5},{8,10},{10,8},{9,1... | collective-permute-start | bytes 393224 | tf_op jit(solution)/shard_map/ppermute | solution.py:282
  26.7 2.1 %shard_map.62 = (f32[1,2,64,256]{3,2,1,0:T(8,128)S(1)}, f32[1,2,64,256]{3,2,1,0:T(8,128)S(1)}) custom-call(s32[2]{0:T(128)S(1)} %pad_add_fusion.place_ref, f32[8,2,8,1024]{3,2,1,0:T(8,128)S(1)} %get-tuple-element.36.own_ref, bf16[4,2,8,1024]{3,2,1,0:T(8,128)(2,1)S(1)} %collective-permute-done.3.refs_0_, ...), custom_call_target="tpu_custom_call" | custom-call | flops 8589934592 | bytes 4194304 | tf_op jit(solution)/shard_map/pallas_call | solution.py:266
  28.8 2.1 %collective-permute-done.7.refs_1_ = f32[2,64,256]{2,1,0:T(8,128)S(1)} collective-permute-done((f32[2,64,256]{2,1,0:T(8,128)S(1)}, f32[2,64,256]{2,1,0:T(8,128)S(1)}, u32[]{:S(2)}, u32[]{:S(2)}) %collective-permute-start.7) | collective-permute-done | bytes 131104 | tf_op jit(solution)/shard_map/ppermute | solution.py:282
  30.9 0.0 collective-permute-done.5.refs_1_
  30.9 2.0 %collective-permute-done.8.refs_0_ = bf16[4,2,8,1024]{3,2,1,0:T(8,128)(2,1)S(1)} collective-permute-done((bf16[4,2,8,1024]{3,2,1,0:T(8,128)(2,1)S(1)}, bf16[4,2,8,1024]{3,2,1,0:T(8,128)(2,1)S(1)}, u32[]{:S(2)}, u32[]{:S(2)}) %collective-permute-start.8) | collective-permute-done | bytes 131104 | tf_op jit(solution)/shard_map/ppermute | solution.py:27
  32.9 0.0 copy-start.4
  32.9 2.1 %shard_map.63 = (f32[2,2,64,256]{3,2,1,0:T(8,128)S(1)}, f32[2,2,64,256]{3,2,1,0:T(8,128)S(1)}) custom-call(s32[2]{0:T(128)S(1)} %pad_add_fusion.place_ref, f32[8,2,8,1024]{3,2,1,0:T(8,128)S(1)} %get-tuple-element.36.own_ref, bf16[4,2,8,1024]{3,2,1,0:T(8,128)(2,1)S(1)} %collective-permute-done.8.refs_0_, ...), custom_call_target="tpu_custom_call" | custom-call | flops 8589934592 | bytes 4194304 | tf_op jit(solution)/shard_map/pallas_call | solution.py:266
  35.0 0.1 collective-permute-start.9
  35.1 1.5 %collective-permute-done.9.refs_1_ = f32[2,2,64,256]{3,2,1,0:T(8,128)S(1)} collective-permute-done((f32[2,2,64,256]{3,2,1,0:T(8,128)S(1)}, f32[2,2,64,256]{3,2,1,0:T(8,128)S(1)}, u32[]{:S(2)}, u32[]{:S(2)}) %collective-permute-start.9) | collective-permute-done | bytes 262176 | tf_op jit(solution)/shard_map/ppermute | solution.py:282
  36.7 1.7 %collective-permute-start.10 = (f32[2,64,256]{2,1,0:T(8,128)S(1)}, f32[2,64,256]{2,1,0:T(8,128)S(1)}, u32[]{:S(2)}, u32[]{:S(2)}) collective-permute-start(f32[2,64,256]{2,1,0:T(8,128)S(1)} %get-tuple-element.54), channel_id=1, source_target_pairs={{0,2},{2,0},{1,3},{3,1},{4,6},{6,4},{5,7},{7,5},{8,10},{10,8},{9,1... | collective-permute-start | bytes 393224 | tf_op jit(solution)/shard_map/ppermute | solution.py:282
  38.4 0.0 copy-done.4
  38.4 0.1 copy.6.mask_ref
  38.5 3.8 %collective-permute-done.10.refs_2_ = f32[2,64,256]{2,1,0:T(8,128)S(1)} collective-permute-done((f32[2,64,256]{2,1,0:T(8,128)S(1)}, f32[2,64,256]{2,1,0:T(8,128)S(1)}, u32[]{:S(2)}, u32[]{:S(2)}) %collective-permute-start.10) | collective-permute-done | bytes 131104 | tf_op jit(solution)/shard_map/ppermute | solution.py:282
  42.3 1.4 %shard_map.65 = f32[8,4,8,256]{3,2,1,0:T(8,128)} custom-call(s32[8,4]{1,0:T(8,128)S(1)} %copy.6.mask_ref, s32[2]{0:T(128)S(1)} %pad_add_fusion.place_ref, f32[2,64,256]{2,1,0:T(8,128)S(1)} %shard_map.61.refs_0_, f32[2,64,256]{2,1,0:T(8,128)S(1)} %get-tuple-element.53.refs_1_, f32[2,64,256]{2,1,0:T(8,128)S(1)} %collective-permute-done.10.refs_2_), custom_call_target="tpu_custom_call" | custom-call | tf_op jit(solution)/shard_map/pallas_call | solution.py:317
  (3 shorter events, 0.1 us)
Async XLA Ops:
  0.0 11.8 %collective-permute-start = (bf16[8,2,8,1024]{3,2,1,0:T(8,128)(2,1)}, bf16[8,2,8,1024]{3,2,1,0:T(8,128)(2,1)S(1)}, u32[]{:S(2)}, u32[]{:S(2)}) collective-permute-start(bf16[8,2,8,1024]{3,2,1,0:T(8,128)(2,1)} %x_ref.1), channel_id=1, source_target_pairs={{4,0},{8,4},{12,8},{5,1},{9,5},{13,9},{6,2},{10,6},{14,10},{7,3},{... | collective-permute-start | bytes 786440 | tf_op jit(solution)/shard_map/ppermute | solution.py:27
  1.3 1.0 %copy-start.1 = (bf16[8,2,8,1024]{3,2,1,0:T(8,128)(2,1)S(1)}, bf16[8,2,8,1024]{3,2,1,0:T(8,128)(2,1)}, u32[]{:S(2)}) copy-start(bf16[8,2,8,1024]{3,2,1,0:T(8,128)(2,1)} %x_ref.1) | copy-start | bytes 786436
  2.2 4.7 %copy-start.2 = (s32[8]{0:T(128)S(1)}, s32[8]{0:T(128)}, u32[]{:S(2)}) copy-start(s32[8]{0:T(128)} %keep_ref.1) | copy-start | bytes 100
  2.2 12.4 %copy-start.3 = (f32[2,2,1024]{2,1,0:T(2,128)S(1)}, f32[2,2,1024]{2,1,0:T(2,128)}, u32[]{:S(2)}) copy-start(f32[2,2,1024]{2,1,0:T(2,128)} %constant.11.clone.refs_3_.refs_2_) | copy-start | bytes 49156
  2.4 4.6 %collective-permute-start.1 = (f32[8,8,1]{2,1,0:T(8,128)S(1)}, f32[8,8,1]{2,1,0:T(8,128)S(1)}, u32[]{:S(2)}, u32[]{:S(2)}) collective-permute-start(f32[8,8,1]{2,1,0:T(8,128)S(1)} %get-tuple-element.31), channel_id=1, source_target_pairs={{0,1},{1,0},{2,3},{3,2},{4,5},{5,4},{6,7},{7,6},{8,9},{9,8},{10,11... | collective-permute-start | bytes 776 | tf_op jit(solution)/shard_map/ppermute | solution.py:232
  2.8 8.9 %collective-permute-start.2 = (f32[8,8,1]{2,1,0:T(8,128)S(1)}, f32[8,8,1]{2,1,0:T(8,128)S(1)}, u32[]{:S(2)}, u32[]{:S(2)}) collective-permute-start(f32[8,8,1]{2,1,0:T(8,128)S(1)} %get-tuple-element.31), channel_id=1, source_target_pairs={{4,1},{5,0},{8,5},{9,4},{12,9},{13,8},{6,3},{7,2},{10,7},{11,6},{1... | collective-permute-start | bytes 776 | tf_op jit(solution)/shard_map/ppermute | solution.py:234
  4.2 1.0 %copy-start = (f32[2,96,512]{2,1,0:T(8,128)S(1)}, f32[2,96,512]{2,1,0:T(8,128)}, u32[]{:S(2)}) copy-start(f32[2,96,512]{2,1,0:T(8,128)} %constant.10.clone.base_ref) | copy-start | bytes 1179652
  12.0 8.2 %collective-permute-start.3 = (bf16[4,2,8,1024]{3,2,1,0:T(8,128)(2,1)S(1)}, bf16[4,2,8,1024]{3,2,1,0:T(8,128)(2,1)S(1)}, u32[]{:S(2)}, u32[]{:S(2)}) collective-permute-start(bf16[4,2,8,1024]{3,2,1,0:T(8,128)(2,1)S(1)} %get-tuple-element.34.refs_1_), channel_id=1, source_target_pairs={{4,0},{8,4},{12,8},{5,1},{9,5},{13,9},{6,2},{10,6},{14,10},{7,3},{... | collective-permute-start | bytes 393224 | tf_op jit(solution)/shard_map/ppermute | solution.py:27
  13.3 9.0 %collective-permute-start.4 = (bf16[4,2,8,1024]{3,2,1,0:T(8,128)(2,1)S(1)}, bf16[4,2,8,1024]{3,2,1,0:T(8,128)(2,1)S(1)}, u32[]{:S(2)}, u32[]{:S(2)}) collective-permute-start(bf16[4,2,8,1024]{3,2,1,0:T(8,128)(2,1)S(1)} %get-tuple-element.35.refs_2_), channel_id=1, source_target_pairs={{4,0},{8,4},{12,8},{5,1},{9,5},{13,9},{6,2},{10,6},{14,10},{7,3},{... | collective-permute-start | bytes 393224 | tf_op jit(solution)/shard_map/ppermute | solution.py:27
  22.3 2.6 %collective-permute-start.6 = (f32[2,2,64,256]{3,2,1,0:T(8,128)S(1)}, f32[2,2,64,256]{3,2,1,0:T(8,128)S(1)}, u32[]{:S(2)}, u32[]{:S(2)}) collective-permute-start(f32[2,2,64,256]{3,2,1,0:T(8,128)S(1)} %get-tuple-element.43), channel_id=1, source_target_pairs={{0,1},{1,0},{2,3},{3,2},{4,5},{5,4},{6,7},{7,6},{8,9},{9,8},{10,11... | collective-permute-start | bytes 786440 | tf_op jit(solution)/shard_map/ppermute | solution.py:282
  22.3 8.6 %collective-permute-start.5 = (bf16[4,2,8,1024]{3,2,1,0:T(8,128)(2,1)S(1)}, bf16[4,2,8,1024]{3,2,1,0:T(8,128)(2,1)S(1)}, u32[]{:S(2)}, u32[]{:S(2)}) collective-permute-start(bf16[4,2,8,1024]{3,2,1,0:T(8,128)(2,1)S(1)} %collective-permute-done.4.refs_1_), channel_id=1, source_target_pairs={{4,0},{8,4},{12,8},{5,1},{9,5},{13,9},{6,2},{10,6},{14,10},{7,3},{... | collective-permute-start | bytes 393224 | tf_op jit(solution)/shard_map/ppermute | solution.py:27
  23.6 9.3 %collective-permute-start.8 = (bf16[4,2,8,1024]{3,2,1,0:T(8,128)(2,1)S(1)}, bf16[4,2,8,1024]{3,2,1,0:T(8,128)(2,1)S(1)}, u32[]{:S(2)}, u32[]{:S(2)}) collective-permute-start(bf16[4,2,8,1024]{3,2,1,0:T(8,128)(2,1)S(1)} %collective-permute-done.3.refs_0_), channel_id=1, source_target_pairs={{4,0},{8,4},{12,8},{5,1},{9,5},{13,9},{6,2},{10,6},{14,10},{7,3},{... | collective-permute-start | bytes 393224 | tf_op jit(solution)/shard_map/ppermute | solution.py:27
  24.9 6.0 %collective-permute-start.7 = (f32[2,64,256]{2,1,0:T(8,128)S(1)}, f32[2,64,256]{2,1,0:T(8,128)S(1)}, u32[]{:S(2)}, u32[]{:S(2)}) collective-permute-start(f32[2,64,256]{2,1,0:T(8,128)S(1)} %get-tuple-element.45), channel_id=1, source_target_pairs={{0,2},{2,0},{1,3},{3,1},{4,6},{6,4},{5,7},{7,5},{8,10},{10,8},{9,1... | collective-permute-start | bytes 393224 | tf_op jit(solution)/shard_map/ppermute | solution.py:282
  32.9 5.5 %copy-start.4 = (s32[8,4]{0,1:T(4,128)S(1)}, s32[8,4]{0,1:T(4,128)}, u32[]{:S(2)}) copy-start(s32[8,4]{0,1:T(4,128)} %param.7) | copy-start | bytes 388
  35.0 1.6 %collective-permute-start.9 = (f32[2,2,64,256]{3,2,1,0:T(8,128)S(1)}, f32[2,2,64,256]{3,2,1,0:T(8,128)S(1)}, u32[]{:S(2)}, u32[]{:S(2)}) collective-permute-start(f32[2,2,64,256]{3,2,1,0:T(8,128)S(1)} %get-tuple-element.52), channel_id=1, source_target_pairs={{0,1},{1,0},{2,3},{3,2},{4,5},{5,4},{6,7},{7,6},{8,9},{9,8},{10,11... | collective-permute-start | bytes 786440 | tf_op jit(solution)/shard_map/ppermute | solution.py:282
  36.7 5.6 %collective-permute-start.10 = (f32[2,64,256]{2,1,0:T(8,128)S(1)}, f32[2,64,256]{2,1,0:T(8,128)S(1)}, u32[]{:S(2)}, u32[]{:S(2)}) collective-permute-start(f32[2,64,256]{2,1,0:T(8,128)S(1)} %get-tuple-element.54), channel_id=1, source_target_pairs={{0,2},{2,0},{1,3},{3,1},{4,6},{6,4},{5,7},{7,5},{8,10},{10,8},{9,1... | collective-permute-start | bytes 393224 | tf_op jit(solution)/shard_map/ppermute | solution.py:282

commit v8 on v7

--- a/solution.py
+++ b/solution.py
@@ -17,7 +17,6 @@
 SUBLANES = 8
 FINE = 32
 BLOCK = 256
-PIECES = 2
 VMEM_LIMIT = 16 * 1024 * 1024
 
 
@@ -50,24 +49,20 @@
         copy_ref[w] = x
 
 
-def whiten_kernel(n_bins, n_pieces, x_ref, *refs):
-    out_refs = refs[-n_pieces:]
-    per_piece = x_ref.shape[0] // n_pieces
+def whiten_kernel(n_bins, x_ref, *refs):
+    out_ref = refs[-1]
     for w in range(x_ref.shape[0]):
         power = bin_power(x_ref[w])
-        for ref in refs[:-n_pieces]:
+        for ref in refs[:-1]:
             power = power + ref[w]
         scale = lax.rsqrt(power / n_bins + EPS)
         for part in range(2):
-            value = x_ref[w, part].astype(jnp.float32) * scale
-            out_refs[w // per_piece][w % per_piece, part] = value.astype(jnp.bfloat16)
-
-
-def own_kernel(n_bins, keep_ref, x_ref, *refs):
-    white_ref, own_ref = refs[-2:]
-    whiten_kernel(n_bins, 1, x_ref, *refs[:-2], white_ref)
-    for w in range(x_ref.shape[0]):
-        own_ref[w] = white_ref[w].astype(jnp.float32) * keep_ref[w].astype(jnp.float32)
+            out_ref[w, part] = (x_ref[w, part].astype(jnp.float32) * scale).astype(jnp.bfloat16)
+
+
+def keep_kernel(keep_ref, white_ref, out_ref):
+    for w in range(white_ref.shape[0]):
+        out_ref[w] = white_ref[w].astype(jnp.float32) * keep_ref[w].astype(jnp.float32)
 
 
 def table_kernel(place_ref, base_ref, table_ref):
@@ -93,46 +88,39 @@
         lax.fori_loop(0, f_dev // (FINE * SUBLANES), body, 0)
 
 
-def cross_tile(own_ref, piece_refs, lanes):
-    ch = own_ref.shape[2]
+def cross_tile(base_ref, partner_ref, lanes):
+    w_dev, _, ch, _ = base_ref.shape
     real = [None] * ch
     imag = [None] * ch
-    windows = [(ref, n) for ref in piece_refs for n in range(ref.shape[0])]
-    for w, (ref, n) in enumerate(windows):
-        partner_re = ref[n, 0, :, lanes].astype(jnp.float32)
-        partner_im = ref[n, 1, :, lanes].astype(jnp.float32)
+    for w in range(w_dev):
+        partner_re = partner_ref[w, 0, :, lanes].astype(jnp.float32)
+        partner_im = partner_ref[w, 1, :, lanes].astype(jnp.float32)
         for i in range(ch):
-            own_re = own_ref[w, 0, i:i + 1, lanes]
-            own_im = own_ref[w, 1, i:i + 1, lanes]
-            re = own_re * partner_re + own_im * partner_im
-            im = own_im * partner_re - own_re * partner_im
+            base_re = base_ref[w, 0, i:i + 1, lanes]
+            base_im = base_ref[w, 1, i:i + 1, lanes]
+            re = base_re * partner_re + base_im * partner_im
+            im = base_im * partner_re - base_re * partner_im
             real[i] = re if w == 0 else real[i] + re
             imag[i] = im if w == 0 else imag[i] + im
     return real, imag
 
 
-def pairs_kernel(n_pieces, n_win, n_freq, place_ref, own_ref, *refs):
-    total_pieces = sum(n_pieces)
-    piece_refs = refs[:total_pieces]
-    twist_ref, table_ref = refs[total_pieces:total_pieces + 2]
-    before_refs = refs[total_pieces + 2:-2 - n_freq]
+def pairs_kernel(n_partners, n_win, n_freq, place_ref, base_ref, *refs):
+    partner_refs = refs[:n_partners]
+    twist_ref, table_ref = refs[n_partners:n_partners + 2]
     out_refs = refs[-2 - n_freq:-2]
     rows_ref, sums_ref = refs[-2:]
-    ch, f_dev = own_ref.shape[2:]
+    ch, f_dev = base_ref.shape[2:]
     pairs = ch * ch
     groups = n_win * n_freq
-    done = out_refs[0].shape[0] - len(n_pieces)
     width = out_refs[0].shape[-1]
     freq, win = place_ref[0], place_ref[1]
     dot = functools.partial(jnp.dot, preferred_element_type=jnp.float32)
-    for before_ref, out_ref in zip(before_refs, out_refs):
-        out_ref[:done] = before_ref[...]
-    for n, count in enumerate(n_pieces):
-        partner_refs = piece_refs[sum(n_pieces[:n]):sum(n_pieces[:n]) + count]
+    for k, partner_ref in enumerate(partner_refs):
 
         def body(tile, carry):
             lanes = pl.ds(pl.multiple_of(tile * LANES, LANES), LANES)
-            real, imag = cross_tile(own_ref, partner_refs, lanes)
+            real, imag = cross_tile(base_ref, partner_ref, lanes)
             cos = twist_ref[freq, 0:1, lanes]
             sin = twist_ref[freq, 1:2, lanes]
             for i in range(0, ch, 2):
@@ -155,7 +143,7 @@
                 block = jnp.where(upper, owner - groups // 2, groups // 2 - 1 - owner)
                 sign = jnp.where(upper, -1.0, 1.0)
                 lags = pl.ds(pl.multiple_of(block * width, LANES), width)
-                out_ref[done + n, turn_win] = sums_ref[0, :, lags] + sign * sums_ref[1, :, lags]
+                out_ref[k, turn_win] = sums_ref[0, :, lags] + sign * sums_ref[1, :, lags]
 
 
 def add_kernel(n_parts, *refs):
@@ -163,14 +151,19 @@
         total = refs[0][:, turn]
         for ref in refs[1:n_parts]:
             total = total + ref[:, turn]
-        out_ref[...] = total
-
-
-def total_kernel(*refs):
+        out_ref[...] = total.astype(out_ref.dtype)
+
+
+def total_kernel(n_parts, *refs):
+    out_ref = refs[-1]
     total = refs[0][...]
-    for ref in refs[1:-1]:
-        total = total + ref[...]
-    refs[-1][...] = total
+    for ref in refs[1:n_parts]:
+        total = total + ref[...].astype(jnp.float32)
+    start = 0
+    for ref in refs[n_parts:-1]:
+        out_ref[start:start + ref.shape[0]] = ref[...].astype(out_ref.dtype)
+        start += ref.shape[0]
+    out_ref[start:] = total.astype(out_ref.dtype)
 
 
 def reverse_lanes(value):
@@ -187,11 +180,9 @@
     ch = out_ref.shape[0]
     lower = place_ref[1] * n_freq + place_ref[0] < groups // 2
     k = 0
-    for parts in (refs[:1], refs[1:-1]):
-        for n in range(parts[0].shape[0]):
-            total = parts[0][n]
-            for ref in parts[1:]:
-                total = total + ref[n]
+    for ref in refs[:-1]:
+        for n in range(ref.shape[0]):
+            total = ref[n].astype(jnp.float32)
             total = jnp.where(lower, reverse_lanes(total), total)
             for i in range(ch):
                 factor = mask_ref[i, k].astype(jnp.float32) * scale
@@ -244,36 +235,32 @@
     twist = phases(F_LO + np.arange(n_bins), np.ones(1)).reshape(2, n_freq, f_dev)
     twist = jnp.asarray(np.moveaxis(twist, 0, 1))
 
-    white, own = pl.pallas_call(
-        functools.partial(own_kernel, n_bins),
-        out_shape=[
-            jax.ShapeDtypeStruct(spectra.shape, jnp.bfloat16),
-            jax.ShapeDtypeStruct(spectra.shape, jnp.float32),
-        ],
-        in_specs=[SMEM] + [VMEM] * n_freq, out_specs=[VMEM] * 2, compiler_params=params,
-    )(keep, copied, *own_power)
-    raw, table, white = lax.optimization_barrier((raw, table, white))
-    piece = jax.ShapeDtypeStruct((w_dev // PIECES,) + raw.shape[1:], jnp.bfloat16)
-    moving = pl.pallas_call(
-        functools.partial(whiten_kernel, n_bins, PIECES),
-        out_shape=[piece] * PIECES,
-        in_specs=[VMEM] * n_freq, out_specs=[VMEM] * PIECES, compiler_params=params,
-    )(raw, *next_power)
-
-    def pairs(partners, before):
-        pieces = [piece for partner in partners for piece in partner]
-        n = len(partners) + (before[0].shape[0] if before else 0)
+    def whiten(block, others):
         return pl.pallas_call(
-            functools.partial(pairs_kernel, [len(partner) for partner in partners], n_win, n_freq),
-            out_shape=[jax.ShapeDtypeStruct((n, n_win, ch * ch, width), jnp.float32)] * n_freq,
-            in_specs=[SMEM] + [VMEM] * (3 + len(pieces) + len(before)), out_specs=[VMEM] * n_freq,
+            functools.partial(whiten_kernel, n_bins),
+            out_shape=jax.ShapeDtypeStruct(block.shape, jnp.bfloat16),
+            in_specs=[VMEM] * (1 + len(others)), out_specs=VMEM, compiler_params=params,
+        )(block, *others)
+
+    def kept(block):
+        return pl.pallas_call(
+            keep_kernel,
+            out_shape=jax.ShapeDtypeStruct(block.shape, jnp.float32),
+            in_specs=[SMEM, VMEM], out_specs=VMEM, compiler_params=params,
+        )(keep, block)
+
+    def pairs(base, partners):
+        return pl.pallas_call(
+            functools.partial(pairs_kernel, len(partners), n_win, n_freq),
+            out_shape=[jax.ShapeDtypeStruct((len(partners), n_win, ch * ch, width), jnp.float32)] * n_freq,
+            in_specs=[SMEM] + [VMEM] * (3 + len(partners)), out_specs=[VMEM] * n_freq,
             scratch_shapes=[
                 pltpu.VMEM((2, 2 * ch * ch, f_dev), jnp.bfloat16),
                 pltpu.VMEM((2, ch * ch, LAGS // 2), jnp.float32),
             ],
             compiler_params=params,
             cost_estimate=cost(2 ** 33, 2 ** 22),
-        )(places, own, *pieces, twist, table, *before)
+        )(places, base, *partners, twist, table)
 
     def turns(parts, axis, size):
         received = [parts[0]]
@@ -282,43 +269,43 @@
             received.append(lax.ppermute(parts[turn], axis, route))
         return received
 
-    def gather_bins(parts):
+    def reduce(parts, before, dtype):
         n = parts[0].shape[0]
-        return pl.pallas_call(
+        kinds = [jnp.float32] + [jnp.bfloat16] * (n_win - 1)
+        sums = pl.pallas_call(
             functools.partial(add_kernel, n_freq),
-            out_shape=[jax.ShapeDtypeStruct((n, ch * ch, width), jnp.float32)] * n_win,
+            out_shape=[jax.ShapeDtypeStruct((n, ch * ch, width), kind) for kind in kinds],
             in_specs=[VMEM] * n_freq, out_specs=[VMEM] * n_win, compiler_params=params,
         )(*turns(parts, "freq", n_freq))
-
-    def total(parts):
+        n += sum(part.shape[0] for part in before)
         return pl.pallas_call(
-            total_kernel,
-            out_shape=jax.ShapeDtypeStruct(parts[0].shape, jnp.float32),
-            in_specs=[VMEM] * len(parts), out_specs=VMEM, compiler_params=params,
-        )(*parts)
-
-    parts = list(pairs([[white], moving], []))
-    early = None
-    for step in range(1, reach):
-        arrived = [from_behind(block, "chan", -1) for block in moving]
+            functools.partial(total_kernel, n_win),
+            out_shape=jax.ShapeDtypeStruct((n, ch * ch, width), dtype),
+            in_specs=[VMEM] * (n_win + len(before)), out_specs=VMEM, compiler_params=params,
+        )(*turns(sums, "win", n_win), *before)
+
+    white = whiten(copied, own_power)
+    above = from_behind(white, "chan", 1)
+    raw, table, white = lax.optimization_barrier((raw, table, white))
+    moving = whiten(raw, next_power)
+    parts = pairs(kept(white), [white, moving])
+    base = kept(above)
+    finished = []
+    for step in range(1, reach - 1):
+        arrived = from_behind(moving, "chan", -1)
+        finished.append(reduce(pairs(base, [moving]), [], jnp.float32))
         if step == 1:
-            arrived, parts = lax.optimization_barrier((arrived, parts))
-            sums = list(gather_bins(parts))
-            early = total(turns(sums, "win", n_win))
-            parts = []
-        else:
-            parts = pairs([moving], parts)
+            near = reduce(parts, [], jnp.float32)
+            arrived, near, finished = lax.optimization_barrier((arrived, near, finished))
         moving = arrived
-    if early is not None:
-        moving[-1], early = lax.optimization_barrier((moving[-1], early))
-        parts = pairs([moving], parts)
-    received = turns(gather_bins(parts), "win", n_win)
+    shipped = reduce(pairs(base, [moving]), finished, jnp.bfloat16)
+    shipped = from_behind(shipped, "chan", -1)
     scale = 1.0 / math.sqrt(w_dev * n_win * n_bins)
     return pl.pallas_call(
         functools.partial(combine_kernel, scale, n_win * n_freq, n_freq),
         out_shape=jax.ShapeDtypeStruct((ch, reach + 1, ch, width), jnp.float32),
-        in_specs=[SMEM] * 2 + [VMEM] * (1 + len(received)), out_specs=VMEM, compiler_params=params,
-    )(pair_mask, places, early, *received)
+        in_specs=[SMEM] * 2 + [VMEM] * 2, out_specs=VMEM, compiler_params=params,
+    )(pair_mask, places, near, shipped)
 
 
 def solution(mesh):

time: 44.1 us -> 44.5 us (level)
  waiting for transfers between devices: 17.4 us -> 12.8 us
  starting transfers between devices: 11.7 us -> 16.1 us
  Pallas kernels: 12.4 us -> 13 us
    ppermute x5 -> x4, waiting for transfers between devices: 9.91 us -> 5.48 us  [from_behind(): return lax.ppermute(block, axis, route)]
    ppermute x5 -> x4, starting transfers between devices: 6.44 us -> 9.65 us  [from_behind(): return lax.ppermute(block, axis, route)]
    ppermute x4 -> x6, starting transfers between devices: 3.5 us -> 4.73 us  [turns(): received.append(lax.ppermute(parts[turn], axis, route))]
    pallas_call x8 -> x13, Pallas kernels: 9.06 us -> 9.69 us  [the longest x3 7.96 us: pairs(): pl.pallas_call(functools.partial(pairs_kernel, len(partners), n_win, n_fr...]
    ppermute x4 -> x6, waiting for transfers between devices: 7.47 us -> 7.27 us  [turns(): received.append(lax.ppermute(parts[turn], axis, route))]
  transfers between devices with their start and end apart: 11 -> 12, of which waited for: 7 -> 4; matrix products, arithmetic and copies ran while one was open for 0% -> 0% of each run, Pallas kernels for 20% -> 21%
where the time goes in v8:
time: 44.5 us; the launch traced here: 44.2 us
  starting transfers between devices  16.1 us (36%)
  Pallas kernels  13 us (29%)
  waiting for transfers between devices  12.8 us (29%)
  local copies, waits for them, and re-layouts  2.03 us (5%)
    ppermute x4, starting transfers between devices, from_behind(): return lax.ppermute(block, axis, route)  9.65 us
    pallas_call x3, Pallas kernels, pairs(): pl.pallas_call(functools.partial(pairs_kernel, len(partners), n_win, n_fr...  7.96 us
    ppermute x6, waiting for transfers between devices, turns(): received.append(lax.ppermute(parts[turn], axis, route))  7.27 us
    ppermute x4, waiting for transfers between devices, from_behind(): return lax.ppermute(block, axis, route)  5.48 us
    ppermute x6, starting transfers between devices, turns(): received.append(lax.ppermute(parts[turn], axis, route))  4.73 us
    unnamed x11, local copies, waits for them, and re-layouts  2.03 us
    pallas_call x1, Pallas kernels, local(): pl.pallas_call(table_kernel, out_shape=jax.ShapeDtypeStruct((4, f_dev, LA...  1.73 us
    pallas_call x1, Pallas kernels, local(): pl.pallas_call(functools.partial(combine_kernel, scale, n_win * n_freq, n...  1.43 us
  transfers between devices with their start and end apart: 12, of which 4 were waited for; matrix products, arithmetic and copies ran while one was open for 0% of the time, Pallas kernels for 21%

profile of v8, /device:TPU:0, one launch (start us, length us, event | category | flops | bytes accessed | tf_op | source)
XLA Modules:
  0.0 44.2 jit_solution(10802181078365526000)
XLA Ops:
  0.0 1.3 %collective-permute-start = (bf16[8,2,8,1024]{3,2,1,0:T(8,128)(2,1)}, bf16[8,2,8,1024]{3,2,1,0:T(8,128)(2,1)S(1)}, u32[]{:S(2)}, u32[]{:S(2)}) collective-permute-start(bf16[8,2,8,1024]{3,2,1,0:T(8,128)(2,1)} %x_ref.1), channel_id=1, source_target_pairs={{4,0},{8,4},{12,8},{5,1},{9,5},{13,9},{6,2},{10,6},{14,10},{7,3},{... | collective-permute-start | bytes 786440 | tf_op jit(solution)/shard_map/ppermute | solution.py:26
  1.3 0.0 copy-start.1
  1.3 0.9 %copy-done.1 = bf16[8,2,8,1024]{3,2,1,0:T(8,128)(2,1)S(1)} copy-done((bf16[8,2,8,1024]{3,2,1,0:T(8,128)(2,1)S(1)}, bf16[8,2,8,1024]{3,2,1,0:T(8,128)(2,1)}, u32[]{:S(2)}) %copy-start.1) | copy-done | bytes 262168
  2.2 0.0 copy-start.2
  2.2 0.0 copy-start.3
  2.2 0.1 shard_map.56
  2.4 0.5 %collective-permute-start.1 = (f32[8,8,1]{2,1,0:T(8,128)S(1)}, f32[8,8,1]{2,1,0:T(8,128)S(1)}, u32[]{:S(2)}, u32[]{:S(2)}) collective-permute-start(f32[8,8,1]{2,1,0:T(8,128)S(1)} %get-tuple-element.26), channel_id=1, source_target_pairs={{0,1},{1,0},{2,3},{3,2},{4,5},{5,4},{6,7},{7,6},{8,9},{9,8},{10,11... | collective-permute-start | bytes 776 | tf_op jit(solution)/shard_map/ppermute | solution.py:223
  2.8 1.3 %collective-permute-start.2 = (f32[8,8,1]{2,1,0:T(8,128)S(1)}, f32[8,8,1]{2,1,0:T(8,128)S(1)}, u32[]{:S(2)}, u32[]{:S(2)}) collective-permute-start(f32[8,8,1]{2,1,0:T(8,128)S(1)} %get-tuple-element.26), channel_id=1, source_target_pairs={{4,1},{5,0},{8,5},{9,4},{12,9},{13,8},{6,3},{7,2},{10,7},{11,6},{1... | collective-permute-start | bytes 776 | tf_op jit(solution)/shard_map/ppermute | solution.py:225
  4.1 0.1 pad_add_fusion.place_ref
  4.2 0.0 copy-start
  4.2 1.0 %copy-done = f32[2,96,512]{2,1,0:T(8,128)S(1)} copy-done((f32[2,96,512]{2,1,0:T(8,128)S(1)}, f32[2,96,512]{2,1,0:T(8,128)}, u32[]{:S(2)}) %copy-start) | copy-done | bytes 393240
  5.2 1.7 %shard_map.55.refs_3_.refs_2_ = bf16[4,1024,512]{2,1,0:T(8,128)(2,1)S(1)} custom-call(s32[2]{0:T(128)S(1)} %pad_add_fusion.place_ref, f32[2,96,512]{2,1,0:T(8,128)S(1)} %copy-done), custom_call_target="tpu_custom_call" | custom-call | bytes 8388608 | tf_op jit(solution)/shard_map/pallas_call | solution.py:230
  6.9 0.0 collective-permute-done.1.refs_0_
  7.0 0.2 shard_map.57.white_ref.refs_0_
  7.2 5.8 %collective-permute-start.6 = (bf16[8,2,8,1024]{3,2,1,0:T(8,128)(2,1)S(1)}, bf16[8,2,8,1024]{3,2,1,0:T(8,128)(2,1)S(1)}, u32[]{:S(2)}, u32[]{:S(2)}) collective-permute-start(bf16[8,2,8,1024]{3,2,1,0:T(8,128)(2,1)S(1)} %shard_map.57.white_ref.refs_0_), channel_id=1, source_target_pairs={{0,4},{4,8},{8,12},{1,5},{5,9},{9,13},{2,6},{6,10},{10,14},{3,7},{... | collective-permute-start | bytes 786440 | tf_op jit(solution)/shard_map/ppermute | solution.py:26
  13.0 0.0 collective-permute-done.x_ref
  13.0 0.0 collective-permute-done.2.refs_0_
  13.0 0.2 shard_map.58.refs_1_.refs_0_
  13.3 1.3 %collective-permute-start.3 = (bf16[8,2,8,1024]{3,2,1,0:T(8,128)(2,1)S(1)}, bf16[8,2,8,1024]{3,2,1,0:T(8,128)(2,1)S(1)}, u32[]{:S(2)}, u32[]{:S(2)}) collective-permute-start(bf16[8,2,8,1024]{3,2,1,0:T(8,128)(2,1)S(1)} %shard_map.58.refs_1_.refs_0_), channel_id=1, source_target_pairs={{4,0},{8,4},{12,8},{5,1},{9,5},{13,9},{6,2},{10,6},{14,10},{7,3},{... | collective-permute-start | bytes 786440 | tf_op jit(solution)/shard_map/ppermute | solution.py:26
  14.6 0.0 copy-done.2
  14.6 0.6 %shard_map.59.base_ref = f32[8,2,8,1024]{3,2,1,0:T(8,128)S(1)} custom-call(s32[8]{0:T(128)S(1)} %copy-done.2, bf16[8,2,8,1024]{3,2,1,0:T(8,128)(2,1)S(1)} %shard_map.57.white_ref.refs_0_), custom_call_target="tpu_custom_call" | custom-call | tf_op jit(solution)/shard_map/pallas_call | solution.py:246
  15.2 0.0 copy-done.3
  15.2 3.7 %shard_map.60 = (f32[2,2,64,256]{3,2,1,0:T(8,128)S(1)}, f32[2,2,64,256]{3,2,1,0:T(8,128)S(1)}) custom-call(s32[2]{0:T(128)S(1)} %pad_add_fusion.place_ref, f32[8,2,8,1024]{3,2,1,0:T(8,128)S(1)} %shard_map.59.base_ref, bf16[8,2,8,1024]{3,2,1,0:T(8,128)(2,1)S(1)} %shard_map.57.white_ref.refs_0_, bf16[8,2,8,1024]{3,2,1,0:T(8,128)(2,1)S(1)} %shard_map.58.refs_1_.refs_0_, ...), custom_call_target="tpu_custom_call" | custom-call | flops 8589934592 | bytes 4194304 | tf_op jit(solution)/shard_map/pallas_call | solution.py:253
  18.9 0.3 collective-permute-start.4
  19.2 0.0 collective-permute-done.6.white_ref
  19.2 0.6 %shard_map.63.base_ref = f32[8,2,8,1024]{3,2,1,0:T(8,128)S(1)} custom-call(s32[8]{0:T(128)S(1)} %copy-done.2, bf16[8,2,8,1024]{3,2,1,0:T(8,128)(2,1)S(1)} %collective-permute-done.6.white_ref), custom_call_target="tpu_custom_call" | custom-call | tf_op jit(solution)/shard_map/pallas_call | solution.py:246
  19.8 2.1 %shard_map.64 = (f32[1,2,64,256]{3,2,1,0:T(8,128)S(1)}, f32[1,2,64,256]{3,2,1,0:T(8,128)S(1)}) custom-call(s32[2]{0:T(128)S(1)} %pad_add_fusion.place_ref, f32[8,2,8,1024]{3,2,1,0:T(8,128)S(1)} %shard_map.63.base_ref, bf16[8,2,8,1024]{3,2,1,0:T(8,128)(2,1)S(1)} %shard_map.58.refs_1_.refs_0_, f32[2,2,1024]{2,1,0:T(2,128)S(1)} %copy-done.3, ...), custom_call_target="tpu_custom_call" | custom-call | flops 8589934592 | bytes 4194304 | tf_op jit(solution)/shard_map/pallas_call | solution.py:253
  21.9 0.4 collective-permute-start.7
  22.3 0.0 collective-permute-done.4.refs_1_
  22.3 2.0 %collective-permute-start.5 = (bf16[2,64,256]{2,1,0:T(8,128)(2,1)S(1)}, bf16[2,64,256]{2,1,0:T(8,128)(2,1)S(1)}, u32[]{:S(2)}, u32[]{:S(2)}) collective-permute-start(bf16[2,64,256]{2,1,0:T(8,128)(2,1)S(1)} %get-tuple-element.33), channel_id=1, source_target_pairs={{0,2},{2,0},{1,3},{3,1},{4,6},{6,4},{5,7},{7,5},{8,10},{10,8},{9,1... | collective-permute-start | bytes 196616 | tf_op jit(solution)/shard_map/ppermute | solution.py:269
  24.3 0.0 collective-permute-done.7.refs_1_
  24.3 1.0 %collective-permute-start.8 = (bf16[1,64,256]{2,1,0:T(8,128)(2,1)S(1)}, bf16[1,64,256]{2,1,0:T(8,128)(2,1)S(1)}, u32[]{:S(2)}, u32[]{:S(2)}) collective-permute-start(bf16[1,64,256]{2,1,0:T(8,128)(2,1)S(1)} %get-tuple-element.37), channel_id=1, source_target_pairs={{0,2},{2,0},{1,3},{3,1},{4,6},{6,4},{5,7},{7,5},{8,10},{10,8},{9,1... | collective-permute-start | bytes 98312 | tf_op jit(solution)/shard_map/ppermute | solution.py:269
  25.3 3.0 %collective-permute-done.8.refs_1_ = bf16[1,64,256]{2,1,0:T(8,128)(2,1)S(1)} collective-permute-done((bf16[1,64,256]{2,1,0:T(8,128)(2,1)S(1)}, bf16[1,64,256]{2,1,0:T(8,128)(2,1)S(1)}, u32[]{:S(2)}, u32[]{:S(2)}) %collective-permute-start.8) | collective-permute-done | bytes 32800 | tf_op jit(solution)/shard_map/ppermute | solution.py:269
  28.3 0.0 collective-permute-done.5.refs_1_
  28.3 0.0 copy-start.4
  28.3 0.0 collective-permute-done.3.refs_0_
  28.4 2.1 %shard_map.67 = (f32[1,2,64,256]{3,2,1,0:T(8,128)S(1)}, f32[1,2,64,256]{3,2,1,0:T(8,128)S(1)}) custom-call(s32[2]{0:T(128)S(1)} %pad_add_fusion.place_ref, f32[8,2,8,1024]{3,2,1,0:T(8,128)S(1)} %shard_map.63.base_ref, bf16[8,2,8,1024]{3,2,1,0:T(8,128)(2,1)S(1)} %collective-permute-done.3.refs_0_, f32[2,2,1024]{2,1,0:T(2,128)S(1)} %copy-done.3, ...), custom_call_target="tpu_custom_call" | custom-call | flops 8589934592 | bytes 4194304 | tf_op jit(solution)/shard_map/pallas_call | solution.py:253
  30.5 0.1 collective-permute-start.9
  30.6 1.3 %collective-permute-done.9.refs_1_ = f32[1,2,64,256]{3,2,1,0:T(8,128)S(1)} collective-permute-done((f32[1,2,64,256]{3,2,1,0:T(8,128)S(1)}, f32[1,2,64,256]{3,2,1,0:T(8,128)S(1)}, u32[]{:S(2)}, u32[]{:S(2)}) %collective-permute-start.9) | collective-permute-done | bytes 131104 | tf_op jit(solution)/shard_map/ppermute | solution.py:269
  31.9 1.0 %collective-permute-start.10 = (bf16[1,64,256]{2,1,0:T(8,128)(2,1)S(1)}, bf16[1,64,256]{2,1,0:T(8,128)(2,1)S(1)}, u32[]{:S(2)}, u32[]{:S(2)}) collective-permute-start(bf16[1,64,256]{2,1,0:T(8,128)(2,1)S(1)} %get-tuple-element.43), channel_id=1, source_target_pairs={{0,2},{2,0},{1,3},{3,1},{4,6},{6,4},{5,7},{7,5},{8,10},{10,8},{9,1... | collective-permute-start | bytes 98312 | tf_op jit(solution)/shard_map/ppermute | solution.py:269
  32.9 3.0 %collective-permute-done.10.refs_1_ = bf16[1,64,256]{2,1,0:T(8,128)(2,1)S(1)} collective-permute-done((bf16[1,64,256]{2,1,0:T(8,128)(2,1)S(1)}, bf16[1,64,256]{2,1,0:T(8,128)(2,1)S(1)}, u32[]{:S(2)}, u32[]{:S(2)}) %collective-permute-start.10) | collective-permute-done | bytes 32800 | tf_op jit(solution)/shard_map/ppermute | solution.py:269
  35.9 1.3 %collective-permute-start.11 = (bf16[2,64,256]{2,1,0:T(8,128)(2,1)S(1)}, bf16[2,64,256]{2,1,0:T(8,128)(2,1)S(1)}, u32[]{:S(2)}, u32[]{:S(2)}) collective-permute-start(bf16[2,64,256]{2,1,0:T(8,128)(2,1)S(1)} %shard_map.69), channel_id=1, source_target_pairs={{4,0},{8,4},{12,8},{5,1},{9,5},{13,9},{6,2},{10,6},{14,10},{7,3},{... | collective-permute-start | bytes 196616 | tf_op jit(solution)/shard_map/ppermute | solution.py:26
  37.2 0.0 copy-done.4
  37.2 0.1 copy.6.mask_ref
  37.3 5.5 %collective-permute-done.11.refs_1_ = bf16[2,64,256]{2,1,0:T(8,128)(2,1)S(1)} collective-permute-done((bf16[2,64,256]{2,1,0:T(8,128)(2,1)S(1)}, bf16[2,64,256]{2,1,0:T(8,128)(2,1)S(1)}, u32[]{:S(2)}, u32[]{:S(2)}) %collective-permute-start.11) | collective-permute-done | bytes 65568 | tf_op jit(solution)/shard_map/ppermute | solution.py:26
  42.8 1.4 %shard_map.70 = f32[8,4,8,256]{3,2,1,0:T(8,128)} custom-call(s32[8,4]{1,0:T(8,128)S(1)} %copy.6.mask_ref, s32[2]{0:T(128)S(1)} %pad_add_fusion.place_ref, f32[2,64,256]{2,1,0:T(8,128)S(1)} %shard_map.62.refs_0_, bf16[2,64,256]{2,1,0:T(8,128)(2,1)S(1)} %collective-permute-done.11.refs_1_), custom_call_target="tpu_custom_call" | custom-call | tf_op jit(solution)/shard_map/pallas_call | solution.py:304
  (6 shorter events, 0.1 us)
Async XLA Ops:
  0.0 13.0 %collective-permute-start = (bf16[8,2,8,1024]{3,2,1,0:T(8,128)(2,1)}, bf16[8,2,8,1024]{3,2,1,0:T(8,128)(2,1)S(1)}, u32[]{:S(2)}, u32[]{:S(2)}) collective-permute-start(bf16[8,2,8,1024]{3,2,1,0:T(8,128)(2,1)} %x_ref.1), channel_id=1, source_target_pairs={{4,0},{8,4},{12,8},{5,1},{9,5},{13,9},{6,2},{10,6},{14,10},{7,3},{... | collective-permute-start | bytes 786440 | tf_op jit(solution)/shard_map/ppermute | solution.py:26
  1.3 1.0 %copy-start.1 = (bf16[8,2,8,1024]{3,2,1,0:T(8,128)(2,1)S(1)}, bf16[8,2,8,1024]{3,2,1,0:T(8,128)(2,1)}, u32[]{:S(2)}) copy-start(bf16[8,2,8,1024]{3,2,1,0:T(8,128)(2,1)} %x_ref.1) | copy-start | bytes 786436
  2.2 12.3 %copy-start.2 = (s32[8]{0:T(128)S(1)}, s32[8]{0:T(128)}, u32[]{:S(2)}) copy-start(s32[8]{0:T(128)} %keep_ref.3) | copy-start | bytes 100
  2.2 12.9 %copy-start.3 = (f32[2,2,1024]{2,1,0:T(2,128)S(1)}, f32[2,2,1024]{2,1,0:T(2,128)}, u32[]{:S(2)}) copy-start(f32[2,2,1024]{2,1,0:T(2,128)} %constant.11.clone.refs_2_.refs_1_) | copy-start | bytes 49156
  2.4 4.6 %collective-permute-start.1 = (f32[8,8,1]{2,1,0:T(8,128)S(1)}, f32[8,8,1]{2,1,0:T(8,128)S(1)}, u32[]{:S(2)}, u32[]{:S(2)}) collective-permute-start(f32[8,8,1]{2,1,0:T(8,128)S(1)} %get-tuple-element.26), channel_id=1, source_target_pairs={{0,1},{1,0},{2,3},{3,2},{4,5},{5,4},{6,7},{7,6},{8,9},{9,8},{10,11... | collective-permute-start | bytes 776 | tf_op jit(solution)/shard_map/ppermute | solution.py:223
  2.8 10.2 %collective-permute-start.2 = (f32[8,8,1]{2,1,0:T(8,128)S(1)}, f32[8,8,1]{2,1,0:T(8,128)S(1)}, u32[]{:S(2)}, u32[]{:S(2)}) collective-permute-start(f32[8,8,1]{2,1,0:T(8,128)S(1)} %get-tuple-element.26), channel_id=1, source_target_pairs={{4,1},{5,0},{8,5},{9,4},{12,9},{13,8},{6,3},{7,2},{10,7},{11,6},{1... | collective-permute-start | bytes 776 | tf_op jit(solution)/shard_map/ppermute | solution.py:225
  4.2 1.0 %copy-start = (f32[2,96,512]{2,1,0:T(8,128)S(1)}, f32[2,96,512]{2,1,0:T(8,128)}, u32[]{:S(2)}) copy-start(f32[2,96,512]{2,1,0:T(8,128)} %constant.10.clone.base_ref) | copy-start | bytes 1179652
  7.2 12.0 %collective-permute-start.6 = (bf16[8,2,8,1024]{3,2,1,0:T(8,128)(2,1)S(1)}, bf16[8,2,8,1024]{3,2,1,0:T(8,128)(2,1)S(1)}, u32[]{:S(2)}, u32[]{:S(2)}) collective-permute-start(bf16[8,2,8,1024]{3,2,1,0:T(8,128)(2,1)S(1)} %shard_map.57.white_ref.refs_0_), channel_id=1, source_target_pairs={{0,4},{4,8},{8,12},{1,5},{5,9},{9,13},{2,6},{6,10},{10,14},{3,7},{... | collective-permute-start | bytes 786440 | tf_op jit(solution)/shard_map/ppermute | solution.py:26
  13.3 15.1 %collective-permute-start.3 = (bf16[8,2,8,1024]{3,2,1,0:T(8,128)(2,1)S(1)}, bf16[8,2,8,1024]{3,2,1,0:T(8,128)(2,1)S(1)}, u32[]{:S(2)}, u32[]{:S(2)}) collective-permute-start(bf16[8,2,8,1024]{3,2,1,0:T(8,128)(2,1)S(1)} %shard_map.58.refs_1_.refs_0_), channel_id=1, source_target_pairs={{4,0},{8,4},{12,8},{5,1},{9,5},{13,9},{6,2},{10,6},{14,10},{7,3},{... | collective-permute-start | bytes 786440 | tf_op jit(solution)/shard_map/ppermute | solution.py:26
  18.9 3.4 %collective-permute-start.4 = (f32[2,2,64,256]{3,2,1,0:T(8,128)S(1)}, f32[2,2,64,256]{3,2,1,0:T(8,128)S(1)}, u32[]{:S(2)}, u32[]{:S(2)}) collective-permute-start(f32[2,2,64,256]{3,2,1,0:T(8,128)S(1)} %get-tuple-element.31), channel_id=1, source_target_pairs={{0,1},{1,0},{2,3},{3,2},{4,5},{5,4},{6,7},{7,6},{8,9},{9,8},{10,11... | collective-permute-start | bytes 786440 | tf_op jit(solution)/shard_map/ppermute | solution.py:269
  21.9 2.4 %collective-permute-start.7 = (f32[1,2,64,256]{3,2,1,0:T(8,128)S(1)}, f32[1,2,64,256]{3,2,1,0:T(8,128)S(1)}, u32[]{:S(2)}, u32[]{:S(2)}) collective-permute-start(f32[1,2,64,256]{3,2,1,0:T(8,128)S(1)} %get-tuple-element.35), channel_id=1, source_target_pairs={{0,1},{1,0},{2,3},{3,2},{4,5},{5,4},{6,7},{7,6},{8,9},{9,8},{10,11... | collective-permute-start | bytes 393224 | tf_op jit(solution)/shard_map/ppermute | solution.py:269
  22.3 6.0 %collective-permute-start.5 = (bf16[2,64,256]{2,1,0:T(8,128)(2,1)S(1)}, bf16[2,64,256]{2,1,0:T(8,128)(2,1)S(1)}, u32[]{:S(2)}, u32[]{:S(2)}) collective-permute-start(bf16[2,64,256]{2,1,0:T(8,128)(2,1)S(1)} %get-tuple-element.33), channel_id=1, source_target_pairs={{0,2},{2,0},{1,3},{3,1},{4,6},{6,4},{5,7},{7,5},{8,10},{10,8},{9,1... | collective-permute-start | bytes 196616 | tf_op jit(solution)/shard_map/ppermute | solution.py:269
  24.3 4.0 %collective-permute-start.8 = (bf16[1,64,256]{2,1,0:T(8,128)(2,1)S(1)}, bf16[1,64,256]{2,1,0:T(8,128)(2,1)S(1)}, u32[]{:S(2)}, u32[]{:S(2)}) collective-permute-start(bf16[1,64,256]{2,1,0:T(8,128)(2,1)S(1)} %get-tuple-element.37), channel_id=1, source_target_pairs={{0,2},{2,0},{1,3},{3,1},{4,6},{6,4},{5,7},{7,5},{8,10},{10,8},{9,1... | collective-permute-start | bytes 98312 | tf_op jit(solution)/shard_map/ppermute | solution.py:269
  28.3 8.9 %copy-start.4 = (s32[8,4]{0,1:T(4,128)S(1)}, s32[8,4]{0,1:T(4,128)}, u32[]{:S(2)}) copy-start(s32[8,4]{0,1:T(4,128)} %param.7) | copy-start | bytes 388
  30.5 1.4 %collective-permute-start.9 = (f32[1,2,64,256]{3,2,1,0:T(8,128)S(1)}, f32[1,2,64,256]{3,2,1,0:T(8,128)S(1)}, u32[]{:S(2)}, u32[]{:S(2)}) collective-permute-start(f32[1,2,64,256]{3,2,1,0:T(8,128)S(1)} %get-tuple-element.41), channel_id=1, source_target_pairs={{0,1},{1,0},{2,3},{3,2},{4,5},{5,4},{6,7},{7,6},{8,9},{9,8},{10,11... | collective-permute-start | bytes 393224 | tf_op jit(solution)/shard_map/ppermute | solution.py:269
  31.9 4.0 %collective-permute-start.10 = (bf16[1,64,256]{2,1,0:T(8,128)(2,1)S(1)}, bf16[1,64,256]{2,1,0:T(8,128)(2,1)S(1)}, u32[]{:S(2)}, u32[]{:S(2)}) collective-permute-start(bf16[1,64,256]{2,1,0:T(8,128)(2,1)S(1)} %get-tuple-element.43), channel_id=1, source_target_pairs={{0,2},{2,0},{1,3},{3,1},{4,6},{6,4},{5,7},{7,5},{8,10},{10,8},{9,1... | collective-permute-start | bytes 98312 | tf_op jit(solution)/shard_map/ppermute | solution.py:269
  35.9 6.9 %collective-permute-start.11 = (bf16[2,64,256]{2,1,0:T(8,128)(2,1)S(1)}, bf16[2,64,256]{2,1,0:T(8,128)(2,1)S(1)}, u32[]{:S(2)}, u32[]{:S(2)}) collective-permute-start(bf16[2,64,256]{2,1,0:T(8,128)(2,1)S(1)} %shard_map.69), channel_id=1, source_target_pairs={{4,0},{8,4},{12,8},{5,1},{9,5},{13,9},{6,2},{10,6},{14,10},{7,3},{... | collective-permute-start | bytes 196616 | tf_op jit(solution)/shard_map/ppermute | solution.py:26

commit v9 on v8

--- a/solution.py
+++ b/solution.py
@@ -62,13 +62,13 @@
 
 def keep_kernel(keep_ref, white_ref, out_ref):
     for w in range(white_ref.shape[0]):
-        out_ref[w] = white_ref[w].astype(jnp.float32) * keep_ref[w].astype(jnp.float32)
-
-
-def table_kernel(place_ref, base_ref, table_ref):
+        out_ref[w] = white_ref[w].astype(jnp.float32) * keep_ref[w, :, :, 0:1]
+
+
+def table_kernel(base_ref, table_ref):
     f_dev, width = table_ref.shape[1:]
     coarse = base_ref.shape[1] - FINE
-    start = place_ref[0] * (f_dev // FINE)
+    start = lax.axis_index("freq") * (f_dev // FINE)
     for block in range(0, width, BLOCK):
         lags = slice(block, block + BLOCK)
         fine_cos = base_ref[0, coarse:, lags]
@@ -105,7 +105,7 @@
     return real, imag
 
 
-def pairs_kernel(n_partners, n_win, n_freq, place_ref, base_ref, *refs):
+def pairs_kernel(n_partners, n_win, n_freq, base_ref, *refs):
     partner_refs = refs[:n_partners]
     twist_ref, table_ref = refs[n_partners:n_partners + 2]
     out_refs = refs[-2 - n_freq:-2]
@@ -114,7 +114,7 @@
     pairs = ch * ch
     groups = n_win * n_freq
     width = out_refs[0].shape[-1]
-    freq, win = place_ref[0], place_ref[1]
+    freq, win = lax.axis_index("freq"), lax.axis_index("win")
     dot = functools.partial(jnp.dot, preferred_element_type=jnp.float32)
     for k, partner_ref in enumerate(partner_refs):
 
@@ -146,24 +146,24 @@
                 out_ref[k, turn_win] = sums_ref[0, :, lags] + sign * sums_ref[1, :, lags]
 
 
-def add_kernel(n_parts, *refs):
-    for turn, out_ref in enumerate(refs[n_parts:]):
-        total = refs[0][:, turn]
-        for ref in refs[1:n_parts]:
+def add_kernel(n_parts, n_before, *refs):
+    parts, befores, out_refs = refs[:n_parts], refs[n_parts:n_parts + n_before], refs[n_parts + n_before:]
+    for turn, out_ref in enumerate(out_refs):
+        start = 0
+        for before in befores:
+            out_ref[start:start + before.shape[0]] = before[:, turn].astype(out_ref.dtype)
+            start += before.shape[0]
+        total = parts[0][:, turn]
+        for ref in parts[1:]:
             total = total + ref[:, turn]
-        out_ref[...] = total.astype(out_ref.dtype)
-
-
-def total_kernel(n_parts, *refs):
-    out_ref = refs[-1]
+        out_ref[start:] = total.astype(out_ref.dtype)
+
+
+def plain_add_kernel(*refs):
     total = refs[0][...]
-    for ref in refs[1:n_parts]:
-        total = total + ref[...].astype(jnp.float32)
-    start = 0
-    for ref in refs[n_parts:-1]:
-        out_ref[start:start + ref.shape[0]] = ref[...].astype(out_ref.dtype)
-        start += ref.shape[0]
-    out_ref[start:] = total.astype(out_ref.dtype)
+    for ref in refs[1:-1]:
+        total = total + ref[...]
+    refs[-1][...] = total
 
 
 def reverse_lanes(value):
@@ -175,23 +175,24 @@
     return jnp.concatenate(pieces[::-1], axis=1)
 
 
-def combine_kernel(scale, groups, n_freq, mask_ref, place_ref, *refs):
+def combine_kernel(n_win, n_freq, factor_ref, *refs):
     out_ref = refs[-1]
     ch = out_ref.shape[0]
-    lower = place_ref[1] * n_freq + place_ref[0] < groups // 2
+    lower = lax.axis_index("win") * n_freq + lax.axis_index("freq") < n_win * n_freq // 2
     k = 0
-    for ref in refs[:-1]:
-        for n in range(ref.shape[0]):
-            total = ref[n].astype(jnp.float32)
-            total = jnp.where(lower, reverse_lanes(total), total)
+    for first in range(0, len(refs) - 1, n_win):
+        parts = refs[first:first + n_win]
+        for n in range(parts[0].shape[0]):
+            total = parts[0][n].astype(jnp.float32)
+            for ref in parts[1:]:
+                total = total + ref[n].astype(jnp.float32)
+            total = jnp.where(lower, reverse_lanes(total), total) * factor_ref[k]
             for i in range(ch):
-                factor = mask_ref[i, k].astype(jnp.float32) * scale
-                out_ref[i, k] = total[i * ch:(i + 1) * ch] * factor
+                out_ref[i, k] = total[i * ch:(i + 1) * ch]
             k += 1
 
 
 VMEM = pl.BlockSpec(memory_space=pltpu.VMEM)
-SMEM = pl.BlockSpec(memory_space=pltpu.SMEM)
 
 
 def local(spectra, keep, pair_mask):
@@ -201,9 +202,7 @@
     width = LAGS // (n_win * n_freq)
     n_bins = f_dev * n_freq
     params = pltpu.CompilerParams(vmem_limit_bytes=VMEM_LIMIT)
-    freq = lax.axis_index("freq")
-
-    places = jnp.stack([freq, lax.axis_index("win")]).astype(jnp.int32)
+
 
     def cost(flops, size):
         return pl.CostEstimate(flops=flops, bytes_accessed=size, transcendentals=0)
@@ -230,8 +229,8 @@
     table = pl.pallas_call(
         table_kernel,
         out_shape=jax.ShapeDtypeStruct((4, f_dev, LAGS // 2), jnp.bfloat16),
-        in_specs=[SMEM, VMEM], out_specs=VMEM, compiler_params=params, cost_estimate=cost(0, 2 ** 23),
-    )(places, jnp.asarray(np.concatenate([coarse, fine], axis=1)))
+        in_specs=[VMEM], out_specs=VMEM, compiler_params=params, cost_estimate=cost(0, 2 ** 23),
+    )(jnp.asarray(np.concatenate([coarse, fine], axis=1)))
     twist = phases(F_LO + np.arange(n_bins), np.ones(1)).reshape(2, n_freq, f_dev)
     twist = jnp.asarray(np.moveaxis(twist, 0, 1))
 
@@ -242,25 +241,27 @@
             in_specs=[VMEM] * (1 + len(others)), out_specs=VMEM, compiler_params=params,
         )(block, *others)
 
+    kept_windows = jnp.broadcast_to(keep.astype(jnp.float32)[:, None, None, None], (w_dev, 1, 1, LANES))
+
     def kept(block):
         return pl.pallas_call(
             keep_kernel,
             out_shape=jax.ShapeDtypeStruct(block.shape, jnp.float32),
-            in_specs=[SMEM, VMEM], out_specs=VMEM, compiler_params=params,
-        )(keep, block)
+            in_specs=[VMEM] * 2, out_specs=VMEM, compiler_params=params,
+        )(kept_windows, block)
 
     def pairs(base, partners):
         return pl.pallas_call(
             functools.partial(pairs_kernel, len(partners), n_win, n_freq),
             out_shape=[jax.ShapeDtypeStruct((len(partners), n_win, ch * ch, width), jnp.float32)] * n_freq,
-            in_specs=[SMEM] + [VMEM] * (3 + len(partners)), out_specs=[VMEM] * n_freq,
+            in_specs=[VMEM] * (3 + len(partners)), out_specs=[VMEM] * n_freq,
             scratch_shapes=[
                 pltpu.VMEM((2, 2 * ch * ch, f_dev), jnp.bfloat16),
                 pltpu.VMEM((2, ch * ch, LAGS // 2), jnp.float32),
             ],
             compiler_params=params,
             cost_estimate=cost(2 ** 33, 2 ** 22),
-        )(places, base, *partners, twist, table)
+        )(base, *partners, twist, table)
 
     def turns(parts, axis, size):
         received = [parts[0]]
@@ -269,20 +270,20 @@
             received.append(lax.ppermute(parts[turn], axis, route))
         return received
 
-    def reduce(parts, before, dtype):
-        n = parts[0].shape[0]
-        kinds = [jnp.float32] + [jnp.bfloat16] * (n_win - 1)
-        sums = pl.pallas_call(
-            functools.partial(add_kernel, n_freq),
+    def sum_bins(parts):
+        return pl.pallas_call(
+            plain_add_kernel,
+            out_shape=jax.ShapeDtypeStruct(parts[0].shape, jnp.float32),
+            in_specs=[VMEM] * n_freq, out_specs=VMEM, compiler_params=params,
+        )(*turns(parts, "freq", n_freq))
+
+    def split_windows(parts, before, kinds):
+        n = sum(part.shape[0] for part in before) + parts[0].shape[0]
+        return pl.pallas_call(
+            functools.partial(add_kernel, n_freq, len(before)),
             out_shape=[jax.ShapeDtypeStruct((n, ch * ch, width), kind) for kind in kinds],
-            in_specs=[VMEM] * n_freq, out_specs=[VMEM] * n_win, compiler_params=params,
-        )(*turns(parts, "freq", n_freq))
-        n += sum(part.shape[0] for part in before)
-        return pl.pallas_call(
-            functools.partial(total_kernel, n_win),
-            out_shape=jax.ShapeDtypeStruct((n, ch * ch, width), dtype),
-            in_specs=[VMEM] * (n_win + len(before)), out_specs=VMEM, compiler_params=params,
-        )(*turns(sums, "win", n_win), *before)
+            in_specs=[VMEM] * (n_freq + len(before)), out_specs=[VMEM] * n_win, compiler_params=params,
+        )(*turns(parts, "freq", n_freq), *before)
 
     white = whiten(copied, own_power)
     above = from_behind(white, "chan", 1)
@@ -290,22 +291,30 @@
     moving = whiten(raw, next_power)
     parts = pairs(kept(white), [white, moving])
     base = kept(above)
-    finished = []
+    before = []
     for step in range(1, reach - 1):
         arrived = from_behind(moving, "chan", -1)
-        finished.append(reduce(pairs(base, [moving]), [], jnp.float32))
+        remote = sum_bins(pairs(base, [moving]))
         if step == 1:
-            near = reduce(parts, [], jnp.float32)
-            arrived, near, finished = lax.optimization_barrier((arrived, near, finished))
+            sums = split_windows(parts, [], [jnp.float32] + [jnp.bfloat16] * (n_win - 1))
+            arrived, sums, remote = lax.optimization_barrier((arrived, sums, remote))
+        before.append(remote)
         moving = arrived
-    shipped = reduce(pairs(base, [moving]), finished, jnp.bfloat16)
-    shipped = from_behind(shipped, "chan", -1)
+    shipped = split_windows(pairs(base, [moving]), before, [jnp.bfloat16] * n_win)
+    received = turns(sums, "win", n_win)
+    received.append(from_behind(shipped[0], "chan", -1))
+    for turn in range(1, n_win):
+        route = [
+            (c * n_win + w, (c - 1) * n_win + (w + turn) % n_win) for c in range(1, n_chan) for w in range(n_win)
+        ]
+        received.append(lax.ppermute(shipped[turn], ("chan", "win"), route))
     scale = 1.0 / math.sqrt(w_dev * n_win * n_bins)
+    factors = jnp.repeat(pair_mask.T.astype(jnp.float32) * scale, ch, axis=1)[..., None]
     return pl.pallas_call(
-        functools.partial(combine_kernel, scale, n_win * n_freq, n_freq),
+        functools.partial(combine_kernel, n_win, n_freq),
         out_shape=jax.ShapeDtypeStruct((ch, reach + 1, ch, width), jnp.float32),
-        in_specs=[SMEM] * 2 + [VMEM] * 2, out_specs=VMEM, compiler_params=params,
-    )(pair_mask, places, near, shipped)
+        in_specs=[VMEM] * (1 + len(received)), out_specs=VMEM, compiler_params=params,
+    )(factors, *received)
 
 
 def solution(mesh):

time: 44.5 us -> 36.7 us (0.82)
  Pallas kernels: 13 us -> 9.26 us
  waiting for transfers between devices: 12.8 us -> 9.84 us
  starting transfers between devices: 16.1 us -> 14.8 us
    ppermute x6 -> x4, waiting for transfers between devices: 7.27 us -> 1.34 us  [turns(): received.append(lax.ppermute(parts[turn], axis, route))]
    ppermute x0 -> x1, waiting for transfers between devices: none -> 4.25 us  [local(): received.append(lax.ppermute(shipped[turn], ('chan', 'win'), route))]
    ppermute x6 -> x4, starting transfers between devices: 4.73 us -> 2.1 us  [turns(): received.append(lax.ppermute(parts[turn], axis, route))]
    pallas_call x3, Pallas kernels: 7.96 us -> 6.3 us  [pairs(): pl.pallas_call(functools.partial(pairs_kernel, len(partners), n_win, n_fr...]
    ppermute x0 -> x1, starting transfers between devices: none -> 1.29 us  [local(): received.append(lax.ppermute(shipped[turn], ('chan', 'win'), route))]
    ppermute x4, waiting for transfers between devices: 5.48 us -> 4.24 us  [from_behind(): return lax.ppermute(block, axis, route)]
    pallas_call x2, Pallas kernels: 1.16 us -> 0.21 us  [kept(): pl.pallas_call(keep_kernel, out_shape=jax.ShapeDtypeStruct(block.shape, j...]
    pallas_call x7 -> x4, Pallas kernels: 1.54 us -> 0.96 us  [the longest x1 0.89 us: local(): pl.pallas_call(functools.partial(combine_kernel, n_win, n_freq), out_shap...]
  transfers between devices with their start and end apart: 12 -> 11, of which waited for: 4 -> 5; matrix products, arithmetic and copies ran while one was open for 0% -> 1% of each run, Pallas kernels for 21% -> 19%
where the time goes in v9:
time: 36.7 us; the launch traced here: 36.3 us
  starting transfers between devices  14.8 us (40%)
  waiting for transfers between devices  9.84 us (27%)
  Pallas kernels  9.26 us (25%)
  local copies, waits for them, and re-layouts  2.18 us (6%)
    ppermute x4, starting transfers between devices, from_behind(): return lax.ppermute(block, axis, route)  9.65 us
    pallas_call x3, Pallas kernels, pairs(): pl.pallas_call(functools.partial(pairs_kernel, len(partners), n_win, n_fr...  6.3 us
    ppermute x1, waiting for transfers between devices, local(): received.append(lax.ppermute(shipped[turn], ('chan', 'win'), route))  4.25 us
    ppermute x4, waiting for transfers between devices, from_behind(): return lax.ppermute(block, axis, route)  4.24 us
    ppermute x4, starting transfers between devices, turns(): received.append(lax.ppermute(parts[turn], axis, route))  2.1 us
    unnamed x10, local copies, waits for them, and re-layouts  1.95 us
    ppermute x4, waiting for transfers between devices, turns(): received.append(lax.ppermute(parts[turn], axis, route))  1.34 us
    ppermute x1, starting transfers between devices, local(): received.append(lax.ppermute(shipped[turn], ('chan', 'win'), route))  1.29 us
  transfers between devices with their start and end apart: 11, of which 5 were waited for; matrix products, arithmetic and copies ran while one was open for 1% of the time, Pallas kernels for 19%

profile of v9, /device:TPU:0, one launch (start us, length us, event | category | flops | bytes accessed | tf_op | source)
XLA Modules:
  0.0 36.3 jit_solution(17698689044501568878)
XLA Ops:
  0.0 1.3 %collective-permute-start = (bf16[8,2,8,1024]{3,2,1,0:T(8,128)(2,1)}, bf16[8,2,8,1024]{3,2,1,0:T(8,128)(2,1)S(1)}, u32[]{:S(2)}, u32[]{:S(2)}) collective-permute-start(bf16[8,2,8,1024]{3,2,1,0:T(8,128)(2,1)} %x_ref.1), channel_id=1, source_target_pairs={{4,0},{8,4},{12,8},{5,1},{9,5},{13,9},{6,2},{10,6},{14,10},{7,3},{... | collective-permute-start | bytes 786440 | tf_op jit(solution)/shard_map/ppermute | solution.py:26
  1.3 0.0 copy-start.1
  1.3 0.9 %copy-done.1 = bf16[8,2,8,1024]{3,2,1,0:T(8,128)(2,1)S(1)} copy-done((bf16[8,2,8,1024]{3,2,1,0:T(8,128)(2,1)S(1)}, bf16[8,2,8,1024]{3,2,1,0:T(8,128)(2,1)}, u32[]{:S(2)}) %copy-start.1) | copy-done | bytes 262168
  2.2 0.0 copy-start.4
  2.2 0.0 copy-start.2
  2.2 0.1 shard_map.56
  2.4 0.5 %collective-permute-start.1 = (f32[8,8,1]{2,1,0:T(8,128)S(1)}, f32[8,8,1]{2,1,0:T(8,128)S(1)}, u32[]{:S(2)}, u32[]{:S(2)}) collective-permute-start(f32[8,8,1]{2,1,0:T(8,128)S(1)} %get-tuple-element.25), channel_id=1, source_target_pairs={{0,1},{1,0},{2,3},{3,2},{4,5},{5,4},{6,7},{7,6},{8,9},{9,8},{10,11... | collective-permute-start | bytes 776 | tf_op jit(solution)/shard_map/ppermute | solution.py:222
  2.8 1.3 %collective-permute-start.2 = (f32[8,8,1]{2,1,0:T(8,128)S(1)}, f32[8,8,1]{2,1,0:T(8,128)S(1)}, u32[]{:S(2)}, u32[]{:S(2)}) collective-permute-start(f32[8,8,1]{2,1,0:T(8,128)S(1)} %get-tuple-element.25), channel_id=1, source_target_pairs={{4,1},{5,0},{8,5},{9,4},{12,9},{13,8},{6,3},{7,2},{10,7},{11,6},{1... | collective-permute-start | bytes 776 | tf_op jit(solution)/shard_map/ppermute | solution.py:224
  4.1 0.0 copy-start
  4.1 1.0 %copy-done = f32[2,96,512]{2,1,0:T(8,128)S(1)} copy-done((f32[2,96,512]{2,1,0:T(8,128)S(1)}, f32[2,96,512]{2,1,0:T(8,128)}, u32[]{:S(2)}) %copy-start) | copy-done | bytes 393240
  5.1 1.2 %shard_map.55.refs_3_.refs_2_ = bf16[4,1024,512]{2,1,0:T(8,128)(2,1)S(1)} custom-call(f32[2,96,512]{2,1,0:T(8,128)S(1)} %copy-done), custom_call_target="tpu_custom_call" | custom-call | bytes 8388608 | tf_op jit(solution)/shard_map/pallas_call | solution.py:229
  6.3 0.0 copy-done.4
  6.4 0.0 collective-permute-done.1.refs_0_
  6.4 0.2 shard_map.57.white_ref.refs_0_
  6.6 5.8 %collective-permute-start.5 = (bf16[8,2,8,1024]{3,2,1,0:T(8,128)(2,1)S(1)}, bf16[8,2,8,1024]{3,2,1,0:T(8,128)(2,1)S(1)}, u32[]{:S(2)}, u32[]{:S(2)}) collective-permute-start(bf16[8,2,8,1024]{3,2,1,0:T(8,128)(2,1)S(1)} %shard_map.57.white_ref.refs_0_), channel_id=1, source_target_pairs={{0,4},{4,8},{8,12},{1,5},{5,9},{9,13},{2,6},{6,10},{10,14},{3,7},{... | collective-permute-start | bytes 786440 | tf_op jit(solution)/shard_map/ppermute | solution.py:26
  12.4 0.0 collective-permute-done.x_ref
  12.4 0.0 collective-permute-done.2.refs_0_
  12.4 0.2 shard_map.58.refs_1_.refs_0_
  12.7 1.3 %collective-permute-start.3 = (bf16[8,2,8,1024]{3,2,1,0:T(8,128)(2,1)S(1)}, bf16[8,2,8,1024]{3,2,1,0:T(8,128)(2,1)S(1)}, u32[]{:S(2)}, u32[]{:S(2)}) collective-permute-start(bf16[8,2,8,1024]{3,2,1,0:T(8,128)(2,1)S(1)} %shard_map.58.refs_1_.refs_0_), channel_id=1, source_target_pairs={{4,0},{8,4},{12,8},{5,1},{9,5},{13,9},{6,2},{10,6},{14,10},{7,3},{... | collective-permute-start | bytes 786440 | tf_op jit(solution)/shard_map/ppermute | solution.py:26
  14.0 0.1 broadcast_in_dim.10.keep_ref
  14.0 0.1 shard_map.59.base_ref
  14.1 0.0 copy-done.2
  14.2 3.2 %shard_map.60 = (f32[2,2,64,256]{3,2,1,0:T(8,128)S(1)}, f32[2,2,64,256]{3,2,1,0:T(8,128)S(1)}) custom-call(f32[8,2,8,1024]{3,2,1,0:T(8,128)S(1)} %shard_map.59.base_ref, bf16[8,2,8,1024]{3,2,1,0:T(8,128)(2,1)S(1)} %shard_map.57.white_ref.refs_0_, bf16[8,2,8,1024]{3,2,1,0:T(8,128)(2,1)S(1)} %shard_map.58.refs_1_.refs_0_, f32[2,2,1024]{2,1,0:T(2,128)S(1)} %copy-done.2, ...), custom_call_target="tpu_custom_call" | custom-call | flops 8589934592 | bytes 4194304 | tf_op jit(solution)/shard_map/pallas_call | solution.py:254
  17.3 0.3 collective-permute-start.4
  17.6 1.0 %collective-permute-done.5.white_ref = bf16[8,2,8,1024]{3,2,1,0:T(8,128)(2,1)S(1)} collective-permute-done((bf16[8,2,8,1024]{3,2,1,0:T(8,128)(2,1)S(1)}, bf16[8,2,8,1024]{3,2,1,0:T(8,128)(2,1)S(1)}, u32[]{:S(2)}, u32[]{:S(2)}) %collective-permute-start.5) | collective-permute-done | bytes 262176 | tf_op jit(solution)/shard_map/ppermute | solution.py:26
  18.6 0.1 shard_map.62.base_ref
  18.7 1.6 %shard_map.63 = (f32[1,2,64,256]{3,2,1,0:T(8,128)S(1)}, f32[1,2,64,256]{3,2,1,0:T(8,128)S(1)}) custom-call(f32[8,2,8,1024]{3,2,1,0:T(8,128)S(1)} %shard_map.62.base_ref, bf16[8,2,8,1024]{3,2,1,0:T(8,128)(2,1)S(1)} %shard_map.58.refs_1_.refs_0_, f32[2,2,1024]{2,1,0:T(2,128)S(1)} %copy-done.2, bf16[4,1024,512]{2,1,0:T(8,128)(2,1)S(1)} %shard_map.55.refs_3_.refs_2_), custom_call_target="tpu_custom_call" | custom-call | flops 8589934592 | bytes 4194304 | tf_op jit(solution)/shard_map/pallas_call | solution.py:254
  20.3 0.1 collective-permute-start.6
  20.4 1.3 %collective-permute-done.6.refs_1_ = f32[1,2,64,256]{3,2,1,0:T(8,128)S(1)} collective-permute-done((f32[1,2,64,256]{3,2,1,0:T(8,128)S(1)}, f32[1,2,64,256]{3,2,1,0:T(8,128)S(1)}, u32[]{:S(2)}, u32[]{:S(2)}) %collective-permute-start.6) | collective-permute-done | bytes 131104 | tf_op jit(solution)/shard_map/ppermute | solution.py:270
  21.7 0.0 collective-permute-done.4.refs_1_
  21.8 1.5 %collective-permute-done.3.refs_0_ = bf16[8,2,8,1024]{3,2,1,0:T(8,128)(2,1)S(1)} collective-permute-done((bf16[8,2,8,1024]{3,2,1,0:T(8,128)(2,1)S(1)}, bf16[8,2,8,1024]{3,2,1,0:T(8,128)(2,1)S(1)}, u32[]{:S(2)}, u32[]{:S(2)}) %collective-permute-start.3) | collective-permute-done | bytes 262176 | tf_op jit(solution)/shard_map/ppermute | solution.py:26
  23.3 0.0 copy-start.3
  23.3 1.6 %shard_map.65 = (f32[1,2,64,256]{3,2,1,0:T(8,128)S(1)}, f32[1,2,64,256]{3,2,1,0:T(8,128)S(1)}) custom-call(f32[8,2,8,1024]{3,2,1,0:T(8,128)S(1)} %shard_map.62.base_ref, bf16[8,2,8,1024]{3,2,1,0:T(8,128)(2,1)S(1)} %collective-permute-done.3.refs_0_, f32[2,2,1024]{2,1,0:T(2,128)S(1)} %copy-done.2, bf16[4,1024,512]{2,1,0:T(8,128)(2,1)S(1)} %shard_map.55.refs_3_.refs_2_), custom_call_target="tpu_custom_call" | custom-call | flops 8589934592 | bytes 4194304 | tf_op jit(solution)/shard_map/pallas_call | solution.py:254
  24.8 0.1 collective-permute-start.8
  24.9 1.7 %collective-permute-start.7 = (bf16[2,64,256]{2,1,0:T(8,128)(2,1)S(1)}, bf16[2,64,256]{2,1,0:T(8,128)(2,1)S(1)}, u32[]{:S(2)}, u32[]{:S(2)}) collective-permute-start(bf16[2,64,256]{2,1,0:T(8,128)(2,1)S(1)} %get-tuple-element.36), channel_id=1, source_target_pairs={{0,2},{2,0},{1,3},{3,1},{4,6},{6,4},{5,7},{7,5},{8,10},{10,8},{9,1... | collective-permute-start | bytes 196616 | tf_op jit(solution)/shard_map/ppermute | solution.py:270
  26.6 0.0 collective-permute-done.8.refs_1_
  26.6 1.3 %collective-permute-start.10 = (bf16[2,64,256]{2,1,0:T(8,128)(2,1)S(1)}, bf16[2,64,256]{2,1,0:T(8,128)(2,1)S(1)}, u32[]{:S(2)}, u32[]{:S(2)}) collective-permute-start(bf16[2,64,256]{2,1,0:T(8,128)(2,1)S(1)} %get-tuple-element.42), channel_id=1, source_target_pairs={{4,2},{6,0},{8,6},{10,4},{12,10},{14,8},{5,3},{7,1},{9,7},{11,5},{... | collective-permute-start | bytes 196616 | tf_op jit(solution)/shard_map/ppermute | solution.py:310
  27.9 1.3 %collective-permute-start.9 = (bf16[2,64,256]{2,1,0:T(8,128)(2,1)S(1)}, bf16[2,64,256]{2,1,0:T(8,128)(2,1)S(1)}, u32[]{:S(2)}, u32[]{:S(2)}) collective-permute-start(bf16[2,64,256]{2,1,0:T(8,128)(2,1)S(1)} %get-tuple-element.41), channel_id=1, source_target_pairs={{4,0},{8,4},{12,8},{5,1},{9,5},{13,9},{6,2},{10,6},{14,10},{7,3},{... | collective-permute-start | bytes 196616 | tf_op jit(solution)/shard_map/ppermute | solution.py:26
  29.2 0.0 copy-done.3
  29.3 0.1 broadcast_in_dim.4
  29.3 0.1 broadcast_in_dim_reshape.4.factor_ref
  29.4 0.0 collective-permute-done.7.refs_1_
  29.4 4.3 %collective-permute-done.10.refs_3_ = bf16[2,64,256]{2,1,0:T(8,128)(2,1)S(1)} collective-permute-done((bf16[2,64,256]{2,1,0:T(8,128)(2,1)S(1)}, bf16[2,64,256]{2,1,0:T(8,128)(2,1)S(1)}, u32[]{:S(2)}, u32[]{:S(2)}) %collective-permute-start.10) | collective-permute-done | bytes 65568 | tf_op jit(solution)/shard_map/ppermute | solution.py:310
  33.7 1.7 %collective-permute-done.9.refs_2_ = bf16[2,64,256]{2,1,0:T(8,128)(2,1)S(1)} collective-permute-done((bf16[2,64,256]{2,1,0:T(8,128)(2,1)S(1)}, bf16[2,64,256]{2,1,0:T(8,128)(2,1)S(1)}, u32[]{:S(2)}, u32[]{:S(2)}) %collective-permute-start.9) | collective-permute-done | bytes 65568 | tf_op jit(solution)/shard_map/ppermute | solution.py:26
  35.4 0.9 %shard_map.67 = f32[8,4,8,256]{3,2,1,0:T(8,128)} custom-call(f32[4,64,1]{2,1,0:T(8,128)S(1)} %broadcast_in_dim_reshape.4.factor_ref, f32[2,64,256]{2,1,0:T(8,128)S(1)} %get-tuple-element.35.refs_0_, bf16[2,64,256]{2,1,0:T(8,128)(2,1)S(1)} %collective-permute-done.7.refs_1_, bf16[2,64,256]{2,1,0:T(8,128)(2,1)S(1)} %collective-permute-done.9.refs_2_, ...), custom_call_target="tpu_custom_call" | custom-call | tf_op jit(solution)/shard_map/pallas_call | solution.py:313
  (5 shorter events, 0.1 us)
Async XLA Ops:
  0.0 12.4 %collective-permute-start = (bf16[8,2,8,1024]{3,2,1,0:T(8,128)(2,1)}, bf16[8,2,8,1024]{3,2,1,0:T(8,128)(2,1)S(1)}, u32[]{:S(2)}, u32[]{:S(2)}) collective-permute-start(bf16[8,2,8,1024]{3,2,1,0:T(8,128)(2,1)} %x_ref.1), channel_id=1, source_target_pairs={{4,0},{8,4},{12,8},{5,1},{9,5},{13,9},{6,2},{10,6},{14,10},{7,3},{... | collective-permute-start | bytes 786440 | tf_op jit(solution)/shard_map/ppermute | solution.py:26
  1.3 1.0 %copy-start.1 = (bf16[8,2,8,1024]{3,2,1,0:T(8,128)(2,1)S(1)}, bf16[8,2,8,1024]{3,2,1,0:T(8,128)(2,1)}, u32[]{:S(2)}) copy-start(bf16[8,2,8,1024]{3,2,1,0:T(8,128)(2,1)} %x_ref.1) | copy-start | bytes 786436
  2.2 4.1 %copy-start.4 = (s32[8]{0:T(128)S(1)}, s32[8]{0:T(128)}, u32[]{:S(2)}) copy-start(s32[8]{0:T(128)} %param.6) | copy-start | bytes 100
  2.2 11.9 %copy-start.2 = (f32[2,2,1024]{2,1,0:T(2,128)S(1)}, f32[2,2,1024]{2,1,0:T(2,128)}, u32[]{:S(2)}) copy-start(f32[2,2,1024]{2,1,0:T(2,128)} %constant.7.clone.refs_2_.refs_1_) | copy-start | bytes 49156
  2.4 4.0 %collective-permute-start.1 = (f32[8,8,1]{2,1,0:T(8,128)S(1)}, f32[8,8,1]{2,1,0:T(8,128)S(1)}, u32[]{:S(2)}, u32[]{:S(2)}) collective-permute-start(f32[8,8,1]{2,1,0:T(8,128)S(1)} %get-tuple-element.25), channel_id=1, source_target_pairs={{0,1},{1,0},{2,3},{3,2},{4,5},{5,4},{6,7},{7,6},{8,9},{9,8},{10,11... | collective-permute-start | bytes 776 | tf_op jit(solution)/shard_map/ppermute | solution.py:222
  2.8 9.6 %collective-permute-start.2 = (f32[8,8,1]{2,1,0:T(8,128)S(1)}, f32[8,8,1]{2,1,0:T(8,128)S(1)}, u32[]{:S(2)}, u32[]{:S(2)}) collective-permute-start(f32[8,8,1]{2,1,0:T(8,128)S(1)} %get-tuple-element.25), channel_id=1, source_target_pairs={{4,1},{5,0},{8,5},{9,4},{12,9},{13,8},{6,3},{7,2},{10,7},{11,6},{1... | collective-permute-start | bytes 776 | tf_op jit(solution)/shard_map/ppermute | solution.py:224
  4.1 1.0 %copy-start = (f32[2,96,512]{2,1,0:T(8,128)S(1)}, f32[2,96,512]{2,1,0:T(8,128)}, u32[]{:S(2)}) copy-start(f32[2,96,512]{2,1,0:T(8,128)} %constant.6.clone.base_ref) | copy-start | bytes 1179652
  6.6 12.0 %collective-permute-start.5 = (bf16[8,2,8,1024]{3,2,1,0:T(8,128)(2,1)S(1)}, bf16[8,2,8,1024]{3,2,1,0:T(8,128)(2,1)S(1)}, u32[]{:S(2)}, u32[]{:S(2)}) collective-permute-start(bf16[8,2,8,1024]{3,2,1,0:T(8,128)(2,1)S(1)} %shard_map.57.white_ref.refs_0_), channel_id=1, source_target_pairs={{0,4},{4,8},{8,12},{1,5},{5,9},{9,13},{2,6},{6,10},{10,14},{3,7},{... | collective-permute-start | bytes 786440 | tf_op jit(solution)/shard_map/ppermute | solution.py:26
  12.7 10.6 %collective-permute-start.3 = (bf16[8,2,8,1024]{3,2,1,0:T(8,128)(2,1)S(1)}, bf16[8,2,8,1024]{3,2,1,0:T(8,128)(2,1)S(1)}, u32[]{:S(2)}, u32[]{:S(2)}) collective-permute-start(bf16[8,2,8,1024]{3,2,1,0:T(8,128)(2,1)S(1)} %shard_map.58.refs_1_.refs_0_), channel_id=1, source_target_pairs={{4,0},{8,4},{12,8},{5,1},{9,5},{13,9},{6,2},{10,6},{14,10},{7,3},{... | collective-permute-start | bytes 786440 | tf_op jit(solution)/shard_map/ppermute | solution.py:26
  17.3 4.4 %collective-permute-start.4 = (f32[2,2,64,256]{3,2,1,0:T(8,128)S(1)}, f32[2,2,64,256]{3,2,1,0:T(8,128)S(1)}, u32[]{:S(2)}, u32[]{:S(2)}) collective-permute-start(f32[2,2,64,256]{3,2,1,0:T(8,128)S(1)} %get-tuple-element.30), channel_id=1, source_target_pairs={{0,1},{1,0},{2,3},{3,2},{4,5},{5,4},{6,7},{7,6},{8,9},{9,8},{10,11... | collective-permute-start | bytes 786440 | tf_op jit(solution)/shard_map/ppermute | solution.py:270
  20.3 1.4 %collective-permute-start.6 = (f32[1,2,64,256]{3,2,1,0:T(8,128)S(1)}, f32[1,2,64,256]{3,2,1,0:T(8,128)S(1)}, u32[]{:S(2)}, u32[]{:S(2)}) collective-permute-start(f32[1,2,64,256]{3,2,1,0:T(8,128)S(1)} %get-tuple-element.34), channel_id=1, source_target_pairs={{0,1},{1,0},{2,3},{3,2},{4,5},{5,4},{6,7},{7,6},{8,9},{9,8},{10,11... | collective-permute-start | bytes 393224 | tf_op jit(solution)/shard_map/ppermute | solution.py:270
  23.3 6.0 %copy-start.3 = (s32[8,4]{0,1:T(4,128)S(1)}, s32[8,4]{0,1:T(4,128)}, u32[]{:S(2)}) copy-start(s32[8,4]{0,1:T(4,128)} %param.7) | copy-start | bytes 388
  24.8 1.8 %collective-permute-start.8 = (f32[1,2,64,256]{3,2,1,0:T(8,128)S(1)}, f32[1,2,64,256]{3,2,1,0:T(8,128)S(1)}, u32[]{:S(2)}, u32[]{:S(2)}) collective-permute-start(f32[1,2,64,256]{3,2,1,0:T(8,128)S(1)} %get-tuple-element.39), channel_id=1, source_target_pairs={{0,1},{1,0},{2,3},{3,2},{4,5},{5,4},{6,7},{7,6},{8,9},{9,8},{10,11... | collective-permute-start | bytes 393224 | tf_op jit(solution)/shard_map/ppermute | solution.py:270
  24.9 4.5 %collective-permute-start.7 = (bf16[2,64,256]{2,1,0:T(8,128)(2,1)S(1)}, bf16[2,64,256]{2,1,0:T(8,128)(2,1)S(1)}, u32[]{:S(2)}, u32[]{:S(2)}) collective-permute-start(bf16[2,64,256]{2,1,0:T(8,128)(2,1)S(1)} %get-tuple-element.36), channel_id=1, source_target_pairs={{0,2},{2,0},{1,3},{3,1},{4,6},{6,4},{5,7},{7,5},{8,10},{10,8},{9,1... | collective-permute-start | bytes 196616 | tf_op jit(solution)/shard_map/ppermute | solution.py:270
  26.6 7.1 %collective-permute-start.10 = (bf16[2,64,256]{2,1,0:T(8,128)(2,1)S(1)}, bf16[2,64,256]{2,1,0:T(8,128)(2,1)S(1)}, u32[]{:S(2)}, u32[]{:S(2)}) collective-permute-start(bf16[2,64,256]{2,1,0:T(8,128)(2,1)S(1)} %get-tuple-element.42), channel_id=1, source_target_pairs={{4,2},{6,0},{8,6},{10,4},{12,10},{14,8},{5,3},{7,1},{9,7},{11,5},{... | collective-permute-start | bytes 196616 | tf_op jit(solution)/shard_map/ppermute | solution.py:310
  27.9 7.5 %collective-permute-start.9 = (bf16[2,64,256]{2,1,0:T(8,128)(2,1)S(1)}, bf16[2,64,256]{2,1,0:T(8,128)(2,1)S(1)}, u32[]{:S(2)}, u32[]{:S(2)}) collective-permute-start(bf16[2,64,256]{2,1,0:T(8,128)(2,1)S(1)} %get-tuple-element.41), channel_id=1, source_target_pairs={{4,0},{8,4},{12,8},{5,1},{9,5},{13,9},{6,2},{10,6},{14,10},{7,3},{... | collective-permute-start | bytes 196616 | tf_op jit(solution)/shard_map/ppermute | solution.py:26

commit v10 on v9

--- a/solution.py
+++ b/solution.py
@@ -207,21 +207,18 @@
     def cost(flops, size):
         return pl.CostEstimate(flops=flops, bytes_accessed=size, transcendentals=0)
 
-    raw = from_behind(spectra, "chan", -1)
     power, copied = pl.pallas_call(
         power_kernel,
         out_shape=[
             jax.ShapeDtypeStruct((w_dev, ch, 1), jnp.float32),
             jax.ShapeDtypeStruct(spectra.shape, spectra.dtype),
         ],
-        in_specs=[VMEM], out_specs=[VMEM] * 2, compiler_params=params, cost_estimate=cost(0, 2 ** 22),
+        in_specs=[VMEM], out_specs=[VMEM] * 2, compiler_params=params, cost_estimate=cost(ch, ch),
     )(spectra)
-    own_power, next_power = [], []
+    own_power = []
     for turn in range(1, n_freq):
         route = [(f, (f + turn) % n_freq) for f in range(n_freq)]
         own_power.append(lax.ppermute(power, "freq", route))
-        route = [(c * n_freq + f, (c - 1) * n_freq + to) for c in range(1, n_chan) for f, to in route]
-        next_power.append(lax.ppermute(power, ("chan", "freq"), route))
 
     half_lags = 2 * np.arange(LAGS // 2) + 1
     coarse = phases(np.arange(0, n_bins, FINE), half_lags)
@@ -229,7 +226,7 @@
     table = pl.pallas_call(
         table_kernel,
         out_shape=jax.ShapeDtypeStruct((4, f_dev, LAGS // 2), jnp.bfloat16),
-        in_specs=[VMEM], out_specs=VMEM, compiler_params=params, cost_estimate=cost(0, 2 ** 23),
+        in_specs=[VMEM], out_specs=VMEM, compiler_params=params, cost_estimate=cost(ch, ch),
     )(jnp.asarray(np.concatenate([coarse, fine], axis=1)))
     twist = phases(F_LO + np.arange(n_bins), np.ones(1)).reshape(2, n_freq, f_dev)
     twist = jnp.asarray(np.moveaxis(twist, 0, 1))
@@ -260,7 +257,7 @@
                 pltpu.VMEM((2, ch * ch, LAGS // 2), jnp.float32),
             ],
             compiler_params=params,
-            cost_estimate=cost(2 ** 33, 2 ** 22),
+            cost_estimate=cost(ch, ch),
         )(base, *partners, twist, table)
 
     def turns(parts, axis, size):
@@ -285,22 +282,24 @@
             in_specs=[VMEM] * (n_freq + len(before)), out_specs=[VMEM] * n_win, compiler_params=params,
         )(*turns(parts, "freq", n_freq), *before)
 
+    table, own_power = lax.optimization_barrier((table, own_power))
     white = whiten(copied, own_power)
     above = from_behind(white, "chan", 1)
-    raw, table, white = lax.optimization_barrier((raw, table, white))
-    moving = whiten(raw, next_power)
-    parts = pairs(kept(white), [white, moving])
+    below = from_behind(white, "chan", -1)
+    far = []
+    for distance in range(2, reach):
+        route = [(c + distance, c) for c in range(1, n_chan - distance)]
+        far.append(lax.ppermute(white, "chan", route))
+    own = kept(white)
+    first = sum_bins(pairs(own, [white]))
+    below, first = lax.optimization_barrier((below, first))
     base = kept(above)
-    before = []
-    for step in range(1, reach - 1):
-        arrived = from_behind(moving, "chan", -1)
-        remote = sum_bins(pairs(base, [moving]))
-        if step == 1:
-            sums = split_windows(parts, [], [jnp.float32] + [jnp.bfloat16] * (n_win - 1))
-            arrived, sums, remote = lax.optimization_barrier((arrived, sums, remote))
-        before.append(remote)
-        moving = arrived
-    shipped = split_windows(pairs(base, [moving]), before, [jnp.bfloat16] * n_win)
+    sums = split_windows(pairs(own, [below]), [first], [jnp.float32] + [jnp.bfloat16] * (n_win - 1))
+    before = [sum_bins(pairs(base, [below]))]
+    for block in far[:-1]:
+        before.append(sum_bins(pairs(base, [block])))
+    far, sums, before = lax.optimization_barrier((far[-1], sums, before))
+    shipped = split_windows(pairs(base, [far]), before, [jnp.bfloat16] * n_win)
     received = turns(sums, "win", n_win)
     received.append(from_behind(shipped[0], "chan", -1))
     for turn in range(1, n_win):

time: 36.7 us -> 37.1 us (1.011)
  waiting for transfers between devices: 9.84 us -> 12.3 us
  starting transfers between devices: 14.8 us -> 13.1 us
    ppermute x4 -> x3, waiting for transfers between devices: 4.24 us -> 8.25 us  [from_behind(): return lax.ppermute(block, axis, route)]
    ppermute x4 -> x3, starting transfers between devices: 9.65 us -> 7.72 us  [from_behind(): return lax.ppermute(block, axis, route)]
    ppermute x1, waiting for transfers between devices: 4.25 us -> 2.61 us  [local(): received.append(lax.ppermute(shipped[turn], ('chan', 'win'), route))]
    ppermute x4 -> x5, starting transfers between devices: 2.1 us -> 2.97 us  [turns(): received.append(lax.ppermute(parts[turn], axis, route))]
    ppermute x1, starting transfers between devices: 1.28 us -> 0.67 us  [local(): far.append(lax.ppermute(white, 'chan', route))]
    ppermute x4 -> x5, waiting for transfers between devices: 1.34 us -> 1.44 us  [turns(): received.append(lax.ppermute(parts[turn], axis, route))]
    pallas_call x3 -> x4, Pallas kernels: 6.3 us -> 6.31 us  [pairs(): pl.pallas_call(functools.partial(pairs_kernel, len(partners), n_win, n_fr...]
  transfers between devices with their start and end apart: 11 -> 11, of which waited for: 5 -> 6; matrix products, arithmetic and copies ran while one was open for 1% -> 1% of each run, Pallas kernels for 19% -> 17%
where the time goes in v10:
time: 37.1 us; the launch traced here: 36.9 us
  starting transfers between devices  13.1 us (35%)
  waiting for transfers between devices  12.3 us (33%)
  Pallas kernels  9.05 us (24%)
  local copies, waits for them, and re-layouts  2.21 us (6%)
    ppermute x3, waiting for transfers between devices, from_behind(): return lax.ppermute(block, axis, route)  8.25 us
    ppermute x3, starting transfers between devices, from_behind(): return lax.ppermute(block, axis, route)  7.72 us
    pallas_call x4, Pallas kernels, pairs(): pl.pallas_call(functools.partial(pairs_kernel, len(partners), n_win, n_fr...  6.31 us
    ppermute x5, starting transfers between devices, turns(): received.append(lax.ppermute(parts[turn], axis, route))  2.97 us
    ppermute x1, waiting for transfers between devices, local(): received.append(lax.ppermute(shipped[turn], ('chan', 'win'), route))  2.61 us
    unnamed x10, local copies, waits for them, and re-layouts  1.97 us
    ppermute x5, waiting for transfers between devices, turns(): received.append(lax.ppermute(parts[turn], axis, route))  1.44 us
    ppermute x1, starting transfers between devices, local(): received.append(lax.ppermute(shipped[turn], ('chan', 'win'), route))  1.29 us
  transfers between devices with their start and end apart: 11, of which 6 were waited for; matrix products, arithmetic and copies ran while one was open for 1% of the time, Pallas kernels for 17%

profile of v10, /device:TPU:0, one launch (start us, length us, event | category | flops | bytes accessed | tf_op | source)
XLA Modules:
  0.0 36.9 jit_solution(2741570437012386540)
XLA Ops:
  0.0 0.0 copy-start.1
  0.0 0.0 copy-start.2
  0.0 1.0 %copy-done.2 = bf16[8,2,8,1024]{3,2,1,0:T(8,128)(2,1)S(1)} copy-done((bf16[8,2,8,1024]{3,2,1,0:T(8,128)(2,1)S(1)}, bf16[8,2,8,1024]{3,2,1,0:T(8,128)(2,1)}, u32[]{:S(2)}) %copy-start.2) | copy-done | bytes 262168
  1.0 0.0 copy-start.4
  1.0 0.1 shard_map.55
  1.1 0.5 %collective-permute-start = (f32[8,8,1]{2,1,0:T(8,128)S(1)}, f32[8,8,1]{2,1,0:T(8,128)S(1)}, u32[]{:S(2)}, u32[]{:S(2)}) collective-permute-start(f32[8,8,1]{2,1,0:T(8,128)S(1)} %get-tuple-element.28), channel_id=1, source_target_pairs={{0,1},{1,0},{2,3},{3,2},{4,5},{5,4},{6,7},{7,6},{8,9},{9,8},{10,11... | collective-permute-start | bytes 776 | tf_op jit(solution)/shard_map/ppermute | solution.py:221
  1.6 0.0 copy-start
  1.6 1.0 %copy-done = f32[2,96,512]{2,1,0:T(8,128)S(1)} copy-done((f32[2,96,512]{2,1,0:T(8,128)S(1)}, f32[2,96,512]{2,1,0:T(8,128)}, u32[]{:S(2)}) %copy-start) | copy-done | bytes 393240
  2.6 1.2 %shard_map.56.refs_2_ = bf16[4,1024,512]{2,1,0:T(8,128)(2,1)S(1)} custom-call(f32[2,96,512]{2,1,0:T(8,128)S(1)} %copy-done), custom_call_target="tpu_custom_call" | custom-call | flops 8 | bytes 8 | tf_op jit(solution)/shard_map/pallas_call | solution.py:226
  3.8 0.0 collective-permute-done.refs_0_
  3.8 0.2 shard_map.57.white_ref.refs_0_
  4.0 1.3 %collective-permute-start.2 = (bf16[8,2,8,1024]{3,2,1,0:T(8,128)(2,1)S(1)}, bf16[8,2,8,1024]{3,2,1,0:T(8,128)(2,1)S(1)}, u32[]{:S(2)}, u32[]{:S(2)}) collective-permute-start(bf16[8,2,8,1024]{3,2,1,0:T(8,128)(2,1)S(1)} %shard_map.57.white_ref.refs_0_), channel_id=1, source_target_pairs={{4,0},{8,4},{12,8},{5,1},{9,5},{13,9},{6,2},{10,6},{14,10},{7,3},{... | collective-permute-start | bytes 786440 | tf_op jit(solution)/shard_map/ppermute | solution.py:26
  5.3 5.1 %collective-permute-start.5 = (bf16[8,2,8,1024]{3,2,1,0:T(8,128)(2,1)S(1)}, bf16[8,2,8,1024]{3,2,1,0:T(8,128)(2,1)S(1)}, u32[]{:S(2)}, u32[]{:S(2)}) collective-permute-start(bf16[8,2,8,1024]{3,2,1,0:T(8,128)(2,1)S(1)} %shard_map.57.white_ref.refs_0_), channel_id=1, source_target_pairs={{0,4},{4,8},{8,12},{1,5},{5,9},{9,13},{2,6},{6,10},{10,14},{3,7},{... | collective-permute-start | bytes 786440 | tf_op jit(solution)/shard_map/ppermute | solution.py:26
  10.5 0.0 copy-done.4
  10.5 0.1 broadcast_in_dim.10.keep_ref
  10.6 0.1 shard_map.58.base_ref
  10.7 0.0 copy-done.1
  10.7 1.6 %shard_map.59 = (f32[1,2,64,256]{3,2,1,0:T(8,128)S(1)}, f32[1,2,64,256]{3,2,1,0:T(8,128)S(1)}) custom-call(f32[8,2,8,1024]{3,2,1,0:T(8,128)S(1)} %shard_map.58.base_ref, bf16[8,2,8,1024]{3,2,1,0:T(8,128)(2,1)S(1)} %shard_map.57.white_ref.refs_0_, f32[2,2,1024]{2,1,0:T(2,128)S(1)} %copy-done.1, bf16[4,1024,512]{2,1,0:T(8,128)(2,1)S(1)} %shard_map.56.refs_2_), custom_call_target="tpu_custom_call" | custom-call | flops 8 | bytes 8 | tf_op jit(solution)/shard_map/pallas_call | solution.py:251
  12.3 0.3 collective-permute-start.3
  12.5 0.7 %collective-permute-start.1 = (bf16[8,2,8,1024]{3,2,1,0:T(8,128)(2,1)S(1)}, bf16[8,2,8,1024]{3,2,1,0:T(8,128)(2,1)S(1)}, u32[]{:S(2)}, u32[]{:S(2)}) collective-permute-start(bf16[8,2,8,1024]{3,2,1,0:T(8,128)(2,1)S(1)} %shard_map.57.white_ref.refs_0_), channel_id=1, source_target_pairs={{12,4},{13,5},{14,6},{15,7},{28,20},{29,21},{30,22},{31,23}} | collective-permute-start | bytes 786440 | tf_op jit(solution)/shard_map/ppermute | solution.py:292
  13.2 0.5 %collective-permute-done.3.refs_1_ = f32[1,2,64,256]{3,2,1,0:T(8,128)S(1)} collective-permute-done((f32[1,2,64,256]{3,2,1,0:T(8,128)S(1)}, f32[1,2,64,256]{3,2,1,0:T(8,128)S(1)}, u32[]{:S(2)}, u32[]{:S(2)}) %collective-permute-start.3) | collective-permute-done | bytes 131104 | tf_op jit(solution)/shard_map/ppermute | solution.py:267
  13.7 1.8 %collective-permute-done.2.refs_0_ = bf16[8,2,8,1024]{3,2,1,0:T(8,128)(2,1)S(1)} collective-permute-done((bf16[8,2,8,1024]{3,2,1,0:T(8,128)(2,1)S(1)}, bf16[8,2,8,1024]{3,2,1,0:T(8,128)(2,1)S(1)}, u32[]{:S(2)}, u32[]{:S(2)}) %collective-permute-start.2) | collective-permute-done | bytes 262176 | tf_op jit(solution)/shard_map/ppermute | solution.py:26
  15.5 1.2 %collective-permute-done.5.white_ref = bf16[8,2,8,1024]{3,2,1,0:T(8,128)(2,1)S(1)} collective-permute-done((bf16[8,2,8,1024]{3,2,1,0:T(8,128)(2,1)S(1)}, bf16[8,2,8,1024]{3,2,1,0:T(8,128)(2,1)S(1)}, u32[]{:S(2)}, u32[]{:S(2)}) %collective-permute-start.5) | collective-permute-done | bytes 262176 | tf_op jit(solution)/shard_map/ppermute | solution.py:26
  16.6 0.1 shard_map.63.base_ref
  16.8 1.6 %shard_map.64 = (f32[1,2,64,256]{3,2,1,0:T(8,128)S(1)}, f32[1,2,64,256]{3,2,1,0:T(8,128)S(1)}) custom-call(f32[8,2,8,1024]{3,2,1,0:T(8,128)S(1)} %shard_map.63.base_ref, bf16[8,2,8,1024]{3,2,1,0:T(8,128)(2,1)S(1)} %collective-permute-done.2.refs_0_, f32[2,2,1024]{2,1,0:T(2,128)S(1)} %copy-done.1, bf16[4,1024,512]{2,1,0:T(8,128)(2,1)S(1)} %shard_map.56.refs_2_), custom_call_target="tpu_custom_call" | custom-call | flops 8 | bytes 8 | tf_op jit(solution)/shard_map/pallas_call | solution.py:251
  18.3 0.1 collective-permute-start.6
  18.4 1.6 %shard_map.61 = (f32[1,2,64,256]{3,2,1,0:T(8,128)S(1)}, f32[1,2,64,256]{3,2,1,0:T(8,128)S(1)}) custom-call(f32[8,2,8,1024]{3,2,1,0:T(8,128)S(1)} %shard_map.58.base_ref, bf16[8,2,8,1024]{3,2,1,0:T(8,128)(2,1)S(1)} %collective-permute-done.2.refs_0_, f32[2,2,1024]{2,1,0:T(2,128)S(1)} %copy-done.1, bf16[4,1024,512]{2,1,0:T(8,128)(2,1)S(1)} %shard_map.56.refs_2_), custom_call_target="tpu_custom_call" | custom-call | flops 8 | bytes 8 | tf_op jit(solution)/shard_map/pallas_call | solution.py:251
  20.0 0.0 copy-start.3
  20.0 0.5 %collective-permute-start.4 = (f32[1,2,64,256]{3,2,1,0:T(8,128)S(1)}, f32[1,2,64,256]{3,2,1,0:T(8,128)S(1)}, u32[]{:S(2)}, u32[]{:S(2)}) collective-permute-start(f32[1,2,64,256]{3,2,1,0:T(8,128)S(1)} %get-tuple-element.35), channel_id=1, source_target_pairs={{0,1},{1,0},{2,3},{3,2},{4,5},{5,4},{6,7},{7,6},{8,9},{9,8},{10,11... | collective-permute-start | bytes 393224 | tf_op jit(solution)/shard_map/ppermute | solution.py:267
  20.6 0.0 collective-permute-done.6.refs_1_
  20.6 1.0 %collective-permute-done.4.refs_1_ = f32[1,2,64,256]{3,2,1,0:T(8,128)S(1)} collective-permute-done((f32[1,2,64,256]{3,2,1,0:T(8,128)S(1)}, f32[1,2,64,256]{3,2,1,0:T(8,128)S(1)}, u32[]{:S(2)}, u32[]{:S(2)}) %collective-permute-start.4) | collective-permute-done | bytes 131104 | tf_op jit(solution)/shard_map/ppermute | solution.py:267
  21.6 0.0 collective-permute-done.1.refs_0_
  21.6 1.6 %shard_map.66 = (f32[1,2,64,256]{3,2,1,0:T(8,128)S(1)}, f32[1,2,64,256]{3,2,1,0:T(8,128)S(1)}) custom-call(f32[8,2,8,1024]{3,2,1,0:T(8,128)S(1)} %shard_map.63.base_ref, bf16[8,2,8,1024]{3,2,1,0:T(8,128)(2,1)S(1)} %collective-permute-done.1.refs_0_, f32[2,2,1024]{2,1,0:T(2,128)S(1)} %copy-done.1, bf16[4,1024,512]{2,1,0:T(8,128)(2,1)S(1)} %shard_map.56.refs_2_), custom_call_target="tpu_custom_call" | custom-call | flops 8 | bytes 8 | tf_op jit(solution)/shard_map/pallas_call | solution.py:251
  23.2 0.4 %collective-permute-start.8 = (f32[1,2,64,256]{3,2,1,0:T(8,128)S(1)}, f32[1,2,64,256]{3,2,1,0:T(8,128)S(1)}, u32[]{:S(2)}, u32[]{:S(2)}) collective-permute-start(f32[1,2,64,256]{3,2,1,0:T(8,128)S(1)} %get-tuple-element.45), channel_id=1, source_target_pairs={{0,1},{1,0},{2,3},{3,2},{4,5},{5,4},{6,7},{7,6},{8,9},{9,8},{10,11... | collective-permute-start | bytes 393224 | tf_op jit(solution)/shard_map/ppermute | solution.py:267
  23.6 1.6 %collective-permute-start.7 = (bf16[2,64,256]{2,1,0:T(8,128)(2,1)S(1)}, bf16[2,64,256]{2,1,0:T(8,128)(2,1)S(1)}, u32[]{:S(2)}, u32[]{:S(2)}) collective-permute-start(bf16[2,64,256]{2,1,0:T(8,128)(2,1)S(1)} %get-tuple-element.42), channel_id=1, source_target_pairs={{0,2},{2,0},{1,3},{3,1},{4,6},{6,4},{5,7},{7,5},{8,10},{10,8},{9,1... | collective-permute-start | bytes 196616 | tf_op jit(solution)/shard_map/ppermute | solution.py:267
  25.2 0.0 collective-permute-done.8.refs_1_
  25.3 1.3 %collective-permute-start.9 = (bf16[2,64,256]{2,1,0:T(8,128)(2,1)S(1)}, bf16[2,64,256]{2,1,0:T(8,128)(2,1)S(1)}, u32[]{:S(2)}, u32[]{:S(2)}) collective-permute-start(bf16[2,64,256]{2,1,0:T(8,128)(2,1)S(1)} %get-tuple-element.47), channel_id=1, source_target_pairs={{4,0},{8,4},{12,8},{5,1},{9,5},{13,9},{6,2},{10,6},{14,10},{7,3},{... | collective-permute-start | bytes 196616 | tf_op jit(solution)/shard_map/ppermute | solution.py:26
  26.6 1.3 %collective-permute-start.10 = (bf16[2,64,256]{2,1,0:T(8,128)(2,1)S(1)}, bf16[2,64,256]{2,1,0:T(8,128)(2,1)S(1)}, u32[]{:S(2)}, u32[]{:S(2)}) collective-permute-start(bf16[2,64,256]{2,1,0:T(8,128)(2,1)S(1)} %get-tuple-element.48), channel_id=1, source_target_pairs={{4,2},{6,0},{8,6},{10,4},{12,10},{14,8},{5,3},{7,1},{9,7},{11,5},{... | collective-permute-start | bytes 196616 | tf_op jit(solution)/shard_map/ppermute | solution.py:309
  27.9 0.0 copy-done.3
  27.9 0.1 broadcast_in_dim.4
  28.0 0.1 broadcast_in_dim_reshape.4.factor_ref
  28.1 0.0 collective-permute-done.7.refs_1_
  28.1 5.3 %collective-permute-done.9.refs_2_ = bf16[2,64,256]{2,1,0:T(8,128)(2,1)S(1)} collective-permute-done((bf16[2,64,256]{2,1,0:T(8,128)(2,1)S(1)}, bf16[2,64,256]{2,1,0:T(8,128)(2,1)S(1)}, u32[]{:S(2)}, u32[]{:S(2)}) %collective-permute-start.9) | collective-permute-done | bytes 65568 | tf_op jit(solution)/shard_map/ppermute | solution.py:26
  33.4 2.6 %collective-permute-done.10.refs_3_ = bf16[2,64,256]{2,1,0:T(8,128)(2,1)S(1)} collective-permute-done((bf16[2,64,256]{2,1,0:T(8,128)(2,1)S(1)}, bf16[2,64,256]{2,1,0:T(8,128)(2,1)S(1)}, u32[]{:S(2)}, u32[]{:S(2)}) %collective-permute-start.10) | collective-permute-done | bytes 65568 | tf_op jit(solution)/shard_map/ppermute | solution.py:309
  36.0 0.9 %shard_map.68 = f32[8,4,8,256]{3,2,1,0:T(8,128)} custom-call(f32[4,64,1]{2,1,0:T(8,128)S(1)} %broadcast_in_dim_reshape.4.factor_ref, f32[2,64,256]{2,1,0:T(8,128)S(1)} %get-tuple-element.41.refs_0_, bf16[2,64,256]{2,1,0:T(8,128)(2,1)S(1)} %collective-permute-done.7.refs_1_, bf16[2,64,256]{2,1,0:T(8,128)(2,1)S(1)} %collective-permute-done.9.refs_2_, ...), custom_call_target="tpu_custom_call" | custom-call | tf_op jit(solution)/shard_map/pallas_call | solution.py:312
  (6 shorter events, 0.1 us)
Async XLA Ops:
  0.0 10.7 %copy-start.1 = (f32[2,2,1024]{2,1,0:T(2,128)S(1)}, f32[2,2,1024]{2,1,0:T(2,128)}, u32[]{:S(2)}) copy-start(f32[2,2,1024]{2,1,0:T(2,128)} %constant.7.clone.refs_1_) | copy-start | bytes 49156
  0.0 1.0 %copy-start.2 = (bf16[8,2,8,1024]{3,2,1,0:T(8,128)(2,1)S(1)}, bf16[8,2,8,1024]{3,2,1,0:T(8,128)(2,1)}, u32[]{:S(2)}) copy-start(bf16[8,2,8,1024]{3,2,1,0:T(8,128)(2,1)} %x_ref.1) | copy-start | bytes 786436
  1.0 9.5 %copy-start.4 = (s32[8]{0:T(128)S(1)}, s32[8]{0:T(128)}, u32[]{:S(2)}) copy-start(s32[8]{0:T(128)} %param.6) | copy-start | bytes 100
  1.1 2.7 %collective-permute-start = (f32[8,8,1]{2,1,0:T(8,128)S(1)}, f32[8,8,1]{2,1,0:T(8,128)S(1)}, u32[]{:S(2)}, u32[]{:S(2)}) collective-permute-start(f32[8,8,1]{2,1,0:T(8,128)S(1)} %get-tuple-element.28), channel_id=1, source_target_pairs={{0,1},{1,0},{2,3},{3,2},{4,5},{5,4},{6,7},{7,6},{8,9},{9,8},{10,11... | collective-permute-start | bytes 776 | tf_op jit(solution)/shard_map/ppermute | solution.py:221
  1.6 1.0 %copy-start = (f32[2,96,512]{2,1,0:T(8,128)S(1)}, f32[2,96,512]{2,1,0:T(8,128)}, u32[]{:S(2)}) copy-start(f32[2,96,512]{2,1,0:T(8,128)} %constant.6.clone.base_ref) | copy-start | bytes 1179652
  4.0 11.5 %collective-permute-start.2 = (bf16[8,2,8,1024]{3,2,1,0:T(8,128)(2,1)S(1)}, bf16[8,2,8,1024]{3,2,1,0:T(8,128)(2,1)S(1)}, u32[]{:S(2)}, u32[]{:S(2)}) collective-permute-start(bf16[8,2,8,1024]{3,2,1,0:T(8,128)(2,1)S(1)} %shard_map.57.white_ref.refs_0_), channel_id=1, source_target_pairs={{4,0},{8,4},{12,8},{5,1},{9,5},{13,9},{6,2},{10,6},{14,10},{7,3},{... | collective-permute-start | bytes 786440 | tf_op jit(solution)/shard_map/ppermute | solution.py:26
  5.3 11.3 %collective-permute-start.5 = (bf16[8,2,8,1024]{3,2,1,0:T(8,128)(2,1)S(1)}, bf16[8,2,8,1024]{3,2,1,0:T(8,128)(2,1)S(1)}, u32[]{:S(2)}, u32[]{:S(2)}) collective-permute-start(bf16[8,2,8,1024]{3,2,1,0:T(8,128)(2,1)S(1)} %shard_map.57.white_ref.refs_0_), channel_id=1, source_target_pairs={{0,4},{4,8},{8,12},{1,5},{5,9},{9,13},{2,6},{6,10},{10,14},{3,7},{... | collective-permute-start | bytes 786440 | tf_op jit(solution)/shard_map/ppermute | solution.py:26
  12.3 1.4 %collective-permute-start.3 = (f32[1,2,64,256]{3,2,1,0:T(8,128)S(1)}, f32[1,2,64,256]{3,2,1,0:T(8,128)S(1)}, u32[]{:S(2)}, u32[]{:S(2)}) collective-permute-start(f32[1,2,64,256]{3,2,1,0:T(8,128)S(1)} %get-tuple-element.32), channel_id=1, source_target_pairs={{0,1},{1,0},{2,3},{3,2},{4,5},{5,4},{6,7},{7,6},{8,9},{9,8},{10,11... | collective-permute-start | bytes 393224 | tf_op jit(solution)/shard_map/ppermute | solution.py:267
  12.5 9.0 %collective-permute-start.1 = (bf16[8,2,8,1024]{3,2,1,0:T(8,128)(2,1)S(1)}, bf16[8,2,8,1024]{3,2,1,0:T(8,128)(2,1)S(1)}, u32[]{:S(2)}, u32[]{:S(2)}) collective-permute-start(bf16[8,2,8,1024]{3,2,1,0:T(8,128)(2,1)S(1)} %shard_map.57.white_ref.refs_0_), channel_id=1, source_target_pairs={{12,4},{13,5},{14,6},{15,7},{28,20},{29,21},{30,22},{31,23}} | collective-permute-start | bytes 786440 | tf_op jit(solution)/shard_map/ppermute | solution.py:292
  18.3 2.2 %collective-permute-start.6 = (f32[1,2,64,256]{3,2,1,0:T(8,128)S(1)}, f32[1,2,64,256]{3,2,1,0:T(8,128)S(1)}, u32[]{:S(2)}, u32[]{:S(2)}) collective-permute-start(f32[1,2,64,256]{3,2,1,0:T(8,128)S(1)} %get-tuple-element.40), channel_id=1, source_target_pairs={{0,1},{1,0},{2,3},{3,2},{4,5},{5,4},{6,7},{7,6},{8,9},{9,8},{10,11... | collective-permute-start | bytes 393224 | tf_op jit(solution)/shard_map/ppermute | solution.py:267
  20.0 7.9 %copy-start.3 = (s32[8,4]{0,1:T(4,128)S(1)}, s32[8,4]{0,1:T(4,128)}, u32[]{:S(2)}) copy-start(s32[8,4]{0,1:T(4,128)} %param.7) | copy-start | bytes 388
  20.0 1.5 %collective-permute-start.4 = (f32[1,2,64,256]{3,2,1,0:T(8,128)S(1)}, f32[1,2,64,256]{3,2,1,0:T(8,128)S(1)}, u32[]{:S(2)}, u32[]{:S(2)}) collective-permute-start(f32[1,2,64,256]{3,2,1,0:T(8,128)S(1)} %get-tuple-element.35), channel_id=1, source_target_pairs={{0,1},{1,0},{2,3},{3,2},{4,5},{5,4},{6,7},{7,6},{8,9},{9,8},{10,11... | collective-permute-start | bytes 393224 | tf_op jit(solution)/shard_map/ppermute | solution.py:267
  23.2 2.1 %collective-permute-start.8 = (f32[1,2,64,256]{3,2,1,0:T(8,128)S(1)}, f32[1,2,64,256]{3,2,1,0:T(8,128)S(1)}, u32[]{:S(2)}, u32[]{:S(2)}) collective-permute-start(f32[1,2,64,256]{3,2,1,0:T(8,128)S(1)} %get-tuple-element.45), channel_id=1, source_target_pairs={{0,1},{1,0},{2,3},{3,2},{4,5},{5,4},{6,7},{7,6},{8,9},{9,8},{10,11... | collective-permute-start | bytes 393224 | tf_op jit(solution)/shard_map/ppermute | solution.py:267
  23.6 4.5 %collective-permute-start.7 = (bf16[2,64,256]{2,1,0:T(8,128)(2,1)S(1)}, bf16[2,64,256]{2,1,0:T(8,128)(2,1)S(1)}, u32[]{:S(2)}, u32[]{:S(2)}) collective-permute-start(bf16[2,64,256]{2,1,0:T(8,128)(2,1)S(1)} %get-tuple-element.42), channel_id=1, source_target_pairs={{0,2},{2,0},{1,3},{3,1},{4,6},{6,4},{5,7},{7,5},{8,10},{10,8},{9,1... | collective-permute-start | bytes 196616 | tf_op jit(solution)/shard_map/ppermute | solution.py:267
  25.3 8.1 %collective-permute-start.9 = (bf16[2,64,256]{2,1,0:T(8,128)(2,1)S(1)}, bf16[2,64,256]{2,1,0:T(8,128)(2,1)S(1)}, u32[]{:S(2)}, u32[]{:S(2)}) collective-permute-start(bf16[2,64,256]{2,1,0:T(8,128)(2,1)S(1)} %get-tuple-element.47), channel_id=1, source_target_pairs={{4,0},{8,4},{12,8},{5,1},{9,5},{13,9},{6,2},{10,6},{14,10},{7,3},{... | collective-permute-start | bytes 196616 | tf_op jit(solution)/shard_map/ppermute | solution.py:26
  26.6 9.4 %collective-permute-start.10 = (bf16[2,64,256]{2,1,0:T(8,128)(2,1)S(1)}, bf16[2,64,256]{2,1,0:T(8,128)(2,1)S(1)}, u32[]{:S(2)}, u32[]{:S(2)}) collective-permute-start(bf16[2,64,256]{2,1,0:T(8,128)(2,1)S(1)} %get-tuple-element.48), channel_id=1, source_target_pairs={{4,2},{6,0},{8,6},{10,4},{12,10},{14,8},{5,3},{7,1},{9,7},{11,5},{... | collective-permute-start | bytes 196616 | tf_op jit(solution)/shard_map/ppermute | solution.py:309

commit v11 on v10

--- a/solution.py
+++ b/solution.py
@@ -42,11 +42,12 @@
     return jnp.sum(x[0] * x[0] + x[1] * x[1], axis=-1, keepdims=True)
 
 
-def power_kernel(x_ref, power_ref, copy_ref):
+def power_kernel(x_ref, base_ref, power_ref, x_copy_ref, base_copy_ref):
     for w in range(x_ref.shape[0]):
         x = x_ref[w]
         power_ref[w] = bin_power(x)
-        copy_ref[w] = x
+        x_copy_ref[w] = x
+    base_copy_ref[...] = base_ref[...]
 
 
 def whiten_kernel(n_bins, x_ref, *refs):
@@ -108,8 +109,12 @@
 def pairs_kernel(n_partners, n_win, n_freq, base_ref, *refs):
     partner_refs = refs[:n_partners]
     twist_ref, table_ref = refs[n_partners:n_partners + 2]
+    before_refs = refs[n_partners + 2:-2 - n_freq]
     out_refs = refs[-2 - n_freq:-2]
     rows_ref, sums_ref = refs[-2:]
+    done = out_refs[0].shape[0] - n_partners
+    for before_ref, out_ref in zip(before_refs, out_refs):
+        out_ref[:done] = before_ref[...]
     ch, f_dev = base_ref.shape[2:]
     pairs = ch * ch
     groups = n_win * n_freq
@@ -143,7 +148,7 @@
                 block = jnp.where(upper, owner - groups // 2, groups // 2 - 1 - owner)
                 sign = jnp.where(upper, -1.0, 1.0)
                 lags = pl.ds(pl.multiple_of(block * width, LANES), width)
-                out_ref[k, turn_win] = sums_ref[0, :, lags] + sign * sums_ref[1, :, lags]
+                out_ref[done + k, turn_win] = sums_ref[0, :, lags] + sign * sums_ref[1, :, lags]
 
 
 def add_kernel(n_parts, n_before, *refs):
@@ -207,27 +212,29 @@
     def cost(flops, size):
         return pl.CostEstimate(flops=flops, bytes_accessed=size, transcendentals=0)
 
-    power, copied = pl.pallas_call(
+    half_lags = 2 * np.arange(LAGS // 2) + 1
+    coarse = phases(np.arange(0, n_bins, FINE), half_lags)
+    fine = phases(F_LO + np.arange(FINE), half_lags)
+    base = np.concatenate([coarse, fine], axis=1)
+    power, copied, base = pl.pallas_call(
         power_kernel,
         out_shape=[
             jax.ShapeDtypeStruct((w_dev, ch, 1), jnp.float32),
             jax.ShapeDtypeStruct(spectra.shape, spectra.dtype),
+            jax.ShapeDtypeStruct(base.shape, jnp.float32),
         ],
-        in_specs=[VMEM], out_specs=[VMEM] * 2, compiler_params=params, cost_estimate=cost(ch, ch),
-    )(spectra)
+        in_specs=[VMEM] * 2, out_specs=[VMEM] * 3, compiler_params=params, cost_estimate=cost(ch, ch),
+    )(spectra, jnp.asarray(base))
     own_power = []
     for turn in range(1, n_freq):
         route = [(f, (f + turn) % n_freq) for f in range(n_freq)]
         own_power.append(lax.ppermute(power, "freq", route))
 
-    half_lags = 2 * np.arange(LAGS // 2) + 1
-    coarse = phases(np.arange(0, n_bins, FINE), half_lags)
-    fine = phases(F_LO + np.arange(FINE), half_lags)
     table = pl.pallas_call(
         table_kernel,
         out_shape=jax.ShapeDtypeStruct((4, f_dev, LAGS // 2), jnp.bfloat16),
         in_specs=[VMEM], out_specs=VMEM, compiler_params=params, cost_estimate=cost(ch, ch),
-    )(jnp.asarray(np.concatenate([coarse, fine], axis=1)))
+    )(base)
     twist = phases(F_LO + np.arange(n_bins), np.ones(1)).reshape(2, n_freq, f_dev)
     twist = jnp.asarray(np.moveaxis(twist, 0, 1))
 
@@ -247,18 +254,19 @@
             in_specs=[VMEM] * 2, out_specs=VMEM, compiler_params=params,
         )(kept_windows, block)
 
-    def pairs(base, partners):
+    def pairs(base, partners, before=()):
+        n = len(partners) + (before[0].shape[0] if before else 0)
         return pl.pallas_call(
             functools.partial(pairs_kernel, len(partners), n_win, n_freq),
-            out_shape=[jax.ShapeDtypeStruct((len(partners), n_win, ch * ch, width), jnp.float32)] * n_freq,
-            in_specs=[VMEM] * (3 + len(partners)), out_specs=[VMEM] * n_freq,
+            out_shape=[jax.ShapeDtypeStruct((n, n_win, ch * ch, width), jnp.float32)] * n_freq,
+            in_specs=[VMEM] * (3 + len(partners) + len(before)), out_specs=[VMEM] * n_freq,
             scratch_shapes=[
                 pltpu.VMEM((2, 2 * ch * ch, f_dev), jnp.bfloat16),
                 pltpu.VMEM((2, ch * ch, LAGS // 2), jnp.float32),
             ],
             compiler_params=params,
             cost_estimate=cost(ch, ch),
-        )(base, *partners, twist, table)
+        )(base, *partners, twist, table, *before)
 
     def turns(parts, axis, size):
         received = [parts[0]]
@@ -291,15 +299,16 @@
         route = [(c + distance, c) for c in range(1, n_chan - distance)]
         far.append(lax.ppermute(white, "chan", route))
     own = kept(white)
-    first = sum_bins(pairs(own, [white]))
+    first = pairs(own, [white])
     below, first = lax.optimization_barrier((below, first))
     base = kept(above)
-    sums = split_windows(pairs(own, [below]), [first], [jnp.float32] + [jnp.bfloat16] * (n_win - 1))
-    before = [sum_bins(pairs(base, [below]))]
-    for block in far[:-1]:
-        before.append(sum_bins(pairs(base, [block])))
-    far, sums, before = lax.optimization_barrier((far[-1], sums, before))
-    shipped = split_windows(pairs(base, [far]), before, [jnp.bfloat16] * n_win)
+    parts = pairs(own, [below], first)
+    before = ()
+    for block in [below] + far[:-1]:
+        before = pairs(base, [block], before)
+    far, parts, before = lax.optimization_barrier((far[-1], parts, before))
+    sums = split_windows(parts, [], [jnp.float32] + [jnp.bfloat16] * (n_win - 1))
+    shipped = split_windows(pairs(base, [far], before), [], [jnp.bfloat16] * n_win)
     received = turns(sums, "win", n_win)
     received.append(from_behind(shipped[0], "chan", -1))
     for turn in range(1, n_win):

time: 37.1 us -> 35.7 us (0.962)
  waiting for transfers between devices: 12.3 us -> 11.5 us
  starting transfers between devices: 13.1 us -> 12.5 us
    ppermute x5 -> x3, waiting for transfers between devices: 1.44 us -> 0.01 us  [turns(): received.append(lax.ppermute(parts[turn], axis, route))]
    ppermute x5 -> x3, starting transfers between devices: 2.97 us -> 2.34 us  [turns(): received.append(lax.ppermute(parts[turn], axis, route))]
    ppermute x3, waiting for transfers between devices: 8.25 us -> 8.69 us  [from_behind(): return lax.ppermute(block, axis, route)]
  transfers between devices with their start and end apart: 11 -> 9, of which waited for: 6 -> 4; matrix products, arithmetic and copies ran while one was open for 1% -> 1% of each run, Pallas kernels for 17% -> 22%
where the time goes in v11:
time: 35.7 us; the launch traced here: 35.5 us
  starting transfers between devices  12.5 us (35%)
  waiting for transfers between devices  11.5 us (32%)
  Pallas kernels  9.04 us (25%)
  local copies, waits for them, and re-layouts  2.2 us (6%)
    ppermute x3, waiting for transfers between devices, from_behind(): return lax.ppermute(block, axis, route)  8.69 us
    ppermute x3, starting transfers between devices, from_behind(): return lax.ppermute(block, axis, route)  7.72 us
    pallas_call x4, Pallas kernels, pairs(): pl.pallas_call(functools.partial(pairs_kernel, len(partners), n_win, n_fr...  6.32 us
    ppermute x1, waiting for transfers between devices, local(): received.append(lax.ppermute(shipped[turn], ('chan', 'win'), route))  2.81 us
    ppermute x3, starting transfers between devices, turns(): received.append(lax.ppermute(parts[turn], axis, route))  2.34 us
    unnamed x10, local copies, waits for them, and re-layouts  1.96 us
    ppermute x1, starting transfers between devices, local(): received.append(lax.ppermute(shipped[turn], ('chan', 'win'), route))  1.29 us
    pallas_call x1, Pallas kernels, local(): pl.pallas_call(table_kernel, out_shape=jax.ShapeDtypeStruct((4, f_dev, LA...  1.19 us
  transfers between devices with their start and end apart: 9, of which 4 were waited for; matrix products, arithmetic and copies ran while one was open for 1% of the time, Pallas kernels for 22%

profile of v11, /device:TPU:0, one launch (start us, length us, event | category | flops | bytes accessed | tf_op | source)
XLA Modules:
  0.0 35.5 jit_solution(4016233900430550302)
XLA Ops:
  0.0 0.0 copy-start
  0.0 1.0 %copy-done = f32[2,96,512]{2,1,0:T(8,128)S(1)} copy-done((f32[2,96,512]{2,1,0:T(8,128)S(1)}, f32[2,96,512]{2,1,0:T(8,128)}, u32[]{:S(2)}) %copy-start) | copy-done | bytes 393240
  1.0 0.0 copy-start.2
  1.0 0.9 %copy-done.2 = bf16[8,2,8,1024]{3,2,1,0:T(8,128)(2,1)S(1)} copy-done((bf16[8,2,8,1024]{3,2,1,0:T(8,128)(2,1)S(1)}, bf16[8,2,8,1024]{3,2,1,0:T(8,128)(2,1)}, u32[]{:S(2)}) %copy-start.2) | copy-done | bytes 262168
  1.9 0.0 copy-start.4
  1.9 0.0 copy-start.1
  2.0 0.1 shard_map.55
  2.1 0.5 %collective-permute-start = (f32[8,8,1]{2,1,0:T(8,128)S(1)}, f32[8,8,1]{2,1,0:T(8,128)S(1)}, u32[]{:S(2)}, u32[]{:S(2)}) collective-permute-start(f32[8,8,1]{2,1,0:T(8,128)S(1)} %get-tuple-element.32), channel_id=1, source_target_pairs={{0,1},{1,0},{2,3},{3,2},{4,5},{5,4},{6,7},{7,6},{8,9},{9,8},{10,11... | collective-permute-start | bytes 776 | tf_op jit(solution)/shard_map/ppermute | solution.py:231
  2.6 1.2 %shard_map.56.refs_2_ = bf16[4,1024,512]{2,1,0:T(8,128)(2,1)S(1)} custom-call(f32[2,96,512]{2,1,0:T(8,128)S(1)} %get-tuple-element.31.base_ref), custom_call_target="tpu_custom_call" | custom-call | flops 8 | bytes 8 | tf_op jit(solution)/shard_map/pallas_call | solution.py:233
  3.8 0.0 collective-permute-done.refs_0_
  3.8 0.2 shard_map.57.white_ref.refs_0_
  4.0 1.3 %collective-permute-start.2 = (bf16[8,2,8,1024]{3,2,1,0:T(8,128)(2,1)S(1)}, bf16[8,2,8,1024]{3,2,1,0:T(8,128)(2,1)S(1)}, u32[]{:S(2)}, u32[]{:S(2)}) collective-permute-start(bf16[8,2,8,1024]{3,2,1,0:T(8,128)(2,1)S(1)} %shard_map.57.white_ref.refs_0_), channel_id=1, source_target_pairs={{4,0},{8,4},{12,8},{5,1},{9,5},{13,9},{6,2},{10,6},{14,10},{7,3},{... | collective-permute-start | bytes 786440 | tf_op jit(solution)/shard_map/ppermute | solution.py:26
  5.3 5.1 %collective-permute-start.3 = (bf16[8,2,8,1024]{3,2,1,0:T(8,128)(2,1)S(1)}, bf16[8,2,8,1024]{3,2,1,0:T(8,128)(2,1)S(1)}, u32[]{:S(2)}, u32[]{:S(2)}) collective-permute-start(bf16[8,2,8,1024]{3,2,1,0:T(8,128)(2,1)S(1)} %shard_map.57.white_ref.refs_0_), channel_id=1, source_target_pairs={{0,4},{4,8},{8,12},{1,5},{5,9},{9,13},{2,6},{6,10},{10,14},{3,7},{... | collective-permute-start | bytes 786440 | tf_op jit(solution)/shard_map/ppermute | solution.py:26
  10.5 0.7 %collective-permute-start.1 = (bf16[8,2,8,1024]{3,2,1,0:T(8,128)(2,1)S(1)}, bf16[8,2,8,1024]{3,2,1,0:T(8,128)(2,1)S(1)}, u32[]{:S(2)}, u32[]{:S(2)}) collective-permute-start(bf16[8,2,8,1024]{3,2,1,0:T(8,128)(2,1)S(1)} %shard_map.57.white_ref.refs_0_), channel_id=1, source_target_pairs={{12,4},{13,5},{14,6},{15,7},{28,20},{29,21},{30,22},{31,23}} | collective-permute-start | bytes 786440 | tf_op jit(solution)/shard_map/ppermute | solution.py:300
  11.1 0.0 copy-done.4
  11.2 0.1 broadcast_in_dim.10.keep_ref
  11.2 0.1 shard_map.58.base_ref
  11.3 0.0 copy-done.1
  11.4 1.6 %shard_map.59 = (f32[1,2,64,256]{3,2,1,0:T(8,128)S(1)}, f32[1,2,64,256]{3,2,1,0:T(8,128)S(1)}) custom-call(f32[8,2,8,1024]{3,2,1,0:T(8,128)S(1)} %shard_map.58.base_ref, bf16[8,2,8,1024]{3,2,1,0:T(8,128)(2,1)S(1)} %shard_map.57.white_ref.refs_0_, f32[2,2,1024]{2,1,0:T(2,128)S(1)} %copy-done.1, bf16[4,1024,512]{2,1,0:T(8,128)(2,1)S(1)} %shard_map.56.refs_2_), custom_call_target="tpu_custom_call" | custom-call | flops 8 | bytes 8 | tf_op jit(solution)/shard_map/pallas_call | solution.py:259
  12.9 2.5 %collective-permute-done.2.refs_0_ = bf16[8,2,8,1024]{3,2,1,0:T(8,128)(2,1)S(1)} collective-permute-done((bf16[8,2,8,1024]{3,2,1,0:T(8,128)(2,1)S(1)}, bf16[8,2,8,1024]{3,2,1,0:T(8,128)(2,1)S(1)}, u32[]{:S(2)}, u32[]{:S(2)}) %collective-permute-start.2) | collective-permute-done | bytes 262176 | tf_op jit(solution)/shard_map/ppermute | solution.py:26
  15.5 1.2 %collective-permute-done.3.white_ref = bf16[8,2,8,1024]{3,2,1,0:T(8,128)(2,1)S(1)} collective-permute-done((bf16[8,2,8,1024]{3,2,1,0:T(8,128)(2,1)S(1)}, bf16[8,2,8,1024]{3,2,1,0:T(8,128)(2,1)S(1)}, u32[]{:S(2)}, u32[]{:S(2)}) %collective-permute-start.3) | collective-permute-done | bytes 262176 | tf_op jit(solution)/shard_map/ppermute | solution.py:26
  16.6 0.1 shard_map.61.base_ref
  16.8 1.6 %shard_map.62 = (f32[1,2,64,256]{3,2,1,0:T(8,128)S(1)}, f32[1,2,64,256]{3,2,1,0:T(8,128)S(1)}) custom-call(f32[8,2,8,1024]{3,2,1,0:T(8,128)S(1)} %shard_map.61.base_ref, bf16[8,2,8,1024]{3,2,1,0:T(8,128)(2,1)S(1)} %collective-permute-done.2.refs_0_, f32[2,2,1024]{2,1,0:T(2,128)S(1)} %copy-done.1, bf16[4,1024,512]{2,1,0:T(8,128)(2,1)S(1)} %shard_map.56.refs_2_), custom_call_target="tpu_custom_call" | custom-call | flops 8 | bytes 8 | tf_op jit(solution)/shard_map/pallas_call | solution.py:259
  18.3 1.6 %shard_map.60 = (f32[2,2,64,256]{3,2,1,0:T(8,128)S(1)}, f32[2,2,64,256]{3,2,1,0:T(8,128)S(1)}) custom-call(f32[8,2,8,1024]{3,2,1,0:T(8,128)S(1)} %shard_map.58.base_ref, bf16[8,2,8,1024]{3,2,1,0:T(8,128)(2,1)S(1)} %collective-permute-done.2.refs_0_, f32[2,2,1024]{2,1,0:T(2,128)S(1)} %copy-done.1, bf16[4,1024,512]{2,1,0:T(8,128)(2,1)S(1)} %shard_map.56.refs_2_, ...), custom_call_target="tpu_custom_call" | custom-call | flops 8 | bytes 8 | tf_op jit(solution)/shard_map/pallas_call | solution.py:259
  19.9 0.0 copy-start.3
  19.9 0.0 collective-permute-done.1.refs_0_
  20.0 0.1 collective-permute-start.4
  20.0 1.6 %shard_map.64 = (f32[2,2,64,256]{3,2,1,0:T(8,128)S(1)}, f32[2,2,64,256]{3,2,1,0:T(8,128)S(1)}) custom-call(f32[8,2,8,1024]{3,2,1,0:T(8,128)S(1)} %shard_map.61.base_ref, bf16[8,2,8,1024]{3,2,1,0:T(8,128)(2,1)S(1)} %collective-permute-done.1.refs_0_, f32[2,2,1024]{2,1,0:T(2,128)S(1)} %copy-done.1, bf16[4,1024,512]{2,1,0:T(8,128)(2,1)S(1)} %shard_map.56.refs_2_, ...), custom_call_target="tpu_custom_call" | custom-call | flops 8 | bytes 8 | tf_op jit(solution)/shard_map/pallas_call | solution.py:259
  21.6 0.6 %collective-permute-start.6 = (f32[2,2,64,256]{3,2,1,0:T(8,128)S(1)}, f32[2,2,64,256]{3,2,1,0:T(8,128)S(1)}, u32[]{:S(2)}, u32[]{:S(2)}) collective-permute-start(f32[2,2,64,256]{3,2,1,0:T(8,128)S(1)} %get-tuple-element.52), channel_id=1, source_target_pairs={{0,1},{1,0},{2,3},{3,2},{4,5},{5,4},{6,7},{7,6},{8,9},{9,8},{10,11... | collective-permute-start | bytes 786440 | tf_op jit(solution)/shard_map/ppermute | solution.py:275
  22.2 0.0 collective-permute-done.4.refs_1_
  22.2 1.7 %collective-permute-start.5 = (bf16[2,64,256]{2,1,0:T(8,128)(2,1)S(1)}, bf16[2,64,256]{2,1,0:T(8,128)(2,1)S(1)}, u32[]{:S(2)}, u32[]{:S(2)}) collective-permute-start(bf16[2,64,256]{2,1,0:T(8,128)(2,1)S(1)} %get-tuple-element.47), channel_id=1, source_target_pairs={{0,2},{2,0},{1,3},{3,1},{4,6},{6,4},{5,7},{7,5},{8,10},{10,8},{9,1... | collective-permute-start | bytes 196616 | tf_op jit(solution)/shard_map/ppermute | solution.py:275
  23.9 0.0 collective-permute-done.6.refs_1_
  24.0 1.3 %collective-permute-start.7 = (bf16[2,64,256]{2,1,0:T(8,128)(2,1)S(1)}, bf16[2,64,256]{2,1,0:T(8,128)(2,1)S(1)}, u32[]{:S(2)}, u32[]{:S(2)}) collective-permute-start(bf16[2,64,256]{2,1,0:T(8,128)(2,1)S(1)} %get-tuple-element.53), channel_id=1, source_target_pairs={{4,0},{8,4},{12,8},{5,1},{9,5},{13,9},{6,2},{10,6},{14,10},{7,3},{... | collective-permute-start | bytes 196616 | tf_op jit(solution)/shard_map/ppermute | solution.py:26
  25.3 1.3 %collective-permute-start.8 = (bf16[2,64,256]{2,1,0:T(8,128)(2,1)S(1)}, bf16[2,64,256]{2,1,0:T(8,128)(2,1)S(1)}, u32[]{:S(2)}, u32[]{:S(2)}) collective-permute-start(bf16[2,64,256]{2,1,0:T(8,128)(2,1)S(1)} %get-tuple-element.54), channel_id=1, source_target_pairs={{4,2},{6,0},{8,6},{10,4},{12,10},{14,8},{5,3},{7,1},{9,7},{11,5},{... | collective-permute-start | bytes 196616 | tf_op jit(solution)/shard_map/ppermute | solution.py:318
  26.6 0.0 copy-done.3
  26.6 0.1 broadcast_in_dim.4
  26.7 0.1 broadcast_in_dim_reshape.4.factor_ref
  26.8 0.0 collective-permute-done.5.refs_1_
  26.8 5.0 %collective-permute-done.7.refs_2_ = bf16[2,64,256]{2,1,0:T(8,128)(2,1)S(1)} collective-permute-done((bf16[2,64,256]{2,1,0:T(8,128)(2,1)S(1)}, bf16[2,64,256]{2,1,0:T(8,128)(2,1)S(1)}, u32[]{:S(2)}, u32[]{:S(2)}) %collective-permute-start.7) | collective-permute-done | bytes 65568 | tf_op jit(solution)/shard_map/ppermute | solution.py:26
  31.8 2.8 %collective-permute-done.8.refs_3_ = bf16[2,64,256]{2,1,0:T(8,128)(2,1)S(1)} collective-permute-done((bf16[2,64,256]{2,1,0:T(8,128)(2,1)S(1)}, bf16[2,64,256]{2,1,0:T(8,128)(2,1)S(1)}, u32[]{:S(2)}, u32[]{:S(2)}) %collective-permute-start.8) | collective-permute-done | bytes 65568 | tf_op jit(solution)/shard_map/ppermute | solution.py:318
  34.6 0.9 %shard_map.66 = f32[8,4,8,256]{3,2,1,0:T(8,128)} custom-call(f32[4,64,1]{2,1,0:T(8,128)S(1)} %broadcast_in_dim_reshape.4.factor_ref, f32[2,64,256]{2,1,0:T(8,128)S(1)} %get-tuple-element.46.refs_0_, bf16[2,64,256]{2,1,0:T(8,128)(2,1)S(1)} %collective-permute-done.5.refs_1_, bf16[2,64,256]{2,1,0:T(8,128)(2,1)S(1)} %collective-permute-done.7.refs_2_, ...), custom_call_target="tpu_custom_call" | custom-call | tf_op jit(solution)/shard_map/pallas_call | solution.py:321
  (4 shorter events, 0.1 us)
Async XLA Ops:
  0.0 1.0 %copy-start = (f32[2,96,512]{2,1,0:T(8,128)S(1)}, f32[2,96,512]{2,1,0:T(8,128)}, u32[]{:S(2)}) copy-start(f32[2,96,512]{2,1,0:T(8,128)} %constant.6.clone.base_ref) | copy-start | bytes 1179652
  1.0 0.9 %copy-start.2 = (bf16[8,2,8,1024]{3,2,1,0:T(8,128)(2,1)S(1)}, bf16[8,2,8,1024]{3,2,1,0:T(8,128)(2,1)}, u32[]{:S(2)}) copy-start(bf16[8,2,8,1024]{3,2,1,0:T(8,128)(2,1)} %x_ref.1) | copy-start | bytes 786436
  1.9 9.2 %copy-start.4 = (s32[8]{0:T(128)S(1)}, s32[8]{0:T(128)}, u32[]{:S(2)}) copy-start(s32[8]{0:T(128)} %param.6) | copy-start | bytes 100
  1.9 9.4 %copy-start.1 = (f32[2,2,1024]{2,1,0:T(2,128)S(1)}, f32[2,2,1024]{2,1,0:T(2,128)}, u32[]{:S(2)}) copy-start(f32[2,2,1024]{2,1,0:T(2,128)} %constant.7.clone.refs_1_) | copy-start | bytes 49156
  2.1 1.7 %collective-permute-start = (f32[8,8,1]{2,1,0:T(8,128)S(1)}, f32[8,8,1]{2,1,0:T(8,128)S(1)}, u32[]{:S(2)}, u32[]{:S(2)}) collective-permute-start(f32[8,8,1]{2,1,0:T(8,128)S(1)} %get-tuple-element.32), channel_id=1, source_target_pairs={{0,1},{1,0},{2,3},{3,2},{4,5},{5,4},{6,7},{7,6},{8,9},{9,8},{10,11... | collective-permute-start | bytes 776 | tf_op jit(solution)/shard_map/ppermute | solution.py:231
  4.0 11.5 %collective-permute-start.2 = (bf16[8,2,8,1024]{3,2,1,0:T(8,128)(2,1)S(1)}, bf16[8,2,8,1024]{3,2,1,0:T(8,128)(2,1)S(1)}, u32[]{:S(2)}, u32[]{:S(2)}) collective-permute-start(bf16[8,2,8,1024]{3,2,1,0:T(8,128)(2,1)S(1)} %shard_map.57.white_ref.refs_0_), channel_id=1, source_target_pairs={{4,0},{8,4},{12,8},{5,1},{9,5},{13,9},{6,2},{10,6},{14,10},{7,3},{... | collective-permute-start | bytes 786440 | tf_op jit(solution)/shard_map/ppermute | solution.py:26
  5.3 11.3 %collective-permute-start.3 = (bf16[8,2,8,1024]{3,2,1,0:T(8,128)(2,1)S(1)}, bf16[8,2,8,1024]{3,2,1,0:T(8,128)(2,1)S(1)}, u32[]{:S(2)}, u32[]{:S(2)}) collective-permute-start(bf16[8,2,8,1024]{3,2,1,0:T(8,128)(2,1)S(1)} %shard_map.57.white_ref.refs_0_), channel_id=1, source_target_pairs={{0,4},{4,8},{8,12},{1,5},{5,9},{9,13},{2,6},{6,10},{10,14},{3,7},{... | collective-permute-start | bytes 786440 | tf_op jit(solution)/shard_map/ppermute | solution.py:26
  10.5 9.5 %collective-permute-start.1 = (bf16[8,2,8,1024]{3,2,1,0:T(8,128)(2,1)S(1)}, bf16[8,2,8,1024]{3,2,1,0:T(8,128)(2,1)S(1)}, u32[]{:S(2)}, u32[]{:S(2)}) collective-permute-start(bf16[8,2,8,1024]{3,2,1,0:T(8,128)(2,1)S(1)} %shard_map.57.white_ref.refs_0_), channel_id=1, source_target_pairs={{12,4},{13,5},{14,6},{15,7},{28,20},{29,21},{30,22},{31,23}} | collective-permute-start | bytes 786440 | tf_op jit(solution)/shard_map/ppermute | solution.py:300
  19.9 6.6 %copy-start.3 = (s32[8,4]{0,1:T(4,128)S(1)}, s32[8,4]{0,1:T(4,128)}, u32[]{:S(2)}) copy-start(s32[8,4]{0,1:T(4,128)} %param.7) | copy-start | bytes 388
  20.0 2.2 %collective-permute-start.4 = (f32[2,2,64,256]{3,2,1,0:T(8,128)S(1)}, f32[2,2,64,256]{3,2,1,0:T(8,128)S(1)}, u32[]{:S(2)}, u32[]{:S(2)}) collective-permute-start(f32[2,2,64,256]{3,2,1,0:T(8,128)S(1)} %get-tuple-element.45), channel_id=1, source_target_pairs={{0,1},{1,0},{2,3},{3,2},{4,5},{5,4},{6,7},{7,6},{8,9},{9,8},{10,11... | collective-permute-start | bytes 786440 | tf_op jit(solution)/shard_map/ppermute | solution.py:275
  21.6 2.3 %collective-permute-start.6 = (f32[2,2,64,256]{3,2,1,0:T(8,128)S(1)}, f32[2,2,64,256]{3,2,1,0:T(8,128)S(1)}, u32[]{:S(2)}, u32[]{:S(2)}) collective-permute-start(f32[2,2,64,256]{3,2,1,0:T(8,128)S(1)} %get-tuple-element.52), channel_id=1, source_target_pairs={{0,1},{1,0},{2,3},{3,2},{4,5},{5,4},{6,7},{7,6},{8,9},{9,8},{10,11... | collective-permute-start | bytes 786440 | tf_op jit(solution)/shard_map/ppermute | solution.py:275
  22.2 4.5 %collective-permute-start.5 = (bf16[2,64,256]{2,1,0:T(8,128)(2,1)S(1)}, bf16[2,64,256]{2,1,0:T(8,128)(2,1)S(1)}, u32[]{:S(2)}, u32[]{:S(2)}) collective-permute-start(bf16[2,64,256]{2,1,0:T(8,128)(2,1)S(1)} %get-tuple-element.47), channel_id=1, source_target_pairs={{0,2},{2,0},{1,3},{3,1},{4,6},{6,4},{5,7},{7,5},{8,10},{10,8},{9,1... | collective-permute-start | bytes 196616 | tf_op jit(solution)/shard_map/ppermute | solution.py:275
  24.0 7.8 %collective-permute-start.7 = (bf16[2,64,256]{2,1,0:T(8,128)(2,1)S(1)}, bf16[2,64,256]{2,1,0:T(8,128)(2,1)S(1)}, u32[]{:S(2)}, u32[]{:S(2)}) collective-permute-start(bf16[2,64,256]{2,1,0:T(8,128)(2,1)S(1)} %get-tuple-element.53), channel_id=1, source_target_pairs={{4,0},{8,4},{12,8},{5,1},{9,5},{13,9},{6,2},{10,6},{14,10},{7,3},{... | collective-permute-start | bytes 196616 | tf_op jit(solution)/shard_map/ppermute | solution.py:26
  25.3 9.3 %collective-permute-start.8 = (bf16[2,64,256]{2,1,0:T(8,128)(2,1)S(1)}, bf16[2,64,256]{2,1,0:T(8,128)(2,1)S(1)}, u32[]{:S(2)}, u32[]{:S(2)}) collective-permute-start(bf16[2,64,256]{2,1,0:T(8,128)(2,1)S(1)} %get-tuple-element.54), channel_id=1, source_target_pairs={{4,2},{6,0},{8,6},{10,4},{12,10},{14,8},{5,3},{7,1},{9,7},{11,5},{... | collective-permute-start | bytes 196616 | tf_op jit(solution)/shard_map/ppermute | solution.py:318

commit v12 on v11

--- a/solution.py
+++ b/solution.py
@@ -42,12 +42,11 @@
     return jnp.sum(x[0] * x[0] + x[1] * x[1], axis=-1, keepdims=True)
 
 
-def power_kernel(x_ref, base_ref, power_ref, x_copy_ref, base_copy_ref):
+def power_kernel(x_ref, power_ref, copy_ref):
     for w in range(x_ref.shape[0]):
         x = x_ref[w]
         power_ref[w] = bin_power(x)
-        x_copy_ref[w] = x
-    base_copy_ref[...] = base_ref[...]
+        copy_ref[w] = x
 
 
 def whiten_kernel(n_bins, x_ref, *refs):
@@ -212,29 +211,19 @@
     def cost(flops, size):
         return pl.CostEstimate(flops=flops, bytes_accessed=size, transcendentals=0)
 
-    half_lags = 2 * np.arange(LAGS // 2) + 1
-    coarse = phases(np.arange(0, n_bins, FINE), half_lags)
-    fine = phases(F_LO + np.arange(FINE), half_lags)
-    base = np.concatenate([coarse, fine], axis=1)
-    power, copied, base = pl.pallas_call(
+    power, copied = pl.pallas_call(
         power_kernel,
         out_shape=[
             jax.ShapeDtypeStruct((w_dev, ch, 1), jnp.float32),
             jax.ShapeDtypeStruct(spectra.shape, spectra.dtype),
-            jax.ShapeDtypeStruct(base.shape, jnp.float32),
         ],
-        in_specs=[VMEM] * 2, out_specs=[VMEM] * 3, compiler_params=params, cost_estimate=cost(ch, ch),
-    )(spectra, jnp.asarray(base))
+        in_specs=[VMEM], out_specs=[VMEM] * 2, compiler_params=params, cost_estimate=cost(ch, ch),
+    )(spectra)
     own_power = []
     for turn in range(1, n_freq):
         route = [(f, (f + turn) % n_freq) for f in range(n_freq)]
         own_power.append(lax.ppermute(power, "freq", route))
 
-    table = pl.pallas_call(
-        table_kernel,
-        out_shape=jax.ShapeDtypeStruct((4, f_dev, LAGS // 2), jnp.bfloat16),
-        in_specs=[VMEM], out_specs=VMEM, compiler_params=params, cost_estimate=cost(ch, ch),
-    )(base)
     twist = phases(F_LO + np.arange(n_bins), np.ones(1)).reshape(2, n_freq, f_dev)
     twist = jnp.asarray(np.moveaxis(twist, 0, 1))
 
@@ -290,7 +279,6 @@
             in_specs=[VMEM] * (n_freq + len(before)), out_specs=[VMEM] * n_win, compiler_params=params,
         )(*turns(parts, "freq", n_freq), *before)
 
-    table, own_power = lax.optimization_barrier((table, own_power))
     white = whiten(copied, own_power)
     above = from_behind(white, "chan", 1)
     below = from_behind(white, "chan", -1)
@@ -298,10 +286,20 @@
     for distance in range(2, reach):
         route = [(c + distance, c) for c in range(1, n_chan - distance)]
         far.append(lax.ppermute(white, "chan", route))
+    half_lags = 2 * np.arange(LAGS // 2) + 1
+    coarse = phases(np.arange(0, n_bins, FINE), half_lags)
+    fine = phases(F_LO + np.arange(FINE), half_lags)
+    white, ends = lax.optimization_barrier((white, jnp.asarray(np.concatenate([coarse, fine], axis=1))))
+    table = pl.pallas_call(
+        table_kernel,
+        out_shape=jax.ShapeDtypeStruct((4, f_dev, LAGS // 2), jnp.bfloat16),
+        in_specs=[VMEM], out_specs=VMEM, compiler_params=params, cost_estimate=cost(ch, ch),
+    )(ends)
     own = kept(white)
     first = pairs(own, [white])
-    below, first = lax.optimization_barrier((below, first))
+    above, first = lax.optimization_barrier((above, first))
     base = kept(above)
+    below, base = lax.optimization_barrier((below, base))
     parts = pairs(own, [below], first)
     before = ()
     for block in [below] + far[:-1]:

time: 35.7 us -> 37.6 us (1.053)
  waiting for transfers between devices: 11.5 us -> 13.2 us
  other arithmetic: 0.01 us -> 0.66 us
  starting transfers between devices: 12.5 us -> 12 us
    ppermute x1, waiting for transfers between devices: 0.01 us -> 0.86 us  [local(): own_power.append(lax.ppermute(power, 'freq', route))]
    ppermute x3, waiting for transfers between devices: 8.69 us -> 9.53 us  [from_behind(): return lax.ppermute(block, axis, route)]
    convert_element_type x1, other arithmetic: 0.01 us -> 0.66 us  [local(): keep.astype(jnp.float32)[:, None, None, None]]
    unnamed x10 -> x8, local copies, waits for them, and re-layouts: 1.96 us -> 1.97 us
  transfers between devices with their start and end apart: 9 -> 9, of which waited for: 4 -> 4; matrix products, arithmetic and copies ran while one was open for 1% -> 2% of each run, Pallas kernels for 22% -> 21%
where the time goes in v12:
time: 37.6 us; the launch traced here: 37.3 us
  waiting for transfers between devices  13.2 us (35%)
  starting transfers between devices  12 us (32%)
  Pallas kernels  9.03 us (24%)
  local copies, waits for them, and re-layouts  2.21 us (6%)
  other arithmetic  0.66 us (2%)
    ppermute x3, waiting for transfers between devices, from_behind(): return lax.ppermute(block, axis, route)  9.53 us
    ppermute x3, starting transfers between devices, from_behind(): return lax.ppermute(block, axis, route)  7.42 us
    pallas_call x4, Pallas kernels, pairs(): pl.pallas_call(functools.partial(pairs_kernel, len(partners), n_win, n_fr...  6.31 us
    ppermute x1, waiting for transfers between devices, local(): received.append(lax.ppermute(shipped[turn], ('chan', 'win'), route))  2.81 us
    ppermute x3, starting transfers between devices, turns(): received.append(lax.ppermute(parts[turn], axis, route))  2.18 us
    unnamed x8, local copies, waits for them, and re-layouts  1.97 us
    ppermute x1, starting transfers between devices, local(): received.append(lax.ppermute(shipped[turn], ('chan', 'win'), route))  1.29 us
    pallas_call x1, Pallas kernels, local(): pl.pallas_call(table_kernel, out_shape=jax.ShapeDtypeStruct((4, f_dev, LA...  1.19 us
  transfers between devices with their start and end apart: 9, of which 4 were waited for; matrix products, arithmetic and copies ran while one was open for 2% of the time, Pallas kernels for 21%

profile of v12, /device:TPU:0, one launch (start us, length us, event | category | flops | bytes accessed | tf_op | source)
XLA Modules:
  0.0 37.3 jit_solution(6397130528088389932)
XLA Ops:
  0.0 0.0 copy-start.1
  0.0 0.0 copy-start.2
  0.0 1.0 %copy-done.2 = bf16[8,2,8,1024]{3,2,1,0:T(8,128)(2,1)S(1)} copy-done((bf16[8,2,8,1024]{3,2,1,0:T(8,128)(2,1)S(1)}, bf16[8,2,8,1024]{3,2,1,0:T(8,128)(2,1)}, u32[]{:S(2)}) %copy-start.2) | copy-done | bytes 262168
  1.0 0.1 shard_map.55
  1.1 0.5 %collective-permute-start = (f32[8,8,1]{2,1,0:T(8,128)S(1)}, f32[8,8,1]{2,1,0:T(8,128)S(1)}, u32[]{:S(2)}, u32[]{:S(2)}) collective-permute-start(f32[8,8,1]{2,1,0:T(8,128)S(1)} %get-tuple-element.32), channel_id=1, source_target_pairs={{0,1},{1,0},{2,3},{3,2},{4,5},{5,4},{6,7},{7,6},{8,9},{9,8},{10,11... | collective-permute-start | bytes 776 | tf_op jit(solution)/shard_map/ppermute | solution.py:225
  1.6 0.9 %collective-permute-done.refs_0_ = f32[8,8,1]{2,1,0:T(8,128)S(1)} collective-permute-done((f32[8,8,1]{2,1,0:T(8,128)S(1)}, f32[8,8,1]{2,1,0:T(8,128)S(1)}, u32[]{:S(2)}, u32[]{:S(2)}) %collective-permute-start) | collective-permute-done | bytes 288 | tf_op jit(solution)/shard_map/ppermute | solution.py:225
  2.4 0.2 shard_map.56.white_ref.refs_0_
  2.7 4.8 %collective-permute-start.3 = (bf16[8,2,8,1024]{3,2,1,0:T(8,128)(2,1)S(1)}, bf16[8,2,8,1024]{3,2,1,0:T(8,128)(2,1)S(1)}, u32[]{:S(2)}, u32[]{:S(2)}) collective-permute-start(bf16[8,2,8,1024]{3,2,1,0:T(8,128)(2,1)S(1)} %shard_map.56.white_ref.refs_0_), channel_id=1, source_target_pairs={{0,4},{4,8},{8,12},{1,5},{5,9},{9,13},{2,6},{6,10},{10,14},{3,7},{... | collective-permute-start | bytes 786440 | tf_op jit(solution)/shard_map/ppermute | solution.py:26
  7.5 1.3 %collective-permute-start.2 = (bf16[8,2,8,1024]{3,2,1,0:T(8,128)(2,1)S(1)}, bf16[8,2,8,1024]{3,2,1,0:T(8,128)(2,1)S(1)}, u32[]{:S(2)}, u32[]{:S(2)}) collective-permute-start(bf16[8,2,8,1024]{3,2,1,0:T(8,128)(2,1)S(1)} %shard_map.56.white_ref.refs_0_), channel_id=1, source_target_pairs={{4,0},{8,4},{12,8},{5,1},{9,5},{13,9},{6,2},{10,6},{14,10},{7,3},{... | collective-permute-start | bytes 786440 | tf_op jit(solution)/shard_map/ppermute | solution.py:26
  8.8 0.7 %collective-permute-start.1 = (bf16[8,2,8,1024]{3,2,1,0:T(8,128)(2,1)S(1)}, bf16[8,2,8,1024]{3,2,1,0:T(8,128)(2,1)S(1)}, u32[]{:S(2)}, u32[]{:S(2)}) collective-permute-start(bf16[8,2,8,1024]{3,2,1,0:T(8,128)(2,1)S(1)} %shard_map.56.white_ref.refs_0_), channel_id=1, source_target_pairs={{12,4},{13,5},{14,6},{15,7},{28,20},{29,21},{30,22},{31,23}} | collective-permute-start | bytes 786440 | tf_op jit(solution)/shard_map/ppermute | solution.py:288
  9.5 0.7 %convert_element_type.8 = f32[8]{0:T(128)S(1)} convert(s32[8]{0:T(128)} %param.6) | non-fusion elementwise | flops 8 | bytes 64 | tf_op jit(solution)/shard_map/convert_element_type | solution.py:237
  10.2 0.0 copy-start
  10.2 1.0 %copy-done = f32[2,96,512]{2,1,0:T(8,128)S(1)} copy-done((f32[2,96,512]{2,1,0:T(8,128)S(1)}, f32[2,96,512]{2,1,0:T(8,128)}, u32[]{:S(2)}) %copy-start) | copy-done | bytes 393240
  11.2 1.2 %shard_map.58.refs_2_ = bf16[4,1024,512]{2,1,0:T(8,128)(2,1)S(1)} custom-call(f32[2,96,512]{2,1,0:T(8,128)S(1)} %copy-done), custom_call_target="tpu_custom_call" | custom-call | flops 8 | bytes 8 | tf_op jit(solution)/shard_map/pallas_call | solution.py:293
  12.4 0.1 broadcast_in_dim.10.keep_ref
  12.4 0.1 shard_map.57.base_ref
  12.5 0.0 copy-done.1
  12.6 1.6 %shard_map.59 = (f32[1,2,64,256]{3,2,1,0:T(8,128)S(1)}, f32[1,2,64,256]{3,2,1,0:T(8,128)S(1)}) custom-call(f32[8,2,8,1024]{3,2,1,0:T(8,128)S(1)} %shard_map.57.base_ref, bf16[8,2,8,1024]{3,2,1,0:T(8,128)(2,1)S(1)} %shard_map.56.white_ref.refs_0_, f32[2,2,1024]{2,1,0:T(2,128)S(1)} %copy-done.1, bf16[4,1024,512]{2,1,0:T(8,128)(2,1)S(1)} %shard_map.58.refs_2_), custom_call_target="tpu_custom_call" | custom-call | flops 8 | bytes 8 | tf_op jit(solution)/shard_map/pallas_call | solution.py:248
  14.1 0.0 collective-permute-done.3.white_ref
  14.1 0.1 shard_map.60.base_ref
  14.3 3.2 %collective-permute-done.2.refs_0_ = bf16[8,2,8,1024]{3,2,1,0:T(8,128)(2,1)S(1)} collective-permute-done((bf16[8,2,8,1024]{3,2,1,0:T(8,128)(2,1)S(1)}, bf16[8,2,8,1024]{3,2,1,0:T(8,128)(2,1)S(1)}, u32[]{:S(2)}, u32[]{:S(2)}) %collective-permute-start.2) | collective-permute-done | bytes 262176 | tf_op jit(solution)/shard_map/ppermute | solution.py:26
  17.5 1.6 %shard_map.62 = (f32[1,2,64,256]{3,2,1,0:T(8,128)S(1)}, f32[1,2,64,256]{3,2,1,0:T(8,128)S(1)}) custom-call(f32[8,2,8,1024]{3,2,1,0:T(8,128)S(1)} %shard_map.60.base_ref, bf16[8,2,8,1024]{3,2,1,0:T(8,128)(2,1)S(1)} %collective-permute-done.2.refs_0_, f32[2,2,1024]{2,1,0:T(2,128)S(1)} %copy-done.1, bf16[4,1024,512]{2,1,0:T(8,128)(2,1)S(1)} %shard_map.58.refs_2_), custom_call_target="tpu_custom_call" | custom-call | flops 8 | bytes 8 | tf_op jit(solution)/shard_map/pallas_call | solution.py:248
  19.1 1.6 %shard_map.61 = (f32[2,2,64,256]{3,2,1,0:T(8,128)S(1)}, f32[2,2,64,256]{3,2,1,0:T(8,128)S(1)}) custom-call(f32[8,2,8,1024]{3,2,1,0:T(8,128)S(1)} %shard_map.57.base_ref, bf16[8,2,8,1024]{3,2,1,0:T(8,128)(2,1)S(1)} %collective-permute-done.2.refs_0_, f32[2,2,1024]{2,1,0:T(2,128)S(1)} %copy-done.1, bf16[4,1024,512]{2,1,0:T(8,128)(2,1)S(1)} %shard_map.58.refs_2_, ...), custom_call_target="tpu_custom_call" | custom-call | flops 8 | bytes 8 | tf_op jit(solution)/shard_map/pallas_call | solution.py:248
  20.7 0.0 copy-start.3
  20.7 0.0 collective-permute-done.1.refs_0_
  20.7 0.1 collective-permute-start.4
  20.8 1.6 %shard_map.64 = (f32[2,2,64,256]{3,2,1,0:T(8,128)S(1)}, f32[2,2,64,256]{3,2,1,0:T(8,128)S(1)}) custom-call(f32[8,2,8,1024]{3,2,1,0:T(8,128)S(1)} %shard_map.60.base_ref, bf16[8,2,8,1024]{3,2,1,0:T(8,128)(2,1)S(1)} %collective-permute-done.1.refs_0_, f32[2,2,1024]{2,1,0:T(2,128)S(1)} %copy-done.1, bf16[4,1024,512]{2,1,0:T(8,128)(2,1)S(1)} %shard_map.58.refs_2_, ...), custom_call_target="tpu_custom_call" | custom-call | flops 8 | bytes 8 | tf_op jit(solution)/shard_map/pallas_call | solution.py:248
  22.4 0.6 %collective-permute-start.6 = (f32[2,2,64,256]{3,2,1,0:T(8,128)S(1)}, f32[2,2,64,256]{3,2,1,0:T(8,128)S(1)}, u32[]{:S(2)}, u32[]{:S(2)}) collective-permute-start(f32[2,2,64,256]{3,2,1,0:T(8,128)S(1)} %get-tuple-element.54), channel_id=1, source_target_pairs={{0,1},{1,0},{2,3},{3,2},{4,5},{5,4},{6,7},{7,6},{8,9},{9,8},{10,11... | collective-permute-start | bytes 786440 | tf_op jit(solution)/shard_map/ppermute | solution.py:264
  22.9 0.0 collective-permute-done.4.refs_1_
  23.0 1.6 %collective-permute-start.5 = (bf16[2,64,256]{2,1,0:T(8,128)(2,1)S(1)}, bf16[2,64,256]{2,1,0:T(8,128)(2,1)S(1)}, u32[]{:S(2)}, u32[]{:S(2)}) collective-permute-start(bf16[2,64,256]{2,1,0:T(8,128)(2,1)S(1)} %get-tuple-element.49), channel_id=1, source_target_pairs={{0,2},{2,0},{1,3},{3,1},{4,6},{6,4},{5,7},{7,5},{8,10},{10,8},{9,1... | collective-permute-start | bytes 196616 | tf_op jit(solution)/shard_map/ppermute | solution.py:264
  24.5 0.0 collective-permute-done.6.refs_1_
  24.5 1.3 %collective-permute-start.7 = (bf16[2,64,256]{2,1,0:T(8,128)(2,1)S(1)}, bf16[2,64,256]{2,1,0:T(8,128)(2,1)S(1)}, u32[]{:S(2)}, u32[]{:S(2)}) collective-permute-start(bf16[2,64,256]{2,1,0:T(8,128)(2,1)S(1)} %get-tuple-element.55), channel_id=1, source_target_pairs={{4,0},{8,4},{12,8},{5,1},{9,5},{13,9},{6,2},{10,6},{14,10},{7,3},{... | collective-permute-start | bytes 196616 | tf_op jit(solution)/shard_map/ppermute | solution.py:26
  25.8 1.3 %collective-permute-start.8 = (bf16[2,64,256]{2,1,0:T(8,128)(2,1)S(1)}, bf16[2,64,256]{2,1,0:T(8,128)(2,1)S(1)}, u32[]{:S(2)}, u32[]{:S(2)}) collective-permute-start(bf16[2,64,256]{2,1,0:T(8,128)(2,1)S(1)} %get-tuple-element.56), channel_id=1, source_target_pairs={{4,2},{6,0},{8,6},{10,4},{12,10},{14,8},{5,3},{7,1},{9,7},{11,5},{... | collective-permute-start | bytes 196616 | tf_op jit(solution)/shard_map/ppermute | solution.py:316
  27.1 0.0 copy-done.3
  27.2 0.1 broadcast_in_dim.4
  27.2 0.1 broadcast_in_dim_reshape.4.factor_ref
  27.3 0.0 collective-permute-done.5.refs_1_
  27.3 6.3 %collective-permute-done.7.refs_2_ = bf16[2,64,256]{2,1,0:T(8,128)(2,1)S(1)} collective-permute-done((bf16[2,64,256]{2,1,0:T(8,128)(2,1)S(1)}, bf16[2,64,256]{2,1,0:T(8,128)(2,1)S(1)}, u32[]{:S(2)}, u32[]{:S(2)}) %collective-permute-start.7) | collective-permute-done | bytes 65568 | tf_op jit(solution)/shard_map/ppermute | solution.py:26
  33.6 2.8 %collective-permute-done.8.refs_3_ = bf16[2,64,256]{2,1,0:T(8,128)(2,1)S(1)} collective-permute-done((bf16[2,64,256]{2,1,0:T(8,128)(2,1)S(1)}, bf16[2,64,256]{2,1,0:T(8,128)(2,1)S(1)}, u32[]{:S(2)}, u32[]{:S(2)}) %collective-permute-start.8) | collective-permute-done | bytes 65568 | tf_op jit(solution)/shard_map/ppermute | solution.py:316
  36.4 0.9 %shard_map.66 = f32[8,4,8,256]{3,2,1,0:T(8,128)} custom-call(f32[4,64,1]{2,1,0:T(8,128)S(1)} %broadcast_in_dim_reshape.4.factor_ref, f32[2,64,256]{2,1,0:T(8,128)S(1)} %get-tuple-element.48.refs_0_, bf16[2,64,256]{2,1,0:T(8,128)(2,1)S(1)} %collective-permute-done.5.refs_1_, bf16[2,64,256]{2,1,0:T(8,128)(2,1)S(1)} %collective-permute-done.7.refs_2_, ...), custom_call_target="tpu_custom_call" | custom-call | tf_op jit(solution)/shard_map/pallas_call | solution.py:319
  (3 shorter events, 0.1 us)
Async XLA Ops:
  0.0 12.5 %copy-start.1 = (f32[2,2,1024]{2,1,0:T(2,128)S(1)}, f32[2,2,1024]{2,1,0:T(2,128)}, u32[]{:S(2)}) copy-start(f32[2,2,1024]{2,1,0:T(2,128)} %constant.6.clone.refs_1_) | copy-start | bytes 49156
  0.0 1.0 %copy-start.2 = (bf16[8,2,8,1024]{3,2,1,0:T(8,128)(2,1)S(1)}, bf16[8,2,8,1024]{3,2,1,0:T(8,128)(2,1)}, u32[]{:S(2)}) copy-start(bf16[8,2,8,1024]{3,2,1,0:T(8,128)(2,1)} %x_ref.1) | copy-start | bytes 786436
  1.1 1.3 %collective-permute-start = (f32[8,8,1]{2,1,0:T(8,128)S(1)}, f32[8,8,1]{2,1,0:T(8,128)S(1)}, u32[]{:S(2)}, u32[]{:S(2)}) collective-permute-start(f32[8,8,1]{2,1,0:T(8,128)S(1)} %get-tuple-element.32), channel_id=1, source_target_pairs={{0,1},{1,0},{2,3},{3,2},{4,5},{5,4},{6,7},{7,6},{8,9},{9,8},{10,11... | collective-permute-start | bytes 776 | tf_op jit(solution)/shard_map/ppermute | solution.py:225
  2.7 11.5 %collective-permute-start.3 = (bf16[8,2,8,1024]{3,2,1,0:T(8,128)(2,1)S(1)}, bf16[8,2,8,1024]{3,2,1,0:T(8,128)(2,1)S(1)}, u32[]{:S(2)}, u32[]{:S(2)}) collective-permute-start(bf16[8,2,8,1024]{3,2,1,0:T(8,128)(2,1)S(1)} %shard_map.56.white_ref.refs_0_), channel_id=1, source_target_pairs={{0,4},{4,8},{8,12},{1,5},{5,9},{9,13},{2,6},{6,10},{10,14},{3,7},{... | collective-permute-start | bytes 786440 | tf_op jit(solution)/shard_map/ppermute | solution.py:26
  7.5 10.0 %collective-permute-start.2 = (bf16[8,2,8,1024]{3,2,1,0:T(8,128)(2,1)S(1)}, bf16[8,2,8,1024]{3,2,1,0:T(8,128)(2,1)S(1)}, u32[]{:S(2)}, u32[]{:S(2)}) collective-permute-start(bf16[8,2,8,1024]{3,2,1,0:T(8,128)(2,1)S(1)} %shard_map.56.white_ref.refs_0_), channel_id=1, source_target_pairs={{4,0},{8,4},{12,8},{5,1},{9,5},{13,9},{6,2},{10,6},{14,10},{7,3},{... | collective-permute-start | bytes 786440 | tf_op jit(solution)/shard_map/ppermute | solution.py:26
  8.8 11.9 %collective-permute-start.1 = (bf16[8,2,8,1024]{3,2,1,0:T(8,128)(2,1)S(1)}, bf16[8,2,8,1024]{3,2,1,0:T(8,128)(2,1)S(1)}, u32[]{:S(2)}, u32[]{:S(2)}) collective-permute-start(bf16[8,2,8,1024]{3,2,1,0:T(8,128)(2,1)S(1)} %shard_map.56.white_ref.refs_0_), channel_id=1, source_target_pairs={{12,4},{13,5},{14,6},{15,7},{28,20},{29,21},{30,22},{31,23}} | collective-permute-start | bytes 786440 | tf_op jit(solution)/shard_map/ppermute | solution.py:288
  10.2 1.0 %copy-start = (f32[2,96,512]{2,1,0:T(8,128)S(1)}, f32[2,96,512]{2,1,0:T(8,128)}, u32[]{:S(2)}) copy-start(f32[2,96,512]{2,1,0:T(8,128)} %constant.7.clone.base_ref) | copy-start | bytes 1179652
  20.7 6.5 %copy-start.3 = (s32[8,4]{0,1:T(4,128)S(1)}, s32[8,4]{0,1:T(4,128)}, u32[]{:S(2)}) copy-start(s32[8,4]{0,1:T(4,128)} %param.7) | copy-start | bytes 388
  20.7 2.2 %collective-permute-start.4 = (f32[2,2,64,256]{3,2,1,0:T(8,128)S(1)}, f32[2,2,64,256]{3,2,1,0:T(8,128)S(1)}, u32[]{:S(2)}, u32[]{:S(2)}) collective-permute-start(f32[2,2,64,256]{3,2,1,0:T(8,128)S(1)} %get-tuple-element.47), channel_id=1, source_target_pairs={{0,1},{1,0},{2,3},{3,2},{4,5},{5,4},{6,7},{7,6},{8,9},{9,8},{10,11... | collective-permute-start | bytes 786440 | tf_op jit(solution)/shard_map/ppermute | solution.py:264
  22.4 2.1 %collective-permute-start.6 = (f32[2,2,64,256]{3,2,1,0:T(8,128)S(1)}, f32[2,2,64,256]{3,2,1,0:T(8,128)S(1)}, u32[]{:S(2)}, u32[]{:S(2)}) collective-permute-start(f32[2,2,64,256]{3,2,1,0:T(8,128)S(1)} %get-tuple-element.54), channel_id=1, source_target_pairs={{0,1},{1,0},{2,3},{3,2},{4,5},{5,4},{6,7},{7,6},{8,9},{9,8},{10,11... | collective-permute-start | bytes 786440 | tf_op jit(solution)/shard_map/ppermute | solution.py:264
  23.0 4.4 %collective-permute-start.5 = (bf16[2,64,256]{2,1,0:T(8,128)(2,1)S(1)}, bf16[2,64,256]{2,1,0:T(8,128)(2,1)S(1)}, u32[]{:S(2)}, u32[]{:S(2)}) collective-permute-start(bf16[2,64,256]{2,1,0:T(8,128)(2,1)S(1)} %get-tuple-element.49), channel_id=1, source_target_pairs={{0,2},{2,0},{1,3},{3,1},{4,6},{6,4},{5,7},{7,5},{8,10},{10,8},{9,1... | collective-permute-start | bytes 196616 | tf_op jit(solution)/shard_map/ppermute | solution.py:264
  24.5 9.1 %collective-permute-start.7 = (bf16[2,64,256]{2,1,0:T(8,128)(2,1)S(1)}, bf16[2,64,256]{2,1,0:T(8,128)(2,1)S(1)}, u32[]{:S(2)}, u32[]{:S(2)}) collective-permute-start(bf16[2,64,256]{2,1,0:T(8,128)(2,1)S(1)} %get-tuple-element.55), channel_id=1, source_target_pairs={{4,0},{8,4},{12,8},{5,1},{9,5},{13,9},{6,2},{10,6},{14,10},{7,3},{... | collective-permute-start | bytes 196616 | tf_op jit(solution)/shard_map/ppermute | solution.py:26
  25.8 10.6 %collective-permute-start.8 = (bf16[2,64,256]{2,1,0:T(8,128)(2,1)S(1)}, bf16[2,64,256]{2,1,0:T(8,128)(2,1)S(1)}, u32[]{:S(2)}, u32[]{:S(2)}) collective-permute-start(bf16[2,64,256]{2,1,0:T(8,128)(2,1)S(1)} %get-tuple-element.56), channel_id=1, source_target_pairs={{4,2},{6,0},{8,6},{10,4},{12,10},{14,8},{5,3},{7,1},{9,7},{11,5},{... | collective-permute-start | bytes 196616 | tf_op jit(solution)/shard_map/ppermute | solution.py:316

commit v13 on v12

--- a/solution.py
+++ b/solution.py
@@ -47,6 +47,11 @@
         x = x_ref[w]
         power_ref[w] = bin_power(x)
         copy_ref[w] = x
+
+
+def partial_kernel(x_ref, power_ref):
+    for w in range(x_ref.shape[0]):
+        power_ref[w] = bin_power(x_ref[w])
 
 
 def whiten_kernel(n_bins, x_ref, *refs):
@@ -211,6 +216,11 @@
     def cost(flops, size):
         return pl.CostEstimate(flops=flops, bytes_accessed=size, transcendentals=0)
 
+    below = from_behind(spectra, "chan", -1)
+    far = []
+    for distance in range(2, reach):
+        route = [(c + distance, c) for c in range(1, n_chan - distance)]
+        far.append(lax.ppermute(spectra, "chan", route))
     power, copied = pl.pallas_call(
         power_kernel,
         out_shape=[
@@ -219,13 +229,19 @@
         ],
         in_specs=[VMEM], out_specs=[VMEM] * 2, compiler_params=params, cost_estimate=cost(ch, ch),
     )(spectra)
-    own_power = []
-    for turn in range(1, n_freq):
-        route = [(f, (f + turn) % n_freq) for f in range(n_freq)]
-        own_power.append(lax.ppermute(power, "freq", route))
-
     twist = phases(F_LO + np.arange(n_bins), np.ones(1)).reshape(2, n_freq, f_dev)
     twist = jnp.asarray(np.moveaxis(twist, 0, 1))
+
+    def swap(power):
+        routes = [[(f, (f + turn) % n_freq) for f in range(n_freq)] for turn in range(1, n_freq)]
+        return [lax.ppermute(power, "freq", route) for route in routes]
+
+    def half_power(block):
+        return pl.pallas_call(
+            partial_kernel,
+            out_shape=jax.ShapeDtypeStruct(power.shape, jnp.float32),
+            in_specs=[VMEM], out_specs=VMEM, compiler_params=params, cost_estimate=cost(ch, ch),
+        )(block)
 
     def whiten(block, others):
         return pl.pallas_call(
@@ -279,13 +295,8 @@
             in_specs=[VMEM] * (n_freq + len(before)), out_specs=[VMEM] * n_win, compiler_params=params,
         )(*turns(parts, "freq", n_freq), *before)
 
-    white = whiten(copied, own_power)
+    white = whiten(copied, swap(power))
     above = from_behind(white, "chan", 1)
-    below = from_behind(white, "chan", -1)
-    far = []
-    for distance in range(2, reach):
-        route = [(c + distance, c) for c in range(1, n_chan - distance)]
-        far.append(lax.ppermute(white, "chan", route))
     half_lags = 2 * np.arange(LAGS // 2) + 1
     coarse = phases(np.arange(0, n_bins, FINE), half_lags)
     fine = phases(F_LO + np.arange(FINE), half_lags)
@@ -297,14 +308,19 @@
     )(ends)
     own = kept(white)
     first = pairs(own, [white])
-    above, first = lax.optimization_barrier((above, first))
+    below, first = lax.optimization_barrier((below, first))
+    below = whiten(below, swap(half_power(below)))
+    parts = pairs(own, [below], first)
+    far, parts = lax.optimization_barrier((far, parts))
+    halves = [half_power(block) for block in far]
+    above, halves = lax.optimization_barrier((above, halves))
+    others = [swap(half) for half in halves]
     base = kept(above)
-    below, base = lax.optimization_barrier((below, base))
-    parts = pairs(own, [below], first)
-    before = ()
-    for block in [below] + far[:-1]:
-        before = pairs(base, [block], before)
-    far, parts, before = lax.optimization_barrier((far[-1], parts, before))
+    before = pairs(base, [below])
+    for block, power in zip(far[:-1], others[:-1]):
+        before = pairs(base, [whiten(block, power)], before)
+    others, before = lax.optimization_barrier((others, before))
+    far = whiten(far[-1], others[-1])
     sums = split_windows(parts, [], [jnp.float32] + [jnp.bfloat16] * (n_win - 1))
     shipped = split_windows(pairs(base, [far], before), [], [jnp.bfloat16] * n_win)
     received = turns(sums, "win", n_win)

time: 37.6 us -> 34.1 us (0.907)
  waiting for transfers between devices: 13.2 us -> 7.14 us
  starting transfers between devices: 12 us -> 13.8 us
  Pallas kernels: 9.03 us -> 10.7 us
  local copies, waits for them, and re-layouts: 2.21 us -> 1.24 us
    ppermute x3, waiting for transfers between devices: 9.53 us -> 1.69 us  [from_behind(): return lax.ppermute(block, axis, route)]
    ppermute x1, waiting for transfers between devices: 2.81 us -> 4.25 us  [local(): received.append(lax.ppermute(shipped[turn], ('chan', 'win'), route))]
    unnamed x8 -> x6, local copies, waits for them, and re-layouts: 1.97 us -> 1.01 us
    pallas_call x1, Pallas kernels: 0.14 us -> 1.09 us  [local(): pl.pallas_call(power_kernel, out_shape=[jax.ShapeDtypeStruct((w_dev, ch,...]
    ppermute x3, starting transfers between devices: 7.42 us -> 8.3 us  [from_behind(): return lax.ppermute(block, axis, route)]
    ppermute x2 -> x4, starting transfers between devices: 1.14 us -> 1.62 us  [the longest x3 0.95 us: swap(): return [lax.ppermute(power, 'freq', route) for route in routes]]
    pallas_call x1 -> x3, Pallas kernels: 0.23 us -> 0.69 us  [whiten(): pl.pallas_call(functools.partial(whiten_kernel, n_bins), out_shape=jax.Sh...]
    ppermute x3, starting transfers between devices: 2.18 us -> 2.62 us  [turns(): received.append(lax.ppermute(parts[turn], axis, route))]
  transfers between devices with their start and end apart: 9 -> 11, of which waited for: 4 -> 4; matrix products, arithmetic and copies ran while one was open for 2% -> 3% of each run, Pallas kernels for 21% -> 29%
where the time goes in v13:
time: 34.1 us; the launch traced here: 33.8 us
  starting transfers between devices  13.8 us (40%)
  Pallas kernels  10.7 us (31%)
  waiting for transfers between devices  7.14 us (21%)
  local copies, waits for them, and re-layouts  1.24 us (4%)
  other arithmetic  0.66 us (2%)
    ppermute x3, starting transfers between devices, from_behind(): return lax.ppermute(block, axis, route)  8.3 us
    pallas_call x4, Pallas kernels, pairs(): pl.pallas_call(functools.partial(pairs_kernel, len(partners), n_win, n_fr...  6.32 us
    ppermute x1, waiting for transfers between devices, local(): received.append(lax.ppermute(shipped[turn], ('chan', 'win'), route))  4.25 us
    ppermute x3, starting transfers between devices, turns(): received.append(lax.ppermute(parts[turn], axis, route))  2.62 us
    ppermute x3, waiting for transfers between devices, from_behind(): return lax.ppermute(block, axis, route)  1.69 us
    ppermute x1, starting transfers between devices, local(): received.append(lax.ppermute(shipped[turn], ('chan', 'win'), route))  1.29 us
    pallas_call x1, Pallas kernels, local(): pl.pallas_call(table_kernel, out_shape=jax.ShapeDtypeStruct((4, f_dev, LA...  1.19 us
    ppermute x3, waiting for transfers between devices, swap(): return [lax.ppermute(power, 'freq', route) for route in routes]  1.19 us
  transfers between devices with their start and end apart: 11, of which 4 were waited for; matrix products, arithmetic and copies ran while one was open for 3% of the time, Pallas kernels for 29%

profile of v13, /device:TPU:0, one launch (start us, length us, event | category | flops | bytes accessed | tf_op | source)
XLA Modules:
  0.0 33.8 jit_solution(13595318471827343680)
XLA Ops:
  0.0 0.0 copy-start.1
  0.0 1.4 %collective-permute-start.2 = (bf16[8,2,8,1024]{3,2,1,0:T(8,128)(2,1)}, bf16[8,2,8,1024]{3,2,1,0:T(8,128)(2,1)S(1)}, u32[]{:S(2)}, u32[]{:S(2)}) collective-permute-start(bf16[8,2,8,1024]{3,2,1,0:T(8,128)(2,1)} %x_ref.1), channel_id=1, source_target_pairs={{4,0},{8,4},{12,8},{5,1},{9,5},{13,9},{6,2},{10,6},{14,10},{7,3},{... | collective-permute-start | bytes 786440 | tf_op jit(solution)/shard_map/ppermute | solution.py:26
  1.4 1.1 %shard_map.55 = (f32[8,8,1]{2,1,0:T(8,128)S(1)}, bf16[8,2,8,1024]{3,2,1,0:T(8,128)(2,1)S(1)}) custom-call(bf16[8,2,8,1024]{3,2,1,0:T(8,128)(2,1)} %x_ref.1), custom_call_target="tpu_custom_call" | custom-call | flops 8 | bytes 8 | tf_op jit(solution)/shard_map/pallas_call | solution.py:224
  2.5 0.5 %collective-permute-start.1 = (f32[8,8,1]{2,1,0:T(8,128)S(1)}, f32[8,8,1]{2,1,0:T(8,128)S(1)}, u32[]{:S(2)}, u32[]{:S(2)}) collective-permute-start(f32[8,8,1]{2,1,0:T(8,128)S(1)} %get-tuple-element.33), channel_id=1, source_target_pairs={{0,1},{1,0},{2,3},{3,2},{4,5},{5,4},{6,7},{7,6},{8,9},{9,8},{10,11... | collective-permute-start | bytes 776 | tf_op jit(solution)/shard_map/ppermute | solution.py:237
  3.0 0.7 %collective-permute-start = (bf16[8,2,8,1024]{3,2,1,0:T(8,128)(2,1)}, bf16[8,2,8,1024]{3,2,1,0:T(8,128)(2,1)S(1)}, u32[]{:S(2)}, u32[]{:S(2)}) collective-permute-start(bf16[8,2,8,1024]{3,2,1,0:T(8,128)(2,1)} %x_ref.1), channel_id=1, source_target_pairs={{12,4},{13,5},{14,6},{15,7},{28,20},{29,21},{30,22},{31,23}} | collective-permute-start | bytes 786440 | tf_op jit(solution)/shard_map/ppermute | solution.py:223
  3.7 0.2 collective-permute-done.1.refs_0_
  3.8 0.2 shard_map.56.white_ref.refs_0_
  4.1 5.6 %collective-permute-start.6 = (bf16[8,2,8,1024]{3,2,1,0:T(8,128)(2,1)S(1)}, bf16[8,2,8,1024]{3,2,1,0:T(8,128)(2,1)S(1)}, u32[]{:S(2)}, u32[]{:S(2)}) collective-permute-start(bf16[8,2,8,1024]{3,2,1,0:T(8,128)(2,1)S(1)} %shard_map.56.white_ref.refs_0_), channel_id=1, source_target_pairs={{0,4},{4,8},{8,12},{1,5},{5,9},{9,13},{2,6},{6,10},{10,14},{3,7},{... | collective-permute-start | bytes 786440 | tf_op jit(solution)/shard_map/ppermute | solution.py:26
  9.7 0.7 %convert_element_type.8 = f32[8]{0:T(128)S(1)} convert(s32[8]{0:T(128)} %param.6) | non-fusion elementwise | flops 8 | bytes 64 | tf_op jit(solution)/shard_map/convert_element_type | solution.py:253
  10.3 0.0 copy-start
  10.3 1.0 %copy-done = f32[2,96,512]{2,1,0:T(8,128)S(1)} copy-done((f32[2,96,512]{2,1,0:T(8,128)S(1)}, f32[2,96,512]{2,1,0:T(8,128)}, u32[]{:S(2)}) %copy-start) | copy-done | bytes 393240
  11.3 1.2 %shard_map.58.refs_2_ = bf16[4,1024,512]{2,1,0:T(8,128)(2,1)S(1)} custom-call(f32[2,96,512]{2,1,0:T(8,128)S(1)} %copy-done), custom_call_target="tpu_custom_call" | custom-call | flops 8 | bytes 8 | tf_op jit(solution)/shard_map/pallas_call | solution.py:304
  12.5 0.1 broadcast_in_dim.10.keep_ref
  12.6 0.1 shard_map.57.base_ref
  12.7 0.0 copy-done.1
  12.7 1.6 %shard_map.59 = (f32[1,2,64,256]{3,2,1,0:T(8,128)S(1)}, f32[1,2,64,256]{3,2,1,0:T(8,128)S(1)}) custom-call(f32[8,2,8,1024]{3,2,1,0:T(8,128)S(1)} %shard_map.57.base_ref, bf16[8,2,8,1024]{3,2,1,0:T(8,128)(2,1)S(1)} %shard_map.56.white_ref.refs_0_, f32[2,2,1024]{2,1,0:T(2,128)S(1)} %copy-done.1, bf16[4,1024,512]{2,1,0:T(8,128)(2,1)S(1)} %shard_map.58.refs_2_), custom_call_target="tpu_custom_call" | custom-call | flops 8 | bytes 8 | tf_op jit(solution)/shard_map/pallas_call | solution.py:264
  14.3 0.0 collective-permute-done.2.x_ref
  14.3 0.1 shard_map.60
  14.5 0.2 collective-permute-start.3
  14.7 1.0 %collective-permute-done.3.refs_0_ = f32[8,8,1]{2,1,0:T(8,128)S(1)} collective-permute-done((f32[8,8,1]{2,1,0:T(8,128)S(1)}, f32[8,8,1]{2,1,0:T(8,128)S(1)}, u32[]{:S(2)}, u32[]{:S(2)}) %collective-permute-start.3) | collective-permute-done | bytes 288 | tf_op jit(solution)/shard_map/ppermute | solution.py:237
  15.7 0.2 shard_map.61.refs_0_
  15.9 1.6 %shard_map.62 = (f32[2,2,64,256]{3,2,1,0:T(8,128)S(1)}, f32[2,2,64,256]{3,2,1,0:T(8,128)S(1)}) custom-call(f32[8,2,8,1024]{3,2,1,0:T(8,128)S(1)} %shard_map.57.base_ref, bf16[8,2,8,1024]{3,2,1,0:T(8,128)(2,1)S(1)} %shard_map.61.refs_0_, f32[2,2,1024]{2,1,0:T(2,128)S(1)} %copy-done.1, bf16[4,1024,512]{2,1,0:T(8,128)(2,1)S(1)} %shard_map.58.refs_2_, ...), custom_call_target="tpu_custom_call" | custom-call | flops 8 | bytes 8 | tf_op jit(solution)/shard_map/pallas_call | solution.py:264
  17.5 0.0 collective-permute-done.x_ref
  17.5 0.1 shard_map.64
  17.7 0.0 collective-permute-done.6.white_ref
  17.7 0.3 collective-permute-start.7
  17.9 0.1 shard_map.65.base_ref
  18.0 1.6 %shard_map.66 = (f32[1,2,64,256]{3,2,1,0:T(8,128)S(1)}, f32[1,2,64,256]{3,2,1,0:T(8,128)S(1)}) custom-call(f32[8,2,8,1024]{3,2,1,0:T(8,128)S(1)} %shard_map.65.base_ref, bf16[8,2,8,1024]{3,2,1,0:T(8,128)(2,1)S(1)} %shard_map.61.refs_0_, f32[2,2,1024]{2,1,0:T(2,128)S(1)} %copy-done.1, bf16[4,1024,512]{2,1,0:T(8,128)(2,1)S(1)} %shard_map.58.refs_2_), custom_call_target="tpu_custom_call" | custom-call | flops 8 | bytes 8 | tf_op jit(solution)/shard_map/pallas_call | solution.py:264
  19.6 0.0 copy-start.2
  19.6 0.4 %collective-permute-start.4 = (f32[2,2,64,256]{3,2,1,0:T(8,128)S(1)}, f32[2,2,64,256]{3,2,1,0:T(8,128)S(1)}, u32[]{:S(2)}, u32[]{:S(2)}) collective-permute-start(f32[2,2,64,256]{3,2,1,0:T(8,128)S(1)} %get-tuple-element.44), channel_id=1, source_target_pairs={{0,1},{1,0},{2,3},{3,2},{4,5},{5,4},{6,7},{7,6},{8,9},{9,8},{10,11... | collective-permute-start | bytes 786440 | tf_op jit(solution)/shard_map/ppermute | solution.py:280
  20.0 0.0 collective-permute-done.7.refs_0_
  20.0 0.2 shard_map.67.refs_0_
  20.2 1.6 %shard_map.68 = (f32[2,2,64,256]{3,2,1,0:T(8,128)S(1)}, f32[2,2,64,256]{3,2,1,0:T(8,128)S(1)}) custom-call(f32[8,2,8,1024]{3,2,1,0:T(8,128)S(1)} %shard_map.65.base_ref, bf16[8,2,8,1024]{3,2,1,0:T(8,128)(2,1)S(1)} %shard_map.67.refs_0_, f32[2,2,1024]{2,1,0:T(2,128)S(1)} %copy-done.1, bf16[4,1024,512]{2,1,0:T(8,128)(2,1)S(1)} %shard_map.58.refs_2_, ...), custom_call_target="tpu_custom_call" | custom-call | flops 8 | bytes 8 | tf_op jit(solution)/shard_map/pallas_call | solution.py:264
  21.8 0.3 collective-permute-start.8
  22.1 0.0 collective-permute-done.4.refs_1_
  22.1 2.0 %collective-permute-start.5 = (bf16[2,64,256]{2,1,0:T(8,128)(2,1)S(1)}, bf16[2,64,256]{2,1,0:T(8,128)(2,1)S(1)}, u32[]{:S(2)}, u32[]{:S(2)}) collective-permute-start(bf16[2,64,256]{2,1,0:T(8,128)(2,1)S(1)} %get-tuple-element.46), channel_id=1, source_target_pairs={{0,2},{2,0},{1,3},{3,1},{4,6},{6,4},{5,7},{7,5},{8,10},{10,8},{9,1... | collective-permute-start | bytes 196616 | tf_op jit(solution)/shard_map/ppermute | solution.py:280
  24.1 0.0 collective-permute-done.8.refs_1_
  24.1 1.3 %collective-permute-start.10 = (bf16[2,64,256]{2,1,0:T(8,128)(2,1)S(1)}, bf16[2,64,256]{2,1,0:T(8,128)(2,1)S(1)}, u32[]{:S(2)}, u32[]{:S(2)}) collective-permute-start(bf16[2,64,256]{2,1,0:T(8,128)(2,1)S(1)} %get-tuple-element.58), channel_id=1, source_target_pairs={{4,2},{6,0},{8,6},{10,4},{12,10},{14,8},{5,3},{7,1},{9,7},{11,5},{... | collective-permute-start | bytes 196616 | tf_op jit(solution)/shard_map/ppermute | solution.py:332
  25.4 1.3 %collective-permute-start.9 = (bf16[2,64,256]{2,1,0:T(8,128)(2,1)S(1)}, bf16[2,64,256]{2,1,0:T(8,128)(2,1)S(1)}, u32[]{:S(2)}, u32[]{:S(2)}) collective-permute-start(bf16[2,64,256]{2,1,0:T(8,128)(2,1)S(1)} %get-tuple-element.57), channel_id=1, source_target_pairs={{4,0},{8,4},{12,8},{5,1},{9,5},{13,9},{6,2},{10,6},{14,10},{7,3},{... | collective-permute-start | bytes 196616 | tf_op jit(solution)/shard_map/ppermute | solution.py:26
  26.7 0.0 copy-done.2
  26.8 0.1 broadcast_in_dim.4
  26.8 0.1 broadcast_in_dim_reshape.4.factor_ref
  26.9 0.0 collective-permute-done.5.refs_1_
  27.0 4.3 %collective-permute-done.10.refs_3_ = bf16[2,64,256]{2,1,0:T(8,128)(2,1)S(1)} collective-permute-done((bf16[2,64,256]{2,1,0:T(8,128)(2,1)S(1)}, bf16[2,64,256]{2,1,0:T(8,128)(2,1)S(1)}, u32[]{:S(2)}, u32[]{:S(2)}) %collective-permute-start.10) | collective-permute-done | bytes 65568 | tf_op jit(solution)/shard_map/ppermute | solution.py:332
  31.2 1.7 %collective-permute-done.9.refs_2_ = bf16[2,64,256]{2,1,0:T(8,128)(2,1)S(1)} collective-permute-done((bf16[2,64,256]{2,1,0:T(8,128)(2,1)S(1)}, bf16[2,64,256]{2,1,0:T(8,128)(2,1)S(1)}, u32[]{:S(2)}, u32[]{:S(2)}) %collective-permute-start.9) | collective-permute-done | bytes 65568 | tf_op jit(solution)/shard_map/ppermute | solution.py:26
  32.9 0.9 %shard_map.70 = f32[8,4,8,256]{3,2,1,0:T(8,128)} custom-call(f32[4,64,1]{2,1,0:T(8,128)S(1)} %broadcast_in_dim_reshape.4.factor_ref, f32[2,64,256]{2,1,0:T(8,128)S(1)} %get-tuple-element.45.refs_0_, bf16[2,64,256]{2,1,0:T(8,128)(2,1)S(1)} %collective-permute-done.5.refs_1_, bf16[2,64,256]{2,1,0:T(8,128)(2,1)S(1)} %collective-permute-done.9.refs_2_, ...), custom_call_target="tpu_custom_call" | custom-call | tf_op jit(solution)/shard_map/pallas_call | solution.py:335
  (3 shorter events, 0.1 us)
Async XLA Ops:
  0.0 12.7 %copy-start.1 = (f32[2,2,1024]{2,1,0:T(2,128)S(1)}, f32[2,2,1024]{2,1,0:T(2,128)}, u32[]{:S(2)}) copy-start(f32[2,2,1024]{2,1,0:T(2,128)} %constant.6.clone.refs_1_) | copy-start | bytes 49156
  0.0 14.3 %collective-permute-start.2 = (bf16[8,2,8,1024]{3,2,1,0:T(8,128)(2,1)}, bf16[8,2,8,1024]{3,2,1,0:T(8,128)(2,1)S(1)}, u32[]{:S(2)}, u32[]{:S(2)}) collective-permute-start(bf16[8,2,8,1024]{3,2,1,0:T(8,128)(2,1)} %x_ref.1), channel_id=1, source_target_pairs={{4,0},{8,4},{12,8},{5,1},{9,5},{13,9},{6,2},{10,6},{14,10},{7,3},{... | collective-permute-start | bytes 786440 | tf_op jit(solution)/shard_map/ppermute | solution.py:26
  2.5 1.3 %collective-permute-start.1 = (f32[8,8,1]{2,1,0:T(8,128)S(1)}, f32[8,8,1]{2,1,0:T(8,128)S(1)}, u32[]{:S(2)}, u32[]{:S(2)}) collective-permute-start(f32[8,8,1]{2,1,0:T(8,128)S(1)} %get-tuple-element.33), channel_id=1, source_target_pairs={{0,1},{1,0},{2,3},{3,2},{4,5},{5,4},{6,7},{7,6},{8,9},{9,8},{10,11... | collective-permute-start | bytes 776 | tf_op jit(solution)/shard_map/ppermute | solution.py:237
  3.0 14.5 %collective-permute-start = (bf16[8,2,8,1024]{3,2,1,0:T(8,128)(2,1)}, bf16[8,2,8,1024]{3,2,1,0:T(8,128)(2,1)S(1)}, u32[]{:S(2)}, u32[]{:S(2)}) collective-permute-start(bf16[8,2,8,1024]{3,2,1,0:T(8,128)(2,1)} %x_ref.1), channel_id=1, source_target_pairs={{12,4},{13,5},{14,6},{15,7},{28,20},{29,21},{30,22},{31,23}} | collective-permute-start | bytes 786440 | tf_op jit(solution)/shard_map/ppermute | solution.py:223
  4.1 13.6 %collective-permute-start.6 = (bf16[8,2,8,1024]{3,2,1,0:T(8,128)(2,1)S(1)}, bf16[8,2,8,1024]{3,2,1,0:T(8,128)(2,1)S(1)}, u32[]{:S(2)}, u32[]{:S(2)}) collective-permute-start(bf16[8,2,8,1024]{3,2,1,0:T(8,128)(2,1)S(1)} %shard_map.56.white_ref.refs_0_), channel_id=1, source_target_pairs={{0,4},{4,8},{8,12},{1,5},{5,9},{9,13},{2,6},{6,10},{10,14},{3,7},{... | collective-permute-start | bytes 786440 | tf_op jit(solution)/shard_map/ppermute | solution.py:26
  10.3 1.0 %copy-start = (f32[2,96,512]{2,1,0:T(8,128)S(1)}, f32[2,96,512]{2,1,0:T(8,128)}, u32[]{:S(2)}) copy-start(f32[2,96,512]{2,1,0:T(8,128)} %constant.7.clone.base_ref) | copy-start | bytes 1179652
  14.5 1.2 %collective-permute-start.3 = (f32[8,8,1]{2,1,0:T(8,128)S(1)}, f32[8,8,1]{2,1,0:T(8,128)S(1)}, u32[]{:S(2)}, u32[]{:S(2)}) collective-permute-start(f32[8,8,1]{2,1,0:T(8,128)S(1)} %shard_map.60), channel_id=1, source_target_pairs={{0,1},{1,0},{2,3},{3,2},{4,5},{5,4},{6,7},{7,6},{8,9},{9,8},{10,11... | collective-permute-start | bytes 776 | tf_op jit(solution)/shard_map/ppermute | solution.py:237
  17.7 2.3 %collective-permute-start.7 = (f32[8,8,1]{2,1,0:T(8,128)S(1)}, f32[8,8,1]{2,1,0:T(8,128)S(1)}, u32[]{:S(2)}, u32[]{:S(2)}) collective-permute-start(f32[8,8,1]{2,1,0:T(8,128)S(1)} %shard_map.64), channel_id=1, source_target_pairs={{0,1},{1,0},{2,3},{3,2},{4,5},{5,4},{6,7},{7,6},{8,9},{9,8},{10,11... | collective-permute-start | bytes 776 | tf_op jit(solution)/shard_map/ppermute | solution.py:237
  19.6 7.1 %copy-start.2 = (s32[8,4]{0,1:T(4,128)S(1)}, s32[8,4]{0,1:T(4,128)}, u32[]{:S(2)}) copy-start(s32[8,4]{0,1:T(4,128)} %param.7) | copy-start | bytes 388
  19.6 2.5 %collective-permute-start.4 = (f32[2,2,64,256]{3,2,1,0:T(8,128)S(1)}, f32[2,2,64,256]{3,2,1,0:T(8,128)S(1)}, u32[]{:S(2)}, u32[]{:S(2)}) collective-permute-start(f32[2,2,64,256]{3,2,1,0:T(8,128)S(1)} %get-tuple-element.44), channel_id=1, source_target_pairs={{0,1},{1,0},{2,3},{3,2},{4,5},{5,4},{6,7},{7,6},{8,9},{9,8},{10,11... | collective-permute-start | bytes 786440 | tf_op jit(solution)/shard_map/ppermute | solution.py:280
  21.8 2.3 %collective-permute-start.8 = (f32[2,2,64,256]{3,2,1,0:T(8,128)S(1)}, f32[2,2,64,256]{3,2,1,0:T(8,128)S(1)}, u32[]{:S(2)}, u32[]{:S(2)}) collective-permute-start(f32[2,2,64,256]{3,2,1,0:T(8,128)S(1)} %get-tuple-element.56), channel_id=1, source_target_pairs={{0,1},{1,0},{2,3},{3,2},{4,5},{5,4},{6,7},{7,6},{8,9},{9,8},{10,11... | collective-permute-start | bytes 786440 | tf_op jit(solution)/shard_map/ppermute | solution.py:280
  22.1 4.8 %collective-permute-start.5 = (bf16[2,64,256]{2,1,0:T(8,128)(2,1)S(1)}, bf16[2,64,256]{2,1,0:T(8,128)(2,1)S(1)}, u32[]{:S(2)}, u32[]{:S(2)}) collective-permute-start(bf16[2,64,256]{2,1,0:T(8,128)(2,1)S(1)} %get-tuple-element.46), channel_id=1, source_target_pairs={{0,2},{2,0},{1,3},{3,1},{4,6},{6,4},{5,7},{7,5},{8,10},{10,8},{9,1... | collective-permute-start | bytes 196616 | tf_op jit(solution)/shard_map/ppermute | solution.py:280
  24.1 7.1 %collective-permute-start.10 = (bf16[2,64,256]{2,1,0:T(8,128)(2,1)S(1)}, bf16[2,64,256]{2,1,0:T(8,128)(2,1)S(1)}, u32[]{:S(2)}, u32[]{:S(2)}) collective-permute-start(bf16[2,64,256]{2,1,0:T(8,128)(2,1)S(1)} %get-tuple-element.58), channel_id=1, source_target_pairs={{4,2},{6,0},{8,6},{10,4},{12,10},{14,8},{5,3},{7,1},{9,7},{11,5},{... | collective-permute-start | bytes 196616 | tf_op jit(solution)/shard_map/ppermute | solution.py:332
  25.4 7.4 %collective-permute-start.9 = (bf16[2,64,256]{2,1,0:T(8,128)(2,1)S(1)}, bf16[2,64,256]{2,1,0:T(8,128)(2,1)S(1)}, u32[]{:S(2)}, u32[]{:S(2)}) collective-permute-start(bf16[2,64,256]{2,1,0:T(8,128)(2,1)S(1)} %get-tuple-element.57), channel_id=1, source_target_pairs={{4,0},{8,4},{12,8},{5,1},{9,5},{13,9},{6,2},{10,6},{14,10},{7,3},{... | collective-permute-start | bytes 196616 | tf_op jit(solution)/shard_map/ppermute | solution.py:26

commit v14 on v13

--- a/solution.py
+++ b/solution.py
@@ -54,12 +54,22 @@
         power_ref[w] = bin_power(x_ref[w])
 
 
-def whiten_kernel(n_bins, x_ref, *refs):
+def own_kernel(n_bins, x_ref, *refs):
+    power_ref = refs[-1]
+    for w in range(x_ref.shape[0]):
+        power = bin_power(x_ref[w])
+        for ref in refs[:-2]:
+            power = power + ref[w]
+        power_ref[w] = power
+    whiten_kernel(n_bins, False, x_ref, power_ref, refs[-2])
+
+
+def whiten_kernel(n_bins, add_own, x_ref, *refs):
     out_ref = refs[-1]
     for w in range(x_ref.shape[0]):
-        power = bin_power(x_ref[w])
+        power = bin_power(x_ref[w]) if add_own else None
         for ref in refs[:-1]:
-            power = power + ref[w]
+            power = ref[w] if power is None else power + ref[w]
         scale = lax.rsqrt(power / n_bins + EPS)
         for part in range(2):
             out_ref[w, part] = (x_ref[w, part].astype(jnp.float32) * scale).astype(jnp.bfloat16)
@@ -67,7 +77,7 @@
 
 def keep_kernel(keep_ref, white_ref, out_ref):
     for w in range(white_ref.shape[0]):
-        out_ref[w] = white_ref[w].astype(jnp.float32) * keep_ref[w, :, :, 0:1]
+        out_ref[w] = white_ref[w].astype(jnp.float32) * keep_ref[:, w:w + 1].astype(jnp.float32)[None]
 
 
 def table_kernel(base_ref, table_ref):
@@ -125,34 +135,38 @@
     width = out_refs[0].shape[-1]
     freq, win = lax.axis_index("freq"), lax.axis_index("win")
     dot = functools.partial(jnp.dot, preferred_element_type=jnp.float32)
-    for k, partner_ref in enumerate(partner_refs):
-
-        def body(tile, carry):
-            lanes = pl.ds(pl.multiple_of(tile * LANES, LANES), LANES)
+    count = n_partners * pairs
+
+    def body(tile, carry):
+        lanes = pl.ds(pl.multiple_of(tile * LANES, LANES), LANES)
+        cos = twist_ref[freq, 0:1, lanes]
+        sin = twist_ref[freq, 1:2, lanes]
+        for k, partner_ref in enumerate(partner_refs):
             real, imag = cross_tile(base_ref, partner_ref, lanes)
-            cos = twist_ref[freq, 0:1, lanes]
-            sin = twist_ref[freq, 1:2, lanes]
             for i in range(0, ch, 2):
+                rows = k * pairs + i * ch
                 re = jnp.concatenate(real[i:i + 2], axis=0)
                 im = jnp.concatenate(imag[i:i + 2], axis=0)
                 for part, value in enumerate((re * cos + im * sin, im * cos - re * sin)):
                     high, low = split(value)
-                    rows_ref[part, i * ch:(i + 2) * ch, lanes] = high
-                    rows_ref[part, pairs + i * ch:pairs + (i + 2) * ch, lanes] = low
-            return carry
-
-        lax.fori_loop(0, f_dev // LANES, body, 0)
-        for part in range(2):
-            both = dot(rows_ref[part], table_ref[2 * part])
-            sums_ref[part] = both[:pairs] + both[pairs:] + dot(rows_ref[part, :pairs], table_ref[2 * part + 1])
-        for turn_freq, out_ref in enumerate(out_refs):
-            for turn_win in range(n_win):
-                owner = (win + turn_win) % n_win * n_freq + (freq + turn_freq) % n_freq
-                upper = owner >= groups // 2
-                block = jnp.where(upper, owner - groups // 2, groups // 2 - 1 - owner)
-                sign = jnp.where(upper, -1.0, 1.0)
-                lags = pl.ds(pl.multiple_of(block * width, LANES), width)
-                out_ref[done + k, turn_win] = sums_ref[0, :, lags] + sign * sums_ref[1, :, lags]
+                    rows_ref[part, rows:rows + 2 * ch, lanes] = high
+                    rows_ref[part, count + rows:count + rows + 2 * ch, lanes] = low
+        return carry
+
+    lax.fori_loop(0, f_dev // LANES, body, 0)
+    for part in range(2):
+        both = dot(rows_ref[part], table_ref[2 * part])
+        sums_ref[part] = both[:count] + both[count:] + dot(rows_ref[part, :count], table_ref[2 * part + 1])
+    for turn_freq, out_ref in enumerate(out_refs):
+        for turn_win in range(n_win):
+            owner = (win + turn_win) % n_win * n_freq + (freq + turn_freq) % n_freq
+            upper = owner >= groups // 2
+            block = jnp.where(upper, owner - groups // 2, groups // 2 - 1 - owner)
+            sign = jnp.where(upper, -1.0, 1.0)
+            lags = pl.ds(pl.multiple_of(block * width, LANES), width)
+            for k in range(n_partners):
+                rows = slice(k * pairs, (k + 1) * pairs)
+                out_ref[done + k, turn_win] = sums_ref[0, rows, lags] + sign * sums_ref[1, rows, lags]
 
 
 def add_kernel(n_parts, n_before, *refs):
@@ -217,10 +231,8 @@
         return pl.CostEstimate(flops=flops, bytes_accessed=size, transcendentals=0)
 
     below = from_behind(spectra, "chan", -1)
-    far = []
-    for distance in range(2, reach):
-        route = [(c + distance, c) for c in range(1, n_chan - distance)]
-        far.append(lax.ppermute(spectra, "chan", route))
+    far_routes = [[(c + away, c) for c in range(1, n_chan - away)] for away in range(2, reach)]
+    far = [lax.ppermute(spectra, "chan", route) for route in far_routes]
     power, copied = pl.pallas_call(
         power_kernel,
         out_shape=[
@@ -243,21 +255,19 @@
             in_specs=[VMEM], out_specs=VMEM, compiler_params=params, cost_estimate=cost(ch, ch),
         )(block)
 
-    def whiten(block, others):
-        return pl.pallas_call(
-            functools.partial(whiten_kernel, n_bins),
+    def whiten(block, others, add_own):
+        return pl.pallas_call(
+            functools.partial(whiten_kernel, n_bins, add_own),
             out_shape=jax.ShapeDtypeStruct(block.shape, jnp.bfloat16),
             in_specs=[VMEM] * (1 + len(others)), out_specs=VMEM, compiler_params=params,
         )(block, *others)
 
-    kept_windows = jnp.broadcast_to(keep.astype(jnp.float32)[:, None, None, None], (w_dev, 1, 1, LANES))
-
     def kept(block):
         return pl.pallas_call(
             keep_kernel,
             out_shape=jax.ShapeDtypeStruct(block.shape, jnp.float32),
             in_specs=[VMEM] * 2, out_specs=VMEM, compiler_params=params,
-        )(kept_windows, block)
+        )(keep.reshape(1, w_dev), block)
 
     def pairs(base, partners, before=()):
         n = len(partners) + (before[0].shape[0] if before else 0)
@@ -266,8 +276,8 @@
             out_shape=[jax.ShapeDtypeStruct((n, n_win, ch * ch, width), jnp.float32)] * n_freq,
             in_specs=[VMEM] * (3 + len(partners) + len(before)), out_specs=[VMEM] * n_freq,
             scratch_shapes=[
-                pltpu.VMEM((2, 2 * ch * ch, f_dev), jnp.bfloat16),
-                pltpu.VMEM((2, ch * ch, LAGS // 2), jnp.float32),
+                pltpu.VMEM((2, 2 * len(partners) * ch * ch, f_dev), jnp.bfloat16),
+                pltpu.VMEM((2, len(partners) * ch * ch, LAGS // 2), jnp.float32),
             ],
             compiler_params=params,
             cost_estimate=cost(ch, ch),
@@ -295,34 +305,37 @@
             in_specs=[VMEM] * (n_freq + len(before)), out_specs=[VMEM] * n_win, compiler_params=params,
         )(*turns(parts, "freq", n_freq), *before)
 
-    white = whiten(copied, swap(power))
-    above = from_behind(white, "chan", 1)
+    others = swap(power)
+    white, power = pl.pallas_call(
+        functools.partial(own_kernel, n_bins),
+        out_shape=[
+            jax.ShapeDtypeStruct(spectra.shape, jnp.bfloat16),
+            jax.ShapeDtypeStruct(power.shape, jnp.float32),
+        ],
+        in_specs=[VMEM] * (1 + len(others)), out_specs=[VMEM] * 2, compiler_params=params,
+    )(copied, *others)
+    far_powers = [lax.ppermute(power, "chan", route) for route in far_routes]
     half_lags = 2 * np.arange(LAGS // 2) + 1
     coarse = phases(np.arange(0, n_bins, FINE), half_lags)
     fine = phases(F_LO + np.arange(FINE), half_lags)
-    white, ends = lax.optimization_barrier((white, jnp.asarray(np.concatenate([coarse, fine], axis=1))))
     table = pl.pallas_call(
         table_kernel,
         out_shape=jax.ShapeDtypeStruct((4, f_dev, LAGS // 2), jnp.bfloat16),
         in_specs=[VMEM], out_specs=VMEM, compiler_params=params, cost_estimate=cost(ch, ch),
-    )(ends)
+    )(jnp.asarray(np.concatenate([coarse, fine], axis=1)))
     own = kept(white)
+    white, table, own = lax.optimization_barrier((white, table, own))
+    above = from_behind(white, "chan", 1)
     first = pairs(own, [white])
     below, first = lax.optimization_barrier((below, first))
-    below = whiten(below, swap(half_power(below)))
+    below = whiten(below, swap(half_power(below)), True)
     parts = pairs(own, [below], first)
     far, parts = lax.optimization_barrier((far, parts))
-    halves = [half_power(block) for block in far]
-    above, halves = lax.optimization_barrier((above, halves))
-    others = [swap(half) for half in halves]
+    far = [whiten(block, [power], False) for block, power in zip(far, far_powers)]
+    above, far = lax.optimization_barrier((above, far))
     base = kept(above)
-    before = pairs(base, [below])
-    for block, power in zip(far[:-1], others[:-1]):
-        before = pairs(base, [whiten(block, power)], before)
-    others, before = lax.optimization_barrier((others, before))
-    far = whiten(far[-1], others[-1])
     sums = split_windows(parts, [], [jnp.float32] + [jnp.bfloat16] * (n_win - 1))
-    shipped = split_windows(pairs(base, [far], before), [], [jnp.bfloat16] * n_win)
+    shipped = split_windows(pairs(base, [below] + far), [], [jnp.bfloat16] * n_win)
     received = turns(sums, "win", n_win)
     received.append(from_behind(shipped[0], "chan", -1))
     for turn in range(1, n_win):

time: 34.1 us -> 34.7 us (1.018)
  the two profiles are of different devices: /device:TPU:0 before, /device:TPU:24 now
where the time goes in v14:
time: 34.7 us; the launch traced here: 34.3 us
  starting transfers between devices  16.7 us (48%)
  Pallas kernels  9.87 us (28%)
  waiting for transfers between devices  6.33 us (18%)
  local copies, waits for them, and re-layouts  1.17 us (3%)
    ppermute x3, starting transfers between devices, from_behind(): return lax.ppermute(block, axis, route)  7.44 us
    pallas_call x3, Pallas kernels, pairs(): pl.pallas_call(functools.partial(pairs_kernel, len(partners), n_win, n_fr...  5.67 us
    ppermute x3, waiting for transfers between devices, turns(): received.append(lax.ppermute(parts[turn], axis, route))  3.52 us
    ppermute x1, starting transfers between devices, local(): far_powers = [lax.ppermute(power, 'chan', route) for route in far_routes]  3.28 us
    ppermute x1, starting transfers between devices, local(): received.append(lax.ppermute(shipped[turn], ('chan', 'win'), route))  2.82 us
    ppermute x3, waiting for transfers between devices, from_behind(): return lax.ppermute(block, axis, route)  2.8 us
    ppermute x1, starting transfers between devices, local(): far = [lax.ppermute(spectra, 'chan', route) for route in far_routes]  1.78 us
    pallas_call x1, Pallas kernels, local(): pl.pallas_call(table_kernel, out_shape=jax.ShapeDtypeStruct((4, f_dev, LA...  1.19 us
  transfers between devices with their start and end apart: 11, of which 4 were waited for; matrix products, arithmetic and copies ran while one was open for 1% of the time, Pallas kernels for 19%

profile of v14, /device:TPU:24, one launch (start us, length us, event | category | flops | bytes accessed | tf_op | source)
XLA Modules:
  0.0 34.3 jit_solution(5047272225586280851)
XLA Ops:
  0.0 0.0 copy-start.1
  0.0 0.0 copy-start.2
  0.0 2.5 %collective-permute-start.2 = (bf16[8,2,8,1024]{3,2,1,0:T(8,128)(2,1)}, bf16[8,2,8,1024]{3,2,1,0:T(8,128)(2,1)S(1)}, u32[]{:S(2)}, u32[]{:S(2)}) collective-permute-start(bf16[8,2,8,1024]{3,2,1,0:T(8,128)(2,1)} %x_ref.1), channel_id=1, source_target_pairs={{4,0},{8,4},{12,8},{5,1},{9,5},{13,9},{6,2},{10,6},{14,10},{7,3},{... | collective-permute-start | bytes 786440 | tf_op jit(solution)/shard_map/ppermute | solution.py:26
  2.5 1.1 %shard_map.55 = (f32[8,8,1]{2,1,0:T(8,128)S(1)}, bf16[8,2,8,1024]{3,2,1,0:T(8,128)(2,1)S(1)}) custom-call(bf16[8,2,8,1024]{3,2,1,0:T(8,128)(2,1)} %x_ref.1), custom_call_target="tpu_custom_call" | custom-call | flops 8 | bytes 8 | tf_op jit(solution)/shard_map/pallas_call | solution.py:236
  3.6 0.0 collective-permute-start.1
  3.7 1.8 %collective-permute-start = (bf16[8,2,8,1024]{3,2,1,0:T(8,128)(2,1)}, bf16[8,2,8,1024]{3,2,1,0:T(8,128)(2,1)S(1)}, u32[]{:S(2)}, u32[]{:S(2)}) collective-permute-start(bf16[8,2,8,1024]{3,2,1,0:T(8,128)(2,1)} %x_ref.1), channel_id=1, source_target_pairs={{12,4},{13,5},{14,6},{15,7},{28,20},{29,21},{30,22},{31,23}} | collective-permute-start | bytes 786440 | tf_op jit(solution)/shard_map/ppermute | solution.py:235
  5.4 0.0 copy-start
  5.5 1.0 %copy-done = f32[2,96,512]{2,1,0:T(8,128)S(1)} copy-done((f32[2,96,512]{2,1,0:T(8,128)S(1)}, f32[2,96,512]{2,1,0:T(8,128)}, u32[]{:S(2)}) %copy-start) | copy-done | bytes 393240
  6.4 1.2 %shard_map.57.refs_2_.refs_3_ = bf16[4,1024,512]{2,1,0:T(8,128)(2,1)S(1)} custom-call(f32[2,96,512]{2,1,0:T(8,128)S(1)} %copy-done), custom_call_target="tpu_custom_call" | custom-call | flops 8 | bytes 8 | tf_op jit(solution)/shard_map/pallas_call | solution.py:321
  7.6 0.0 collective-permute-done.1.refs_0_
  7.7 0.2 shard_map.56
  7.9 0.0 copy-done.2
  7.9 0.1 shard_map.58.base_ref
  8.0 1.3 %collective-permute-start.6 = (bf16[8,2,8,1024]{3,2,1,0:T(8,128)(2,1)S(1)}, bf16[8,2,8,1024]{3,2,1,0:T(8,128)(2,1)S(1)}, u32[]{:S(2)}, u32[]{:S(2)}) collective-permute-start(bf16[8,2,8,1024]{3,2,1,0:T(8,128)(2,1)S(1)} %get-tuple-element.34.white_ref.refs_0_), channel_id=1, source_target_pairs={{0,4},{4,8},{8,12},{1,5},{5,9},{9,13},{2,6},{6,10},{10,14},{3,7},{... | collective-permute-start | bytes 786440 | tf_op jit(solution)/shard_map/ppermute | solution.py:26
  9.3 0.0 copy-done.1
  9.3 1.6 %shard_map.59 = (f32[1,2,64,256]{3,2,1,0:T(8,128)S(1)}, f32[1,2,64,256]{3,2,1,0:T(8,128)S(1)}) custom-call(f32[8,2,8,1024]{3,2,1,0:T(8,128)S(1)} %shard_map.58.base_ref, bf16[8,2,8,1024]{3,2,1,0:T(8,128)(2,1)S(1)} %get-tuple-element.34.white_ref.refs_0_, f32[2,2,1024]{2,1,0:T(2,128)S(1)} %copy-done.1, bf16[4,1024,512]{2,1,0:T(8,128)(2,1)S(1)} %shard_map.57.refs_2_.refs_3_), custom_call_target="tpu_custom_call" | custom-call | flops 8 | bytes 8 | tf_op jit(solution)/shard_map/pallas_call | solution.py:274
  10.9 0.0 collective-permute-done.2.x_ref
  10.9 0.1 shard_map.60
  11.1 0.2 collective-permute-start.3
  11.3 3.3 %collective-permute-start.7 = (f32[8,8,1]{2,1,0:T(8,128)S(1)}, f32[8,8,1]{2,1,0:T(8,128)S(1)}, u32[]{:S(2)}, u32[]{:S(2)}) collective-permute-start(f32[8,8,1]{2,1,0:T(8,128)S(1)} %get-tuple-element.48), channel_id=1, source_target_pairs={{12,4},{13,5},{14,6},{15,7},{28,20},{29,21},{30,22},{31,23}} | collective-permute-start | bytes 776 | tf_op jit(solution)/shard_map/ppermute | solution.py:317
  14.6 0.0 collective-permute-done.3.refs_0_
  14.6 0.2 shard_map.61.refs_0_
  14.8 1.6 %shard_map.62 = (f32[2,2,64,256]{3,2,1,0:T(8,128)S(1)}, f32[2,2,64,256]{3,2,1,0:T(8,128)S(1)}) custom-call(f32[8,2,8,1024]{3,2,1,0:T(8,128)S(1)} %shard_map.58.base_ref, bf16[8,2,8,1024]{3,2,1,0:T(8,128)(2,1)S(1)} %shard_map.61.refs_0_, f32[2,2,1024]{2,1,0:T(2,128)S(1)} %copy-done.1, bf16[4,1024,512]{2,1,0:T(8,128)(2,1)S(1)} %shard_map.57.refs_2_.refs_3_, ...), custom_call_target="tpu_custom_call" | custom-call | flops 8 | bytes 8 | tf_op jit(solution)/shard_map/pallas_call | solution.py:274
  16.4 0.0 copy-start.3
  16.4 0.0 collective-permute-done.x_ref
  16.4 0.0 collective-permute-done.7.refs_0_
  16.5 0.1 shard_map.64.refs_1_
  16.6 1.8 %collective-permute-done.6.white_ref = bf16[8,2,8,1024]{3,2,1,0:T(8,128)(2,1)S(1)} collective-permute-done((bf16[8,2,8,1024]{3,2,1,0:T(8,128)(2,1)S(1)}, bf16[8,2,8,1024]{3,2,1,0:T(8,128)(2,1)S(1)}, u32[]{:S(2)}, u32[]{:S(2)}) %collective-permute-start.6) | collective-permute-done | bytes 262176 | tf_op jit(solution)/shard_map/ppermute | solution.py:26
  18.3 0.1 shard_map.65.base_ref
  18.4 2.5 %shard_map.66 = (f32[2,2,64,256]{3,2,1,0:T(8,128)S(1)}, f32[2,2,64,256]{3,2,1,0:T(8,128)S(1)}) custom-call(f32[8,2,8,1024]{3,2,1,0:T(8,128)S(1)} %shard_map.65.base_ref, bf16[8,2,8,1024]{3,2,1,0:T(8,128)(2,1)S(1)} %shard_map.61.refs_0_, bf16[8,2,8,1024]{3,2,1,0:T(8,128)(2,1)S(1)} %shard_map.64.refs_1_, f32[2,2,1024]{2,1,0:T(2,128)S(1)} %copy-done.1, ...), custom_call_target="tpu_custom_call" | custom-call | flops 8 | bytes 8 | tf_op jit(solution)/shard_map/pallas_call | solution.py:274
  21.0 0.1 collective-permute-start.8
  21.0 0.5 %collective-permute-start.4 = (f32[2,2,64,256]{3,2,1,0:T(8,128)S(1)}, f32[2,2,64,256]{3,2,1,0:T(8,128)S(1)}, u32[]{:S(2)}, u32[]{:S(2)}) collective-permute-start(f32[2,2,64,256]{3,2,1,0:T(8,128)S(1)} %get-tuple-element.44), channel_id=1, source_target_pairs={{0,1},{1,0},{2,3},{3,2},{4,5},{5,4},{6,7},{7,6},{8,9},{9,8},{10,11... | collective-permute-start | bytes 786440 | tf_op jit(solution)/shard_map/ppermute | solution.py:290
  21.5 1.0 %collective-permute-done.8.refs_1_ = f32[2,2,64,256]{3,2,1,0:T(8,128)S(1)} collective-permute-done((f32[2,2,64,256]{3,2,1,0:T(8,128)S(1)}, f32[2,2,64,256]{3,2,1,0:T(8,128)S(1)}, u32[]{:S(2)}, u32[]{:S(2)}) %collective-permute-start.8) | collective-permute-done | bytes 262176 | tf_op jit(solution)/shard_map/ppermute | solution.py:290
  22.6 2.8 %collective-permute-start.10 = (bf16[2,64,256]{2,1,0:T(8,128)(2,1)S(1)}, bf16[2,64,256]{2,1,0:T(8,128)(2,1)S(1)}, u32[]{:S(2)}, u32[]{:S(2)}) collective-permute-start(bf16[2,64,256]{2,1,0:T(8,128)(2,1)S(1)} %get-tuple-element.54), channel_id=1, source_target_pairs={{4,2},{6,0},{8,6},{10,4},{12,10},{14,8},{5,3},{7,1},{9,7},{11,5},{... | collective-permute-start | bytes 196616 | tf_op jit(solution)/shard_map/ppermute | solution.py:345
  25.4 3.7 %collective-permute-start.9 = (bf16[2,64,256]{2,1,0:T(8,128)(2,1)S(1)}, bf16[2,64,256]{2,1,0:T(8,128)(2,1)S(1)}, u32[]{:S(2)}, u32[]{:S(2)}) collective-permute-start(bf16[2,64,256]{2,1,0:T(8,128)(2,1)S(1)} %get-tuple-element.53), channel_id=1, source_target_pairs={{4,0},{8,4},{12,8},{5,1},{9,5},{13,9},{6,2},{10,6},{14,10},{7,3},{... | collective-permute-start | bytes 196616 | tf_op jit(solution)/shard_map/ppermute | solution.py:26
  29.1 0.0 collective-permute-done.4.refs_1_
  29.1 0.6 %collective-permute-start.5 = (bf16[2,64,256]{2,1,0:T(8,128)(2,1)S(1)}, bf16[2,64,256]{2,1,0:T(8,128)(2,1)S(1)}, u32[]{:S(2)}, u32[]{:S(2)}) collective-permute-start(bf16[2,64,256]{2,1,0:T(8,128)(2,1)S(1)} %get-tuple-element.46), channel_id=1, source_target_pairs={{0,2},{2,0},{1,3},{3,1},{4,6},{6,4},{5,7},{7,5},{8,10},{10,8},{9,1... | collective-permute-start | bytes 196616 | tf_op jit(solution)/shard_map/ppermute | solution.py:290
  29.7 0.0 copy-done.3
  29.7 0.1 broadcast_in_dim.3
  29.8 0.1 broadcast_in_dim_reshape.4.factor_ref
  29.9 0.0 collective-permute-done.10.refs_3_
  29.9 1.0 %collective-permute-done.9.refs_2_ = bf16[2,64,256]{2,1,0:T(8,128)(2,1)S(1)} collective-permute-done((bf16[2,64,256]{2,1,0:T(8,128)(2,1)S(1)}, bf16[2,64,256]{2,1,0:T(8,128)(2,1)S(1)}, u32[]{:S(2)}, u32[]{:S(2)}) %collective-permute-start.9) | collective-permute-done | bytes 65568 | tf_op jit(solution)/shard_map/ppermute | solution.py:26
  31.0 2.5 %collective-permute-done.5.refs_1_ = bf16[2,64,256]{2,1,0:T(8,128)(2,1)S(1)} collective-permute-done((bf16[2,64,256]{2,1,0:T(8,128)(2,1)S(1)}, bf16[2,64,256]{2,1,0:T(8,128)(2,1)S(1)}, u32[]{:S(2)}, u32[]{:S(2)}) %collective-permute-start.5) | collective-permute-done | bytes 65568 | tf_op jit(solution)/shard_map/ppermute | solution.py:290
  33.5 0.9 %shard_map.68 = f32[8,4,8,256]{3,2,1,0:T(8,128)} custom-call(f32[4,64,1]{2,1,0:T(8,128)S(1)} %broadcast_in_dim_reshape.4.factor_ref, f32[2,64,256]{2,1,0:T(8,128)S(1)} %get-tuple-element.45.refs_0_, bf16[2,64,256]{2,1,0:T(8,128)(2,1)S(1)} %collective-permute-done.5.refs_1_, bf16[2,64,256]{2,1,0:T(8,128)(2,1)S(1)} %collective-permute-done.9.refs_2_, ...), custom_call_target="tpu_custom_call" | custom-call | tf_op jit(solution)/shard_map/pallas_call | solution.py:348
  (3 shorter events, 0.1 us)
Async XLA Ops:
  0.0 9.3 %copy-start.1 = (f32[2,2,1024]{2,1,0:T(2,128)S(1)}, f32[2,2,1024]{2,1,0:T(2,128)}, u32[]{:S(2)}) copy-start(f32[2,2,1024]{2,1,0:T(2,128)} %constant.6.clone.refs_1_.refs_2_) | copy-start | bytes 49156
  0.0 7.9 %copy-start.2 = (s32[8]{0:T(128)S(1)}, s32[8]{0:T(128)}, u32[]{:S(2)}) copy-start(s32[8]{0:T(128)} %param.6) | copy-start | bytes 100
  0.0 10.9 %collective-permute-start.2 = (bf16[8,2,8,1024]{3,2,1,0:T(8,128)(2,1)}, bf16[8,2,8,1024]{3,2,1,0:T(8,128)(2,1)S(1)}, u32[]{:S(2)}, u32[]{:S(2)}) collective-permute-start(bf16[8,2,8,1024]{3,2,1,0:T(8,128)(2,1)} %x_ref.1), channel_id=1, source_target_pairs={{4,0},{8,4},{12,8},{5,1},{9,5},{13,9},{6,2},{10,6},{14,10},{7,3},{... | collective-permute-start | bytes 786440 | tf_op jit(solution)/shard_map/ppermute | solution.py:26
  3.6 4.0 %collective-permute-start.1 = (f32[8,8,1]{2,1,0:T(8,128)S(1)}, f32[8,8,1]{2,1,0:T(8,128)S(1)}, u32[]{:S(2)}, u32[]{:S(2)}) collective-permute-start(f32[8,8,1]{2,1,0:T(8,128)S(1)} %get-tuple-element.31), channel_id=1, source_target_pairs={{0,1},{1,0},{2,3},{3,2},{4,5},{5,4},{6,7},{7,6},{8,9},{9,8},{10,11... | collective-permute-start | bytes 776 | tf_op jit(solution)/shard_map/ppermute | solution.py:249
  3.7 12.8 %collective-permute-start = (bf16[8,2,8,1024]{3,2,1,0:T(8,128)(2,1)}, bf16[8,2,8,1024]{3,2,1,0:T(8,128)(2,1)S(1)}, u32[]{:S(2)}, u32[]{:S(2)}) collective-permute-start(bf16[8,2,8,1024]{3,2,1,0:T(8,128)(2,1)} %x_ref.1), channel_id=1, source_target_pairs={{12,4},{13,5},{14,6},{15,7},{28,20},{29,21},{30,22},{31,23}} | collective-permute-start | bytes 786440 | tf_op jit(solution)/shard_map/ppermute | solution.py:235
  5.4 1.0 %copy-start = (f32[2,96,512]{2,1,0:T(8,128)S(1)}, f32[2,96,512]{2,1,0:T(8,128)}, u32[]{:S(2)}) copy-start(f32[2,96,512]{2,1,0:T(8,128)} %constant.7.clone.base_ref) | copy-start | bytes 1179652
  8.0 10.3 %collective-permute-start.6 = (bf16[8,2,8,1024]{3,2,1,0:T(8,128)(2,1)S(1)}, bf16[8,2,8,1024]{3,2,1,0:T(8,128)(2,1)S(1)}, u32[]{:S(2)}, u32[]{:S(2)}) collective-permute-start(bf16[8,2,8,1024]{3,2,1,0:T(8,128)(2,1)S(1)} %get-tuple-element.34.white_ref.refs_0_), channel_id=1, source_target_pairs={{0,4},{4,8},{8,12},{1,5},{5,9},{9,13},{2,6},{6,10},{10,14},{3,7},{... | collective-permute-start | bytes 786440 | tf_op jit(solution)/shard_map/ppermute | solution.py:26
  11.1 3.5 %collective-permute-start.3 = (f32[8,8,1]{2,1,0:T(8,128)S(1)}, f32[8,8,1]{2,1,0:T(8,128)S(1)}, u32[]{:S(2)}, u32[]{:S(2)}) collective-permute-start(f32[8,8,1]{2,1,0:T(8,128)S(1)} %shard_map.60), channel_id=1, source_target_pairs={{0,1},{1,0},{2,3},{3,2},{4,5},{5,4},{6,7},{7,6},{8,9},{9,8},{10,11... | collective-permute-start | bytes 776 | tf_op jit(solution)/shard_map/ppermute | solution.py:249
  11.3 5.2 %collective-permute-start.7 = (f32[8,8,1]{2,1,0:T(8,128)S(1)}, f32[8,8,1]{2,1,0:T(8,128)S(1)}, u32[]{:S(2)}, u32[]{:S(2)}) collective-permute-start(f32[8,8,1]{2,1,0:T(8,128)S(1)} %get-tuple-element.48), channel_id=1, source_target_pairs={{12,4},{13,5},{14,6},{15,7},{28,20},{29,21},{30,22},{31,23}} | collective-permute-start | bytes 776 | tf_op jit(solution)/shard_map/ppermute | solution.py:317
  16.4 13.3 %copy-start.3 = (s32[8,4]{0,1:T(4,128)S(1)}, s32[8,4]{0,1:T(4,128)}, u32[]{:S(2)}) copy-start(s32[8,4]{0,1:T(4,128)} %param.7) | copy-start | bytes 388
  21.0 1.6 %collective-permute-start.8 = (f32[2,2,64,256]{3,2,1,0:T(8,128)S(1)}, f32[2,2,64,256]{3,2,1,0:T(8,128)S(1)}, u32[]{:S(2)}, u32[]{:S(2)}) collective-permute-start(f32[2,2,64,256]{3,2,1,0:T(8,128)S(1)} %get-tuple-element.52), channel_id=1, source_target_pairs={{0,1},{1,0},{2,3},{3,2},{4,5},{5,4},{6,7},{7,6},{8,9},{9,8},{10,11... | collective-permute-start | bytes 786440 | tf_op jit(solution)/shard_map/ppermute | solution.py:290
  21.0 8.0 %collective-permute-start.4 = (f32[2,2,64,256]{3,2,1,0:T(8,128)S(1)}, f32[2,2,64,256]{3,2,1,0:T(8,128)S(1)}, u32[]{:S(2)}, u32[]{:S(2)}) collective-permute-start(f32[2,2,64,256]{3,2,1,0:T(8,128)S(1)} %get-tuple-element.44), channel_id=1, source_target_pairs={{0,1},{1,0},{2,3},{3,2},{4,5},{5,4},{6,7},{7,6},{8,9},{9,8},{10,11... | collective-permute-start | bytes 786440 | tf_op jit(solution)/shard_map/ppermute | solution.py:290
  22.6 7.3 %collective-permute-start.10 = (bf16[2,64,256]{2,1,0:T(8,128)(2,1)S(1)}, bf16[2,64,256]{2,1,0:T(8,128)(2,1)S(1)}, u32[]{:S(2)}, u32[]{:S(2)}) collective-permute-start(bf16[2,64,256]{2,1,0:T(8,128)(2,1)S(1)} %get-tuple-element.54), channel_id=1, source_target_pairs={{4,2},{6,0},{8,6},{10,4},{12,10},{14,8},{5,3},{7,1},{9,7},{11,5},{... | collective-permute-start | bytes 196616 | tf_op jit(solution)/shard_map/ppermute | solution.py:345
  25.4 5.5 %collective-permute-start.9 = (bf16[2,64,256]{2,1,0:T(8,128)(2,1)S(1)}, bf16[2,64,256]{2,1,0:T(8,128)(2,1)S(1)}, u32[]{:S(2)}, u32[]{:S(2)}) collective-permute-start(bf16[2,64,256]{2,1,0:T(8,128)(2,1)S(1)} %get-tuple-element.53), channel_id=1, source_target_pairs={{4,0},{8,4},{12,8},{5,1},{9,5},{13,9},{6,2},{10,6},{14,10},{7,3},{... | collective-permute-start | bytes 196616 | tf_op jit(solution)/shard_map/ppermute | solution.py:26
  29.1 4.3 %collective-permute-start.5 = (bf16[2,64,256]{2,1,0:T(8,128)(2,1)S(1)}, bf16[2,64,256]{2,1,0:T(8,128)(2,1)S(1)}, u32[]{:S(2)}, u32[]{:S(2)}) collective-permute-start(bf16[2,64,256]{2,1,0:T(8,128)(2,1)S(1)} %get-tuple-element.46), channel_id=1, source_target_pairs={{0,2},{2,0},{1,3},{3,1},{4,6},{6,4},{5,7},{7,5},{8,10},{10,8},{9,1... | collective-permute-start | bytes 196616 | tf_op jit(solution)/shard_map/ppermute | solution.py:290

commit v15 on v14

--- a/solution.py
+++ b/solution.py
@@ -54,22 +54,12 @@
         power_ref[w] = bin_power(x_ref[w])
 
 
-def own_kernel(n_bins, x_ref, *refs):
-    power_ref = refs[-1]
+def whiten_kernel(n_bins, x_ref, *refs):
+    out_ref = refs[-1]
     for w in range(x_ref.shape[0]):
         power = bin_power(x_ref[w])
-        for ref in refs[:-2]:
+        for ref in refs[:-1]:
             power = power + ref[w]
-        power_ref[w] = power
-    whiten_kernel(n_bins, False, x_ref, power_ref, refs[-2])
-
-
-def whiten_kernel(n_bins, add_own, x_ref, *refs):
-    out_ref = refs[-1]
-    for w in range(x_ref.shape[0]):
-        power = bin_power(x_ref[w]) if add_own else None
-        for ref in refs[:-1]:
-            power = ref[w] if power is None else power + ref[w]
         scale = lax.rsqrt(power / n_bins + EPS)
         for part in range(2):
             out_ref[w, part] = (x_ref[w, part].astype(jnp.float32) * scale).astype(jnp.bfloat16)
@@ -232,7 +222,6 @@
 
     below = from_behind(spectra, "chan", -1)
     far_routes = [[(c + away, c) for c in range(1, n_chan - away)] for away in range(2, reach)]
-    far = [lax.ppermute(spectra, "chan", route) for route in far_routes]
     power, copied = pl.pallas_call(
         power_kernel,
         out_shape=[
@@ -255,9 +244,9 @@
             in_specs=[VMEM], out_specs=VMEM, compiler_params=params, cost_estimate=cost(ch, ch),
         )(block)
 
-    def whiten(block, others, add_own):
-        return pl.pallas_call(
-            functools.partial(whiten_kernel, n_bins, add_own),
+    def whiten(block, others):
+        return pl.pallas_call(
+            functools.partial(whiten_kernel, n_bins),
             out_shape=jax.ShapeDtypeStruct(block.shape, jnp.bfloat16),
             in_specs=[VMEM] * (1 + len(others)), out_specs=VMEM, compiler_params=params,
         )(block, *others)
@@ -305,16 +294,8 @@
             in_specs=[VMEM] * (n_freq + len(before)), out_specs=[VMEM] * n_win, compiler_params=params,
         )(*turns(parts, "freq", n_freq), *before)
 
-    others = swap(power)
-    white, power = pl.pallas_call(
-        functools.partial(own_kernel, n_bins),
-        out_shape=[
-            jax.ShapeDtypeStruct(spectra.shape, jnp.bfloat16),
-            jax.ShapeDtypeStruct(power.shape, jnp.float32),
-        ],
-        in_specs=[VMEM] * (1 + len(others)), out_specs=[VMEM] * 2, compiler_params=params,
-    )(copied, *others)
-    far_powers = [lax.ppermute(power, "chan", route) for route in far_routes]
+    white = whiten(copied, swap(power))
+    far = [lax.ppermute(white, "chan", route) for route in far_routes]
     half_lags = 2 * np.arange(LAGS // 2) + 1
     coarse = phases(np.arange(0, n_bins, FINE), half_lags)
     fine = phases(F_LO + np.arange(FINE), half_lags)
@@ -328,10 +309,9 @@
     above = from_behind(white, "chan", 1)
     first = pairs(own, [white])
     below, first = lax.optimization_barrier((below, first))
-    below = whiten(below, swap(half_power(below)), True)
+    below = whiten(below, swap(half_power(below)))
     parts = pairs(own, [below], first)
     far, parts = lax.optimization_barrier((far, parts))
-    far = [whiten(block, [power], False) for block, power in zip(far, far_powers)]
     above, far = lax.optimization_barrier((above, far))
     base = kept(above)
     sums = split_windows(parts, [], [jnp.float32] + [jnp.bfloat16] * (n_win - 1))

time: 34.7 us -> 33.8 us (0.974)
  the two profiles are of different devices: /device:TPU:24 before, /device:TPU:0 now
where the time goes in v15:
time: 33.8 us; the launch traced here: 33.3 us
  starting transfers between devices  13.6 us (40%)
  Pallas kernels  8.75 us (26%)
  waiting for transfers between devices  8.64 us (26%)
  local copies, waits for them, and re-layouts  2.12 us (6%)
    ppermute x3, starting transfers between devices, from_behind(): return lax.ppermute(block, axis, route)  8.33 us
    pallas_call x3, Pallas kernels, pairs(): pl.pallas_call(functools.partial(pairs_kernel, len(partners), n_win, n_fr...  5.67 us
    ppermute x3, waiting for transfers between devices, from_behind(): return lax.ppermute(block, axis, route)  3.32 us
    ppermute x1, waiting for transfers between devices, local(): received.append(lax.ppermute(shipped[turn], ('chan', 'win'), route))  3.29 us
    ppermute x3, starting transfers between devices, turns(): received.append(lax.ppermute(parts[turn], axis, route))  2.56 us
    unnamed x10, local copies, waits for them, and re-layouts  1.95 us
    ppermute x1, starting transfers between devices, local(): received.append(lax.ppermute(shipped[turn], ('chan', 'win'), route))  1.29 us
    pallas_call x1, Pallas kernels, local(): pl.pallas_call(table_kernel, out_shape=jax.ShapeDtypeStruct((4, f_dev, LA...  1.19 us
  transfers between devices with their start and end apart: 10, of which 5 were waited for; matrix products, arithmetic and copies ran while one was open for 1% of the time, Pallas kernels for 16%

profile of v15, /device:TPU:0, one launch (start us, length us, event | category | flops | bytes accessed | tf_op | source)
XLA Modules:
  0.0 33.3 jit_solution(1909343815658751428)
XLA Ops:
  0.0 1.3 %collective-permute-start.2 = (bf16[8,2,8,1024]{3,2,1,0:T(8,128)(2,1)}, bf16[8,2,8,1024]{3,2,1,0:T(8,128)(2,1)S(1)}, u32[]{:S(2)}, u32[]{:S(2)}) collective-permute-start(bf16[8,2,8,1024]{3,2,1,0:T(8,128)(2,1)} %x_ref.1), channel_id=1, source_target_pairs={{4,0},{8,4},{12,8},{5,1},{9,5},{13,9},{6,2},{10,6},{14,10},{7,3},{... | collective-permute-start | bytes 786440 | tf_op jit(solution)/shard_map/ppermute | solution.py:26
  1.3 0.0 copy-start.1
  1.3 0.9 %copy-done.1 = bf16[8,2,8,1024]{3,2,1,0:T(8,128)(2,1)S(1)} copy-done((bf16[8,2,8,1024]{3,2,1,0:T(8,128)(2,1)S(1)}, bf16[8,2,8,1024]{3,2,1,0:T(8,128)(2,1)}, u32[]{:S(2)}) %copy-start.1) | copy-done | bytes 262168
  2.2 0.0 copy-start.3
  2.2 0.0 copy-start.2
  2.2 0.1 shard_map.55
  2.4 0.5 %collective-permute-start = (f32[8,8,1]{2,1,0:T(8,128)S(1)}, f32[8,8,1]{2,1,0:T(8,128)S(1)}, u32[]{:S(2)}, u32[]{:S(2)}) collective-permute-start(f32[8,8,1]{2,1,0:T(8,128)S(1)} %get-tuple-element.29), channel_id=1, source_target_pairs={{0,1},{1,0},{2,3},{3,2},{4,5},{5,4},{6,7},{7,6},{8,9},{9,8},{10,11... | collective-permute-start | bytes 776 | tf_op jit(solution)/shard_map/ppermute | solution.py:238
  2.8 0.0 copy-start
  2.8 1.0 %copy-done = f32[2,96,512]{2,1,0:T(8,128)S(1)} copy-done((f32[2,96,512]{2,1,0:T(8,128)S(1)}, f32[2,96,512]{2,1,0:T(8,128)}, u32[]{:S(2)}) %copy-start) | copy-done | bytes 393240
  3.8 1.2 %shard_map.57.refs_2_.refs_3_ = bf16[4,1024,512]{2,1,0:T(8,128)(2,1)S(1)} custom-call(f32[2,96,512]{2,1,0:T(8,128)S(1)} %copy-done), custom_call_target="tpu_custom_call" | custom-call | flops 8 | bytes 8 | tf_op jit(solution)/shard_map/pallas_call | solution.py:302
  5.0 0.0 collective-permute-done.refs_0_
  5.0 0.2 shard_map.56.white_ref.refs_0_
  5.3 0.7 %collective-permute-start.1 = (bf16[8,2,8,1024]{3,2,1,0:T(8,128)(2,1)S(1)}, bf16[8,2,8,1024]{3,2,1,0:T(8,128)(2,1)S(1)}, u32[]{:S(2)}, u32[]{:S(2)}) collective-permute-start(bf16[8,2,8,1024]{3,2,1,0:T(8,128)(2,1)S(1)} %shard_map.56.white_ref.refs_0_), channel_id=1, source_target_pairs={{12,4},{13,5},{14,6},{15,7},{28,20},{29,21},{30,22},{31,23}} | collective-permute-start | bytes 786440 | tf_op jit(solution)/shard_map/ppermute | solution.py:298
  6.0 0.0 copy-done.3
  6.0 0.1 shard_map.58.base_ref
  6.1 5.8 %collective-permute-start.6 = (bf16[8,2,8,1024]{3,2,1,0:T(8,128)(2,1)S(1)}, bf16[8,2,8,1024]{3,2,1,0:T(8,128)(2,1)S(1)}, u32[]{:S(2)}, u32[]{:S(2)}) collective-permute-start(bf16[8,2,8,1024]{3,2,1,0:T(8,128)(2,1)S(1)} %shard_map.56.white_ref.refs_0_), channel_id=1, source_target_pairs={{0,4},{4,8},{8,12},{1,5},{5,9},{9,13},{2,6},{6,10},{10,14},{3,7},{... | collective-permute-start | bytes 786440 | tf_op jit(solution)/shard_map/ppermute | solution.py:26
  11.9 0.0 copy-done.2
  11.9 1.6 %shard_map.59 = (f32[1,2,64,256]{3,2,1,0:T(8,128)S(1)}, f32[1,2,64,256]{3,2,1,0:T(8,128)S(1)}) custom-call(f32[8,2,8,1024]{3,2,1,0:T(8,128)S(1)} %shard_map.58.base_ref, bf16[8,2,8,1024]{3,2,1,0:T(8,128)(2,1)S(1)} %shard_map.56.white_ref.refs_0_, f32[2,2,1024]{2,1,0:T(2,128)S(1)} %copy-done.2, bf16[4,1024,512]{2,1,0:T(8,128)(2,1)S(1)} %shard_map.57.refs_2_.refs_3_), custom_call_target="tpu_custom_call" | custom-call | flops 8 | bytes 8 | tf_op jit(solution)/shard_map/pallas_call | solution.py:263
  13.5 0.0 collective-permute-done.2.x_ref
  13.5 0.1 shard_map.60
  13.6 0.2 collective-permute-start.3
  13.8 1.0 %collective-permute-done.3.refs_0_ = f32[8,8,1]{2,1,0:T(8,128)S(1)} collective-permute-done((f32[8,8,1]{2,1,0:T(8,128)S(1)}, f32[8,8,1]{2,1,0:T(8,128)S(1)}, u32[]{:S(2)}, u32[]{:S(2)}) %collective-permute-start.3) | collective-permute-done | bytes 288 | tf_op jit(solution)/shard_map/ppermute | solution.py:238
  14.8 0.2 shard_map.61.refs_0_
  15.1 1.6 %shard_map.62 = (f32[2,2,64,256]{3,2,1,0:T(8,128)S(1)}, f32[2,2,64,256]{3,2,1,0:T(8,128)S(1)}) custom-call(f32[8,2,8,1024]{3,2,1,0:T(8,128)S(1)} %shard_map.58.base_ref, bf16[8,2,8,1024]{3,2,1,0:T(8,128)(2,1)S(1)} %shard_map.61.refs_0_, f32[2,2,1024]{2,1,0:T(2,128)S(1)} %copy-done.2, bf16[4,1024,512]{2,1,0:T(8,128)(2,1)S(1)} %shard_map.57.refs_2_.refs_3_, ...), custom_call_target="tpu_custom_call" | custom-call | flops 8 | bytes 8 | tf_op jit(solution)/shard_map/pallas_call | solution.py:263
  16.7 0.0 copy-start.4
  16.7 0.0 collective-permute-done.1.refs_1_
  16.7 1.4 %collective-permute-done.6.white_ref = bf16[8,2,8,1024]{3,2,1,0:T(8,128)(2,1)S(1)} collective-permute-done((bf16[8,2,8,1024]{3,2,1,0:T(8,128)(2,1)S(1)}, bf16[8,2,8,1024]{3,2,1,0:T(8,128)(2,1)S(1)}, u32[]{:S(2)}, u32[]{:S(2)}) %collective-permute-start.6) | collective-permute-done | bytes 262176 | tf_op jit(solution)/shard_map/ppermute | solution.py:26
  18.1 0.1 shard_map.64.base_ref
  18.2 2.5 %shard_map.65 = (f32[2,2,64,256]{3,2,1,0:T(8,128)S(1)}, f32[2,2,64,256]{3,2,1,0:T(8,128)S(1)}) custom-call(f32[8,2,8,1024]{3,2,1,0:T(8,128)S(1)} %shard_map.64.base_ref, bf16[8,2,8,1024]{3,2,1,0:T(8,128)(2,1)S(1)} %shard_map.61.refs_0_, bf16[8,2,8,1024]{3,2,1,0:T(8,128)(2,1)S(1)} %collective-permute-done.1.refs_1_, f32[2,2,1024]{2,1,0:T(2,128)S(1)} %copy-done.2, ...), custom_call_target="tpu_custom_call" | custom-call | flops 8 | bytes 8 | tf_op jit(solution)/shard_map/pallas_call | solution.py:263
  20.7 0.1 collective-permute-start.7
  20.8 0.5 %collective-permute-start.4 = (f32[2,2,64,256]{3,2,1,0:T(8,128)S(1)}, f32[2,2,64,256]{3,2,1,0:T(8,128)S(1)}, u32[]{:S(2)}, u32[]{:S(2)}) collective-permute-start(f32[2,2,64,256]{3,2,1,0:T(8,128)S(1)} %get-tuple-element.41), channel_id=1, source_target_pairs={{0,1},{1,0},{2,3},{3,2},{4,5},{5,4},{6,7},{7,6},{8,9},{9,8},{10,11... | collective-permute-start | bytes 786440 | tf_op jit(solution)/shard_map/ppermute | solution.py:279
  21.3 1.0 %collective-permute-done.7.refs_1_ = f32[2,2,64,256]{3,2,1,0:T(8,128)S(1)} collective-permute-done((f32[2,2,64,256]{3,2,1,0:T(8,128)S(1)}, f32[2,2,64,256]{3,2,1,0:T(8,128)S(1)}, u32[]{:S(2)}, u32[]{:S(2)}) %collective-permute-start.7) | collective-permute-done | bytes 262176 | tf_op jit(solution)/shard_map/ppermute | solution.py:279
  22.3 1.3 %collective-permute-start.8 = (bf16[2,64,256]{2,1,0:T(8,128)(2,1)S(1)}, bf16[2,64,256]{2,1,0:T(8,128)(2,1)S(1)}, u32[]{:S(2)}, u32[]{:S(2)}) collective-permute-start(bf16[2,64,256]{2,1,0:T(8,128)(2,1)S(1)} %get-tuple-element.49), channel_id=1, source_target_pairs={{4,0},{8,4},{12,8},{5,1},{9,5},{13,9},{6,2},{10,6},{14,10},{7,3},{... | collective-permute-start | bytes 196616 | tf_op jit(solution)/shard_map/ppermute | solution.py:26
  23.6 1.3 %collective-permute-start.9 = (bf16[2,64,256]{2,1,0:T(8,128)(2,1)S(1)}, bf16[2,64,256]{2,1,0:T(8,128)(2,1)S(1)}, u32[]{:S(2)}, u32[]{:S(2)}) collective-permute-start(bf16[2,64,256]{2,1,0:T(8,128)(2,1)S(1)} %get-tuple-element.50), channel_id=1, source_target_pairs={{4,2},{6,0},{8,6},{10,4},{12,10},{14,8},{5,3},{7,1},{9,7},{11,5},{... | collective-permute-start | bytes 196616 | tf_op jit(solution)/shard_map/ppermute | solution.py:325
  24.9 0.0 collective-permute-done.4.refs_1_
  25.0 2.0 %collective-permute-start.5 = (bf16[2,64,256]{2,1,0:T(8,128)(2,1)S(1)}, bf16[2,64,256]{2,1,0:T(8,128)(2,1)S(1)}, u32[]{:S(2)}, u32[]{:S(2)}) collective-permute-start(bf16[2,64,256]{2,1,0:T(8,128)(2,1)S(1)} %get-tuple-element.43), channel_id=1, source_target_pairs={{0,2},{2,0},{1,3},{3,1},{4,6},{6,4},{5,7},{7,5},{8,10},{10,8},{9,1... | collective-permute-start | bytes 196616 | tf_op jit(solution)/shard_map/ppermute | solution.py:279
  27.0 0.0 copy-done.4
  27.0 0.1 broadcast_in_dim.3
  27.0 0.1 broadcast_in_dim_reshape.4.factor_ref
  27.1 1.9 %collective-permute-done.8.refs_2_ = bf16[2,64,256]{2,1,0:T(8,128)(2,1)S(1)} collective-permute-done((bf16[2,64,256]{2,1,0:T(8,128)(2,1)S(1)}, bf16[2,64,256]{2,1,0:T(8,128)(2,1)S(1)}, u32[]{:S(2)}, u32[]{:S(2)}) %collective-permute-start.8) | collective-permute-done | bytes 65568 | tf_op jit(solution)/shard_map/ppermute | solution.py:26
  29.1 3.3 %collective-permute-done.9.refs_3_ = bf16[2,64,256]{2,1,0:T(8,128)(2,1)S(1)} collective-permute-done((bf16[2,64,256]{2,1,0:T(8,128)(2,1)S(1)}, bf16[2,64,256]{2,1,0:T(8,128)(2,1)S(1)}, u32[]{:S(2)}, u32[]{:S(2)}) %collective-permute-start.9) | collective-permute-done | bytes 65568 | tf_op jit(solution)/shard_map/ppermute | solution.py:325
  32.4 0.0 collective-permute-done.5.refs_1_
  32.4 0.9 %shard_map.67 = f32[8,4,8,256]{3,2,1,0:T(8,128)} custom-call(f32[4,64,1]{2,1,0:T(8,128)S(1)} %broadcast_in_dim_reshape.4.factor_ref, f32[2,64,256]{2,1,0:T(8,128)S(1)} %get-tuple-element.42.refs_0_, bf16[2,64,256]{2,1,0:T(8,128)(2,1)S(1)} %collective-permute-done.5.refs_1_, bf16[2,64,256]{2,1,0:T(8,128)(2,1)S(1)} %collective-permute-done.8.refs_2_, ...), custom_call_target="tpu_custom_call" | custom-call | tf_op jit(solution)/shard_map/pallas_call | solution.py:328
  (3 shorter events, 0.1 us)
Async XLA Ops:
  0.0 13.5 %collective-permute-start.2 = (bf16[8,2,8,1024]{3,2,1,0:T(8,128)(2,1)}, bf16[8,2,8,1024]{3,2,1,0:T(8,128)(2,1)S(1)}, u32[]{:S(2)}, u32[]{:S(2)}) collective-permute-start(bf16[8,2,8,1024]{3,2,1,0:T(8,128)(2,1)} %x_ref.1), channel_id=1, source_target_pairs={{4,0},{8,4},{12,8},{5,1},{9,5},{13,9},{6,2},{10,6},{14,10},{7,3},{... | collective-permute-start | bytes 786440 | tf_op jit(solution)/shard_map/ppermute | solution.py:26
  1.3 1.0 %copy-start.1 = (bf16[8,2,8,1024]{3,2,1,0:T(8,128)(2,1)S(1)}, bf16[8,2,8,1024]{3,2,1,0:T(8,128)(2,1)}, u32[]{:S(2)}) copy-start(bf16[8,2,8,1024]{3,2,1,0:T(8,128)(2,1)} %x_ref.1) | copy-start | bytes 786436
  2.2 3.7 %copy-start.3 = (s32[8]{0:T(128)S(1)}, s32[8]{0:T(128)}, u32[]{:S(2)}) copy-start(s32[8]{0:T(128)} %param.6) | copy-start | bytes 100
  2.2 9.6 %copy-start.2 = (f32[2,2,1024]{2,1,0:T(2,128)S(1)}, f32[2,2,1024]{2,1,0:T(2,128)}, u32[]{:S(2)}) copy-start(f32[2,2,1024]{2,1,0:T(2,128)} %constant.6.clone.refs_1_.refs_2_) | copy-start | bytes 49156
  2.4 2.7 %collective-permute-start = (f32[8,8,1]{2,1,0:T(8,128)S(1)}, f32[8,8,1]{2,1,0:T(8,128)S(1)}, u32[]{:S(2)}, u32[]{:S(2)}) collective-permute-start(f32[8,8,1]{2,1,0:T(8,128)S(1)} %get-tuple-element.29), channel_id=1, source_target_pairs={{0,1},{1,0},{2,3},{3,2},{4,5},{5,4},{6,7},{7,6},{8,9},{9,8},{10,11... | collective-permute-start | bytes 776 | tf_op jit(solution)/shard_map/ppermute | solution.py:238
  2.8 1.0 %copy-start = (f32[2,96,512]{2,1,0:T(8,128)S(1)}, f32[2,96,512]{2,1,0:T(8,128)}, u32[]{:S(2)}) copy-start(f32[2,96,512]{2,1,0:T(8,128)} %constant.7.clone.base_ref) | copy-start | bytes 1179652
  5.3 11.4 %collective-permute-start.1 = (bf16[8,2,8,1024]{3,2,1,0:T(8,128)(2,1)S(1)}, bf16[8,2,8,1024]{3,2,1,0:T(8,128)(2,1)S(1)}, u32[]{:S(2)}, u32[]{:S(2)}) collective-permute-start(bf16[8,2,8,1024]{3,2,1,0:T(8,128)(2,1)S(1)} %shard_map.56.white_ref.refs_0_), channel_id=1, source_target_pairs={{12,4},{13,5},{14,6},{15,7},{28,20},{29,21},{30,22},{31,23}} | collective-permute-start | bytes 786440 | tf_op jit(solution)/shard_map/ppermute | solution.py:298
  6.1 12.0 %collective-permute-start.6 = (bf16[8,2,8,1024]{3,2,1,0:T(8,128)(2,1)S(1)}, bf16[8,2,8,1024]{3,2,1,0:T(8,128)(2,1)S(1)}, u32[]{:S(2)}, u32[]{:S(2)}) collective-permute-start(bf16[8,2,8,1024]{3,2,1,0:T(8,128)(2,1)S(1)} %shard_map.56.white_ref.refs_0_), channel_id=1, source_target_pairs={{0,4},{4,8},{8,12},{1,5},{5,9},{9,13},{2,6},{6,10},{10,14},{3,7},{... | collective-permute-start | bytes 786440 | tf_op jit(solution)/shard_map/ppermute | solution.py:26
  13.6 1.2 %collective-permute-start.3 = (f32[8,8,1]{2,1,0:T(8,128)S(1)}, f32[8,8,1]{2,1,0:T(8,128)S(1)}, u32[]{:S(2)}, u32[]{:S(2)}) collective-permute-start(f32[8,8,1]{2,1,0:T(8,128)S(1)} %shard_map.60), channel_id=1, source_target_pairs={{0,1},{1,0},{2,3},{3,2},{4,5},{5,4},{6,7},{7,6},{8,9},{9,8},{10,11... | collective-permute-start | bytes 776 | tf_op jit(solution)/shard_map/ppermute | solution.py:238
  16.7 10.3 %copy-start.4 = (s32[8,4]{0,1:T(4,128)S(1)}, s32[8,4]{0,1:T(4,128)}, u32[]{:S(2)}) copy-start(s32[8,4]{0,1:T(4,128)} %param.7) | copy-start | bytes 388
  20.7 1.6 %collective-permute-start.7 = (f32[2,2,64,256]{3,2,1,0:T(8,128)S(1)}, f32[2,2,64,256]{3,2,1,0:T(8,128)S(1)}, u32[]{:S(2)}, u32[]{:S(2)}) collective-permute-start(f32[2,2,64,256]{3,2,1,0:T(8,128)S(1)} %get-tuple-element.48), channel_id=1, source_target_pairs={{0,1},{1,0},{2,3},{3,2},{4,5},{5,4},{6,7},{7,6},{8,9},{9,8},{10,11... | collective-permute-start | bytes 786440 | tf_op jit(solution)/shard_map/ppermute | solution.py:279
  20.8 4.2 %collective-permute-start.4 = (f32[2,2,64,256]{3,2,1,0:T(8,128)S(1)}, f32[2,2,64,256]{3,2,1,0:T(8,128)S(1)}, u32[]{:S(2)}, u32[]{:S(2)}) collective-permute-start(f32[2,2,64,256]{3,2,1,0:T(8,128)S(1)} %get-tuple-element.41), channel_id=1, source_target_pairs={{0,1},{1,0},{2,3},{3,2},{4,5},{5,4},{6,7},{7,6},{8,9},{9,8},{10,11... | collective-permute-start | bytes 786440 | tf_op jit(solution)/shard_map/ppermute | solution.py:279
  22.3 6.8 %collective-permute-start.8 = (bf16[2,64,256]{2,1,0:T(8,128)(2,1)S(1)}, bf16[2,64,256]{2,1,0:T(8,128)(2,1)S(1)}, u32[]{:S(2)}, u32[]{:S(2)}) collective-permute-start(bf16[2,64,256]{2,1,0:T(8,128)(2,1)S(1)} %get-tuple-element.49), channel_id=1, source_target_pairs={{4,0},{8,4},{12,8},{5,1},{9,5},{13,9},{6,2},{10,6},{14,10},{7,3},{... | collective-permute-start | bytes 196616 | tf_op jit(solution)/shard_map/ppermute | solution.py:26
  23.6 8.8 %collective-permute-start.9 = (bf16[2,64,256]{2,1,0:T(8,128)(2,1)S(1)}, bf16[2,64,256]{2,1,0:T(8,128)(2,1)S(1)}, u32[]{:S(2)}, u32[]{:S(2)}) collective-permute-start(bf16[2,64,256]{2,1,0:T(8,128)(2,1)S(1)} %get-tuple-element.50), channel_id=1, source_target_pairs={{4,2},{6,0},{8,6},{10,4},{12,10},{14,8},{5,3},{7,1},{9,7},{11,5},{... | collective-permute-start | bytes 196616 | tf_op jit(solution)/shard_map/ppermute | solution.py:325
  25.0 7.4 %collective-permute-start.5 = (bf16[2,64,256]{2,1,0:T(8,128)(2,1)S(1)}, bf16[2,64,256]{2,1,0:T(8,128)(2,1)S(1)}, u32[]{:S(2)}, u32[]{:S(2)}) collective-permute-start(bf16[2,64,256]{2,1,0:T(8,128)(2,1)S(1)} %get-tuple-element.43), channel_id=1, source_target_pairs={{0,2},{2,0},{1,3},{3,1},{4,6},{6,4},{5,7},{7,5},{8,10},{10,8},{9,1... | collective-permute-start | bytes 196616 | tf_op jit(solution)/shard_map/ppermute | solution.py:279

commit v16 on v15

--- a/solution.py
+++ b/solution.py
@@ -296,17 +296,17 @@
 
     white = whiten(copied, swap(power))
     far = [lax.ppermute(white, "chan", route) for route in far_routes]
+    above = lax.ppermute(white, "chan", [(c - 1, c) for c in range(1, n_chan - 1)])
     half_lags = 2 * np.arange(LAGS // 2) + 1
     coarse = phases(np.arange(0, n_bins, FINE), half_lags)
     fine = phases(F_LO + np.arange(FINE), half_lags)
+    white, ends = lax.optimization_barrier((white, jnp.asarray(np.concatenate([coarse, fine], axis=1))))
     table = pl.pallas_call(
         table_kernel,
         out_shape=jax.ShapeDtypeStruct((4, f_dev, LAGS // 2), jnp.bfloat16),
         in_specs=[VMEM], out_specs=VMEM, compiler_params=params, cost_estimate=cost(ch, ch),
-    )(jnp.asarray(np.concatenate([coarse, fine], axis=1)))
+    )(ends)
     own = kept(white)
-    white, table, own = lax.optimization_barrier((white, table, own))
-    above = from_behind(white, "chan", 1)
     first = pairs(own, [white])
     below, first = lax.optimization_barrier((below, first))
     below = whiten(below, swap(half_power(below)))
@@ -317,10 +317,10 @@
     sums = split_windows(parts, [], [jnp.float32] + [jnp.bfloat16] * (n_win - 1))
     shipped = split_windows(pairs(base, [below] + far), [], [jnp.bfloat16] * n_win)
     received = turns(sums, "win", n_win)
-    received.append(from_behind(shipped[0], "chan", -1))
+    received.append(lax.ppermute(shipped[0], "chan", [(c, c - 1) for c in range(1, n_chan - 1)]))
     for turn in range(1, n_win):
         route = [
-            (c * n_win + w, (c - 1) * n_win + (w + turn) % n_win) for c in range(1, n_chan) for w in range(n_win)
+            (c * n_win + w, (c - 1) * n_win + (w + turn) % n_win) for c in range(1, n_chan - 1) for w in range(n_win)
         ]
         received.append(lax.ppermute(shipped[turn], ("chan", "win"), route))
     scale = 1.0 / math.sqrt(w_dev * n_win * n_bins)

time: 33.8 us -> 32.7 us (0.967)
  waiting for transfers between devices: 8.64 us -> 7.72 us
    ppermute x0 -> x2, starting transfers between devices: none -> 7.38 us  [the longest x1 6.09 us: local(): lax.ppermute(white, 'chan', [(c - 1, c) for c in range(1, n_chan - 1)])]
    ppermute x3 -> x1, starting transfers between devices: 8.33 us -> 1.28 us  [from_behind(): return lax.ppermute(block, axis, route)]
    ppermute x3 -> x1, waiting for transfers between devices: 3.32 us -> 0.01 us  [from_behind(): return lax.ppermute(block, axis, route)]
    ppermute x0 -> x2, waiting for transfers between devices: none -> 1.39 us  [the longest x1 1.39 us: local(): lax.ppermute(shipped[0], 'chan', [(c, c - 1) for c in range(1, n_chan - 1)])]
    ppermute x2, waiting for transfers between devices: 0.99 us -> 2.05 us  [swap(): return [lax.ppermute(power, 'freq', route) for route in routes]]
where the time goes in v16:
time: 32.7 us; the launch traced here: 32.5 us
  starting transfers between devices  13.7 us (42%)
  Pallas kernels  8.76 us (27%)
  waiting for transfers between devices  7.72 us (24%)
  local copies, waits for them, and re-layouts  2.12 us (6%)
    ppermute x1, starting transfers between devices, local(): lax.ppermute(white, 'chan', [(c - 1, c) for c in range(1, n_chan - 1)])  6.09 us
    pallas_call x3, Pallas kernels, pairs(): pl.pallas_call(functools.partial(pairs_kernel, len(partners), n_win, n_fr...  5.68 us
    ppermute x1, waiting for transfers between devices, local(): received.append(lax.ppermute(shipped[turn], ('chan', 'win'), route))  3.24 us
    ppermute x3, starting transfers between devices, turns(): received.append(lax.ppermute(parts[turn], axis, route))  2.56 us
    ppermute x2, waiting for transfers between devices, swap(): return [lax.ppermute(power, 'freq', route) for route in routes]  2.05 us
    unnamed x10, local copies, waits for them, and re-layouts  1.95 us
    ppermute x1, waiting for transfers between devices, local(): lax.ppermute(shipped[0], 'chan', [(c, c - 1) for c in range(1, n_chan - 1)])  1.39 us
    ppermute x1, starting transfers between devices, local(): lax.ppermute(shipped[0], 'chan', [(c, c - 1) for c in range(1, n_chan - 1)])  1.29 us
  transfers between devices with their start and end apart: 10, of which 5 were waited for; matrix products, arithmetic and copies ran while one was open for 1% of the time, Pallas kernels for 16%

profile of v16, /device:TPU:0, one launch (start us, length us, event | category | flops | bytes accessed | tf_op | source)
XLA Modules:
  0.0 32.5 jit_solution(10687203391152327684)
XLA Ops:
  0.0 1.3 %collective-permute-start.2 = (bf16[8,2,8,1024]{3,2,1,0:T(8,128)(2,1)}, bf16[8,2,8,1024]{3,2,1,0:T(8,128)(2,1)S(1)}, u32[]{:S(2)}, u32[]{:S(2)}) collective-permute-start(bf16[8,2,8,1024]{3,2,1,0:T(8,128)(2,1)} %x_ref.1), channel_id=1, source_target_pairs={{4,0},{8,4},{12,8},{5,1},{9,5},{13,9},{6,2},{10,6},{14,10},{7,3},{... | collective-permute-start | bytes 786440 | tf_op jit(solution)/shard_map/ppermute | solution.py:26
  1.3 0.0 copy-start.1
  1.3 0.9 %copy-done.1 = bf16[8,2,8,1024]{3,2,1,0:T(8,128)(2,1)S(1)} copy-done((bf16[8,2,8,1024]{3,2,1,0:T(8,128)(2,1)S(1)}, bf16[8,2,8,1024]{3,2,1,0:T(8,128)(2,1)}, u32[]{:S(2)}) %copy-start.1) | copy-done | bytes 262168
  2.2 0.0 copy-start.3
  2.2 0.0 copy-start.2
  2.2 0.1 shard_map.55
  2.4 0.5 %collective-permute-start = (f32[8,8,1]{2,1,0:T(8,128)S(1)}, f32[8,8,1]{2,1,0:T(8,128)S(1)}, u32[]{:S(2)}, u32[]{:S(2)}) collective-permute-start(f32[8,8,1]{2,1,0:T(8,128)S(1)} %get-tuple-element.28), channel_id=1, source_target_pairs={{0,1},{1,0},{2,3},{3,2},{4,5},{5,4},{6,7},{7,6},{8,9},{9,8},{10,11... | collective-permute-start | bytes 776 | tf_op jit(solution)/shard_map/ppermute | solution.py:238
  2.8 0.9 %collective-permute-done.refs_0_ = f32[8,8,1]{2,1,0:T(8,128)S(1)} collective-permute-done((f32[8,8,1]{2,1,0:T(8,128)S(1)}, f32[8,8,1]{2,1,0:T(8,128)S(1)}, u32[]{:S(2)}, u32[]{:S(2)}) %collective-permute-start) | collective-permute-done | bytes 288 | tf_op jit(solution)/shard_map/ppermute | solution.py:238
  3.7 0.2 shard_map.56.white_ref.refs_0_
  3.9 0.7 %collective-permute-start.1 = (bf16[8,2,8,1024]{3,2,1,0:T(8,128)(2,1)S(1)}, bf16[8,2,8,1024]{3,2,1,0:T(8,128)(2,1)S(1)}, u32[]{:S(2)}, u32[]{:S(2)}) collective-permute-start(bf16[8,2,8,1024]{3,2,1,0:T(8,128)(2,1)S(1)} %shard_map.56.white_ref.refs_0_), channel_id=1, source_target_pairs={{12,4},{13,5},{14,6},{15,7},{28,20},{29,21},{30,22},{31,23}} | collective-permute-start | bytes 786440 | tf_op jit(solution)/shard_map/ppermute | solution.py:298
  4.6 6.1 %collective-permute-start.6 = (bf16[8,2,8,1024]{3,2,1,0:T(8,128)(2,1)S(1)}, bf16[8,2,8,1024]{3,2,1,0:T(8,128)(2,1)S(1)}, u32[]{:S(2)}, u32[]{:S(2)}) collective-permute-start(bf16[8,2,8,1024]{3,2,1,0:T(8,128)(2,1)S(1)} %shard_map.56.white_ref.refs_0_), channel_id=1, source_target_pairs={{0,4},{4,8},{1,5},{5,9},{2,6},{6,10},{3,7},{7,11},{16,20},{20,24},... | collective-permute-start | bytes 786440 | tf_op jit(solution)/shard_map/ppermute | solution.py:299
  10.7 0.0 copy-start
  10.7 1.0 %copy-done = f32[2,96,512]{2,1,0:T(8,128)S(1)} copy-done((f32[2,96,512]{2,1,0:T(8,128)S(1)}, f32[2,96,512]{2,1,0:T(8,128)}, u32[]{:S(2)}) %copy-start) | copy-done | bytes 393240
  11.7 1.2 %shard_map.58.refs_2_.refs_3_ = bf16[4,1024,512]{2,1,0:T(8,128)(2,1)S(1)} custom-call(f32[2,96,512]{2,1,0:T(8,128)S(1)} %copy-done), custom_call_target="tpu_custom_call" | custom-call | flops 8 | bytes 8 | tf_op jit(solution)/shard_map/pallas_call | solution.py:304
  12.9 0.0 copy-done.3
  12.9 0.1 shard_map.57.base_ref
  13.0 0.0 copy-done.2
  13.1 1.6 %shard_map.59 = (f32[1,2,64,256]{3,2,1,0:T(8,128)S(1)}, f32[1,2,64,256]{3,2,1,0:T(8,128)S(1)}) custom-call(f32[8,2,8,1024]{3,2,1,0:T(8,128)S(1)} %shard_map.57.base_ref, bf16[8,2,8,1024]{3,2,1,0:T(8,128)(2,1)S(1)} %shard_map.56.white_ref.refs_0_, f32[2,2,1024]{2,1,0:T(2,128)S(1)} %copy-done.2, bf16[4,1024,512]{2,1,0:T(8,128)(2,1)S(1)} %shard_map.58.refs_2_.refs_3_), custom_call_target="tpu_custom_call" | custom-call | flops 8 | bytes 8 | tf_op jit(solution)/shard_map/pallas_call | solution.py:263
  14.6 0.0 collective-permute-done.2.x_ref
  14.7 0.1 shard_map.60
  14.8 0.0 collective-permute-start.3
  14.8 1.2 %collective-permute-done.3.refs_0_ = f32[8,8,1]{2,1,0:T(8,128)S(1)} collective-permute-done((f32[8,8,1]{2,1,0:T(8,128)S(1)}, f32[8,8,1]{2,1,0:T(8,128)S(1)}, u32[]{:S(2)}, u32[]{:S(2)}) %collective-permute-start.3) | collective-permute-done | bytes 288 | tf_op jit(solution)/shard_map/ppermute | solution.py:238
  16.0 0.2 shard_map.61.refs_0_
  16.3 1.6 %shard_map.62 = (f32[2,2,64,256]{3,2,1,0:T(8,128)S(1)}, f32[2,2,64,256]{3,2,1,0:T(8,128)S(1)}) custom-call(f32[8,2,8,1024]{3,2,1,0:T(8,128)S(1)} %shard_map.57.base_ref, bf16[8,2,8,1024]{3,2,1,0:T(8,128)(2,1)S(1)} %shard_map.61.refs_0_, f32[2,2,1024]{2,1,0:T(2,128)S(1)} %copy-done.2, bf16[4,1024,512]{2,1,0:T(8,128)(2,1)S(1)} %shard_map.58.refs_2_.refs_3_, ...), custom_call_target="tpu_custom_call" | custom-call | flops 8 | bytes 8 | tf_op jit(solution)/shard_map/pallas_call | solution.py:263
  17.9 0.0 copy-start.4
  17.9 0.0 collective-permute-done.1.refs_1_
  17.9 0.0 collective-permute-done.6.white_ref
  17.9 0.1 shard_map.64.base_ref
  18.0 2.5 %shard_map.65 = (f32[2,2,64,256]{3,2,1,0:T(8,128)S(1)}, f32[2,2,64,256]{3,2,1,0:T(8,128)S(1)}) custom-call(f32[8,2,8,1024]{3,2,1,0:T(8,128)S(1)} %shard_map.64.base_ref, bf16[8,2,8,1024]{3,2,1,0:T(8,128)(2,1)S(1)} %shard_map.61.refs_0_, bf16[8,2,8,1024]{3,2,1,0:T(8,128)(2,1)S(1)} %collective-permute-done.1.refs_1_, f32[2,2,1024]{2,1,0:T(2,128)S(1)} %copy-done.2, ...), custom_call_target="tpu_custom_call" | custom-call | flops 8 | bytes 8 | tf_op jit(solution)/shard_map/pallas_call | solution.py:263
  20.5 0.2 collective-permute-start.7
  20.7 0.4 %collective-permute-start.4 = (f32[2,2,64,256]{3,2,1,0:T(8,128)S(1)}, f32[2,2,64,256]{3,2,1,0:T(8,128)S(1)}, u32[]{:S(2)}, u32[]{:S(2)}) collective-permute-start(f32[2,2,64,256]{3,2,1,0:T(8,128)S(1)} %get-tuple-element.39), channel_id=1, source_target_pairs={{0,1},{1,0},{2,3},{3,2},{4,5},{5,4},{6,7},{7,6},{8,9},{9,8},{10,11... | collective-permute-start | bytes 786440 | tf_op jit(solution)/shard_map/ppermute | solution.py:279
  21.1 1.0 %collective-permute-done.7.refs_1_ = f32[2,2,64,256]{3,2,1,0:T(8,128)S(1)} collective-permute-done((f32[2,2,64,256]{3,2,1,0:T(8,128)S(1)}, f32[2,2,64,256]{3,2,1,0:T(8,128)S(1)}, u32[]{:S(2)}, u32[]{:S(2)}) %collective-permute-start.7) | collective-permute-done | bytes 262176 | tf_op jit(solution)/shard_map/ppermute | solution.py:279
  22.1 1.3 %collective-permute-start.8 = (bf16[2,64,256]{2,1,0:T(8,128)(2,1)S(1)}, bf16[2,64,256]{2,1,0:T(8,128)(2,1)S(1)}, u32[]{:S(2)}, u32[]{:S(2)}) collective-permute-start(bf16[2,64,256]{2,1,0:T(8,128)(2,1)S(1)} %get-tuple-element.47), channel_id=1, source_target_pairs={{4,0},{8,4},{5,1},{9,5},{6,2},{10,6},{7,3},{11,7},{20,16},{24,20},... | collective-permute-start | bytes 196616 | tf_op jit(solution)/shard_map/ppermute | solution.py:320
  23.4 1.3 %collective-permute-start.9 = (bf16[2,64,256]{2,1,0:T(8,128)(2,1)S(1)}, bf16[2,64,256]{2,1,0:T(8,128)(2,1)S(1)}, u32[]{:S(2)}, u32[]{:S(2)}) collective-permute-start(bf16[2,64,256]{2,1,0:T(8,128)(2,1)S(1)} %get-tuple-element.48), channel_id=1, source_target_pairs={{4,2},{6,0},{8,6},{10,4},{5,3},{7,1},{9,7},{11,5},{20,18},{22,16},... | collective-permute-start | bytes 196616 | tf_op jit(solution)/shard_map/ppermute | solution.py:325
  24.7 0.0 collective-permute-done.4.refs_1_
  24.8 2.0 %collective-permute-start.5 = (bf16[2,64,256]{2,1,0:T(8,128)(2,1)S(1)}, bf16[2,64,256]{2,1,0:T(8,128)(2,1)S(1)}, u32[]{:S(2)}, u32[]{:S(2)}) collective-permute-start(bf16[2,64,256]{2,1,0:T(8,128)(2,1)S(1)} %get-tuple-element.41), channel_id=1, source_target_pairs={{0,2},{2,0},{1,3},{3,1},{4,6},{6,4},{5,7},{7,5},{8,10},{10,8},{9,1... | collective-permute-start | bytes 196616 | tf_op jit(solution)/shard_map/ppermute | solution.py:279
  26.8 0.0 copy-done.4
  26.8 0.1 broadcast_in_dim.3
  26.9 0.1 broadcast_in_dim_reshape.4.factor_ref
  27.0 1.4 %collective-permute-done.8.refs_2_ = bf16[2,64,256]{2,1,0:T(8,128)(2,1)S(1)} collective-permute-done((bf16[2,64,256]{2,1,0:T(8,128)(2,1)S(1)}, bf16[2,64,256]{2,1,0:T(8,128)(2,1)S(1)}, u32[]{:S(2)}, u32[]{:S(2)}) %collective-permute-start.8) | collective-permute-done | bytes 65568 | tf_op jit(solution)/shard_map/ppermute | solution.py:320
  28.3 3.2 %collective-permute-done.9.refs_3_ = bf16[2,64,256]{2,1,0:T(8,128)(2,1)S(1)} collective-permute-done((bf16[2,64,256]{2,1,0:T(8,128)(2,1)S(1)}, bf16[2,64,256]{2,1,0:T(8,128)(2,1)S(1)}, u32[]{:S(2)}, u32[]{:S(2)}) %collective-permute-start.9) | collective-permute-done | bytes 65568 | tf_op jit(solution)/shard_map/ppermute | solution.py:325
  31.6 0.0 collective-permute-done.5.refs_1_
  31.6 0.9 %shard_map.67 = f32[8,4,8,256]{3,2,1,0:T(8,128)} custom-call(f32[4,64,1]{2,1,0:T(8,128)S(1)} %broadcast_in_dim_reshape.4.factor_ref, f32[2,64,256]{2,1,0:T(8,128)S(1)} %get-tuple-element.40.refs_0_, bf16[2,64,256]{2,1,0:T(8,128)(2,1)S(1)} %collective-permute-done.5.refs_1_, bf16[2,64,256]{2,1,0:T(8,128)(2,1)S(1)} %collective-permute-done.8.refs_2_, ...), custom_call_target="tpu_custom_call" | custom-call | tf_op jit(solution)/shard_map/pallas_call | solution.py:328
  (3 shorter events, 0.1 us)
Async XLA Ops:
  0.0 14.6 %collective-permute-start.2 = (bf16[8,2,8,1024]{3,2,1,0:T(8,128)(2,1)}, bf16[8,2,8,1024]{3,2,1,0:T(8,128)(2,1)S(1)}, u32[]{:S(2)}, u32[]{:S(2)}) collective-permute-start(bf16[8,2,8,1024]{3,2,1,0:T(8,128)(2,1)} %x_ref.1), channel_id=1, source_target_pairs={{4,0},{8,4},{12,8},{5,1},{9,5},{13,9},{6,2},{10,6},{14,10},{7,3},{... | collective-permute-start | bytes 786440 | tf_op jit(solution)/shard_map/ppermute | solution.py:26
  1.3 1.0 %copy-start.1 = (bf16[8,2,8,1024]{3,2,1,0:T(8,128)(2,1)S(1)}, bf16[8,2,8,1024]{3,2,1,0:T(8,128)(2,1)}, u32[]{:S(2)}) copy-start(bf16[8,2,8,1024]{3,2,1,0:T(8,128)(2,1)} %x_ref.1) | copy-start | bytes 786436
  2.2 10.7 %copy-start.3 = (s32[8]{0:T(128)S(1)}, s32[8]{0:T(128)}, u32[]{:S(2)}) copy-start(s32[8]{0:T(128)} %param.6) | copy-start | bytes 100
  2.2 10.8 %copy-start.2 = (f32[2,2,1024]{2,1,0:T(2,128)S(1)}, f32[2,2,1024]{2,1,0:T(2,128)}, u32[]{:S(2)}) copy-start(f32[2,2,1024]{2,1,0:T(2,128)} %constant.6.clone.refs_1_.refs_2_) | copy-start | bytes 49156
  2.4 1.3 %collective-permute-start = (f32[8,8,1]{2,1,0:T(8,128)S(1)}, f32[8,8,1]{2,1,0:T(8,128)S(1)}, u32[]{:S(2)}, u32[]{:S(2)}) collective-permute-start(f32[8,8,1]{2,1,0:T(8,128)S(1)} %get-tuple-element.28), channel_id=1, source_target_pairs={{0,1},{1,0},{2,3},{3,2},{4,5},{5,4},{6,7},{7,6},{8,9},{9,8},{10,11... | collective-permute-start | bytes 776 | tf_op jit(solution)/shard_map/ppermute | solution.py:238
  3.9 13.9 %collective-permute-start.1 = (bf16[8,2,8,1024]{3,2,1,0:T(8,128)(2,1)S(1)}, bf16[8,2,8,1024]{3,2,1,0:T(8,128)(2,1)S(1)}, u32[]{:S(2)}, u32[]{:S(2)}) collective-permute-start(bf16[8,2,8,1024]{3,2,1,0:T(8,128)(2,1)S(1)} %shard_map.56.white_ref.refs_0_), channel_id=1, source_target_pairs={{12,4},{13,5},{14,6},{15,7},{28,20},{29,21},{30,22},{31,23}} | collective-permute-start | bytes 786440 | tf_op jit(solution)/shard_map/ppermute | solution.py:298
  4.6 13.2 %collective-permute-start.6 = (bf16[8,2,8,1024]{3,2,1,0:T(8,128)(2,1)S(1)}, bf16[8,2,8,1024]{3,2,1,0:T(8,128)(2,1)S(1)}, u32[]{:S(2)}, u32[]{:S(2)}) collective-permute-start(bf16[8,2,8,1024]{3,2,1,0:T(8,128)(2,1)S(1)} %shard_map.56.white_ref.refs_0_), channel_id=1, source_target_pairs={{0,4},{4,8},{1,5},{5,9},{2,6},{6,10},{3,7},{7,11},{16,20},{20,24},... | collective-permute-start | bytes 786440 | tf_op jit(solution)/shard_map/ppermute | solution.py:299
  10.7 1.0 %copy-start = (f32[2,96,512]{2,1,0:T(8,128)S(1)}, f32[2,96,512]{2,1,0:T(8,128)}, u32[]{:S(2)}) copy-start(f32[2,96,512]{2,1,0:T(8,128)} %constant.7.clone.base_ref) | copy-start | bytes 1179652
  14.8 1.2 %collective-permute-start.3 = (f32[8,8,1]{2,1,0:T(8,128)S(1)}, f32[8,8,1]{2,1,0:T(8,128)S(1)}, u32[]{:S(2)}, u32[]{:S(2)}) collective-permute-start(f32[8,8,1]{2,1,0:T(8,128)S(1)} %shard_map.60), channel_id=1, source_target_pairs={{0,1},{1,0},{2,3},{3,2},{4,5},{5,4},{6,7},{7,6},{8,9},{9,8},{10,11... | collective-permute-start | bytes 776 | tf_op jit(solution)/shard_map/ppermute | solution.py:238
  17.9 8.9 %copy-start.4 = (s32[8,4]{0,1:T(4,128)S(1)}, s32[8,4]{0,1:T(4,128)}, u32[]{:S(2)}) copy-start(s32[8,4]{0,1:T(4,128)} %param.7) | copy-start | bytes 388
  20.5 1.6 %collective-permute-start.7 = (f32[2,2,64,256]{3,2,1,0:T(8,128)S(1)}, f32[2,2,64,256]{3,2,1,0:T(8,128)S(1)}, u32[]{:S(2)}, u32[]{:S(2)}) collective-permute-start(f32[2,2,64,256]{3,2,1,0:T(8,128)S(1)} %get-tuple-element.46), channel_id=1, source_target_pairs={{0,1},{1,0},{2,3},{3,2},{4,5},{5,4},{6,7},{7,6},{8,9},{9,8},{10,11... | collective-permute-start | bytes 786440 | tf_op jit(solution)/shard_map/ppermute | solution.py:279
  20.7 4.0 %collective-permute-start.4 = (f32[2,2,64,256]{3,2,1,0:T(8,128)S(1)}, f32[2,2,64,256]{3,2,1,0:T(8,128)S(1)}, u32[]{:S(2)}, u32[]{:S(2)}) collective-permute-start(f32[2,2,64,256]{3,2,1,0:T(8,128)S(1)} %get-tuple-element.39), channel_id=1, source_target_pairs={{0,1},{1,0},{2,3},{3,2},{4,5},{5,4},{6,7},{7,6},{8,9},{9,8},{10,11... | collective-permute-start | bytes 786440 | tf_op jit(solution)/shard_map/ppermute | solution.py:279
  22.1 6.2 %collective-permute-start.8 = (bf16[2,64,256]{2,1,0:T(8,128)(2,1)S(1)}, bf16[2,64,256]{2,1,0:T(8,128)(2,1)S(1)}, u32[]{:S(2)}, u32[]{:S(2)}) collective-permute-start(bf16[2,64,256]{2,1,0:T(8,128)(2,1)S(1)} %get-tuple-element.47), channel_id=1, source_target_pairs={{4,0},{8,4},{5,1},{9,5},{6,2},{10,6},{7,3},{11,7},{20,16},{24,20},... | collective-permute-start | bytes 196616 | tf_op jit(solution)/shard_map/ppermute | solution.py:320
  23.4 8.1 %collective-permute-start.9 = (bf16[2,64,256]{2,1,0:T(8,128)(2,1)S(1)}, bf16[2,64,256]{2,1,0:T(8,128)(2,1)S(1)}, u32[]{:S(2)}, u32[]{:S(2)}) collective-permute-start(bf16[2,64,256]{2,1,0:T(8,128)(2,1)S(1)} %get-tuple-element.48), channel_id=1, source_target_pairs={{4,2},{6,0},{8,6},{10,4},{5,3},{7,1},{9,7},{11,5},{20,18},{22,16},... | collective-permute-start | bytes 196616 | tf_op jit(solution)/shard_map/ppermute | solution.py:325
  24.8 6.8 %collective-permute-start.5 = (bf16[2,64,256]{2,1,0:T(8,128)(2,1)S(1)}, bf16[2,64,256]{2,1,0:T(8,128)(2,1)S(1)}, u32[]{:S(2)}, u32[]{:S(2)}) collective-permute-start(bf16[2,64,256]{2,1,0:T(8,128)(2,1)S(1)} %get-tuple-element.41), channel_id=1, source_target_pairs={{0,2},{2,0},{1,3},{3,1},{4,6},{6,4},{5,7},{7,5},{8,10},{10,8},{9,1... | collective-permute-start | bytes 196616 | tf_op jit(solution)/shard_map/ppermute | solution.py:279

commit v17 on v16

--- a/solution.py
+++ b/solution.py
@@ -113,12 +113,8 @@
 def pairs_kernel(n_partners, n_win, n_freq, base_ref, *refs):
     partner_refs = refs[:n_partners]
     twist_ref, table_ref = refs[n_partners:n_partners + 2]
-    before_refs = refs[n_partners + 2:-2 - n_freq]
     out_refs = refs[-2 - n_freq:-2]
     rows_ref, sums_ref = refs[-2:]
-    done = out_refs[0].shape[0] - n_partners
-    for before_ref, out_ref in zip(before_refs, out_refs):
-        out_ref[:done] = before_ref[...]
     ch, f_dev = base_ref.shape[2:]
     pairs = ch * ch
     groups = n_win * n_freq
@@ -156,27 +152,22 @@
             lags = pl.ds(pl.multiple_of(block * width, LANES), width)
             for k in range(n_partners):
                 rows = slice(k * pairs, (k + 1) * pairs)
-                out_ref[done + k, turn_win] = sums_ref[0, rows, lags] + sign * sums_ref[1, rows, lags]
-
-
-def add_kernel(n_parts, n_before, *refs):
-    parts, befores, out_refs = refs[:n_parts], refs[n_parts:n_parts + n_before], refs[n_parts + n_before:]
-    for turn, out_ref in enumerate(out_refs):
-        start = 0
-        for before in befores:
-            out_ref[start:start + before.shape[0]] = before[:, turn].astype(out_ref.dtype)
-            start += before.shape[0]
-        total = parts[0][:, turn]
-        for ref in parts[1:]:
+                out_ref[k, turn_win] = sums_ref[0, rows, lags] + sign * sums_ref[1, rows, lags]
+
+
+def add_kernel(n_parts, *refs):
+    for turn, out_ref in enumerate(refs[n_parts:]):
+        total = refs[0][:, turn]
+        for ref in refs[1:n_parts]:
             total = total + ref[:, turn]
-        out_ref[start:] = total.astype(out_ref.dtype)
-
-
-def plain_add_kernel(*refs):
+        out_ref[...] = total.astype(out_ref.dtype)
+
+
+def total_kernel(*refs):
     total = refs[0][...]
     for ref in refs[1:-1]:
-        total = total + ref[...]
-    refs[-1][...] = total
+        total = total + ref[...].astype(jnp.float32)
+    refs[-1][...] = total.astype(refs[-1].dtype)
 
 
 def reverse_lanes(value):
@@ -193,8 +184,7 @@
     ch = out_ref.shape[0]
     lower = lax.axis_index("win") * n_freq + lax.axis_index("freq") < n_win * n_freq // 2
     k = 0
-    for first in range(0, len(refs) - 1, n_win):
-        parts = refs[first:first + n_win]
+    for parts in (refs[:n_win], refs[n_win:-1]):
         for n in range(parts[0].shape[0]):
             total = parts[0][n].astype(jnp.float32)
             for ref in parts[1:]:
@@ -258,19 +248,19 @@
             in_specs=[VMEM] * 2, out_specs=VMEM, compiler_params=params,
         )(keep.reshape(1, w_dev), block)
 
-    def pairs(base, partners, before=()):
-        n = len(partners) + (before[0].shape[0] if before else 0)
-        return pl.pallas_call(
-            functools.partial(pairs_kernel, len(partners), n_win, n_freq),
+    def pairs(base, partners):
+        n = len(partners)
+        return pl.pallas_call(
+            functools.partial(pairs_kernel, n, n_win, n_freq),
             out_shape=[jax.ShapeDtypeStruct((n, n_win, ch * ch, width), jnp.float32)] * n_freq,
-            in_specs=[VMEM] * (3 + len(partners) + len(before)), out_specs=[VMEM] * n_freq,
+            in_specs=[VMEM] * (3 + n), out_specs=[VMEM] * n_freq,
             scratch_shapes=[
-                pltpu.VMEM((2, 2 * len(partners) * ch * ch, f_dev), jnp.bfloat16),
-                pltpu.VMEM((2, len(partners) * ch * ch, LAGS // 2), jnp.float32),
+                pltpu.VMEM((2, 2 * n * ch * ch, f_dev), jnp.bfloat16),
+                pltpu.VMEM((2, n * ch * ch, LAGS // 2), jnp.float32),
             ],
             compiler_params=params,
             cost_estimate=cost(ch, ch),
-        )(base, *partners, twist, table, *before)
+        )(base, *partners, twist, table)
 
     def turns(parts, axis, size):
         received = [parts[0]]
@@ -279,20 +269,13 @@
             received.append(lax.ppermute(parts[turn], axis, route))
         return received
 
-    def sum_bins(parts):
-        return pl.pallas_call(
-            plain_add_kernel,
-            out_shape=jax.ShapeDtypeStruct(parts[0].shape, jnp.float32),
-            in_specs=[VMEM] * n_freq, out_specs=VMEM, compiler_params=params,
+    def split_windows(parts, kinds):
+        n = parts[0].shape[0]
+        return pl.pallas_call(
+            functools.partial(add_kernel, n_freq),
+            out_shape=[jax.ShapeDtypeStruct((n, ch * ch, width), kind) for kind in kinds],
+            in_specs=[VMEM] * n_freq, out_specs=[VMEM] * n_win, compiler_params=params,
         )(*turns(parts, "freq", n_freq))
-
-    def split_windows(parts, before, kinds):
-        n = sum(part.shape[0] for part in before) + parts[0].shape[0]
-        return pl.pallas_call(
-            functools.partial(add_kernel, n_freq, len(before)),
-            out_shape=[jax.ShapeDtypeStruct((n, ch * ch, width), kind) for kind in kinds],
-            in_specs=[VMEM] * (n_freq + len(before)), out_specs=[VMEM] * n_win, compiler_params=params,
-        )(*turns(parts, "freq", n_freq), *before)
 
     white = whiten(copied, swap(power))
     far = [lax.ppermute(white, "chan", route) for route in far_routes]
@@ -307,29 +290,26 @@
         in_specs=[VMEM], out_specs=VMEM, compiler_params=params, cost_estimate=cost(ch, ch),
     )(ends)
     own = kept(white)
-    first = pairs(own, [white])
-    below, first = lax.optimization_barrier((below, first))
     below = whiten(below, swap(half_power(below)))
-    parts = pairs(own, [below], first)
+    parts = pairs(own, [white, below])
     far, parts = lax.optimization_barrier((far, parts))
     above, far = lax.optimization_barrier((above, far))
-    base = kept(above)
-    sums = split_windows(parts, [], [jnp.float32] + [jnp.bfloat16] * (n_win - 1))
-    shipped = split_windows(pairs(base, [below] + far), [], [jnp.bfloat16] * n_win)
-    received = turns(sums, "win", n_win)
-    received.append(lax.ppermute(shipped[0], "chan", [(c, c - 1) for c in range(1, n_chan - 1)]))
-    for turn in range(1, n_win):
-        route = [
-            (c * n_win + w, (c - 1) * n_win + (w + turn) % n_win) for c in range(1, n_chan - 1) for w in range(n_win)
-        ]
-        received.append(lax.ppermute(shipped[turn], ("chan", "win"), route))
+    kinds = [jnp.float32] + [jnp.bfloat16] * (n_win - 1)
+    near = turns(split_windows(parts, kinds), "win", n_win)
+    remote = turns(split_windows(pairs(kept(above), [below] + far), kinds), "win", n_win)
+    shipped = pl.pallas_call(
+        total_kernel,
+        out_shape=jax.ShapeDtypeStruct(remote[0].shape, jnp.bfloat16),
+        in_specs=[VMEM] * n_win, out_specs=VMEM, compiler_params=params,
+    )(*remote)
+    shipped = lax.ppermute(shipped, "chan", [(c, c - 1) for c in range(1, n_chan - 1)])
     scale = 1.0 / math.sqrt(w_dev * n_win * n_bins)
     factors = jnp.repeat(pair_mask.T.astype(jnp.float32) * scale, ch, axis=1)[..., None]
     return pl.pallas_call(
         functools.partial(combine_kernel, n_win, n_freq),
         out_shape=jax.ShapeDtypeStruct((ch, reach + 1, ch, width), jnp.float32),
-        in_specs=[VMEM] * (1 + len(received)), out_specs=VMEM, compiler_params=params,
-    )(factors, *received)
+        in_specs=[VMEM] * (2 + n_win), out_specs=VMEM, compiler_params=params,
+    )(factors, *near, shipped)
 
 
 def solution(mesh):

time: 32.7 us -> 34 us (1.040)
  waiting for transfers between devices: 7.72 us -> 10.7 us
  starting transfers between devices: 13.7 us -> 12.6 us
  Pallas kernels: 8.76 us -> 8.1 us
    ppermute x3 -> x4, waiting for transfers between devices: 1.03 us -> 3.48 us  [turns(): received.append(lax.ppermute(parts[turn], axis, route))]
    ppermute x2 -> x1, starting transfers between devices: 2.58 us -> 1.29 us  [local(): lax.ppermute(shipped, 'chan', [(c, c - 1) for c in range(1, n_chan - 1)])]
    ppermute x2, waiting for transfers between devices: 2.05 us -> 0.86 us  [swap(): return [lax.ppermute(power, 'freq', route) for route in routes]]
    ppermute x2 -> x1, waiting for transfers between devices: 4.63 us -> 5.64 us  [local(): lax.ppermute(shipped, 'chan', [(c, c - 1) for c in range(1, n_chan - 1)])]
    ppermute x1, waiting for transfers between devices: 0.01 us -> 0.7 us  [from_behind(): return lax.ppermute(block, axis, route)]
    pallas_call x5, Pallas kernels: 5.74 us -> 5.09 us  [the longest x2 5.02 us: pairs(): pl.pallas_call(functools.partial(pairs_kernel, n, n_win, n_freq), out_sha...]
    ppermute x3 -> x4, starting transfers between devices: 2.56 us -> 2.81 us  [turns(): received.append(lax.ppermute(parts[turn], axis, route))]
  transfers between devices with their start and end apart: 10 -> 10, of which waited for: 5 -> 6; matrix products, arithmetic and copies ran while one was open for 1% -> 1% of each run, Pallas kernels for 16% -> 14%
where the time goes in v17:
time: 34 us; the launch traced here: 33.7 us
  starting transfers between devices  12.6 us (37%)
  waiting for transfers between devices  10.7 us (31%)
  Pallas kernels  8.1 us (24%)
  local copies, waits for them, and re-layouts  2.11 us (6%)
    ppermute x1, starting transfers between devices, local(): lax.ppermute(white, 'chan', [(c - 1, c) for c in range(1, n_chan - 1)])  6.09 us
    ppermute x1, waiting for transfers between devices, local(): lax.ppermute(shipped, 'chan', [(c, c - 1) for c in range(1, n_chan - 1)])  5.64 us
    pallas_call x2, Pallas kernels, pairs(): pl.pallas_call(functools.partial(pairs_kernel, n, n_win, n_freq), out_sha...  5.02 us
    ppermute x4, waiting for transfers between devices, turns(): received.append(lax.ppermute(parts[turn], axis, route))  3.48 us
    ppermute x4, starting transfers between devices, turns(): received.append(lax.ppermute(parts[turn], axis, route))  2.81 us
    unnamed x10, local copies, waits for them, and re-layouts  1.95 us
    ppermute x1, starting transfers between devices, local(): lax.ppermute(shipped, 'chan', [(c, c - 1) for c in range(1, n_chan - 1)])  1.29 us
    ppermute x1, starting transfers between devices, from_behind(): return lax.ppermute(block, axis, route)  1.28 us
  transfers between devices with their start and end apart: 10, of which 6 were waited for; matrix products, arithmetic and copies ran while one was open for 1% of the time, Pallas kernels for 14%

profile of v17, /device:TPU:0, one launch (start us, length us, event | category | flops | bytes accessed | tf_op | source)
XLA Modules:
  0.0 33.7 jit_solution(11059749818381648306)
XLA Ops:
  0.0 1.3 %collective-permute-start.2 = (bf16[8,2,8,1024]{3,2,1,0:T(8,128)(2,1)}, bf16[8,2,8,1024]{3,2,1,0:T(8,128)(2,1)S(1)}, u32[]{:S(2)}, u32[]{:S(2)}) collective-permute-start(bf16[8,2,8,1024]{3,2,1,0:T(8,128)(2,1)} %x_ref.1), channel_id=1, source_target_pairs={{4,0},{8,4},{12,8},{5,1},{9,5},{13,9},{6,2},{10,6},{14,10},{7,3},{... | collective-permute-start | bytes 786440 | tf_op jit(solution)/shard_map/ppermute | solution.py:26
  1.3 0.0 copy-start.1
  1.3 0.9 %copy-done.1 = bf16[8,2,8,1024]{3,2,1,0:T(8,128)(2,1)S(1)} copy-done((bf16[8,2,8,1024]{3,2,1,0:T(8,128)(2,1)S(1)}, bf16[8,2,8,1024]{3,2,1,0:T(8,128)(2,1)}, u32[]{:S(2)}) %copy-start.1) | copy-done | bytes 262168
  2.2 0.0 copy-start.3
  2.2 0.0 copy-start.2
  2.2 0.1 shard_map.55
  2.4 0.5 %collective-permute-start = (f32[8,8,1]{2,1,0:T(8,128)S(1)}, f32[8,8,1]{2,1,0:T(8,128)S(1)}, u32[]{:S(2)}, u32[]{:S(2)}) collective-permute-start(f32[8,8,1]{2,1,0:T(8,128)S(1)} %get-tuple-element.23), channel_id=1, source_target_pairs={{0,1},{1,0},{2,3},{3,2},{4,5},{5,4},{6,7},{7,6},{8,9},{9,8},{10,11... | collective-permute-start | bytes 776 | tf_op jit(solution)/shard_map/ppermute | solution.py:228
  2.8 0.9 %collective-permute-done.refs_0_ = f32[8,8,1]{2,1,0:T(8,128)S(1)} collective-permute-done((f32[8,8,1]{2,1,0:T(8,128)S(1)}, f32[8,8,1]{2,1,0:T(8,128)S(1)}, u32[]{:S(2)}, u32[]{:S(2)}) %collective-permute-start) | collective-permute-done | bytes 288 | tf_op jit(solution)/shard_map/ppermute | solution.py:228
  3.7 0.2 shard_map.56.white_ref.refs_0_
  3.9 0.7 %collective-permute-start.1 = (bf16[8,2,8,1024]{3,2,1,0:T(8,128)(2,1)S(1)}, bf16[8,2,8,1024]{3,2,1,0:T(8,128)(2,1)S(1)}, u32[]{:S(2)}, u32[]{:S(2)}) collective-permute-start(bf16[8,2,8,1024]{3,2,1,0:T(8,128)(2,1)S(1)} %shard_map.56.white_ref.refs_0_), channel_id=1, source_target_pairs={{12,4},{13,5},{14,6},{15,7},{28,20},{29,21},{30,22},{31,23}} | collective-permute-start | bytes 786440 | tf_op jit(solution)/shard_map/ppermute | solution.py:281
  4.6 6.1 %collective-permute-start.6 = (bf16[8,2,8,1024]{3,2,1,0:T(8,128)(2,1)S(1)}, bf16[8,2,8,1024]{3,2,1,0:T(8,128)(2,1)S(1)}, u32[]{:S(2)}, u32[]{:S(2)}) collective-permute-start(bf16[8,2,8,1024]{3,2,1,0:T(8,128)(2,1)S(1)} %shard_map.56.white_ref.refs_0_), channel_id=1, source_target_pairs={{0,4},{4,8},{1,5},{5,9},{2,6},{6,10},{3,7},{7,11},{16,20},{20,24},... | collective-permute-start | bytes 786440 | tf_op jit(solution)/shard_map/ppermute | solution.py:282
  10.7 0.7 %collective-permute-done.2.x_ref = bf16[8,2,8,1024]{3,2,1,0:T(8,128)(2,1)S(1)} collective-permute-done((bf16[8,2,8,1024]{3,2,1,0:T(8,128)(2,1)}, bf16[8,2,8,1024]{3,2,1,0:T(8,128)(2,1)S(1)}, u32[]{:S(2)}, u32[]{:S(2)}) %collective-permute-start.2) | collective-permute-done | bytes 262176 | tf_op jit(solution)/shard_map/ppermute | solution.py:26
  11.4 0.1 shard_map.58
  11.6 0.0 collective-permute-start.3
  11.6 0.0 copy-start
  11.6 1.0 %copy-done = f32[2,96,512]{2,1,0:T(8,128)S(1)} copy-done((f32[2,96,512]{2,1,0:T(8,128)S(1)}, f32[2,96,512]{2,1,0:T(8,128)}, u32[]{:S(2)}) %copy-start) | copy-done | bytes 393240
  12.6 1.2 %shard_map.60.refs_3_ = bf16[4,1024,512]{2,1,0:T(8,128)(2,1)S(1)} custom-call(f32[2,96,512]{2,1,0:T(8,128)S(1)} %copy-done), custom_call_target="tpu_custom_call" | custom-call | flops 8 | bytes 8 | tf_op jit(solution)/shard_map/pallas_call | solution.py:287
  13.8 0.0 copy-done.3
  13.8 0.1 shard_map.57.base_ref
  13.9 0.0 collective-permute-done.3.refs_0_
  13.9 0.2 shard_map.59.refs_1_.refs_0_
  14.2 0.0 copy-done.2
  14.2 2.5 %shard_map.61 = (f32[2,2,64,256]{3,2,1,0:T(8,128)S(1)}, f32[2,2,64,256]{3,2,1,0:T(8,128)S(1)}) custom-call(f32[8,2,8,1024]{3,2,1,0:T(8,128)S(1)} %shard_map.57.base_ref, bf16[8,2,8,1024]{3,2,1,0:T(8,128)(2,1)S(1)} %shard_map.56.white_ref.refs_0_, bf16[8,2,8,1024]{3,2,1,0:T(8,128)(2,1)S(1)} %shard_map.59.refs_1_.refs_0_, f32[2,2,1024]{2,1,0:T(2,128)S(1)} %copy-done.2, ...), custom_call_target="tpu_custom_call" | custom-call | flops 8 | bytes 8 | tf_op jit(solution)/shard_map/pallas_call | solution.py:253
  16.7 0.0 copy-start.4
  16.7 0.0 collective-permute-done.1.refs_1_
  16.7 0.0 collective-permute-done.6.white_ref
  16.7 0.1 shard_map.63.base_ref
  16.8 2.5 %shard_map.64 = (f32[2,2,64,256]{3,2,1,0:T(8,128)S(1)}, f32[2,2,64,256]{3,2,1,0:T(8,128)S(1)}) custom-call(f32[8,2,8,1024]{3,2,1,0:T(8,128)S(1)} %shard_map.63.base_ref, bf16[8,2,8,1024]{3,2,1,0:T(8,128)(2,1)S(1)} %shard_map.59.refs_1_.refs_0_, bf16[8,2,8,1024]{3,2,1,0:T(8,128)(2,1)S(1)} %collective-permute-done.1.refs_1_, f32[2,2,1024]{2,1,0:T(2,128)S(1)} %copy-done.2, ...), custom_call_target="tpu_custom_call" | custom-call | flops 8 | bytes 8 | tf_op jit(solution)/shard_map/pallas_call | solution.py:253
  19.3 0.6 %collective-permute-start.7 = (f32[2,2,64,256]{3,2,1,0:T(8,128)S(1)}, f32[2,2,64,256]{3,2,1,0:T(8,128)S(1)}, u32[]{:S(2)}, u32[]{:S(2)}) collective-permute-start(f32[2,2,64,256]{3,2,1,0:T(8,128)S(1)} %get-tuple-element.36), channel_id=1, source_target_pairs={{0,1},{1,0},{2,3},{3,2},{4,5},{5,4},{6,7},{7,6},{8,9},{9,8},{10,11... | collective-permute-start | bytes 786440 | tf_op jit(solution)/shard_map/ppermute | solution.py:269
  19.9 0.1 collective-permute-start.4
  20.0 1.1 %collective-permute-done.7.refs_1_ = f32[2,2,64,256]{3,2,1,0:T(8,128)S(1)} collective-permute-done((f32[2,2,64,256]{3,2,1,0:T(8,128)S(1)}, f32[2,2,64,256]{3,2,1,0:T(8,128)S(1)}, u32[]{:S(2)}, u32[]{:S(2)}) %collective-permute-start.7) | collective-permute-done | bytes 262176 | tf_op jit(solution)/shard_map/ppermute | solution.py:269
  21.1 1.7 %collective-permute-start.8 = (bf16[2,64,256]{2,1,0:T(8,128)(2,1)S(1)}, bf16[2,64,256]{2,1,0:T(8,128)(2,1)S(1)}, u32[]{:S(2)}, u32[]{:S(2)}) collective-permute-start(bf16[2,64,256]{2,1,0:T(8,128)(2,1)S(1)} %get-tuple-element.38), channel_id=1, source_target_pairs={{0,2},{2,0},{1,3},{3,1},{4,6},{6,4},{5,7},{7,5},{8,10},{10,8},{9,1... | collective-permute-start | bytes 196616 | tf_op jit(solution)/shard_map/ppermute | solution.py:269
  22.8 0.0 collective-permute-done.4.refs_1_
  22.9 0.4 %collective-permute-start.5 = (bf16[2,64,256]{2,1,0:T(8,128)(2,1)S(1)}, bf16[2,64,256]{2,1,0:T(8,128)(2,1)S(1)}, u32[]{:S(2)}, u32[]{:S(2)}) collective-permute-start(bf16[2,64,256]{2,1,0:T(8,128)(2,1)S(1)} %get-tuple-element.31), channel_id=1, source_target_pairs={{0,2},{2,0},{1,3},{3,1},{4,6},{6,4},{5,7},{7,5},{8,10},{10,8},{9,1... | collective-permute-start | bytes 196616 | tf_op jit(solution)/shard_map/ppermute | solution.py:269
  23.3 2.2 %collective-permute-done.8.refs_1_ = bf16[2,64,256]{2,1,0:T(8,128)(2,1)S(1)} collective-permute-done((bf16[2,64,256]{2,1,0:T(8,128)(2,1)S(1)}, bf16[2,64,256]{2,1,0:T(8,128)(2,1)S(1)}, u32[]{:S(2)}, u32[]{:S(2)}) %collective-permute-start.8) | collective-permute-done | bytes 65568 | tf_op jit(solution)/shard_map/ppermute | solution.py:269
  25.6 1.3 %collective-permute-start.9 = (bf16[2,64,256]{2,1,0:T(8,128)(2,1)S(1)}, bf16[2,64,256]{2,1,0:T(8,128)(2,1)S(1)}, u32[]{:S(2)}, u32[]{:S(2)}) collective-permute-start(bf16[2,64,256]{2,1,0:T(8,128)(2,1)S(1)} %shard_map.66), channel_id=1, source_target_pairs={{4,0},{8,4},{5,1},{9,5},{6,2},{10,6},{7,3},{11,7},{20,16},{24,20},... | collective-permute-start | bytes 196616 | tf_op jit(solution)/shard_map/ppermute | solution.py:305
  26.9 0.0 copy-done.4
  26.9 0.1 broadcast_in_dim.3
  26.9 0.1 broadcast_in_dim_reshape.4.factor_ref
  27.0 0.2 collective-permute-done.5.refs_1_
  27.2 5.6 %collective-permute-done.9.refs_2_ = bf16[2,64,256]{2,1,0:T(8,128)(2,1)S(1)} collective-permute-done((bf16[2,64,256]{2,1,0:T(8,128)(2,1)S(1)}, bf16[2,64,256]{2,1,0:T(8,128)(2,1)S(1)}, u32[]{:S(2)}, u32[]{:S(2)}) %collective-permute-start.9) | collective-permute-done | bytes 65568 | tf_op jit(solution)/shard_map/ppermute | solution.py:305
  32.8 0.9 %shard_map.67 = f32[8,4,8,256]{3,2,1,0:T(8,128)} custom-call(f32[4,64,1]{2,1,0:T(8,128)S(1)} %broadcast_in_dim_reshape.4.factor_ref, f32[2,64,256]{2,1,0:T(8,128)S(1)} %get-tuple-element.30.refs_0_, bf16[2,64,256]{2,1,0:T(8,128)(2,1)S(1)} %collective-permute-done.5.refs_1_, bf16[2,64,256]{2,1,0:T(8,128)(2,1)S(1)} %collective-permute-done.9.refs_2_), custom_call_target="tpu_custom_call" | custom-call | tf_op jit(solution)/shard_map/pallas_call | solution.py:308
  (4 shorter events, 0.1 us)
Async XLA Ops:
  0.0 11.4 %collective-permute-start.2 = (bf16[8,2,8,1024]{3,2,1,0:T(8,128)(2,1)}, bf16[8,2,8,1024]{3,2,1,0:T(8,128)(2,1)S(1)}, u32[]{:S(2)}, u32[]{:S(2)}) collective-permute-start(bf16[8,2,8,1024]{3,2,1,0:T(8,128)(2,1)} %x_ref.1), channel_id=1, source_target_pairs={{4,0},{8,4},{12,8},{5,1},{9,5},{13,9},{6,2},{10,6},{14,10},{7,3},{... | collective-permute-start | bytes 786440 | tf_op jit(solution)/shard_map/ppermute | solution.py:26
  1.3 1.0 %copy-start.1 = (bf16[8,2,8,1024]{3,2,1,0:T(8,128)(2,1)S(1)}, bf16[8,2,8,1024]{3,2,1,0:T(8,128)(2,1)}, u32[]{:S(2)}) copy-start(bf16[8,2,8,1024]{3,2,1,0:T(8,128)(2,1)} %x_ref.1) | copy-start | bytes 786436
  2.2 11.5 %copy-start.3 = (s32[8]{0:T(128)S(1)}, s32[8]{0:T(128)}, u32[]{:S(2)}) copy-start(s32[8]{0:T(128)} %param.6) | copy-start | bytes 100
  2.2 11.9 %copy-start.2 = (f32[2,2,1024]{2,1,0:T(2,128)S(1)}, f32[2,2,1024]{2,1,0:T(2,128)}, u32[]{:S(2)}) copy-start(f32[2,2,1024]{2,1,0:T(2,128)} %constant.6.clone.refs_2_) | copy-start | bytes 49156
  2.4 1.3 %collective-permute-start = (f32[8,8,1]{2,1,0:T(8,128)S(1)}, f32[8,8,1]{2,1,0:T(8,128)S(1)}, u32[]{:S(2)}, u32[]{:S(2)}) collective-permute-start(f32[8,8,1]{2,1,0:T(8,128)S(1)} %get-tuple-element.23), channel_id=1, source_target_pairs={{0,1},{1,0},{2,3},{3,2},{4,5},{5,4},{6,7},{7,6},{8,9},{9,8},{10,11... | collective-permute-start | bytes 776 | tf_op jit(solution)/shard_map/ppermute | solution.py:228
  3.9 12.8 %collective-permute-start.1 = (bf16[8,2,8,1024]{3,2,1,0:T(8,128)(2,1)S(1)}, bf16[8,2,8,1024]{3,2,1,0:T(8,128)(2,1)S(1)}, u32[]{:S(2)}, u32[]{:S(2)}) collective-permute-start(bf16[8,2,8,1024]{3,2,1,0:T(8,128)(2,1)S(1)} %shard_map.56.white_ref.refs_0_), channel_id=1, source_target_pairs={{12,4},{13,5},{14,6},{15,7},{28,20},{29,21},{30,22},{31,23}} | collective-permute-start | bytes 786440 | tf_op jit(solution)/shard_map/ppermute | solution.py:281
  4.6 12.1 %collective-permute-start.6 = (bf16[8,2,8,1024]{3,2,1,0:T(8,128)(2,1)S(1)}, bf16[8,2,8,1024]{3,2,1,0:T(8,128)(2,1)S(1)}, u32[]{:S(2)}, u32[]{:S(2)}) collective-permute-start(bf16[8,2,8,1024]{3,2,1,0:T(8,128)(2,1)S(1)} %shard_map.56.white_ref.refs_0_), channel_id=1, source_target_pairs={{0,4},{4,8},{1,5},{5,9},{2,6},{6,10},{3,7},{7,11},{16,20},{20,24},... | collective-permute-start | bytes 786440 | tf_op jit(solution)/shard_map/ppermute | solution.py:282
  11.6 2.3 %collective-permute-start.3 = (f32[8,8,1]{2,1,0:T(8,128)S(1)}, f32[8,8,1]{2,1,0:T(8,128)S(1)}, u32[]{:S(2)}, u32[]{:S(2)}) collective-permute-start(f32[8,8,1]{2,1,0:T(8,128)S(1)} %shard_map.58), channel_id=1, source_target_pairs={{0,1},{1,0},{2,3},{3,2},{4,5},{5,4},{6,7},{7,6},{8,9},{9,8},{10,11... | collective-permute-start | bytes 776 | tf_op jit(solution)/shard_map/ppermute | solution.py:228
  11.6 1.0 %copy-start = (f32[2,96,512]{2,1,0:T(8,128)S(1)}, f32[2,96,512]{2,1,0:T(8,128)}, u32[]{:S(2)}) copy-start(f32[2,96,512]{2,1,0:T(8,128)} %constant.7.clone.base_ref) | copy-start | bytes 1179652
  16.7 10.2 %copy-start.4 = (s32[8,4]{0,1:T(4,128)S(1)}, s32[8,4]{0,1:T(4,128)}, u32[]{:S(2)}) copy-start(s32[8,4]{0,1:T(4,128)} %param.7) | copy-start | bytes 388
  19.3 1.7 %collective-permute-start.7 = (f32[2,2,64,256]{3,2,1,0:T(8,128)S(1)}, f32[2,2,64,256]{3,2,1,0:T(8,128)S(1)}, u32[]{:S(2)}, u32[]{:S(2)}) collective-permute-start(f32[2,2,64,256]{3,2,1,0:T(8,128)S(1)} %get-tuple-element.36), channel_id=1, source_target_pairs={{0,1},{1,0},{2,3},{3,2},{4,5},{5,4},{6,7},{7,6},{8,9},{9,8},{10,11... | collective-permute-start | bytes 786440 | tf_op jit(solution)/shard_map/ppermute | solution.py:269
  19.9 2.9 %collective-permute-start.4 = (f32[2,2,64,256]{3,2,1,0:T(8,128)S(1)}, f32[2,2,64,256]{3,2,1,0:T(8,128)S(1)}, u32[]{:S(2)}, u32[]{:S(2)}) collective-permute-start(f32[2,2,64,256]{3,2,1,0:T(8,128)S(1)} %get-tuple-element.29), channel_id=1, source_target_pairs={{0,1},{1,0},{2,3},{3,2},{4,5},{5,4},{6,7},{7,6},{8,9},{9,8},{10,11... | collective-permute-start | bytes 786440 | tf_op jit(solution)/shard_map/ppermute | solution.py:269
  21.1 4.4 %collective-permute-start.8 = (bf16[2,64,256]{2,1,0:T(8,128)(2,1)S(1)}, bf16[2,64,256]{2,1,0:T(8,128)(2,1)S(1)}, u32[]{:S(2)}, u32[]{:S(2)}) collective-permute-start(bf16[2,64,256]{2,1,0:T(8,128)(2,1)S(1)} %get-tuple-element.38), channel_id=1, source_target_pairs={{0,2},{2,0},{1,3},{3,1},{4,6},{6,4},{5,7},{7,5},{8,10},{10,8},{9,1... | collective-permute-start | bytes 196616 | tf_op jit(solution)/shard_map/ppermute | solution.py:269
  22.9 4.3 %collective-permute-start.5 = (bf16[2,64,256]{2,1,0:T(8,128)(2,1)S(1)}, bf16[2,64,256]{2,1,0:T(8,128)(2,1)S(1)}, u32[]{:S(2)}, u32[]{:S(2)}) collective-permute-start(bf16[2,64,256]{2,1,0:T(8,128)(2,1)S(1)} %get-tuple-element.31), channel_id=1, source_target_pairs={{0,2},{2,0},{1,3},{3,1},{4,6},{6,4},{5,7},{7,5},{8,10},{10,8},{9,1... | collective-permute-start | bytes 196616 | tf_op jit(solution)/shard_map/ppermute | solution.py:269
  25.6 7.3 %collective-permute-start.9 = (bf16[2,64,256]{2,1,0:T(8,128)(2,1)S(1)}, bf16[2,64,256]{2,1,0:T(8,128)(2,1)S(1)}, u32[]{:S(2)}, u32[]{:S(2)}) collective-permute-start(bf16[2,64,256]{2,1,0:T(8,128)(2,1)S(1)} %shard_map.66), channel_id=1, source_target_pairs={{4,0},{8,4},{5,1},{9,5},{6,2},{10,6},{7,3},{11,7},{20,16},{24,20},... | collective-permute-start | bytes 196616 | tf_op jit(solution)/shard_map/ppermute | solution.py:305

commit v18 on v17

--- a/solution.py
+++ b/solution.py
@@ -110,7 +110,7 @@
     return real, imag
 
 
-def pairs_kernel(n_partners, n_win, n_freq, base_ref, *refs):
+def pairs_kernel(n_partners, n_win, n_freq, by_window, base_ref, *refs):
     partner_refs = refs[:n_partners]
     twist_ref, table_ref = refs[n_partners:n_partners + 2]
     out_refs = refs[-2 - n_freq:-2]
@@ -144,8 +144,13 @@
         both = dot(rows_ref[part], table_ref[2 * part])
         sums_ref[part] = both[:count] + both[count:] + dot(rows_ref[part, :count], table_ref[2 * part + 1])
     for turn_freq, out_ref in enumerate(out_refs):
+        core = (freq + turn_freq) % n_freq
         for turn_win in range(n_win):
-            owner = (win + turn_win) % n_win * n_freq + (freq + turn_freq) % n_freq
+            if by_window:
+                away = turn_win // n_freq * n_freq + core
+                owner = (win + away) % n_win * n_freq + (core + turn_win) % n_freq
+            else:
+                owner = (win + turn_win) % n_win * n_freq + core
             upper = owner >= groups // 2
             block = jnp.where(upper, owner - groups // 2, groups // 2 - 1 - owner)
             sign = jnp.where(upper, -1.0, 1.0)
@@ -163,11 +168,23 @@
         out_ref[...] = total.astype(out_ref.dtype)
 
 
-def total_kernel(*refs):
-    total = refs[0][...]
-    for ref in refs[1:-1]:
-        total = total + ref[...].astype(jnp.float32)
-    refs[-1][...] = total.astype(refs[-1].dtype)
+def group_kernel(n_parts, *refs):
+    out_refs = refs[n_parts:]
+    per_ship = refs[0].shape[1] // len(out_refs)
+    for ship, out_ref in enumerate(out_refs):
+        for turn in range(per_ship):
+            total = refs[0][:, ship * per_ship + turn]
+            for ref in refs[1:n_parts]:
+                total = total + ref[:, ship * per_ship + turn]
+            out_ref[turn] = total.astype(out_ref.dtype)
+
+
+def ungroup_kernel(n_ships, *refs):
+    for turn, out_ref in enumerate(refs[n_ships:]):
+        total = refs[0][turn].astype(jnp.float32)
+        for ref in refs[1:n_ships]:
+            total = total + ref[turn].astype(jnp.float32)
+        out_ref[...] = total
 
 
 def reverse_lanes(value):
@@ -248,10 +265,10 @@
             in_specs=[VMEM] * 2, out_specs=VMEM, compiler_params=params,
         )(keep.reshape(1, w_dev), block)
 
-    def pairs(base, partners):
+    def pairs(base, partners, by_window):
         n = len(partners)
         return pl.pallas_call(
-            functools.partial(pairs_kernel, n, n_win, n_freq),
+            functools.partial(pairs_kernel, n, n_win, n_freq, by_window),
             out_shape=[jax.ShapeDtypeStruct((n, n_win, ch * ch, width), jnp.float32)] * n_freq,
             in_specs=[VMEM] * (3 + n), out_specs=[VMEM] * n_freq,
             scratch_shapes=[
@@ -291,25 +308,39 @@
     )(ends)
     own = kept(white)
     below = whiten(below, swap(half_power(below)))
-    parts = pairs(own, [white, below])
+    parts = pairs(own, [white, below], False)
     far, parts = lax.optimization_barrier((far, parts))
     above, far = lax.optimization_barrier((above, far))
     kinds = [jnp.float32] + [jnp.bfloat16] * (n_win - 1)
     near = turns(split_windows(parts, kinds), "win", n_win)
-    remote = turns(split_windows(pairs(kept(above), [below] + far), kinds), "win", n_win)
+    remote = turns(pairs(kept(above), [below] + far, True), "freq", n_freq)
+    shape = (remote[0].shape[0], ch * ch, width)
+    n_ships = n_win // n_freq
     shipped = pl.pallas_call(
-        total_kernel,
-        out_shape=jax.ShapeDtypeStruct(remote[0].shape, jnp.bfloat16),
-        in_specs=[VMEM] * n_win, out_specs=VMEM, compiler_params=params,
+        functools.partial(group_kernel, n_freq),
+        out_shape=[jax.ShapeDtypeStruct((n_freq,) + shape, jnp.bfloat16)] * n_ships,
+        in_specs=[VMEM] * n_freq, out_specs=[VMEM] * n_ships, compiler_params=params,
     )(*remote)
-    shipped = lax.ppermute(shipped, "chan", [(c, c - 1) for c in range(1, n_chan - 1)])
+    arrived = []
+    for ship, block in enumerate(shipped):
+        route = [
+            ((c * n_win + w) * n_freq + f, ((c - 1) * n_win + (w + ship * n_freq + f) % n_win) * n_freq + f)
+            for c in range(1, n_chan - 1) for w in range(n_win) for f in range(n_freq)
+        ]
+        arrived.append(lax.ppermute(block, ("chan", "win", "freq"), route))
+    arrived = pl.pallas_call(
+        functools.partial(ungroup_kernel, n_ships),
+        out_shape=[jax.ShapeDtypeStruct(shape, jnp.float32)] * n_freq,
+        in_specs=[VMEM] * n_ships, out_specs=[VMEM] * n_freq, compiler_params=params,
+    )(*arrived)
+    arrived = turns(arrived, "freq", n_freq)
     scale = 1.0 / math.sqrt(w_dev * n_win * n_bins)
     factors = jnp.repeat(pair_mask.T.astype(jnp.float32) * scale, ch, axis=1)[..., None]
     return pl.pallas_call(
         functools.partial(combine_kernel, n_win, n_freq),
         out_shape=jax.ShapeDtypeStruct((ch, reach + 1, ch, width), jnp.float32),
-        in_specs=[VMEM] * (2 + n_win), out_specs=VMEM, compiler_params=params,
-    )(factors, *near, shipped)
+        in_specs=[VMEM] * (1 + n_win + n_freq), out_specs=VMEM, compiler_params=params,
+    )(factors, *near, *arrived)
 
 
 def solution(mesh):

time: 34 us -> 32.4 us (0.953)
  waiting for transfers between devices: 10.7 us -> 9.3 us
    ppermute x4, waiting for transfers between devices: 3.48 us -> 2.08 us  [turns(): received.append(lax.ppermute(parts[turn], axis, route))]
    pallas_call x3 -> x4, Pallas kernels: 5.03 us -> 5.06 us  [the longest x2 5.02 us: pairs(): pl.pallas_call(functools.partial(pairs_kernel, n, n_win, n_freq, by_windo...]
  transfers between devices with their start and end apart: 10 -> 10, of which waited for: 6 -> 5; matrix products, arithmetic and copies ran while one was open for 1% -> 1% of each run, Pallas kernels for 14% -> 14%
where the time goes in v18:
time: 32.4 us; the launch traced here: 32.2 us
  starting transfers between devices  12.4 us (38%)
  waiting for transfers between devices  9.3 us (29%)
  Pallas kernels  8.12 us (25%)
  local copies, waits for them, and re-layouts  2.12 us (7%)
    ppermute x1, starting transfers between devices, local(): lax.ppermute(white, 'chan', [(c - 1, c) for c in range(1, n_chan - 1)])  6.09 us
    ppermute x1, waiting for transfers between devices, local(): arrived.append(lax.ppermute(block, ('chan', 'win', 'freq'), route))  5.66 us
    pallas_call x2, Pallas kernels, pairs(): pl.pallas_call(functools.partial(pairs_kernel, n, n_win, n_freq, by_windo...  5.02 us
    ppermute x4, starting transfers between devices, turns(): received.append(lax.ppermute(parts[turn], axis, route))  2.61 us
    ppermute x4, waiting for transfers between devices, turns(): received.append(lax.ppermute(parts[turn], axis, route))  2.08 us
    unnamed x10, local copies, waits for them, and re-layouts  1.95 us
    ppermute x1, starting transfers between devices, local(): arrived.append(lax.ppermute(block, ('chan', 'win', 'freq'), route))  1.29 us
    ppermute x1, starting transfers between devices, from_behind(): return lax.ppermute(block, axis, route)  1.28 us
  transfers between devices with their start and end apart: 10, of which 5 were waited for; matrix products, arithmetic and copies ran while one was open for 1% of the time, Pallas kernels for 14%

profile of v18, /device:TPU:0, one launch (start us, length us, event | category | flops | bytes accessed | tf_op | source)
XLA Modules:
  0.0 32.2 jit_solution(2791567778056303548)
XLA Ops:
  0.0 1.3 %collective-permute-start.2 = (bf16[8,2,8,1024]{3,2,1,0:T(8,128)(2,1)}, bf16[8,2,8,1024]{3,2,1,0:T(8,128)(2,1)S(1)}, u32[]{:S(2)}, u32[]{:S(2)}) collective-permute-start(bf16[8,2,8,1024]{3,2,1,0:T(8,128)(2,1)} %x_ref.1), channel_id=1, source_target_pairs={{4,0},{8,4},{12,8},{5,1},{9,5},{13,9},{6,2},{10,6},{14,10},{7,3},{... | collective-permute-start | bytes 786440 | tf_op jit(solution)/shard_map/ppermute | solution.py:26
  1.3 0.0 copy-start.1
  1.3 0.9 %copy-done.1 = bf16[8,2,8,1024]{3,2,1,0:T(8,128)(2,1)S(1)} copy-done((bf16[8,2,8,1024]{3,2,1,0:T(8,128)(2,1)S(1)}, bf16[8,2,8,1024]{3,2,1,0:T(8,128)(2,1)}, u32[]{:S(2)}) %copy-start.1) | copy-done | bytes 262168
  2.2 0.0 copy-start.3
  2.2 0.0 copy-start.2
  2.2 0.1 shard_map.55
  2.4 0.5 %collective-permute-start = (f32[8,8,1]{2,1,0:T(8,128)S(1)}, f32[8,8,1]{2,1,0:T(8,128)S(1)}, u32[]{:S(2)}, u32[]{:S(2)}) collective-permute-start(f32[8,8,1]{2,1,0:T(8,128)S(1)} %get-tuple-element.23), channel_id=1, source_target_pairs={{0,1},{1,0},{2,3},{3,2},{4,5},{5,4},{6,7},{7,6},{8,9},{9,8},{10,11... | collective-permute-start | bytes 776 | tf_op jit(solution)/shard_map/ppermute | solution.py:245
  2.8 0.9 %collective-permute-done.refs_0_ = f32[8,8,1]{2,1,0:T(8,128)S(1)} collective-permute-done((f32[8,8,1]{2,1,0:T(8,128)S(1)}, f32[8,8,1]{2,1,0:T(8,128)S(1)}, u32[]{:S(2)}, u32[]{:S(2)}) %collective-permute-start) | collective-permute-done | bytes 288 | tf_op jit(solution)/shard_map/ppermute | solution.py:245
  3.7 0.2 shard_map.56.white_ref.refs_0_
  3.9 0.7 %collective-permute-start.1 = (bf16[8,2,8,1024]{3,2,1,0:T(8,128)(2,1)S(1)}, bf16[8,2,8,1024]{3,2,1,0:T(8,128)(2,1)S(1)}, u32[]{:S(2)}, u32[]{:S(2)}) collective-permute-start(bf16[8,2,8,1024]{3,2,1,0:T(8,128)(2,1)S(1)} %shard_map.56.white_ref.refs_0_), channel_id=1, source_target_pairs={{12,4},{13,5},{14,6},{15,7},{28,20},{29,21},{30,22},{31,23}} | collective-permute-start | bytes 786440 | tf_op jit(solution)/shard_map/ppermute | solution.py:298
  4.6 6.1 %collective-permute-start.6 = (bf16[8,2,8,1024]{3,2,1,0:T(8,128)(2,1)S(1)}, bf16[8,2,8,1024]{3,2,1,0:T(8,128)(2,1)S(1)}, u32[]{:S(2)}, u32[]{:S(2)}) collective-permute-start(bf16[8,2,8,1024]{3,2,1,0:T(8,128)(2,1)S(1)} %shard_map.56.white_ref.refs_0_), channel_id=1, source_target_pairs={{0,4},{4,8},{1,5},{5,9},{2,6},{6,10},{3,7},{7,11},{16,20},{20,24},... | collective-permute-start | bytes 786440 | tf_op jit(solution)/shard_map/ppermute | solution.py:299
  10.7 0.7 %collective-permute-done.2.x_ref = bf16[8,2,8,1024]{3,2,1,0:T(8,128)(2,1)S(1)} collective-permute-done((bf16[8,2,8,1024]{3,2,1,0:T(8,128)(2,1)}, bf16[8,2,8,1024]{3,2,1,0:T(8,128)(2,1)S(1)}, u32[]{:S(2)}, u32[]{:S(2)}) %collective-permute-start.2) | collective-permute-done | bytes 262176 | tf_op jit(solution)/shard_map/ppermute | solution.py:26
  11.4 0.1 shard_map.58
  11.6 0.0 collective-permute-start.3
  11.6 0.0 copy-start
  11.6 1.0 %copy-done = f32[2,96,512]{2,1,0:T(8,128)S(1)} copy-done((f32[2,96,512]{2,1,0:T(8,128)S(1)}, f32[2,96,512]{2,1,0:T(8,128)}, u32[]{:S(2)}) %copy-start) | copy-done | bytes 393240
  12.6 1.2 %shard_map.60.refs_3_ = bf16[4,1024,512]{2,1,0:T(8,128)(2,1)S(1)} custom-call(f32[2,96,512]{2,1,0:T(8,128)S(1)} %copy-done), custom_call_target="tpu_custom_call" | custom-call | flops 8 | bytes 8 | tf_op jit(solution)/shard_map/pallas_call | solution.py:304
  13.8 0.0 copy-done.3
  13.8 0.1 shard_map.57.base_ref
  13.9 0.0 collective-permute-done.3.refs_0_
  13.9 0.2 shard_map.59.refs_1_.refs_0_
  14.2 0.0 copy-done.2
  14.2 2.5 %shard_map.61 = (f32[2,2,64,256]{3,2,1,0:T(8,128)S(1)}, f32[2,2,64,256]{3,2,1,0:T(8,128)S(1)}) custom-call(f32[8,2,8,1024]{3,2,1,0:T(8,128)S(1)} %shard_map.57.base_ref, bf16[8,2,8,1024]{3,2,1,0:T(8,128)(2,1)S(1)} %shard_map.56.white_ref.refs_0_, bf16[8,2,8,1024]{3,2,1,0:T(8,128)(2,1)S(1)} %shard_map.59.refs_1_.refs_0_, f32[2,2,1024]{2,1,0:T(2,128)S(1)} %copy-done.2, ...), custom_call_target="tpu_custom_call" | custom-call | flops 8 | bytes 8 | tf_op jit(solution)/shard_map/pallas_call | solution.py:270
  16.7 0.0 copy-start.4
  16.7 0.0 collective-permute-done.1.refs_1_
  16.7 0.0 collective-permute-done.6.white_ref
  16.7 0.1 shard_map.63.base_ref
  16.8 2.5 %shard_map.64 = (f32[2,2,64,256]{3,2,1,0:T(8,128)S(1)}, f32[2,2,64,256]{3,2,1,0:T(8,128)S(1)}) custom-call(f32[8,2,8,1024]{3,2,1,0:T(8,128)S(1)} %shard_map.63.base_ref, bf16[8,2,8,1024]{3,2,1,0:T(8,128)(2,1)S(1)} %shard_map.59.refs_1_.refs_0_, bf16[8,2,8,1024]{3,2,1,0:T(8,128)(2,1)S(1)} %collective-permute-done.1.refs_1_, f32[2,2,1024]{2,1,0:T(2,128)S(1)} %copy-done.2, ...), custom_call_target="tpu_custom_call" | custom-call | flops 8 | bytes 8 | tf_op jit(solution)/shard_map/pallas_call | solution.py:270
  19.3 0.6 %collective-permute-start.7 = (f32[2,2,64,256]{3,2,1,0:T(8,128)S(1)}, f32[2,2,64,256]{3,2,1,0:T(8,128)S(1)}, u32[]{:S(2)}, u32[]{:S(2)}) collective-permute-start(f32[2,2,64,256]{3,2,1,0:T(8,128)S(1)} %get-tuple-element.36), channel_id=1, source_target_pairs={{0,1},{1,0},{2,3},{3,2},{4,5},{5,4},{6,7},{7,6},{8,9},{9,8},{10,11... | collective-permute-start | bytes 786440 | tf_op jit(solution)/shard_map/ppermute | solution.py:286
  19.9 0.1 collective-permute-start.4
  20.0 1.1 %collective-permute-done.7.refs_1_ = f32[2,2,64,256]{3,2,1,0:T(8,128)S(1)} collective-permute-done((f32[2,2,64,256]{3,2,1,0:T(8,128)S(1)}, f32[2,2,64,256]{3,2,1,0:T(8,128)S(1)}, u32[]{:S(2)}, u32[]{:S(2)}) %collective-permute-start.7) | collective-permute-done | bytes 262176 | tf_op jit(solution)/shard_map/ppermute | solution.py:286
  21.1 1.3 %collective-permute-start.8 = (bf16[2,2,64,256]{3,2,1,0:T(8,128)(2,1)S(1)}, bf16[2,2,64,256]{3,2,1,0:T(8,128)(2,1)S(1)}, u32[]{:S(2)}, u32[]{:S(2)}) collective-permute-start(bf16[2,2,64,256]{3,2,1,0:T(8,128)(2,1)S(1)} %shard_map.65), channel_id=1, source_target_pairs={{4,0},{5,3},{6,2},{7,1},{8,4},{9,7},{10,6},{11,5},{20,16},{21,19},... | collective-permute-start | bytes 393224 | tf_op jit(solution)/shard_map/ppermute | solution.py:330
  22.4 0.0 collective-permute-done.4.refs_1_
  22.4 1.7 %collective-permute-start.5 = (bf16[2,64,256]{2,1,0:T(8,128)(2,1)S(1)}, bf16[2,64,256]{2,1,0:T(8,128)(2,1)S(1)}, u32[]{:S(2)}, u32[]{:S(2)}) collective-permute-start(bf16[2,64,256]{2,1,0:T(8,128)(2,1)S(1)} %get-tuple-element.31), channel_id=1, source_target_pairs={{0,2},{2,0},{1,3},{3,1},{4,6},{6,4},{5,7},{7,5},{8,10},{10,8},{9,1... | collective-permute-start | bytes 196616 | tf_op jit(solution)/shard_map/ppermute | solution.py:286
  24.2 5.7 %collective-permute-done.8.refs_0_ = bf16[2,2,64,256]{3,2,1,0:T(8,128)(2,1)S(1)} collective-permute-done((bf16[2,2,64,256]{3,2,1,0:T(8,128)(2,1)S(1)}, bf16[2,2,64,256]{3,2,1,0:T(8,128)(2,1)S(1)}, u32[]{:S(2)}, u32[]{:S(2)}) %collective-permute-start.8) | collective-permute-done | bytes 131104 | tf_op jit(solution)/shard_map/ppermute | solution.py:330
  29.9 0.2 collective-permute-start.9
  30.1 0.0 copy-done.4
  30.1 0.1 broadcast_in_dim.3
  30.2 0.1 broadcast_in_dim_reshape.4.factor_ref
  30.3 0.0 collective-permute-done.5.refs_1_
  30.3 1.0 %collective-permute-done.9.refs_3_ = f32[2,64,256]{2,1,0:T(8,128)S(1)} collective-permute-done((f32[2,64,256]{2,1,0:T(8,128)S(1)}, f32[2,64,256]{2,1,0:T(8,128)S(1)}, u32[]{:S(2)}, u32[]{:S(2)}) %collective-permute-start.9) | collective-permute-done | bytes 131104 | tf_op jit(solution)/shard_map/ppermute | solution.py:286
  31.3 0.9 %shard_map.67 = f32[8,4,8,256]{3,2,1,0:T(8,128)} custom-call(f32[4,64,1]{2,1,0:T(8,128)S(1)} %broadcast_in_dim_reshape.4.factor_ref, f32[2,64,256]{2,1,0:T(8,128)S(1)} %get-tuple-element.30.refs_0_, bf16[2,64,256]{2,1,0:T(8,128)(2,1)S(1)} %collective-permute-done.5.refs_1_, f32[2,64,256]{2,1,0:T(8,128)S(1)} %get-tuple-element.37.refs_2_, ...), custom_call_target="tpu_custom_call" | custom-call | tf_op jit(solution)/shard_map/pallas_call | solution.py:339
  (4 shorter events, 0.1 us)
Async XLA Ops:
  0.0 11.4 %collective-permute-start.2 = (bf16[8,2,8,1024]{3,2,1,0:T(8,128)(2,1)}, bf16[8,2,8,1024]{3,2,1,0:T(8,128)(2,1)S(1)}, u32[]{:S(2)}, u32[]{:S(2)}) collective-permute-start(bf16[8,2,8,1024]{3,2,1,0:T(8,128)(2,1)} %x_ref.1), channel_id=1, source_target_pairs={{4,0},{8,4},{12,8},{5,1},{9,5},{13,9},{6,2},{10,6},{14,10},{7,3},{... | collective-permute-start | bytes 786440 | tf_op jit(solution)/shard_map/ppermute | solution.py:26
  1.3 1.0 %copy-start.1 = (bf16[8,2,8,1024]{3,2,1,0:T(8,128)(2,1)S(1)}, bf16[8,2,8,1024]{3,2,1,0:T(8,128)(2,1)}, u32[]{:S(2)}) copy-start(bf16[8,2,8,1024]{3,2,1,0:T(8,128)(2,1)} %x_ref.1) | copy-start | bytes 786436
  2.2 11.5 %copy-start.3 = (s32[8]{0:T(128)S(1)}, s32[8]{0:T(128)}, u32[]{:S(2)}) copy-start(s32[8]{0:T(128)} %param.6) | copy-start | bytes 100
  2.2 11.9 %copy-start.2 = (f32[2,2,1024]{2,1,0:T(2,128)S(1)}, f32[2,2,1024]{2,1,0:T(2,128)}, u32[]{:S(2)}) copy-start(f32[2,2,1024]{2,1,0:T(2,128)} %constant.6.clone.refs_2_) | copy-start | bytes 49156
  2.4 1.3 %collective-permute-start = (f32[8,8,1]{2,1,0:T(8,128)S(1)}, f32[8,8,1]{2,1,0:T(8,128)S(1)}, u32[]{:S(2)}, u32[]{:S(2)}) collective-permute-start(f32[8,8,1]{2,1,0:T(8,128)S(1)} %get-tuple-element.23), channel_id=1, source_target_pairs={{0,1},{1,0},{2,3},{3,2},{4,5},{5,4},{6,7},{7,6},{8,9},{9,8},{10,11... | collective-permute-start | bytes 776 | tf_op jit(solution)/shard_map/ppermute | solution.py:245
  3.9 12.8 %collective-permute-start.1 = (bf16[8,2,8,1024]{3,2,1,0:T(8,128)(2,1)S(1)}, bf16[8,2,8,1024]{3,2,1,0:T(8,128)(2,1)S(1)}, u32[]{:S(2)}, u32[]{:S(2)}) collective-permute-start(bf16[8,2,8,1024]{3,2,1,0:T(8,128)(2,1)S(1)} %shard_map.56.white_ref.refs_0_), channel_id=1, source_target_pairs={{12,4},{13,5},{14,6},{15,7},{28,20},{29,21},{30,22},{31,23}} | collective-permute-start | bytes 786440 | tf_op jit(solution)/shard_map/ppermute | solution.py:298
  4.6 12.1 %collective-permute-start.6 = (bf16[8,2,8,1024]{3,2,1,0:T(8,128)(2,1)S(1)}, bf16[8,2,8,1024]{3,2,1,0:T(8,128)(2,1)S(1)}, u32[]{:S(2)}, u32[]{:S(2)}) collective-permute-start(bf16[8,2,8,1024]{3,2,1,0:T(8,128)(2,1)S(1)} %shard_map.56.white_ref.refs_0_), channel_id=1, source_target_pairs={{0,4},{4,8},{1,5},{5,9},{2,6},{6,10},{3,7},{7,11},{16,20},{20,24},... | collective-permute-start | bytes 786440 | tf_op jit(solution)/shard_map/ppermute | solution.py:299
  11.6 2.3 %collective-permute-start.3 = (f32[8,8,1]{2,1,0:T(8,128)S(1)}, f32[8,8,1]{2,1,0:T(8,128)S(1)}, u32[]{:S(2)}, u32[]{:S(2)}) collective-permute-start(f32[8,8,1]{2,1,0:T(8,128)S(1)} %shard_map.58), channel_id=1, source_target_pairs={{0,1},{1,0},{2,3},{3,2},{4,5},{5,4},{6,7},{7,6},{8,9},{9,8},{10,11... | collective-permute-start | bytes 776 | tf_op jit(solution)/shard_map/ppermute | solution.py:245
  11.6 1.0 %copy-start = (f32[2,96,512]{2,1,0:T(8,128)S(1)}, f32[2,96,512]{2,1,0:T(8,128)}, u32[]{:S(2)}) copy-start(f32[2,96,512]{2,1,0:T(8,128)} %constant.7.clone.base_ref) | copy-start | bytes 1179652
  16.7 13.4 %copy-start.4 = (s32[8,4]{0,1:T(4,128)S(1)}, s32[8,4]{0,1:T(4,128)}, u32[]{:S(2)}) copy-start(s32[8,4]{0,1:T(4,128)} %param.7) | copy-start | bytes 388
  19.3 1.7 %collective-permute-start.7 = (f32[2,2,64,256]{3,2,1,0:T(8,128)S(1)}, f32[2,2,64,256]{3,2,1,0:T(8,128)S(1)}, u32[]{:S(2)}, u32[]{:S(2)}) collective-permute-start(f32[2,2,64,256]{3,2,1,0:T(8,128)S(1)} %get-tuple-element.36), channel_id=1, source_target_pairs={{0,1},{1,0},{2,3},{3,2},{4,5},{5,4},{6,7},{7,6},{8,9},{9,8},{10,11... | collective-permute-start | bytes 786440 | tf_op jit(solution)/shard_map/ppermute | solution.py:286
  19.9 2.5 %collective-permute-start.4 = (f32[2,2,64,256]{3,2,1,0:T(8,128)S(1)}, f32[2,2,64,256]{3,2,1,0:T(8,128)S(1)}, u32[]{:S(2)}, u32[]{:S(2)}) collective-permute-start(f32[2,2,64,256]{3,2,1,0:T(8,128)S(1)} %get-tuple-element.29), channel_id=1, source_target_pairs={{0,1},{1,0},{2,3},{3,2},{4,5},{5,4},{6,7},{7,6},{8,9},{9,8},{10,11... | collective-permute-start | bytes 786440 | tf_op jit(solution)/shard_map/ppermute | solution.py:286
  21.1 8.8 %collective-permute-start.8 = (bf16[2,2,64,256]{3,2,1,0:T(8,128)(2,1)S(1)}, bf16[2,2,64,256]{3,2,1,0:T(8,128)(2,1)S(1)}, u32[]{:S(2)}, u32[]{:S(2)}) collective-permute-start(bf16[2,2,64,256]{3,2,1,0:T(8,128)(2,1)S(1)} %shard_map.65), channel_id=1, source_target_pairs={{4,0},{5,3},{6,2},{7,1},{8,4},{9,7},{10,6},{11,5},{20,16},{21,19},... | collective-permute-start | bytes 393224 | tf_op jit(solution)/shard_map/ppermute | solution.py:330
  22.4 7.8 %collective-permute-start.5 = (bf16[2,64,256]{2,1,0:T(8,128)(2,1)S(1)}, bf16[2,64,256]{2,1,0:T(8,128)(2,1)S(1)}, u32[]{:S(2)}, u32[]{:S(2)}) collective-permute-start(bf16[2,64,256]{2,1,0:T(8,128)(2,1)S(1)} %get-tuple-element.31), channel_id=1, source_target_pairs={{0,2},{2,0},{1,3},{3,1},{4,6},{6,4},{5,7},{7,5},{8,10},{10,8},{9,1... | collective-permute-start | bytes 196616 | tf_op jit(solution)/shard_map/ppermute | solution.py:286
  29.9 1.4 %collective-permute-start.9 = (f32[2,64,256]{2,1,0:T(8,128)S(1)}, f32[2,64,256]{2,1,0:T(8,128)S(1)}, u32[]{:S(2)}, u32[]{:S(2)}) collective-permute-start(f32[2,64,256]{2,1,0:T(8,128)S(1)} %get-tuple-element.38), channel_id=1, source_target_pairs={{0,1},{1,0},{2,3},{3,2},{4,5},{5,4},{6,7},{7,6},{8,9},{9,8},{10,11... | collective-permute-start | bytes 393224 | tf_op jit(solution)/shard_map/ppermute | solution.py:286

commit v19 on v18

--- a/solution.py
+++ b/solution.py
@@ -113,8 +113,12 @@
 def pairs_kernel(n_partners, n_win, n_freq, by_window, base_ref, *refs):
     partner_refs = refs[:n_partners]
     twist_ref, table_ref = refs[n_partners:n_partners + 2]
+    before_refs = refs[n_partners + 2:-2 - n_freq]
     out_refs = refs[-2 - n_freq:-2]
     rows_ref, sums_ref = refs[-2:]
+    done = out_refs[0].shape[0] - n_partners
+    for before_ref, out_ref in zip(before_refs, out_refs):
+        out_ref[:done] = before_ref[...]
     ch, f_dev = base_ref.shape[2:]
     pairs = ch * ch
     groups = n_win * n_freq
@@ -157,7 +161,7 @@
             lags = pl.ds(pl.multiple_of(block * width, LANES), width)
             for k in range(n_partners):
                 rows = slice(k * pairs, (k + 1) * pairs)
-                out_ref[k, turn_win] = sums_ref[0, rows, lags] + sign * sums_ref[1, rows, lags]
+                out_ref[done + k, turn_win] = sums_ref[0, rows, lags] + sign * sums_ref[1, rows, lags]
 
 
 def add_kernel(n_parts, *refs):
@@ -227,8 +231,8 @@
     def cost(flops, size):
         return pl.CostEstimate(flops=flops, bytes_accessed=size, transcendentals=0)
 
-    below = from_behind(spectra, "chan", -1)
     far_routes = [[(c + away, c) for c in range(1, n_chan - away)] for away in range(2, reach)]
+    far = [lax.ppermute(spectra, "chan", route) for route in far_routes]
     power, copied = pl.pallas_call(
         power_kernel,
         out_shape=[
@@ -265,19 +269,20 @@
             in_specs=[VMEM] * 2, out_specs=VMEM, compiler_params=params,
         )(keep.reshape(1, w_dev), block)
 
-    def pairs(base, partners, by_window):
+    def pairs(base, partners, by_window, before=()):
         n = len(partners)
+        total = n + (before[0].shape[0] if before else 0)
         return pl.pallas_call(
             functools.partial(pairs_kernel, n, n_win, n_freq, by_window),
-            out_shape=[jax.ShapeDtypeStruct((n, n_win, ch * ch, width), jnp.float32)] * n_freq,
-            in_specs=[VMEM] * (3 + n), out_specs=[VMEM] * n_freq,
+            out_shape=[jax.ShapeDtypeStruct((total, n_win, ch * ch, width), jnp.float32)] * n_freq,
+            in_specs=[VMEM] * (3 + n + len(before)), out_specs=[VMEM] * n_freq,
             scratch_shapes=[
                 pltpu.VMEM((2, 2 * n * ch * ch, f_dev), jnp.bfloat16),
                 pltpu.VMEM((2, n * ch * ch, LAGS // 2), jnp.float32),
             ],
             compiler_params=params,
             cost_estimate=cost(ch, ch),
-        )(base, *partners, twist, table)
+        )(base, *partners, twist, table, *before)
 
     def turns(parts, axis, size):
         received = [parts[0]]
@@ -295,7 +300,7 @@
         )(*turns(parts, "freq", n_freq))
 
     white = whiten(copied, swap(power))
-    far = [lax.ppermute(white, "chan", route) for route in far_routes]
+    below = from_behind(white, "chan", -1)
     above = lax.ppermute(white, "chan", [(c - 1, c) for c in range(1, n_chan - 1)])
     half_lags = 2 * np.arange(LAGS // 2) + 1
     coarse = phases(np.arange(0, n_bins, FINE), half_lags)
@@ -307,13 +312,14 @@
         in_specs=[VMEM], out_specs=VMEM, compiler_params=params, cost_estimate=cost(ch, ch),
     )(ends)
     own = kept(white)
-    below = whiten(below, swap(half_power(below)))
-    parts = pairs(own, [white, below], False)
-    far, parts = lax.optimization_barrier((far, parts))
-    above, far = lax.optimization_barrier((above, far))
+    far = [whiten(block, swap(half_power(block))) for block in far]
+    first = pairs(own, [white], False)
+    below, above, far, first = lax.optimization_barrier((below, above, far, first))
+    remote = pairs(kept(above), [below] + far, True)
+    remote, first = lax.optimization_barrier((remote, first))
     kinds = [jnp.float32] + [jnp.bfloat16] * (n_win - 1)
-    near = turns(split_windows(parts, kinds), "win", n_win)
-    remote = turns(pairs(kept(above), [below] + far, True), "freq", n_freq)
+    near = turns(split_windows(pairs(own, [below], False, first), kinds), "win", n_win)
+    remote = turns(remote, "freq", n_freq)
     shape = (remote[0].shape[0], ch * ch, width)
     n_ships = n_win // n_freq
     shipped = pl.pallas_call(

time: 32.4 us -> 32.8 us (1.012)
  Pallas kernels: 8.12 us -> 8.78 us
    ppermute x1, waiting for transfers between devices: 0.01 us -> 1.18 us  [local(): lax.ppermute(white, 'chan', [(c - 1, c) for c in range(1, n_chan - 1)])]
    ppermute x4, waiting for transfers between devices: 2.08 us -> 1.03 us  [turns(): received.append(lax.ppermute(parts[turn], axis, route))]
    pallas_call x2 -> x3, Pallas kernels: 5.02 us -> 5.68 us  [pairs(): pl.pallas_call(functools.partial(pairs_kernel, n, n_win, n_freq, by_windo...]
    ppermute x1, waiting for transfers between devices: 0.7 us -> 0.34 us  [from_behind(): return lax.ppermute(block, axis, route)]
  transfers between devices with their start and end apart: 10 -> 10, of which waited for: 5 -> 5; matrix products, arithmetic and copies ran while one was open for 1% -> 1% of each run, Pallas kernels for 14% -> 16%
where the time goes in v19:
time: 32.8 us; the launch traced here: 32.5 us
  starting transfers between devices  12.2 us (37%)
  waiting for transfers between devices  9.23 us (28%)
  Pallas kernels  8.78 us (27%)
  local copies, waits for them, and re-layouts  2.12 us (6%)
    ppermute x1, starting transfers between devices, local(): lax.ppermute(white, 'chan', [(c - 1, c) for c in range(1, n_chan - 1)])  6.08 us
    ppermute x1, waiting for transfers between devices, local(): arrived.append(lax.ppermute(block, ('chan', 'win', 'freq'), route))  5.81 us
    pallas_call x3, Pallas kernels, pairs(): pl.pallas_call(functools.partial(pairs_kernel, n, n_win, n_freq, by_windo...  5.68 us
    ppermute x4, starting transfers between devices, turns(): received.append(lax.ppermute(parts[turn], axis, route))  2.38 us
    unnamed x10, local copies, waits for them, and re-layouts  1.95 us
    ppermute x1, starting transfers between devices, from_behind(): return lax.ppermute(block, axis, route)  1.29 us
    ppermute x1, starting transfers between devices, local(): arrived.append(lax.ppermute(block, ('chan', 'win', 'freq'), route))  1.29 us
    pallas_call x1, Pallas kernels, local(): pl.pallas_call(table_kernel, out_shape=jax.ShapeDtypeStruct((4, f_dev, LA...  1.19 us
  transfers between devices with their start and end apart: 10, of which 5 were waited for; matrix products, arithmetic and copies ran while one was open for 1% of the time, Pallas kernels for 16%

profile of v19, /device:TPU:0, one launch (start us, length us, event | category | flops | bytes accessed | tf_op | source)
XLA Modules:
  0.0 32.5 jit_solution(8210680787464862184)
XLA Ops:
  0.0 0.7 %collective-permute-start.3 = (bf16[8,2,8,1024]{3,2,1,0:T(8,128)(2,1)}, bf16[8,2,8,1024]{3,2,1,0:T(8,128)(2,1)S(1)}, u32[]{:S(2)}, u32[]{:S(2)}) collective-permute-start(bf16[8,2,8,1024]{3,2,1,0:T(8,128)(2,1)} %x_ref.1), channel_id=1, source_target_pairs={{12,4},{13,5},{14,6},{15,7},{28,20},{29,21},{30,22},{31,23}} | collective-permute-start | bytes 786440 | tf_op jit(solution)/shard_map/ppermute | solution.py:235
  0.7 0.0 copy-start.1
  0.7 0.9 %copy-done.1 = bf16[8,2,8,1024]{3,2,1,0:T(8,128)(2,1)S(1)} copy-done((bf16[8,2,8,1024]{3,2,1,0:T(8,128)(2,1)S(1)}, bf16[8,2,8,1024]{3,2,1,0:T(8,128)(2,1)}, u32[]{:S(2)}) %copy-start.1) | copy-done | bytes 262168
  1.6 0.0 copy-start.3
  1.6 0.0 copy-start.2
  1.6 0.1 shard_map.55
  1.8 0.5 %collective-permute-start = (f32[8,8,1]{2,1,0:T(8,128)S(1)}, f32[8,8,1]{2,1,0:T(8,128)S(1)}, u32[]{:S(2)}, u32[]{:S(2)}) collective-permute-start(f32[8,8,1]{2,1,0:T(8,128)S(1)} %get-tuple-element.29), channel_id=1, source_target_pairs={{0,1},{1,0},{2,3},{3,2},{4,5},{5,4},{6,7},{7,6},{8,9},{9,8},{10,11... | collective-permute-start | bytes 776 | tf_op jit(solution)/shard_map/ppermute | solution.py:249
  2.2 0.9 %collective-permute-done.refs_0_ = f32[8,8,1]{2,1,0:T(8,128)S(1)} collective-permute-done((f32[8,8,1]{2,1,0:T(8,128)S(1)}, f32[8,8,1]{2,1,0:T(8,128)S(1)}, u32[]{:S(2)}, u32[]{:S(2)}) %collective-permute-start) | collective-permute-done | bytes 288 | tf_op jit(solution)/shard_map/ppermute | solution.py:249
  3.1 0.2 shard_map.56.white_ref.refs_0_
  3.3 1.3 %collective-permute-start.1 = (bf16[8,2,8,1024]{3,2,1,0:T(8,128)(2,1)S(1)}, bf16[8,2,8,1024]{3,2,1,0:T(8,128)(2,1)S(1)}, u32[]{:S(2)}, u32[]{:S(2)}) collective-permute-start(bf16[8,2,8,1024]{3,2,1,0:T(8,128)(2,1)S(1)} %shard_map.56.white_ref.refs_0_), channel_id=1, source_target_pairs={{4,0},{8,4},{12,8},{5,1},{9,5},{13,9},{6,2},{10,6},{14,10},{7,3},{... | collective-permute-start | bytes 786440 | tf_op jit(solution)/shard_map/ppermute | solution.py:26
  4.6 6.1 %collective-permute-start.2 = (bf16[8,2,8,1024]{3,2,1,0:T(8,128)(2,1)S(1)}, bf16[8,2,8,1024]{3,2,1,0:T(8,128)(2,1)S(1)}, u32[]{:S(2)}, u32[]{:S(2)}) collective-permute-start(bf16[8,2,8,1024]{3,2,1,0:T(8,128)(2,1)S(1)} %shard_map.56.white_ref.refs_0_), channel_id=1, source_target_pairs={{0,4},{4,8},{1,5},{5,9},{2,6},{6,10},{3,7},{7,11},{16,20},{20,24},... | collective-permute-start | bytes 786440 | tf_op jit(solution)/shard_map/ppermute | solution.py:304
  10.7 0.0 copy-start
  10.7 1.0 %copy-done = f32[2,96,512]{2,1,0:T(8,128)S(1)} copy-done((f32[2,96,512]{2,1,0:T(8,128)S(1)}, f32[2,96,512]{2,1,0:T(8,128)}, u32[]{:S(2)}) %copy-start) | copy-done | bytes 393240
  11.7 1.2 %shard_map.60.refs_2_.refs_3_ = bf16[4,1024,512]{2,1,0:T(8,128)(2,1)S(1)} custom-call(f32[2,96,512]{2,1,0:T(8,128)S(1)} %copy-done), custom_call_target="tpu_custom_call" | custom-call | flops 8 | bytes 8 | tf_op jit(solution)/shard_map/pallas_call | solution.py:309
  12.9 0.0 collective-permute-done.3.x_ref
  12.9 0.1 shard_map.58
  13.1 0.0 collective-permute-start.4
  13.1 0.0 copy-done.3
  13.1 0.1 shard_map.57.base_ref
  13.2 0.0 copy-done.2
  13.2 1.6 %shard_map.61 = (f32[1,2,64,256]{3,2,1,0:T(8,128)S(1)}, f32[1,2,64,256]{3,2,1,0:T(8,128)S(1)}) custom-call(f32[8,2,8,1024]{3,2,1,0:T(8,128)S(1)} %shard_map.57.base_ref, bf16[8,2,8,1024]{3,2,1,0:T(8,128)(2,1)S(1)} %shard_map.56.white_ref.refs_0_, f32[2,2,1024]{2,1,0:T(2,128)S(1)} %copy-done.2, bf16[4,1024,512]{2,1,0:T(8,128)(2,1)S(1)} %shard_map.60.refs_2_.refs_3_), custom_call_target="tpu_custom_call" | custom-call | flops 8 | bytes 8 | tf_op jit(solution)/shard_map/pallas_call | solution.py:275
  14.8 0.0 collective-permute-done.4.refs_0_
  14.8 0.2 shard_map.59.refs_1_
  15.1 0.3 %collective-permute-done.1.refs_0_ = bf16[8,2,8,1024]{3,2,1,0:T(8,128)(2,1)S(1)} collective-permute-done((bf16[8,2,8,1024]{3,2,1,0:T(8,128)(2,1)S(1)}, bf16[8,2,8,1024]{3,2,1,0:T(8,128)(2,1)S(1)}, u32[]{:S(2)}, u32[]{:S(2)}) %collective-permute-start.1) | collective-permute-done | bytes 262176 | tf_op jit(solution)/shard_map/ppermute | solution.py:26
  15.4 1.2 %collective-permute-done.2.white_ref = bf16[8,2,8,1024]{3,2,1,0:T(8,128)(2,1)S(1)} collective-permute-done((bf16[8,2,8,1024]{3,2,1,0:T(8,128)(2,1)S(1)}, bf16[8,2,8,1024]{3,2,1,0:T(8,128)(2,1)S(1)}, u32[]{:S(2)}, u32[]{:S(2)}) %collective-permute-start.2) | collective-permute-done | bytes 262176 | tf_op jit(solution)/shard_map/ppermute | solution.py:304
  16.6 0.1 shard_map.62.base_ref
  16.7 2.5 %shard_map.63 = (f32[2,2,64,256]{3,2,1,0:T(8,128)S(1)}, f32[2,2,64,256]{3,2,1,0:T(8,128)S(1)}) custom-call(f32[8,2,8,1024]{3,2,1,0:T(8,128)S(1)} %shard_map.62.base_ref, bf16[8,2,8,1024]{3,2,1,0:T(8,128)(2,1)S(1)} %collective-permute-done.1.refs_0_, bf16[8,2,8,1024]{3,2,1,0:T(8,128)(2,1)S(1)} %shard_map.59.refs_1_, f32[2,2,1024]{2,1,0:T(2,128)S(1)} %copy-done.2, ...), custom_call_target="tpu_custom_call" | custom-call | flops 8 | bytes 8 | tf_op jit(solution)/shard_map/pallas_call | solution.py:275
  19.2 0.0 copy-start.4
  19.2 0.1 collective-permute-start.7
  19.3 1.6 %shard_map.64 = (f32[2,2,64,256]{3,2,1,0:T(8,128)S(1)}, f32[2,2,64,256]{3,2,1,0:T(8,128)S(1)}) custom-call(f32[8,2,8,1024]{3,2,1,0:T(8,128)S(1)} %shard_map.57.base_ref, bf16[8,2,8,1024]{3,2,1,0:T(8,128)(2,1)S(1)} %collective-permute-done.1.refs_0_, f32[2,2,1024]{2,1,0:T(2,128)S(1)} %copy-done.2, bf16[4,1024,512]{2,1,0:T(8,128)(2,1)S(1)} %shard_map.60.refs_2_.refs_3_, ...), custom_call_target="tpu_custom_call" | custom-call | flops 8 | bytes 8 | tf_op jit(solution)/shard_map/pallas_call | solution.py:275
  20.9 0.6 %collective-permute-start.5 = (f32[2,2,64,256]{3,2,1,0:T(8,128)S(1)}, f32[2,2,64,256]{3,2,1,0:T(8,128)S(1)}, u32[]{:S(2)}, u32[]{:S(2)}) collective-permute-start(f32[2,2,64,256]{3,2,1,0:T(8,128)S(1)} %get-tuple-element.44), channel_id=1, source_target_pairs={{0,1},{1,0},{2,3},{3,2},{4,5},{5,4},{6,7},{7,6},{8,9},{9,8},{10,11... | collective-permute-start | bytes 786440 | tf_op jit(solution)/shard_map/ppermute | solution.py:291
  21.5 0.0 collective-permute-done.7.refs_1_
  21.5 1.3 %collective-permute-start.8 = (bf16[2,2,64,256]{3,2,1,0:T(8,128)(2,1)S(1)}, bf16[2,2,64,256]{3,2,1,0:T(8,128)(2,1)S(1)}, u32[]{:S(2)}, u32[]{:S(2)}) collective-permute-start(bf16[2,2,64,256]{3,2,1,0:T(8,128)(2,1)S(1)} %shard_map.66), channel_id=1, source_target_pairs={{4,0},{5,3},{6,2},{7,1},{8,4},{9,7},{10,6},{11,5},{20,16},{21,19},... | collective-permute-start | bytes 393224 | tf_op jit(solution)/shard_map/ppermute | solution.py:336
  22.8 0.0 collective-permute-done.5.refs_1_
  22.8 1.5 %collective-permute-start.6 = (bf16[2,64,256]{2,1,0:T(8,128)(2,1)S(1)}, bf16[2,64,256]{2,1,0:T(8,128)(2,1)S(1)}, u32[]{:S(2)}, u32[]{:S(2)}) collective-permute-start(bf16[2,64,256]{2,1,0:T(8,128)(2,1)S(1)} %get-tuple-element.46), channel_id=1, source_target_pairs={{0,2},{2,0},{1,3},{3,1},{4,6},{6,4},{5,7},{7,5},{8,10},{10,8},{9,1... | collective-permute-start | bytes 196616 | tf_op jit(solution)/shard_map/ppermute | solution.py:291
  24.4 5.8 %collective-permute-done.8.refs_0_ = bf16[2,2,64,256]{3,2,1,0:T(8,128)(2,1)S(1)} collective-permute-done((bf16[2,2,64,256]{3,2,1,0:T(8,128)(2,1)S(1)}, bf16[2,2,64,256]{3,2,1,0:T(8,128)(2,1)S(1)}, u32[]{:S(2)}, u32[]{:S(2)}) %collective-permute-start.8) | collective-permute-done | bytes 131104 | tf_op jit(solution)/shard_map/ppermute | solution.py:336
  30.2 0.2 collective-permute-start.9
  30.4 0.0 copy-done.4
  30.4 0.1 broadcast_in_dim.3
  30.5 0.1 broadcast_in_dim_reshape.4.factor_ref
  30.6 0.0 collective-permute-done.6.refs_1_
  30.6 1.0 %collective-permute-done.9.refs_3_ = f32[2,64,256]{2,1,0:T(8,128)S(1)} collective-permute-done((f32[2,64,256]{2,1,0:T(8,128)S(1)}, f32[2,64,256]{2,1,0:T(8,128)S(1)}, u32[]{:S(2)}, u32[]{:S(2)}) %collective-permute-start.9) | collective-permute-done | bytes 131104 | tf_op jit(solution)/shard_map/ppermute | solution.py:291
  31.6 0.9 %shard_map.68 = f32[8,4,8,256]{3,2,1,0:T(8,128)} custom-call(f32[4,64,1]{2,1,0:T(8,128)S(1)} %broadcast_in_dim_reshape.4.factor_ref, f32[2,64,256]{2,1,0:T(8,128)S(1)} %get-tuple-element.45.refs_0_, bf16[2,64,256]{2,1,0:T(8,128)(2,1)S(1)} %collective-permute-done.6.refs_1_, f32[2,64,256]{2,1,0:T(8,128)S(1)} %get-tuple-element.49.refs_2_, ...), custom_call_target="tpu_custom_call" | custom-call | tf_op jit(solution)/shard_map/pallas_call | solution.py:345
  (4 shorter events, 0.1 us)
Async XLA Ops:
  0.0 12.9 %collective-permute-start.3 = (bf16[8,2,8,1024]{3,2,1,0:T(8,128)(2,1)}, bf16[8,2,8,1024]{3,2,1,0:T(8,128)(2,1)S(1)}, u32[]{:S(2)}, u32[]{:S(2)}) collective-permute-start(bf16[8,2,8,1024]{3,2,1,0:T(8,128)(2,1)} %x_ref.1), channel_id=1, source_target_pairs={{12,4},{13,5},{14,6},{15,7},{28,20},{29,21},{30,22},{31,23}} | collective-permute-start | bytes 786440 | tf_op jit(solution)/shard_map/ppermute | solution.py:235
  0.7 1.0 %copy-start.1 = (bf16[8,2,8,1024]{3,2,1,0:T(8,128)(2,1)S(1)}, bf16[8,2,8,1024]{3,2,1,0:T(8,128)(2,1)}, u32[]{:S(2)}) copy-start(bf16[8,2,8,1024]{3,2,1,0:T(8,128)(2,1)} %x_ref.1) | copy-start | bytes 786436
  1.6 11.5 %copy-start.3 = (s32[8]{0:T(128)S(1)}, s32[8]{0:T(128)}, u32[]{:S(2)}) copy-start(s32[8]{0:T(128)} %param.6) | copy-start | bytes 100
  1.6 11.6 %copy-start.2 = (f32[2,2,1024]{2,1,0:T(2,128)S(1)}, f32[2,2,1024]{2,1,0:T(2,128)}, u32[]{:S(2)}) copy-start(f32[2,2,1024]{2,1,0:T(2,128)} %constant.6.clone.refs_1_.refs_2_) | copy-start | bytes 49156
  1.8 1.3 %collective-permute-start = (f32[8,8,1]{2,1,0:T(8,128)S(1)}, f32[8,8,1]{2,1,0:T(8,128)S(1)}, u32[]{:S(2)}, u32[]{:S(2)}) collective-permute-start(f32[8,8,1]{2,1,0:T(8,128)S(1)} %get-tuple-element.29), channel_id=1, source_target_pairs={{0,1},{1,0},{2,3},{3,2},{4,5},{5,4},{6,7},{7,6},{8,9},{9,8},{10,11... | collective-permute-start | bytes 776 | tf_op jit(solution)/shard_map/ppermute | solution.py:249
  3.3 12.1 %collective-permute-start.1 = (bf16[8,2,8,1024]{3,2,1,0:T(8,128)(2,1)S(1)}, bf16[8,2,8,1024]{3,2,1,0:T(8,128)(2,1)S(1)}, u32[]{:S(2)}, u32[]{:S(2)}) collective-permute-start(bf16[8,2,8,1024]{3,2,1,0:T(8,128)(2,1)S(1)} %shard_map.56.white_ref.refs_0_), channel_id=1, source_target_pairs={{4,0},{8,4},{12,8},{5,1},{9,5},{13,9},{6,2},{10,6},{14,10},{7,3},{... | collective-permute-start | bytes 786440 | tf_op jit(solution)/shard_map/ppermute | solution.py:26
  4.6 11.9 %collective-permute-start.2 = (bf16[8,2,8,1024]{3,2,1,0:T(8,128)(2,1)S(1)}, bf16[8,2,8,1024]{3,2,1,0:T(8,128)(2,1)S(1)}, u32[]{:S(2)}, u32[]{:S(2)}) collective-permute-start(bf16[8,2,8,1024]{3,2,1,0:T(8,128)(2,1)S(1)} %shard_map.56.white_ref.refs_0_), channel_id=1, source_target_pairs={{0,4},{4,8},{1,5},{5,9},{2,6},{6,10},{3,7},{7,11},{16,20},{20,24},... | collective-permute-start | bytes 786440 | tf_op jit(solution)/shard_map/ppermute | solution.py:304
  10.7 1.0 %copy-start = (f32[2,96,512]{2,1,0:T(8,128)S(1)}, f32[2,96,512]{2,1,0:T(8,128)}, u32[]{:S(2)}) copy-start(f32[2,96,512]{2,1,0:T(8,128)} %constant.7.clone.base_ref) | copy-start | bytes 1179652
  13.1 1.7 %collective-permute-start.4 = (f32[8,8,1]{2,1,0:T(8,128)S(1)}, f32[8,8,1]{2,1,0:T(8,128)S(1)}, u32[]{:S(2)}, u32[]{:S(2)}) collective-permute-start(f32[8,8,1]{2,1,0:T(8,128)S(1)} %shard_map.58), channel_id=1, source_target_pairs={{0,1},{1,0},{2,3},{3,2},{4,5},{5,4},{6,7},{7,6},{8,9},{9,8},{10,11... | collective-permute-start | bytes 776 | tf_op jit(solution)/shard_map/ppermute | solution.py:249
  19.2 11.2 %copy-start.4 = (s32[8,4]{0,1:T(4,128)S(1)}, s32[8,4]{0,1:T(4,128)}, u32[]{:S(2)}) copy-start(s32[8,4]{0,1:T(4,128)} %param.7) | copy-start | bytes 388
  19.2 2.2 %collective-permute-start.7 = (f32[2,2,64,256]{3,2,1,0:T(8,128)S(1)}, f32[2,2,64,256]{3,2,1,0:T(8,128)S(1)}, u32[]{:S(2)}, u32[]{:S(2)}) collective-permute-start(f32[2,2,64,256]{3,2,1,0:T(8,128)S(1)} %get-tuple-element.48), channel_id=1, source_target_pairs={{0,1},{1,0},{2,3},{3,2},{4,5},{5,4},{6,7},{7,6},{8,9},{9,8},{10,11... | collective-permute-start | bytes 786440 | tf_op jit(solution)/shard_map/ppermute | solution.py:291
  20.9 1.9 %collective-permute-start.5 = (f32[2,2,64,256]{3,2,1,0:T(8,128)S(1)}, f32[2,2,64,256]{3,2,1,0:T(8,128)S(1)}, u32[]{:S(2)}, u32[]{:S(2)}) collective-permute-start(f32[2,2,64,256]{3,2,1,0:T(8,128)S(1)} %get-tuple-element.44), channel_id=1, source_target_pairs={{0,1},{1,0},{2,3},{3,2},{4,5},{5,4},{6,7},{7,6},{8,9},{9,8},{10,11... | collective-permute-start | bytes 786440 | tf_op jit(solution)/shard_map/ppermute | solution.py:291
  21.5 8.7 %collective-permute-start.8 = (bf16[2,2,64,256]{3,2,1,0:T(8,128)(2,1)S(1)}, bf16[2,2,64,256]{3,2,1,0:T(8,128)(2,1)S(1)}, u32[]{:S(2)}, u32[]{:S(2)}) collective-permute-start(bf16[2,2,64,256]{3,2,1,0:T(8,128)(2,1)S(1)} %shard_map.66), channel_id=1, source_target_pairs={{4,0},{5,3},{6,2},{7,1},{8,4},{9,7},{10,6},{11,5},{20,16},{21,19},... | collective-permute-start | bytes 393224 | tf_op jit(solution)/shard_map/ppermute | solution.py:336
  22.8 7.8 %collective-permute-start.6 = (bf16[2,64,256]{2,1,0:T(8,128)(2,1)S(1)}, bf16[2,64,256]{2,1,0:T(8,128)(2,1)S(1)}, u32[]{:S(2)}, u32[]{:S(2)}) collective-permute-start(bf16[2,64,256]{2,1,0:T(8,128)(2,1)S(1)} %get-tuple-element.46), channel_id=1, source_target_pairs={{0,2},{2,0},{1,3},{3,1},{4,6},{6,4},{5,7},{7,5},{8,10},{10,8},{9,1... | collective-permute-start | bytes 196616 | tf_op jit(solution)/shard_map/ppermute | solution.py:291
  30.2 1.4 %collective-permute-start.9 = (f32[2,64,256]{2,1,0:T(8,128)S(1)}, f32[2,64,256]{2,1,0:T(8,128)S(1)}, u32[]{:S(2)}, u32[]{:S(2)}) collective-permute-start(f32[2,64,256]{2,1,0:T(8,128)S(1)} %get-tuple-element.50), channel_id=1, source_target_pairs={{0,1},{1,0},{2,3},{3,2},{4,5},{5,4},{6,7},{7,6},{8,9},{9,8},{10,11... | collective-permute-start | bytes 393224 | tf_op jit(solution)/shard_map/ppermute | solution.py:291

commit v20 on v18

--- a/solution.py
+++ b/solution.py
@@ -54,12 +54,23 @@
         power_ref[w] = bin_power(x_ref[w])
 
 
-def whiten_kernel(n_bins, x_ref, *refs):
+def own_kernel(n_bins, x_ref, *refs):
+    white_ref, power_ref = refs[-2:]
+    for w in range(x_ref.shape[0]):
+        power = bin_power(x_ref[w])
+        for ref in refs[:-2]:
+            power = power + ref[w]
+        power_ref[w] = jnp.broadcast_to(power, power_ref.shape[1:])
+    whiten_kernel(n_bins, False, x_ref, power_ref, white_ref)
+
+
+def whiten_kernel(n_bins, add_own, x_ref, *refs):
     out_ref = refs[-1]
     for w in range(x_ref.shape[0]):
-        power = bin_power(x_ref[w])
+        power = bin_power(x_ref[w]) if add_own else None
         for ref in refs[:-1]:
-            power = power + ref[w]
+            other = ref[w][:, 0:1]
+            power = other if power is None else power + other
         scale = lax.rsqrt(power / n_bins + EPS)
         for part in range(2):
             out_ref[w, part] = (x_ref[w, part].astype(jnp.float32) * scale).astype(jnp.bfloat16)
@@ -229,6 +240,7 @@
 
     below = from_behind(spectra, "chan", -1)
     far_routes = [[(c + away, c) for c in range(1, n_chan - away)] for away in range(2, reach)]
+    far = [lax.ppermute(spectra, "chan", route) for route in far_routes]
     power, copied = pl.pallas_call(
         power_kernel,
         out_shape=[
@@ -251,9 +263,9 @@
             in_specs=[VMEM], out_specs=VMEM, compiler_params=params, cost_estimate=cost(ch, ch),
         )(block)
 
-    def whiten(block, others):
-        return pl.pallas_call(
-            functools.partial(whiten_kernel, n_bins),
+    def whiten(block, others, add_own):
+        return pl.pallas_call(
+            functools.partial(whiten_kernel, n_bins, add_own),
             out_shape=jax.ShapeDtypeStruct(block.shape, jnp.bfloat16),
             in_specs=[VMEM] * (1 + len(others)), out_specs=VMEM, compiler_params=params,
         )(block, *others)
@@ -294,8 +306,16 @@
             in_specs=[VMEM] * n_freq, out_specs=[VMEM] * n_win, compiler_params=params,
         )(*turns(parts, "freq", n_freq))
 
-    white = whiten(copied, swap(power))
-    far = [lax.ppermute(white, "chan", route) for route in far_routes]
+    others = swap(power)
+    white, whole_power = pl.pallas_call(
+        functools.partial(own_kernel, n_bins),
+        out_shape=[
+            jax.ShapeDtypeStruct(spectra.shape, jnp.bfloat16),
+            jax.ShapeDtypeStruct((w_dev, ch, LANES), jnp.float32),
+        ],
+        in_specs=[VMEM] * (1 + len(others)), out_specs=[VMEM] * 2, compiler_params=params,
+    )(copied, *others)
+    far_powers = [lax.ppermute(whole_power, "chan", route) for route in far_routes]
     above = lax.ppermute(white, "chan", [(c - 1, c) for c in range(1, n_chan - 1)])
     half_lags = 2 * np.arange(LAGS // 2) + 1
     coarse = phases(np.arange(0, n_bins, FINE), half_lags)
@@ -307,9 +327,10 @@
         in_specs=[VMEM], out_specs=VMEM, compiler_params=params, cost_estimate=cost(ch, ch),
     )(ends)
     own = kept(white)
-    below = whiten(below, swap(half_power(below)))
+    below = whiten(below, swap(half_power(below)), True)
     parts = pairs(own, [white, below], False)
-    far, parts = lax.optimization_barrier((far, parts))
+    far, far_powers, parts = lax.optimization_barrier((far, far_powers, parts))
+    far = [whiten(block, [power], False) for block, power in zip(far, far_powers)]
     above, far = lax.optimization_barrier((above, far))
     kinds = [jnp.float32] + [jnp.bfloat16] * (n_win - 1)
     near = turns(split_windows(parts, kinds), "win", n_win)

time: 32.4 us -> 33.2 us (1.025)
    ppermute x2, waiting for transfers between devices: 0.86 us -> 0.19 us  [swap(): return [lax.ppermute(power, 'freq', route) for route in routes]]
    ppermute x1 -> x2, starting transfers between devices: 0.68 us -> 1.33 us  [the longest x1 0.67 us: local(): far = [lax.ppermute(spectra, 'chan', route) for route in far_routes]]
    ppermute x1, waiting for transfers between devices: 5.66 us -> 6.29 us  [local(): arrived.append(lax.ppermute(block, ('chan', 'win', 'freq'), route))]
    ppermute x1, starting transfers between devices: 6.09 us -> 5.59 us  [local(): lax.ppermute(white, 'chan', [(c - 1, c) for c in range(1, n_chan - 1)])]
    ppermute x1, waiting for transfers between devices: 0.7 us -> 1.14 us  [from_behind(): return lax.ppermute(block, axis, route)]
  transfers between devices with their start and end apart: 10 -> 11, of which waited for: 5 -> 5; matrix products, arithmetic and copies ran while one was open for 1% -> 1% of each run, Pallas kernels for 14% -> 15%
where the time goes in v20:
time: 33.2 us; the launch traced here: 32.9 us
  starting transfers between devices  12.7 us (38%)
  waiting for transfers between devices  9.61 us (29%)
  Pallas kernels  8.3 us (25%)
  local copies, waits for them, and re-layouts  2.12 us (6%)
    ppermute x1, waiting for transfers between devices, local(): arrived.append(lax.ppermute(block, ('chan', 'win', 'freq'), route))  6.29 us
    ppermute x1, starting transfers between devices, local(): lax.ppermute(white, 'chan', [(c - 1, c) for c in range(1, n_chan - 1)])  5.59 us
    pallas_call x2, Pallas kernels, pairs(): pl.pallas_call(functools.partial(pairs_kernel, n, n_win, n_freq, by_windo...  5.02 us
    ppermute x4, starting transfers between devices, turns(): received.append(lax.ppermute(parts[turn], axis, route))  2.69 us
    ppermute x4, waiting for transfers between devices, turns(): received.append(lax.ppermute(parts[turn], axis, route))  1.98 us
    unnamed x10, local copies, waits for them, and re-layouts  1.95 us
    ppermute x1, starting transfers between devices, local(): arrived.append(lax.ppermute(block, ('chan', 'win', 'freq'), route))  1.29 us
    ppermute x1, starting transfers between devices, from_behind(): return lax.ppermute(block, axis, route)  1.28 us
  transfers between devices with their start and end apart: 11, of which 5 were waited for; matrix products, arithmetic and copies ran while one was open for 1% of the time, Pallas kernels for 15%

profile of v20, /device:TPU:0, one launch (start us, length us, event | category | flops | bytes accessed | tf_op | source)
XLA Modules:
  0.0 32.9 jit_solution(1023414105846597698)
XLA Ops:
  0.0 1.3 %collective-permute-start.3 = (bf16[8,2,8,1024]{3,2,1,0:T(8,128)(2,1)}, bf16[8,2,8,1024]{3,2,1,0:T(8,128)(2,1)S(1)}, u32[]{:S(2)}, u32[]{:S(2)}) collective-permute-start(bf16[8,2,8,1024]{3,2,1,0:T(8,128)(2,1)} %x_ref.1), channel_id=1, source_target_pairs={{4,0},{8,4},{12,8},{5,1},{9,5},{13,9},{6,2},{10,6},{14,10},{7,3},{... | collective-permute-start | bytes 786440 | tf_op jit(solution)/shard_map/ppermute | solution.py:26
  1.3 0.0 copy-start.1
  1.3 0.9 %copy-done.1 = bf16[8,2,8,1024]{3,2,1,0:T(8,128)(2,1)S(1)} copy-done((bf16[8,2,8,1024]{3,2,1,0:T(8,128)(2,1)S(1)}, bf16[8,2,8,1024]{3,2,1,0:T(8,128)(2,1)}, u32[]{:S(2)}) %copy-start.1) | copy-done | bytes 262168
  2.2 0.0 copy-start.3
  2.2 0.0 copy-start.2
  2.2 0.1 shard_map.55
  2.4 0.5 %collective-permute-start.1 = (f32[8,8,1]{2,1,0:T(8,128)S(1)}, f32[8,8,1]{2,1,0:T(8,128)S(1)}, u32[]{:S(2)}, u32[]{:S(2)}) collective-permute-start(f32[8,8,1]{2,1,0:T(8,128)S(1)} %get-tuple-element.26), channel_id=1, source_target_pairs={{0,1},{1,0},{2,3},{3,2},{4,5},{5,4},{6,7},{7,6},{8,9},{9,8},{10,11... | collective-permute-start | bytes 776 | tf_op jit(solution)/shard_map/ppermute | solution.py:257
  2.8 0.7 %collective-permute-start = (bf16[8,2,8,1024]{3,2,1,0:T(8,128)(2,1)S(1)}, bf16[8,2,8,1024]{3,2,1,0:T(8,128)(2,1)S(1)}, u32[]{:S(2)}, u32[]{:S(2)}) collective-permute-start(bf16[8,2,8,1024]{3,2,1,0:T(8,128)(2,1)S(1)} %copy-done.1), channel_id=1, source_target_pairs={{12,4},{13,5},{14,6},{15,7},{28,20},{29,21},{30,22},{31,23}} | collective-permute-start | bytes 786440 | tf_op jit(solution)/shard_map/ppermute | solution.py:243
  3.5 0.2 collective-permute-done.1.refs_0_
  3.7 0.3 shard_map.56
  4.0 5.6 %collective-permute-start.7 = (bf16[8,2,8,1024]{3,2,1,0:T(8,128)(2,1)S(1)}, bf16[8,2,8,1024]{3,2,1,0:T(8,128)(2,1)S(1)}, u32[]{:S(2)}, u32[]{:S(2)}) collective-permute-start(bf16[8,2,8,1024]{3,2,1,0:T(8,128)(2,1)S(1)} %get-tuple-element.29.white_ref.refs_0_), channel_id=1, source_target_pairs={{0,4},{4,8},{1,5},{5,9},{2,6},{6,10},{3,7},{7,11},{16,20},{20,24},... | collective-permute-start | bytes 786440 | tf_op jit(solution)/shard_map/ppermute | solution.py:319
  9.6 0.7 %collective-permute-start.2 = (f32[8,8,128]{2,1,0:T(8,128)S(1)}, f32[8,8,128]{2,1,0:T(8,128)S(1)}, u32[]{:S(2)}, u32[]{:S(2)}) collective-permute-start(f32[8,8,128]{2,1,0:T(8,128)S(1)} %get-tuple-element.27), channel_id=1, source_target_pairs={{12,4},{13,5},{14,6},{15,7},{28,20},{29,21},{30,22},{31,23}} | collective-permute-start | bytes 98312 | tf_op jit(solution)/shard_map/ppermute | solution.py:318
  10.3 1.1 %collective-permute-done.3.x_ref = bf16[8,2,8,1024]{3,2,1,0:T(8,128)(2,1)S(1)} collective-permute-done((bf16[8,2,8,1024]{3,2,1,0:T(8,128)(2,1)}, bf16[8,2,8,1024]{3,2,1,0:T(8,128)(2,1)S(1)}, u32[]{:S(2)}, u32[]{:S(2)}) %collective-permute-start.3) | collective-permute-done | bytes 262176 | tf_op jit(solution)/shard_map/ppermute | solution.py:26
  11.4 0.1 shard_map.58
  11.6 0.0 collective-permute-start.4
  11.6 0.0 copy-start
  11.6 1.0 %copy-done = f32[2,96,512]{2,1,0:T(8,128)S(1)} copy-done((f32[2,96,512]{2,1,0:T(8,128)S(1)}, f32[2,96,512]{2,1,0:T(8,128)}, u32[]{:S(2)}) %copy-start) | copy-done | bytes 393240
  12.6 1.2 %shard_map.60.refs_3_ = bf16[4,1024,512]{2,1,0:T(8,128)(2,1)S(1)} custom-call(f32[2,96,512]{2,1,0:T(8,128)S(1)} %copy-done), custom_call_target="tpu_custom_call" | custom-call | flops 8 | bytes 8 | tf_op jit(solution)/shard_map/pallas_call | solution.py:324
  13.8 0.0 copy-done.3
  13.8 0.1 shard_map.57.base_ref
  13.9 0.0 collective-permute-done.4.refs_0_
  13.9 0.2 shard_map.59.refs_1_.refs_0_
  14.2 0.0 copy-done.2
  14.2 2.5 %shard_map.61 = (f32[2,2,64,256]{3,2,1,0:T(8,128)S(1)}, f32[2,2,64,256]{3,2,1,0:T(8,128)S(1)}) custom-call(f32[8,2,8,1024]{3,2,1,0:T(8,128)S(1)} %shard_map.57.base_ref, bf16[8,2,8,1024]{3,2,1,0:T(8,128)(2,1)S(1)} %get-tuple-element.29.white_ref.refs_0_, bf16[8,2,8,1024]{3,2,1,0:T(8,128)(2,1)S(1)} %shard_map.59.refs_1_.refs_0_, f32[2,2,1024]{2,1,0:T(2,128)S(1)} %copy-done.2, ...), custom_call_target="tpu_custom_call" | custom-call | flops 8 | bytes 8 | tf_op jit(solution)/shard_map/pallas_call | solution.py:282
  16.7 0.0 copy-start.4
  16.7 0.0 collective-permute-done.2.refs_0_
  16.7 0.0 collective-permute-done.x_ref
  16.7 0.1 shard_map.63.refs_1_
  16.8 0.0 collective-permute-done.7.white_ref
  16.9 0.1 shard_map.64.base_ref
  17.0 2.5 %shard_map.65 = (f32[2,2,64,256]{3,2,1,0:T(8,128)S(1)}, f32[2,2,64,256]{3,2,1,0:T(8,128)S(1)}) custom-call(f32[8,2,8,1024]{3,2,1,0:T(8,128)S(1)} %shard_map.64.base_ref, bf16[8,2,8,1024]{3,2,1,0:T(8,128)(2,1)S(1)} %shard_map.59.refs_1_.refs_0_, bf16[8,2,8,1024]{3,2,1,0:T(8,128)(2,1)S(1)} %shard_map.63.refs_1_, f32[2,2,1024]{2,1,0:T(2,128)S(1)} %copy-done.2, ...), custom_call_target="tpu_custom_call" | custom-call | flops 8 | bytes 8 | tf_op jit(solution)/shard_map/pallas_call | solution.py:282
  19.5 0.6 %collective-permute-start.8 = (f32[2,2,64,256]{3,2,1,0:T(8,128)S(1)}, f32[2,2,64,256]{3,2,1,0:T(8,128)S(1)}, u32[]{:S(2)}, u32[]{:S(2)}) collective-permute-start(f32[2,2,64,256]{3,2,1,0:T(8,128)S(1)} %get-tuple-element.42), channel_id=1, source_target_pairs={{0,1},{1,0},{2,3},{3,2},{4,5},{5,4},{6,7},{7,6},{8,9},{9,8},{10,11... | collective-permute-start | bytes 786440 | tf_op jit(solution)/shard_map/ppermute | solution.py:298
  20.0 0.1 collective-permute-start.5
  20.1 1.1 %collective-permute-done.8.refs_1_ = f32[2,2,64,256]{3,2,1,0:T(8,128)S(1)} collective-permute-done((f32[2,2,64,256]{3,2,1,0:T(8,128)S(1)}, f32[2,2,64,256]{3,2,1,0:T(8,128)S(1)}, u32[]{:S(2)}, u32[]{:S(2)}) %collective-permute-start.8) | collective-permute-done | bytes 262176 | tf_op jit(solution)/shard_map/ppermute | solution.py:298
  21.2 1.3 %collective-permute-start.9 = (bf16[2,2,64,256]{3,2,1,0:T(8,128)(2,1)S(1)}, bf16[2,2,64,256]{3,2,1,0:T(8,128)(2,1)S(1)}, u32[]{:S(2)}, u32[]{:S(2)}) collective-permute-start(bf16[2,2,64,256]{3,2,1,0:T(8,128)(2,1)S(1)} %shard_map.66), channel_id=1, source_target_pairs={{4,0},{5,3},{6,2},{7,1},{8,4},{9,7},{10,6},{11,5},{20,16},{21,19},... | collective-permute-start | bytes 393224 | tf_op jit(solution)/shard_map/ppermute | solution.py:351
  22.5 0.0 collective-permute-done.5.refs_1_
  22.6 1.7 %collective-permute-start.6 = (bf16[2,64,256]{2,1,0:T(8,128)(2,1)S(1)}, bf16[2,64,256]{2,1,0:T(8,128)(2,1)S(1)}, u32[]{:S(2)}, u32[]{:S(2)}) collective-permute-start(bf16[2,64,256]{2,1,0:T(8,128)(2,1)S(1)} %get-tuple-element.36), channel_id=1, source_target_pairs={{0,2},{2,0},{1,3},{3,1},{4,6},{6,4},{5,7},{7,5},{8,10},{10,8},{9,1... | collective-permute-start | bytes 196616 | tf_op jit(solution)/shard_map/ppermute | solution.py:298
  24.3 6.3 %collective-permute-done.9.refs_0_ = bf16[2,2,64,256]{3,2,1,0:T(8,128)(2,1)S(1)} collective-permute-done((bf16[2,2,64,256]{3,2,1,0:T(8,128)(2,1)S(1)}, bf16[2,2,64,256]{3,2,1,0:T(8,128)(2,1)S(1)}, u32[]{:S(2)}, u32[]{:S(2)}) %collective-permute-start.9) | collective-permute-done | bytes 131104 | tf_op jit(solution)/shard_map/ppermute | solution.py:351
  30.6 0.3 collective-permute-start.10
  30.9 0.0 copy-done.4
  30.9 0.1 broadcast_in_dim.3
  31.0 0.1 broadcast_in_dim_reshape.4.factor_ref
  31.1 0.0 collective-permute-done.6.refs_1_
  31.1 0.9 %collective-permute-done.10.refs_3_ = f32[2,64,256]{2,1,0:T(8,128)S(1)} collective-permute-done((f32[2,64,256]{2,1,0:T(8,128)S(1)}, f32[2,64,256]{2,1,0:T(8,128)S(1)}, u32[]{:S(2)}, u32[]{:S(2)}) %collective-permute-start.10) | collective-permute-done | bytes 131104 | tf_op jit(solution)/shard_map/ppermute | solution.py:298
  32.0 0.9 %shard_map.68 = f32[8,4,8,256]{3,2,1,0:T(8,128)} custom-call(f32[4,64,1]{2,1,0:T(8,128)S(1)} %broadcast_in_dim_reshape.4.factor_ref, f32[2,64,256]{2,1,0:T(8,128)S(1)} %get-tuple-element.35.refs_0_, bf16[2,64,256]{2,1,0:T(8,128)(2,1)S(1)} %collective-permute-done.6.refs_1_, f32[2,64,256]{2,1,0:T(8,128)S(1)} %get-tuple-element.43.refs_2_, ...), custom_call_target="tpu_custom_call" | custom-call | tf_op jit(solution)/shard_map/pallas_call | solution.py:360
  (4 shorter events, 0.1 us)
Async XLA Ops:
  0.0 11.4 %collective-permute-start.3 = (bf16[8,2,8,1024]{3,2,1,0:T(8,128)(2,1)}, bf16[8,2,8,1024]{3,2,1,0:T(8,128)(2,1)S(1)}, u32[]{:S(2)}, u32[]{:S(2)}) collective-permute-start(bf16[8,2,8,1024]{3,2,1,0:T(8,128)(2,1)} %x_ref.1), channel_id=1, source_target_pairs={{4,0},{8,4},{12,8},{5,1},{9,5},{13,9},{6,2},{10,6},{14,10},{7,3},{... | collective-permute-start | bytes 786440 | tf_op jit(solution)/shard_map/ppermute | solution.py:26
  1.3 1.0 %copy-start.1 = (bf16[8,2,8,1024]{3,2,1,0:T(8,128)(2,1)S(1)}, bf16[8,2,8,1024]{3,2,1,0:T(8,128)(2,1)}, u32[]{:S(2)}) copy-start(bf16[8,2,8,1024]{3,2,1,0:T(8,128)(2,1)} %x_ref.1) | copy-start | bytes 786436
  2.2 11.5 %copy-start.3 = (s32[8]{0:T(128)S(1)}, s32[8]{0:T(128)}, u32[]{:S(2)}) copy-start(s32[8]{0:T(128)} %param.6) | copy-start | bytes 100
  2.2 11.9 %copy-start.2 = (f32[2,2,1024]{2,1,0:T(2,128)S(1)}, f32[2,2,1024]{2,1,0:T(2,128)}, u32[]{:S(2)}) copy-start(f32[2,2,1024]{2,1,0:T(2,128)} %constant.6.clone.refs_2_) | copy-start | bytes 49156
  2.4 1.3 %collective-permute-start.1 = (f32[8,8,1]{2,1,0:T(8,128)S(1)}, f32[8,8,1]{2,1,0:T(8,128)S(1)}, u32[]{:S(2)}, u32[]{:S(2)}) collective-permute-start(f32[8,8,1]{2,1,0:T(8,128)S(1)} %get-tuple-element.26), channel_id=1, source_target_pairs={{0,1},{1,0},{2,3},{3,2},{4,5},{5,4},{6,7},{7,6},{8,9},{9,8},{10,11... | collective-permute-start | bytes 776 | tf_op jit(solution)/shard_map/ppermute | solution.py:257
  2.8 13.9 %collective-permute-start = (bf16[8,2,8,1024]{3,2,1,0:T(8,128)(2,1)S(1)}, bf16[8,2,8,1024]{3,2,1,0:T(8,128)(2,1)S(1)}, u32[]{:S(2)}, u32[]{:S(2)}) collective-permute-start(bf16[8,2,8,1024]{3,2,1,0:T(8,128)(2,1)S(1)} %copy-done.1), channel_id=1, source_target_pairs={{12,4},{13,5},{14,6},{15,7},{28,20},{29,21},{30,22},{31,23}} | collective-permute-start | bytes 786440 | tf_op jit(solution)/shard_map/ppermute | solution.py:243
  4.0 12.8 %collective-permute-start.7 = (bf16[8,2,8,1024]{3,2,1,0:T(8,128)(2,1)S(1)}, bf16[8,2,8,1024]{3,2,1,0:T(8,128)(2,1)S(1)}, u32[]{:S(2)}, u32[]{:S(2)}) collective-permute-start(bf16[8,2,8,1024]{3,2,1,0:T(8,128)(2,1)S(1)} %get-tuple-element.29.white_ref.refs_0_), channel_id=1, source_target_pairs={{0,4},{4,8},{1,5},{5,9},{2,6},{6,10},{3,7},{7,11},{16,20},{20,24},... | collective-permute-start | bytes 786440 | tf_op jit(solution)/shard_map/ppermute | solution.py:319
  9.6 7.1 %collective-permute-start.2 = (f32[8,8,128]{2,1,0:T(8,128)S(1)}, f32[8,8,128]{2,1,0:T(8,128)S(1)}, u32[]{:S(2)}, u32[]{:S(2)}) collective-permute-start(f32[8,8,128]{2,1,0:T(8,128)S(1)} %get-tuple-element.27), channel_id=1, source_target_pairs={{12,4},{13,5},{14,6},{15,7},{28,20},{29,21},{30,22},{31,23}} | collective-permute-start | bytes 98312 | tf_op jit(solution)/shard_map/ppermute | solution.py:318
  11.6 2.3 %collective-permute-start.4 = (f32[8,8,1]{2,1,0:T(8,128)S(1)}, f32[8,8,1]{2,1,0:T(8,128)S(1)}, u32[]{:S(2)}, u32[]{:S(2)}) collective-permute-start(f32[8,8,1]{2,1,0:T(8,128)S(1)} %shard_map.58), channel_id=1, source_target_pairs={{0,1},{1,0},{2,3},{3,2},{4,5},{5,4},{6,7},{7,6},{8,9},{9,8},{10,11... | collective-permute-start | bytes 776 | tf_op jit(solution)/shard_map/ppermute | solution.py:257
  11.6 1.0 %copy-start = (f32[2,96,512]{2,1,0:T(8,128)S(1)}, f32[2,96,512]{2,1,0:T(8,128)}, u32[]{:S(2)}) copy-start(f32[2,96,512]{2,1,0:T(8,128)} %constant.7.clone.base_ref) | copy-start | bytes 1179652
  16.7 14.3 %copy-start.4 = (s32[8,4]{0,1:T(4,128)S(1)}, s32[8,4]{0,1:T(4,128)}, u32[]{:S(2)}) copy-start(s32[8,4]{0,1:T(4,128)} %param.7) | copy-start | bytes 388
  19.5 1.7 %collective-permute-start.8 = (f32[2,2,64,256]{3,2,1,0:T(8,128)S(1)}, f32[2,2,64,256]{3,2,1,0:T(8,128)S(1)}, u32[]{:S(2)}, u32[]{:S(2)}) collective-permute-start(f32[2,2,64,256]{3,2,1,0:T(8,128)S(1)} %get-tuple-element.42), channel_id=1, source_target_pairs={{0,1},{1,0},{2,3},{3,2},{4,5},{5,4},{6,7},{7,6},{8,9},{9,8},{10,11... | collective-permute-start | bytes 786440 | tf_op jit(solution)/shard_map/ppermute | solution.py:298
  20.0 2.5 %collective-permute-start.5 = (f32[2,2,64,256]{3,2,1,0:T(8,128)S(1)}, f32[2,2,64,256]{3,2,1,0:T(8,128)S(1)}, u32[]{:S(2)}, u32[]{:S(2)}) collective-permute-start(f32[2,2,64,256]{3,2,1,0:T(8,128)S(1)} %get-tuple-element.34), channel_id=1, source_target_pairs={{0,1},{1,0},{2,3},{3,2},{4,5},{5,4},{6,7},{7,6},{8,9},{9,8},{10,11... | collective-permute-start | bytes 786440 | tf_op jit(solution)/shard_map/ppermute | solution.py:298
  21.2 9.4 %collective-permute-start.9 = (bf16[2,2,64,256]{3,2,1,0:T(8,128)(2,1)S(1)}, bf16[2,2,64,256]{3,2,1,0:T(8,128)(2,1)S(1)}, u32[]{:S(2)}, u32[]{:S(2)}) collective-permute-start(bf16[2,2,64,256]{3,2,1,0:T(8,128)(2,1)S(1)} %shard_map.66), channel_id=1, source_target_pairs={{4,0},{5,3},{6,2},{7,1},{8,4},{9,7},{10,6},{11,5},{20,16},{21,19},... | collective-permute-start | bytes 393224 | tf_op jit(solution)/shard_map/ppermute | solution.py:351
  22.6 8.5 %collective-permute-start.6 = (bf16[2,64,256]{2,1,0:T(8,128)(2,1)S(1)}, bf16[2,64,256]{2,1,0:T(8,128)(2,1)S(1)}, u32[]{:S(2)}, u32[]{:S(2)}) collective-permute-start(bf16[2,64,256]{2,1,0:T(8,128)(2,1)S(1)} %get-tuple-element.36), channel_id=1, source_target_pairs={{0,2},{2,0},{1,3},{3,1},{4,6},{6,4},{5,7},{7,5},{8,10},{10,8},{9,1... | collective-permute-start | bytes 196616 | tf_op jit(solution)/shard_map/ppermute | solution.py:298
  30.6 1.4 %collective-permute-start.10 = (f32[2,64,256]{2,1,0:T(8,128)S(1)}, f32[2,64,256]{2,1,0:T(8,128)S(1)}, u32[]{:S(2)}, u32[]{:S(2)}) collective-permute-start(f32[2,64,256]{2,1,0:T(8,128)S(1)} %get-tuple-element.44), channel_id=1, source_target_pairs={{0,1},{1,0},{2,3},{3,2},{4,5},{5,4},{6,7},{7,6},{8,9},{9,8},{10,11... | collective-permute-start | bytes 393224 | tf_op jit(solution)/shard_map/ppermute | solution.py:298

commit v21 on v18

--- a/solution.py
+++ b/solution.py
@@ -140,9 +140,13 @@
         return carry
 
     lax.fori_loop(0, f_dev // LANES, body, 0)
-    for part in range(2):
+
+    def transform(part, carry):
         both = dot(rows_ref[part], table_ref[2 * part])
         sums_ref[part] = both[:count] + both[count:] + dot(rows_ref[part, :count], table_ref[2 * part + 1])
+        return carry
+
+    lax.fori_loop(0, 2, transform, 0)
     for turn_freq, out_ref in enumerate(out_refs):
         core = (freq + turn_freq) % n_freq
         for turn_win in range(n_win):

time: 32.4 us -> 32.7 us (level)
  Pallas kernels: 8.12 us -> 8.45 us
    pallas_call x2, Pallas kernels: 5.02 us -> 5.35 us  [pairs(): pl.pallas_call(functools.partial(pairs_kernel, n, n_win, n_freq, by_windo...]
  transfers between devices with their start and end apart: 10 -> 10, of which waited for: 5 -> 5; matrix products, arithmetic and copies ran while one was open for 1% -> 1% of each run, Pallas kernels for 14% -> 15%
where the time goes in v21:
time: 32.7 us; the launch traced here: 32.5 us
  starting transfers between devices  12.3 us (38%)
  waiting for transfers between devices  9.46 us (29%)
  Pallas kernels  8.45 us (26%)
  local copies, waits for them, and re-layouts  2.11 us (6%)
    ppermute x1, starting transfers between devices, local(): lax.ppermute(white, 'chan', [(c - 1, c) for c in range(1, n_chan - 1)])  6.09 us
    ppermute x1, waiting for transfers between devices, local(): arrived.append(lax.ppermute(block, ('chan', 'win', 'freq'), route))  5.68 us
    pallas_call x2, Pallas kernels, pairs(): pl.pallas_call(functools.partial(pairs_kernel, n, n_win, n_freq, by_windo...  5.35 us
    ppermute x4, starting transfers between devices, turns(): received.append(lax.ppermute(parts[turn], axis, route))  2.43 us
    ppermute x4, waiting for transfers between devices, turns(): received.append(lax.ppermute(parts[turn], axis, route))  2.22 us
    unnamed x10, local copies, waits for them, and re-layouts  1.95 us
    ppermute x1, starting transfers between devices, local(): arrived.append(lax.ppermute(block, ('chan', 'win', 'freq'), route))  1.29 us
    ppermute x1, starting transfers between devices, from_behind(): return lax.ppermute(block, axis, route)  1.28 us
  transfers between devices with their start and end apart: 10, of which 5 were waited for; matrix products, arithmetic and copies ran while one was open for 1% of the time, Pallas kernels for 15%

profile of v21, /device:TPU:0, one launch (start us, length us, event | category | flops | bytes accessed | tf_op | source)
XLA Modules:
  0.0 32.5 jit_solution(11415139171348339773)
XLA Ops:
  0.0 1.3 %collective-permute-start.2 = (bf16[8,2,8,1024]{3,2,1,0:T(8,128)(2,1)}, bf16[8,2,8,1024]{3,2,1,0:T(8,128)(2,1)S(1)}, u32[]{:S(2)}, u32[]{:S(2)}) collective-permute-start(bf16[8,2,8,1024]{3,2,1,0:T(8,128)(2,1)} %x_ref.1), channel_id=1, source_target_pairs={{4,0},{8,4},{12,8},{5,1},{9,5},{13,9},{6,2},{10,6},{14,10},{7,3},{... | collective-permute-start | bytes 786440 | tf_op jit(solution)/shard_map/ppermute | solution.py:26
  1.3 0.0 copy-start.1
  1.3 0.9 %copy-done.1 = bf16[8,2,8,1024]{3,2,1,0:T(8,128)(2,1)S(1)} copy-done((bf16[8,2,8,1024]{3,2,1,0:T(8,128)(2,1)S(1)}, bf16[8,2,8,1024]{3,2,1,0:T(8,128)(2,1)}, u32[]{:S(2)}) %copy-start.1) | copy-done | bytes 262168
  2.2 0.0 copy-start.3
  2.2 0.0 copy-start.2
  2.2 0.1 shard_map.55
  2.4 0.5 %collective-permute-start = (f32[8,8,1]{2,1,0:T(8,128)S(1)}, f32[8,8,1]{2,1,0:T(8,128)S(1)}, u32[]{:S(2)}, u32[]{:S(2)}) collective-permute-start(f32[8,8,1]{2,1,0:T(8,128)S(1)} %get-tuple-element.23), channel_id=1, source_target_pairs={{0,1},{1,0},{2,3},{3,2},{4,5},{5,4},{6,7},{7,6},{8,9},{9,8},{10,11... | collective-permute-start | bytes 776 | tf_op jit(solution)/shard_map/ppermute | solution.py:249
  2.8 0.9 %collective-permute-done.refs_0_ = f32[8,8,1]{2,1,0:T(8,128)S(1)} collective-permute-done((f32[8,8,1]{2,1,0:T(8,128)S(1)}, f32[8,8,1]{2,1,0:T(8,128)S(1)}, u32[]{:S(2)}, u32[]{:S(2)}) %collective-permute-start) | collective-permute-done | bytes 288 | tf_op jit(solution)/shard_map/ppermute | solution.py:249
  3.7 0.2 shard_map.56.white_ref.refs_0_
  3.9 0.7 %collective-permute-start.1 = (bf16[8,2,8,1024]{3,2,1,0:T(8,128)(2,1)S(1)}, bf16[8,2,8,1024]{3,2,1,0:T(8,128)(2,1)S(1)}, u32[]{:S(2)}, u32[]{:S(2)}) collective-permute-start(bf16[8,2,8,1024]{3,2,1,0:T(8,128)(2,1)S(1)} %shard_map.56.white_ref.refs_0_), channel_id=1, source_target_pairs={{12,4},{13,5},{14,6},{15,7},{28,20},{29,21},{30,22},{31,23}} | collective-permute-start | bytes 786440 | tf_op jit(solution)/shard_map/ppermute | solution.py:302
  4.6 6.1 %collective-permute-start.6 = (bf16[8,2,8,1024]{3,2,1,0:T(8,128)(2,1)S(1)}, bf16[8,2,8,1024]{3,2,1,0:T(8,128)(2,1)S(1)}, u32[]{:S(2)}, u32[]{:S(2)}) collective-permute-start(bf16[8,2,8,1024]{3,2,1,0:T(8,128)(2,1)S(1)} %shard_map.56.white_ref.refs_0_), channel_id=1, source_target_pairs={{0,4},{4,8},{1,5},{5,9},{2,6},{6,10},{3,7},{7,11},{16,20},{20,24},... | collective-permute-start | bytes 786440 | tf_op jit(solution)/shard_map/ppermute | solution.py:303
  10.7 0.7 %collective-permute-done.2.x_ref = bf16[8,2,8,1024]{3,2,1,0:T(8,128)(2,1)S(1)} collective-permute-done((bf16[8,2,8,1024]{3,2,1,0:T(8,128)(2,1)}, bf16[8,2,8,1024]{3,2,1,0:T(8,128)(2,1)S(1)}, u32[]{:S(2)}, u32[]{:S(2)}) %collective-permute-start.2) | collective-permute-done | bytes 262176 | tf_op jit(solution)/shard_map/ppermute | solution.py:26
  11.4 0.1 shard_map.58
  11.6 0.0 collective-permute-start.3
  11.6 0.0 copy-start
  11.6 1.0 %copy-done = f32[2,96,512]{2,1,0:T(8,128)S(1)} copy-done((f32[2,96,512]{2,1,0:T(8,128)S(1)}, f32[2,96,512]{2,1,0:T(8,128)}, u32[]{:S(2)}) %copy-start) | copy-done | bytes 393240
  12.6 1.2 %shard_map.60.refs_3_ = bf16[4,1024,512]{2,1,0:T(8,128)(2,1)S(1)} custom-call(f32[2,96,512]{2,1,0:T(8,128)S(1)} %copy-done), custom_call_target="tpu_custom_call" | custom-call | flops 8 | bytes 8 | tf_op jit(solution)/shard_map/pallas_call | solution.py:308
  13.8 0.0 copy-done.3
  13.8 0.1 shard_map.57.base_ref
  13.9 0.0 collective-permute-done.3.refs_0_
  13.9 0.2 shard_map.59.refs_1_.refs_0_
  14.2 0.0 copy-done.2
  14.2 2.7 %shard_map.61 = (f32[2,2,64,256]{3,2,1,0:T(8,128)S(1)}, f32[2,2,64,256]{3,2,1,0:T(8,128)S(1)}) custom-call(f32[8,2,8,1024]{3,2,1,0:T(8,128)S(1)} %shard_map.57.base_ref, bf16[8,2,8,1024]{3,2,1,0:T(8,128)(2,1)S(1)} %shard_map.56.white_ref.refs_0_, bf16[8,2,8,1024]{3,2,1,0:T(8,128)(2,1)S(1)} %shard_map.59.refs_1_.refs_0_, f32[2,2,1024]{2,1,0:T(2,128)S(1)} %copy-done.2, ...), custom_call_target="tpu_custom_call" | custom-call | flops 8 | bytes 8 | tf_op jit(solution)/shard_map/pallas_call | solution.py:274
  16.8 0.0 copy-start.4
  16.9 0.0 collective-permute-done.1.refs_1_
  16.9 0.0 collective-permute-done.6.white_ref
  16.9 0.1 shard_map.63.base_ref
  17.0 2.7 %shard_map.64 = (f32[2,2,64,256]{3,2,1,0:T(8,128)S(1)}, f32[2,2,64,256]{3,2,1,0:T(8,128)S(1)}) custom-call(f32[8,2,8,1024]{3,2,1,0:T(8,128)S(1)} %shard_map.63.base_ref, bf16[8,2,8,1024]{3,2,1,0:T(8,128)(2,1)S(1)} %shard_map.59.refs_1_.refs_0_, bf16[8,2,8,1024]{3,2,1,0:T(8,128)(2,1)S(1)} %collective-permute-done.1.refs_1_, f32[2,2,1024]{2,1,0:T(2,128)S(1)} %copy-done.2, ...), custom_call_target="tpu_custom_call" | custom-call | flops 8 | bytes 8 | tf_op jit(solution)/shard_map/pallas_call | solution.py:274
  19.7 0.6 %collective-permute-start.7 = (f32[2,2,64,256]{3,2,1,0:T(8,128)S(1)}, f32[2,2,64,256]{3,2,1,0:T(8,128)S(1)}, u32[]{:S(2)}, u32[]{:S(2)}) collective-permute-start(f32[2,2,64,256]{3,2,1,0:T(8,128)S(1)} %get-tuple-element.36), channel_id=1, source_target_pairs={{0,1},{1,0},{2,3},{3,2},{4,5},{5,4},{6,7},{7,6},{8,9},{9,8},{10,11... | collective-permute-start | bytes 786440 | tf_op jit(solution)/shard_map/ppermute | solution.py:290
  20.2 0.1 collective-permute-start.4
  20.3 1.1 %collective-permute-done.7.refs_1_ = f32[2,2,64,256]{3,2,1,0:T(8,128)S(1)} collective-permute-done((f32[2,2,64,256]{3,2,1,0:T(8,128)S(1)}, f32[2,2,64,256]{3,2,1,0:T(8,128)S(1)}, u32[]{:S(2)}, u32[]{:S(2)}) %collective-permute-start.7) | collective-permute-done | bytes 262176 | tf_op jit(solution)/shard_map/ppermute | solution.py:290
  21.4 1.3 %collective-permute-start.8 = (bf16[2,2,64,256]{3,2,1,0:T(8,128)(2,1)S(1)}, bf16[2,2,64,256]{3,2,1,0:T(8,128)(2,1)S(1)}, u32[]{:S(2)}, u32[]{:S(2)}) collective-permute-start(bf16[2,2,64,256]{3,2,1,0:T(8,128)(2,1)S(1)} %shard_map.65), channel_id=1, source_target_pairs={{4,0},{5,3},{6,2},{7,1},{8,4},{9,7},{10,6},{11,5},{20,16},{21,19},... | collective-permute-start | bytes 393224 | tf_op jit(solution)/shard_map/ppermute | solution.py:334
  22.7 0.0 collective-permute-done.4.refs_1_
  22.8 1.7 %collective-permute-start.5 = (bf16[2,64,256]{2,1,0:T(8,128)(2,1)S(1)}, bf16[2,64,256]{2,1,0:T(8,128)(2,1)S(1)}, u32[]{:S(2)}, u32[]{:S(2)}) collective-permute-start(bf16[2,64,256]{2,1,0:T(8,128)(2,1)S(1)} %get-tuple-element.31), channel_id=1, source_target_pairs={{0,2},{2,0},{1,3},{3,1},{4,6},{6,4},{5,7},{7,5},{8,10},{10,8},{9,1... | collective-permute-start | bytes 196616 | tf_op jit(solution)/shard_map/ppermute | solution.py:290
  24.5 5.7 %collective-permute-done.8.refs_0_ = bf16[2,2,64,256]{3,2,1,0:T(8,128)(2,1)S(1)} collective-permute-done((bf16[2,2,64,256]{3,2,1,0:T(8,128)(2,1)S(1)}, bf16[2,2,64,256]{3,2,1,0:T(8,128)(2,1)S(1)}, u32[]{:S(2)}, u32[]{:S(2)}) %collective-permute-start.8) | collective-permute-done | bytes 131104 | tf_op jit(solution)/shard_map/ppermute | solution.py:334
  30.2 0.1 collective-permute-start.9
  30.3 0.0 copy-done.4
  30.3 0.1 broadcast_in_dim.3
  30.4 0.1 broadcast_in_dim_reshape.4.factor_ref
  30.5 0.0 collective-permute-done.5.refs_1_
  30.5 1.1 %collective-permute-done.9.refs_3_ = f32[2,64,256]{2,1,0:T(8,128)S(1)} collective-permute-done((f32[2,64,256]{2,1,0:T(8,128)S(1)}, f32[2,64,256]{2,1,0:T(8,128)S(1)}, u32[]{:S(2)}, u32[]{:S(2)}) %collective-permute-start.9) | collective-permute-done | bytes 131104 | tf_op jit(solution)/shard_map/ppermute | solution.py:290
  31.6 0.9 %shard_map.67 = f32[8,4,8,256]{3,2,1,0:T(8,128)} custom-call(f32[4,64,1]{2,1,0:T(8,128)S(1)} %broadcast_in_dim_reshape.4.factor_ref, f32[2,64,256]{2,1,0:T(8,128)S(1)} %get-tuple-element.30.refs_0_, bf16[2,64,256]{2,1,0:T(8,128)(2,1)S(1)} %collective-permute-done.5.refs_1_, f32[2,64,256]{2,1,0:T(8,128)S(1)} %get-tuple-element.37.refs_2_, ...), custom_call_target="tpu_custom_call" | custom-call | tf_op jit(solution)/shard_map/pallas_call | solution.py:343
  (4 shorter events, 0.1 us)
Async XLA Ops:
  0.0 11.4 %collective-permute-start.2 = (bf16[8,2,8,1024]{3,2,1,0:T(8,128)(2,1)}, bf16[8,2,8,1024]{3,2,1,0:T(8,128)(2,1)S(1)}, u32[]{:S(2)}, u32[]{:S(2)}) collective-permute-start(bf16[8,2,8,1024]{3,2,1,0:T(8,128)(2,1)} %x_ref.1), channel_id=1, source_target_pairs={{4,0},{8,4},{12,8},{5,1},{9,5},{13,9},{6,2},{10,6},{14,10},{7,3},{... | collective-permute-start | bytes 786440 | tf_op jit(solution)/shard_map/ppermute | solution.py:26
  1.3 1.0 %copy-start.1 = (bf16[8,2,8,1024]{3,2,1,0:T(8,128)(2,1)S(1)}, bf16[8,2,8,1024]{3,2,1,0:T(8,128)(2,1)}, u32[]{:S(2)}) copy-start(bf16[8,2,8,1024]{3,2,1,0:T(8,128)(2,1)} %x_ref.1) | copy-start | bytes 786436
  2.2 11.5 %copy-start.3 = (s32[8]{0:T(128)S(1)}, s32[8]{0:T(128)}, u32[]{:S(2)}) copy-start(s32[8]{0:T(128)} %param.6) | copy-start | bytes 100
  2.2 11.9 %copy-start.2 = (f32[2,2,1024]{2,1,0:T(2,128)S(1)}, f32[2,2,1024]{2,1,0:T(2,128)}, u32[]{:S(2)}) copy-start(f32[2,2,1024]{2,1,0:T(2,128)} %constant.6.clone.refs_2_) | copy-start | bytes 49156
  2.4 1.3 %collective-permute-start = (f32[8,8,1]{2,1,0:T(8,128)S(1)}, f32[8,8,1]{2,1,0:T(8,128)S(1)}, u32[]{:S(2)}, u32[]{:S(2)}) collective-permute-start(f32[8,8,1]{2,1,0:T(8,128)S(1)} %get-tuple-element.23), channel_id=1, source_target_pairs={{0,1},{1,0},{2,3},{3,2},{4,5},{5,4},{6,7},{7,6},{8,9},{9,8},{10,11... | collective-permute-start | bytes 776 | tf_op jit(solution)/shard_map/ppermute | solution.py:249
  3.9 12.9 %collective-permute-start.1 = (bf16[8,2,8,1024]{3,2,1,0:T(8,128)(2,1)S(1)}, bf16[8,2,8,1024]{3,2,1,0:T(8,128)(2,1)S(1)}, u32[]{:S(2)}, u32[]{:S(2)}) collective-permute-start(bf16[8,2,8,1024]{3,2,1,0:T(8,128)(2,1)S(1)} %shard_map.56.white_ref.refs_0_), channel_id=1, source_target_pairs={{12,4},{13,5},{14,6},{15,7},{28,20},{29,21},{30,22},{31,23}} | collective-permute-start | bytes 786440 | tf_op jit(solution)/shard_map/ppermute | solution.py:302
  4.6 12.2 %collective-permute-start.6 = (bf16[8,2,8,1024]{3,2,1,0:T(8,128)(2,1)S(1)}, bf16[8,2,8,1024]{3,2,1,0:T(8,128)(2,1)S(1)}, u32[]{:S(2)}, u32[]{:S(2)}) collective-permute-start(bf16[8,2,8,1024]{3,2,1,0:T(8,128)(2,1)S(1)} %shard_map.56.white_ref.refs_0_), channel_id=1, source_target_pairs={{0,4},{4,8},{1,5},{5,9},{2,6},{6,10},{3,7},{7,11},{16,20},{20,24},... | collective-permute-start | bytes 786440 | tf_op jit(solution)/shard_map/ppermute | solution.py:303
  11.6 2.3 %collective-permute-start.3 = (f32[8,8,1]{2,1,0:T(8,128)S(1)}, f32[8,8,1]{2,1,0:T(8,128)S(1)}, u32[]{:S(2)}, u32[]{:S(2)}) collective-permute-start(f32[8,8,1]{2,1,0:T(8,128)S(1)} %shard_map.58), channel_id=1, source_target_pairs={{0,1},{1,0},{2,3},{3,2},{4,5},{5,4},{6,7},{7,6},{8,9},{9,8},{10,11... | collective-permute-start | bytes 776 | tf_op jit(solution)/shard_map/ppermute | solution.py:249
  11.6 1.0 %copy-start = (f32[2,96,512]{2,1,0:T(8,128)S(1)}, f32[2,96,512]{2,1,0:T(8,128)}, u32[]{:S(2)}) copy-start(f32[2,96,512]{2,1,0:T(8,128)} %constant.7.clone.base_ref) | copy-start | bytes 1179652
  16.8 13.4 %copy-start.4 = (s32[8,4]{0,1:T(4,128)S(1)}, s32[8,4]{0,1:T(4,128)}, u32[]{:S(2)}) copy-start(s32[8,4]{0,1:T(4,128)} %param.7) | copy-start | bytes 388
  19.7 1.7 %collective-permute-start.7 = (f32[2,2,64,256]{3,2,1,0:T(8,128)S(1)}, f32[2,2,64,256]{3,2,1,0:T(8,128)S(1)}, u32[]{:S(2)}, u32[]{:S(2)}) collective-permute-start(f32[2,2,64,256]{3,2,1,0:T(8,128)S(1)} %get-tuple-element.36), channel_id=1, source_target_pairs={{0,1},{1,0},{2,3},{3,2},{4,5},{5,4},{6,7},{7,6},{8,9},{9,8},{10,11... | collective-permute-start | bytes 786440 | tf_op jit(solution)/shard_map/ppermute | solution.py:290
  20.2 2.5 %collective-permute-start.4 = (f32[2,2,64,256]{3,2,1,0:T(8,128)S(1)}, f32[2,2,64,256]{3,2,1,0:T(8,128)S(1)}, u32[]{:S(2)}, u32[]{:S(2)}) collective-permute-start(f32[2,2,64,256]{3,2,1,0:T(8,128)S(1)} %get-tuple-element.29), channel_id=1, source_target_pairs={{0,1},{1,0},{2,3},{3,2},{4,5},{5,4},{6,7},{7,6},{8,9},{9,8},{10,11... | collective-permute-start | bytes 786440 | tf_op jit(solution)/shard_map/ppermute | solution.py:290
  21.4 8.8 %collective-permute-start.8 = (bf16[2,2,64,256]{3,2,1,0:T(8,128)(2,1)S(1)}, bf16[2,2,64,256]{3,2,1,0:T(8,128)(2,1)S(1)}, u32[]{:S(2)}, u32[]{:S(2)}) collective-permute-start(bf16[2,2,64,256]{3,2,1,0:T(8,128)(2,1)S(1)} %shard_map.65), channel_id=1, source_target_pairs={{4,0},{5,3},{6,2},{7,1},{8,4},{9,7},{10,6},{11,5},{20,16},{21,19},... | collective-permute-start | bytes 393224 | tf_op jit(solution)/shard_map/ppermute | solution.py:334
  22.8 7.7 %collective-permute-start.5 = (bf16[2,64,256]{2,1,0:T(8,128)(2,1)S(1)}, bf16[2,64,256]{2,1,0:T(8,128)(2,1)S(1)}, u32[]{:S(2)}, u32[]{:S(2)}) collective-permute-start(bf16[2,64,256]{2,1,0:T(8,128)(2,1)S(1)} %get-tuple-element.31), channel_id=1, source_target_pairs={{0,2},{2,0},{1,3},{3,1},{4,6},{6,4},{5,7},{7,5},{8,10},{10,8},{9,1... | collective-permute-start | bytes 196616 | tf_op jit(solution)/shard_map/ppermute | solution.py:290
  30.2 1.4 %collective-permute-start.9 = (f32[2,64,256]{2,1,0:T(8,128)S(1)}, f32[2,64,256]{2,1,0:T(8,128)S(1)}, u32[]{:S(2)}, u32[]{:S(2)}) collective-permute-start(f32[2,64,256]{2,1,0:T(8,128)S(1)} %get-tuple-element.38), channel_id=1, source_target_pairs={{0,1},{1,0},{2,3},{3,2},{4,5},{5,4},{6,7},{7,6},{8,9},{9,8},{10,11... | collective-permute-start | bytes 393224 | tf_op jit(solution)/shard_map/ppermute | solution.py:290

commit v22 on v21

--- a/solution.py
+++ b/solution.py
@@ -141,12 +141,15 @@
 
     lax.fori_loop(0, f_dev // LANES, body, 0)
 
-    def transform(part, carry):
-        both = dot(rows_ref[part], table_ref[2 * part])
-        sums_ref[part] = both[:count] + both[count:] + dot(rows_ref[part, :count], table_ref[2 * part + 1])
+    def transform(step, carry):
+        part = step % 2
+        lags = pl.ds(pl.multiple_of(step // 2 * BLOCK, BLOCK), BLOCK)
+        both = dot(rows_ref[part], table_ref[2 * part, :, lags])
+        low = dot(rows_ref[part, :count], table_ref[2 * part + 1, :, lags])
+        sums_ref[part, :, lags] = both[:count] + both[count:] + low
         return carry
 
-    lax.fori_loop(0, 2, transform, 0)
+    lax.fori_loop(0, 2 * (table_ref.shape[-1] // BLOCK), transform, 0)
     for turn_freq, out_ref in enumerate(out_refs):
         core = (freq + turn_freq) % n_freq
         for turn_win in range(n_win):

time: 32.7 us -> 33.3 us (1.018)
  Pallas kernels: 8.45 us -> 9.24 us
    pallas_call x2, Pallas kernels: 5.35 us -> 6.14 us  [pairs(): pl.pallas_call(functools.partial(pairs_kernel, n, n_win, n_freq, by_windo...]
  transfers between devices with their start and end apart: 10 -> 10, of which waited for: 5 -> 5; matrix products, arithmetic and copies ran while one was open for 1% -> 1% of each run, Pallas kernels for 15% -> 16%
where the time goes in v22:
time: 33.3 us; the launch traced here: 33.1 us
  starting transfers between devices  12.3 us (37%)
  waiting for transfers between devices  9.25 us (28%)
  Pallas kernels  9.24 us (28%)
  local copies, waits for them, and re-layouts  2.11 us (6%)
    pallas_call x2, Pallas kernels, pairs(): pl.pallas_call(functools.partial(pairs_kernel, n, n_win, n_freq, by_windo...  6.14 us
    ppermute x1, starting transfers between devices, local(): lax.ppermute(white, 'chan', [(c - 1, c) for c in range(1, n_chan - 1)])  6.09 us
    ppermute x1, waiting for transfers between devices, local(): arrived.append(lax.ppermute(block, ('chan', 'win', 'freq'), route))  5.47 us
    ppermute x4, starting transfers between devices, turns(): received.append(lax.ppermute(parts[turn], axis, route))  2.44 us
    ppermute x4, waiting for transfers between devices, turns(): received.append(lax.ppermute(parts[turn], axis, route))  2.22 us
    unnamed x10, local copies, waits for them, and re-layouts  1.95 us
    ppermute x1, starting transfers between devices, local(): arrived.append(lax.ppermute(block, ('chan', 'win', 'freq'), route))  1.29 us
    ppermute x1, starting transfers between devices, from_behind(): return lax.ppermute(block, axis, route)  1.28 us
  transfers between devices with their start and end apart: 10, of which 5 were waited for; matrix products, arithmetic and copies ran while one was open for 1% of the time, Pallas kernels for 16%

profile of v22, /device:TPU:0, one launch (start us, length us, event | category | flops | bytes accessed | tf_op | source)
XLA Modules:
  0.0 33.1 jit_solution(2254446908999539288)
XLA Ops:
  0.0 1.3 %collective-permute-start.2 = (bf16[8,2,8,1024]{3,2,1,0:T(8,128)(2,1)}, bf16[8,2,8,1024]{3,2,1,0:T(8,128)(2,1)S(1)}, u32[]{:S(2)}, u32[]{:S(2)}) collective-permute-start(bf16[8,2,8,1024]{3,2,1,0:T(8,128)(2,1)} %x_ref.1), channel_id=1, source_target_pairs={{4,0},{8,4},{12,8},{5,1},{9,5},{13,9},{6,2},{10,6},{14,10},{7,3},{... | collective-permute-start | bytes 786440 | tf_op jit(solution)/shard_map/ppermute | solution.py:26
  1.3 0.0 copy-start.1
  1.3 0.9 %copy-done.1 = bf16[8,2,8,1024]{3,2,1,0:T(8,128)(2,1)S(1)} copy-done((bf16[8,2,8,1024]{3,2,1,0:T(8,128)(2,1)S(1)}, bf16[8,2,8,1024]{3,2,1,0:T(8,128)(2,1)}, u32[]{:S(2)}) %copy-start.1) | copy-done | bytes 262168
  2.2 0.0 copy-start.3
  2.2 0.0 copy-start.2
  2.2 0.1 shard_map.55
  2.4 0.5 %collective-permute-start = (f32[8,8,1]{2,1,0:T(8,128)S(1)}, f32[8,8,1]{2,1,0:T(8,128)S(1)}, u32[]{:S(2)}, u32[]{:S(2)}) collective-permute-start(f32[8,8,1]{2,1,0:T(8,128)S(1)} %get-tuple-element.23), channel_id=1, source_target_pairs={{0,1},{1,0},{2,3},{3,2},{4,5},{5,4},{6,7},{7,6},{8,9},{9,8},{10,11... | collective-permute-start | bytes 776 | tf_op jit(solution)/shard_map/ppermute | solution.py:252
  2.8 0.9 %collective-permute-done.refs_0_ = f32[8,8,1]{2,1,0:T(8,128)S(1)} collective-permute-done((f32[8,8,1]{2,1,0:T(8,128)S(1)}, f32[8,8,1]{2,1,0:T(8,128)S(1)}, u32[]{:S(2)}, u32[]{:S(2)}) %collective-permute-start) | collective-permute-done | bytes 288 | tf_op jit(solution)/shard_map/ppermute | solution.py:252
  3.7 0.2 shard_map.56.white_ref.refs_0_
  3.9 0.7 %collective-permute-start.1 = (bf16[8,2,8,1024]{3,2,1,0:T(8,128)(2,1)S(1)}, bf16[8,2,8,1024]{3,2,1,0:T(8,128)(2,1)S(1)}, u32[]{:S(2)}, u32[]{:S(2)}) collective-permute-start(bf16[8,2,8,1024]{3,2,1,0:T(8,128)(2,1)S(1)} %shard_map.56.white_ref.refs_0_), channel_id=1, source_target_pairs={{12,4},{13,5},{14,6},{15,7},{28,20},{29,21},{30,22},{31,23}} | collective-permute-start | bytes 786440 | tf_op jit(solution)/shard_map/ppermute | solution.py:305
  4.6 6.1 %collective-permute-start.6 = (bf16[8,2,8,1024]{3,2,1,0:T(8,128)(2,1)S(1)}, bf16[8,2,8,1024]{3,2,1,0:T(8,128)(2,1)S(1)}, u32[]{:S(2)}, u32[]{:S(2)}) collective-permute-start(bf16[8,2,8,1024]{3,2,1,0:T(8,128)(2,1)S(1)} %shard_map.56.white_ref.refs_0_), channel_id=1, source_target_pairs={{0,4},{4,8},{1,5},{5,9},{2,6},{6,10},{3,7},{7,11},{16,20},{20,24},... | collective-permute-start | bytes 786440 | tf_op jit(solution)/shard_map/ppermute | solution.py:306
  10.7 0.7 %collective-permute-done.2.x_ref = bf16[8,2,8,1024]{3,2,1,0:T(8,128)(2,1)S(1)} collective-permute-done((bf16[8,2,8,1024]{3,2,1,0:T(8,128)(2,1)}, bf16[8,2,8,1024]{3,2,1,0:T(8,128)(2,1)S(1)}, u32[]{:S(2)}, u32[]{:S(2)}) %collective-permute-start.2) | collective-permute-done | bytes 262176 | tf_op jit(solution)/shard_map/ppermute | solution.py:26
  11.4 0.1 shard_map.58
  11.6 0.0 collective-permute-start.3
  11.6 0.0 copy-start
  11.6 1.0 %copy-done = f32[2,96,512]{2,1,0:T(8,128)S(1)} copy-done((f32[2,96,512]{2,1,0:T(8,128)S(1)}, f32[2,96,512]{2,1,0:T(8,128)}, u32[]{:S(2)}) %copy-start) | copy-done | bytes 393240
  12.6 1.2 %shard_map.60.refs_3_ = bf16[4,1024,512]{2,1,0:T(8,128)(2,1)S(1)} custom-call(f32[2,96,512]{2,1,0:T(8,128)S(1)} %copy-done), custom_call_target="tpu_custom_call" | custom-call | flops 8 | bytes 8 | tf_op jit(solution)/shard_map/pallas_call | solution.py:311
  13.8 0.0 copy-done.3
  13.8 0.1 shard_map.57.base_ref
  13.9 0.0 collective-permute-done.3.refs_0_
  13.9 0.2 shard_map.59.refs_1_.refs_0_
  14.2 0.0 copy-done.2
  14.2 3.1 %shard_map.61 = (f32[2,2,64,256]{3,2,1,0:T(8,128)S(1)}, f32[2,2,64,256]{3,2,1,0:T(8,128)S(1)}) custom-call(f32[8,2,8,1024]{3,2,1,0:T(8,128)S(1)} %shard_map.57.base_ref, bf16[8,2,8,1024]{3,2,1,0:T(8,128)(2,1)S(1)} %shard_map.56.white_ref.refs_0_, bf16[8,2,8,1024]{3,2,1,0:T(8,128)(2,1)S(1)} %shard_map.59.refs_1_.refs_0_, f32[2,2,1024]{2,1,0:T(2,128)S(1)} %copy-done.2, ...), custom_call_target="tpu_custom_call" | custom-call | flops 8 | bytes 8 | tf_op jit(solution)/shard_map/pallas_call | solution.py:277
  17.2 0.0 copy-start.4
  17.3 0.0 collective-permute-done.1.refs_1_
  17.3 0.0 collective-permute-done.6.white_ref
  17.3 0.1 shard_map.63.base_ref
  17.4 3.1 %shard_map.64 = (f32[2,2,64,256]{3,2,1,0:T(8,128)S(1)}, f32[2,2,64,256]{3,2,1,0:T(8,128)S(1)}) custom-call(f32[8,2,8,1024]{3,2,1,0:T(8,128)S(1)} %shard_map.63.base_ref, bf16[8,2,8,1024]{3,2,1,0:T(8,128)(2,1)S(1)} %shard_map.59.refs_1_.refs_0_, bf16[8,2,8,1024]{3,2,1,0:T(8,128)(2,1)S(1)} %collective-permute-done.1.refs_1_, f32[2,2,1024]{2,1,0:T(2,128)S(1)} %copy-done.2, ...), custom_call_target="tpu_custom_call" | custom-call | flops 8 | bytes 8 | tf_op jit(solution)/shard_map/pallas_call | solution.py:277
  20.5 0.6 %collective-permute-start.7 = (f32[2,2,64,256]{3,2,1,0:T(8,128)S(1)}, f32[2,2,64,256]{3,2,1,0:T(8,128)S(1)}, u32[]{:S(2)}, u32[]{:S(2)}) collective-permute-start(f32[2,2,64,256]{3,2,1,0:T(8,128)S(1)} %get-tuple-element.36), channel_id=1, source_target_pairs={{0,1},{1,0},{2,3},{3,2},{4,5},{5,4},{6,7},{7,6},{8,9},{9,8},{10,11... | collective-permute-start | bytes 786440 | tf_op jit(solution)/shard_map/ppermute | solution.py:293
  21.0 0.1 collective-permute-start.4
  21.1 1.1 %collective-permute-done.7.refs_1_ = f32[2,2,64,256]{3,2,1,0:T(8,128)S(1)} collective-permute-done((f32[2,2,64,256]{3,2,1,0:T(8,128)S(1)}, f32[2,2,64,256]{3,2,1,0:T(8,128)S(1)}, u32[]{:S(2)}, u32[]{:S(2)}) %collective-permute-start.7) | collective-permute-done | bytes 262176 | tf_op jit(solution)/shard_map/ppermute | solution.py:293
  22.2 1.3 %collective-permute-start.8 = (bf16[2,2,64,256]{3,2,1,0:T(8,128)(2,1)S(1)}, bf16[2,2,64,256]{3,2,1,0:T(8,128)(2,1)S(1)}, u32[]{:S(2)}, u32[]{:S(2)}) collective-permute-start(bf16[2,2,64,256]{3,2,1,0:T(8,128)(2,1)S(1)} %shard_map.65), channel_id=1, source_target_pairs={{4,0},{5,3},{6,2},{7,1},{8,4},{9,7},{10,6},{11,5},{20,16},{21,19},... | collective-permute-start | bytes 393224 | tf_op jit(solution)/shard_map/ppermute | solution.py:337
  23.5 0.0 collective-permute-done.4.refs_1_
  23.6 1.7 %collective-permute-start.5 = (bf16[2,64,256]{2,1,0:T(8,128)(2,1)S(1)}, bf16[2,64,256]{2,1,0:T(8,128)(2,1)S(1)}, u32[]{:S(2)}, u32[]{:S(2)}) collective-permute-start(bf16[2,64,256]{2,1,0:T(8,128)(2,1)S(1)} %get-tuple-element.31), channel_id=1, source_target_pairs={{0,2},{2,0},{1,3},{3,1},{4,6},{6,4},{5,7},{7,5},{8,10},{10,8},{9,1... | collective-permute-start | bytes 196616 | tf_op jit(solution)/shard_map/ppermute | solution.py:293
  25.3 5.5 %collective-permute-done.8.refs_0_ = bf16[2,2,64,256]{3,2,1,0:T(8,128)(2,1)S(1)} collective-permute-done((bf16[2,2,64,256]{3,2,1,0:T(8,128)(2,1)S(1)}, bf16[2,2,64,256]{3,2,1,0:T(8,128)(2,1)S(1)}, u32[]{:S(2)}, u32[]{:S(2)}) %collective-permute-start.8) | collective-permute-done | bytes 131104 | tf_op jit(solution)/shard_map/ppermute | solution.py:337
  30.8 0.1 collective-permute-start.9
  30.9 0.0 copy-done.4
  30.9 0.1 broadcast_in_dim.3
  31.0 0.1 broadcast_in_dim_reshape.4.factor_ref
  31.1 0.0 collective-permute-done.5.refs_1_
  31.1 1.1 %collective-permute-done.9.refs_3_ = f32[2,64,256]{2,1,0:T(8,128)S(1)} collective-permute-done((f32[2,64,256]{2,1,0:T(8,128)S(1)}, f32[2,64,256]{2,1,0:T(8,128)S(1)}, u32[]{:S(2)}, u32[]{:S(2)}) %collective-permute-start.9) | collective-permute-done | bytes 131104 | tf_op jit(solution)/shard_map/ppermute | solution.py:293
  32.2 0.9 %shard_map.67 = f32[8,4,8,256]{3,2,1,0:T(8,128)} custom-call(f32[4,64,1]{2,1,0:T(8,128)S(1)} %broadcast_in_dim_reshape.4.factor_ref, f32[2,64,256]{2,1,0:T(8,128)S(1)} %get-tuple-element.30.refs_0_, bf16[2,64,256]{2,1,0:T(8,128)(2,1)S(1)} %collective-permute-done.5.refs_1_, f32[2,64,256]{2,1,0:T(8,128)S(1)} %get-tuple-element.37.refs_2_, ...), custom_call_target="tpu_custom_call" | custom-call | tf_op jit(solution)/shard_map/pallas_call | solution.py:346
  (4 shorter events, 0.1 us)
Async XLA Ops:
  0.0 11.4 %collective-permute-start.2 = (bf16[8,2,8,1024]{3,2,1,0:T(8,128)(2,1)}, bf16[8,2,8,1024]{3,2,1,0:T(8,128)(2,1)S(1)}, u32[]{:S(2)}, u32[]{:S(2)}) collective-permute-start(bf16[8,2,8,1024]{3,2,1,0:T(8,128)(2,1)} %x_ref.1), channel_id=1, source_target_pairs={{4,0},{8,4},{12,8},{5,1},{9,5},{13,9},{6,2},{10,6},{14,10},{7,3},{... | collective-permute-start | bytes 786440 | tf_op jit(solution)/shard_map/ppermute | solution.py:26
  1.3 1.0 %copy-start.1 = (bf16[8,2,8,1024]{3,2,1,0:T(8,128)(2,1)S(1)}, bf16[8,2,8,1024]{3,2,1,0:T(8,128)(2,1)}, u32[]{:S(2)}) copy-start(bf16[8,2,8,1024]{3,2,1,0:T(8,128)(2,1)} %x_ref.1) | copy-start | bytes 786436
  2.2 11.5 %copy-start.3 = (s32[8]{0:T(128)S(1)}, s32[8]{0:T(128)}, u32[]{:S(2)}) copy-start(s32[8]{0:T(128)} %param.6) | copy-start | bytes 100
  2.2 11.9 %copy-start.2 = (f32[2,2,1024]{2,1,0:T(2,128)S(1)}, f32[2,2,1024]{2,1,0:T(2,128)}, u32[]{:S(2)}) copy-start(f32[2,2,1024]{2,1,0:T(2,128)} %constant.6.clone.refs_2_) | copy-start | bytes 49156
  2.4 1.3 %collective-permute-start = (f32[8,8,1]{2,1,0:T(8,128)S(1)}, f32[8,8,1]{2,1,0:T(8,128)S(1)}, u32[]{:S(2)}, u32[]{:S(2)}) collective-permute-start(f32[8,8,1]{2,1,0:T(8,128)S(1)} %get-tuple-element.23), channel_id=1, source_target_pairs={{0,1},{1,0},{2,3},{3,2},{4,5},{5,4},{6,7},{7,6},{8,9},{9,8},{10,11... | collective-permute-start | bytes 776 | tf_op jit(solution)/shard_map/ppermute | solution.py:252
  3.9 13.3 %collective-permute-start.1 = (bf16[8,2,8,1024]{3,2,1,0:T(8,128)(2,1)S(1)}, bf16[8,2,8,1024]{3,2,1,0:T(8,128)(2,1)S(1)}, u32[]{:S(2)}, u32[]{:S(2)}) collective-permute-start(bf16[8,2,8,1024]{3,2,1,0:T(8,128)(2,1)S(1)} %shard_map.56.white_ref.refs_0_), channel_id=1, source_target_pairs={{12,4},{13,5},{14,6},{15,7},{28,20},{29,21},{30,22},{31,23}} | collective-permute-start | bytes 786440 | tf_op jit(solution)/shard_map/ppermute | solution.py:305
  4.6 12.6 %collective-permute-start.6 = (bf16[8,2,8,1024]{3,2,1,0:T(8,128)(2,1)S(1)}, bf16[8,2,8,1024]{3,2,1,0:T(8,128)(2,1)S(1)}, u32[]{:S(2)}, u32[]{:S(2)}) collective-permute-start(bf16[8,2,8,1024]{3,2,1,0:T(8,128)(2,1)S(1)} %shard_map.56.white_ref.refs_0_), channel_id=1, source_target_pairs={{0,4},{4,8},{1,5},{5,9},{2,6},{6,10},{3,7},{7,11},{16,20},{20,24},... | collective-permute-start | bytes 786440 | tf_op jit(solution)/shard_map/ppermute | solution.py:306
  11.6 2.3 %collective-permute-start.3 = (f32[8,8,1]{2,1,0:T(8,128)S(1)}, f32[8,8,1]{2,1,0:T(8,128)S(1)}, u32[]{:S(2)}, u32[]{:S(2)}) collective-permute-start(f32[8,8,1]{2,1,0:T(8,128)S(1)} %shard_map.58), channel_id=1, source_target_pairs={{0,1},{1,0},{2,3},{3,2},{4,5},{5,4},{6,7},{7,6},{8,9},{9,8},{10,11... | collective-permute-start | bytes 776 | tf_op jit(solution)/shard_map/ppermute | solution.py:252
  11.6 1.0 %copy-start = (f32[2,96,512]{2,1,0:T(8,128)S(1)}, f32[2,96,512]{2,1,0:T(8,128)}, u32[]{:S(2)}) copy-start(f32[2,96,512]{2,1,0:T(8,128)} %constant.7.clone.base_ref) | copy-start | bytes 1179652
  17.2 13.6 %copy-start.4 = (s32[8,4]{0,1:T(4,128)S(1)}, s32[8,4]{0,1:T(4,128)}, u32[]{:S(2)}) copy-start(s32[8,4]{0,1:T(4,128)} %param.7) | copy-start | bytes 388
  20.5 1.7 %collective-permute-start.7 = (f32[2,2,64,256]{3,2,1,0:T(8,128)S(1)}, f32[2,2,64,256]{3,2,1,0:T(8,128)S(1)}, u32[]{:S(2)}, u32[]{:S(2)}) collective-permute-start(f32[2,2,64,256]{3,2,1,0:T(8,128)S(1)} %get-tuple-element.36), channel_id=1, source_target_pairs={{0,1},{1,0},{2,3},{3,2},{4,5},{5,4},{6,7},{7,6},{8,9},{9,8},{10,11... | collective-permute-start | bytes 786440 | tf_op jit(solution)/shard_map/ppermute | solution.py:293
  21.0 2.5 %collective-permute-start.4 = (f32[2,2,64,256]{3,2,1,0:T(8,128)S(1)}, f32[2,2,64,256]{3,2,1,0:T(8,128)S(1)}, u32[]{:S(2)}, u32[]{:S(2)}) collective-permute-start(f32[2,2,64,256]{3,2,1,0:T(8,128)S(1)} %get-tuple-element.29), channel_id=1, source_target_pairs={{0,1},{1,0},{2,3},{3,2},{4,5},{5,4},{6,7},{7,6},{8,9},{9,8},{10,11... | collective-permute-start | bytes 786440 | tf_op jit(solution)/shard_map/ppermute | solution.py:293
  22.2 8.5 %collective-permute-start.8 = (bf16[2,2,64,256]{3,2,1,0:T(8,128)(2,1)S(1)}, bf16[2,2,64,256]{3,2,1,0:T(8,128)(2,1)S(1)}, u32[]{:S(2)}, u32[]{:S(2)}) collective-permute-start(bf16[2,2,64,256]{3,2,1,0:T(8,128)(2,1)S(1)} %shard_map.65), channel_id=1, source_target_pairs={{4,0},{5,3},{6,2},{7,1},{8,4},{9,7},{10,6},{11,5},{20,16},{21,19},... | collective-permute-start | bytes 393224 | tf_op jit(solution)/shard_map/ppermute | solution.py:337
  23.6 7.5 %collective-permute-start.5 = (bf16[2,64,256]{2,1,0:T(8,128)(2,1)S(1)}, bf16[2,64,256]{2,1,0:T(8,128)(2,1)S(1)}, u32[]{:S(2)}, u32[]{:S(2)}) collective-permute-start(bf16[2,64,256]{2,1,0:T(8,128)(2,1)S(1)} %get-tuple-element.31), channel_id=1, source_target_pairs={{0,2},{2,0},{1,3},{3,1},{4,6},{6,4},{5,7},{7,5},{8,10},{10,8},{9,1... | collective-permute-start | bytes 196616 | tf_op jit(solution)/shard_map/ppermute | solution.py:293
  30.8 1.4 %collective-permute-start.9 = (f32[2,64,256]{2,1,0:T(8,128)S(1)}, f32[2,64,256]{2,1,0:T(8,128)S(1)}, u32[]{:S(2)}, u32[]{:S(2)}) collective-permute-start(f32[2,64,256]{2,1,0:T(8,128)S(1)} %get-tuple-element.38), channel_id=1, source_target_pairs={{0,1},{1,0},{2,3},{3,2},{4,5},{5,4},{6,7},{7,6},{8,9},{9,8},{10,11... | collective-permute-start | bytes 393224 | tf_op jit(solution)/shard_map/ppermute | solution.py:293

commit v23 on v18

--- a/solution.py
+++ b/solution.py
@@ -67,7 +67,10 @@
 
 def keep_kernel(keep_ref, white_ref, out_ref):
     for w in range(white_ref.shape[0]):
-        out_ref[w] = white_ref[w].astype(jnp.float32) * keep_ref[:, w:w + 1].astype(jnp.float32)[None]
+        value = white_ref[w].astype(jnp.float32) * keep_ref[:, w:w + 1].astype(jnp.float32)[None]
+        out_ref[w, 0] = value[0]
+        out_ref[w, 1] = value[1]
+        out_ref[w, 2] = value[0] + value[1]
 
 
 def table_kernel(base_ref, table_ref):
@@ -95,18 +98,17 @@
 
 def cross_tile(base_ref, partner_ref, lanes):
     w_dev, _, ch, _ = base_ref.shape
-    real = [None] * ch
-    imag = [None] * ch
+    sums = [[None] * ch for _ in range(3)]
     for w in range(w_dev):
         partner_re = partner_ref[w, 0, :, lanes].astype(jnp.float32)
         partner_im = partner_ref[w, 1, :, lanes].astype(jnp.float32)
+        factors = (partner_re + partner_im, partner_re - partner_im, partner_re)
         for i in range(ch):
-            base_re = base_ref[w, 0, i:i + 1, lanes]
-            base_im = base_ref[w, 1, i:i + 1, lanes]
-            re = base_re * partner_re + base_im * partner_im
-            im = base_im * partner_re - base_re * partner_im
-            real[i] = re if w == 0 else real[i] + re
-            imag[i] = im if w == 0 else imag[i] + im
+            for n, factor in enumerate(factors):
+                product = base_ref[w, n, i:i + 1, lanes] * factor
+                sums[n][i] = product if w == 0 else sums[n][i] + product
+    real = [both - im for im, both in zip(sums[1], sums[2])]
+    imag = [both - re for re, both in zip(sums[0], sums[2])]
     return real, imag
 
 
@@ -184,7 +186,7 @@
         total = refs[0][turn].astype(jnp.float32)
         for ref in refs[1:n_ships]:
             total = total + ref[turn].astype(jnp.float32)
-        out_ref[...] = total
+        out_ref[...] = total.astype(out_ref.dtype)
 
 
 def reverse_lanes(value):
@@ -261,7 +263,7 @@
     def kept(block):
         return pl.pallas_call(
             keep_kernel,
-            out_shape=jax.ShapeDtypeStruct(block.shape, jnp.float32),
+            out_shape=jax.ShapeDtypeStruct((w_dev, 3) + block.shape[2:], jnp.float32),
             in_specs=[VMEM] * 2, out_specs=VMEM, compiler_params=params,
         )(keep.reshape(1, w_dev), block)
 
@@ -330,7 +332,7 @@
         arrived.append(lax.ppermute(block, ("chan", "win", "freq"), route))
     arrived = pl.pallas_call(
         functools.partial(ungroup_kernel, n_ships),
-        out_shape=[jax.ShapeDtypeStruct(shape, jnp.float32)] * n_freq,
+        out_shape=[jax.ShapeDtypeStruct(shape, jnp.bfloat16 if n_ships == 1 else jnp.float32)] * n_freq,
         in_specs=[VMEM] * n_ships, out_specs=[VMEM] * n_freq, compiler_params=params,
     )(*arrived)
     arrived = turns(arrived, "freq", n_freq)

time: 32.4 us -> 32.1 us (level)
  no operation moved by 1% of the time
where the time goes in v23:
time: 32.1 us; the launch traced here: 31.9 us
  starting transfers between devices  12.6 us (39%)
  waiting for transfers between devices  9.02 us (28%)
  Pallas kernels  7.91 us (25%)
  local copies, waits for them, and re-layouts  2.12 us (7%)
    ppermute x1, starting transfers between devices, local(): lax.ppermute(white, 'chan', [(c - 1, c) for c in range(1, n_chan - 1)])  6.09 us
    ppermute x1, waiting for transfers between devices, local(): arrived.append(lax.ppermute(block, ('chan', 'win', 'freq'), route))  5.57 us
    pallas_call x2, Pallas kernels, pairs(): pl.pallas_call(functools.partial(pairs_kernel, n, n_win, n_freq, by_windo...  4.79 us
    ppermute x4, starting transfers between devices, turns(): received.append(lax.ppermute(parts[turn], axis, route))  2.8 us
    unnamed x10, local copies, waits for them, and re-layouts  1.95 us
    ppermute x4, waiting for transfers between devices, turns(): received.append(lax.ppermute(parts[turn], axis, route))  1.89 us
    ppermute x1, starting transfers between devices, local(): arrived.append(lax.ppermute(block, ('chan', 'win', 'freq'), route))  1.29 us
    ppermute x1, starting transfers between devices, from_behind(): return lax.ppermute(block, axis, route)  1.28 us
  transfers between devices with their start and end apart: 10, of which 5 were waited for; matrix products, arithmetic and copies ran while one was open for 1% of the time, Pallas kernels for 14%

profile of v23, /device:TPU:0, one launch (start us, length us, event | category | flops | bytes accessed | tf_op | source)
XLA Modules:
  0.0 31.9 jit_solution(17572635159848758523)
XLA Ops:
  0.0 1.3 %collective-permute-start.2 = (bf16[8,2,8,1024]{3,2,1,0:T(8,128)(2,1)}, bf16[8,2,8,1024]{3,2,1,0:T(8,128)(2,1)S(1)}, u32[]{:S(2)}, u32[]{:S(2)}) collective-permute-start(bf16[8,2,8,1024]{3,2,1,0:T(8,128)(2,1)} %x_ref.1), channel_id=1, source_target_pairs={{4,0},{8,4},{12,8},{5,1},{9,5},{13,9},{6,2},{10,6},{14,10},{7,3},{... | collective-permute-start | bytes 786440 | tf_op jit(solution)/shard_map/ppermute | solution.py:26
  1.3 0.0 copy-start.1
  1.3 0.9 %copy-done.1 = bf16[8,2,8,1024]{3,2,1,0:T(8,128)(2,1)S(1)} copy-done((bf16[8,2,8,1024]{3,2,1,0:T(8,128)(2,1)S(1)}, bf16[8,2,8,1024]{3,2,1,0:T(8,128)(2,1)}, u32[]{:S(2)}) %copy-start.1) | copy-done | bytes 262168
  2.2 0.0 copy-start.3
  2.2 0.0 copy-start.2
  2.2 0.1 shard_map.55
  2.4 0.5 %collective-permute-start = (f32[8,8,1]{2,1,0:T(8,128)S(1)}, f32[8,8,1]{2,1,0:T(8,128)S(1)}, u32[]{:S(2)}, u32[]{:S(2)}) collective-permute-start(f32[8,8,1]{2,1,0:T(8,128)S(1)} %get-tuple-element.23), channel_id=1, source_target_pairs={{0,1},{1,0},{2,3},{3,2},{4,5},{5,4},{6,7},{7,6},{8,9},{9,8},{10,11... | collective-permute-start | bytes 776 | tf_op jit(solution)/shard_map/ppermute | solution.py:247
  2.8 0.9 %collective-permute-done.refs_0_ = f32[8,8,1]{2,1,0:T(8,128)S(1)} collective-permute-done((f32[8,8,1]{2,1,0:T(8,128)S(1)}, f32[8,8,1]{2,1,0:T(8,128)S(1)}, u32[]{:S(2)}, u32[]{:S(2)}) %collective-permute-start) | collective-permute-done | bytes 288 | tf_op jit(solution)/shard_map/ppermute | solution.py:247
  3.7 0.2 shard_map.56.white_ref.refs_0_
  3.9 0.7 %collective-permute-start.1 = (bf16[8,2,8,1024]{3,2,1,0:T(8,128)(2,1)S(1)}, bf16[8,2,8,1024]{3,2,1,0:T(8,128)(2,1)S(1)}, u32[]{:S(2)}, u32[]{:S(2)}) collective-permute-start(bf16[8,2,8,1024]{3,2,1,0:T(8,128)(2,1)S(1)} %shard_map.56.white_ref.refs_0_), channel_id=1, source_target_pairs={{12,4},{13,5},{14,6},{15,7},{28,20},{29,21},{30,22},{31,23}} | collective-permute-start | bytes 786440 | tf_op jit(solution)/shard_map/ppermute | solution.py:300
  4.6 6.1 %collective-permute-start.6 = (bf16[8,2,8,1024]{3,2,1,0:T(8,128)(2,1)S(1)}, bf16[8,2,8,1024]{3,2,1,0:T(8,128)(2,1)S(1)}, u32[]{:S(2)}, u32[]{:S(2)}) collective-permute-start(bf16[8,2,8,1024]{3,2,1,0:T(8,128)(2,1)S(1)} %shard_map.56.white_ref.refs_0_), channel_id=1, source_target_pairs={{0,4},{4,8},{1,5},{5,9},{2,6},{6,10},{3,7},{7,11},{16,20},{20,24},... | collective-permute-start | bytes 786440 | tf_op jit(solution)/shard_map/ppermute | solution.py:301
  10.7 0.7 %collective-permute-done.2.x_ref = bf16[8,2,8,1024]{3,2,1,0:T(8,128)(2,1)S(1)} collective-permute-done((bf16[8,2,8,1024]{3,2,1,0:T(8,128)(2,1)}, bf16[8,2,8,1024]{3,2,1,0:T(8,128)(2,1)S(1)}, u32[]{:S(2)}, u32[]{:S(2)}) %collective-permute-start.2) | collective-permute-done | bytes 262176 | tf_op jit(solution)/shard_map/ppermute | solution.py:26
  11.4 0.1 shard_map.58
  11.6 0.0 collective-permute-start.3
  11.6 0.0 copy-start
  11.6 1.0 %copy-done = f32[2,96,512]{2,1,0:T(8,128)S(1)} copy-done((f32[2,96,512]{2,1,0:T(8,128)S(1)}, f32[2,96,512]{2,1,0:T(8,128)}, u32[]{:S(2)}) %copy-start) | copy-done | bytes 393240
  12.6 1.2 %shard_map.60.refs_3_ = bf16[4,1024,512]{2,1,0:T(8,128)(2,1)S(1)} custom-call(f32[2,96,512]{2,1,0:T(8,128)S(1)} %copy-done), custom_call_target="tpu_custom_call" | custom-call | flops 8 | bytes 8 | tf_op jit(solution)/shard_map/pallas_call | solution.py:306
  13.8 0.0 copy-done.3
  13.8 0.1 shard_map.57.base_ref
  13.9 0.0 collective-permute-done.3.refs_0_
  13.9 0.2 shard_map.59.refs_1_.refs_0_
  14.2 0.0 copy-done.2
  14.2 2.4 %shard_map.61 = (f32[2,2,64,256]{3,2,1,0:T(8,128)S(1)}, f32[2,2,64,256]{3,2,1,0:T(8,128)S(1)}) custom-call(f32[8,3,8,1024]{3,2,1,0:T(8,128)S(1)} %shard_map.57.base_ref, bf16[8,2,8,1024]{3,2,1,0:T(8,128)(2,1)S(1)} %shard_map.56.white_ref.refs_0_, bf16[8,2,8,1024]{3,2,1,0:T(8,128)(2,1)S(1)} %shard_map.59.refs_1_.refs_0_, f32[2,2,1024]{2,1,0:T(2,128)S(1)} %copy-done.2, ...), custom_call_target="tpu_custom_call" | custom-call | flops 8 | bytes 8 | tf_op jit(solution)/shard_map/pallas_call | solution.py:272
  16.6 0.0 copy-start.4
  16.6 0.0 collective-permute-done.1.refs_1_
  16.6 0.0 collective-permute-done.6.white_ref
  16.6 0.1 shard_map.63.base_ref
  16.7 2.4 %shard_map.64 = (f32[2,2,64,256]{3,2,1,0:T(8,128)S(1)}, f32[2,2,64,256]{3,2,1,0:T(8,128)S(1)}) custom-call(f32[8,3,8,1024]{3,2,1,0:T(8,128)S(1)} %shard_map.63.base_ref, bf16[8,2,8,1024]{3,2,1,0:T(8,128)(2,1)S(1)} %shard_map.59.refs_1_.refs_0_, bf16[8,2,8,1024]{3,2,1,0:T(8,128)(2,1)S(1)} %collective-permute-done.1.refs_1_, f32[2,2,1024]{2,1,0:T(2,128)S(1)} %copy-done.2, ...), custom_call_target="tpu_custom_call" | custom-call | flops 8 | bytes 8 | tf_op jit(solution)/shard_map/pallas_call | solution.py:272
  19.1 0.6 %collective-permute-start.7 = (f32[2,2,64,256]{3,2,1,0:T(8,128)S(1)}, f32[2,2,64,256]{3,2,1,0:T(8,128)S(1)}, u32[]{:S(2)}, u32[]{:S(2)}) collective-permute-start(f32[2,2,64,256]{3,2,1,0:T(8,128)S(1)} %get-tuple-element.36), channel_id=1, source_target_pairs={{0,1},{1,0},{2,3},{3,2},{4,5},{5,4},{6,7},{7,6},{8,9},{9,8},{10,11... | collective-permute-start | bytes 786440 | tf_op jit(solution)/shard_map/ppermute | solution.py:288
  19.7 0.1 collective-permute-start.4
  19.8 1.1 %collective-permute-done.7.refs_1_ = f32[2,2,64,256]{3,2,1,0:T(8,128)S(1)} collective-permute-done((f32[2,2,64,256]{3,2,1,0:T(8,128)S(1)}, f32[2,2,64,256]{3,2,1,0:T(8,128)S(1)}, u32[]{:S(2)}, u32[]{:S(2)}) %collective-permute-start.7) | collective-permute-done | bytes 262176 | tf_op jit(solution)/shard_map/ppermute | solution.py:288
  20.9 1.3 %collective-permute-start.8 = (bf16[2,2,64,256]{3,2,1,0:T(8,128)(2,1)S(1)}, bf16[2,2,64,256]{3,2,1,0:T(8,128)(2,1)S(1)}, u32[]{:S(2)}, u32[]{:S(2)}) collective-permute-start(bf16[2,2,64,256]{3,2,1,0:T(8,128)(2,1)S(1)} %shard_map.65), channel_id=1, source_target_pairs={{4,0},{5,3},{6,2},{7,1},{8,4},{9,7},{10,6},{11,5},{20,16},{21,19},... | collective-permute-start | bytes 393224 | tf_op jit(solution)/shard_map/ppermute | solution.py:332
  22.2 0.0 collective-permute-done.4.refs_1_
  22.2 1.8 %collective-permute-start.5 = (bf16[2,64,256]{2,1,0:T(8,128)(2,1)S(1)}, bf16[2,64,256]{2,1,0:T(8,128)(2,1)S(1)}, u32[]{:S(2)}, u32[]{:S(2)}) collective-permute-start(bf16[2,64,256]{2,1,0:T(8,128)(2,1)S(1)} %get-tuple-element.31), channel_id=1, source_target_pairs={{0,2},{2,0},{1,3},{3,1},{4,6},{6,4},{5,7},{7,5},{8,10},{10,8},{9,1... | collective-permute-start | bytes 196616 | tf_op jit(solution)/shard_map/ppermute | solution.py:288
  24.1 5.6 %collective-permute-done.8.refs_0_ = bf16[2,2,64,256]{3,2,1,0:T(8,128)(2,1)S(1)} collective-permute-done((bf16[2,2,64,256]{3,2,1,0:T(8,128)(2,1)S(1)}, bf16[2,2,64,256]{3,2,1,0:T(8,128)(2,1)S(1)}, u32[]{:S(2)}, u32[]{:S(2)}) %collective-permute-start.8) | collective-permute-done | bytes 131104 | tf_op jit(solution)/shard_map/ppermute | solution.py:332
  29.7 0.3 %collective-permute-start.9 = (bf16[2,64,256]{2,1,0:T(8,128)(2,1)S(1)}, bf16[2,64,256]{2,1,0:T(8,128)(2,1)S(1)}, u32[]{:S(2)}, u32[]{:S(2)}) collective-permute-start(bf16[2,64,256]{2,1,0:T(8,128)(2,1)S(1)} %get-tuple-element.38), channel_id=1, source_target_pairs={{0,1},{1,0},{2,3},{3,2},{4,5},{5,4},{6,7},{7,6},{8,9},{9,8},{10,11... | collective-permute-start | bytes 196616 | tf_op jit(solution)/shard_map/ppermute | solution.py:288
  30.0 0.0 copy-done.4
  30.0 0.1 broadcast_in_dim.3
  30.1 0.1 broadcast_in_dim_reshape.4.factor_ref
  30.2 0.0 collective-permute-done.5.refs_1_
  30.2 0.8 %collective-permute-done.9.refs_3_ = bf16[2,64,256]{2,1,0:T(8,128)(2,1)S(1)} collective-permute-done((bf16[2,64,256]{2,1,0:T(8,128)(2,1)S(1)}, bf16[2,64,256]{2,1,0:T(8,128)(2,1)S(1)}, u32[]{:S(2)}, u32[]{:S(2)}) %collective-permute-start.9) | collective-permute-done | bytes 65568 | tf_op jit(solution)/shard_map/ppermute | solution.py:288
  31.0 0.9 %shard_map.67 = f32[8,4,8,256]{3,2,1,0:T(8,128)} custom-call(f32[4,64,1]{2,1,0:T(8,128)S(1)} %broadcast_in_dim_reshape.4.factor_ref, f32[2,64,256]{2,1,0:T(8,128)S(1)} %get-tuple-element.30.refs_0_, bf16[2,64,256]{2,1,0:T(8,128)(2,1)S(1)} %collective-permute-done.5.refs_1_, bf16[2,64,256]{2,1,0:T(8,128)(2,1)S(1)} %get-tuple-element.37.refs_2_, ...), custom_call_target="tpu_custom_call" | custom-call | tf_op jit(solution)/shard_map/pallas_call | solution.py:341
  (4 shorter events, 0.1 us)
Async XLA Ops:
  0.0 11.4 %collective-permute-start.2 = (bf16[8,2,8,1024]{3,2,1,0:T(8,128)(2,1)}, bf16[8,2,8,1024]{3,2,1,0:T(8,128)(2,1)S(1)}, u32[]{:S(2)}, u32[]{:S(2)}) collective-permute-start(bf16[8,2,8,1024]{3,2,1,0:T(8,128)(2,1)} %x_ref.1), channel_id=1, source_target_pairs={{4,0},{8,4},{12,8},{5,1},{9,5},{13,9},{6,2},{10,6},{14,10},{7,3},{... | collective-permute-start | bytes 786440 | tf_op jit(solution)/shard_map/ppermute | solution.py:26
  1.3 1.0 %copy-start.1 = (bf16[8,2,8,1024]{3,2,1,0:T(8,128)(2,1)S(1)}, bf16[8,2,8,1024]{3,2,1,0:T(8,128)(2,1)}, u32[]{:S(2)}) copy-start(bf16[8,2,8,1024]{3,2,1,0:T(8,128)(2,1)} %x_ref.1) | copy-start | bytes 786436
  2.2 11.5 %copy-start.3 = (s32[8]{0:T(128)S(1)}, s32[8]{0:T(128)}, u32[]{:S(2)}) copy-start(s32[8]{0:T(128)} %param.6) | copy-start | bytes 100
  2.2 11.9 %copy-start.2 = (f32[2,2,1024]{2,1,0:T(2,128)S(1)}, f32[2,2,1024]{2,1,0:T(2,128)}, u32[]{:S(2)}) copy-start(f32[2,2,1024]{2,1,0:T(2,128)} %constant.6.clone.refs_2_) | copy-start | bytes 49156
  2.4 1.3 %collective-permute-start = (f32[8,8,1]{2,1,0:T(8,128)S(1)}, f32[8,8,1]{2,1,0:T(8,128)S(1)}, u32[]{:S(2)}, u32[]{:S(2)}) collective-permute-start(f32[8,8,1]{2,1,0:T(8,128)S(1)} %get-tuple-element.23), channel_id=1, source_target_pairs={{0,1},{1,0},{2,3},{3,2},{4,5},{5,4},{6,7},{7,6},{8,9},{9,8},{10,11... | collective-permute-start | bytes 776 | tf_op jit(solution)/shard_map/ppermute | solution.py:247
  3.9 12.7 %collective-permute-start.1 = (bf16[8,2,8,1024]{3,2,1,0:T(8,128)(2,1)S(1)}, bf16[8,2,8,1024]{3,2,1,0:T(8,128)(2,1)S(1)}, u32[]{:S(2)}, u32[]{:S(2)}) collective-permute-start(bf16[8,2,8,1024]{3,2,1,0:T(8,128)(2,1)S(1)} %shard_map.56.white_ref.refs_0_), channel_id=1, source_target_pairs={{12,4},{13,5},{14,6},{15,7},{28,20},{29,21},{30,22},{31,23}} | collective-permute-start | bytes 786440 | tf_op jit(solution)/shard_map/ppermute | solution.py:300
  4.6 12.0 %collective-permute-start.6 = (bf16[8,2,8,1024]{3,2,1,0:T(8,128)(2,1)S(1)}, bf16[8,2,8,1024]{3,2,1,0:T(8,128)(2,1)S(1)}, u32[]{:S(2)}, u32[]{:S(2)}) collective-permute-start(bf16[8,2,8,1024]{3,2,1,0:T(8,128)(2,1)S(1)} %shard_map.56.white_ref.refs_0_), channel_id=1, source_target_pairs={{0,4},{4,8},{1,5},{5,9},{2,6},{6,10},{3,7},{7,11},{16,20},{20,24},... | collective-permute-start | bytes 786440 | tf_op jit(solution)/shard_map/ppermute | solution.py:301
  11.6 2.4 %collective-permute-start.3 = (f32[8,8,1]{2,1,0:T(8,128)S(1)}, f32[8,8,1]{2,1,0:T(8,128)S(1)}, u32[]{:S(2)}, u32[]{:S(2)}) collective-permute-start(f32[8,8,1]{2,1,0:T(8,128)S(1)} %shard_map.58), channel_id=1, source_target_pairs={{0,1},{1,0},{2,3},{3,2},{4,5},{5,4},{6,7},{7,6},{8,9},{9,8},{10,11... | collective-permute-start | bytes 776 | tf_op jit(solution)/shard_map/ppermute | solution.py:247
  11.6 1.0 %copy-start = (f32[2,96,512]{2,1,0:T(8,128)S(1)}, f32[2,96,512]{2,1,0:T(8,128)}, u32[]{:S(2)}) copy-start(f32[2,96,512]{2,1,0:T(8,128)} %constant.7.clone.base_ref) | copy-start | bytes 1179652
  16.6 13.4 %copy-start.4 = (s32[8,4]{0,1:T(4,128)S(1)}, s32[8,4]{0,1:T(4,128)}, u32[]{:S(2)}) copy-start(s32[8,4]{0,1:T(4,128)} %param.7) | copy-start | bytes 388
  19.1 1.7 %collective-permute-start.7 = (f32[2,2,64,256]{3,2,1,0:T(8,128)S(1)}, f32[2,2,64,256]{3,2,1,0:T(8,128)S(1)}, u32[]{:S(2)}, u32[]{:S(2)}) collective-permute-start(f32[2,2,64,256]{3,2,1,0:T(8,128)S(1)} %get-tuple-element.36), channel_id=1, source_target_pairs={{0,1},{1,0},{2,3},{3,2},{4,5},{5,4},{6,7},{7,6},{8,9},{9,8},{10,11... | collective-permute-start | bytes 786440 | tf_op jit(solution)/shard_map/ppermute | solution.py:288
  19.7 2.5 %collective-permute-start.4 = (f32[2,2,64,256]{3,2,1,0:T(8,128)S(1)}, f32[2,2,64,256]{3,2,1,0:T(8,128)S(1)}, u32[]{:S(2)}, u32[]{:S(2)}) collective-permute-start(f32[2,2,64,256]{3,2,1,0:T(8,128)S(1)} %get-tuple-element.29), channel_id=1, source_target_pairs={{0,1},{1,0},{2,3},{3,2},{4,5},{5,4},{6,7},{7,6},{8,9},{9,8},{10,11... | collective-permute-start | bytes 786440 | tf_op jit(solution)/shard_map/ppermute | solution.py:288
  20.9 8.8 %collective-permute-start.8 = (bf16[2,2,64,256]{3,2,1,0:T(8,128)(2,1)S(1)}, bf16[2,2,64,256]{3,2,1,0:T(8,128)(2,1)S(1)}, u32[]{:S(2)}, u32[]{:S(2)}) collective-permute-start(bf16[2,2,64,256]{3,2,1,0:T(8,128)(2,1)S(1)} %shard_map.65), channel_id=1, source_target_pairs={{4,0},{5,3},{6,2},{7,1},{8,4},{9,7},{10,6},{11,5},{20,16},{21,19},... | collective-permute-start | bytes 393224 | tf_op jit(solution)/shard_map/ppermute | solution.py:332
  22.2 7.9 %collective-permute-start.5 = (bf16[2,64,256]{2,1,0:T(8,128)(2,1)S(1)}, bf16[2,64,256]{2,1,0:T(8,128)(2,1)S(1)}, u32[]{:S(2)}, u32[]{:S(2)}) collective-permute-start(bf16[2,64,256]{2,1,0:T(8,128)(2,1)S(1)} %get-tuple-element.31), channel_id=1, source_target_pairs={{0,2},{2,0},{1,3},{3,1},{4,6},{6,4},{5,7},{7,5},{8,10},{10,8},{9,1... | collective-permute-start | bytes 196616 | tf_op jit(solution)/shard_map/ppermute | solution.py:288
  29.7 1.3 %collective-permute-start.9 = (bf16[2,64,256]{2,1,0:T(8,128)(2,1)S(1)}, bf16[2,64,256]{2,1,0:T(8,128)(2,1)S(1)}, u32[]{:S(2)}, u32[]{:S(2)}) collective-permute-start(bf16[2,64,256]{2,1,0:T(8,128)(2,1)S(1)} %get-tuple-element.38), channel_id=1, source_target_pairs={{0,1},{1,0},{2,3},{3,2},{4,5},{5,4},{6,7},{7,6},{8,9},{9,8},{10,11... | collective-permute-start | bytes 196616 | tf_op jit(solution)/shard_map/ppermute | solution.py:288

commit v24 on v23

--- a/solution.py
+++ b/solution.py
@@ -125,8 +125,7 @@
     dot = functools.partial(jnp.dot, preferred_element_type=jnp.float32)
     count = n_partners * pairs
 
-    def body(tile, carry):
-        lanes = pl.ds(pl.multiple_of(tile * LANES, LANES), LANES)
+    def prepare(lanes):
         cos = twist_ref[freq, 0:1, lanes]
         sin = twist_ref[freq, 1:2, lanes]
         for k, partner_ref in enumerate(partner_refs):
@@ -139,12 +138,24 @@
                     high, low = split(value)
                     rows_ref[part, rows:rows + 2 * ch, lanes] = high
                     rows_ref[part, count + rows:count + rows + 2 * ch, lanes] = low
+
+    def body(tile, carry):
+        prepare(pl.ds(pl.multiple_of(tile * LANES, LANES), LANES))
         return carry
 
-    lax.fori_loop(0, f_dev // LANES, body, 0)
+    def transform(part, bins):
+        both = dot(rows_ref[part, :, bins], table_ref[2 * part, bins])
+        return both[:count] + both[count:] + dot(rows_ref[part, :count, bins], table_ref[2 * part + 1, bins])
+
+    tiles = f_dev // LANES
+    early = tiles - tiles // 2
+    lax.fori_loop(0, early, body, 0)
     for part in range(2):
-        both = dot(rows_ref[part], table_ref[2 * part])
-        sums_ref[part] = both[:count] + both[count:] + dot(rows_ref[part, :count], table_ref[2 * part + 1])
+        sums_ref[part] = transform(part, slice(0, early * LANES))
+    for tile in range(early, tiles):
+        prepare(slice(tile * LANES, (tile + 1) * LANES))
+    for part in range(2):
+        sums_ref[part] += transform(part, slice(early * LANES, f_dev))
     for turn_freq, out_ref in enumerate(out_refs):
         core = (freq + turn_freq) % n_freq
         for turn_win in range(n_win):

time: 32.1 us -> 31.9 us (level)
  Pallas kernels: 7.91 us -> 7.45 us
    pallas_call x2, Pallas kernels: 4.79 us -> 4.33 us  [pairs(): pl.pallas_call(functools.partial(pairs_kernel, n, n_win, n_freq, by_windo...]
  transfers between devices with their start and end apart: 10 -> 10, of which waited for: 5 -> 6; matrix products, arithmetic and copies ran while one was open for 1% -> 1% of each run, Pallas kernels for 14% -> 13%
where the time goes in v24:
time: 31.9 us; the launch traced here: 31.7 us
  starting transfers between devices  12.7 us (40%)
  waiting for transfers between devices  9.18 us (29%)
  Pallas kernels  7.45 us (23%)
  local copies, waits for them, and re-layouts  2.12 us (7%)
    ppermute x1, starting transfers between devices, local(): lax.ppermute(white, 'chan', [(c - 1, c) for c in range(1, n_chan - 1)])  6.09 us
    ppermute x1, waiting for transfers between devices, local(): arrived.append(lax.ppermute(block, ('chan', 'win', 'freq'), route))  5.57 us
    pallas_call x2, Pallas kernels, pairs(): pl.pallas_call(functools.partial(pairs_kernel, n, n_win, n_freq, by_windo...  4.33 us
    ppermute x4, starting transfers between devices, turns(): received.append(lax.ppermute(parts[turn], axis, route))  2.89 us
    unnamed x10, local copies, waits for them, and re-layouts  1.95 us
    ppermute x4, waiting for transfers between devices, turns(): received.append(lax.ppermute(parts[turn], axis, route))  1.83 us
    ppermute x1, starting transfers between devices, local(): arrived.append(lax.ppermute(block, ('chan', 'win', 'freq'), route))  1.29 us
    ppermute x1, starting transfers between devices, from_behind(): return lax.ppermute(block, axis, route)  1.28 us
  transfers between devices with their start and end apart: 10, of which 6 were waited for; matrix products, arithmetic and copies ran while one was open for 1% of the time, Pallas kernels for 13%

profile of v24, /device:TPU:0, one launch (start us, length us, event | category | flops | bytes accessed | tf_op | source)
XLA Modules:
  0.0 31.7 jit_solution(2911408863404335504)
XLA Ops:
  0.0 1.3 %collective-permute-start.2 = (bf16[8,2,8,1024]{3,2,1,0:T(8,128)(2,1)}, bf16[8,2,8,1024]{3,2,1,0:T(8,128)(2,1)S(1)}, u32[]{:S(2)}, u32[]{:S(2)}) collective-permute-start(bf16[8,2,8,1024]{3,2,1,0:T(8,128)(2,1)} %x_ref.1), channel_id=1, source_target_pairs={{4,0},{8,4},{12,8},{5,1},{9,5},{13,9},{6,2},{10,6},{14,10},{7,3},{... | collective-permute-start | bytes 786440 | tf_op jit(solution)/shard_map/ppermute | solution.py:26
  1.3 0.0 copy-start.1
  1.3 0.9 %copy-done.1 = bf16[8,2,8,1024]{3,2,1,0:T(8,128)(2,1)S(1)} copy-done((bf16[8,2,8,1024]{3,2,1,0:T(8,128)(2,1)S(1)}, bf16[8,2,8,1024]{3,2,1,0:T(8,128)(2,1)}, u32[]{:S(2)}) %copy-start.1) | copy-done | bytes 262168
  2.2 0.0 copy-start.3
  2.2 0.0 copy-start.2
  2.2 0.1 shard_map.55
  2.4 0.5 %collective-permute-start = (f32[8,8,1]{2,1,0:T(8,128)S(1)}, f32[8,8,1]{2,1,0:T(8,128)S(1)}, u32[]{:S(2)}, u32[]{:S(2)}) collective-permute-start(f32[8,8,1]{2,1,0:T(8,128)S(1)} %get-tuple-element.23), channel_id=1, source_target_pairs={{0,1},{1,0},{2,3},{3,2},{4,5},{5,4},{6,7},{7,6},{8,9},{9,8},{10,11... | collective-permute-start | bytes 776 | tf_op jit(solution)/shard_map/ppermute | solution.py:258
  2.8 0.9 %collective-permute-done.refs_0_ = f32[8,8,1]{2,1,0:T(8,128)S(1)} collective-permute-done((f32[8,8,1]{2,1,0:T(8,128)S(1)}, f32[8,8,1]{2,1,0:T(8,128)S(1)}, u32[]{:S(2)}, u32[]{:S(2)}) %collective-permute-start) | collective-permute-done | bytes 288 | tf_op jit(solution)/shard_map/ppermute | solution.py:258
  3.7 0.2 shard_map.56.white_ref.refs_0_
  3.9 0.7 %collective-permute-start.1 = (bf16[8,2,8,1024]{3,2,1,0:T(8,128)(2,1)S(1)}, bf16[8,2,8,1024]{3,2,1,0:T(8,128)(2,1)S(1)}, u32[]{:S(2)}, u32[]{:S(2)}) collective-permute-start(bf16[8,2,8,1024]{3,2,1,0:T(8,128)(2,1)S(1)} %shard_map.56.white_ref.refs_0_), channel_id=1, source_target_pairs={{12,4},{13,5},{14,6},{15,7},{28,20},{29,21},{30,22},{31,23}} | collective-permute-start | bytes 786440 | tf_op jit(solution)/shard_map/ppermute | solution.py:311
  4.6 6.1 %collective-permute-start.6 = (bf16[8,2,8,1024]{3,2,1,0:T(8,128)(2,1)S(1)}, bf16[8,2,8,1024]{3,2,1,0:T(8,128)(2,1)S(1)}, u32[]{:S(2)}, u32[]{:S(2)}) collective-permute-start(bf16[8,2,8,1024]{3,2,1,0:T(8,128)(2,1)S(1)} %shard_map.56.white_ref.refs_0_), channel_id=1, source_target_pairs={{0,4},{4,8},{1,5},{5,9},{2,6},{6,10},{3,7},{7,11},{16,20},{20,24},... | collective-permute-start | bytes 786440 | tf_op jit(solution)/shard_map/ppermute | solution.py:312
  10.7 0.7 %collective-permute-done.2.x_ref = bf16[8,2,8,1024]{3,2,1,0:T(8,128)(2,1)S(1)} collective-permute-done((bf16[8,2,8,1024]{3,2,1,0:T(8,128)(2,1)}, bf16[8,2,8,1024]{3,2,1,0:T(8,128)(2,1)S(1)}, u32[]{:S(2)}, u32[]{:S(2)}) %collective-permute-start.2) | collective-permute-done | bytes 262176 | tf_op jit(solution)/shard_map/ppermute | solution.py:26
  11.4 0.1 shard_map.58
  11.6 0.0 collective-permute-start.3
  11.6 0.0 copy-start
  11.6 1.0 %copy-done = f32[2,96,512]{2,1,0:T(8,128)S(1)} copy-done((f32[2,96,512]{2,1,0:T(8,128)S(1)}, f32[2,96,512]{2,1,0:T(8,128)}, u32[]{:S(2)}) %copy-start) | copy-done | bytes 393240
  12.6 1.2 %shard_map.60.refs_3_ = bf16[4,1024,512]{2,1,0:T(8,128)(2,1)S(1)} custom-call(f32[2,96,512]{2,1,0:T(8,128)S(1)} %copy-done), custom_call_target="tpu_custom_call" | custom-call | flops 8 | bytes 8 | tf_op jit(solution)/shard_map/pallas_call | solution.py:317
  13.8 0.0 copy-done.3
  13.8 0.1 shard_map.57.base_ref
  13.9 0.0 collective-permute-done.3.refs_0_
  13.9 0.2 shard_map.59.refs_1_.refs_0_
  14.2 0.0 copy-done.2
  14.2 2.2 %shard_map.61 = (f32[2,2,64,256]{3,2,1,0:T(8,128)S(1)}, f32[2,2,64,256]{3,2,1,0:T(8,128)S(1)}) custom-call(f32[8,3,8,1024]{3,2,1,0:T(8,128)S(1)} %shard_map.57.base_ref, bf16[8,2,8,1024]{3,2,1,0:T(8,128)(2,1)S(1)} %shard_map.56.white_ref.refs_0_, bf16[8,2,8,1024]{3,2,1,0:T(8,128)(2,1)S(1)} %shard_map.59.refs_1_.refs_0_, f32[2,2,1024]{2,1,0:T(2,128)S(1)} %copy-done.2, ...), custom_call_target="tpu_custom_call" | custom-call | flops 8 | bytes 8 | tf_op jit(solution)/shard_map/pallas_call | solution.py:283
  16.4 0.0 copy-start.4
  16.4 0.0 collective-permute-done.1.refs_1_
  16.4 0.2 collective-permute-done.6.white_ref
  16.6 0.1 shard_map.63.base_ref
  16.7 2.2 %shard_map.64 = (f32[2,2,64,256]{3,2,1,0:T(8,128)S(1)}, f32[2,2,64,256]{3,2,1,0:T(8,128)S(1)}) custom-call(f32[8,3,8,1024]{3,2,1,0:T(8,128)S(1)} %shard_map.63.base_ref, bf16[8,2,8,1024]{3,2,1,0:T(8,128)(2,1)S(1)} %shard_map.59.refs_1_.refs_0_, bf16[8,2,8,1024]{3,2,1,0:T(8,128)(2,1)S(1)} %collective-permute-done.1.refs_1_, f32[2,2,1024]{2,1,0:T(2,128)S(1)} %copy-done.2, ...), custom_call_target="tpu_custom_call" | custom-call | flops 8 | bytes 8 | tf_op jit(solution)/shard_map/pallas_call | solution.py:283
  18.9 0.4 %collective-permute-start.7 = (f32[2,2,64,256]{3,2,1,0:T(8,128)S(1)}, f32[2,2,64,256]{3,2,1,0:T(8,128)S(1)}, u32[]{:S(2)}, u32[]{:S(2)}) collective-permute-start(f32[2,2,64,256]{3,2,1,0:T(8,128)S(1)} %get-tuple-element.36), channel_id=1, source_target_pairs={{0,1},{1,0},{2,3},{3,2},{4,5},{5,4},{6,7},{7,6},{8,9},{9,8},{10,11... | collective-permute-start | bytes 786440 | tf_op jit(solution)/shard_map/ppermute | solution.py:299
  19.3 0.2 collective-permute-start.4
  19.5 1.0 %collective-permute-done.7.refs_1_ = f32[2,2,64,256]{3,2,1,0:T(8,128)S(1)} collective-permute-done((f32[2,2,64,256]{3,2,1,0:T(8,128)S(1)}, f32[2,2,64,256]{3,2,1,0:T(8,128)S(1)}, u32[]{:S(2)}, u32[]{:S(2)}) %collective-permute-start.7) | collective-permute-done | bytes 262176 | tf_op jit(solution)/shard_map/ppermute | solution.py:299
  20.5 1.3 %collective-permute-start.8 = (bf16[2,2,64,256]{3,2,1,0:T(8,128)(2,1)S(1)}, bf16[2,2,64,256]{3,2,1,0:T(8,128)(2,1)S(1)}, u32[]{:S(2)}, u32[]{:S(2)}) collective-permute-start(bf16[2,2,64,256]{3,2,1,0:T(8,128)(2,1)S(1)} %shard_map.65), channel_id=1, source_target_pairs={{4,0},{5,3},{6,2},{7,1},{8,4},{9,7},{10,6},{11,5},{20,16},{21,19},... | collective-permute-start | bytes 393224 | tf_op jit(solution)/shard_map/ppermute | solution.py:343
  21.8 0.0 collective-permute-done.4.refs_1_
  21.9 2.0 %collective-permute-start.5 = (bf16[2,64,256]{2,1,0:T(8,128)(2,1)S(1)}, bf16[2,64,256]{2,1,0:T(8,128)(2,1)S(1)}, u32[]{:S(2)}, u32[]{:S(2)}) collective-permute-start(bf16[2,64,256]{2,1,0:T(8,128)(2,1)S(1)} %get-tuple-element.31), channel_id=1, source_target_pairs={{0,2},{2,0},{1,3},{3,1},{4,6},{6,4},{5,7},{7,5},{8,10},{10,8},{9,1... | collective-permute-start | bytes 196616 | tf_op jit(solution)/shard_map/ppermute | solution.py:299
  23.9 5.6 %collective-permute-done.8.refs_0_ = bf16[2,2,64,256]{3,2,1,0:T(8,128)(2,1)S(1)} collective-permute-done((bf16[2,2,64,256]{3,2,1,0:T(8,128)(2,1)S(1)}, bf16[2,2,64,256]{3,2,1,0:T(8,128)(2,1)S(1)}, u32[]{:S(2)}, u32[]{:S(2)}) %collective-permute-start.8) | collective-permute-done | bytes 131104 | tf_op jit(solution)/shard_map/ppermute | solution.py:343
  29.4 0.3 %collective-permute-start.9 = (bf16[2,64,256]{2,1,0:T(8,128)(2,1)S(1)}, bf16[2,64,256]{2,1,0:T(8,128)(2,1)S(1)}, u32[]{:S(2)}, u32[]{:S(2)}) collective-permute-start(bf16[2,64,256]{2,1,0:T(8,128)(2,1)S(1)} %get-tuple-element.38), channel_id=1, source_target_pairs={{0,1},{1,0},{2,3},{3,2},{4,5},{5,4},{6,7},{7,6},{8,9},{9,8},{10,11... | collective-permute-start | bytes 196616 | tf_op jit(solution)/shard_map/ppermute | solution.py:299
  29.8 0.0 copy-done.4
  29.8 0.1 broadcast_in_dim.3
  29.8 0.1 broadcast_in_dim_reshape.4.factor_ref
  29.9 0.0 collective-permute-done.5.refs_1_
  30.0 0.8 %collective-permute-done.9.refs_3_ = bf16[2,64,256]{2,1,0:T(8,128)(2,1)S(1)} collective-permute-done((bf16[2,64,256]{2,1,0:T(8,128)(2,1)S(1)}, bf16[2,64,256]{2,1,0:T(8,128)(2,1)S(1)}, u32[]{:S(2)}, u32[]{:S(2)}) %collective-permute-start.9) | collective-permute-done | bytes 65568 | tf_op jit(solution)/shard_map/ppermute | solution.py:299
  30.8 0.9 %shard_map.67 = f32[8,4,8,256]{3,2,1,0:T(8,128)} custom-call(f32[4,64,1]{2,1,0:T(8,128)S(1)} %broadcast_in_dim_reshape.4.factor_ref, f32[2,64,256]{2,1,0:T(8,128)S(1)} %get-tuple-element.30.refs_0_, bf16[2,64,256]{2,1,0:T(8,128)(2,1)S(1)} %collective-permute-done.5.refs_1_, bf16[2,64,256]{2,1,0:T(8,128)(2,1)S(1)} %get-tuple-element.37.refs_2_, ...), custom_call_target="tpu_custom_call" | custom-call | tf_op jit(solution)/shard_map/pallas_call | solution.py:352
  (4 shorter events, 0.1 us)
Async XLA Ops:
  0.0 11.4 %collective-permute-start.2 = (bf16[8,2,8,1024]{3,2,1,0:T(8,128)(2,1)}, bf16[8,2,8,1024]{3,2,1,0:T(8,128)(2,1)S(1)}, u32[]{:S(2)}, u32[]{:S(2)}) collective-permute-start(bf16[8,2,8,1024]{3,2,1,0:T(8,128)(2,1)} %x_ref.1), channel_id=1, source_target_pairs={{4,0},{8,4},{12,8},{5,1},{9,5},{13,9},{6,2},{10,6},{14,10},{7,3},{... | collective-permute-start | bytes 786440 | tf_op jit(solution)/shard_map/ppermute | solution.py:26
  1.3 1.0 %copy-start.1 = (bf16[8,2,8,1024]{3,2,1,0:T(8,128)(2,1)S(1)}, bf16[8,2,8,1024]{3,2,1,0:T(8,128)(2,1)}, u32[]{:S(2)}) copy-start(bf16[8,2,8,1024]{3,2,1,0:T(8,128)(2,1)} %x_ref.1) | copy-start | bytes 786436
  2.2 11.5 %copy-start.3 = (s32[8]{0:T(128)S(1)}, s32[8]{0:T(128)}, u32[]{:S(2)}) copy-start(s32[8]{0:T(128)} %param.6) | copy-start | bytes 100
  2.2 11.9 %copy-start.2 = (f32[2,2,1024]{2,1,0:T(2,128)S(1)}, f32[2,2,1024]{2,1,0:T(2,128)}, u32[]{:S(2)}) copy-start(f32[2,2,1024]{2,1,0:T(2,128)} %constant.6.clone.refs_2_) | copy-start | bytes 49156
  2.4 1.3 %collective-permute-start = (f32[8,8,1]{2,1,0:T(8,128)S(1)}, f32[8,8,1]{2,1,0:T(8,128)S(1)}, u32[]{:S(2)}, u32[]{:S(2)}) collective-permute-start(f32[8,8,1]{2,1,0:T(8,128)S(1)} %get-tuple-element.23), channel_id=1, source_target_pairs={{0,1},{1,0},{2,3},{3,2},{4,5},{5,4},{6,7},{7,6},{8,9},{9,8},{10,11... | collective-permute-start | bytes 776 | tf_op jit(solution)/shard_map/ppermute | solution.py:258
  3.9 12.4 %collective-permute-start.1 = (bf16[8,2,8,1024]{3,2,1,0:T(8,128)(2,1)S(1)}, bf16[8,2,8,1024]{3,2,1,0:T(8,128)(2,1)S(1)}, u32[]{:S(2)}, u32[]{:S(2)}) collective-permute-start(bf16[8,2,8,1024]{3,2,1,0:T(8,128)(2,1)S(1)} %shard_map.56.white_ref.refs_0_), channel_id=1, source_target_pairs={{12,4},{13,5},{14,6},{15,7},{28,20},{29,21},{30,22},{31,23}} | collective-permute-start | bytes 786440 | tf_op jit(solution)/shard_map/ppermute | solution.py:311
  4.6 12.0 %collective-permute-start.6 = (bf16[8,2,8,1024]{3,2,1,0:T(8,128)(2,1)S(1)}, bf16[8,2,8,1024]{3,2,1,0:T(8,128)(2,1)S(1)}, u32[]{:S(2)}, u32[]{:S(2)}) collective-permute-start(bf16[8,2,8,1024]{3,2,1,0:T(8,128)(2,1)S(1)} %shard_map.56.white_ref.refs_0_), channel_id=1, source_target_pairs={{0,4},{4,8},{1,5},{5,9},{2,6},{6,10},{3,7},{7,11},{16,20},{20,24},... | collective-permute-start | bytes 786440 | tf_op jit(solution)/shard_map/ppermute | solution.py:312
  11.6 2.4 %collective-permute-start.3 = (f32[8,8,1]{2,1,0:T(8,128)S(1)}, f32[8,8,1]{2,1,0:T(8,128)S(1)}, u32[]{:S(2)}, u32[]{:S(2)}) collective-permute-start(f32[8,8,1]{2,1,0:T(8,128)S(1)} %shard_map.58), channel_id=1, source_target_pairs={{0,1},{1,0},{2,3},{3,2},{4,5},{5,4},{6,7},{7,6},{8,9},{9,8},{10,11... | collective-permute-start | bytes 776 | tf_op jit(solution)/shard_map/ppermute | solution.py:258
  11.6 1.0 %copy-start = (f32[2,96,512]{2,1,0:T(8,128)S(1)}, f32[2,96,512]{2,1,0:T(8,128)}, u32[]{:S(2)}) copy-start(f32[2,96,512]{2,1,0:T(8,128)} %constant.7.clone.base_ref) | copy-start | bytes 1179652
  16.4 13.4 %copy-start.4 = (s32[8,4]{0,1:T(4,128)S(1)}, s32[8,4]{0,1:T(4,128)}, u32[]{:S(2)}) copy-start(s32[8,4]{0,1:T(4,128)} %param.7) | copy-start | bytes 388
  18.9 1.6 %collective-permute-start.7 = (f32[2,2,64,256]{3,2,1,0:T(8,128)S(1)}, f32[2,2,64,256]{3,2,1,0:T(8,128)S(1)}, u32[]{:S(2)}, u32[]{:S(2)}) collective-permute-start(f32[2,2,64,256]{3,2,1,0:T(8,128)S(1)} %get-tuple-element.36), channel_id=1, source_target_pairs={{0,1},{1,0},{2,3},{3,2},{4,5},{5,4},{6,7},{7,6},{8,9},{9,8},{10,11... | collective-permute-start | bytes 786440 | tf_op jit(solution)/shard_map/ppermute | solution.py:299
  19.3 2.6 %collective-permute-start.4 = (f32[2,2,64,256]{3,2,1,0:T(8,128)S(1)}, f32[2,2,64,256]{3,2,1,0:T(8,128)S(1)}, u32[]{:S(2)}, u32[]{:S(2)}) collective-permute-start(f32[2,2,64,256]{3,2,1,0:T(8,128)S(1)} %get-tuple-element.29), channel_id=1, source_target_pairs={{0,1},{1,0},{2,3},{3,2},{4,5},{5,4},{6,7},{7,6},{8,9},{9,8},{10,11... | collective-permute-start | bytes 786440 | tf_op jit(solution)/shard_map/ppermute | solution.py:299
  20.5 8.9 %collective-permute-start.8 = (bf16[2,2,64,256]{3,2,1,0:T(8,128)(2,1)S(1)}, bf16[2,2,64,256]{3,2,1,0:T(8,128)(2,1)S(1)}, u32[]{:S(2)}, u32[]{:S(2)}) collective-permute-start(bf16[2,2,64,256]{3,2,1,0:T(8,128)(2,1)S(1)} %shard_map.65), channel_id=1, source_target_pairs={{4,0},{5,3},{6,2},{7,1},{8,4},{9,7},{10,6},{11,5},{20,16},{21,19},... | collective-permute-start | bytes 393224 | tf_op jit(solution)/shard_map/ppermute | solution.py:343
  21.9 8.1 %collective-permute-start.5 = (bf16[2,64,256]{2,1,0:T(8,128)(2,1)S(1)}, bf16[2,64,256]{2,1,0:T(8,128)(2,1)S(1)}, u32[]{:S(2)}, u32[]{:S(2)}) collective-permute-start(bf16[2,64,256]{2,1,0:T(8,128)(2,1)S(1)} %get-tuple-element.31), channel_id=1, source_target_pairs={{0,2},{2,0},{1,3},{3,1},{4,6},{6,4},{5,7},{7,5},{8,10},{10,8},{9,1... | collective-permute-start | bytes 196616 | tf_op jit(solution)/shard_map/ppermute | solution.py:299
  29.4 1.3 %collective-permute-start.9 = (bf16[2,64,256]{2,1,0:T(8,128)(2,1)S(1)}, bf16[2,64,256]{2,1,0:T(8,128)(2,1)S(1)}, u32[]{:S(2)}, u32[]{:S(2)}) collective-permute-start(bf16[2,64,256]{2,1,0:T(8,128)(2,1)S(1)} %get-tuple-element.38), channel_id=1, source_target_pairs={{0,1},{1,0},{2,3},{3,2},{4,5},{5,4},{6,7},{7,6},{8,9},{9,8},{10,11... | collective-permute-start | bytes 196616 | tf_op jit(solution)/shard_map/ppermute | solution.py:299

commit v25 on v24

--- a/solution.py
+++ b/solution.py
@@ -17,6 +17,7 @@
 SUBLANES = 8
 FINE = 32
 BLOCK = 256
+STEPS = 4
 VMEM_LIMIT = 16 * 1024 * 1024
 
 
@@ -148,14 +149,14 @@
         return both[:count] + both[count:] + dot(rows_ref[part, :count, bins], table_ref[2 * part + 1, bins])
 
     tiles = f_dev // LANES
-    early = tiles - tiles // 2
-    lax.fori_loop(0, early, body, 0)
-    for part in range(2):
-        sums_ref[part] = transform(part, slice(0, early * LANES))
-    for tile in range(early, tiles):
-        prepare(slice(tile * LANES, (tile + 1) * LANES))
-    for part in range(2):
-        sums_ref[part] += transform(part, slice(early * LANES, f_dev))
+    per_step = max(1, tiles // STEPS)
+    lax.fori_loop(0, per_step, body, 0)
+    for first in range(0, tiles, per_step):
+        for part in range(2):
+            value = transform(part, slice(first * LANES, (first + per_step) * LANES))
+            sums_ref[part] = value if first == 0 else sums_ref[part] + value
+        for tile in range(first + per_step, min(first + 2 * per_step, tiles)):
+            prepare(slice(tile * LANES, (tile + 1) * LANES))
     for turn_freq, out_ref in enumerate(out_refs):
         core = (freq + turn_freq) % n_freq
         for turn_win in range(n_win):

time: 31.9 us -> 31.8 us (level)
  no operation moved by 1% of the time
where the time goes in v25:
time: 31.8 us; the launch traced here: 31.5 us
  starting transfers between devices  12.7 us (40%)
  waiting for transfers between devices  9.32 us (29%)
  Pallas kernels  7.18 us (23%)
  local copies, waits for them, and re-layouts  2.12 us (7%)
    ppermute x1, starting transfers between devices, local(): lax.ppermute(white, 'chan', [(c - 1, c) for c in range(1, n_chan - 1)])  6.09 us
    ppermute x1, waiting for transfers between devices, local(): arrived.append(lax.ppermute(block, ('chan', 'win', 'freq'), route))  5.58 us
    pallas_call x2, Pallas kernels, pairs(): pl.pallas_call(functools.partial(pairs_kernel, n, n_win, n_freq, by_windo...  4.05 us
    ppermute x4, starting transfers between devices, turns(): received.append(lax.ppermute(parts[turn], axis, route))  2.89 us
    unnamed x10, local copies, waits for them, and re-layouts  1.95 us
    ppermute x4, waiting for transfers between devices, turns(): received.append(lax.ppermute(parts[turn], axis, route))  1.83 us
    ppermute x1, starting transfers between devices, local(): arrived.append(lax.ppermute(block, ('chan', 'win', 'freq'), route))  1.29 us
    ppermute x1, starting transfers between devices, from_behind(): return lax.ppermute(block, axis, route)  1.28 us
  transfers between devices with their start and end apart: 10, of which 6 were waited for; matrix products, arithmetic and copies ran while one was open for 1% of the time, Pallas kernels for 13%

profile of v25, /device:TPU:0, one launch (start us, length us, event | category | flops | bytes accessed | tf_op | source)
XLA Modules:
  0.0 31.5 jit_solution(865074934296251818)
XLA Ops:
  0.0 1.3 %collective-permute-start.2 = (bf16[8,2,8,1024]{3,2,1,0:T(8,128)(2,1)}, bf16[8,2,8,1024]{3,2,1,0:T(8,128)(2,1)S(1)}, u32[]{:S(2)}, u32[]{:S(2)}) collective-permute-start(bf16[8,2,8,1024]{3,2,1,0:T(8,128)(2,1)} %x_ref.1), channel_id=1, source_target_pairs={{4,0},{8,4},{12,8},{5,1},{9,5},{13,9},{6,2},{10,6},{14,10},{7,3},{... | collective-permute-start | bytes 786440 | tf_op jit(solution)/shard_map/ppermute | solution.py:27
  1.3 0.0 copy-start.1
  1.3 0.9 %copy-done.1 = bf16[8,2,8,1024]{3,2,1,0:T(8,128)(2,1)S(1)} copy-done((bf16[8,2,8,1024]{3,2,1,0:T(8,128)(2,1)S(1)}, bf16[8,2,8,1024]{3,2,1,0:T(8,128)(2,1)}, u32[]{:S(2)}) %copy-start.1) | copy-done | bytes 262168
  2.2 0.0 copy-start.3
  2.2 0.0 copy-start.2
  2.2 0.1 shard_map.55
  2.4 0.5 %collective-permute-start = (f32[8,8,1]{2,1,0:T(8,128)S(1)}, f32[8,8,1]{2,1,0:T(8,128)S(1)}, u32[]{:S(2)}, u32[]{:S(2)}) collective-permute-start(f32[8,8,1]{2,1,0:T(8,128)S(1)} %get-tuple-element.23), channel_id=1, source_target_pairs={{0,1},{1,0},{2,3},{3,2},{4,5},{5,4},{6,7},{7,6},{8,9},{9,8},{10,11... | collective-permute-start | bytes 776 | tf_op jit(solution)/shard_map/ppermute | solution.py:259
  2.8 0.9 %collective-permute-done.refs_0_ = f32[8,8,1]{2,1,0:T(8,128)S(1)} collective-permute-done((f32[8,8,1]{2,1,0:T(8,128)S(1)}, f32[8,8,1]{2,1,0:T(8,128)S(1)}, u32[]{:S(2)}, u32[]{:S(2)}) %collective-permute-start) | collective-permute-done | bytes 288 | tf_op jit(solution)/shard_map/ppermute | solution.py:259
  3.7 0.2 shard_map.56.white_ref.refs_0_
  3.9 0.7 %collective-permute-start.1 = (bf16[8,2,8,1024]{3,2,1,0:T(8,128)(2,1)S(1)}, bf16[8,2,8,1024]{3,2,1,0:T(8,128)(2,1)S(1)}, u32[]{:S(2)}, u32[]{:S(2)}) collective-permute-start(bf16[8,2,8,1024]{3,2,1,0:T(8,128)(2,1)S(1)} %shard_map.56.white_ref.refs_0_), channel_id=1, source_target_pairs={{12,4},{13,5},{14,6},{15,7},{28,20},{29,21},{30,22},{31,23}} | collective-permute-start | bytes 786440 | tf_op jit(solution)/shard_map/ppermute | solution.py:312
  4.6 6.1 %collective-permute-start.6 = (bf16[8,2,8,1024]{3,2,1,0:T(8,128)(2,1)S(1)}, bf16[8,2,8,1024]{3,2,1,0:T(8,128)(2,1)S(1)}, u32[]{:S(2)}, u32[]{:S(2)}) collective-permute-start(bf16[8,2,8,1024]{3,2,1,0:T(8,128)(2,1)S(1)} %shard_map.56.white_ref.refs_0_), channel_id=1, source_target_pairs={{0,4},{4,8},{1,5},{5,9},{2,6},{6,10},{3,7},{7,11},{16,20},{20,24},... | collective-permute-start | bytes 786440 | tf_op jit(solution)/shard_map/ppermute | solution.py:313
  10.7 0.7 %collective-permute-done.2.x_ref = bf16[8,2,8,1024]{3,2,1,0:T(8,128)(2,1)S(1)} collective-permute-done((bf16[8,2,8,1024]{3,2,1,0:T(8,128)(2,1)}, bf16[8,2,8,1024]{3,2,1,0:T(8,128)(2,1)S(1)}, u32[]{:S(2)}, u32[]{:S(2)}) %collective-permute-start.2) | collective-permute-done | bytes 262176 | tf_op jit(solution)/shard_map/ppermute | solution.py:27
  11.4 0.1 shard_map.58
  11.6 0.0 collective-permute-start.3
  11.6 0.0 copy-start
  11.6 1.0 %copy-done = f32[2,96,512]{2,1,0:T(8,128)S(1)} copy-done((f32[2,96,512]{2,1,0:T(8,128)S(1)}, f32[2,96,512]{2,1,0:T(8,128)}, u32[]{:S(2)}) %copy-start) | copy-done | bytes 393240
  12.6 1.2 %shard_map.60.refs_3_ = bf16[4,1024,512]{2,1,0:T(8,128)(2,1)S(1)} custom-call(f32[2,96,512]{2,1,0:T(8,128)S(1)} %copy-done), custom_call_target="tpu_custom_call" | custom-call | flops 8 | bytes 8 | tf_op jit(solution)/shard_map/pallas_call | solution.py:318
  13.8 0.0 copy-done.3
  13.8 0.1 shard_map.57.base_ref
  13.9 0.0 collective-permute-done.3.refs_0_
  13.9 0.2 shard_map.59.refs_1_.refs_0_
  14.2 0.0 copy-done.2
  14.2 2.0 %shard_map.61 = (f32[2,2,64,256]{3,2,1,0:T(8,128)S(1)}, f32[2,2,64,256]{3,2,1,0:T(8,128)S(1)}) custom-call(f32[8,3,8,1024]{3,2,1,0:T(8,128)S(1)} %shard_map.57.base_ref, bf16[8,2,8,1024]{3,2,1,0:T(8,128)(2,1)S(1)} %shard_map.56.white_ref.refs_0_, bf16[8,2,8,1024]{3,2,1,0:T(8,128)(2,1)S(1)} %shard_map.59.refs_1_.refs_0_, f32[2,2,1024]{2,1,0:T(2,128)S(1)} %copy-done.2, ...), custom_call_target="tpu_custom_call" | custom-call | flops 8 | bytes 8 | tf_op jit(solution)/shard_map/pallas_call | solution.py:284
  16.2 0.0 copy-start.4
  16.2 0.0 collective-permute-done.1.refs_1_
  16.2 0.3 %collective-permute-done.6.white_ref = bf16[8,2,8,1024]{3,2,1,0:T(8,128)(2,1)S(1)} collective-permute-done((bf16[8,2,8,1024]{3,2,1,0:T(8,128)(2,1)S(1)}, bf16[8,2,8,1024]{3,2,1,0:T(8,128)(2,1)S(1)}, u32[]{:S(2)}, u32[]{:S(2)}) %collective-permute-start.6) | collective-permute-done | bytes 262176 | tf_op jit(solution)/shard_map/ppermute | solution.py:313
  16.6 0.1 shard_map.63.base_ref
  16.7 2.0 %shard_map.64 = (f32[2,2,64,256]{3,2,1,0:T(8,128)S(1)}, f32[2,2,64,256]{3,2,1,0:T(8,128)S(1)}) custom-call(f32[8,3,8,1024]{3,2,1,0:T(8,128)S(1)} %shard_map.63.base_ref, bf16[8,2,8,1024]{3,2,1,0:T(8,128)(2,1)S(1)} %shard_map.59.refs_1_.refs_0_, bf16[8,2,8,1024]{3,2,1,0:T(8,128)(2,1)S(1)} %collective-permute-done.1.refs_1_, f32[2,2,1024]{2,1,0:T(2,128)S(1)} %copy-done.2, ...), custom_call_target="tpu_custom_call" | custom-call | flops 8 | bytes 8 | tf_op jit(solution)/shard_map/pallas_call | solution.py:284
  18.7 0.3 collective-permute-start.7
  19.0 0.3 collective-permute-start.4
  19.3 1.0 %collective-permute-done.7.refs_1_ = f32[2,2,64,256]{3,2,1,0:T(8,128)S(1)} collective-permute-done((f32[2,2,64,256]{3,2,1,0:T(8,128)S(1)}, f32[2,2,64,256]{3,2,1,0:T(8,128)S(1)}, u32[]{:S(2)}, u32[]{:S(2)}) %collective-permute-start.7) | collective-permute-done | bytes 262176 | tf_op jit(solution)/shard_map/ppermute | solution.py:300
  20.4 1.3 %collective-permute-start.8 = (bf16[2,2,64,256]{3,2,1,0:T(8,128)(2,1)S(1)}, bf16[2,2,64,256]{3,2,1,0:T(8,128)(2,1)S(1)}, u32[]{:S(2)}, u32[]{:S(2)}) collective-permute-start(bf16[2,2,64,256]{3,2,1,0:T(8,128)(2,1)S(1)} %shard_map.65), channel_id=1, source_target_pairs={{4,0},{5,3},{6,2},{7,1},{8,4},{9,7},{10,6},{11,5},{20,16},{21,19},... | collective-permute-start | bytes 393224 | tf_op jit(solution)/shard_map/ppermute | solution.py:344
  21.7 0.0 collective-permute-done.4.refs_1_
  21.7 2.0 %collective-permute-start.5 = (bf16[2,64,256]{2,1,0:T(8,128)(2,1)S(1)}, bf16[2,64,256]{2,1,0:T(8,128)(2,1)S(1)}, u32[]{:S(2)}, u32[]{:S(2)}) collective-permute-start(bf16[2,64,256]{2,1,0:T(8,128)(2,1)S(1)} %get-tuple-element.31), channel_id=1, source_target_pairs={{0,2},{2,0},{1,3},{3,1},{4,6},{6,4},{5,7},{7,5},{8,10},{10,8},{9,1... | collective-permute-start | bytes 196616 | tf_op jit(solution)/shard_map/ppermute | solution.py:300
  23.7 5.6 %collective-permute-done.8.refs_0_ = bf16[2,2,64,256]{3,2,1,0:T(8,128)(2,1)S(1)} collective-permute-done((bf16[2,2,64,256]{3,2,1,0:T(8,128)(2,1)S(1)}, bf16[2,2,64,256]{3,2,1,0:T(8,128)(2,1)S(1)}, u32[]{:S(2)}, u32[]{:S(2)}) %collective-permute-start.8) | collective-permute-done | bytes 131104 | tf_op jit(solution)/shard_map/ppermute | solution.py:344
  29.3 0.3 %collective-permute-start.9 = (bf16[2,64,256]{2,1,0:T(8,128)(2,1)S(1)}, bf16[2,64,256]{2,1,0:T(8,128)(2,1)S(1)}, u32[]{:S(2)}, u32[]{:S(2)}) collective-permute-start(bf16[2,64,256]{2,1,0:T(8,128)(2,1)S(1)} %get-tuple-element.38), channel_id=1, source_target_pairs={{0,1},{1,0},{2,3},{3,2},{4,5},{5,4},{6,7},{7,6},{8,9},{9,8},{10,11... | collective-permute-start | bytes 196616 | tf_op jit(solution)/shard_map/ppermute | solution.py:300
  29.6 0.0 copy-done.4
  29.6 0.1 broadcast_in_dim.3
  29.7 0.1 broadcast_in_dim_reshape.4.factor_ref
  29.8 0.0 collective-permute-done.5.refs_1_
  29.8 0.8 %collective-permute-done.9.refs_3_ = bf16[2,64,256]{2,1,0:T(8,128)(2,1)S(1)} collective-permute-done((bf16[2,64,256]{2,1,0:T(8,128)(2,1)S(1)}, bf16[2,64,256]{2,1,0:T(8,128)(2,1)S(1)}, u32[]{:S(2)}, u32[]{:S(2)}) %collective-permute-start.9) | collective-permute-done | bytes 65568 | tf_op jit(solution)/shard_map/ppermute | solution.py:300
  30.6 0.9 %shard_map.67 = f32[8,4,8,256]{3,2,1,0:T(8,128)} custom-call(f32[4,64,1]{2,1,0:T(8,128)S(1)} %broadcast_in_dim_reshape.4.factor_ref, f32[2,64,256]{2,1,0:T(8,128)S(1)} %get-tuple-element.30.refs_0_, bf16[2,64,256]{2,1,0:T(8,128)(2,1)S(1)} %collective-permute-done.5.refs_1_, bf16[2,64,256]{2,1,0:T(8,128)(2,1)S(1)} %get-tuple-element.37.refs_2_, ...), custom_call_target="tpu_custom_call" | custom-call | tf_op jit(solution)/shard_map/pallas_call | solution.py:353
  (4 shorter events, 0.1 us)
Async XLA Ops:
  0.0 11.4 %collective-permute-start.2 = (bf16[8,2,8,1024]{3,2,1,0:T(8,128)(2,1)}, bf16[8,2,8,1024]{3,2,1,0:T(8,128)(2,1)S(1)}, u32[]{:S(2)}, u32[]{:S(2)}) collective-permute-start(bf16[8,2,8,1024]{3,2,1,0:T(8,128)(2,1)} %x_ref.1), channel_id=1, source_target_pairs={{4,0},{8,4},{12,8},{5,1},{9,5},{13,9},{6,2},{10,6},{14,10},{7,3},{... | collective-permute-start | bytes 786440 | tf_op jit(solution)/shard_map/ppermute | solution.py:27
  1.3 1.0 %copy-start.1 = (bf16[8,2,8,1024]{3,2,1,0:T(8,128)(2,1)S(1)}, bf16[8,2,8,1024]{3,2,1,0:T(8,128)(2,1)}, u32[]{:S(2)}) copy-start(bf16[8,2,8,1024]{3,2,1,0:T(8,128)(2,1)} %x_ref.1) | copy-start | bytes 786436
  2.2 11.5 %copy-start.3 = (s32[8]{0:T(128)S(1)}, s32[8]{0:T(128)}, u32[]{:S(2)}) copy-start(s32[8]{0:T(128)} %param.6) | copy-start | bytes 100
  2.2 11.9 %copy-start.2 = (f32[2,2,1024]{2,1,0:T(2,128)S(1)}, f32[2,2,1024]{2,1,0:T(2,128)}, u32[]{:S(2)}) copy-start(f32[2,2,1024]{2,1,0:T(2,128)} %constant.6.clone.refs_2_) | copy-start | bytes 49156
  2.4 1.3 %collective-permute-start = (f32[8,8,1]{2,1,0:T(8,128)S(1)}, f32[8,8,1]{2,1,0:T(8,128)S(1)}, u32[]{:S(2)}, u32[]{:S(2)}) collective-permute-start(f32[8,8,1]{2,1,0:T(8,128)S(1)} %get-tuple-element.23), channel_id=1, source_target_pairs={{0,1},{1,0},{2,3},{3,2},{4,5},{5,4},{6,7},{7,6},{8,9},{9,8},{10,11... | collective-permute-start | bytes 776 | tf_op jit(solution)/shard_map/ppermute | solution.py:259
  3.9 12.3 %collective-permute-start.1 = (bf16[8,2,8,1024]{3,2,1,0:T(8,128)(2,1)S(1)}, bf16[8,2,8,1024]{3,2,1,0:T(8,128)(2,1)S(1)}, u32[]{:S(2)}, u32[]{:S(2)}) collective-permute-start(bf16[8,2,8,1024]{3,2,1,0:T(8,128)(2,1)S(1)} %shard_map.56.white_ref.refs_0_), channel_id=1, source_target_pairs={{12,4},{13,5},{14,6},{15,7},{28,20},{29,21},{30,22},{31,23}} | collective-permute-start | bytes 786440 | tf_op jit(solution)/shard_map/ppermute | solution.py:312
  4.6 12.0 %collective-permute-start.6 = (bf16[8,2,8,1024]{3,2,1,0:T(8,128)(2,1)S(1)}, bf16[8,2,8,1024]{3,2,1,0:T(8,128)(2,1)S(1)}, u32[]{:S(2)}, u32[]{:S(2)}) collective-permute-start(bf16[8,2,8,1024]{3,2,1,0:T(8,128)(2,1)S(1)} %shard_map.56.white_ref.refs_0_), channel_id=1, source_target_pairs={{0,4},{4,8},{1,5},{5,9},{2,6},{6,10},{3,7},{7,11},{16,20},{20,24},... | collective-permute-start | bytes 786440 | tf_op jit(solution)/shard_map/ppermute | solution.py:313
  11.6 2.4 %collective-permute-start.3 = (f32[8,8,1]{2,1,0:T(8,128)S(1)}, f32[8,8,1]{2,1,0:T(8,128)S(1)}, u32[]{:S(2)}, u32[]{:S(2)}) collective-permute-start(f32[8,8,1]{2,1,0:T(8,128)S(1)} %shard_map.58), channel_id=1, source_target_pairs={{0,1},{1,0},{2,3},{3,2},{4,5},{5,4},{6,7},{7,6},{8,9},{9,8},{10,11... | collective-permute-start | bytes 776 | tf_op jit(solution)/shard_map/ppermute | solution.py:259
  11.6 1.0 %copy-start = (f32[2,96,512]{2,1,0:T(8,128)S(1)}, f32[2,96,512]{2,1,0:T(8,128)}, u32[]{:S(2)}) copy-start(f32[2,96,512]{2,1,0:T(8,128)} %constant.7.clone.base_ref) | copy-start | bytes 1179652
  16.2 13.4 %copy-start.4 = (s32[8,4]{0,1:T(4,128)S(1)}, s32[8,4]{0,1:T(4,128)}, u32[]{:S(2)}) copy-start(s32[8,4]{0,1:T(4,128)} %param.7) | copy-start | bytes 388
  18.7 1.6 %collective-permute-start.7 = (f32[2,2,64,256]{3,2,1,0:T(8,128)S(1)}, f32[2,2,64,256]{3,2,1,0:T(8,128)S(1)}, u32[]{:S(2)}, u32[]{:S(2)}) collective-permute-start(f32[2,2,64,256]{3,2,1,0:T(8,128)S(1)} %get-tuple-element.36), channel_id=1, source_target_pairs={{0,1},{1,0},{2,3},{3,2},{4,5},{5,4},{6,7},{7,6},{8,9},{9,8},{10,11... | collective-permute-start | bytes 786440 | tf_op jit(solution)/shard_map/ppermute | solution.py:300
  19.0 2.7 %collective-permute-start.4 = (f32[2,2,64,256]{3,2,1,0:T(8,128)S(1)}, f32[2,2,64,256]{3,2,1,0:T(8,128)S(1)}, u32[]{:S(2)}, u32[]{:S(2)}) collective-permute-start(f32[2,2,64,256]{3,2,1,0:T(8,128)S(1)} %get-tuple-element.29), channel_id=1, source_target_pairs={{0,1},{1,0},{2,3},{3,2},{4,5},{5,4},{6,7},{7,6},{8,9},{9,8},{10,11... | collective-permute-start | bytes 786440 | tf_op jit(solution)/shard_map/ppermute | solution.py:300
  20.4 8.9 %collective-permute-start.8 = (bf16[2,2,64,256]{3,2,1,0:T(8,128)(2,1)S(1)}, bf16[2,2,64,256]{3,2,1,0:T(8,128)(2,1)S(1)}, u32[]{:S(2)}, u32[]{:S(2)}) collective-permute-start(bf16[2,2,64,256]{3,2,1,0:T(8,128)(2,1)S(1)} %shard_map.65), channel_id=1, source_target_pairs={{4,0},{5,3},{6,2},{7,1},{8,4},{9,7},{10,6},{11,5},{20,16},{21,19},... | collective-permute-start | bytes 393224 | tf_op jit(solution)/shard_map/ppermute | solution.py:344
  21.7 8.1 %collective-permute-start.5 = (bf16[2,64,256]{2,1,0:T(8,128)(2,1)S(1)}, bf16[2,64,256]{2,1,0:T(8,128)(2,1)S(1)}, u32[]{:S(2)}, u32[]{:S(2)}) collective-permute-start(bf16[2,64,256]{2,1,0:T(8,128)(2,1)S(1)} %get-tuple-element.31), channel_id=1, source_target_pairs={{0,2},{2,0},{1,3},{3,1},{4,6},{6,4},{5,7},{7,5},{8,10},{10,8},{9,1... | collective-permute-start | bytes 196616 | tf_op jit(solution)/shard_map/ppermute | solution.py:300
  29.3 1.3 %collective-permute-start.9 = (bf16[2,64,256]{2,1,0:T(8,128)(2,1)S(1)}, bf16[2,64,256]{2,1,0:T(8,128)(2,1)S(1)}, u32[]{:S(2)}, u32[]{:S(2)}) collective-permute-start(bf16[2,64,256]{2,1,0:T(8,128)(2,1)S(1)} %get-tuple-element.38), channel_id=1, source_target_pairs={{0,1},{1,0},{2,3},{3,2},{4,5},{5,4},{6,7},{7,6},{8,9},{9,8},{10,11... | collective-permute-start | bytes 196616 | tf_op jit(solution)/shard_map/ppermute | solution.py:300

commit v26 on v25

--- a/solution.py
+++ b/solution.py
@@ -326,8 +326,9 @@
     far, parts = lax.optimization_barrier((far, parts))
     above, far = lax.optimization_barrier((above, far))
     kinds = [jnp.float32] + [jnp.bfloat16] * (n_win - 1)
+    remote = turns(pairs(kept(above), [below] + far, True), "freq", n_freq)
+    remote, parts = lax.optimization_barrier((remote, parts))
     near = turns(split_windows(parts, kinds), "win", n_win)
-    remote = turns(pairs(kept(above), [below] + far, True), "freq", n_freq)
     shape = (remote[0].shape[0], ch * ch, width)
     n_ships = n_win // n_freq
     shipped = pl.pallas_call(

time: 31.8 us -> 35.7 us (1.12)
  waiting for transfers between devices: 9.32 us -> 14 us
  starting transfers between devices: 12.7 us -> 11.9 us
    ppermute x4, waiting for transfers between devices: 1.83 us -> 4.33 us  [turns(): received.append(lax.ppermute(parts[turn], axis, route))]
    ppermute x1, waiting for transfers between devices: 5.58 us -> 7.8 us  [local(): arrived.append(lax.ppermute(block, ('chan', 'win', 'freq'), route))]
    ppermute x4, starting transfers between devices: 2.89 us -> 2.11 us  [turns(): received.append(lax.ppermute(parts[turn], axis, route))]
  transfers between devices with their start and end apart: 10 -> 10, of which waited for: 6 -> 6; matrix products, arithmetic and copies ran while one was open for 1% -> 0% of each run, Pallas kernels for 13% -> 12%
where the time goes in v26:
time: 35.7 us; the launch traced here: 35.4 us
  waiting for transfers between devices  14 us (39%)
  starting transfers between devices  11.9 us (33%)
  Pallas kernels  7.18 us (20%)
  local copies, waits for them, and re-layouts  2.12 us (6%)
    ppermute x1, waiting for transfers between devices, local(): arrived.append(lax.ppermute(block, ('chan', 'win', 'freq'), route))  7.8 us
    ppermute x1, starting transfers between devices, local(): lax.ppermute(white, 'chan', [(c - 1, c) for c in range(1, n_chan - 1)])  6.09 us
    ppermute x4, waiting for transfers between devices, turns(): received.append(lax.ppermute(parts[turn], axis, route))  4.33 us
    pallas_call x2, Pallas kernels, pairs(): pl.pallas_call(functools.partial(pairs_kernel, n, n_win, n_freq, by_windo...  4.05 us
    ppermute x4, starting transfers between devices, turns(): received.append(lax.ppermute(parts[turn], axis, route))  2.11 us
    unnamed x10, local copies, waits for them, and re-layouts  1.95 us
    ppermute x1, starting transfers between devices, local(): arrived.append(lax.ppermute(block, ('chan', 'win', 'freq'), route))  1.29 us
    ppermute x1, starting transfers between devices, from_behind(): return lax.ppermute(block, axis, route)  1.28 us
  transfers between devices with their start and end apart: 10, of which 6 were waited for; matrix products, arithmetic and copies ran while one was open for 0% of the time, Pallas kernels for 12%

profile of v26, /device:TPU:0, one launch (start us, length us, event | category | flops | bytes accessed | tf_op | source)
XLA Modules:
  0.0 35.4 jit_solution(2600578679822956535)
XLA Ops:
  0.0 1.3 %collective-permute-start.3 = (bf16[8,2,8,1024]{3,2,1,0:T(8,128)(2,1)}, bf16[8,2,8,1024]{3,2,1,0:T(8,128)(2,1)S(1)}, u32[]{:S(2)}, u32[]{:S(2)}) collective-permute-start(bf16[8,2,8,1024]{3,2,1,0:T(8,128)(2,1)} %x_ref.1), channel_id=1, source_target_pairs={{4,0},{8,4},{12,8},{5,1},{9,5},{13,9},{6,2},{10,6},{14,10},{7,3},{... | collective-permute-start | bytes 786440 | tf_op jit(solution)/shard_map/ppermute | solution.py:27
  1.3 0.0 copy-start.1
  1.3 0.9 %copy-done.1 = bf16[8,2,8,1024]{3,2,1,0:T(8,128)(2,1)S(1)} copy-done((bf16[8,2,8,1024]{3,2,1,0:T(8,128)(2,1)S(1)}, bf16[8,2,8,1024]{3,2,1,0:T(8,128)(2,1)}, u32[]{:S(2)}) %copy-start.1) | copy-done | bytes 262168
  2.2 0.0 copy-start.3
  2.2 0.0 copy-start.2
  2.2 0.1 shard_map.55
  2.4 0.5 %collective-permute-start = (f32[8,8,1]{2,1,0:T(8,128)S(1)}, f32[8,8,1]{2,1,0:T(8,128)S(1)}, u32[]{:S(2)}, u32[]{:S(2)}) collective-permute-start(f32[8,8,1]{2,1,0:T(8,128)S(1)} %get-tuple-element.27), channel_id=1, source_target_pairs={{0,1},{1,0},{2,3},{3,2},{4,5},{5,4},{6,7},{7,6},{8,9},{9,8},{10,11... | collective-permute-start | bytes 776 | tf_op jit(solution)/shard_map/ppermute | solution.py:259
  2.8 0.9 %collective-permute-done.refs_0_ = f32[8,8,1]{2,1,0:T(8,128)S(1)} collective-permute-done((f32[8,8,1]{2,1,0:T(8,128)S(1)}, f32[8,8,1]{2,1,0:T(8,128)S(1)}, u32[]{:S(2)}, u32[]{:S(2)}) %collective-permute-start) | collective-permute-done | bytes 288 | tf_op jit(solution)/shard_map/ppermute | solution.py:259
  3.7 0.2 shard_map.56.white_ref.refs_0_
  3.9 0.7 %collective-permute-start.2 = (bf16[8,2,8,1024]{3,2,1,0:T(8,128)(2,1)S(1)}, bf16[8,2,8,1024]{3,2,1,0:T(8,128)(2,1)S(1)}, u32[]{:S(2)}, u32[]{:S(2)}) collective-permute-start(bf16[8,2,8,1024]{3,2,1,0:T(8,128)(2,1)S(1)} %shard_map.56.white_ref.refs_0_), channel_id=1, source_target_pairs={{12,4},{13,5},{14,6},{15,7},{28,20},{29,21},{30,22},{31,23}} | collective-permute-start | bytes 786440 | tf_op jit(solution)/shard_map/ppermute | solution.py:312
  4.6 6.1 %collective-permute-start.1 = (bf16[8,2,8,1024]{3,2,1,0:T(8,128)(2,1)S(1)}, bf16[8,2,8,1024]{3,2,1,0:T(8,128)(2,1)S(1)}, u32[]{:S(2)}, u32[]{:S(2)}) collective-permute-start(bf16[8,2,8,1024]{3,2,1,0:T(8,128)(2,1)S(1)} %shard_map.56.white_ref.refs_0_), channel_id=1, source_target_pairs={{0,4},{4,8},{1,5},{5,9},{2,6},{6,10},{3,7},{7,11},{16,20},{20,24},... | collective-permute-start | bytes 786440 | tf_op jit(solution)/shard_map/ppermute | solution.py:313
  10.7 0.7 %collective-permute-done.3.x_ref = bf16[8,2,8,1024]{3,2,1,0:T(8,128)(2,1)S(1)} collective-permute-done((bf16[8,2,8,1024]{3,2,1,0:T(8,128)(2,1)}, bf16[8,2,8,1024]{3,2,1,0:T(8,128)(2,1)S(1)}, u32[]{:S(2)}, u32[]{:S(2)}) %collective-permute-start.3) | collective-permute-done | bytes 262176 | tf_op jit(solution)/shard_map/ppermute | solution.py:27
  11.4 0.1 shard_map.58
  11.6 0.0 collective-permute-start.4
  11.6 0.0 copy-start
  11.6 1.0 %copy-done = f32[2,96,512]{2,1,0:T(8,128)S(1)} copy-done((f32[2,96,512]{2,1,0:T(8,128)S(1)}, f32[2,96,512]{2,1,0:T(8,128)}, u32[]{:S(2)}) %copy-start) | copy-done | bytes 393240
  12.6 1.2 %shard_map.60.refs_3_ = bf16[4,1024,512]{2,1,0:T(8,128)(2,1)S(1)} custom-call(f32[2,96,512]{2,1,0:T(8,128)S(1)} %copy-done), custom_call_target="tpu_custom_call" | custom-call | flops 8 | bytes 8 | tf_op jit(solution)/shard_map/pallas_call | solution.py:318
  13.8 0.0 copy-done.3
  13.8 0.1 shard_map.57.base_ref
  13.9 0.0 collective-permute-done.4.refs_0_
  13.9 0.2 shard_map.59.refs_1_.refs_0_
  14.2 0.0 copy-done.2
  14.2 2.0 %shard_map.61 = (f32[2,2,64,256]{3,2,1,0:T(8,128)S(1)}, f32[2,2,64,256]{3,2,1,0:T(8,128)S(1)}) custom-call(f32[8,3,8,1024]{3,2,1,0:T(8,128)S(1)} %shard_map.57.base_ref, bf16[8,2,8,1024]{3,2,1,0:T(8,128)(2,1)S(1)} %shard_map.56.white_ref.refs_0_, bf16[8,2,8,1024]{3,2,1,0:T(8,128)(2,1)S(1)} %shard_map.59.refs_1_.refs_0_, f32[2,2,1024]{2,1,0:T(2,128)S(1)} %copy-done.2, ...), custom_call_target="tpu_custom_call" | custom-call | flops 8 | bytes 8 | tf_op jit(solution)/shard_map/pallas_call | solution.py:284
  16.2 0.0 copy-start.4
  16.2 0.0 collective-permute-done.2.refs_1_
  16.2 0.3 collective-permute-done.1.white_ref
  16.6 0.1 shard_map.62.base_ref
  16.7 2.0 %shard_map.63 = (f32[2,2,64,256]{3,2,1,0:T(8,128)S(1)}, f32[2,2,64,256]{3,2,1,0:T(8,128)S(1)}) custom-call(f32[8,3,8,1024]{3,2,1,0:T(8,128)S(1)} %shard_map.62.base_ref, bf16[8,2,8,1024]{3,2,1,0:T(8,128)(2,1)S(1)} %shard_map.59.refs_1_.refs_0_, bf16[8,2,8,1024]{3,2,1,0:T(8,128)(2,1)S(1)} %collective-permute-done.2.refs_1_, f32[2,2,1024]{2,1,0:T(2,128)S(1)} %copy-done.2, ...), custom_call_target="tpu_custom_call" | custom-call | flops 8 | bytes 8 | tf_op jit(solution)/shard_map/pallas_call | solution.py:284
  18.7 0.3 collective-permute-start.5
  19.0 1.3 %collective-permute-done.5.refs_1_ = f32[2,2,64,256]{3,2,1,0:T(8,128)S(1)} collective-permute-done((f32[2,2,64,256]{3,2,1,0:T(8,128)S(1)}, f32[2,2,64,256]{3,2,1,0:T(8,128)S(1)}, u32[]{:S(2)}, u32[]{:S(2)}) %collective-permute-start.5) | collective-permute-done | bytes 262176 | tf_op jit(solution)/shard_map/ppermute | solution.py:300
  20.3 0.2 collective-permute-start.6
  20.6 1.3 %collective-permute-start.8 = (bf16[2,2,64,256]{3,2,1,0:T(8,128)(2,1)S(1)}, bf16[2,2,64,256]{3,2,1,0:T(8,128)(2,1)S(1)}, u32[]{:S(2)}, u32[]{:S(2)}) collective-permute-start(bf16[2,2,64,256]{3,2,1,0:T(8,128)(2,1)S(1)} %shard_map.65), channel_id=1, source_target_pairs={{4,0},{5,3},{6,2},{7,1},{8,4},{9,7},{10,6},{11,5},{20,16},{21,19},... | collective-permute-start | bytes 393224 | tf_op jit(solution)/shard_map/ppermute | solution.py:345
  21.9 7.8 %collective-permute-done.8.refs_0_ = bf16[2,2,64,256]{3,2,1,0:T(8,128)(2,1)S(1)} collective-permute-done((bf16[2,2,64,256]{3,2,1,0:T(8,128)(2,1)S(1)}, bf16[2,2,64,256]{3,2,1,0:T(8,128)(2,1)S(1)}, u32[]{:S(2)}, u32[]{:S(2)}) %collective-permute-start.8) | collective-permute-done | bytes 131104 | tf_op jit(solution)/shard_map/ppermute | solution.py:345
  29.7 0.5 %collective-permute-start.9 = (bf16[2,64,256]{2,1,0:T(8,128)(2,1)S(1)}, bf16[2,64,256]{2,1,0:T(8,128)(2,1)S(1)}, u32[]{:S(2)}, u32[]{:S(2)}) collective-permute-start(bf16[2,64,256]{2,1,0:T(8,128)(2,1)S(1)} %get-tuple-element.46), channel_id=1, source_target_pairs={{0,1},{1,0},{2,3},{3,2},{4,5},{5,4},{6,7},{7,6},{8,9},{9,8},{10,11... | collective-permute-start | bytes 196616 | tf_op jit(solution)/shard_map/ppermute | solution.py:300
  30.2 0.0 collective-permute-done.6.refs_1_
  30.2 1.2 %collective-permute-start.7 = (bf16[2,64,256]{2,1,0:T(8,128)(2,1)S(1)}, bf16[2,64,256]{2,1,0:T(8,128)(2,1)S(1)}, u32[]{:S(2)}, u32[]{:S(2)}) collective-permute-start(bf16[2,64,256]{2,1,0:T(8,128)(2,1)S(1)} %get-tuple-element.42), channel_id=1, source_target_pairs={{0,2},{2,0},{1,3},{3,1},{4,6},{6,4},{5,7},{7,5},{8,10},{10,8},{9,1... | collective-permute-start | bytes 196616 | tf_op jit(solution)/shard_map/ppermute | solution.py:300
  31.4 0.0 copy-done.4
  31.4 0.1 broadcast_in_dim.3
  31.4 0.1 broadcast_in_dim_reshape.4.factor_ref
  31.5 0.0 collective-permute-done.9.refs_3_
  31.6 3.0 %collective-permute-done.7.refs_1_ = bf16[2,64,256]{2,1,0:T(8,128)(2,1)S(1)} collective-permute-done((bf16[2,64,256]{2,1,0:T(8,128)(2,1)S(1)}, bf16[2,64,256]{2,1,0:T(8,128)(2,1)S(1)}, u32[]{:S(2)}, u32[]{:S(2)}) %collective-permute-start.7) | collective-permute-done | bytes 65568 | tf_op jit(solution)/shard_map/ppermute | solution.py:300
  34.5 0.9 %shard_map.67 = f32[8,4,8,256]{3,2,1,0:T(8,128)} custom-call(f32[4,64,1]{2,1,0:T(8,128)S(1)} %broadcast_in_dim_reshape.4.factor_ref, f32[2,64,256]{2,1,0:T(8,128)S(1)} %get-tuple-element.41.refs_0_, bf16[2,64,256]{2,1,0:T(8,128)(2,1)S(1)} %collective-permute-done.7.refs_1_, bf16[2,64,256]{2,1,0:T(8,128)(2,1)S(1)} %get-tuple-element.45.refs_2_, ...), custom_call_target="tpu_custom_call" | custom-call | tf_op jit(solution)/shard_map/pallas_call | solution.py:354
  (4 shorter events, 0.1 us)
Async XLA Ops:
  0.0 11.4 %collective-permute-start.3 = (bf16[8,2,8,1024]{3,2,1,0:T(8,128)(2,1)}, bf16[8,2,8,1024]{3,2,1,0:T(8,128)(2,1)S(1)}, u32[]{:S(2)}, u32[]{:S(2)}) collective-permute-start(bf16[8,2,8,1024]{3,2,1,0:T(8,128)(2,1)} %x_ref.1), channel_id=1, source_target_pairs={{4,0},{8,4},{12,8},{5,1},{9,5},{13,9},{6,2},{10,6},{14,10},{7,3},{... | collective-permute-start | bytes 786440 | tf_op jit(solution)/shard_map/ppermute | solution.py:27
  1.3 1.0 %copy-start.1 = (bf16[8,2,8,1024]{3,2,1,0:T(8,128)(2,1)S(1)}, bf16[8,2,8,1024]{3,2,1,0:T(8,128)(2,1)}, u32[]{:S(2)}) copy-start(bf16[8,2,8,1024]{3,2,1,0:T(8,128)(2,1)} %x_ref.1) | copy-start | bytes 786436
  2.2 11.5 %copy-start.3 = (s32[8]{0:T(128)S(1)}, s32[8]{0:T(128)}, u32[]{:S(2)}) copy-start(s32[8]{0:T(128)} %param.6) | copy-start | bytes 100
  2.2 11.9 %copy-start.2 = (f32[2,2,1024]{2,1,0:T(2,128)S(1)}, f32[2,2,1024]{2,1,0:T(2,128)}, u32[]{:S(2)}) copy-start(f32[2,2,1024]{2,1,0:T(2,128)} %constant.6.clone.refs_2_) | copy-start | bytes 49156
  2.4 1.3 %collective-permute-start = (f32[8,8,1]{2,1,0:T(8,128)S(1)}, f32[8,8,1]{2,1,0:T(8,128)S(1)}, u32[]{:S(2)}, u32[]{:S(2)}) collective-permute-start(f32[8,8,1]{2,1,0:T(8,128)S(1)} %get-tuple-element.27), channel_id=1, source_target_pairs={{0,1},{1,0},{2,3},{3,2},{4,5},{5,4},{6,7},{7,6},{8,9},{9,8},{10,11... | collective-permute-start | bytes 776 | tf_op jit(solution)/shard_map/ppermute | solution.py:259
  3.9 12.3 %collective-permute-start.2 = (bf16[8,2,8,1024]{3,2,1,0:T(8,128)(2,1)S(1)}, bf16[8,2,8,1024]{3,2,1,0:T(8,128)(2,1)S(1)}, u32[]{:S(2)}, u32[]{:S(2)}) collective-permute-start(bf16[8,2,8,1024]{3,2,1,0:T(8,128)(2,1)S(1)} %shard_map.56.white_ref.refs_0_), channel_id=1, source_target_pairs={{12,4},{13,5},{14,6},{15,7},{28,20},{29,21},{30,22},{31,23}} | collective-permute-start | bytes 786440 | tf_op jit(solution)/shard_map/ppermute | solution.py:312
  4.6 12.0 %collective-permute-start.1 = (bf16[8,2,8,1024]{3,2,1,0:T(8,128)(2,1)S(1)}, bf16[8,2,8,1024]{3,2,1,0:T(8,128)(2,1)S(1)}, u32[]{:S(2)}, u32[]{:S(2)}) collective-permute-start(bf16[8,2,8,1024]{3,2,1,0:T(8,128)(2,1)S(1)} %shard_map.56.white_ref.refs_0_), channel_id=1, source_target_pairs={{0,4},{4,8},{1,5},{5,9},{2,6},{6,10},{3,7},{7,11},{16,20},{20,24},... | collective-permute-start | bytes 786440 | tf_op jit(solution)/shard_map/ppermute | solution.py:313
  11.6 2.4 %collective-permute-start.4 = (f32[8,8,1]{2,1,0:T(8,128)S(1)}, f32[8,8,1]{2,1,0:T(8,128)S(1)}, u32[]{:S(2)}, u32[]{:S(2)}) collective-permute-start(f32[8,8,1]{2,1,0:T(8,128)S(1)} %shard_map.58), channel_id=1, source_target_pairs={{0,1},{1,0},{2,3},{3,2},{4,5},{5,4},{6,7},{7,6},{8,9},{9,8},{10,11... | collective-permute-start | bytes 776 | tf_op jit(solution)/shard_map/ppermute | solution.py:259
  11.6 1.0 %copy-start = (f32[2,96,512]{2,1,0:T(8,128)S(1)}, f32[2,96,512]{2,1,0:T(8,128)}, u32[]{:S(2)}) copy-start(f32[2,96,512]{2,1,0:T(8,128)} %constant.7.clone.base_ref) | copy-start | bytes 1179652
  16.2 15.1 %copy-start.4 = (s32[8,4]{0,1:T(4,128)S(1)}, s32[8,4]{0,1:T(4,128)}, u32[]{:S(2)}) copy-start(s32[8,4]{0,1:T(4,128)} %param.7) | copy-start | bytes 388
  18.7 1.6 %collective-permute-start.5 = (f32[2,2,64,256]{3,2,1,0:T(8,128)S(1)}, f32[2,2,64,256]{3,2,1,0:T(8,128)S(1)}, u32[]{:S(2)}, u32[]{:S(2)}) collective-permute-start(f32[2,2,64,256]{3,2,1,0:T(8,128)S(1)} %get-tuple-element.36), channel_id=1, source_target_pairs={{0,1},{1,0},{2,3},{3,2},{4,5},{5,4},{6,7},{7,6},{8,9},{9,8},{10,11... | collective-permute-start | bytes 786440 | tf_op jit(solution)/shard_map/ppermute | solution.py:300
  20.3 9.8 %collective-permute-start.6 = (f32[2,2,64,256]{3,2,1,0:T(8,128)S(1)}, f32[2,2,64,256]{3,2,1,0:T(8,128)S(1)}, u32[]{:S(2)}, u32[]{:S(2)}) collective-permute-start(f32[2,2,64,256]{3,2,1,0:T(8,128)S(1)} %get-tuple-element.40), channel_id=1, source_target_pairs={{0,1},{1,0},{2,3},{3,2},{4,5},{5,4},{6,7},{7,6},{8,9},{9,8},{10,11... | collective-permute-start | bytes 786440 | tf_op jit(solution)/shard_map/ppermute | solution.py:300
  20.6 9.1 %collective-permute-start.8 = (bf16[2,2,64,256]{3,2,1,0:T(8,128)(2,1)S(1)}, bf16[2,2,64,256]{3,2,1,0:T(8,128)(2,1)S(1)}, u32[]{:S(2)}, u32[]{:S(2)}) collective-permute-start(bf16[2,2,64,256]{3,2,1,0:T(8,128)(2,1)S(1)} %shard_map.65), channel_id=1, source_target_pairs={{4,0},{5,3},{6,2},{7,1},{8,4},{9,7},{10,6},{11,5},{20,16},{21,19},... | collective-permute-start | bytes 393224 | tf_op jit(solution)/shard_map/ppermute | solution.py:345
  29.7 1.9 %collective-permute-start.9 = (bf16[2,64,256]{2,1,0:T(8,128)(2,1)S(1)}, bf16[2,64,256]{2,1,0:T(8,128)(2,1)S(1)}, u32[]{:S(2)}, u32[]{:S(2)}) collective-permute-start(bf16[2,64,256]{2,1,0:T(8,128)(2,1)S(1)} %get-tuple-element.46), channel_id=1, source_target_pairs={{0,1},{1,0},{2,3},{3,2},{4,5},{5,4},{6,7},{7,6},{8,9},{9,8},{10,11... | collective-permute-start | bytes 196616 | tf_op jit(solution)/shard_map/ppermute | solution.py:300
  30.2 4.3 %collective-permute-start.7 = (bf16[2,64,256]{2,1,0:T(8,128)(2,1)S(1)}, bf16[2,64,256]{2,1,0:T(8,128)(2,1)S(1)}, u32[]{:S(2)}, u32[]{:S(2)}) collective-permute-start(bf16[2,64,256]{2,1,0:T(8,128)(2,1)S(1)} %get-tuple-element.42), channel_id=1, source_target_pairs={{0,2},{2,0},{1,3},{3,1},{4,6},{6,4},{5,7},{7,5},{8,10},{10,8},{9,1... | collective-permute-start | bytes 196616 | tf_op jit(solution)/shard_map/ppermute | solution.py:300
